TPU v7x, 32 devices: a whole 2x2x4 slice. The times are simulated.
32 devices in a mesh: layer: 2 (over x), expert: 16 (over z, y, core).
Axes of the slice: x: 2, y: 2, z: 4, core: 2. Of those that a mesh axis runs over, the one named last changes fastest.
Arguments:
- grad_hidden: bfloat16 [8192, 384], P(('layer', 'expert')), parts along dimension 0, may hold values from -6 to 6
- grad_out: bfloat16 [8192, 1024], P(('layer', 'expert')), parts along dimension 0, may hold values from -0.41992188 to 0.41992188
- grad_route: int32 [8192, 1], P(('layer', 'expert')), parts along dimension 0, may hold values from 0 to 15; in each aligned block of 256 rows (0 to 255, 256 to 511, ...) at most 32 rows name the same one
- live_rows: int32 [32], P(('layer', 'expert')), parts along dimension 0, may hold values from 1 to 256, 3072 in all
- w_down: bfloat16 [32, 384, 1024], P(('layer', 'expert')), parts along dimension 0, may hold values from -0.3125 to 0.3125
- w_moment: bfloat16 [32, 384, 1024], P(('layer', 'expert')), parts along dimension 0, may hold values from -6 to 6
- perm: int32 [32], P('layer'), parts along dimension 0, may hold values from 0 to 15, each once
- fwd_hidden: bfloat16 [8192, 384], P(('layer', 'expert')), parts along dimension 0, may hold values from -6 to 6
- fwd_route: int32 [8192, 1], P(('layer', 'expert')), parts along dimension 0, may hold values from 0 to 15; in each aligned block of 256 rows (0 to 255, 256 to 511, ...) at most 32 rows name the same one
- fwd_gate: float32 [8192], P(('layer', 'expert')), parts along dimension 0, may hold values from 0.25 to 1
Outputs:
- placed_weight: bfloat16 [32, 384, 1024], P(('layer', 'expert')), parts along dimension 0
- placed_moment: bfloat16 [32, 384, 1024], P(('layer', 'expert')), parts along dimension 0
- fwd_out: bfloat16 [8192, 1024], P(('layer', 'expert')), parts along dimension 0
There are 2 independent parts, one for each index of `layer`. A program takes and returns all parts, laid end to end along the dimension named above; each array names one. Nothing has to cross between parts.
Inputs may be any that keep to these rules, and one draw needn't show every extreme that they name: `grad_route`: among the 256 rows of one device no expert is named more than 32 times, and in some device's rows some expert is named exactly 32 times. `fwd_route`: among the 256 rows of one device no expert is named more than 32 times, and in some device's rows some expert is named exactly 32 times. `live_rows`: within each layer the counts sum to three quarters of 4096, and some device has all 256 rows live. `perm`: each device number appears once.
All inputs are finite; a program needn't handle non-finite values.
Results may differ from a plain program's by a relative error of at most 0.0065.
Values may be sent and summed in bfloat16 or wider, within the bound.
No kernel may reach another device: no remote copies, remote signals or barrier semaphores. Data moves between devices by JAX's collectives and lax.ppermute only.
A program may use at most 64 MiB of HBM per device.

v0:
```python
import functools

import jax
import jax.numpy as jnp
from jax import lax
from jax.experimental import pallas as pl
from jax.experimental.pallas import tpu as pltpu
from jax.sharding import PartitionSpec as P

linear_term = 3.4445
cubic_term = -4.775
quintic_term = 2.0315
moment_decay = 0.9
step_scale = 0.25
norm_floor = 1e-07

F32 = jnp.float32
BF16 = jnp.bfloat16
VMEM = pl.BlockSpec(memory_space=pltpu.VMEM)
SMEM = pl.BlockSpec(memory_space=pltpu.SMEM)
ANY = pl.BlockSpec(memory_space=pl.ANY)
MIB = 1 << 20


def chunk_at(ref, lead, k, rows, columns):
    return ref.at[
        lead,
        pl.ds(pl.multiple_of((k // 2) * rows, rows), rows),
        pl.ds(pl.multiple_of((k % 2) * columns, columns), columns),
    ]


def slot_rows(route, live, groups, capacity, perm_ref):
    rows = route.shape[1]
    experts = lax.broadcasted_iota(jnp.int32, (groups, rows), 0)
    onehot = jnp.where((experts == route) & live, 1.0, 0.0).astype(BF16)
    before = lax.broadcasted_iota(jnp.int32, (rows, rows), 0)
    after = lax.broadcasted_iota(jnp.int32, (rows, rows), 1)
    upto = jnp.where(before <= after, 1.0, 0.0).astype(BF16)
    ranks = jnp.dot(onehot, upto, preferred_element_type=F32)
    rank = jnp.sum(ranks * onehot.astype(F32), axis=0, keepdims=True).astype(jnp.int32) - 1
    target = jnp.zeros_like(route)
    for e in range(groups):
        target = jnp.where(route == e, perm_ref[e], target)
    return jnp.where(live, target * capacity + rank, -1)


def selector_of(slot, slots):
    rows = slot.shape[1]
    places = lax.broadcasted_iota(jnp.int32, (slots, rows), 0)
    return jnp.where(places == slot, 1.0, 0.0).astype(BF16)


def pack_kernel(groups, live_ref, perm_ref, route_ref, fwd_route_ref, hidden_ref, out_ref, fwd_ref, packed_ref, slot_ref):
    rows, ff = hidden_ref.shape
    d = out_ref.shape[1]
    capacity = packed_ref.shape[0] // groups
    place = lax.broadcasted_iota(jnp.int32, (1, rows), 1)
    slot = slot_rows(route_ref[...], place < live_ref[0], groups, capacity, perm_ref)
    selector = selector_of(slot, groups * capacity)
    packed_ref[:, :ff] = jnp.dot(selector, hidden_ref[...], preferred_element_type=F32).astype(BF16)
    packed_ref[:, ff : ff + d] = jnp.dot(selector, out_ref[...], preferred_element_type=F32).astype(BF16)
    fwd_slot = slot_rows(fwd_route_ref[...], place >= 0, groups, capacity, perm_ref)
    slot_ref[...] = fwd_slot
    fwd_selector = selector_of(fwd_slot, groups * capacity)
    packed_ref[:, ff + d :] = jnp.dot(fwd_selector, fwd_ref[...], preferred_element_type=F32).astype(BF16)


def pack_rows(live_rows, perm, route, fwd_route, hidden, grad_out, fwd_hidden, groups, capacity):
    rows, ff = hidden.shape
    width = 2 * ff + grad_out.shape[1]
    return pl.pallas_call(
        functools.partial(pack_kernel, groups),
        out_shape=(
            jax.ShapeDtypeStruct((groups * capacity, width), BF16),
            jax.ShapeDtypeStruct((1, rows), jnp.int32),
        ),
        in_specs=[SMEM, SMEM] + [VMEM] * 5,
        out_specs=(VMEM, VMEM),
        compiler_params=pltpu.CompilerParams(vmem_limit_bytes=32 * MIB),
        cost_estimate=pl.CostEstimate(
            flops=2 * groups * capacity * rows * width, bytes_accessed=6 * rows * width, transcendentals=0
        ),
        name="pack_rows",
    )(live_rows, perm, route.reshape(1, rows), fwd_route.reshape(1, rows), hidden, grad_out, fwd_hidden)


def split_kernel(me_ref, moment_ref, weight_ref, *piece_refs):
    for s, piece in enumerate(piece_refs):
        rows, columns = piece.shape[1:]
        for lead, source in enumerate((moment_ref, weight_ref)):
            piece[lead] = chunk_at(source, 0, me_ref[0] ^ s, rows, columns)[...]


def split(me, moment, weight, groups):
    _, ff, d = weight.shape
    piece = jax.ShapeDtypeStruct((2, ff // (groups // 2), d // 2), BF16)
    return pl.pallas_call(
        split_kernel,
        out_shape=(piece,) * groups,
        in_specs=[SMEM, VMEM, VMEM],
        out_specs=(VMEM,) * groups,
        compiler_params=pltpu.CompilerParams(vmem_limit_bytes=32 * MIB),
        cost_estimate=pl.CostEstimate(flops=0, bytes_accessed=8 * ff * d, transcendentals=0),
        name="split",
    )(me, moment, weight)


def reorder_kernel(me_ref, perm_ref, *refs):
    groups = (len(refs) - 1) // 2
    sources, targets, held = refs[:groups], refs[groups : 2 * groups], refs[-1]
    me = me_ref[0]
    for s, source in enumerate(sources):
        held[me ^ perm_ref[me ^ s]] = source[...]
    for s, target in enumerate(targets):
        target[...] = held[s]


def reorder(me, perm, pieces):
    groups = len(pieces)
    piece = jax.ShapeDtypeStruct(pieces[0].shape, BF16)
    return pl.pallas_call(
        reorder_kernel,
        out_shape=(piece,) * groups,
        in_specs=[SMEM, SMEM] + [VMEM] * groups,
        out_specs=(VMEM,) * groups,
        scratch_shapes=[pltpu.VMEM((groups,) + pieces[0].shape, BF16)],
        compiler_params=pltpu.CompilerParams(vmem_limit_bytes=32 * MIB),
        cost_estimate=pl.CostEstimate(flops=0, bytes_accessed=4 * groups * pieces[0].size, transcendentals=0),
        name="reorder",
    )(me, perm, *pieces)


def update_kernel(groups, me_ref, packed_ref, *refs):
    pieces = refs[:groups]
    weight_new_ref, moment_new_ref, produced_ref, held = refs[groups:]
    _, ff, d = held.shape
    for s, piece in enumerate(pieces):
        rows, columns = piece.shape[1:]
        for lead in range(2):
            chunk_at(held, lead, me_ref[0] ^ s, rows, columns)[...] = piece[lead]
    grad = lax.dot_general(
        packed_ref[:, :ff], packed_ref[:, ff : ff + d], (((0,), (0,)), ((), ())), preferred_element_type=F32
    )
    moment_new = (moment_decay * held[0].astype(F32) + grad).astype(BF16)
    moment_new_ref[...] = moment_new
    moment_f = moment_new.astype(F32)
    frobenius = jnp.sqrt(jnp.sum(moment_f * moment_f))
    current = (moment_f / (frobenius + norm_floor)).astype(BF16)
    for _ in range(2):
        gramian = lax.dot_general(
            current, current, (((1,), (1,)), ((), ())), preferred_element_type=F32
        ).astype(BF16)
        squared = jnp.dot(gramian, gramian, preferred_element_type=F32)
        poly = (cubic_term * gramian.astype(F32) + quintic_term * squared).astype(BF16)
        current = (
            linear_term * current.astype(F32) + jnp.dot(poly, current, preferred_element_type=F32)
        ).astype(BF16)
    weight_new = (held[1].astype(F32) - step_scale * current.astype(F32)).astype(BF16)
    weight_new_ref[...] = weight_new
    produced_ref[...] = jnp.dot(packed_ref[:, ff + d :], weight_new, preferred_element_type=F32).astype(BF16)


def update(me, packed, pieces, ff, d):
    groups = len(pieces)
    slots = packed.shape[0]
    shape = jax.ShapeDtypeStruct((ff, d), BF16)
    return pl.pallas_call(
        functools.partial(update_kernel, groups),
        out_shape=(shape, shape, jax.ShapeDtypeStruct((slots, d), BF16)),
        in_specs=[SMEM] + [VMEM] * (1 + groups),
        out_specs=(VMEM,) * 3,
        scratch_shapes=[pltpu.VMEM((2, ff, d), BF16)],
        compiler_params=pltpu.CompilerParams(vmem_limit_bytes=48 * MIB),
        cost_estimate=pl.CostEstimate(
            flops=4 * ff * d * slots + 8 * ff * ff * d + 4 * ff**3,
            bytes_accessed=8 * ff * d + 2 * packed.size + 2 * slots * d,
            transcendentals=1,
        ),
        name="update",
    )(me, packed, *pieces)


def finish_kernel(slot_ref, gate_ref, returned_ref, out_ref):
    rows = slot_ref.shape[1]
    selector = selector_of(slot_ref[...], returned_ref.shape[0])
    expert_out = lax.dot_general(
        selector, returned_ref[...], (((0,), (0,)), ((), ())), preferred_element_type=F32
    )
    down = lax.broadcasted_iota(jnp.int32, (rows, rows), 0)
    across = lax.broadcasted_iota(jnp.int32, (rows, rows), 1)
    gate = jnp.sum(jnp.where(down == across, gate_ref[...], 0.0), axis=1, keepdims=True)
    out_ref[...] = (gate * expert_out).astype(BF16)


def finish(slot, gate, returned):
    rows = slot.shape[1]
    slots, d = returned.shape
    return pl.pallas_call(
        finish_kernel,
        out_shape=jax.ShapeDtypeStruct((rows, d), BF16),
        in_specs=[VMEM] * 3,
        out_specs=VMEM,
        compiler_params=pltpu.CompilerParams(vmem_limit_bytes=32 * MIB),
        cost_estimate=pl.CostEstimate(
            flops=2 * slots * rows * d, bytes_accessed=2 * d * (slots + rows), transcendentals=0
        ),
        name="finish",
    )(slot, gate.reshape(1, rows), returned)


def exchange(array):
    return lax.all_to_all(array, "expert", split_axis=0, concat_axis=0, tiled=True)


def swap(pieces):
    groups = len(pieces)
    moved = [
        lax.ppermute(pieces[s], "expert", [(i, i ^ s) for i in range(groups)]) for s in range(1, groups)
    ]
    return [pieces[0]] + moved


def partner_plan(
    grad_hidden, grad_out, grad_route, live_rows, w_down, w_moment, perm, fwd_hidden, fwd_route, fwd_gate
):
    groups = lax.axis_size("expert")
    me = lax.axis_index("expert").astype(jnp.int32).reshape(1)
    capacity = max(4, 2 * grad_hidden.shape[0] // groups)
    ff, d = w_down.shape[1:]
    spread = swap(split(me, w_moment, w_down, groups))
    packed, fwd_slot = pack_rows(
        live_rows, perm, grad_route, fwd_route, grad_hidden, grad_out, fwd_hidden, groups, capacity
    )
    received = exchange(packed.reshape(groups, capacity, -1)).reshape(groups * capacity, -1)
    placed = swap(reorder(me, perm, spread))
    weight_new, moment_new, produced = update(me, received, placed, ff, d)
    returned = exchange(produced.reshape(groups, capacity, d)).reshape(groups * capacity, d)
    return weight_new[None], moment_new[None], finish(fwd_slot, fwd_gate, returned)


def lookup(route_ids, mapping):
    columns = jnp.arange(mapping.shape[0], dtype=jnp.int32)
    hits = route_ids[:, None] == columns[None, :]
    return jnp.sum(jnp.where(hits, mapping[None, :], 0), axis=1)


def slot_matrix(target, is_live, groups, capacity):
    columns = jnp.arange(groups, dtype=jnp.int32)
    onehot = ((target[:, None] == columns[None, :]) & is_live[:, None]).astype(jnp.int32)
    ranked = jnp.sum(jnp.cumsum(onehot, axis=0) * onehot, axis=1) - 1
    slot_of = jnp.where(is_live, target * capacity + ranked, -1)
    slots = jnp.arange(groups * capacity, dtype=jnp.int32)
    return (slots[:, None] == slot_of[None, :]).astype(jnp.bfloat16)


def orthogonalize(moment):
    moment_f = moment.astype(jnp.float32)
    frobenius = jnp.sqrt(jnp.sum(moment_f * moment_f))
    current = (moment_f / (frobenius + norm_floor)).astype(jnp.bfloat16)
    for sweep_index in range(2):
        gramian = lax.dot_general(
            current, current, (((1,), (1,)), ((), ())), preferred_element_type=jnp.float32
        ).astype(jnp.bfloat16)
        squared = jnp.dot(gramian, gramian, preferred_element_type=jnp.float32)
        poly = (cubic_term * gramian.astype(jnp.float32) + quintic_term * squared).astype(
            jnp.bfloat16
        )
        current = (
            linear_term * current.astype(jnp.float32)
            + jnp.dot(poly, current, preferred_element_type=jnp.float32)
        ).astype(jnp.bfloat16)
    return current


def relocate(weight, moment, perm):
    groups = lax.axis_size("expert")
    weight_flat = weight.reshape(groups, -1)
    moment_flat = moment.reshape(groups, -1)
    spread_w, spread_m = (
        lax.all_to_all(weight_flat, "expert", split_axis=0, concat_axis=0, tiled=True),
        lax.all_to_all(moment_flat, "expert", split_axis=0, concat_axis=0, tiled=True),
    )
    devices = jnp.arange(groups, dtype=jnp.int32)
    inverse = jnp.sum(jnp.where(perm[None, :] == devices[:, None], devices[None, :], 0), axis=1)
    ordered_w = jnp.take(spread_w, inverse, axis=0)
    ordered_m = jnp.take(spread_m, inverse, axis=0)
    back_w, back_m = (
        lax.all_to_all(ordered_w, "expert", split_axis=0, concat_axis=0, tiled=True),
        lax.all_to_all(ordered_m, "expert", split_axis=0, concat_axis=0, tiled=True),
    )
    return (back_w.reshape(weight.shape), back_m.reshape(moment.shape))


def routed_plan(
    grad_hidden,
    grad_out,
    grad_route,
    live_rows,
    w_down,
    w_moment,
    perm,
    fwd_hidden,
    fwd_route,
    fwd_gate,
):
    groups = lax.axis_size("expert")
    grad_count = grad_hidden.shape[0]
    capacity = max(4, 2 * grad_count // groups)
    is_live = jnp.arange(grad_count, dtype=jnp.int32) < live_rows[0]
    route_ids = grad_route[:, 0]
    weight, moment = relocate(w_down, w_moment, perm)
    target = lookup(route_ids, perm)
    selector = slot_matrix(target, is_live, groups, capacity)
    hidden_buf = (
        jnp.dot(selector, grad_hidden, preferred_element_type=jnp.float32)
        .astype(jnp.bfloat16)
        .reshape(groups, capacity, -1)
    )
    outgrad_buf = (
        jnp.dot(selector, grad_out, preferred_element_type=jnp.float32)
        .astype(jnp.bfloat16)
        .reshape(groups, capacity, -1)
    )
    recv_hidden, recv_outgrad = (
        lax.all_to_all(hidden_buf, "expert", split_axis=0, concat_axis=0, tiled=True),
        lax.all_to_all(outgrad_buf, "expert", split_axis=0, concat_axis=0, tiled=True),
    )
    grad = lax.dot_general(
        recv_hidden.reshape(groups * capacity, -1),
        recv_outgrad.reshape(groups * capacity, -1),
        (((0,), (0,)), ((), ())),
        preferred_element_type=jnp.float32,
    )
    moment_new = (moment_decay * moment[0].astype(jnp.float32) + grad).astype(jnp.bfloat16)
    ortho = orthogonalize(moment_new)
    weight_new = (weight[0].astype(jnp.float32) - step_scale * ortho.astype(jnp.float32)).astype(
        jnp.bfloat16
    )
    weight_new = weight_new[None]
    moment_new = moment_new[None]
    fwd_ids = fwd_route[:, 0]
    placed_weight, placed_moment = (weight_new, moment_new)
    fwd_target = lookup(fwd_ids, perm)
    fwd_weight = weight_new[0]
    fwd_count = fwd_hidden.shape[0]
    fwd_capacity = max(4, 2 * fwd_count // groups)
    fwd_selector = slot_matrix(fwd_target, jnp.ones((fwd_count,), dtype=bool), groups, fwd_capacity)
    fwd_buf = (
        jnp.dot(fwd_selector, fwd_hidden, preferred_element_type=jnp.float32)
        .astype(jnp.bfloat16)
        .reshape(groups, fwd_capacity, -1)
    )
    produced = jnp.einsum(
        "gkf,fd->gkd",
        lax.all_to_all(fwd_buf, "expert", split_axis=0, concat_axis=0, tiled=True),
        fwd_weight,
        preferred_element_type=jnp.float32,
    ).astype(jnp.bfloat16)
    returned = lax.all_to_all(produced, "expert", split_axis=0, concat_axis=0, tiled=True)
    fwd_rows_out = lax.dot_general(
        fwd_selector,
        returned.reshape(groups * fwd_capacity, -1),
        (((0,), (0,)), ((), ())),
        preferred_element_type=jnp.float32,
    )
    fwd_out = (fwd_rows_out * fwd_gate[:, None]).astype(jnp.bfloat16)
    return (placed_weight, placed_moment, fwd_out)


def solution(mesh):
    groups = mesh.shape["expert"]
    in_specs = (
        P(("layer", "expert"), None),
        P(("layer", "expert"), None),
        P(("layer", "expert"), None),
        P(("layer", "expert")),
        P(("layer", "expert"), None, None),
        P(("layer", "expert"), None, None),
        P("layer"),
        P(("layer", "expert"), None),
        P(("layer", "expert"), None),
        P(("layer", "expert")),
    )
    out_specs = (
        P(("layer", "expert"), None, None),
        P(("layer", "expert"), None, None),
        P(("layer", "expert"), None),
    )

    def per_device(*args):
        few = groups & (groups - 1) == 0 and groups <= 2 * args[0].shape[0] // groups
        return (partner_plan if few else routed_plan)(*args)

    return jax.shard_map(
        per_device, mesh=mesh, in_specs=in_specs, out_specs=out_specs, check_vma=False
    )
```

profile of v0, /device:TPU:0, one launch (start us, length us, event | category | flops | bytes accessed | tf_op | source)
XLA Modules:
  0.0 173.1 jit_solution(17745333964091577682)
XLA Ops:
  6.2 1.5 pack_rows.1
  7.8 1.3 copy-done
  9.0 7.5 %all-to-all-start = ((bf16[16,32,1792]{2,1,0:T(8,128)(2,1)}), bf16[16,32,1792]{2,1,0:T(8,128)(2,1)S(1)}, u32[]{:S(2)}, u32[]{:S(2)}) async-start(bf16[16,32,1792]{2,1,0:T(8,128)(2,1)} %bitcast.12), calls=%async_computation | async-start | bytes 3670016 | tf_op jit(solution)/shard_map/all_to_all | solution.py:213
  17.2 1.7 collective-permute-start.1
  18.9 1.7 collective-permute-start.3
  20.7 2.6 %collective-permute-start.5 = (bf16[2,48,512]{2,1,0:T(8,128)(2,1)S(1)}, bf16[2,48,512]{2,1,0:T(8,128)(2,1)S(1)}, u32[]{:S(2)}, u32[]{:S(2)}) collective-permute-start(bf16[2,48,512]{2,1,0:T(8,128)(2,1)S(1)} %get-tuple-element.47), channel_id=1, source_target_pairs={{0,6},{1,7},{2,4},{3,5},{4,2},{5,3},{6,0},{7,1},{8,14},{9,15},{10,... | collective-permute-start | bytes 294920 | tf_op jit(solution)/shard_map/ppermute | solution.py:219
  23.3 9.8 %collective-permute-done.1.refs_2_ = bf16[2,48,512]{2,1,0:T(8,128)(2,1)S(1)} collective-permute-done((bf16[2,48,512]{2,1,0:T(8,128)(2,1)S(1)}, bf16[2,48,512]{2,1,0:T(8,128)(2,1)S(1)}, u32[]{:S(2)}, u32[]{:S(2)}) %collective-permute-start.1) | collective-permute-done | bytes 98336 | tf_op jit(solution)/shard_map/ppermute | solution.py:219
  33.1 4.3 %collective-permute-done.2.refs_3_ = bf16[2,48,512]{2,1,0:T(8,128)(2,1)S(1)} collective-permute-done((bf16[2,48,512]{2,1,0:T(8,128)(2,1)S(1)}, bf16[2,48,512]{2,1,0:T(8,128)(2,1)S(1)}, u32[]{:S(2)}, u32[]{:S(2)}) %collective-permute-start.2) | collective-permute-done | bytes 98336 | tf_op jit(solution)/shard_map/ppermute | solution.py:219
  37.5 12.2 %collective-permute-done.3.refs_4_ = bf16[2,48,512]{2,1,0:T(8,128)(2,1)S(1)} collective-permute-done((bf16[2,48,512]{2,1,0:T(8,128)(2,1)S(1)}, bf16[2,48,512]{2,1,0:T(8,128)(2,1)S(1)}, u32[]{:S(2)}, u32[]{:S(2)}) %collective-permute-start.3) | collective-permute-done | bytes 98336 | tf_op jit(solution)/shard_map/ppermute | solution.py:219
  49.6 3.5 %collective-permute-start.8 = (bf16[2,48,512]{2,1,0:T(8,128)(2,1)S(1)}, bf16[2,48,512]{2,1,0:T(8,128)(2,1)S(1)}, u32[]{:S(2)}, u32[]{:S(2)}) collective-permute-start(bf16[2,48,512]{2,1,0:T(8,128)(2,1)S(1)} %get-tuple-element.50), channel_id=1, source_target_pairs={{0,9},{1,8},{2,11},{3,10},{4,13},{5,12},{6,15},{7,14},{8,1},{9,0},... | collective-permute-start | bytes 294920 | tf_op jit(solution)/shard_map/ppermute | solution.py:219
  53.1 3.4 %collective-permute-start.9 = (bf16[2,48,512]{2,1,0:T(8,128)(2,1)S(1)}, bf16[2,48,512]{2,1,0:T(8,128)(2,1)S(1)}, u32[]{:S(2)}, u32[]{:S(2)}) collective-permute-start(bf16[2,48,512]{2,1,0:T(8,128)(2,1)S(1)} %get-tuple-element.51), channel_id=1, source_target_pairs={{0,10},{1,11},{2,8},{3,9},{4,14},{5,15},{6,12},{7,13},{8,2},{9,3},... | collective-permute-start | bytes 294920 | tf_op jit(solution)/shard_map/ppermute | solution.py:219
  58.2 2.2 %collective-permute-start.11 = (bf16[2,48,512]{2,1,0:T(8,128)(2,1)S(1)}, bf16[2,48,512]{2,1,0:T(8,128)(2,1)S(1)}, u32[]{:S(2)}, u32[]{:S(2)}) collective-permute-start(bf16[2,48,512]{2,1,0:T(8,128)(2,1)S(1)} %get-tuple-element.53), channel_id=1, source_target_pairs={{0,12},{1,13},{2,14},{3,15},{4,8},{5,9},{6,10},{7,11},{8,4},{9,5},... | collective-permute-start | bytes 294920 | tf_op jit(solution)/shard_map/ppermute | solution.py:219
  60.4 12.7 %collective-permute-done.7.refs_8_ = bf16[2,48,512]{2,1,0:T(8,128)(2,1)S(1)} collective-permute-done((bf16[2,48,512]{2,1,0:T(8,128)(2,1)S(1)}, bf16[2,48,512]{2,1,0:T(8,128)(2,1)S(1)}, u32[]{:S(2)}, u32[]{:S(2)}) %collective-permute-start.7) | collective-permute-done | bytes 98336 | tf_op jit(solution)/shard_map/ppermute | solution.py:219
  74.3 3.4 %collective-permute-start.13 = (bf16[2,48,512]{2,1,0:T(8,128)(2,1)S(1)}, bf16[2,48,512]{2,1,0:T(8,128)(2,1)S(1)}, u32[]{:S(2)}, u32[]{:S(2)}) collective-permute-start(bf16[2,48,512]{2,1,0:T(8,128)(2,1)S(1)} %get-tuple-element.55), channel_id=1, source_target_pairs={{0,14},{1,15},{2,12},{3,13},{4,10},{5,11},{6,8},{7,9},{8,6},{9,7},... | collective-permute-start | bytes 294920 | tf_op jit(solution)/shard_map/ppermute | solution.py:219
  77.7 1.6 collective-permute-done.9.refs_10_
  79.3 5.4 %collective-permute-done.10.refs_11_ = bf16[2,48,512]{2,1,0:T(8,128)(2,1)S(1)} collective-permute-done((bf16[2,48,512]{2,1,0:T(8,128)(2,1)S(1)}, bf16[2,48,512]{2,1,0:T(8,128)(2,1)S(1)}, u32[]{:S(2)}, u32[]{:S(2)}) %collective-permute-start.10) | collective-permute-done | bytes 98336 | tf_op jit(solution)/shard_map/ppermute | solution.py:219
  84.7 2.1 %collective-permute-done.14.refs_15_ = bf16[2,48,512]{2,1,0:T(8,128)(2,1)S(1)} collective-permute-done((bf16[2,48,512]{2,1,0:T(8,128)(2,1)S(1)}, bf16[2,48,512]{2,1,0:T(8,128)(2,1)S(1)}, u32[]{:S(2)}, u32[]{:S(2)}) %collective-permute-start.14) | collective-permute-done | bytes 98336 | tf_op jit(solution)/shard_map/ppermute | solution.py:219
  88.5 1.4 collective-permute-start.17
  89.9 8.6 %collective-permute-start.18 = (bf16[2,48,512]{2,1,0:T(8,128)(2,1)S(1)}, bf16[2,48,512]{2,1,0:T(8,128)(2,1)S(1)}, u32[]{:S(2)}, u32[]{:S(2)}) collective-permute-start(bf16[2,48,512]{2,1,0:T(8,128)(2,1)S(1)} %get-tuple-element.61), channel_id=1, source_target_pairs={{0,4},{1,5},{2,6},{3,7},{4,0},{5,1},{6,2},{7,3},{8,12},{9,13},{10,... | collective-permute-start | bytes 294920 | tf_op jit(solution)/shard_map/ppermute | solution.py:219
  101.0 1.7 collective-permute-start.22
  102.7 1.3 collective-permute-start.23
  104.0 2.1 %collective-permute-start.24 = (bf16[2,48,512]{2,1,0:T(8,128)(2,1)S(1)}, bf16[2,48,512]{2,1,0:T(8,128)(2,1)S(1)}, u32[]{:S(2)}, u32[]{:S(2)}) collective-permute-start(bf16[2,48,512]{2,1,0:T(8,128)(2,1)S(1)} %get-tuple-element.67), channel_id=1, source_target_pairs={{0,10},{1,11},{2,8},{3,9},{4,14},{5,15},{6,12},{7,13},{8,2},{9,3},... | collective-permute-start | bytes 294920 | tf_op jit(solution)/shard_map/ppermute | solution.py:219
  106.2 1.6 collective-permute-start.25
  107.8 2.6 %collective-permute-done.21.refs_7_ = bf16[2,48,512]{2,1,0:T(8,128)(2,1)S(1)} collective-permute-done((bf16[2,48,512]{2,1,0:T(8,128)(2,1)S(1)}, bf16[2,48,512]{2,1,0:T(8,128)(2,1)S(1)}, u32[]{:S(2)}, u32[]{:S(2)}) %collective-permute-start.21) | collective-permute-done | bytes 98336 | tf_op jit(solution)/shard_map/ppermute | solution.py:219
  110.4 2.2 %collective-permute-start.26 = (bf16[2,48,512]{2,1,0:T(8,128)(2,1)S(1)}, bf16[2,48,512]{2,1,0:T(8,128)(2,1)S(1)}, u32[]{:S(2)}, u32[]{:S(2)}) collective-permute-start(bf16[2,48,512]{2,1,0:T(8,128)(2,1)S(1)} %get-tuple-element.69), channel_id=1, source_target_pairs={{0,12},{1,13},{2,14},{3,15},{4,8},{5,9},{6,10},{7,11},{8,4},{9,5},... | collective-permute-start | bytes 294920 | tf_op jit(solution)/shard_map/ppermute | solution.py:219
  113.7 8.2 %collective-permute-done.23.refs_9_ = bf16[2,48,512]{2,1,0:T(8,128)(2,1)S(1)} collective-permute-done((bf16[2,48,512]{2,1,0:T(8,128)(2,1)S(1)}, bf16[2,48,512]{2,1,0:T(8,128)(2,1)S(1)}, u32[]{:S(2)}, u32[]{:S(2)}) %collective-permute-start.23) | collective-permute-done | bytes 98336 | tf_op jit(solution)/shard_map/ppermute | solution.py:219
  121.9 2.2 %collective-permute-start.28 = (bf16[2,48,512]{2,1,0:T(8,128)(2,1)S(1)}, bf16[2,48,512]{2,1,0:T(8,128)(2,1)S(1)}, u32[]{:S(2)}, u32[]{:S(2)}) collective-permute-start(bf16[2,48,512]{2,1,0:T(8,128)(2,1)S(1)} %get-tuple-element.71), channel_id=1, source_target_pairs={{0,14},{1,15},{2,12},{3,13},{4,10},{5,11},{6,8},{7,9},{8,6},{9,7},... | collective-permute-start | bytes 294920 | tf_op jit(solution)/shard_map/ppermute | solution.py:219
  124.1 2.5 %collective-permute-start.29 = (bf16[2,48,512]{2,1,0:T(8,128)(2,1)S(1)}, bf16[2,48,512]{2,1,0:T(8,128)(2,1)S(1)}, u32[]{:S(2)}, u32[]{:S(2)}) collective-permute-start(bf16[2,48,512]{2,1,0:T(8,128)(2,1)S(1)} %get-tuple-element.72), channel_id=1, source_target_pairs={{0,15},{1,14},{2,13},{3,12},{4,11},{5,10},{6,9},{7,8},{8,7},{9,6},... | collective-permute-start | bytes 294920 | tf_op jit(solution)/shard_map/ppermute | solution.py:219
  126.6 5.6 %collective-permute-done.25.refs_11_ = bf16[2,48,512]{2,1,0:T(8,128)(2,1)S(1)} collective-permute-done((bf16[2,48,512]{2,1,0:T(8,128)(2,1)S(1)}, bf16[2,48,512]{2,1,0:T(8,128)(2,1)S(1)}, u32[]{:S(2)}, u32[]{:S(2)}) %collective-permute-start.25) | collective-permute-done | bytes 98336 | tf_op jit(solution)/shard_map/ppermute | solution.py:219
  132.2 5.2 %update.1 = (bf16[384,1024]{1,0:T(8,128)(2,1)}, bf16[384,1024]{1,0:T(8,128)(2,1)}, bf16[512,1024]{1,0:T(8,128)(2,1)S(1)}) custom-call(s32[1]{0:T(128)} %bitcast.me_ref, bf16[512,1792]{1,0:T(8,128)(2,1)S(1)} %bitcast.11, bf16[2,48,512]{2,1,0:T(8,128)(2,1)S(1)} %get-tuple-element.57.refs_0_, bf16[2,48,512]{2,1,0:T(8,128)(2,1)S(1)} %collective-permute-done.15.refs_1_, ...), custom_call_target="tpu_custom_call" | custom-call | flops 2239758336 | bytes 6029312 | tf_op jit(solution)/shard_map/update/pallas_call | solution.py:168
  137.4 34.4 %all_to_all.10 = bf16[16,32,1024]{2,1,0:T(8,128)(2,1)S(1)} all-to-all(bf16[16,32,1024]{2,1,0:T(8,128)(2,1)S(1)} %bitcast.13), channel_id=1, replica_groups=mesh['layer'=2,'expert'=16] {'expert'}, dimensions={0} | all-to-all | bytes 2097152 | tf_op jit(solution)/shard_map/all_to_all | solution.py:213
  171.9 1.3 finish.1
  (58 shorter events, 13.8 us)
Async XLA Ops:
  9.0 77.8 %copy-start.5 = (s32[16]{0:T(128)S(1)}, s32[16]{0:T(128)}, u32[]{:S(2)}) copy-start(s32[16]{0:T(128)} %perm_ref.3) | copy-start | bytes 196
  9.0 123.2 %all-to-all-start = ((bf16[16,32,1792]{2,1,0:T(8,128)(2,1)}), bf16[16,32,1792]{2,1,0:T(8,128)(2,1)S(1)}, u32[]{:S(2)}, u32[]{:S(2)}) async-start(bf16[16,32,1792]{2,1,0:T(8,128)(2,1)} %bitcast.12), calls=%async_computation | async-start | bytes 3670016 | tf_op jit(solution)/shard_map/all_to_all | solution.py:213
  16.7 4.0 %collective-permute-start = (bf16[2,48,512]{2,1,0:T(8,128)(2,1)S(1)}, bf16[2,48,512]{2,1,0:T(8,128)(2,1)S(1)}, u32[]{:S(2)}, u32[]{:S(2)}) collective-permute-start(bf16[2,48,512]{2,1,0:T(8,128)(2,1)S(1)} %get-tuple-element.42), channel_id=1, source_target_pairs={{0,1},{1,0},{2,3},{3,2},{4,5},{5,4},{6,7},{7,6},{8,9},{9,8},{10,11... | collective-permute-start | bytes 294920 | tf_op jit(solution)/shard_map/ppermute | solution.py:219
  17.2 15.9 %collective-permute-start.1 = (bf16[2,48,512]{2,1,0:T(8,128)(2,1)S(1)}, bf16[2,48,512]{2,1,0:T(8,128)(2,1)S(1)}, u32[]{:S(2)}, u32[]{:S(2)}) collective-permute-start(bf16[2,48,512]{2,1,0:T(8,128)(2,1)S(1)} %get-tuple-element.43), channel_id=1, source_target_pairs={{0,2},{1,3},{2,0},{3,1},{4,6},{5,7},{6,4},{7,5},{8,10},{9,11},{10,... | collective-permute-start | bytes 294920 | tf_op jit(solution)/shard_map/ppermute | solution.py:219
  18.9 18.6 %collective-permute-start.2 = (bf16[2,48,512]{2,1,0:T(8,128)(2,1)S(1)}, bf16[2,48,512]{2,1,0:T(8,128)(2,1)S(1)}, u32[]{:S(2)}, u32[]{:S(2)}) collective-permute-start(bf16[2,48,512]{2,1,0:T(8,128)(2,1)S(1)} %get-tuple-element.44), channel_id=1, source_target_pairs={{0,3},{1,2},{2,1},{3,0},{4,7},{5,6},{6,5},{7,4},{8,11},{9,10},{10,... | collective-permute-start | bytes 294920 | tf_op jit(solution)/shard_map/ppermute | solution.py:219
  18.9 30.7 %collective-permute-start.3 = (bf16[2,48,512]{2,1,0:T(8,128)(2,1)S(1)}, bf16[2,48,512]{2,1,0:T(8,128)(2,1)S(1)}, u32[]{:S(2)}, u32[]{:S(2)}) collective-permute-start(bf16[2,48,512]{2,1,0:T(8,128)(2,1)S(1)} %get-tuple-element.45), channel_id=1, source_target_pairs={{0,4},{1,5},{2,6},{3,7},{4,0},{5,1},{6,2},{7,3},{8,12},{9,13},{10,... | collective-permute-start | bytes 294920 | tf_op jit(solution)/shard_map/ppermute | solution.py:219
  20.6 32.5 %collective-permute-start.4 = (bf16[2,48,512]{2,1,0:T(8,128)(2,1)S(1)}, bf16[2,48,512]{2,1,0:T(8,128)(2,1)S(1)}, u32[]{:S(2)}, u32[]{:S(2)}) collective-permute-start(bf16[2,48,512]{2,1,0:T(8,128)(2,1)S(1)} %get-tuple-element.46), channel_id=1, source_target_pairs={{0,5},{1,4},{2,7},{3,6},{4,1},{5,0},{6,3},{7,2},{8,13},{9,12},{10,... | collective-permute-start | bytes 294920 | tf_op jit(solution)/shard_map/ppermute | solution.py:219
  20.7 36.3 %collective-permute-start.5 = (bf16[2,48,512]{2,1,0:T(8,128)(2,1)S(1)}, bf16[2,48,512]{2,1,0:T(8,128)(2,1)S(1)}, u32[]{:S(2)}, u32[]{:S(2)}) collective-permute-start(bf16[2,48,512]{2,1,0:T(8,128)(2,1)S(1)} %get-tuple-element.47), channel_id=1, source_target_pairs={{0,6},{1,7},{2,4},{3,5},{4,2},{5,3},{6,0},{7,1},{8,14},{9,15},{10,... | collective-permute-start | bytes 294920 | tf_op jit(solution)/shard_map/ppermute | solution.py:219
  33.1 25.1 %collective-permute-start.6 = (bf16[2,48,512]{2,1,0:T(8,128)(2,1)S(1)}, bf16[2,48,512]{2,1,0:T(8,128)(2,1)S(1)}, u32[]{:S(2)}, u32[]{:S(2)}) collective-permute-start(bf16[2,48,512]{2,1,0:T(8,128)(2,1)S(1)} %get-tuple-element.48), channel_id=1, source_target_pairs={{0,7},{1,6},{2,5},{3,4},{4,3},{5,2},{6,1},{7,0},{8,15},{9,14},{10,... | collective-permute-start | bytes 294920 | tf_op jit(solution)/shard_map/ppermute | solution.py:219
  37.5 35.7 %collective-permute-start.7 = (bf16[2,48,512]{2,1,0:T(8,128)(2,1)S(1)}, bf16[2,48,512]{2,1,0:T(8,128)(2,1)S(1)}, u32[]{:S(2)}, u32[]{:S(2)}) collective-permute-start(bf16[2,48,512]{2,1,0:T(8,128)(2,1)S(1)} %get-tuple-element.49), channel_id=1, source_target_pairs={{0,8},{1,9},{2,10},{3,11},{4,12},{5,13},{6,14},{7,15},{8,0},{9,1},... | collective-permute-start | bytes 294920 | tf_op jit(solution)/shard_map/ppermute | solution.py:219
  49.6 24.7 %collective-permute-start.8 = (bf16[2,48,512]{2,1,0:T(8,128)(2,1)S(1)}, bf16[2,48,512]{2,1,0:T(8,128)(2,1)S(1)}, u32[]{:S(2)}, u32[]{:S(2)}) collective-permute-start(bf16[2,48,512]{2,1,0:T(8,128)(2,1)S(1)} %get-tuple-element.50), channel_id=1, source_target_pairs={{0,9},{1,8},{2,11},{3,10},{4,13},{5,12},{6,15},{7,14},{8,1},{9,0},... | collective-permute-start | bytes 294920 | tf_op jit(solution)/shard_map/ppermute | solution.py:219
  53.1 26.3 %collective-permute-start.9 = (bf16[2,48,512]{2,1,0:T(8,128)(2,1)S(1)}, bf16[2,48,512]{2,1,0:T(8,128)(2,1)S(1)}, u32[]{:S(2)}, u32[]{:S(2)}) collective-permute-start(bf16[2,48,512]{2,1,0:T(8,128)(2,1)S(1)} %get-tuple-element.51), channel_id=1, source_target_pairs={{0,10},{1,11},{2,8},{3,9},{4,14},{5,15},{6,12},{7,13},{8,2},{9,3},... | collective-permute-start | bytes 294920 | tf_op jit(solution)/shard_map/ppermute | solution.py:219
  57.0 27.7 %collective-permute-start.10 = (bf16[2,48,512]{2,1,0:T(8,128)(2,1)S(1)}, bf16[2,48,512]{2,1,0:T(8,128)(2,1)S(1)}, u32[]{:S(2)}, u32[]{:S(2)}) collective-permute-start(bf16[2,48,512]{2,1,0:T(8,128)(2,1)S(1)} %get-tuple-element.52), channel_id=1, source_target_pairs={{0,11},{1,10},{2,9},{3,8},{4,15},{5,14},{6,13},{7,12},{8,3},{9,2},... | collective-permute-start | bytes 294920 | tf_op jit(solution)/shard_map/ppermute | solution.py:219
  58.2 26.5 %collective-permute-start.11 = (bf16[2,48,512]{2,1,0:T(8,128)(2,1)S(1)}, bf16[2,48,512]{2,1,0:T(8,128)(2,1)S(1)}, u32[]{:S(2)}, u32[]{:S(2)}) collective-permute-start(bf16[2,48,512]{2,1,0:T(8,128)(2,1)S(1)} %get-tuple-element.53), channel_id=1, source_target_pairs={{0,12},{1,13},{2,14},{3,15},{4,8},{5,9},{6,10},{7,11},{8,4},{9,5},... | collective-permute-start | bytes 294920 | tf_op jit(solution)/shard_map/ppermute | solution.py:219
  73.2 11.5 %collective-permute-start.12 = (bf16[2,48,512]{2,1,0:T(8,128)(2,1)S(1)}, bf16[2,48,512]{2,1,0:T(8,128)(2,1)S(1)}, u32[]{:S(2)}, u32[]{:S(2)}) collective-permute-start(bf16[2,48,512]{2,1,0:T(8,128)(2,1)S(1)} %get-tuple-element.54), channel_id=1, source_target_pairs={{0,13},{1,12},{2,15},{3,14},{4,9},{5,8},{6,11},{7,10},{8,5},{9,4},... | collective-permute-start | bytes 294920 | tf_op jit(solution)/shard_map/ppermute | solution.py:219
  74.3 10.4 %collective-permute-start.13 = (bf16[2,48,512]{2,1,0:T(8,128)(2,1)S(1)}, bf16[2,48,512]{2,1,0:T(8,128)(2,1)S(1)}, u32[]{:S(2)}, u32[]{:S(2)}) collective-permute-start(bf16[2,48,512]{2,1,0:T(8,128)(2,1)S(1)} %get-tuple-element.55), channel_id=1, source_target_pairs={{0,14},{1,15},{2,12},{3,13},{4,10},{5,11},{6,8},{7,9},{8,6},{9,7},... | collective-permute-start | bytes 294920 | tf_op jit(solution)/shard_map/ppermute | solution.py:219
  79.3 7.5 %collective-permute-start.14 = (bf16[2,48,512]{2,1,0:T(8,128)(2,1)S(1)}, bf16[2,48,512]{2,1,0:T(8,128)(2,1)S(1)}, u32[]{:S(2)}, u32[]{:S(2)}) collective-permute-start(bf16[2,48,512]{2,1,0:T(8,128)(2,1)S(1)} %get-tuple-element.56), channel_id=1, source_target_pairs={{0,15},{1,14},{2,13},{3,12},{4,11},{5,10},{6,9},{7,8},{8,7},{9,6},... | collective-permute-start | bytes 294920 | tf_op jit(solution)/shard_map/ppermute | solution.py:219
  87.6 11.1 %collective-permute-start.15 = (bf16[2,48,512]{2,1,0:T(8,128)(2,1)S(1)}, bf16[2,48,512]{2,1,0:T(8,128)(2,1)S(1)}, u32[]{:S(2)}, u32[]{:S(2)}) collective-permute-start(bf16[2,48,512]{2,1,0:T(8,128)(2,1)S(1)} %get-tuple-element.58), channel_id=1, source_target_pairs={{0,1},{1,0},{2,3},{3,2},{4,5},{5,4},{6,7},{7,6},{8,9},{9,8},{10,11... | collective-permute-start | bytes 294920 | tf_op jit(solution)/shard_map/ppermute | solution.py:219
  88.5 11.4 %collective-permute-start.16 = (bf16[2,48,512]{2,1,0:T(8,128)(2,1)S(1)}, bf16[2,48,512]{2,1,0:T(8,128)(2,1)S(1)}, u32[]{:S(2)}, u32[]{:S(2)}) collective-permute-start(bf16[2,48,512]{2,1,0:T(8,128)(2,1)S(1)} %get-tuple-element.59), channel_id=1, source_target_pairs={{0,2},{1,3},{2,0},{3,1},{4,6},{5,7},{6,4},{7,5},{8,10},{9,11},{10,... | collective-permute-start | bytes 294920 | tf_op jit(solution)/shard_map/ppermute | solution.py:219
  88.5 12.6 %collective-permute-start.17 = (bf16[2,48,512]{2,1,0:T(8,128)(2,1)S(1)}, bf16[2,48,512]{2,1,0:T(8,128)(2,1)S(1)}, u32[]{:S(2)}, u32[]{:S(2)}) collective-permute-start(bf16[2,48,512]{2,1,0:T(8,128)(2,1)S(1)} %get-tuple-element.60), channel_id=1, source_target_pairs={{0,3},{1,2},{2,1},{3,0},{4,7},{5,6},{6,5},{7,4},{8,11},{9,10},{10,... | collective-permute-start | bytes 294920 | tf_op jit(solution)/shard_map/ppermute | solution.py:219
  89.9 12.8 %collective-permute-start.18 = (bf16[2,48,512]{2,1,0:T(8,128)(2,1)S(1)}, bf16[2,48,512]{2,1,0:T(8,128)(2,1)S(1)}, u32[]{:S(2)}, u32[]{:S(2)}) collective-permute-start(bf16[2,48,512]{2,1,0:T(8,128)(2,1)S(1)} %get-tuple-element.61), channel_id=1, source_target_pairs={{0,4},{1,5},{2,6},{3,7},{4,0},{5,1},{6,2},{7,3},{8,12},{9,13},{10,... | collective-permute-start | bytes 294920 | tf_op jit(solution)/shard_map/ppermute | solution.py:219
  98.5 5.6 %collective-permute-start.19 = (bf16[2,48,512]{2,1,0:T(8,128)(2,1)S(1)}, bf16[2,48,512]{2,1,0:T(8,128)(2,1)S(1)}, u32[]{:S(2)}, u32[]{:S(2)}) collective-permute-start(bf16[2,48,512]{2,1,0:T(8,128)(2,1)S(1)} %get-tuple-element.62), channel_id=1, source_target_pairs={{0,5},{1,4},{2,7},{3,6},{4,1},{5,0},{6,3},{7,2},{8,13},{9,12},{10,... | collective-permute-start | bytes 294920 | tf_op jit(solution)/shard_map/ppermute | solution.py:219
  98.7 7.5 %collective-permute-start.20 = (bf16[2,48,512]{2,1,0:T(8,128)(2,1)S(1)}, bf16[2,48,512]{2,1,0:T(8,128)(2,1)S(1)}, u32[]{:S(2)}, u32[]{:S(2)}) collective-permute-start(bf16[2,48,512]{2,1,0:T(8,128)(2,1)S(1)} %get-tuple-element.63), channel_id=1, source_target_pairs={{0,6},{1,7},{2,4},{3,5},{4,2},{5,3},{6,0},{7,1},{8,14},{9,15},{10,... | collective-permute-start | bytes 294920 | tf_op jit(solution)/shard_map/ppermute | solution.py:219
  99.9 10.5 %collective-permute-start.21 = (bf16[2,48,512]{2,1,0:T(8,128)(2,1)S(1)}, bf16[2,48,512]{2,1,0:T(8,128)(2,1)S(1)}, u32[]{:S(2)}, u32[]{:S(2)}) collective-permute-start(bf16[2,48,512]{2,1,0:T(8,128)(2,1)S(1)} %get-tuple-element.64), channel_id=1, source_target_pairs={{0,7},{1,6},{2,5},{3,4},{4,3},{5,2},{6,1},{7,0},{8,15},{9,14},{10,... | collective-permute-start | bytes 294920 | tf_op jit(solution)/shard_map/ppermute | solution.py:219
  101.0 11.5 %collective-permute-start.22 = (bf16[2,48,512]{2,1,0:T(8,128)(2,1)S(1)}, bf16[2,48,512]{2,1,0:T(8,128)(2,1)S(1)}, u32[]{:S(2)}, u32[]{:S(2)}) collective-permute-start(bf16[2,48,512]{2,1,0:T(8,128)(2,1)S(1)} %get-tuple-element.65), channel_id=1, source_target_pairs={{0,8},{1,9},{2,10},{3,11},{4,12},{5,13},{6,14},{7,15},{8,0},{9,1},... | collective-permute-start | bytes 294920 | tf_op jit(solution)/shard_map/ppermute | solution.py:219
  102.7 19.2 %collective-permute-start.23 = (bf16[2,48,512]{2,1,0:T(8,128)(2,1)S(1)}, bf16[2,48,512]{2,1,0:T(8,128)(2,1)S(1)}, u32[]{:S(2)}, u32[]{:S(2)}) collective-permute-start(bf16[2,48,512]{2,1,0:T(8,128)(2,1)S(1)} %get-tuple-element.66), channel_id=1, source_target_pairs={{0,9},{1,8},{2,11},{3,10},{4,13},{5,12},{6,15},{7,14},{8,1},{9,0},... | collective-permute-start | bytes 294920 | tf_op jit(solution)/shard_map/ppermute | solution.py:219
  104.0 20.1 %collective-permute-start.24 = (bf16[2,48,512]{2,1,0:T(8,128)(2,1)S(1)}, bf16[2,48,512]{2,1,0:T(8,128)(2,1)S(1)}, u32[]{:S(2)}, u32[]{:S(2)}) collective-permute-start(bf16[2,48,512]{2,1,0:T(8,128)(2,1)S(1)} %get-tuple-element.67), channel_id=1, source_target_pairs={{0,10},{1,11},{2,8},{3,9},{4,14},{5,15},{6,12},{7,13},{8,2},{9,3},... | collective-permute-start | bytes 294920 | tf_op jit(solution)/shard_map/ppermute | solution.py:219
  106.2 26.0 %collective-permute-start.25 = (bf16[2,48,512]{2,1,0:T(8,128)(2,1)S(1)}, bf16[2,48,512]{2,1,0:T(8,128)(2,1)S(1)}, u32[]{:S(2)}, u32[]{:S(2)}) collective-permute-start(bf16[2,48,512]{2,1,0:T(8,128)(2,1)S(1)} %get-tuple-element.68), channel_id=1, source_target_pairs={{0,11},{1,10},{2,9},{3,8},{4,15},{5,14},{6,13},{7,12},{8,3},{9,2},... | collective-permute-start | bytes 294920 | tf_op jit(solution)/shard_map/ppermute | solution.py:219
  110.4 21.8 %collective-permute-start.26 = (bf16[2,48,512]{2,1,0:T(8,128)(2,1)S(1)}, bf16[2,48,512]{2,1,0:T(8,128)(2,1)S(1)}, u32[]{:S(2)}, u32[]{:S(2)}) collective-permute-start(bf16[2,48,512]{2,1,0:T(8,128)(2,1)S(1)} %get-tuple-element.69), channel_id=1, source_target_pairs={{0,12},{1,13},{2,14},{3,15},{4,8},{5,9},{6,10},{7,11},{8,4},{9,5},... | collective-permute-start | bytes 294920 | tf_op jit(solution)/shard_map/ppermute | solution.py:219
  112.6 19.6 %collective-permute-start.27 = (bf16[2,48,512]{2,1,0:T(8,128)(2,1)S(1)}, bf16[2,48,512]{2,1,0:T(8,128)(2,1)S(1)}, u32[]{:S(2)}, u32[]{:S(2)}) collective-permute-start(bf16[2,48,512]{2,1,0:T(8,128)(2,1)S(1)} %get-tuple-element.70), channel_id=1, source_target_pairs={{0,13},{1,12},{2,15},{3,14},{4,9},{5,8},{6,11},{7,10},{8,5},{9,4},... | collective-permute-start | bytes 294920 | tf_op jit(solution)/shard_map/ppermute | solution.py:219
  121.9 10.3 %collective-permute-start.28 = (bf16[2,48,512]{2,1,0:T(8,128)(2,1)S(1)}, bf16[2,48,512]{2,1,0:T(8,128)(2,1)S(1)}, u32[]{:S(2)}, u32[]{:S(2)}) collective-permute-start(bf16[2,48,512]{2,1,0:T(8,128)(2,1)S(1)} %get-tuple-element.71), channel_id=1, source_target_pairs={{0,14},{1,15},{2,12},{3,13},{4,10},{5,11},{6,8},{7,9},{8,6},{9,7},... | collective-permute-start | bytes 294920 | tf_op jit(solution)/shard_map/ppermute | solution.py:219
  124.1 8.1 %collective-permute-start.29 = (bf16[2,48,512]{2,1,0:T(8,128)(2,1)S(1)}, bf16[2,48,512]{2,1,0:T(8,128)(2,1)S(1)}, u32[]{:S(2)}, u32[]{:S(2)}) collective-permute-start(bf16[2,48,512]{2,1,0:T(8,128)(2,1)S(1)} %get-tuple-element.72), channel_id=1, source_target_pairs={{0,15},{1,14},{2,13},{3,12},{4,11},{5,10},{6,9},{7,8},{8,7},{9,6},... | collective-permute-start | bytes 294920 | tf_op jit(solution)/shard_map/ppermute | solution.py:219
  (10 other events, 55.7 us)
where the time goes:
time: 174 us; the launch traced here: 173 us
  waiting for transfers between devices  66 us (38%)
  starting transfers between devices  56.1 us (32%)
  blocking collectives  34.4 us (20%)
  Pallas kernels  8.93 us (5%)
  local copies, waits for them, and re-layouts  6.18 us (4%)
    ppermute x30, waiting for transfers between devices, swap(): lax.ppermute(pieces[s], 'expert', [(i, i ^ s) for i in range(groups)])  66 us
    ppermute x30, starting transfers between devices, swap(): lax.ppermute(pieces[s], 'expert', [(i, i ^ s) for i in range(groups)])  48.6 us
    all_to_all x1, blocking collectives, exchange(): lax.all_to_all(array, 'expert', split_axis=0, concat_axis=0, tiled=True)  34.4 us
    all_to_all x1, starting transfers between devices, exchange(): lax.all_to_all(array, 'expert', split_axis=0, concat_axis=0, tiled=True)  7.51 us
    unnamed x22, local copies, waits for them, and re-layouts  6.18 us
    pallas_call x1, Pallas kernels, update(): pl.pallas_call(functools.partial(update_kernel, groups), out_shape=(shape...  5.21 us
  transfers between devices with their start and end apart: 31, of which 12 were waited for; matrix products, arithmetic and copies ran while one was open for 0% of the time, Pallas kernels for 1%

commit v1 on v0

--- a/solution.py
+++ b/solution.py
@@ -16,10 +16,23 @@
 
 F32 = jnp.float32
 BF16 = jnp.bfloat16
+HBM = pl.BlockSpec(memory_space=pltpu.HBM)
 VMEM = pl.BlockSpec(memory_space=pltpu.VMEM)
 SMEM = pl.BlockSpec(memory_space=pltpu.SMEM)
 ANY = pl.BlockSpec(memory_space=pl.ANY)
 MIB = 1 << 20
+
+
+def fetched(refs, held, sem):
+    copies = [pltpu.make_async_copy(ref, room, sem.at[n]) for n, (ref, room) in enumerate(zip(refs, held))]
+    for copy in copies:
+        copy.start()
+    for copy in copies:
+        copy.wait()
+
+
+def rooms(arrays):
+    return [pltpu.VMEM(a.shape, a.dtype) for a in arrays] + [pltpu.SemaphoreType.DMA((len(arrays),))]
 
 
 def chunk_at(ref, lead, k, rows, columns):
@@ -51,7 +64,10 @@
     return jnp.where(places == slot, 1.0, 0.0).astype(BF16)
 
 
-def pack_kernel(groups, live_ref, perm_ref, route_ref, fwd_route_ref, hidden_ref, out_ref, fwd_ref, packed_ref, slot_ref):
+def pack_kernel(groups, live_ref, perm_ref, *refs):
+    sources, (packed_ref, slot_ref), held, sem = refs[:5], refs[5:7], refs[7:12], refs[12]
+    fetched(sources, held, sem)
+    route_ref, fwd_route_ref, hidden_ref, out_ref, fwd_ref = held
     rows, ff = hidden_ref.shape
     d = out_ref.shape[1]
     capacity = packed_ref.shape[0] // groups
@@ -69,26 +85,30 @@
 def pack_rows(live_rows, perm, route, fwd_route, hidden, grad_out, fwd_hidden, groups, capacity):
     rows, ff = hidden.shape
     width = 2 * ff + grad_out.shape[1]
+    sources = (route.reshape(1, rows), fwd_route.reshape(1, rows), hidden, grad_out, fwd_hidden)
     return pl.pallas_call(
         functools.partial(pack_kernel, groups),
         out_shape=(
             jax.ShapeDtypeStruct((groups * capacity, width), BF16),
             jax.ShapeDtypeStruct((1, rows), jnp.int32),
         ),
-        in_specs=[SMEM, SMEM] + [VMEM] * 5,
+        in_specs=[SMEM, SMEM] + [HBM] * 5,
         out_specs=(VMEM, VMEM),
+        scratch_shapes=rooms(sources),
         compiler_params=pltpu.CompilerParams(vmem_limit_bytes=32 * MIB),
         cost_estimate=pl.CostEstimate(
             flops=2 * groups * capacity * rows * width, bytes_accessed=6 * rows * width, transcendentals=0
         ),
         name="pack_rows",
-    )(live_rows, perm, route.reshape(1, rows), fwd_route.reshape(1, rows), hidden, grad_out, fwd_hidden)
-
-
-def split_kernel(me_ref, moment_ref, weight_ref, *piece_refs):
-    for s, piece in enumerate(piece_refs):
+    )(live_rows, perm, *sources)
+
+
+def split_kernel(me_ref, moment_ref, weight_ref, *refs):
+    pieces, held, sem = refs[:-3], refs[-3:-1], refs[-1]
+    fetched((moment_ref, weight_ref), held, sem)
+    for s, piece in enumerate(pieces):
         rows, columns = piece.shape[1:]
-        for lead, source in enumerate((moment_ref, weight_ref)):
+        for lead, source in enumerate(held):
             piece[lead] = chunk_at(source, 0, me_ref[0] ^ s, rows, columns)[...]
 
 
@@ -98,8 +118,9 @@
     return pl.pallas_call(
         split_kernel,
         out_shape=(piece,) * groups,
-        in_specs=[SMEM, VMEM, VMEM],
+        in_specs=[SMEM, HBM, HBM],
         out_specs=(VMEM,) * groups,
+        scratch_shapes=rooms((moment, weight)),
         compiler_params=pltpu.CompilerParams(vmem_limit_bytes=32 * MIB),
         cost_estimate=pl.CostEstimate(flops=0, bytes_accessed=8 * ff * d, transcendentals=0),
         name="split",
@@ -213,12 +234,17 @@
     return lax.all_to_all(array, "expert", split_axis=0, concat_axis=0, tiled=True)
 
 
+def mixed_order(groups):
+    far, near = list(range(groups // 2, groups)), list(range(groups // 2 - 1, 0, -1))
+    return [s for pair in zip(far, near + [None]) for s in pair if s is not None]
+
+
 def swap(pieces):
     groups = len(pieces)
-    moved = [
-        lax.ppermute(pieces[s], "expert", [(i, i ^ s) for i in range(groups)]) for s in range(1, groups)
-    ]
-    return [pieces[0]] + moved
+    moved = {0: pieces[0]}
+    for s in mixed_order(groups):
+        moved[s] = lax.ppermute(pieces[s], "expert", [(i, i ^ s) for i in range(groups)])
+    return [moved[s] for s in range(groups)]
 
 
 def partner_plan(

time: 174 us -> 174 us (level)
  no operation moved by 1% of the time
where the time goes in v1:
time: 174 us
  waiting for transfers between devices  65.9 us (38%)
  starting transfers between devices  56.2 us (32%)
  blocking collectives  34.4 us (20%)
  Pallas kernels  9.66 us (6%)
  local copies, waits for them, and re-layouts  6.18 us (4%)
    ppermute x30, waiting for transfers between devices, swap(): lax.ppermute(pieces[s], 'expert', [(i, i ^ s) for i in range(groups)])  65.9 us
    ppermute x30, starting transfers between devices, swap(): lax.ppermute(pieces[s], 'expert', [(i, i ^ s) for i in range(groups)])  48.6 us
    all_to_all x1, blocking collectives, exchange(): lax.all_to_all(array, 'expert', split_axis=0, concat_axis=0, tiled=True)  34.4 us
    all_to_all x1, starting transfers between devices, exchange(): lax.all_to_all(array, 'expert', split_axis=0, concat_axis=0, tiled=True)  7.51 us
    unnamed x22, local copies, waits for them, and re-layouts  6.18 us
    pallas_call x1, Pallas kernels, update(): pl.pallas_call(functools.partial(update_kernel, groups), out_shape=(shape...  5.21 us
  transfers between devices with their start and end apart: 31, of which 12 were waited for; matrix products, arithmetic and copies ran while one was open for 0% of the time, Pallas kernels for 1%

profile of v1, /device:TPU:0, one launch (start us, length us, event | category | flops | bytes accessed | tf_op | source)
XLA Modules:
  0.0 173.7 jit_solution(3195394358548698858)
XLA Ops:
  6.2 2.1 %pack_rows.1 = (bf16[512,1792]{1,0:T(8,128)(2,1)S(1)}, s32[1,256]{1,0:T(1,128)S(1)}) custom-call(s32[1]{0:T(128)S(6)} %copy.13.live_ref, s32[16]{0:T(128)S(1)} %copy-done.4, s32[1,256]{1,0:T(1,128)S(1)} %bitcast.15, s32[1,256]{1,0:T(1,128)S(1)} %bitcast.16, bf16[256,384]{1,0:T(8,128)(2,1)S(1)} %copy-done.7, bf16[256,1024]{1,0:T(8,128)(2,1)S(1)} %copy-done.6, ...), custom_call_target="tpu_custom_call" | custom-call | flops 469762048 | bytes 2752512 | tf_op jit(solution)/shard_map/pack_rows/pallas_call | solution.py:89
  8.4 1.3 copy-done
  9.6 7.5 %all-to-all-start = ((bf16[16,32,1792]{2,1,0:T(8,128)(2,1)}), bf16[16,32,1792]{2,1,0:T(8,128)(2,1)S(1)}, u32[]{:S(2)}, u32[]{:S(2)}) async-start(bf16[16,32,1792]{2,1,0:T(8,128)(2,1)} %bitcast.12), calls=%async_computation | async-start | bytes 3670016 | tf_op jit(solution)/shard_map/all_to_all | solution.py:234
  17.9 1.7 collective-permute-start.1
  19.6 1.7 collective-permute-start.3
  21.4 2.6 %collective-permute-start.5 = (bf16[2,48,512]{2,1,0:T(8,128)(2,1)S(1)}, bf16[2,48,512]{2,1,0:T(8,128)(2,1)S(1)}, u32[]{:S(2)}, u32[]{:S(2)}) collective-permute-start(bf16[2,48,512]{2,1,0:T(8,128)(2,1)S(1)} %get-tuple-element.47), channel_id=1, source_target_pairs={{0,6},{1,7},{2,4},{3,5},{4,2},{5,3},{6,0},{7,1},{8,14},{9,15},{10,... | collective-permute-start | bytes 294920 | tf_op jit(solution)/shard_map/ppermute | solution.py:246
  24.0 9.7 %collective-permute-done.1.refs_2_ = bf16[2,48,512]{2,1,0:T(8,128)(2,1)S(1)} collective-permute-done((bf16[2,48,512]{2,1,0:T(8,128)(2,1)S(1)}, bf16[2,48,512]{2,1,0:T(8,128)(2,1)S(1)}, u32[]{:S(2)}, u32[]{:S(2)}) %collective-permute-start.1) | collective-permute-done | bytes 98336 | tf_op jit(solution)/shard_map/ppermute | solution.py:246
  33.7 4.3 %collective-permute-done.2.refs_3_ = bf16[2,48,512]{2,1,0:T(8,128)(2,1)S(1)} collective-permute-done((bf16[2,48,512]{2,1,0:T(8,128)(2,1)S(1)}, bf16[2,48,512]{2,1,0:T(8,128)(2,1)S(1)}, u32[]{:S(2)}, u32[]{:S(2)}) %collective-permute-start.2) | collective-permute-done | bytes 98336 | tf_op jit(solution)/shard_map/ppermute | solution.py:246
  38.1 12.2 %collective-permute-done.3.refs_4_ = bf16[2,48,512]{2,1,0:T(8,128)(2,1)S(1)} collective-permute-done((bf16[2,48,512]{2,1,0:T(8,128)(2,1)S(1)}, bf16[2,48,512]{2,1,0:T(8,128)(2,1)S(1)}, u32[]{:S(2)}, u32[]{:S(2)}) %collective-permute-start.3) | collective-permute-done | bytes 98336 | tf_op jit(solution)/shard_map/ppermute | solution.py:246
  50.2 3.5 %collective-permute-start.8 = (bf16[2,48,512]{2,1,0:T(8,128)(2,1)S(1)}, bf16[2,48,512]{2,1,0:T(8,128)(2,1)S(1)}, u32[]{:S(2)}, u32[]{:S(2)}) collective-permute-start(bf16[2,48,512]{2,1,0:T(8,128)(2,1)S(1)} %get-tuple-element.50), channel_id=1, source_target_pairs={{0,9},{1,8},{2,11},{3,10},{4,13},{5,12},{6,15},{7,14},{8,1},{9,0},... | collective-permute-start | bytes 294920 | tf_op jit(solution)/shard_map/ppermute | solution.py:246
  53.7 3.4 %collective-permute-start.9 = (bf16[2,48,512]{2,1,0:T(8,128)(2,1)S(1)}, bf16[2,48,512]{2,1,0:T(8,128)(2,1)S(1)}, u32[]{:S(2)}, u32[]{:S(2)}) collective-permute-start(bf16[2,48,512]{2,1,0:T(8,128)(2,1)S(1)} %get-tuple-element.51), channel_id=1, source_target_pairs={{0,10},{1,11},{2,8},{3,9},{4,14},{5,15},{6,12},{7,13},{8,2},{9,3},... | collective-permute-start | bytes 294920 | tf_op jit(solution)/shard_map/ppermute | solution.py:246
  58.8 2.2 %collective-permute-start.11 = (bf16[2,48,512]{2,1,0:T(8,128)(2,1)S(1)}, bf16[2,48,512]{2,1,0:T(8,128)(2,1)S(1)}, u32[]{:S(2)}, u32[]{:S(2)}) collective-permute-start(bf16[2,48,512]{2,1,0:T(8,128)(2,1)S(1)} %get-tuple-element.53), channel_id=1, source_target_pairs={{0,12},{1,13},{2,14},{3,15},{4,8},{5,9},{6,10},{7,11},{8,4},{9,5},... | collective-permute-start | bytes 294920 | tf_op jit(solution)/shard_map/ppermute | solution.py:246
  61.0 12.7 %collective-permute-done.7.refs_8_ = bf16[2,48,512]{2,1,0:T(8,128)(2,1)S(1)} collective-permute-done((bf16[2,48,512]{2,1,0:T(8,128)(2,1)S(1)}, bf16[2,48,512]{2,1,0:T(8,128)(2,1)S(1)}, u32[]{:S(2)}, u32[]{:S(2)}) %collective-permute-start.7) | collective-permute-done | bytes 98336 | tf_op jit(solution)/shard_map/ppermute | solution.py:246
  74.9 3.4 %collective-permute-start.13 = (bf16[2,48,512]{2,1,0:T(8,128)(2,1)S(1)}, bf16[2,48,512]{2,1,0:T(8,128)(2,1)S(1)}, u32[]{:S(2)}, u32[]{:S(2)}) collective-permute-start(bf16[2,48,512]{2,1,0:T(8,128)(2,1)S(1)} %get-tuple-element.55), channel_id=1, source_target_pairs={{0,14},{1,15},{2,12},{3,13},{4,10},{5,11},{6,8},{7,9},{8,6},{9,7},... | collective-permute-start | bytes 294920 | tf_op jit(solution)/shard_map/ppermute | solution.py:246
  78.3 1.6 collective-permute-done.9.refs_10_
  79.9 5.4 %collective-permute-done.10.refs_11_ = bf16[2,48,512]{2,1,0:T(8,128)(2,1)S(1)} collective-permute-done((bf16[2,48,512]{2,1,0:T(8,128)(2,1)S(1)}, bf16[2,48,512]{2,1,0:T(8,128)(2,1)S(1)}, u32[]{:S(2)}, u32[]{:S(2)}) %collective-permute-start.10) | collective-permute-done | bytes 98336 | tf_op jit(solution)/shard_map/ppermute | solution.py:246
  85.3 2.1 %collective-permute-done.14.refs_15_ = bf16[2,48,512]{2,1,0:T(8,128)(2,1)S(1)} collective-permute-done((bf16[2,48,512]{2,1,0:T(8,128)(2,1)S(1)}, bf16[2,48,512]{2,1,0:T(8,128)(2,1)S(1)}, u32[]{:S(2)}, u32[]{:S(2)}) %collective-permute-start.14) | collective-permute-done | bytes 98336 | tf_op jit(solution)/shard_map/ppermute | solution.py:246
  89.1 1.4 collective-permute-start.17
  90.5 8.6 %collective-permute-start.18 = (bf16[2,48,512]{2,1,0:T(8,128)(2,1)S(1)}, bf16[2,48,512]{2,1,0:T(8,128)(2,1)S(1)}, u32[]{:S(2)}, u32[]{:S(2)}) collective-permute-start(bf16[2,48,512]{2,1,0:T(8,128)(2,1)S(1)} %get-tuple-element.61), channel_id=1, source_target_pairs={{0,4},{1,5},{2,6},{3,7},{4,0},{5,1},{6,2},{7,3},{8,12},{9,13},{10,... | collective-permute-start | bytes 294920 | tf_op jit(solution)/shard_map/ppermute | solution.py:246
  101.6 1.7 collective-permute-start.22
  103.3 1.3 collective-permute-start.23
  104.6 2.1 %collective-permute-start.24 = (bf16[2,48,512]{2,1,0:T(8,128)(2,1)S(1)}, bf16[2,48,512]{2,1,0:T(8,128)(2,1)S(1)}, u32[]{:S(2)}, u32[]{:S(2)}) collective-permute-start(bf16[2,48,512]{2,1,0:T(8,128)(2,1)S(1)} %get-tuple-element.67), channel_id=1, source_target_pairs={{0,10},{1,11},{2,8},{3,9},{4,14},{5,15},{6,12},{7,13},{8,2},{9,3},... | collective-permute-start | bytes 294920 | tf_op jit(solution)/shard_map/ppermute | solution.py:246
  106.8 1.6 collective-permute-start.25
  108.4 2.6 %collective-permute-done.21.refs_7_ = bf16[2,48,512]{2,1,0:T(8,128)(2,1)S(1)} collective-permute-done((bf16[2,48,512]{2,1,0:T(8,128)(2,1)S(1)}, bf16[2,48,512]{2,1,0:T(8,128)(2,1)S(1)}, u32[]{:S(2)}, u32[]{:S(2)}) %collective-permute-start.21) | collective-permute-done | bytes 98336 | tf_op jit(solution)/shard_map/ppermute | solution.py:246
  111.0 2.2 %collective-permute-start.26 = (bf16[2,48,512]{2,1,0:T(8,128)(2,1)S(1)}, bf16[2,48,512]{2,1,0:T(8,128)(2,1)S(1)}, u32[]{:S(2)}, u32[]{:S(2)}) collective-permute-start(bf16[2,48,512]{2,1,0:T(8,128)(2,1)S(1)} %get-tuple-element.69), channel_id=1, source_target_pairs={{0,12},{1,13},{2,14},{3,15},{4,8},{5,9},{6,10},{7,11},{8,4},{9,5},... | collective-permute-start | bytes 294920 | tf_op jit(solution)/shard_map/ppermute | solution.py:246
  114.3 8.2 %collective-permute-done.23.refs_9_ = bf16[2,48,512]{2,1,0:T(8,128)(2,1)S(1)} collective-permute-done((bf16[2,48,512]{2,1,0:T(8,128)(2,1)S(1)}, bf16[2,48,512]{2,1,0:T(8,128)(2,1)S(1)}, u32[]{:S(2)}, u32[]{:S(2)}) %collective-permute-start.23) | collective-permute-done | bytes 98336 | tf_op jit(solution)/shard_map/ppermute | solution.py:246
  122.5 2.2 %collective-permute-start.28 = (bf16[2,48,512]{2,1,0:T(8,128)(2,1)S(1)}, bf16[2,48,512]{2,1,0:T(8,128)(2,1)S(1)}, u32[]{:S(2)}, u32[]{:S(2)}) collective-permute-start(bf16[2,48,512]{2,1,0:T(8,128)(2,1)S(1)} %get-tuple-element.71), channel_id=1, source_target_pairs={{0,14},{1,15},{2,12},{3,13},{4,10},{5,11},{6,8},{7,9},{8,6},{9,7},... | collective-permute-start | bytes 294920 | tf_op jit(solution)/shard_map/ppermute | solution.py:246
  124.7 2.5 %collective-permute-start.29 = (bf16[2,48,512]{2,1,0:T(8,128)(2,1)S(1)}, bf16[2,48,512]{2,1,0:T(8,128)(2,1)S(1)}, u32[]{:S(2)}, u32[]{:S(2)}) collective-permute-start(bf16[2,48,512]{2,1,0:T(8,128)(2,1)S(1)} %get-tuple-element.72), channel_id=1, source_target_pairs={{0,15},{1,14},{2,13},{3,12},{4,11},{5,10},{6,9},{7,8},{8,7},{9,6},... | collective-permute-start | bytes 294920 | tf_op jit(solution)/shard_map/ppermute | solution.py:246
  127.2 5.6 %collective-permute-done.25.refs_11_ = bf16[2,48,512]{2,1,0:T(8,128)(2,1)S(1)} collective-permute-done((bf16[2,48,512]{2,1,0:T(8,128)(2,1)S(1)}, bf16[2,48,512]{2,1,0:T(8,128)(2,1)S(1)}, u32[]{:S(2)}, u32[]{:S(2)}) %collective-permute-start.25) | collective-permute-done | bytes 98336 | tf_op jit(solution)/shard_map/ppermute | solution.py:246
  132.8 5.2 %update.1 = (bf16[384,1024]{1,0:T(8,128)(2,1)}, bf16[384,1024]{1,0:T(8,128)(2,1)}, bf16[512,1024]{1,0:T(8,128)(2,1)S(1)}) custom-call(s32[1]{0:T(128)} %bitcast.me_ref, bf16[512,1792]{1,0:T(8,128)(2,1)S(1)} %bitcast.11, bf16[2,48,512]{2,1,0:T(8,128)(2,1)S(1)} %get-tuple-element.57.refs_0_, bf16[2,48,512]{2,1,0:T(8,128)(2,1)S(1)} %collective-permute-done.15.refs_1_, ...), custom_call_target="tpu_custom_call" | custom-call | flops 2239758336 | bytes 6029312 | tf_op jit(solution)/shard_map/update/pallas_call | solution.py:189
  138.0 34.4 %all_to_all.10 = bf16[16,32,1024]{2,1,0:T(8,128)(2,1)S(1)} all-to-all(bf16[16,32,1024]{2,1,0:T(8,128)(2,1)S(1)} %bitcast.13), channel_id=1, replica_groups=mesh['layer'=2,'expert'=16] {'expert'}, dimensions={0} | all-to-all | bytes 2097152 | tf_op jit(solution)/shard_map/all_to_all | solution.py:234
  172.5 1.3 finish.1
  (58 shorter events, 14.0 us)
Async XLA Ops:
  9.6 77.8 %copy-start.5 = (s32[16]{0:T(128)S(1)}, s32[16]{0:T(128)}, u32[]{:S(2)}) copy-start(s32[16]{0:T(128)} %perm_ref.3) | copy-start | bytes 196
  9.6 123.2 %all-to-all-start = ((bf16[16,32,1792]{2,1,0:T(8,128)(2,1)}), bf16[16,32,1792]{2,1,0:T(8,128)(2,1)S(1)}, u32[]{:S(2)}, u32[]{:S(2)}) async-start(bf16[16,32,1792]{2,1,0:T(8,128)(2,1)} %bitcast.12), calls=%async_computation | async-start | bytes 3670016 | tf_op jit(solution)/shard_map/all_to_all | solution.py:234
  17.5 4.0 %collective-permute-start = (bf16[2,48,512]{2,1,0:T(8,128)(2,1)S(1)}, bf16[2,48,512]{2,1,0:T(8,128)(2,1)S(1)}, u32[]{:S(2)}, u32[]{:S(2)}) collective-permute-start(bf16[2,48,512]{2,1,0:T(8,128)(2,1)S(1)} %get-tuple-element.42), channel_id=1, source_target_pairs={{0,1},{1,0},{2,3},{3,2},{4,5},{5,4},{6,7},{7,6},{8,9},{9,8},{10,11... | collective-permute-start | bytes 294920 | tf_op jit(solution)/shard_map/ppermute | solution.py:246
  17.9 15.8 %collective-permute-start.1 = (bf16[2,48,512]{2,1,0:T(8,128)(2,1)S(1)}, bf16[2,48,512]{2,1,0:T(8,128)(2,1)S(1)}, u32[]{:S(2)}, u32[]{:S(2)}) collective-permute-start(bf16[2,48,512]{2,1,0:T(8,128)(2,1)S(1)} %get-tuple-element.43), channel_id=1, source_target_pairs={{0,2},{1,3},{2,0},{3,1},{4,6},{5,7},{6,4},{7,5},{8,10},{9,11},{10,... | collective-permute-start | bytes 294920 | tf_op jit(solution)/shard_map/ppermute | solution.py:246
  19.6 18.4 %collective-permute-start.2 = (bf16[2,48,512]{2,1,0:T(8,128)(2,1)S(1)}, bf16[2,48,512]{2,1,0:T(8,128)(2,1)S(1)}, u32[]{:S(2)}, u32[]{:S(2)}) collective-permute-start(bf16[2,48,512]{2,1,0:T(8,128)(2,1)S(1)} %get-tuple-element.44), channel_id=1, source_target_pairs={{0,3},{1,2},{2,1},{3,0},{4,7},{5,6},{6,5},{7,4},{8,11},{9,10},{10,... | collective-permute-start | bytes 294920 | tf_op jit(solution)/shard_map/ppermute | solution.py:246
  19.6 30.6 %collective-permute-start.3 = (bf16[2,48,512]{2,1,0:T(8,128)(2,1)S(1)}, bf16[2,48,512]{2,1,0:T(8,128)(2,1)S(1)}, u32[]{:S(2)}, u32[]{:S(2)}) collective-permute-start(bf16[2,48,512]{2,1,0:T(8,128)(2,1)S(1)} %get-tuple-element.45), channel_id=1, source_target_pairs={{0,4},{1,5},{2,6},{3,7},{4,0},{5,1},{6,2},{7,3},{8,12},{9,13},{10,... | collective-permute-start | bytes 294920 | tf_op jit(solution)/shard_map/ppermute | solution.py:246
  21.3 32.4 %collective-permute-start.4 = (bf16[2,48,512]{2,1,0:T(8,128)(2,1)S(1)}, bf16[2,48,512]{2,1,0:T(8,128)(2,1)S(1)}, u32[]{:S(2)}, u32[]{:S(2)}) collective-permute-start(bf16[2,48,512]{2,1,0:T(8,128)(2,1)S(1)} %get-tuple-element.46), channel_id=1, source_target_pairs={{0,5},{1,4},{2,7},{3,6},{4,1},{5,0},{6,3},{7,2},{8,13},{9,12},{10,... | collective-permute-start | bytes 294920 | tf_op jit(solution)/shard_map/ppermute | solution.py:246
  21.4 36.2 %collective-permute-start.5 = (bf16[2,48,512]{2,1,0:T(8,128)(2,1)S(1)}, bf16[2,48,512]{2,1,0:T(8,128)(2,1)S(1)}, u32[]{:S(2)}, u32[]{:S(2)}) collective-permute-start(bf16[2,48,512]{2,1,0:T(8,128)(2,1)S(1)} %get-tuple-element.47), channel_id=1, source_target_pairs={{0,6},{1,7},{2,4},{3,5},{4,2},{5,3},{6,0},{7,1},{8,14},{9,15},{10,... | collective-permute-start | bytes 294920 | tf_op jit(solution)/shard_map/ppermute | solution.py:246
  33.7 25.1 %collective-permute-start.6 = (bf16[2,48,512]{2,1,0:T(8,128)(2,1)S(1)}, bf16[2,48,512]{2,1,0:T(8,128)(2,1)S(1)}, u32[]{:S(2)}, u32[]{:S(2)}) collective-permute-start(bf16[2,48,512]{2,1,0:T(8,128)(2,1)S(1)} %get-tuple-element.48), channel_id=1, source_target_pairs={{0,7},{1,6},{2,5},{3,4},{4,3},{5,2},{6,1},{7,0},{8,15},{9,14},{10,... | collective-permute-start | bytes 294920 | tf_op jit(solution)/shard_map/ppermute | solution.py:246
  38.0 35.7 %collective-permute-start.7 = (bf16[2,48,512]{2,1,0:T(8,128)(2,1)S(1)}, bf16[2,48,512]{2,1,0:T(8,128)(2,1)S(1)}, u32[]{:S(2)}, u32[]{:S(2)}) collective-permute-start(bf16[2,48,512]{2,1,0:T(8,128)(2,1)S(1)} %get-tuple-element.49), channel_id=1, source_target_pairs={{0,8},{1,9},{2,10},{3,11},{4,12},{5,13},{6,14},{7,15},{8,0},{9,1},... | collective-permute-start | bytes 294920 | tf_op jit(solution)/shard_map/ppermute | solution.py:246
  50.2 24.7 %collective-permute-start.8 = (bf16[2,48,512]{2,1,0:T(8,128)(2,1)S(1)}, bf16[2,48,512]{2,1,0:T(8,128)(2,1)S(1)}, u32[]{:S(2)}, u32[]{:S(2)}) collective-permute-start(bf16[2,48,512]{2,1,0:T(8,128)(2,1)S(1)} %get-tuple-element.50), channel_id=1, source_target_pairs={{0,9},{1,8},{2,11},{3,10},{4,13},{5,12},{6,15},{7,14},{8,1},{9,0},... | collective-permute-start | bytes 294920 | tf_op jit(solution)/shard_map/ppermute | solution.py:246
  53.7 26.3 %collective-permute-start.9 = (bf16[2,48,512]{2,1,0:T(8,128)(2,1)S(1)}, bf16[2,48,512]{2,1,0:T(8,128)(2,1)S(1)}, u32[]{:S(2)}, u32[]{:S(2)}) collective-permute-start(bf16[2,48,512]{2,1,0:T(8,128)(2,1)S(1)} %get-tuple-element.51), channel_id=1, source_target_pairs={{0,10},{1,11},{2,8},{3,9},{4,14},{5,15},{6,12},{7,13},{8,2},{9,3},... | collective-permute-start | bytes 294920 | tf_op jit(solution)/shard_map/ppermute | solution.py:246
  57.6 27.7 %collective-permute-start.10 = (bf16[2,48,512]{2,1,0:T(8,128)(2,1)S(1)}, bf16[2,48,512]{2,1,0:T(8,128)(2,1)S(1)}, u32[]{:S(2)}, u32[]{:S(2)}) collective-permute-start(bf16[2,48,512]{2,1,0:T(8,128)(2,1)S(1)} %get-tuple-element.52), channel_id=1, source_target_pairs={{0,11},{1,10},{2,9},{3,8},{4,15},{5,14},{6,13},{7,12},{8,3},{9,2},... | collective-permute-start | bytes 294920 | tf_op jit(solution)/shard_map/ppermute | solution.py:246
  58.8 26.5 %collective-permute-start.11 = (bf16[2,48,512]{2,1,0:T(8,128)(2,1)S(1)}, bf16[2,48,512]{2,1,0:T(8,128)(2,1)S(1)}, u32[]{:S(2)}, u32[]{:S(2)}) collective-permute-start(bf16[2,48,512]{2,1,0:T(8,128)(2,1)S(1)} %get-tuple-element.53), channel_id=1, source_target_pairs={{0,12},{1,13},{2,14},{3,15},{4,8},{5,9},{6,10},{7,11},{8,4},{9,5},... | collective-permute-start | bytes 294920 | tf_op jit(solution)/shard_map/ppermute | solution.py:246
  73.8 11.5 %collective-permute-start.12 = (bf16[2,48,512]{2,1,0:T(8,128)(2,1)S(1)}, bf16[2,48,512]{2,1,0:T(8,128)(2,1)S(1)}, u32[]{:S(2)}, u32[]{:S(2)}) collective-permute-start(bf16[2,48,512]{2,1,0:T(8,128)(2,1)S(1)} %get-tuple-element.54), channel_id=1, source_target_pairs={{0,13},{1,12},{2,15},{3,14},{4,9},{5,8},{6,11},{7,10},{8,5},{9,4},... | collective-permute-start | bytes 294920 | tf_op jit(solution)/shard_map/ppermute | solution.py:246
  74.9 10.4 %collective-permute-start.13 = (bf16[2,48,512]{2,1,0:T(8,128)(2,1)S(1)}, bf16[2,48,512]{2,1,0:T(8,128)(2,1)S(1)}, u32[]{:S(2)}, u32[]{:S(2)}) collective-permute-start(bf16[2,48,512]{2,1,0:T(8,128)(2,1)S(1)} %get-tuple-element.55), channel_id=1, source_target_pairs={{0,14},{1,15},{2,12},{3,13},{4,10},{5,11},{6,8},{7,9},{8,6},{9,7},... | collective-permute-start | bytes 294920 | tf_op jit(solution)/shard_map/ppermute | solution.py:246
  79.9 7.5 %collective-permute-start.14 = (bf16[2,48,512]{2,1,0:T(8,128)(2,1)S(1)}, bf16[2,48,512]{2,1,0:T(8,128)(2,1)S(1)}, u32[]{:S(2)}, u32[]{:S(2)}) collective-permute-start(bf16[2,48,512]{2,1,0:T(8,128)(2,1)S(1)} %get-tuple-element.56), channel_id=1, source_target_pairs={{0,15},{1,14},{2,13},{3,12},{4,11},{5,10},{6,9},{7,8},{8,7},{9,6},... | collective-permute-start | bytes 294920 | tf_op jit(solution)/shard_map/ppermute | solution.py:246
  88.2 11.1 %collective-permute-start.15 = (bf16[2,48,512]{2,1,0:T(8,128)(2,1)S(1)}, bf16[2,48,512]{2,1,0:T(8,128)(2,1)S(1)}, u32[]{:S(2)}, u32[]{:S(2)}) collective-permute-start(bf16[2,48,512]{2,1,0:T(8,128)(2,1)S(1)} %get-tuple-element.58), channel_id=1, source_target_pairs={{0,1},{1,0},{2,3},{3,2},{4,5},{5,4},{6,7},{7,6},{8,9},{9,8},{10,11... | collective-permute-start | bytes 294920 | tf_op jit(solution)/shard_map/ppermute | solution.py:246
  89.1 11.4 %collective-permute-start.16 = (bf16[2,48,512]{2,1,0:T(8,128)(2,1)S(1)}, bf16[2,48,512]{2,1,0:T(8,128)(2,1)S(1)}, u32[]{:S(2)}, u32[]{:S(2)}) collective-permute-start(bf16[2,48,512]{2,1,0:T(8,128)(2,1)S(1)} %get-tuple-element.59), channel_id=1, source_target_pairs={{0,2},{1,3},{2,0},{3,1},{4,6},{5,7},{6,4},{7,5},{8,10},{9,11},{10,... | collective-permute-start | bytes 294920 | tf_op jit(solution)/shard_map/ppermute | solution.py:246
  89.1 12.6 %collective-permute-start.17 = (bf16[2,48,512]{2,1,0:T(8,128)(2,1)S(1)}, bf16[2,48,512]{2,1,0:T(8,128)(2,1)S(1)}, u32[]{:S(2)}, u32[]{:S(2)}) collective-permute-start(bf16[2,48,512]{2,1,0:T(8,128)(2,1)S(1)} %get-tuple-element.60), channel_id=1, source_target_pairs={{0,3},{1,2},{2,1},{3,0},{4,7},{5,6},{6,5},{7,4},{8,11},{9,10},{10,... | collective-permute-start | bytes 294920 | tf_op jit(solution)/shard_map/ppermute | solution.py:246
  90.5 12.8 %collective-permute-start.18 = (bf16[2,48,512]{2,1,0:T(8,128)(2,1)S(1)}, bf16[2,48,512]{2,1,0:T(8,128)(2,1)S(1)}, u32[]{:S(2)}, u32[]{:S(2)}) collective-permute-start(bf16[2,48,512]{2,1,0:T(8,128)(2,1)S(1)} %get-tuple-element.61), channel_id=1, source_target_pairs={{0,4},{1,5},{2,6},{3,7},{4,0},{5,1},{6,2},{7,3},{8,12},{9,13},{10,... | collective-permute-start | bytes 294920 | tf_op jit(solution)/shard_map/ppermute | solution.py:246
  99.1 5.6 %collective-permute-start.19 = (bf16[2,48,512]{2,1,0:T(8,128)(2,1)S(1)}, bf16[2,48,512]{2,1,0:T(8,128)(2,1)S(1)}, u32[]{:S(2)}, u32[]{:S(2)}) collective-permute-start(bf16[2,48,512]{2,1,0:T(8,128)(2,1)S(1)} %get-tuple-element.62), channel_id=1, source_target_pairs={{0,5},{1,4},{2,7},{3,6},{4,1},{5,0},{6,3},{7,2},{8,13},{9,12},{10,... | collective-permute-start | bytes 294920 | tf_op jit(solution)/shard_map/ppermute | solution.py:246
  99.3 7.5 %collective-permute-start.20 = (bf16[2,48,512]{2,1,0:T(8,128)(2,1)S(1)}, bf16[2,48,512]{2,1,0:T(8,128)(2,1)S(1)}, u32[]{:S(2)}, u32[]{:S(2)}) collective-permute-start(bf16[2,48,512]{2,1,0:T(8,128)(2,1)S(1)} %get-tuple-element.63), channel_id=1, source_target_pairs={{0,6},{1,7},{2,4},{3,5},{4,2},{5,3},{6,0},{7,1},{8,14},{9,15},{10,... | collective-permute-start | bytes 294920 | tf_op jit(solution)/shard_map/ppermute | solution.py:246
  100.5 10.5 %collective-permute-start.21 = (bf16[2,48,512]{2,1,0:T(8,128)(2,1)S(1)}, bf16[2,48,512]{2,1,0:T(8,128)(2,1)S(1)}, u32[]{:S(2)}, u32[]{:S(2)}) collective-permute-start(bf16[2,48,512]{2,1,0:T(8,128)(2,1)S(1)} %get-tuple-element.64), channel_id=1, source_target_pairs={{0,7},{1,6},{2,5},{3,4},{4,3},{5,2},{6,1},{7,0},{8,15},{9,14},{10,... | collective-permute-start | bytes 294920 | tf_op jit(solution)/shard_map/ppermute | solution.py:246
  101.6 11.5 %collective-permute-start.22 = (bf16[2,48,512]{2,1,0:T(8,128)(2,1)S(1)}, bf16[2,48,512]{2,1,0:T(8,128)(2,1)S(1)}, u32[]{:S(2)}, u32[]{:S(2)}) collective-permute-start(bf16[2,48,512]{2,1,0:T(8,128)(2,1)S(1)} %get-tuple-element.65), channel_id=1, source_target_pairs={{0,8},{1,9},{2,10},{3,11},{4,12},{5,13},{6,14},{7,15},{8,0},{9,1},... | collective-permute-start | bytes 294920 | tf_op jit(solution)/shard_map/ppermute | solution.py:246
  103.3 19.2 %collective-permute-start.23 = (bf16[2,48,512]{2,1,0:T(8,128)(2,1)S(1)}, bf16[2,48,512]{2,1,0:T(8,128)(2,1)S(1)}, u32[]{:S(2)}, u32[]{:S(2)}) collective-permute-start(bf16[2,48,512]{2,1,0:T(8,128)(2,1)S(1)} %get-tuple-element.66), channel_id=1, source_target_pairs={{0,9},{1,8},{2,11},{3,10},{4,13},{5,12},{6,15},{7,14},{8,1},{9,0},... | collective-permute-start | bytes 294920 | tf_op jit(solution)/shard_map/ppermute | solution.py:246
  104.6 20.1 %collective-permute-start.24 = (bf16[2,48,512]{2,1,0:T(8,128)(2,1)S(1)}, bf16[2,48,512]{2,1,0:T(8,128)(2,1)S(1)}, u32[]{:S(2)}, u32[]{:S(2)}) collective-permute-start(bf16[2,48,512]{2,1,0:T(8,128)(2,1)S(1)} %get-tuple-element.67), channel_id=1, source_target_pairs={{0,10},{1,11},{2,8},{3,9},{4,14},{5,15},{6,12},{7,13},{8,2},{9,3},... | collective-permute-start | bytes 294920 | tf_op jit(solution)/shard_map/ppermute | solution.py:246
  106.8 26.0 %collective-permute-start.25 = (bf16[2,48,512]{2,1,0:T(8,128)(2,1)S(1)}, bf16[2,48,512]{2,1,0:T(8,128)(2,1)S(1)}, u32[]{:S(2)}, u32[]{:S(2)}) collective-permute-start(bf16[2,48,512]{2,1,0:T(8,128)(2,1)S(1)} %get-tuple-element.68), channel_id=1, source_target_pairs={{0,11},{1,10},{2,9},{3,8},{4,15},{5,14},{6,13},{7,12},{8,3},{9,2},... | collective-permute-start | bytes 294920 | tf_op jit(solution)/shard_map/ppermute | solution.py:246
  111.0 21.8 %collective-permute-start.26 = (bf16[2,48,512]{2,1,0:T(8,128)(2,1)S(1)}, bf16[2,48,512]{2,1,0:T(8,128)(2,1)S(1)}, u32[]{:S(2)}, u32[]{:S(2)}) collective-permute-start(bf16[2,48,512]{2,1,0:T(8,128)(2,1)S(1)} %get-tuple-element.69), channel_id=1, source_target_pairs={{0,12},{1,13},{2,14},{3,15},{4,8},{5,9},{6,10},{7,11},{8,4},{9,5},... | collective-permute-start | bytes 294920 | tf_op jit(solution)/shard_map/ppermute | solution.py:246
  113.2 19.6 %collective-permute-start.27 = (bf16[2,48,512]{2,1,0:T(8,128)(2,1)S(1)}, bf16[2,48,512]{2,1,0:T(8,128)(2,1)S(1)}, u32[]{:S(2)}, u32[]{:S(2)}) collective-permute-start(bf16[2,48,512]{2,1,0:T(8,128)(2,1)S(1)} %get-tuple-element.70), channel_id=1, source_target_pairs={{0,13},{1,12},{2,15},{3,14},{4,9},{5,8},{6,11},{7,10},{8,5},{9,4},... | collective-permute-start | bytes 294920 | tf_op jit(solution)/shard_map/ppermute | solution.py:246
  122.5 10.3 %collective-permute-start.28 = (bf16[2,48,512]{2,1,0:T(8,128)(2,1)S(1)}, bf16[2,48,512]{2,1,0:T(8,128)(2,1)S(1)}, u32[]{:S(2)}, u32[]{:S(2)}) collective-permute-start(bf16[2,48,512]{2,1,0:T(8,128)(2,1)S(1)} %get-tuple-element.71), channel_id=1, source_target_pairs={{0,14},{1,15},{2,12},{3,13},{4,10},{5,11},{6,8},{7,9},{8,6},{9,7},... | collective-permute-start | bytes 294920 | tf_op jit(solution)/shard_map/ppermute | solution.py:246
  124.7 8.1 %collective-permute-start.29 = (bf16[2,48,512]{2,1,0:T(8,128)(2,1)S(1)}, bf16[2,48,512]{2,1,0:T(8,128)(2,1)S(1)}, u32[]{:S(2)}, u32[]{:S(2)}) collective-permute-start(bf16[2,48,512]{2,1,0:T(8,128)(2,1)S(1)} %get-tuple-element.72), channel_id=1, source_target_pairs={{0,15},{1,14},{2,13},{3,12},{4,11},{5,10},{6,9},{7,8},{8,7},{9,6},... | collective-permute-start | bytes 294920 | tf_op jit(solution)/shard_map/ppermute | solution.py:246
  (10 other events, 55.7 us)

commit v2 on v1

--- a/solution.py
+++ b/solution.py
@@ -95,7 +95,7 @@
         in_specs=[SMEM, SMEM] + [HBM] * 5,
         out_specs=(VMEM, VMEM),
         scratch_shapes=rooms(sources),
-        compiler_params=pltpu.CompilerParams(vmem_limit_bytes=32 * MIB),
+        compiler_params=pltpu.CompilerParams(vmem_limit_bytes=60 * MIB),
         cost_estimate=pl.CostEstimate(
             flops=2 * groups * capacity * rows * width, bytes_accessed=6 * rows * width, transcendentals=0
         ),
@@ -106,7 +106,7 @@
 def split_kernel(me_ref, moment_ref, weight_ref, *refs):
     pieces, held, sem = refs[:-3], refs[-3:-1], refs[-1]
     fetched((moment_ref, weight_ref), held, sem)
-    for s, piece in enumerate(pieces):
+    for s, piece in zip(mixed_order(len(pieces)), pieces):
         rows, columns = piece.shape[1:]
         for lead, source in enumerate(held):
             piece[lead] = chunk_at(source, 0, me_ref[0] ^ s, rows, columns)[...]
@@ -121,7 +121,7 @@
         in_specs=[SMEM, HBM, HBM],
         out_specs=(VMEM,) * groups,
         scratch_shapes=rooms((moment, weight)),
-        compiler_params=pltpu.CompilerParams(vmem_limit_bytes=32 * MIB),
+        compiler_params=pltpu.CompilerParams(vmem_limit_bytes=60 * MIB),
         cost_estimate=pl.CostEstimate(flops=0, bytes_accessed=8 * ff * d, transcendentals=0),
         name="split",
     )(me, moment, weight)
@@ -130,10 +130,10 @@
 def reorder_kernel(me_ref, perm_ref, *refs):
     groups = (len(refs) - 1) // 2
     sources, targets, held = refs[:groups], refs[groups : 2 * groups], refs[-1]
-    me = me_ref[0]
-    for s, source in enumerate(sources):
+    me, order = me_ref[0], mixed_order(groups)
+    for s, source in zip(order, sources):
         held[me ^ perm_ref[me ^ s]] = source[...]
-    for s, target in enumerate(targets):
+    for s, target in zip(order, targets):
         target[...] = held[s]
 
 
@@ -156,7 +156,7 @@
     pieces = refs[:groups]
     weight_new_ref, moment_new_ref, produced_ref, held = refs[groups:]
     _, ff, d = held.shape
-    for s, piece in enumerate(pieces):
+    for s, piece in zip(mixed_order(groups), pieces):
         rows, columns = piece.shape[1:]
         for lead in range(2):
             chunk_at(held, lead, me_ref[0] ^ s, rows, columns)[...] = piece[lead]
@@ -236,15 +236,15 @@
 
 def mixed_order(groups):
     far, near = list(range(groups // 2, groups)), list(range(groups // 2 - 1, 0, -1))
-    return [s for pair in zip(far, near + [None]) for s in pair if s is not None]
+    return [0] + [s for pair in zip(far, near + [None]) for s in pair if s is not None]
 
 
 def swap(pieces):
     groups = len(pieces)
-    moved = {0: pieces[0]}
-    for s in mixed_order(groups):
-        moved[s] = lax.ppermute(pieces[s], "expert", [(i, i ^ s) for i in range(groups)])
-    return [moved[s] for s in range(groups)]
+    order = mixed_order(groups)
+    return [pieces[0]] + [
+        lax.ppermute(piece, "expert", [(i, i ^ s) for i in range(groups)]) for s, piece in zip(order[1:], pieces[1:])
+    ]
 
 
 def partner_plan(

time: 174 us -> 164 us (0.943)
  starting transfers between devices: 56.2 us -> 48.8 us
  local copies, waits for them, and re-layouts: 6.18 us -> 0.91 us
  Pallas kernels: 9.66 us -> 14.1 us
  blocking collectives: 34.4 us -> 30.4 us
    ppermute x30, starting transfers between devices: 48.6 us -> 41.4 us  [swap(): lax.ppermute(piece, 'expert', [(i, i ^ s) for i in range(groups)])]
    unnamed x22 -> x8, local copies, waits for them, and re-layouts: 6.18 us -> 0.91 us
    all_to_all x1, blocking collectives: 34.4 us -> 30.4 us  [exchange(): lax.all_to_all(array, 'expert', split_axis=0, concat_axis=0, tiled=True)]
    pallas_call x1, Pallas kernels: 0.29 us -> 2.63 us  [split(): pl.pallas_call(split_kernel, out_shape=(piece,) * groups, in_specs=[SMEM,...]
    pallas_call x1, Pallas kernels: 2.14 us -> 4.19 us  [pack_rows(): pl.pallas_call(functools.partial(pack_kernel, groups), out_shape=(jax.Sha...]
  transfers between devices with their start and end apart: 31 -> 31, of which waited for: 12 -> 13; matrix products, arithmetic and copies ran while one was open for 0% -> 0% of each run, Pallas kernels for 1% -> 2%
where the time goes in v2:
time: 164 us; the launch traced here: 163 us
  waiting for transfers between devices  67.4 us (41%)
  starting transfers between devices  48.8 us (30%)
  blocking collectives  30.4 us (19%)
  Pallas kernels  14.1 us (9%)
    ppermute x30, waiting for transfers between devices, swap(): lax.ppermute(piece, 'expert', [(i, i ^ s) for i in range(groups)])  67.4 us
    ppermute x30, starting transfers between devices, swap(): lax.ppermute(piece, 'expert', [(i, i ^ s) for i in range(groups)])  41.4 us
    all_to_all x1, blocking collectives, exchange(): lax.all_to_all(array, 'expert', split_axis=0, concat_axis=0, tiled=True)  30.4 us
    all_to_all x1, starting transfers between devices, exchange(): lax.all_to_all(array, 'expert', split_axis=0, concat_axis=0, tiled=True)  7.38 us
    pallas_call x1, Pallas kernels, update(): pl.pallas_call(functools.partial(update_kernel, groups), out_shape=(shape...  5.22 us
    pallas_call x1, Pallas kernels, pack_rows(): pl.pallas_call(functools.partial(pack_kernel, groups), out_shape=(jax.Sha...  4.19 us
  transfers between devices with their start and end apart: 31, of which 13 were waited for; matrix products, arithmetic and copies ran while one was open for 0% of the time, Pallas kernels for 2%

profile of v2, /device:TPU:0, one launch (start us, length us, event | category | flops | bytes accessed | tf_op | source)
XLA Modules:
  0.0 162.9 jit_solution(5521125675720825425)
XLA Ops:
  1.3 4.2 %pack_rows.1 = (bf16[512,1792]{1,0:T(8,128)(2,1)}, s32[1,256]{1,0:T(1,128)}) custom-call(s32[1]{0:T(128)S(6)} %copy.13.live_ref, s32[16]{0:T(128)} %perm_ref.3, s32[1,256]{1,0:T(1,128)} %bitcast.15, s32[1,256]{1,0:T(1,128)} %bitcast.16, bf16[256,384]{1,0:T(8,128)(2,1)} %refs_2_.1, bf16[256,1024]{1,0:T(8,128)(2,1)} %refs_3_.1, bf16[256,384]{1,0:T(8,128)(2,1)} %refs_4_.1), custom_call_target="tpu_custom_call" | custom-call | flops 469762048 | bytes 2752512 | tf_op jit(solution)/shard_map/pack_rows/pallas_call | solution.py:89
  5.5 7.4 %all-to-all-start = ((bf16[16,32,1792]{2,1,0:T(8,128)(2,1)}), bf16[16,32,1792]{2,1,0:T(8,128)(2,1)S(1)}, u32[]{:S(2)}, u32[]{:S(2)}) async-start(bf16[16,32,1792]{2,1,0:T(8,128)(2,1)} %bitcast.14), calls=%async_computation | async-start | bytes 3670016 | tf_op jit(solution)/shard_map/all_to_all | solution.py:234
  12.9 2.6 %split.1 = (bf16[2,48,512]{2,1,0:T(8,128)(2,1)}, bf16[2,48,512]{2,1,0:T(8,128)(2,1)}, bf16[2,48,512]{2,1,0:T(8,128)(2,1)}, bf16[2,48,512]{2,1,0:T(8,128)(2,1)}, ...) custom-call(s32[1]{0:T(128)} %bitcast.me_ref, ...), custom_call_target="tpu_custom_call" | custom-call | bytes 3145728 | tf_op jit(solution)/shard_map/split/pallas_call | solution.py:118
  15.5 2.9 %collective-permute-start = (bf16[2,48,512]{2,1,0:T(8,128)(2,1)}, bf16[2,48,512]{2,1,0:T(8,128)(2,1)S(1)}, u32[]{:S(2)}, u32[]{:S(2)}) collective-permute-start(bf16[2,48,512]{2,1,0:T(8,128)(2,1)} %get-tuple-element.42), channel_id=1, source_target_pairs={{0,8},{1,9},{2,10},{3,11},{4,12},{5,13},{6,14},{7,15},{8,0},{9,1},... | collective-permute-start | bytes 294920 | tf_op jit(solution)/shard_map/ppermute | solution.py:246
  18.4 1.8 %collective-permute-start.1 = (bf16[2,48,512]{2,1,0:T(8,128)(2,1)}, bf16[2,48,512]{2,1,0:T(8,128)(2,1)S(1)}, u32[]{:S(2)}, u32[]{:S(2)}) collective-permute-start(bf16[2,48,512]{2,1,0:T(8,128)(2,1)} %get-tuple-element.43), channel_id=1, source_target_pairs={{0,7},{1,6},{2,5},{3,4},{4,3},{5,2},{6,1},{7,0},{8,15},{9,14},{10,... | collective-permute-start | bytes 294920 | tf_op jit(solution)/shard_map/ppermute | solution.py:246
  20.2 0.8 collective-permute-start.2
  21.2 3.7 %collective-permute-start.4 = (bf16[2,48,512]{2,1,0:T(8,128)(2,1)}, bf16[2,48,512]{2,1,0:T(8,128)(2,1)S(1)}, u32[]{:S(2)}, u32[]{:S(2)}) collective-permute-start(bf16[2,48,512]{2,1,0:T(8,128)(2,1)} %get-tuple-element.46), channel_id=1, source_target_pairs={{0,10},{1,11},{2,8},{3,9},{4,14},{5,15},{6,12},{7,13},{8,2},{9,3},... | collective-permute-start | bytes 294920 | tf_op jit(solution)/shard_map/ppermute | solution.py:246
  24.9 40.3 %collective-permute-done.refs_1_ = bf16[2,48,512]{2,1,0:T(8,128)(2,1)S(1)} collective-permute-done((bf16[2,48,512]{2,1,0:T(8,128)(2,1)}, bf16[2,48,512]{2,1,0:T(8,128)(2,1)S(1)}, u32[]{:S(2)}, u32[]{:S(2)}) %collective-permute-start) | collective-permute-done | bytes 98336 | tf_op jit(solution)/shard_map/ppermute | solution.py:246
  65.2 2.6 %collective-permute-start.6 = (bf16[2,48,512]{2,1,0:T(8,128)(2,1)}, bf16[2,48,512]{2,1,0:T(8,128)(2,1)S(1)}, u32[]{:S(2)}, u32[]{:S(2)}) collective-permute-start(bf16[2,48,512]{2,1,0:T(8,128)(2,1)} %get-tuple-element.48), channel_id=1, source_target_pairs={{0,11},{1,10},{2,9},{3,8},{4,15},{5,14},{6,13},{7,12},{8,3},{9,2},... | collective-permute-start | bytes 294920 | tf_op jit(solution)/shard_map/ppermute | solution.py:246
  68.0 2.4 %collective-permute-start.8 = (bf16[2,48,512]{2,1,0:T(8,128)(2,1)}, bf16[2,48,512]{2,1,0:T(8,128)(2,1)S(1)}, u32[]{:S(2)}, u32[]{:S(2)}) collective-permute-start(bf16[2,48,512]{2,1,0:T(8,128)(2,1)} %get-tuple-element.50), channel_id=1, source_target_pairs={{0,12},{1,13},{2,14},{3,15},{4,8},{5,9},{6,10},{7,11},{8,4},{9,5},... | collective-permute-start | bytes 294920 | tf_op jit(solution)/shard_map/ppermute | solution.py:246
  70.4 2.7 %collective-permute-done.5.refs_6_ = bf16[2,48,512]{2,1,0:T(8,128)(2,1)S(1)} collective-permute-done((bf16[2,48,512]{2,1,0:T(8,128)(2,1)}, bf16[2,48,512]{2,1,0:T(8,128)(2,1)S(1)}, u32[]{:S(2)}, u32[]{:S(2)}) %collective-permute-start.5) | collective-permute-done | bytes 98336 | tf_op jit(solution)/shard_map/ppermute | solution.py:246
  73.1 2.1 %collective-permute-start.10 = (bf16[2,48,512]{2,1,0:T(8,128)(2,1)}, bf16[2,48,512]{2,1,0:T(8,128)(2,1)S(1)}, u32[]{:S(2)}, u32[]{:S(2)}) collective-permute-start(bf16[2,48,512]{2,1,0:T(8,128)(2,1)} %get-tuple-element.52), channel_id=1, source_target_pairs={{0,13},{1,12},{2,15},{3,14},{4,9},{5,8},{6,11},{7,10},{8,5},{9,4},... | collective-permute-start | bytes 294920 | tf_op jit(solution)/shard_map/ppermute | solution.py:246
  75.7 4.2 %collective-permute-start.12 = (bf16[2,48,512]{2,1,0:T(8,128)(2,1)}, bf16[2,48,512]{2,1,0:T(8,128)(2,1)S(1)}, u32[]{:S(2)}, u32[]{:S(2)}) collective-permute-start(bf16[2,48,512]{2,1,0:T(8,128)(2,1)} %get-tuple-element.54), channel_id=1, source_target_pairs={{0,14},{1,15},{2,12},{3,13},{4,10},{5,11},{6,8},{7,9},{8,6},{9,7},... | collective-permute-start | bytes 294920 | tf_op jit(solution)/shard_map/ppermute | solution.py:246
  80.0 1.1 collective-permute-start.14
  81.1 2.6 %collective-permute-done.12.refs_13_ = bf16[2,48,512]{2,1,0:T(8,128)(2,1)S(1)} collective-permute-done((bf16[2,48,512]{2,1,0:T(8,128)(2,1)}, bf16[2,48,512]{2,1,0:T(8,128)(2,1)S(1)}, u32[]{:S(2)}, u32[]{:S(2)}) %collective-permute-start.12) | collective-permute-done | bytes 98336 | tf_op jit(solution)/shard_map/ppermute | solution.py:246
  83.7 3.9 %collective-permute-done.14.refs_15_ = bf16[2,48,512]{2,1,0:T(8,128)(2,1)S(1)} collective-permute-done((bf16[2,48,512]{2,1,0:T(8,128)(2,1)}, bf16[2,48,512]{2,1,0:T(8,128)(2,1)S(1)}, u32[]{:S(2)}, u32[]{:S(2)}) %collective-permute-start.14) | collective-permute-done | bytes 98336 | tf_op jit(solution)/shard_map/ppermute | solution.py:246
  87.6 0.9 copy-done
  89.2 5.6 %collective-permute-start.15 = (bf16[2,48,512]{2,1,0:T(8,128)(2,1)S(1)}, bf16[2,48,512]{2,1,0:T(8,128)(2,1)S(1)}, u32[]{:S(2)}, u32[]{:S(2)}) collective-permute-start(bf16[2,48,512]{2,1,0:T(8,128)(2,1)S(1)} %get-tuple-element.58), channel_id=1, source_target_pairs={{0,8},{1,9},{2,10},{3,11},{4,12},{5,13},{6,14},{7,15},{8,0},{9,1},... | collective-permute-start | bytes 294920 | tf_op jit(solution)/shard_map/ppermute | solution.py:246
  94.8 1.7 %collective-permute-start.17 = (bf16[2,48,512]{2,1,0:T(8,128)(2,1)S(1)}, bf16[2,48,512]{2,1,0:T(8,128)(2,1)S(1)}, u32[]{:S(2)}, u32[]{:S(2)}) collective-permute-start(bf16[2,48,512]{2,1,0:T(8,128)(2,1)S(1)} %get-tuple-element.60), channel_id=1, source_target_pairs={{0,9},{1,8},{2,11},{3,10},{4,13},{5,12},{6,15},{7,14},{8,1},{9,0},... | collective-permute-start | bytes 294920 | tf_op jit(solution)/shard_map/ppermute | solution.py:246
  96.6 1.0 collective-permute-start.18
  97.6 2.7 %collective-permute-start.19 = (bf16[2,48,512]{2,1,0:T(8,128)(2,1)S(1)}, bf16[2,48,512]{2,1,0:T(8,128)(2,1)S(1)}, u32[]{:S(2)}, u32[]{:S(2)}) collective-permute-start(bf16[2,48,512]{2,1,0:T(8,128)(2,1)S(1)} %get-tuple-element.62), channel_id=1, source_target_pairs={{0,10},{1,11},{2,8},{3,9},{4,14},{5,15},{6,12},{7,13},{8,2},{9,3},... | collective-permute-start | bytes 294920 | tf_op jit(solution)/shard_map/ppermute | solution.py:246
  100.8 2.1 %collective-permute-done.16.refs_2_ = bf16[2,48,512]{2,1,0:T(8,128)(2,1)S(1)} collective-permute-done((bf16[2,48,512]{2,1,0:T(8,128)(2,1)S(1)}, bf16[2,48,512]{2,1,0:T(8,128)(2,1)S(1)}, u32[]{:S(2)}, u32[]{:S(2)}) %collective-permute-start.16) | collective-permute-done | bytes 98336 | tf_op jit(solution)/shard_map/ppermute | solution.py:246
  103.6 3.1 %collective-permute-done.18.refs_4_ = bf16[2,48,512]{2,1,0:T(8,128)(2,1)S(1)} collective-permute-done((bf16[2,48,512]{2,1,0:T(8,128)(2,1)S(1)}, bf16[2,48,512]{2,1,0:T(8,128)(2,1)S(1)}, u32[]{:S(2)}, u32[]{:S(2)}) %collective-permute-start.18) | collective-permute-done | bytes 98336 | tf_op jit(solution)/shard_map/ppermute | solution.py:246
  107.4 1.4 collective-permute-done.19.refs_5_
  108.9 1.3 collective-permute-done.20.refs_6_
  110.1 1.5 collective-permute-start.25
  112.8 4.9 %collective-permute-done.22.refs_8_ = bf16[2,48,512]{2,1,0:T(8,128)(2,1)S(1)} collective-permute-done((bf16[2,48,512]{2,1,0:T(8,128)(2,1)S(1)}, bf16[2,48,512]{2,1,0:T(8,128)(2,1)S(1)}, u32[]{:S(2)}, u32[]{:S(2)}) %collective-permute-start.22) | collective-permute-done | bytes 98336 | tf_op jit(solution)/shard_map/ppermute | solution.py:246
  117.8 4.8 %collective-permute-start.29 = (bf16[2,48,512]{2,1,0:T(8,128)(2,1)S(1)}, bf16[2,48,512]{2,1,0:T(8,128)(2,1)S(1)}, u32[]{:S(2)}, u32[]{:S(2)}) collective-permute-start(bf16[2,48,512]{2,1,0:T(8,128)(2,1)S(1)} %get-tuple-element.72), channel_id=1, source_target_pairs={{0,15},{1,14},{2,13},{3,12},{4,11},{5,10},{6,9},{7,8},{8,7},{9,6},... | collective-permute-start | bytes 294920 | tf_op jit(solution)/shard_map/ppermute | solution.py:246
  122.6 3.4 %collective-permute-done.27.refs_13_ = bf16[2,48,512]{2,1,0:T(8,128)(2,1)S(1)} collective-permute-done((bf16[2,48,512]{2,1,0:T(8,128)(2,1)S(1)}, bf16[2,48,512]{2,1,0:T(8,128)(2,1)S(1)}, u32[]{:S(2)}, u32[]{:S(2)}) %collective-permute-start.27) | collective-permute-done | bytes 98336 | tf_op jit(solution)/shard_map/ppermute | solution.py:246
  126.1 5.2 %update.1 = (bf16[384,1024]{1,0:T(8,128)(2,1)}, bf16[384,1024]{1,0:T(8,128)(2,1)}, bf16[512,1024]{1,0:T(8,128)(2,1)S(1)}) custom-call(s32[1]{0:T(128)} %bitcast.me_ref, bf16[512,1792]{1,0:T(8,128)(2,1)S(1)} %bitcast.11, bf16[2,48,512]{2,1,0:T(8,128)(2,1)S(1)} %get-tuple-element.57.refs_0_, bf16[2,48,512]{2,1,0:T(8,128)(2,1)S(1)} %collective-permute-done.15.refs_1_, ...), custom_call_target="tpu_custom_call" | custom-call | flops 2239758336 | bytes 6029312 | tf_op jit(solution)/shard_map/update/pallas_call | solution.py:189
  131.3 30.4 %all_to_all.10 = bf16[16,32,1024]{2,1,0:T(8,128)(2,1)S(1)} all-to-all(bf16[16,32,1024]{2,1,0:T(8,128)(2,1)S(1)} %bitcast.12), channel_id=1, replica_groups=mesh['layer'=2,'expert'=16] {'expert'}, dimensions={0} | all-to-all | bytes 2097152 | tf_op jit(solution)/shard_map/all_to_all | solution.py:234
  161.7 1.3 finish.1
  (44 shorter events, 4.8 us)
Async XLA Ops:
  5.5 82.1 %copy-start.3 = (s32[16]{0:T(128)S(1)}, s32[16]{0:T(128)}, u32[]{:S(2)}) copy-start(s32[16]{0:T(128)} %perm_ref.3) | copy-start | bytes 196
  5.5 120.6 %all-to-all-start = ((bf16[16,32,1792]{2,1,0:T(8,128)(2,1)}), bf16[16,32,1792]{2,1,0:T(8,128)(2,1)S(1)}, u32[]{:S(2)}, u32[]{:S(2)}) async-start(bf16[16,32,1792]{2,1,0:T(8,128)(2,1)} %bitcast.14), calls=%async_computation | async-start | bytes 3670016 | tf_op jit(solution)/shard_map/all_to_all | solution.py:234
  15.5 49.7 %collective-permute-start = (bf16[2,48,512]{2,1,0:T(8,128)(2,1)}, bf16[2,48,512]{2,1,0:T(8,128)(2,1)S(1)}, u32[]{:S(2)}, u32[]{:S(2)}) collective-permute-start(bf16[2,48,512]{2,1,0:T(8,128)(2,1)} %get-tuple-element.42), channel_id=1, source_target_pairs={{0,8},{1,9},{2,10},{3,11},{4,12},{5,13},{6,14},{7,15},{8,0},{9,1},... | collective-permute-start | bytes 294920 | tf_op jit(solution)/shard_map/ppermute | solution.py:246
  18.4 46.8 %collective-permute-start.1 = (bf16[2,48,512]{2,1,0:T(8,128)(2,1)}, bf16[2,48,512]{2,1,0:T(8,128)(2,1)S(1)}, u32[]{:S(2)}, u32[]{:S(2)}) collective-permute-start(bf16[2,48,512]{2,1,0:T(8,128)(2,1)} %get-tuple-element.43), channel_id=1, source_target_pairs={{0,7},{1,6},{2,5},{3,4},{4,3},{5,2},{6,1},{7,0},{8,15},{9,14},{10,... | collective-permute-start | bytes 294920 | tf_op jit(solution)/shard_map/ppermute | solution.py:246
  20.2 47.6 %collective-permute-start.2 = (bf16[2,48,512]{2,1,0:T(8,128)(2,1)}, bf16[2,48,512]{2,1,0:T(8,128)(2,1)S(1)}, u32[]{:S(2)}, u32[]{:S(2)}) collective-permute-start(bf16[2,48,512]{2,1,0:T(8,128)(2,1)} %get-tuple-element.44), channel_id=1, source_target_pairs={{0,9},{1,8},{2,11},{3,10},{4,13},{5,12},{6,15},{7,14},{8,1},{9,0},... | collective-permute-start | bytes 294920 | tf_op jit(solution)/shard_map/ppermute | solution.py:246
  21.0 47.0 %collective-permute-start.3 = (bf16[2,48,512]{2,1,0:T(8,128)(2,1)}, bf16[2,48,512]{2,1,0:T(8,128)(2,1)S(1)}, u32[]{:S(2)}, u32[]{:S(2)}) collective-permute-start(bf16[2,48,512]{2,1,0:T(8,128)(2,1)} %get-tuple-element.45), channel_id=1, source_target_pairs={{0,6},{1,7},{2,4},{3,5},{4,2},{5,3},{6,0},{7,1},{8,14},{9,15},{10,... | collective-permute-start | bytes 294920 | tf_op jit(solution)/shard_map/ppermute | solution.py:246
  21.2 49.2 %collective-permute-start.4 = (bf16[2,48,512]{2,1,0:T(8,128)(2,1)}, bf16[2,48,512]{2,1,0:T(8,128)(2,1)S(1)}, u32[]{:S(2)}, u32[]{:S(2)}) collective-permute-start(bf16[2,48,512]{2,1,0:T(8,128)(2,1)} %get-tuple-element.46), channel_id=1, source_target_pairs={{0,10},{1,11},{2,8},{3,9},{4,14},{5,15},{6,12},{7,13},{8,2},{9,3},... | collective-permute-start | bytes 294920 | tf_op jit(solution)/shard_map/ppermute | solution.py:246
  65.2 7.8 %collective-permute-start.5 = (bf16[2,48,512]{2,1,0:T(8,128)(2,1)}, bf16[2,48,512]{2,1,0:T(8,128)(2,1)S(1)}, u32[]{:S(2)}, u32[]{:S(2)}) collective-permute-start(bf16[2,48,512]{2,1,0:T(8,128)(2,1)} %get-tuple-element.47), channel_id=1, source_target_pairs={{0,5},{1,4},{2,7},{3,6},{4,1},{5,0},{6,3},{7,2},{8,13},{9,12},{10,... | collective-permute-start | bytes 294920 | tf_op jit(solution)/shard_map/ppermute | solution.py:246
  65.2 10.0 %collective-permute-start.6 = (bf16[2,48,512]{2,1,0:T(8,128)(2,1)}, bf16[2,48,512]{2,1,0:T(8,128)(2,1)S(1)}, u32[]{:S(2)}, u32[]{:S(2)}) collective-permute-start(bf16[2,48,512]{2,1,0:T(8,128)(2,1)} %get-tuple-element.48), channel_id=1, source_target_pairs={{0,11},{1,10},{2,9},{3,8},{4,15},{5,14},{6,13},{7,12},{8,3},{9,2},... | collective-permute-start | bytes 294920 | tf_op jit(solution)/shard_map/ppermute | solution.py:246
  67.9 7.9 %collective-permute-start.7 = (bf16[2,48,512]{2,1,0:T(8,128)(2,1)}, bf16[2,48,512]{2,1,0:T(8,128)(2,1)S(1)}, u32[]{:S(2)}, u32[]{:S(2)}) collective-permute-start(bf16[2,48,512]{2,1,0:T(8,128)(2,1)} %get-tuple-element.49), channel_id=1, source_target_pairs={{0,4},{1,5},{2,6},{3,7},{4,0},{5,1},{6,2},{7,3},{8,12},{9,13},{10,... | collective-permute-start | bytes 294920 | tf_op jit(solution)/shard_map/ppermute | solution.py:246
  68.0 12.0 %collective-permute-start.8 = (bf16[2,48,512]{2,1,0:T(8,128)(2,1)}, bf16[2,48,512]{2,1,0:T(8,128)(2,1)S(1)}, u32[]{:S(2)}, u32[]{:S(2)}) collective-permute-start(bf16[2,48,512]{2,1,0:T(8,128)(2,1)} %get-tuple-element.50), channel_id=1, source_target_pairs={{0,12},{1,13},{2,14},{3,15},{4,8},{5,9},{6,10},{7,11},{8,4},{9,5},... | collective-permute-start | bytes 294920 | tf_op jit(solution)/shard_map/ppermute | solution.py:246
  70.4 9.6 %collective-permute-start.9 = (bf16[2,48,512]{2,1,0:T(8,128)(2,1)}, bf16[2,48,512]{2,1,0:T(8,128)(2,1)S(1)}, u32[]{:S(2)}, u32[]{:S(2)}) collective-permute-start(bf16[2,48,512]{2,1,0:T(8,128)(2,1)} %get-tuple-element.51), channel_id=1, source_target_pairs={{0,3},{1,2},{2,1},{3,0},{4,7},{5,6},{6,5},{7,4},{8,11},{9,10},{10,... | collective-permute-start | bytes 294920 | tf_op jit(solution)/shard_map/ppermute | solution.py:246
  73.1 8.0 %collective-permute-start.10 = (bf16[2,48,512]{2,1,0:T(8,128)(2,1)}, bf16[2,48,512]{2,1,0:T(8,128)(2,1)S(1)}, u32[]{:S(2)}, u32[]{:S(2)}) collective-permute-start(bf16[2,48,512]{2,1,0:T(8,128)(2,1)} %get-tuple-element.52), channel_id=1, source_target_pairs={{0,13},{1,12},{2,15},{3,14},{4,9},{5,8},{6,11},{7,10},{8,5},{9,4},... | collective-permute-start | bytes 294920 | tf_op jit(solution)/shard_map/ppermute | solution.py:246
  75.2 5.9 %collective-permute-start.11 = (bf16[2,48,512]{2,1,0:T(8,128)(2,1)}, bf16[2,48,512]{2,1,0:T(8,128)(2,1)S(1)}, u32[]{:S(2)}, u32[]{:S(2)}) collective-permute-start(bf16[2,48,512]{2,1,0:T(8,128)(2,1)} %get-tuple-element.53), channel_id=1, source_target_pairs={{0,2},{1,3},{2,0},{3,1},{4,6},{5,7},{6,4},{7,5},{8,10},{9,11},{10,... | collective-permute-start | bytes 294920 | tf_op jit(solution)/shard_map/ppermute | solution.py:246
  75.7 8.0 %collective-permute-start.12 = (bf16[2,48,512]{2,1,0:T(8,128)(2,1)}, bf16[2,48,512]{2,1,0:T(8,128)(2,1)S(1)}, u32[]{:S(2)}, u32[]{:S(2)}) collective-permute-start(bf16[2,48,512]{2,1,0:T(8,128)(2,1)} %get-tuple-element.54), channel_id=1, source_target_pairs={{0,14},{1,15},{2,12},{3,13},{4,10},{5,11},{6,8},{7,9},{8,6},{9,7},... | collective-permute-start | bytes 294920 | tf_op jit(solution)/shard_map/ppermute | solution.py:246
  80.0 3.7 %collective-permute-start.13 = (bf16[2,48,512]{2,1,0:T(8,128)(2,1)}, bf16[2,48,512]{2,1,0:T(8,128)(2,1)S(1)}, u32[]{:S(2)}, u32[]{:S(2)}) collective-permute-start(bf16[2,48,512]{2,1,0:T(8,128)(2,1)} %get-tuple-element.55), channel_id=1, source_target_pairs={{0,1},{1,0},{2,3},{3,2},{4,5},{5,4},{6,7},{7,6},{8,9},{9,8},{10,11... | collective-permute-start | bytes 294920 | tf_op jit(solution)/shard_map/ppermute | solution.py:246
  80.0 7.6 %collective-permute-start.14 = (bf16[2,48,512]{2,1,0:T(8,128)(2,1)}, bf16[2,48,512]{2,1,0:T(8,128)(2,1)S(1)}, u32[]{:S(2)}, u32[]{:S(2)}) collective-permute-start(bf16[2,48,512]{2,1,0:T(8,128)(2,1)} %get-tuple-element.56), channel_id=1, source_target_pairs={{0,15},{1,14},{2,13},{3,12},{4,11},{5,10},{6,9},{7,8},{8,7},{9,6},... | collective-permute-start | bytes 294920 | tf_op jit(solution)/shard_map/ppermute | solution.py:246
  89.2 11.6 %collective-permute-start.15 = (bf16[2,48,512]{2,1,0:T(8,128)(2,1)S(1)}, bf16[2,48,512]{2,1,0:T(8,128)(2,1)S(1)}, u32[]{:S(2)}, u32[]{:S(2)}) collective-permute-start(bf16[2,48,512]{2,1,0:T(8,128)(2,1)S(1)} %get-tuple-element.58), channel_id=1, source_target_pairs={{0,8},{1,9},{2,10},{3,11},{4,12},{5,13},{6,14},{7,15},{8,0},{9,1},... | collective-permute-start | bytes 294920 | tf_op jit(solution)/shard_map/ppermute | solution.py:246
  94.8 8.1 %collective-permute-start.16 = (bf16[2,48,512]{2,1,0:T(8,128)(2,1)S(1)}, bf16[2,48,512]{2,1,0:T(8,128)(2,1)S(1)}, u32[]{:S(2)}, u32[]{:S(2)}) collective-permute-start(bf16[2,48,512]{2,1,0:T(8,128)(2,1)S(1)} %get-tuple-element.59), channel_id=1, source_target_pairs={{0,7},{1,6},{2,5},{3,4},{4,3},{5,2},{6,1},{7,0},{8,15},{9,14},{10,... | collective-permute-start | bytes 294920 | tf_op jit(solution)/shard_map/ppermute | solution.py:246
  94.8 8.1 %collective-permute-start.17 = (bf16[2,48,512]{2,1,0:T(8,128)(2,1)S(1)}, bf16[2,48,512]{2,1,0:T(8,128)(2,1)S(1)}, u32[]{:S(2)}, u32[]{:S(2)}) collective-permute-start(bf16[2,48,512]{2,1,0:T(8,128)(2,1)S(1)} %get-tuple-element.60), channel_id=1, source_target_pairs={{0,9},{1,8},{2,11},{3,10},{4,13},{5,12},{6,15},{7,14},{8,1},{9,0},... | collective-permute-start | bytes 294920 | tf_op jit(solution)/shard_map/ppermute | solution.py:246
  96.6 10.1 %collective-permute-start.18 = (bf16[2,48,512]{2,1,0:T(8,128)(2,1)S(1)}, bf16[2,48,512]{2,1,0:T(8,128)(2,1)S(1)}, u32[]{:S(2)}, u32[]{:S(2)}) collective-permute-start(bf16[2,48,512]{2,1,0:T(8,128)(2,1)S(1)} %get-tuple-element.61), channel_id=1, source_target_pairs={{0,6},{1,7},{2,4},{3,5},{4,2},{5,3},{6,0},{7,1},{8,14},{9,15},{10,... | collective-permute-start | bytes 294920 | tf_op jit(solution)/shard_map/ppermute | solution.py:246
  97.6 11.3 %collective-permute-start.19 = (bf16[2,48,512]{2,1,0:T(8,128)(2,1)S(1)}, bf16[2,48,512]{2,1,0:T(8,128)(2,1)S(1)}, u32[]{:S(2)}, u32[]{:S(2)}) collective-permute-start(bf16[2,48,512]{2,1,0:T(8,128)(2,1)S(1)} %get-tuple-element.62), channel_id=1, source_target_pairs={{0,10},{1,11},{2,8},{3,9},{4,14},{5,15},{6,12},{7,13},{8,2},{9,3},... | collective-permute-start | bytes 294920 | tf_op jit(solution)/shard_map/ppermute | solution.py:246
  100.8 9.3 %collective-permute-start.20 = (bf16[2,48,512]{2,1,0:T(8,128)(2,1)S(1)}, bf16[2,48,512]{2,1,0:T(8,128)(2,1)S(1)}, u32[]{:S(2)}, u32[]{:S(2)}) collective-permute-start(bf16[2,48,512]{2,1,0:T(8,128)(2,1)S(1)} %get-tuple-element.63), channel_id=1, source_target_pairs={{0,5},{1,4},{2,7},{3,6},{4,1},{5,0},{6,3},{7,2},{8,13},{9,12},{10,... | collective-permute-start | bytes 294920 | tf_op jit(solution)/shard_map/ppermute | solution.py:246
  102.9 9.3 %collective-permute-start.21 = (bf16[2,48,512]{2,1,0:T(8,128)(2,1)S(1)}, bf16[2,48,512]{2,1,0:T(8,128)(2,1)S(1)}, u32[]{:S(2)}, u32[]{:S(2)}) collective-permute-start(bf16[2,48,512]{2,1,0:T(8,128)(2,1)S(1)} %get-tuple-element.64), channel_id=1, source_target_pairs={{0,11},{1,10},{2,9},{3,8},{4,15},{5,14},{6,13},{7,12},{8,3},{9,2},... | collective-permute-start | bytes 294920 | tf_op jit(solution)/shard_map/ppermute | solution.py:246
  102.9 14.8 %collective-permute-start.22 = (bf16[2,48,512]{2,1,0:T(8,128)(2,1)S(1)}, bf16[2,48,512]{2,1,0:T(8,128)(2,1)S(1)}, u32[]{:S(2)}, u32[]{:S(2)}) collective-permute-start(bf16[2,48,512]{2,1,0:T(8,128)(2,1)S(1)} %get-tuple-element.65), channel_id=1, source_target_pairs={{0,4},{1,5},{2,6},{3,7},{4,0},{5,1},{6,2},{7,3},{8,12},{9,13},{10,... | collective-permute-start | bytes 294920 | tf_op jit(solution)/shard_map/ppermute | solution.py:246
  106.6 11.1 %collective-permute-start.23 = (bf16[2,48,512]{2,1,0:T(8,128)(2,1)S(1)}, bf16[2,48,512]{2,1,0:T(8,128)(2,1)S(1)}, u32[]{:S(2)}, u32[]{:S(2)}) collective-permute-start(bf16[2,48,512]{2,1,0:T(8,128)(2,1)S(1)} %get-tuple-element.66), channel_id=1, source_target_pairs={{0,12},{1,13},{2,14},{3,15},{4,8},{5,9},{6,10},{7,11},{8,4},{9,5},... | collective-permute-start | bytes 294920 | tf_op jit(solution)/shard_map/ppermute | solution.py:246
  108.9 8.9 %collective-permute-start.24 = (bf16[2,48,512]{2,1,0:T(8,128)(2,1)S(1)}, bf16[2,48,512]{2,1,0:T(8,128)(2,1)S(1)}, u32[]{:S(2)}, u32[]{:S(2)}) collective-permute-start(bf16[2,48,512]{2,1,0:T(8,128)(2,1)S(1)} %get-tuple-element.67), channel_id=1, source_target_pairs={{0,3},{1,2},{2,1},{3,0},{4,7},{5,6},{6,5},{7,4},{8,11},{9,10},{10,... | collective-permute-start | bytes 294920 | tf_op jit(solution)/shard_map/ppermute | solution.py:246
  110.1 12.4 %collective-permute-start.25 = (bf16[2,48,512]{2,1,0:T(8,128)(2,1)S(1)}, bf16[2,48,512]{2,1,0:T(8,128)(2,1)S(1)}, u32[]{:S(2)}, u32[]{:S(2)}) collective-permute-start(bf16[2,48,512]{2,1,0:T(8,128)(2,1)S(1)} %get-tuple-element.68), channel_id=1, source_target_pairs={{0,13},{1,12},{2,15},{3,14},{4,9},{5,8},{6,11},{7,10},{8,5},{9,4},... | collective-permute-start | bytes 294920 | tf_op jit(solution)/shard_map/ppermute | solution.py:246
  112.2 10.4 %collective-permute-start.26 = (bf16[2,48,512]{2,1,0:T(8,128)(2,1)S(1)}, bf16[2,48,512]{2,1,0:T(8,128)(2,1)S(1)}, u32[]{:S(2)}, u32[]{:S(2)}) collective-permute-start(bf16[2,48,512]{2,1,0:T(8,128)(2,1)S(1)} %get-tuple-element.69), channel_id=1, source_target_pairs={{0,2},{1,3},{2,0},{3,1},{4,6},{5,7},{6,4},{7,5},{8,10},{9,11},{10,... | collective-permute-start | bytes 294920 | tf_op jit(solution)/shard_map/ppermute | solution.py:246
  117.7 8.3 %collective-permute-start.27 = (bf16[2,48,512]{2,1,0:T(8,128)(2,1)S(1)}, bf16[2,48,512]{2,1,0:T(8,128)(2,1)S(1)}, u32[]{:S(2)}, u32[]{:S(2)}) collective-permute-start(bf16[2,48,512]{2,1,0:T(8,128)(2,1)S(1)} %get-tuple-element.70), channel_id=1, source_target_pairs={{0,14},{1,15},{2,12},{3,13},{4,10},{5,11},{6,8},{7,9},{8,6},{9,7},... | collective-permute-start | bytes 294920 | tf_op jit(solution)/shard_map/ppermute | solution.py:246
  117.7 8.3 %collective-permute-start.28 = (bf16[2,48,512]{2,1,0:T(8,128)(2,1)S(1)}, bf16[2,48,512]{2,1,0:T(8,128)(2,1)S(1)}, u32[]{:S(2)}, u32[]{:S(2)}) collective-permute-start(bf16[2,48,512]{2,1,0:T(8,128)(2,1)S(1)} %get-tuple-element.71), channel_id=1, source_target_pairs={{0,1},{1,0},{2,3},{3,2},{4,5},{5,4},{6,7},{7,6},{8,9},{9,8},{10,11... | collective-permute-start | bytes 294920 | tf_op jit(solution)/shard_map/ppermute | solution.py:246
  117.8 8.3 %collective-permute-start.29 = (bf16[2,48,512]{2,1,0:T(8,128)(2,1)S(1)}, bf16[2,48,512]{2,1,0:T(8,128)(2,1)S(1)}, u32[]{:S(2)}, u32[]{:S(2)}) collective-permute-start(bf16[2,48,512]{2,1,0:T(8,128)(2,1)S(1)} %get-tuple-element.72), channel_id=1, source_target_pairs={{0,15},{1,14},{2,13},{3,12},{4,11},{5,10},{6,9},{7,8},{8,7},{9,6},... | collective-permute-start | bytes 294920 | tf_op jit(solution)/shard_map/ppermute | solution.py:246
  (3 other events, 61.6 us)

commit v3 on v2

--- a/solution.py
+++ b/solution.py
@@ -23,24 +23,136 @@
 MIB = 1 << 20
 
 
-def fetched(refs, held, sem):
-    copies = [pltpu.make_async_copy(ref, room, sem.at[n]) for n, (ref, room) in enumerate(zip(refs, held))]
+def plane_of(groups):
+    return 1 << ((groups.bit_length() - 1) // 2)
+
+
+def line_order(line):
+    return [0] + sorted(range(1, line), key=lambda k: (k.bit_length() < line.bit_length() - 1, k))
+
+
+def along_line(pieces, groups):
+    plane = plane_of(groups)
+    return [
+        lax.ppermute(piece, "expert", [(i, i ^ (k * plane)) for i in range(groups)]) if k else piece
+        for k, piece in zip(line_order(groups // plane), pieces)
+    ]
+
+
+def in_plane(stack, groups):
+    stacks = [stack]
+    for bit in reversed(range(plane_of(groups).bit_length() - 1)):
+        stacks += [lax.ppermute(held, "expert", [(i, i ^ (1 << bit)) for i in range(groups)]) for held in stacks]
+    return stacks
+
+
+def plane_offsets(groups):
+    offsets = [0]
+    for bit in reversed(range(plane_of(groups).bit_length() - 1)):
+        offsets += [offset ^ (1 << bit) for offset in offsets]
+    return offsets
+
+
+def block_at(k, rows):
+    return pl.ds(pl.multiple_of(k * rows, rows), rows)
+
+
+def split_kernel(plane, me_ref, moment_ref, weight_ref, *refs):
+    pieces, sem = refs[:-1], refs[-1]
+    line = len(pieces) // 2
+    place = me_ref[0] // plane
+    copies = [
+        pltpu.make_async_copy(
+            source.at[0, block_at(place ^ k, pieces[0].shape[0])], pieces[lead * line + n], sem.at[lead * line + n]
+        )
+        for lead, source in enumerate((moment_ref, weight_ref))
+        for n, k in enumerate(line_order(line))
+    ]
     for copy in copies:
         copy.start()
     for copy in copies:
         copy.wait()
 
 
-def rooms(arrays):
-    return [pltpu.VMEM(a.shape, a.dtype) for a in arrays] + [pltpu.SemaphoreType.DMA((len(arrays),))]
-
-
-def chunk_at(ref, lead, k, rows, columns):
-    return ref.at[
-        lead,
-        pl.ds(pl.multiple_of((k // 2) * rows, rows), rows),
-        pl.ds(pl.multiple_of((k % 2) * columns, columns), columns),
-    ]
+def split(me, moment, weight, groups):
+    _, ff, d = weight.shape
+    plane = plane_of(groups)
+    line = groups // plane
+    piece = jax.ShapeDtypeStruct((ff // line, d), BF16)
+    pieces = pl.pallas_call(
+        functools.partial(split_kernel, plane),
+        out_shape=(piece,) * (2 * line),
+        in_specs=[SMEM, HBM, HBM],
+        out_specs=(VMEM,) * (2 * line),
+        scratch_shapes=[pltpu.SemaphoreType.DMA((2 * line,))],
+        compiler_params=pltpu.CompilerParams(vmem_limit_bytes=60 * MIB),
+        cost_estimate=pl.CostEstimate(flops=0, bytes_accessed=8 * ff * d, transcendentals=0),
+        name="split",
+    )(me, moment, weight)
+    return pieces[:line], pieces[line:]
+
+
+def stack_kernel(order, *refs):
+    stack_ref = refs[-1]
+    for k, piece in zip(order, refs):
+        stack_ref[k] = piece[...]
+
+
+def stacked(pieces):
+    line = len(pieces)
+    shape = (line,) + pieces[0].shape
+    return pl.pallas_call(
+        functools.partial(stack_kernel, line_order(line)),
+        out_shape=jax.ShapeDtypeStruct(shape, BF16),
+        in_specs=[VMEM] * line,
+        out_specs=VMEM,
+        compiler_params=pltpu.CompilerParams(vmem_limit_bytes=32 * MIB),
+        cost_estimate=pl.CostEstimate(flops=0, bytes_accessed=4 * line * pieces[0].size, transcendentals=0),
+        name="stack",
+    )(*pieces)
+
+
+def pick_kernel(groups, me_ref, perm_ref, *refs):
+    plane = plane_of(groups)
+    line = groups // plane
+    stacks, targets = refs[:plane], refs[plane:]
+    me = me_ref[0]
+    for k, target in zip(line_order(line), targets):
+        expert = 0
+        for e in range(groups):
+            expert = jnp.where(perm_ref[e] == me ^ (k * plane), e, expert)
+        offset, place = (expert ^ me) % plane, (expert ^ me) // plane
+        for stack, held in zip(plane_offsets(groups), stacks):
+
+            @pl.when(offset == stack)
+            def _():
+                target[...] = held[place]
+
+
+def pick(me, perm, stacks, groups):
+    line = stacks[0].shape[0]
+    piece = jax.ShapeDtypeStruct(stacks[0].shape[1:], BF16)
+    return pl.pallas_call(
+        functools.partial(pick_kernel, groups),
+        out_shape=(piece,) * line,
+        in_specs=[SMEM, SMEM] + [VMEM] * len(stacks),
+        out_specs=(VMEM,) * line,
+        compiler_params=pltpu.CompilerParams(vmem_limit_bytes=32 * MIB),
+        cost_estimate=pl.CostEstimate(flops=0, bytes_accessed=4 * stacks[0].size, transcendentals=0),
+        name="pick",
+    )(me, perm, *stacks)
+
+
+def relocated(me, perm, pieces, groups):
+    stacks = in_plane(stacked(along_line(pieces, groups)), groups)
+    return along_line(pick(me, perm, stacks, groups), groups)
+
+
+def assembled(plane, me_ref, pieces, held):
+    rows = pieces[0].shape[0]
+    for k, piece in zip(line_order(len(pieces)), pieces):
+        held[block_at((me_ref[0] // plane) ^ k, rows)] = piece[...]
+    return held[...].astype(F32)
 
 
 def slot_rows(route, live, groups, capacity, perm_ref):
@@ -66,19 +178,26 @@
 
 def pack_kernel(groups, live_ref, perm_ref, *refs):
     sources, (packed_ref, slot_ref), held, sem = refs[:5], refs[5:7], refs[7:12], refs[12]
-    fetched(sources, held, sem)
     route_ref, fwd_route_ref, hidden_ref, out_ref, fwd_ref = held
+    copies = [pltpu.make_async_copy(ref, room, sem.at[n]) for n, (ref, room) in enumerate(zip(sources, held))]
+    for copy in copies:
+        copy.start()
     rows, ff = hidden_ref.shape
     d = out_ref.shape[1]
-    capacity = packed_ref.shape[0] // groups
+    slots = packed_ref.shape[0]
+    capacity = slots // groups
     place = lax.broadcasted_iota(jnp.int32, (1, rows), 1)
-    slot = slot_rows(route_ref[...], place < live_ref[0], groups, capacity, perm_ref)
-    selector = selector_of(slot, groups * capacity)
-    packed_ref[:, :ff] = jnp.dot(selector, hidden_ref[...], preferred_element_type=F32).astype(BF16)
-    packed_ref[:, ff : ff + d] = jnp.dot(selector, out_ref[...], preferred_element_type=F32).astype(BF16)
+    copies[0].wait()
+    selector = selector_of(slot_rows(route_ref[...], place < live_ref[0], groups, capacity, perm_ref), slots)
+    copies[1].wait()
     fwd_slot = slot_rows(fwd_route_ref[...], place >= 0, groups, capacity, perm_ref)
     slot_ref[...] = fwd_slot
-    fwd_selector = selector_of(fwd_slot, groups * capacity)
+    fwd_selector = selector_of(fwd_slot, slots)
+    copies[2].wait()
+    packed_ref[:, :ff] = jnp.dot(selector, hidden_ref[...], preferred_element_type=F32).astype(BF16)
+    copies[3].wait()
+    packed_ref[:, ff : ff + d] = jnp.dot(selector, out_ref[...], preferred_element_type=F32).astype(BF16)
+    copies[4].wait()
     packed_ref[:, ff + d :] = jnp.dot(fwd_selector, fwd_ref[...], preferred_element_type=F32).astype(BF16)
 
 
@@ -94,7 +213,7 @@
         ),
         in_specs=[SMEM, SMEM] + [HBM] * 5,
         out_specs=(VMEM, VMEM),
-        scratch_shapes=rooms(sources),
+        scratch_shapes=[pltpu.VMEM(a.shape, a.dtype) for a in sources] + [pltpu.SemaphoreType.DMA((len(sources),))],
         compiler_params=pltpu.CompilerParams(vmem_limit_bytes=60 * MIB),
         cost_estimate=pl.CostEstimate(
             flops=2 * groups * capacity * rows * width, bytes_accessed=6 * rows * width, transcendentals=0
@@ -103,67 +222,13 @@
     )(live_rows, perm, *sources)
 
 
-def split_kernel(me_ref, moment_ref, weight_ref, *refs):
-    pieces, held, sem = refs[:-3], refs[-3:-1], refs[-1]
-    fetched((moment_ref, weight_ref), held, sem)
-    for s, piece in zip(mixed_order(len(pieces)), pieces):
-        rows, columns = piece.shape[1:]
-        for lead, source in enumerate(held):
-            piece[lead] = chunk_at(source, 0, me_ref[0] ^ s, rows, columns)[...]
-
-
-def split(me, moment, weight, groups):
-    _, ff, d = weight.shape
-    piece = jax.ShapeDtypeStruct((2, ff // (groups // 2), d // 2), BF16)
-    return pl.pallas_call(
-        split_kernel,
-        out_shape=(piece,) * groups,
-        in_specs=[SMEM, HBM, HBM],
-        out_specs=(VMEM,) * groups,
-        scratch_shapes=rooms((moment, weight)),
-        compiler_params=pltpu.CompilerParams(vmem_limit_bytes=60 * MIB),
-        cost_estimate=pl.CostEstimate(flops=0, bytes_accessed=8 * ff * d, transcendentals=0),
-        name="split",
-    )(me, moment, weight)
-
-
-def reorder_kernel(me_ref, perm_ref, *refs):
-    groups = (len(refs) - 1) // 2
-    sources, targets, held = refs[:groups], refs[groups : 2 * groups], refs[-1]
-    me, order = me_ref[0], mixed_order(groups)
-    for s, source in zip(order, sources):
-        held[me ^ perm_ref[me ^ s]] = source[...]
-    for s, target in zip(order, targets):
-        target[...] = held[s]
-
-
-def reorder(me, perm, pieces):
-    groups = len(pieces)
-    piece = jax.ShapeDtypeStruct(pieces[0].shape, BF16)
-    return pl.pallas_call(
-        reorder_kernel,
-        out_shape=(piece,) * groups,
-        in_specs=[SMEM, SMEM] + [VMEM] * groups,
-        out_specs=(VMEM,) * groups,
-        scratch_shapes=[pltpu.VMEM((groups,) + pieces[0].shape, BF16)],
-        compiler_params=pltpu.CompilerParams(vmem_limit_bytes=32 * MIB),
-        cost_estimate=pl.CostEstimate(flops=0, bytes_accessed=4 * groups * pieces[0].size, transcendentals=0),
-        name="reorder",
-    )(me, perm, *pieces)
-
-
-def update_kernel(groups, me_ref, packed_ref, *refs):
-    pieces = refs[:groups]
-    weight_new_ref, moment_new_ref, produced_ref, held = refs[groups:]
-    _, ff, d = held.shape
-    for s, piece in zip(mixed_order(groups), pieces):
-        rows, columns = piece.shape[1:]
-        for lead in range(2):
-            chunk_at(held, lead, me_ref[0] ^ s, rows, columns)[...] = piece[lead]
+def orthogonal_kernel(plane, me_ref, packed_ref, *refs):
+    pieces, (moment_new_ref, ortho_ref, held) = refs[:-3], refs[-3:]
+    ff, d = ortho_ref.shape
     grad = lax.dot_general(
         packed_ref[:, :ff], packed_ref[:, ff : ff + d], (((0,), (0,)), ((), ())), preferred_element_type=F32
     )
-    moment_new = (moment_decay * held[0].astype(F32) + grad).astype(BF16)
+    moment_new = (moment_decay * assembled(plane, me_ref, pieces, held) + grad).astype(BF16)
     moment_new_ref[...] = moment_new
     moment_f = moment_new.astype(F32)
     frobenius = jnp.sqrt(jnp.sum(moment_f * moment_f))
@@ -177,29 +242,54 @@
         current = (
             linear_term * current.astype(F32) + jnp.dot(poly, current, preferred_element_type=F32)
         ).astype(BF16)
-    weight_new = (held[1].astype(F32) - step_scale * current.astype(F32)).astype(BF16)
+    ortho_ref[...] = current
+
+
+def orthogonal(me, packed, pieces, groups):
+    line = len(pieces)
+    rows, d = pieces[0].shape
+    ff = rows * line
+    shape = jax.ShapeDtypeStruct((ff, d), BF16)
+    return pl.pallas_call(
+        functools.partial(orthogonal_kernel, plane_of(groups)),
+        out_shape=(shape, shape),
+        in_specs=[SMEM] + [VMEM] * (1 + line),
+        out_specs=(VMEM, VMEM),
+        scratch_shapes=[pltpu.VMEM((ff, d), BF16)],
+        compiler_params=pltpu.CompilerParams(vmem_limit_bytes=40 * MIB),
+        cost_estimate=pl.CostEstimate(
+            flops=2 * ff * d * packed.shape[0] + 8 * ff * ff * d + 4 * ff**3,
+            bytes_accessed=6 * ff * d + 2 * packed.size,
+            transcendentals=1,
+        ),
+        name="orthogonal",
+    )(me, packed, *pieces)
+
+
+def produce_kernel(plane, me_ref, packed_ref, ortho_ref, *refs):
+    pieces, (weight_new_ref, produced_ref, held) = refs[:-3], refs[-3:]
+    ff, d = ortho_ref.shape
+    weight = assembled(plane, me_ref, pieces, held)
+    weight_new = (weight - step_scale * ortho_ref[...].astype(F32)).astype(BF16)
     weight_new_ref[...] = weight_new
     produced_ref[...] = jnp.dot(packed_ref[:, ff + d :], weight_new, preferred_element_type=F32).astype(BF16)
 
 
-def update(me, packed, pieces, ff, d):
-    groups = len(pieces)
+def produce(me, packed, ortho, pieces, groups):
     slots = packed.shape[0]
-    shape = jax.ShapeDtypeStruct((ff, d), BF16)
+    ff, d = ortho.shape
     return pl.pallas_call(
-        functools.partial(update_kernel, groups),
-        out_shape=(shape, shape, jax.ShapeDtypeStruct((slots, d), BF16)),
-        in_specs=[SMEM] + [VMEM] * (1 + groups),
-        out_specs=(VMEM,) * 3,
-        scratch_shapes=[pltpu.VMEM((2, ff, d), BF16)],
-        compiler_params=pltpu.CompilerParams(vmem_limit_bytes=48 * MIB),
+        functools.partial(produce_kernel, plane_of(groups)),
+        out_shape=(jax.ShapeDtypeStruct((ff, d), BF16), jax.ShapeDtypeStruct((slots, d), BF16)),
+        in_specs=[SMEM] + [VMEM] * (2 + len(pieces)),
+        out_specs=(VMEM, VMEM),
+        scratch_shapes=[pltpu.VMEM((ff, d), BF16)],
+        compiler_params=pltpu.CompilerParams(vmem_limit_bytes=40 * MIB),
         cost_estimate=pl.CostEstimate(
-            flops=4 * ff * d * slots + 8 * ff * ff * d + 4 * ff**3,
-            bytes_accessed=8 * ff * d + 2 * packed.size + 2 * slots * d,
-            transcendentals=1,
+            flops=2 * slots * ff * d, bytes_accessed=8 * ff * d + 2 * slots * (ff + d), transcendentals=0
         ),
-        name="update",
-    )(me, packed, *pieces)
+        name="produce",
+    )(me, packed, ortho, *pieces)
 
 
 def finish_kernel(slot_ref, gate_ref, returned_ref, out_ref):
@@ -234,33 +324,23 @@
     return lax.all_to_all(array, "expert", split_axis=0, concat_axis=0, tiled=True)
 
 
-def mixed_order(groups):
-    far, near = list(range(groups // 2, groups)), list(range(groups // 2 - 1, 0, -1))
-    return [0] + [s for pair in zip(far, near + [None]) for s in pair if s is not None]
-
-
-def swap(pieces):
-    groups = len(pieces)
-    order = mixed_order(groups)
-    return [pieces[0]] + [
-        lax.ppermute(piece, "expert", [(i, i ^ s) for i in range(groups)]) for s, piece in zip(order[1:], pieces[1:])
-    ]
-
-
-def partner_plan(
+def relocation_plan(
     grad_hidden, grad_out, grad_route, live_rows, w_down, w_moment, perm, fwd_hidden, fwd_route, fwd_gate
 ):
     groups = lax.axis_size("expert")
     me = lax.axis_index("expert").astype(jnp.int32).reshape(1)
     capacity = max(4, 2 * grad_hidden.shape[0] // groups)
-    ff, d = w_down.shape[1:]
-    spread = swap(split(me, w_moment, w_down, groups))
+    d = w_down.shape[2]
+    moment_pieces, weight_pieces = split(me, w_moment, w_down, groups)
+    live_rows, moment_pieces = lax.optimization_barrier((live_rows, moment_pieces))
     packed, fwd_slot = pack_rows(
         live_rows, perm, grad_route, fwd_route, grad_hidden, grad_out, fwd_hidden, groups, capacity
     )
     received = exchange(packed.reshape(groups, capacity, -1)).reshape(groups * capacity, -1)
-    placed = swap(reorder(me, perm, spread))
-    weight_new, moment_new, produced = update(me, received, placed, ff, d)
+    moment_placed = relocated(me, perm, moment_pieces, groups)
+    weight_placed = relocated(me, perm, weight_pieces, groups)
+    moment_new, ortho = orthogonal(me, received, moment_placed, groups)
+    weight_new, produced = produce(me, received, ortho, weight_placed, groups)
     returned = exchange(produced.reshape(groups, capacity, d)).reshape(groups * capacity, d)
     return weight_new[None], moment_new[None], finish(fwd_slot, fwd_gate, returned)
 
@@ -416,7 +496,7 @@
 
     def per_device(*args):
         few = groups & (groups - 1) == 0 and groups <= 2 * args[0].shape[0] // groups
-        return (partner_plan if few else routed_plan)(*args)
+        return (relocation_plan if few else routed_plan)(*args)
 
     return jax.shard_map(
         per_device, mesh=mesh, in_specs=in_specs, out_specs=out_specs, check_vma=False

time: 164 us -> 187 us (1.14)
  waiting for transfers between devices: 67.4 us -> 104 us
  starting transfers between devices: 48.8 us -> 31.4 us
  blocking collectives: 30.4 us -> 32.6 us
    ppermute x30 -> x18, waiting for transfers between devices: 67.4 us -> 104 us  [the longest x12 80.5 us: along_line(): lax.ppermute(piece, 'expert', [(i, i ^ k * plane) for i in range(groups)])]
    ppermute x30 -> x18, starting transfers between devices: 41.4 us -> 24 us  [the longest x12 20.3 us: along_line(): lax.ppermute(piece, 'expert', [(i, i ^ k * plane) for i in range(groups)])]
    all_to_all x1, blocking collectives: 30.4 us -> 32.6 us  [exchange(): lax.all_to_all(array, 'expert', split_axis=0, concat_axis=0, tiled=True)]
    pallas_call x3 -> x7, Pallas kernels: 8.61 us -> 10.2 us  [the longest x1 3.62 us: orthogonal(): pl.pallas_call(functools.partial(orthogonal_kernel, plane_of(groups)), ou...]
  transfers between devices with their start and end apart: 31 -> 19, of which waited for: 13 -> 8; matrix products, arithmetic and copies ran while one was open for 0% -> 0% of each run, Pallas kernels for 2% -> 5%
where the time goes in v3:
time: 187 us; the launch traced here: 186 us
  waiting for transfers between devices  104 us (56%)
  blocking collectives  32.6 us (17%)
  starting transfers between devices  31.4 us (17%)
  Pallas kernels  15.7 us (8%)
    ppermute x12, waiting for transfers between devices, along_line(): lax.ppermute(piece, 'expert', [(i, i ^ k * plane) for i in range(groups)])  80.5 us
    all_to_all x1, blocking collectives, exchange(): lax.all_to_all(array, 'expert', split_axis=0, concat_axis=0, tiled=True)  32.6 us
    ppermute x6, waiting for transfers between devices, in_plane(): lax.ppermute(held, 'expert', [(i, i ^ 1 << bit) for i in range(groups)])  23.1 us
    ppermute x12, starting transfers between devices, along_line(): lax.ppermute(piece, 'expert', [(i, i ^ k * plane) for i in range(groups)])  20.3 us
    all_to_all x1, starting transfers between devices, exchange(): lax.all_to_all(array, 'expert', split_axis=0, concat_axis=0, tiled=True)  7.38 us
    pallas_call x1, Pallas kernels, pack_rows(): pl.pallas_call(functools.partial(pack_kernel, groups), out_shape=(jax.Sha...  4.17 us
  transfers between devices with their start and end apart: 19, of which 8 were waited for; matrix products, arithmetic and copies ran while one was open for 0% of the time, Pallas kernels for 5%

profile of v3, /device:TPU:0, one launch (start us, length us, event | category | flops | bytes accessed | tf_op | source)
XLA Modules:
  0.0 186.5 jit_solution(14676794803160316880)
XLA Ops:
  1.3 4.2 %pack_rows.1 = (bf16[512,1792]{1,0:T(8,128)(2,1)}, s32[1,256]{1,0:T(1,128)}) custom-call(s32[1]{0:T(128)S(6)} %copy.13.live_ref, s32[16]{0:T(128)} %perm_ref.5, s32[1,256]{1,0:T(1,128)} %bitcast.17, s32[1,256]{1,0:T(1,128)} %bitcast.18, bf16[256,384]{1,0:T(8,128)(2,1)} %refs_2_.1, bf16[256,1024]{1,0:T(8,128)(2,1)} %refs_3_.1, bf16[256,384]{1,0:T(8,128)(2,1)} %refs_4_.1), custom_call_target="tpu_custom_call" | custom-call | flops 469762048 | bytes 2752512 | tf_op jit(solution)/shard_map/pack_rows/pallas_call | solution.py:208
  5.5 7.4 %all-to-all-start = ((bf16[16,32,1792]{2,1,0:T(8,128)(2,1)}), bf16[16,32,1792]{2,1,0:T(8,128)(2,1)S(1)}, u32[]{:S(2)}, u32[]{:S(2)}) async-start(bf16[16,32,1792]{2,1,0:T(8,128)(2,1)} %bitcast.15), calls=%async_computation | async-start | bytes 3670016 | tf_op jit(solution)/shard_map/all_to_all | solution.py:324
  12.8 2.7 %split.1 = (bf16[96,1024]{1,0:T(8,128)(2,1)}, bf16[96,1024]{1,0:T(8,128)(2,1)}, bf16[96,1024]{1,0:T(8,128)(2,1)}, bf16[96,1024]{1,0:T(8,128)(2,1)}, bf16[96,1024...) custom-call(s32[1]{0:T(128)} %bitcast.me_ref, ...), custom_call_target="tpu_custom_call" | custom-call | bytes 3145728 | tf_op jit(solution)/shard_map/split/pallas_call | solution.py:82
  15.5 2.9 %collective-permute-start = (bf16[96,1024]{1,0:T(8,128)(2,1)}, bf16[96,1024]{1,0:T(8,128)(2,1)S(1)}, u32[]{:S(2)}, u32[]{:S(2)}) collective-permute-start(bf16[96,1024]{1,0:T(8,128)(2,1)} %get-tuple-element.37), channel_id=1, source_target_pairs={{0,8},{1,9},{2,10},{3,11},{4,12},{5,13},{6,14},{7,15},{8,0},{9,1},... | collective-permute-start | bytes 589832 | tf_op jit(solution)/shard_map/ppermute | solution.py:37
  18.4 1.5 collective-permute-start.1
  19.9 2.9 %collective-permute-start.9 = (bf16[96,1024]{1,0:T(8,128)(2,1)}, bf16[96,1024]{1,0:T(8,128)(2,1)S(1)}, u32[]{:S(2)}, u32[]{:S(2)}) collective-permute-start(bf16[96,1024]{1,0:T(8,128)(2,1)} %get-tuple-element.46), channel_id=1, source_target_pairs={{0,8},{1,9},{2,10},{3,11},{4,12},{5,13},{6,14},{7,15},{8,0},{9,1},... | collective-permute-start | bytes 589832 | tf_op jit(solution)/shard_map/ppermute | solution.py:37
  22.8 1.5 collective-permute-start.10
  24.3 53.6 %collective-permute-done.refs_1_ = bf16[96,1024]{1,0:T(8,128)(2,1)S(1)} collective-permute-done((bf16[96,1024]{1,0:T(8,128)(2,1)}, bf16[96,1024]{1,0:T(8,128)(2,1)S(1)}, u32[]{:S(2)}, u32[]{:S(2)}) %collective-permute-start) | collective-permute-done | bytes 196640 | tf_op jit(solution)/shard_map/ppermute | solution.py:37
  77.8 0.9 copy-done.1
  78.8 0.1 stack.2.refs_0_
  78.8 1.6 collective-permute-start.3
  80.4 5.9 %collective-permute-done.9.refs_1_ = bf16[96,1024]{1,0:T(8,128)(2,1)S(1)} collective-permute-done((bf16[96,1024]{1,0:T(8,128)(2,1)}, bf16[96,1024]{1,0:T(8,128)(2,1)S(1)}, u32[]{:S(2)}, u32[]{:S(2)}) %collective-permute-start.9) | collective-permute-done | bytes 196640 | tf_op jit(solution)/shard_map/ppermute | solution.py:37
  86.3 1.9 %collective-permute-done.11.refs_3_ = bf16[96,1024]{1,0:T(8,128)(2,1)S(1)} collective-permute-done((bf16[96,1024]{1,0:T(8,128)(2,1)}, bf16[96,1024]{1,0:T(8,128)(2,1)S(1)}, u32[]{:S(2)}, u32[]{:S(2)}) %collective-permute-start.11) | collective-permute-done | bytes 196640 | tf_op jit(solution)/shard_map/ppermute | solution.py:37
  88.2 0.9 copy-done
  89.1 0.1 stack.3.refs_0_
  89.2 1.6 collective-permute-start.12
  90.8 8.6 %collective-permute-done.3.refs_1_ = bf16[4,96,1024]{2,1,0:T(8,128)(2,1)S(1)} collective-permute-done((bf16[4,96,1024]{2,1,0:T(8,128)(2,1)S(1)}, bf16[4,96,1024]{2,1,0:T(8,128)(2,1)S(1)}, u32[]{:S(2)}, u32[]{:S(2)}) %collective-permute-start.3) | collective-permute-done | bytes 786464 | tf_op jit(solution)/shard_map/ppermute | solution.py:45
  99.4 0.5 collective-permute-start.13
  99.9 14.5 %collective-permute-done.12.refs_1_ = bf16[4,96,1024]{2,1,0:T(8,128)(2,1)S(1)} collective-permute-done((bf16[4,96,1024]{2,1,0:T(8,128)(2,1)S(1)}, bf16[4,96,1024]{2,1,0:T(8,128)(2,1)S(1)}, u32[]{:S(2)}, u32[]{:S(2)}) %collective-permute-start.12) | collective-permute-done | bytes 786464 | tf_op jit(solution)/shard_map/ppermute | solution.py:45
  114.4 0.7 pick.2
  115.1 4.8 %collective-permute-start.6 = (bf16[96,1024]{1,0:T(8,128)(2,1)S(1)}, bf16[96,1024]{1,0:T(8,128)(2,1)S(1)}, u32[]{:S(2)}, u32[]{:S(2)}) collective-permute-start(bf16[96,1024]{1,0:T(8,128)(2,1)S(1)} %get-tuple-element.41), channel_id=1, source_target_pairs={{0,8},{1,9},{2,10},{3,11},{4,12},{5,13},{6,14},{7,15},{8,0},{9,1},... | collective-permute-start | bytes 589832 | tf_op jit(solution)/shard_map/ppermute | solution.py:37
  119.9 2.4 %collective-permute-start.7 = (bf16[96,1024]{1,0:T(8,128)(2,1)S(1)}, bf16[96,1024]{1,0:T(8,128)(2,1)S(1)}, u32[]{:S(2)}, u32[]{:S(2)}) collective-permute-start(bf16[96,1024]{1,0:T(8,128)(2,1)S(1)} %get-tuple-element.42), channel_id=1, source_target_pairs={{0,12},{1,13},{2,14},{3,15},{4,8},{5,9},{6,10},{7,11},{8,4},{9,5},... | collective-permute-start | bytes 589832 | tf_op jit(solution)/shard_map/ppermute | solution.py:37
  122.3 1.5 pick.3
  123.9 2.0 %collective-permute-start.15 = (bf16[96,1024]{1,0:T(8,128)(2,1)}, bf16[96,1024]{1,0:T(8,128)(2,1)S(1)}, u32[]{:S(2)}, u32[]{:S(2)}) collective-permute-start(bf16[96,1024]{1,0:T(8,128)(2,1)} %get-tuple-element.50), channel_id=1, source_target_pairs={{0,8},{1,9},{2,10},{3,11},{4,12},{5,13},{6,14},{7,15},{8,0},{9,1},... | collective-permute-start | bytes 589832 | tf_op jit(solution)/shard_map/ppermute | solution.py:37
  125.9 2.4 %collective-permute-start.16 = (bf16[96,1024]{1,0:T(8,128)(2,1)}, bf16[96,1024]{1,0:T(8,128)(2,1)S(1)}, u32[]{:S(2)}, u32[]{:S(2)}) collective-permute-start(bf16[96,1024]{1,0:T(8,128)(2,1)} %get-tuple-element.51), channel_id=1, source_target_pairs={{0,12},{1,13},{2,14},{3,15},{4,8},{5,9},{6,10},{7,11},{8,4},{9,5},... | collective-permute-start | bytes 589832 | tf_op jit(solution)/shard_map/ppermute | solution.py:37
  128.3 5.9 %collective-permute-done.6.refs_1_ = bf16[96,1024]{1,0:T(8,128)(2,1)S(1)} collective-permute-done((bf16[96,1024]{1,0:T(8,128)(2,1)S(1)}, bf16[96,1024]{1,0:T(8,128)(2,1)S(1)}, u32[]{:S(2)}, u32[]{:S(2)}) %collective-permute-start.6) | collective-permute-done | bytes 196640 | tf_op jit(solution)/shard_map/ppermute | solution.py:37
  134.2 1.1 collective-permute-done.8.refs_3_
  135.3 3.6 %orthogonal.1 = (bf16[384,1024]{1,0:T(8,128)(2,1)}, bf16[384,1024]{1,0:T(8,128)(2,1)S(1)}) custom-call(s32[1]{0:T(128)} %bitcast.me_ref, bf16[512,1792]{1,0:T(8,128)(2,1)S(1)} %bitcast.10, bf16[96,1024]{1,0:T(8,128)(2,1)S(1)} %get-tuple-element.40.refs_0_, bf16[96,1024]{1,0:T(8,128)(2,1)S(1)} %collective-permute-done.6.refs_1_, ...), custom_call_target="tpu_custom_call" | custom-call | flops 1837105152 | bytes 4194304 | tf_op jit(solution)/shard_map/orthogonal/pallas_call | solution.py:253
  138.9 12.1 %collective-permute-done.15.refs_1_ = bf16[96,1024]{1,0:T(8,128)(2,1)S(1)} collective-permute-done((bf16[96,1024]{1,0:T(8,128)(2,1)}, bf16[96,1024]{1,0:T(8,128)(2,1)S(1)}, u32[]{:S(2)}, u32[]{:S(2)}) %collective-permute-start.15) | collective-permute-done | bytes 196640 | tf_op jit(solution)/shard_map/ppermute | solution.py:37
  151.0 1.6 produce.1
  152.6 32.6 %all_to_all.10 = bf16[16,32,1024]{2,1,0:T(8,128)(2,1)S(1)} all-to-all(bf16[16,32,1024]{2,1,0:T(8,128)(2,1)S(1)} %bitcast.13), channel_id=1, replica_groups=mesh['layer'=2,'expert'=16] {'expert'}, dimensions={0} | all-to-all | bytes 2097152 | tf_op jit(solution)/shard_map/all_to_all | solution.py:324
  185.2 1.3 finish.1
  (26 shorter events, 0.1 us)
Async XLA Ops:
  5.5 129.9 %all-to-all-start = ((bf16[16,32,1792]{2,1,0:T(8,128)(2,1)}), bf16[16,32,1792]{2,1,0:T(8,128)(2,1)S(1)}, u32[]{:S(2)}, u32[]{:S(2)}) async-start(bf16[16,32,1792]{2,1,0:T(8,128)(2,1)} %bitcast.15), calls=%async_computation | async-start | bytes 3670016 | tf_op jit(solution)/shard_map/all_to_all | solution.py:324
  15.5 98.8 %copy-start.2 = (s32[16]{0:T(128)S(1)}, s32[16]{0:T(128)}, u32[]{:S(2)}) copy-start(s32[16]{0:T(128)} %perm_ref.5) | copy-start | bytes 196
  15.5 62.3 %collective-permute-start = (bf16[96,1024]{1,0:T(8,128)(2,1)}, bf16[96,1024]{1,0:T(8,128)(2,1)S(1)}, u32[]{:S(2)}, u32[]{:S(2)}) collective-permute-start(bf16[96,1024]{1,0:T(8,128)(2,1)} %get-tuple-element.37), channel_id=1, source_target_pairs={{0,8},{1,9},{2,10},{3,11},{4,12},{5,13},{6,14},{7,15},{8,0},{9,1},... | collective-permute-start | bytes 589832 | tf_op jit(solution)/shard_map/ppermute | solution.py:37
  18.4 59.4 %collective-permute-start.1 = (bf16[96,1024]{1,0:T(8,128)(2,1)}, bf16[96,1024]{1,0:T(8,128)(2,1)S(1)}, u32[]{:S(2)}, u32[]{:S(2)}) collective-permute-start(bf16[96,1024]{1,0:T(8,128)(2,1)} %get-tuple-element.38), channel_id=1, source_target_pairs={{0,12},{1,13},{2,14},{3,15},{4,8},{5,9},{6,10},{7,11},{8,4},{9,5},... | collective-permute-start | bytes 589832 | tf_op jit(solution)/shard_map/ppermute | solution.py:37
  19.9 58.0 %collective-permute-start.2 = (bf16[96,1024]{1,0:T(8,128)(2,1)}, bf16[96,1024]{1,0:T(8,128)(2,1)S(1)}, u32[]{:S(2)}, u32[]{:S(2)}) collective-permute-start(bf16[96,1024]{1,0:T(8,128)(2,1)} %get-tuple-element.39), channel_id=1, source_target_pairs={{0,4},{1,5},{2,6},{3,7},{4,0},{5,1},{6,2},{7,3},{8,12},{9,13},{10,... | collective-permute-start | bytes 589832 | tf_op jit(solution)/shard_map/ppermute | solution.py:37
  19.9 66.4 %collective-permute-start.9 = (bf16[96,1024]{1,0:T(8,128)(2,1)}, bf16[96,1024]{1,0:T(8,128)(2,1)S(1)}, u32[]{:S(2)}, u32[]{:S(2)}) collective-permute-start(bf16[96,1024]{1,0:T(8,128)(2,1)} %get-tuple-element.46), channel_id=1, source_target_pairs={{0,8},{1,9},{2,10},{3,11},{4,12},{5,13},{6,14},{7,15},{8,0},{9,1},... | collective-permute-start | bytes 589832 | tf_op jit(solution)/shard_map/ppermute | solution.py:37
  22.8 63.5 %collective-permute-start.10 = (bf16[96,1024]{1,0:T(8,128)(2,1)}, bf16[96,1024]{1,0:T(8,128)(2,1)S(1)}, u32[]{:S(2)}, u32[]{:S(2)}) collective-permute-start(bf16[96,1024]{1,0:T(8,128)(2,1)} %get-tuple-element.47), channel_id=1, source_target_pairs={{0,12},{1,13},{2,14},{3,15},{4,8},{5,9},{6,10},{7,11},{8,4},{9,5},... | collective-permute-start | bytes 589832 | tf_op jit(solution)/shard_map/ppermute | solution.py:37
  77.8 10.4 %collective-permute-start.11 = (bf16[96,1024]{1,0:T(8,128)(2,1)}, bf16[96,1024]{1,0:T(8,128)(2,1)S(1)}, u32[]{:S(2)}, u32[]{:S(2)}) collective-permute-start(bf16[96,1024]{1,0:T(8,128)(2,1)} %get-tuple-element.48), channel_id=1, source_target_pairs={{0,4},{1,5},{2,6},{3,7},{4,0},{5,1},{6,2},{7,3},{8,12},{9,13},{10,... | collective-permute-start | bytes 589832 | tf_op jit(solution)/shard_map/ppermute | solution.py:37
  77.8 0.9 copy-start.1
  78.8 20.5 %collective-permute-start.3 = (bf16[4,96,1024]{2,1,0:T(8,128)(2,1)S(1)}, bf16[4,96,1024]{2,1,0:T(8,128)(2,1)S(1)}, u32[]{:S(2)}, u32[]{:S(2)}) collective-permute-start(bf16[4,96,1024]{2,1,0:T(8,128)(2,1)S(1)} %stack.2.refs_0_), channel_id=1, source_target_pairs={{0,2},{1,3},{2,0},{3,1},{4,6},{5,7},{6,4},{7,5},{8,10},{9,11},{10,... | collective-permute-start | bytes 2359304 | tf_op jit(solution)/shard_map/ppermute | solution.py:45
  88.2 0.9 copy-start
  89.2 25.1 %collective-permute-start.12 = (bf16[4,96,1024]{2,1,0:T(8,128)(2,1)S(1)}, bf16[4,96,1024]{2,1,0:T(8,128)(2,1)S(1)}, u32[]{:S(2)}, u32[]{:S(2)}) collective-permute-start(bf16[4,96,1024]{2,1,0:T(8,128)(2,1)S(1)} %stack.3.refs_0_), channel_id=1, source_target_pairs={{0,2},{1,3},{2,0},{3,1},{4,6},{5,7},{6,4},{7,5},{8,10},{9,11},{10,... | collective-permute-start | bytes 2359304 | tf_op jit(solution)/shard_map/ppermute | solution.py:45
  90.8 23.6 %collective-permute-start.4 = (bf16[4,96,1024]{2,1,0:T(8,128)(2,1)S(1)}, bf16[4,96,1024]{2,1,0:T(8,128)(2,1)S(1)}, u32[]{:S(2)}, u32[]{:S(2)}) collective-permute-start(bf16[4,96,1024]{2,1,0:T(8,128)(2,1)S(1)} %stack.2.refs_0_), channel_id=1, source_target_pairs={{0,1},{1,0},{2,3},{3,2},{4,5},{5,4},{6,7},{7,6},{8,9},{9,8},{10,11... | collective-permute-start | bytes 2359304 | tf_op jit(solution)/shard_map/ppermute | solution.py:45
  99.4 15.0 %collective-permute-start.5 = (bf16[4,96,1024]{2,1,0:T(8,128)(2,1)S(1)}, bf16[4,96,1024]{2,1,0:T(8,128)(2,1)S(1)}, u32[]{:S(2)}, u32[]{:S(2)}) collective-permute-start(bf16[4,96,1024]{2,1,0:T(8,128)(2,1)S(1)} %collective-permute-done.3.refs_1_), channel_id=1, source_target_pairs={{0,1},{1,0},{2,3},{3,2},{4,5},{5,4},{6,7},{7,6},{8,9},{9,8},{10,11... | collective-permute-start | bytes 2359304 | tf_op jit(solution)/shard_map/ppermute | solution.py:45
  99.4 23.0 %collective-permute-start.13 = (bf16[4,96,1024]{2,1,0:T(8,128)(2,1)S(1)}, bf16[4,96,1024]{2,1,0:T(8,128)(2,1)S(1)}, u32[]{:S(2)}, u32[]{:S(2)}) collective-permute-start(bf16[4,96,1024]{2,1,0:T(8,128)(2,1)S(1)} %stack.3.refs_0_), channel_id=1, source_target_pairs={{0,1},{1,0},{2,3},{3,2},{4,5},{5,4},{6,7},{7,6},{8,9},{9,8},{10,11... | collective-permute-start | bytes 2359304 | tf_op jit(solution)/shard_map/ppermute | solution.py:45
  114.4 8.0 %collective-permute-start.14 = (bf16[4,96,1024]{2,1,0:T(8,128)(2,1)S(1)}, bf16[4,96,1024]{2,1,0:T(8,128)(2,1)S(1)}, u32[]{:S(2)}, u32[]{:S(2)}) collective-permute-start(bf16[4,96,1024]{2,1,0:T(8,128)(2,1)S(1)} %collective-permute-done.12.refs_1_), channel_id=1, source_target_pairs={{0,1},{1,0},{2,3},{3,2},{4,5},{5,4},{6,7},{7,6},{8,9},{9,8},{10,11... | collective-permute-start | bytes 2359304 | tf_op jit(solution)/shard_map/ppermute | solution.py:45
  115.1 19.0 %collective-permute-start.6 = (bf16[96,1024]{1,0:T(8,128)(2,1)S(1)}, bf16[96,1024]{1,0:T(8,128)(2,1)S(1)}, u32[]{:S(2)}, u32[]{:S(2)}) collective-permute-start(bf16[96,1024]{1,0:T(8,128)(2,1)S(1)} %get-tuple-element.41), channel_id=1, source_target_pairs={{0,8},{1,9},{2,10},{3,11},{4,12},{5,13},{6,14},{7,15},{8,0},{9,1},... | collective-permute-start | bytes 589832 | tf_op jit(solution)/shard_map/ppermute | solution.py:37
  119.9 14.2 %collective-permute-start.7 = (bf16[96,1024]{1,0:T(8,128)(2,1)S(1)}, bf16[96,1024]{1,0:T(8,128)(2,1)S(1)}, u32[]{:S(2)}, u32[]{:S(2)}) collective-permute-start(bf16[96,1024]{1,0:T(8,128)(2,1)S(1)} %get-tuple-element.42), channel_id=1, source_target_pairs={{0,12},{1,13},{2,14},{3,15},{4,8},{5,9},{6,10},{7,11},{8,4},{9,5},... | collective-permute-start | bytes 589832 | tf_op jit(solution)/shard_map/ppermute | solution.py:37
  122.3 13.0 %collective-permute-start.8 = (bf16[96,1024]{1,0:T(8,128)(2,1)S(1)}, bf16[96,1024]{1,0:T(8,128)(2,1)S(1)}, u32[]{:S(2)}, u32[]{:S(2)}) collective-permute-start(bf16[96,1024]{1,0:T(8,128)(2,1)S(1)} %get-tuple-element.43), channel_id=1, source_target_pairs={{0,4},{1,5},{2,6},{3,7},{4,0},{5,1},{6,2},{7,3},{8,12},{9,13},{10,... | collective-permute-start | bytes 589832 | tf_op jit(solution)/shard_map/ppermute | solution.py:37
  123.9 27.1 %collective-permute-start.15 = (bf16[96,1024]{1,0:T(8,128)(2,1)}, bf16[96,1024]{1,0:T(8,128)(2,1)S(1)}, u32[]{:S(2)}, u32[]{:S(2)}) collective-permute-start(bf16[96,1024]{1,0:T(8,128)(2,1)} %get-tuple-element.50), channel_id=1, source_target_pairs={{0,8},{1,9},{2,10},{3,11},{4,12},{5,13},{6,14},{7,15},{8,0},{9,1},... | collective-permute-start | bytes 589832 | tf_op jit(solution)/shard_map/ppermute | solution.py:37
  125.9 25.1 %collective-permute-start.16 = (bf16[96,1024]{1,0:T(8,128)(2,1)}, bf16[96,1024]{1,0:T(8,128)(2,1)S(1)}, u32[]{:S(2)}, u32[]{:S(2)}) collective-permute-start(bf16[96,1024]{1,0:T(8,128)(2,1)} %get-tuple-element.51), channel_id=1, source_target_pairs={{0,12},{1,13},{2,14},{3,15},{4,8},{5,9},{6,10},{7,11},{8,4},{9,5},... | collective-permute-start | bytes 589832 | tf_op jit(solution)/shard_map/ppermute | solution.py:37
  134.2 16.9 %collective-permute-start.17 = (bf16[96,1024]{1,0:T(8,128)(2,1)}, bf16[96,1024]{1,0:T(8,128)(2,1)S(1)}, u32[]{:S(2)}, u32[]{:S(2)}) collective-permute-start(bf16[96,1024]{1,0:T(8,128)(2,1)} %get-tuple-element.52), channel_id=1, source_target_pairs={{0,4},{1,5},{2,6},{3,7},{4,0},{5,1},{6,2},{7,3},{8,12},{9,13},{10,... | collective-permute-start | bytes 589832 | tf_op jit(solution)/shard_map/ppermute | solution.py:37
  152.6 32.6 %copy-start.3 = (f32[256]{0:T(256)S(1)}, f32[256]{0:T(256)}, u32[]{:S(2)}) copy-start(f32[256]{0:T(256)} %param.19) | copy-start | bytes 3076
  152.6 32.6 %copy-start.4 = (s32[1,256]{1,0:T(1,128)S(1)}, s32[1,256]{1,0:T(1,128)}, u32[]{:S(2)}) copy-start(s32[1,256]{1,0:T(1,128)} %get-tuple-element.55.slot_ref) | copy-start | bytes 3076

commit v4 on v3

--- a/solution.py
+++ b/solution.py
@@ -55,6 +55,22 @@
 
 def block_at(k, rows):
     return pl.ds(pl.multiple_of(k * rows, rows), rows)
+
+
+def after_kernel(*refs):
+    pass
+
+
+def after(array, *earlier):
+    return pl.pallas_call(
+        after_kernel,
+        out_shape=jax.ShapeDtypeStruct(array.shape, array.dtype),
+        in_specs=[ANY] * (1 + len(earlier)),
+        out_specs=ANY,
+        input_output_aliases={0: 0},
+        cost_estimate=pl.CostEstimate(flops=0, bytes_accessed=0, transcendentals=0),
+        name="after",
+    )(array, *earlier)
 
 
 def split_kernel(plane, me_ref, moment_ref, weight_ref, *refs):
@@ -143,9 +159,8 @@
     )(me, perm, *stacks)
 
 
-def relocated(me, perm, pieces, groups):
-    stacks = in_plane(stacked(along_line(pieces, groups)), groups)
-    return along_line(pick(me, perm, stacks, groups), groups)
+def relocated(me, perm, stack, groups):
+    return along_line(pick(me, perm, in_plane(stack, groups), groups), groups)
 
 
 def assembled(plane, me_ref, pieces, held):
@@ -177,7 +192,7 @@
 
 
 def pack_kernel(groups, live_ref, perm_ref, *refs):
-    sources, (packed_ref, slot_ref), held, sem = refs[:5], refs[5:7], refs[7:12], refs[12]
+    sources, (packed_ref, slot_ref), held, sem = refs[:5], refs[6:8], refs[8:13], refs[13]
     route_ref, fwd_route_ref, hidden_ref, out_ref, fwd_ref = held
     copies = [pltpu.make_async_copy(ref, room, sem.at[n]) for n, (ref, room) in enumerate(zip(sources, held))]
     for copy in copies:
@@ -201,7 +216,7 @@
     packed_ref[:, ff + d :] = jnp.dot(fwd_selector, fwd_ref[...], preferred_element_type=F32).astype(BF16)
 
 
-def pack_rows(live_rows, perm, route, fwd_route, hidden, grad_out, fwd_hidden, groups, capacity):
+def pack_rows(live_rows, perm, route, fwd_route, hidden, grad_out, fwd_hidden, earlier, groups, capacity):
     rows, ff = hidden.shape
     width = 2 * ff + grad_out.shape[1]
     sources = (route.reshape(1, rows), fwd_route.reshape(1, rows), hidden, grad_out, fwd_hidden)
@@ -211,7 +226,7 @@
             jax.ShapeDtypeStruct((groups * capacity, width), BF16),
             jax.ShapeDtypeStruct((1, rows), jnp.int32),
         ),
-        in_specs=[SMEM, SMEM] + [HBM] * 5,
+        in_specs=[SMEM, SMEM] + [HBM] * 5 + [ANY],
         out_specs=(VMEM, VMEM),
         scratch_shapes=[pltpu.VMEM(a.shape, a.dtype) for a in sources] + [pltpu.SemaphoreType.DMA((len(sources),))],
         compiler_params=pltpu.CompilerParams(vmem_limit_bytes=60 * MIB),
@@ -219,7 +234,7 @@
             flops=2 * groups * capacity * rows * width, bytes_accessed=6 * rows * width, transcendentals=0
         ),
         name="pack_rows",
-    )(live_rows, perm, *sources)
+    )(live_rows, perm, *sources, earlier)
 
 
 def orthogonal_kernel(plane, me_ref, packed_ref, *refs):
@@ -332,13 +347,15 @@
     capacity = max(4, 2 * grad_hidden.shape[0] // groups)
     d = w_down.shape[2]
     moment_pieces, weight_pieces = split(me, w_moment, w_down, groups)
-    live_rows, moment_pieces = lax.optimization_barrier((live_rows, moment_pieces))
     packed, fwd_slot = pack_rows(
-        live_rows, perm, grad_route, fwd_route, grad_hidden, grad_out, fwd_hidden, groups, capacity
-    )
+        live_rows, perm, grad_route, fwd_route, grad_hidden, grad_out, fwd_hidden, weight_pieces[0], groups, capacity
+    )
+    moment_stack = stacked(along_line(moment_pieces, groups))
+    weight_stack = stacked(along_line(weight_pieces, groups))
+    packed = after(packed, moment_stack, weight_stack)
     received = exchange(packed.reshape(groups, capacity, -1)).reshape(groups * capacity, -1)
-    moment_placed = relocated(me, perm, moment_pieces, groups)
-    weight_placed = relocated(me, perm, weight_pieces, groups)
+    moment_placed = relocated(me, perm, moment_stack, groups)
+    weight_placed = relocated(me, perm, weight_stack, groups)
     moment_new, ortho = orthogonal(me, received, moment_placed, groups)
     weight_new, produced = produce(me, received, ortho, weight_placed, groups)
     returned = exchange(produced.reshape(groups, capacity, d)).reshape(groups * capacity, d)

time: 187 us -> 175 us (0.936)
  waiting for transfers between devices: 104 us -> 92.9 us
    ppermute x12, waiting for transfers between devices: 80.5 us -> 39 us  [along_line(): lax.ppermute(piece, 'expert', [(i, i ^ k * plane) for i in range(groups)])]
    ppermute x6, waiting for transfers between devices: 23.1 us -> 53.9 us  [in_plane(): lax.ppermute(held, 'expert', [(i, i ^ 1 << bit) for i in range(groups)])]
    ppermute x12, starting transfers between devices: 20.3 us -> 17.6 us  [along_line(): lax.ppermute(piece, 'expert', [(i, i ^ k * plane) for i in range(groups)])]
    all_to_all x1, starting transfers between devices: 7.38 us -> 9.37 us  [exchange(): lax.all_to_all(array, 'expert', split_axis=0, concat_axis=0, tiled=True)]
  transfers between devices with their start and end apart: 19 -> 19, of which waited for: 8 -> 8; matrix products, arithmetic and copies ran while one was open for 0% -> 0% of each run, Pallas kernels for 5% -> 6%
where the time goes in v4:
time: 175 us
  waiting for transfers between devices  92.9 us (53%)
  blocking collectives  32.3 us (18%)
  starting transfers between devices  29.6 us (17%)
  Pallas kernels  15.7 us (9%)
  local copies, waits for them, and re-layouts  2.71 us (2%)
    ppermute x6, waiting for transfers between devices, in_plane(): lax.ppermute(held, 'expert', [(i, i ^ 1 << bit) for i in range(groups)])  53.9 us
    ppermute x12, waiting for transfers between devices, along_line(): lax.ppermute(piece, 'expert', [(i, i ^ k * plane) for i in range(groups)])  39 us
    all_to_all x1, blocking collectives, exchange(): lax.all_to_all(array, 'expert', split_axis=0, concat_axis=0, tiled=True)  32.3 us
    ppermute x12, starting transfers between devices, along_line(): lax.ppermute(piece, 'expert', [(i, i ^ k * plane) for i in range(groups)])  17.6 us
    all_to_all x1, starting transfers between devices, exchange(): lax.all_to_all(array, 'expert', split_axis=0, concat_axis=0, tiled=True)  9.37 us
    pallas_call x1, Pallas kernels, pack_rows(): pl.pallas_call(functools.partial(pack_kernel, groups), out_shape=(jax.Sha...  4.15 us
    pallas_call x1, Pallas kernels, orthogonal(): pl.pallas_call(functools.partial(orthogonal_kernel, plane_of(groups)), ou...  3.62 us
  transfers between devices with their start and end apart: 19, of which 8 were waited for; matrix products, arithmetic and copies ran while one was open for 0% of the time, Pallas kernels for 6%

profile of v4, /device:TPU:0, one launch (start us, length us, event | category | flops | bytes accessed | tf_op | source)
XLA Modules:
  0.0 174.6 jit_solution(6526408571110287545)
XLA Ops:
  0.6 2.7 %split.1 = (bf16[96,1024]{1,0:T(8,128)(2,1)}, bf16[96,1024]{1,0:T(8,128)(2,1)}, bf16[96,1024]{1,0:T(8,128)(2,1)}, bf16[96,1024]{1,0:T(8,128)(2,1)}, bf16[96,1024...) custom-call(s32[1]{0:T(128)} %bitcast.me_ref, ...), custom_call_target="tpu_custom_call" | custom-call | bytes 3145728 | tf_op jit(solution)/shard_map/split/pallas_call | solution.py:98
  3.3 4.1 %collective-permute-start.3 = (bf16[96,1024]{1,0:T(8,128)(2,1)}, bf16[96,1024]{1,0:T(8,128)(2,1)S(1)}, u32[]{:S(2)}, u32[]{:S(2)}) collective-permute-start(bf16[96,1024]{1,0:T(8,128)(2,1)} %get-tuple-element.31), channel_id=1, source_target_pairs={{0,8},{1,9},{2,10},{3,11},{4,12},{5,13},{6,14},{7,15},{8,0},{9,1},... | collective-permute-start | bytes 589832 | tf_op jit(solution)/shard_map/ppermute | solution.py:37
  7.5 3.9 %collective-permute-start.4 = (bf16[96,1024]{1,0:T(8,128)(2,1)}, bf16[96,1024]{1,0:T(8,128)(2,1)S(1)}, u32[]{:S(2)}, u32[]{:S(2)}) collective-permute-start(bf16[96,1024]{1,0:T(8,128)(2,1)} %get-tuple-element.32), channel_id=1, source_target_pairs={{0,12},{1,13},{2,14},{3,15},{4,8},{5,9},{6,10},{7,11},{8,4},{9,5},... | collective-permute-start | bytes 589832 | tf_op jit(solution)/shard_map/ppermute | solution.py:37
  11.4 0.9 collective-permute-start.1
  12.3 14.6 %collective-permute-done.3.refs_1_ = bf16[96,1024]{1,0:T(8,128)(2,1)S(1)} collective-permute-done((bf16[96,1024]{1,0:T(8,128)(2,1)}, bf16[96,1024]{1,0:T(8,128)(2,1)S(1)}, u32[]{:S(2)}, u32[]{:S(2)}) %collective-permute-start.3) | collective-permute-done | bytes 196640 | tf_op jit(solution)/shard_map/ppermute | solution.py:37
  26.9 0.1 collective-permute-start.2
  27.6 4.2 %pack_rows.1 = (bf16[512,1792]{1,0:T(8,128)(2,1)}, s32[1,256]{1,0:T(1,128)}) custom-call(s32[1]{0:T(128)S(6)} %copy.15.live_ref, s32[16]{0:T(128)} %perm_ref.5, s32[1,256]{1,0:T(1,128)} %bitcast.17, s32[1,256]{1,0:T(1,128)} %bitcast.18, bf16[256,384]{1,0:T(8,128)(2,1)} %refs_2_.1, bf16[256,1024]{1,0:T(8,128)(2,1)} %refs_3_.1, bf16[256,384]{1,0:T(8,128)(2,1)} %refs_4_.1, ...), custom_call_target="tpu_custom_call" | custom-call | flops 469762048 | bytes 2752512 | tf_op jit(solution)/shard_map/pack_rows/pallas_call | solution.py:223
  31.9 0.9 copy-done
  32.8 1.7 collective-permute-done.refs_1_
  34.5 3.3 %collective-permute-done.2.refs_3_ = bf16[96,1024]{1,0:T(8,128)(2,1)S(1)} collective-permute-done((bf16[96,1024]{1,0:T(8,128)(2,1)}, bf16[96,1024]{1,0:T(8,128)(2,1)S(1)}, u32[]{:S(2)}, u32[]{:S(2)}) %collective-permute-start.2) | collective-permute-done | bytes 196640 | tf_op jit(solution)/shard_map/ppermute | solution.py:37
  37.9 0.9 copy-done.2
  38.8 9.4 %all-to-all-start = ((bf16[16,32,1792]{2,1,0:T(8,128)(2,1)}), bf16[16,32,1792]{2,1,0:T(8,128)(2,1)S(1)}, u32[]{:S(2)}, u32[]{:S(2)}) async-start(bf16[16,32,1792]{2,1,0:T(8,128)(2,1)} %bitcast.15), calls=%async_computation | async-start | bytes 3670016 | tf_op jit(solution)/shard_map/all_to_all | solution.py:339
  48.2 2.0 %collective-permute-start.6 = (bf16[4,96,1024]{2,1,0:T(8,128)(2,1)S(1)}, bf16[4,96,1024]{2,1,0:T(8,128)(2,1)S(1)}, u32[]{:S(2)}, u32[]{:S(2)}) collective-permute-start(bf16[4,96,1024]{2,1,0:T(8,128)(2,1)S(1)} %copy-done.3), channel_id=1, source_target_pairs={{0,2},{1,3},{2,0},{3,1},{4,6},{5,7},{6,4},{7,5},{8,10},{9,11},{10,... | collective-permute-start | bytes 2359304 | tf_op jit(solution)/shard_map/ppermute | solution.py:45
  50.2 0.1 collective-permute-start.12
  50.3 38.0 %collective-permute-done.6.refs_1_ = bf16[4,96,1024]{2,1,0:T(8,128)(2,1)S(1)} collective-permute-done((bf16[4,96,1024]{2,1,0:T(8,128)(2,1)S(1)}, bf16[4,96,1024]{2,1,0:T(8,128)(2,1)S(1)}, u32[]{:S(2)}, u32[]{:S(2)}) %collective-permute-start.6) | collective-permute-done | bytes 786464 | tf_op jit(solution)/shard_map/ppermute | solution.py:45
  88.3 0.5 collective-permute-start.13
  88.8 15.9 %collective-permute-done.12.refs_1_ = bf16[4,96,1024]{2,1,0:T(8,128)(2,1)S(1)} collective-permute-done((bf16[4,96,1024]{2,1,0:T(8,128)(2,1)S(1)}, bf16[4,96,1024]{2,1,0:T(8,128)(2,1)S(1)}, u32[]{:S(2)}, u32[]{:S(2)}) %collective-permute-start.12) | collective-permute-done | bytes 786464 | tf_op jit(solution)/shard_map/ppermute | solution.py:45
  104.7 0.7 pick.2
  105.5 2.4 %collective-permute-start.9 = (bf16[96,1024]{1,0:T(8,128)(2,1)S(1)}, bf16[96,1024]{1,0:T(8,128)(2,1)S(1)}, u32[]{:S(2)}, u32[]{:S(2)}) collective-permute-start(bf16[96,1024]{1,0:T(8,128)(2,1)S(1)} %get-tuple-element.35), channel_id=1, source_target_pairs={{0,8},{1,9},{2,10},{3,11},{4,12},{5,13},{6,14},{7,15},{8,0},{9,1},... | collective-permute-start | bytes 589832 | tf_op jit(solution)/shard_map/ppermute | solution.py:37
  107.9 1.5 collective-permute-start.10
  109.4 1.6 pick.3
  110.9 2.9 %collective-permute-start.15 = (bf16[96,1024]{1,0:T(8,128)(2,1)}, bf16[96,1024]{1,0:T(8,128)(2,1)S(1)}, u32[]{:S(2)}, u32[]{:S(2)}) collective-permute-start(bf16[96,1024]{1,0:T(8,128)(2,1)} %get-tuple-element.40), channel_id=1, source_target_pairs={{0,8},{1,9},{2,10},{3,11},{4,12},{5,13},{6,14},{7,15},{8,0},{9,1},... | collective-permute-start | bytes 589832 | tf_op jit(solution)/shard_map/ppermute | solution.py:37
  113.8 1.5 collective-permute-start.16
  115.3 7.3 %collective-permute-done.9.refs_1_ = bf16[96,1024]{1,0:T(8,128)(2,1)S(1)} collective-permute-done((bf16[96,1024]{1,0:T(8,128)(2,1)S(1)}, bf16[96,1024]{1,0:T(8,128)(2,1)S(1)}, u32[]{:S(2)}, u32[]{:S(2)}) %collective-permute-start.9) | collective-permute-done | bytes 196640 | tf_op jit(solution)/shard_map/ppermute | solution.py:37
  122.6 0.3 collective-permute-start.17
  122.9 0.7 collective-permute-done.11.refs_3_
  123.5 0.9 copy-done.10
  124.4 3.6 %orthogonal.1 = (bf16[384,1024]{1,0:T(8,128)(2,1)}, bf16[384,1024]{1,0:T(8,128)(2,1)S(1)}) custom-call(s32[1]{0:T(128)} %bitcast.me_ref, bf16[512,1792]{1,0:T(8,128)(2,1)S(1)} %bitcast.10, bf16[96,1024]{1,0:T(8,128)(2,1)S(1)} %copy-done.10, bf16[96,1024]{1,0:T(8,128)(2,1)S(1)} %collective-permute-done.9.refs_1_, ...), custom_call_target="tpu_custom_call" | custom-call | flops 1837105152 | bytes 4194304 | tf_op jit(solution)/shard_map/orthogonal/pallas_call | solution.py:268
  128.1 11.4 %collective-permute-done.15.refs_1_ = bf16[96,1024]{1,0:T(8,128)(2,1)S(1)} collective-permute-done((bf16[96,1024]{1,0:T(8,128)(2,1)}, bf16[96,1024]{1,0:T(8,128)(2,1)S(1)}, u32[]{:S(2)}, u32[]{:S(2)}) %collective-permute-start.15) | collective-permute-done | bytes 196640 | tf_op jit(solution)/shard_map/ppermute | solution.py:37
  139.4 1.6 produce.1
  141.0 32.3 %all_to_all.10 = bf16[16,32,1024]{2,1,0:T(8,128)(2,1)S(1)} all-to-all(bf16[16,32,1024]{2,1,0:T(8,128)(2,1)S(1)} %bitcast.13), channel_id=1, replica_groups=mesh['layer'=2,'expert'=16] {'expert'}, dimensions={0} | all-to-all | bytes 2097152 | tf_op jit(solution)/shard_map/all_to_all | solution.py:339
  173.4 1.3 finish.1
  (39 shorter events, 0.3 us)
Async XLA Ops:
  3.3 28.5 %copy-start.5 = (bf16[96,1024]{1,0:T(8,128)(2,1)S(1)}, bf16[96,1024]{1,0:T(8,128)(2,1)}, u32[]{:S(2)}) copy-start(bf16[96,1024]{1,0:T(8,128)(2,1)} %get-tuple-element.25.refs_5_.refs_0_) | copy-start | bytes 589828
  3.3 34.5 %copy-start.4 = (bf16[96,1024]{1,0:T(8,128)(2,1)S(1)}, bf16[96,1024]{1,0:T(8,128)(2,1)}, u32[]{:S(2)}) copy-start(bf16[96,1024]{1,0:T(8,128)(2,1)} %get-tuple-element.27.refs_0_) | copy-start | bytes 589828
  3.3 23.5 %collective-permute-start.3 = (bf16[96,1024]{1,0:T(8,128)(2,1)}, bf16[96,1024]{1,0:T(8,128)(2,1)S(1)}, u32[]{:S(2)}, u32[]{:S(2)}) collective-permute-start(bf16[96,1024]{1,0:T(8,128)(2,1)} %get-tuple-element.31), channel_id=1, source_target_pairs={{0,8},{1,9},{2,10},{3,11},{4,12},{5,13},{6,14},{7,15},{8,0},{9,1},... | collective-permute-start | bytes 589832 | tf_op jit(solution)/shard_map/ppermute | solution.py:37
  7.5 27.0 %collective-permute-start = (bf16[96,1024]{1,0:T(8,128)(2,1)}, bf16[96,1024]{1,0:T(8,128)(2,1)S(1)}, u32[]{:S(2)}, u32[]{:S(2)}) collective-permute-start(bf16[96,1024]{1,0:T(8,128)(2,1)} %get-tuple-element.28), channel_id=1, source_target_pairs={{0,8},{1,9},{2,10},{3,11},{4,12},{5,13},{6,14},{7,15},{8,0},{9,1},... | collective-permute-start | bytes 589832 | tf_op jit(solution)/shard_map/ppermute | solution.py:37
  7.5 24.3 %collective-permute-start.4 = (bf16[96,1024]{1,0:T(8,128)(2,1)}, bf16[96,1024]{1,0:T(8,128)(2,1)S(1)}, u32[]{:S(2)}, u32[]{:S(2)}) collective-permute-start(bf16[96,1024]{1,0:T(8,128)(2,1)} %get-tuple-element.32), channel_id=1, source_target_pairs={{0,12},{1,13},{2,14},{3,15},{4,8},{5,9},{6,10},{7,11},{8,4},{9,5},... | collective-permute-start | bytes 589832 | tf_op jit(solution)/shard_map/ppermute | solution.py:37
  11.4 20.4 %collective-permute-start.5 = (bf16[96,1024]{1,0:T(8,128)(2,1)}, bf16[96,1024]{1,0:T(8,128)(2,1)S(1)}, u32[]{:S(2)}, u32[]{:S(2)}) collective-permute-start(bf16[96,1024]{1,0:T(8,128)(2,1)} %get-tuple-element.33), channel_id=1, source_target_pairs={{0,4},{1,5},{2,6},{3,7},{4,0},{5,1},{6,2},{7,3},{8,12},{9,13},{10,... | collective-permute-start | bytes 589832 | tf_op jit(solution)/shard_map/ppermute | solution.py:37
  11.4 23.1 %collective-permute-start.1 = (bf16[96,1024]{1,0:T(8,128)(2,1)}, bf16[96,1024]{1,0:T(8,128)(2,1)S(1)}, u32[]{:S(2)}, u32[]{:S(2)}) collective-permute-start(bf16[96,1024]{1,0:T(8,128)(2,1)} %get-tuple-element.29), channel_id=1, source_target_pairs={{0,12},{1,13},{2,14},{3,15},{4,8},{5,9},{6,10},{7,11},{8,4},{9,5},... | collective-permute-start | bytes 589832 | tf_op jit(solution)/shard_map/ppermute | solution.py:37
  26.9 11.0 %collective-permute-start.2 = (bf16[96,1024]{1,0:T(8,128)(2,1)}, bf16[96,1024]{1,0:T(8,128)(2,1)S(1)}, u32[]{:S(2)}, u32[]{:S(2)}) collective-permute-start(bf16[96,1024]{1,0:T(8,128)(2,1)} %get-tuple-element.30), channel_id=1, source_target_pairs={{0,4},{1,5},{2,6},{3,7},{4,0},{5,1},{6,2},{7,3},{8,12},{9,13},{10,... | collective-permute-start | bytes 589832 | tf_op jit(solution)/shard_map/ppermute | solution.py:37
  31.9 0.9 copy-start
  37.9 0.9 copy-start.2
  38.8 9.4 %copy-start.3 = (bf16[4,96,1024]{2,1,0:T(8,128)(2,1)S(1)}, bf16[4,96,1024]{2,1,0:T(8,128)(2,1)}, u32[]{:S(2)}) copy-start(bf16[4,96,1024]{2,1,0:T(8,128)(2,1)} %copy-done.2) | copy-start | bytes 2359300
  38.8 11.4 %copy-start.1 = (bf16[4,96,1024]{2,1,0:T(8,128)(2,1)S(1)}, bf16[4,96,1024]{2,1,0:T(8,128)(2,1)}, u32[]{:S(2)}) copy-start(bf16[4,96,1024]{2,1,0:T(8,128)(2,1)} %copy-done) | copy-start | bytes 2359300
  38.8 65.9 %copy-start.6 = (s32[16]{0:T(128)S(1)}, s32[16]{0:T(128)}, u32[]{:S(2)}) copy-start(s32[16]{0:T(128)} %perm_ref.5) | copy-start | bytes 196
  38.8 84.7 %all-to-all-start = ((bf16[16,32,1792]{2,1,0:T(8,128)(2,1)}), bf16[16,32,1792]{2,1,0:T(8,128)(2,1)S(1)}, u32[]{:S(2)}, u32[]{:S(2)}) async-start(bf16[16,32,1792]{2,1,0:T(8,128)(2,1)} %bitcast.15), calls=%async_computation | async-start | bytes 3670016 | tf_op jit(solution)/shard_map/all_to_all | solution.py:339
  48.2 40.1 %collective-permute-start.6 = (bf16[4,96,1024]{2,1,0:T(8,128)(2,1)S(1)}, bf16[4,96,1024]{2,1,0:T(8,128)(2,1)S(1)}, u32[]{:S(2)}, u32[]{:S(2)}) collective-permute-start(bf16[4,96,1024]{2,1,0:T(8,128)(2,1)S(1)} %copy-done.3), channel_id=1, source_target_pairs={{0,2},{1,3},{2,0},{3,1},{4,6},{5,7},{6,4},{7,5},{8,10},{9,11},{10,... | collective-permute-start | bytes 2359304 | tf_op jit(solution)/shard_map/ppermute | solution.py:45
  50.2 54.5 %collective-permute-start.12 = (bf16[4,96,1024]{2,1,0:T(8,128)(2,1)S(1)}, bf16[4,96,1024]{2,1,0:T(8,128)(2,1)S(1)}, u32[]{:S(2)}, u32[]{:S(2)}) collective-permute-start(bf16[4,96,1024]{2,1,0:T(8,128)(2,1)S(1)} %copy-done.1), channel_id=1, source_target_pairs={{0,2},{1,3},{2,0},{3,1},{4,6},{5,7},{6,4},{7,5},{8,10},{9,11},{10,... | collective-permute-start | bytes 2359304 | tf_op jit(solution)/shard_map/ppermute | solution.py:45
  50.3 54.4 %collective-permute-start.7 = (bf16[4,96,1024]{2,1,0:T(8,128)(2,1)S(1)}, bf16[4,96,1024]{2,1,0:T(8,128)(2,1)S(1)}, u32[]{:S(2)}, u32[]{:S(2)}) collective-permute-start(bf16[4,96,1024]{2,1,0:T(8,128)(2,1)S(1)} %copy-done.3), channel_id=1, source_target_pairs={{0,1},{1,0},{2,3},{3,2},{4,5},{5,4},{6,7},{7,6},{8,9},{9,8},{10,11... | collective-permute-start | bytes 2359304 | tf_op jit(solution)/shard_map/ppermute | solution.py:45
  88.3 16.4 %collective-permute-start.8 = (bf16[4,96,1024]{2,1,0:T(8,128)(2,1)S(1)}, bf16[4,96,1024]{2,1,0:T(8,128)(2,1)S(1)}, u32[]{:S(2)}, u32[]{:S(2)}) collective-permute-start(bf16[4,96,1024]{2,1,0:T(8,128)(2,1)S(1)} %collective-permute-done.6.refs_1_), channel_id=1, source_target_pairs={{0,1},{1,0},{2,3},{3,2},{4,5},{5,4},{6,7},{7,6},{8,9},{9,8},{10,11... | collective-permute-start | bytes 2359304 | tf_op jit(solution)/shard_map/ppermute | solution.py:45
  88.3 21.1 %collective-permute-start.13 = (bf16[4,96,1024]{2,1,0:T(8,128)(2,1)S(1)}, bf16[4,96,1024]{2,1,0:T(8,128)(2,1)S(1)}, u32[]{:S(2)}, u32[]{:S(2)}) collective-permute-start(bf16[4,96,1024]{2,1,0:T(8,128)(2,1)S(1)} %copy-done.1), channel_id=1, source_target_pairs={{0,1},{1,0},{2,3},{3,2},{4,5},{5,4},{6,7},{7,6},{8,9},{9,8},{10,11... | collective-permute-start | bytes 2359304 | tf_op jit(solution)/shard_map/ppermute | solution.py:45
  104.7 4.7 %collective-permute-start.14 = (bf16[4,96,1024]{2,1,0:T(8,128)(2,1)S(1)}, bf16[4,96,1024]{2,1,0:T(8,128)(2,1)S(1)}, u32[]{:S(2)}, u32[]{:S(2)}) collective-permute-start(bf16[4,96,1024]{2,1,0:T(8,128)(2,1)S(1)} %collective-permute-done.12.refs_1_), channel_id=1, source_target_pairs={{0,1},{1,0},{2,3},{3,2},{4,5},{5,4},{6,7},{7,6},{8,9},{9,8},{10,11... | collective-permute-start | bytes 2359304 | tf_op jit(solution)/shard_map/ppermute | solution.py:45
  105.4 17.4 %copy-start.9 = (bf16[96,1024]{1,0:T(8,128)(2,1)}, bf16[96,1024]{1,0:T(8,128)(2,1)S(1)}, u32[]{:S(2)}) copy-start(bf16[96,1024]{1,0:T(8,128)(2,1)S(1)} %get-tuple-element.34.refs_0_) | copy-start | bytes 589828
  105.5 17.1 %collective-permute-start.9 = (bf16[96,1024]{1,0:T(8,128)(2,1)S(1)}, bf16[96,1024]{1,0:T(8,128)(2,1)S(1)}, u32[]{:S(2)}, u32[]{:S(2)}) collective-permute-start(bf16[96,1024]{1,0:T(8,128)(2,1)S(1)} %get-tuple-element.35), channel_id=1, source_target_pairs={{0,8},{1,9},{2,10},{3,11},{4,12},{5,13},{6,14},{7,15},{8,0},{9,1},... | collective-permute-start | bytes 589832 | tf_op jit(solution)/shard_map/ppermute | solution.py:37
  107.9 15.0 %collective-permute-start.10 = (bf16[96,1024]{1,0:T(8,128)(2,1)S(1)}, bf16[96,1024]{1,0:T(8,128)(2,1)S(1)}, u32[]{:S(2)}, u32[]{:S(2)}) collective-permute-start(bf16[96,1024]{1,0:T(8,128)(2,1)S(1)} %get-tuple-element.36), channel_id=1, source_target_pairs={{0,12},{1,13},{2,14},{3,15},{4,8},{5,9},{6,10},{7,11},{8,4},{9,5},... | collective-permute-start | bytes 589832 | tf_op jit(solution)/shard_map/ppermute | solution.py:37
  109.3 14.2 %collective-permute-start.11 = (bf16[96,1024]{1,0:T(8,128)(2,1)S(1)}, bf16[96,1024]{1,0:T(8,128)(2,1)S(1)}, u32[]{:S(2)}, u32[]{:S(2)}) collective-permute-start(bf16[96,1024]{1,0:T(8,128)(2,1)S(1)} %get-tuple-element.37), channel_id=1, source_target_pairs={{0,4},{1,5},{2,6},{3,7},{4,0},{5,1},{6,2},{7,3},{8,12},{9,13},{10,... | collective-permute-start | bytes 589832 | tf_op jit(solution)/shard_map/ppermute | solution.py:37
  110.9 28.5 %collective-permute-start.15 = (bf16[96,1024]{1,0:T(8,128)(2,1)}, bf16[96,1024]{1,0:T(8,128)(2,1)S(1)}, u32[]{:S(2)}, u32[]{:S(2)}) collective-permute-start(bf16[96,1024]{1,0:T(8,128)(2,1)} %get-tuple-element.40), channel_id=1, source_target_pairs={{0,8},{1,9},{2,10},{3,11},{4,12},{5,13},{6,14},{7,15},{8,0},{9,1},... | collective-permute-start | bytes 589832 | tf_op jit(solution)/shard_map/ppermute | solution.py:37
  113.8 25.6 %collective-permute-start.16 = (bf16[96,1024]{1,0:T(8,128)(2,1)}, bf16[96,1024]{1,0:T(8,128)(2,1)S(1)}, u32[]{:S(2)}, u32[]{:S(2)}) collective-permute-start(bf16[96,1024]{1,0:T(8,128)(2,1)} %get-tuple-element.41), channel_id=1, source_target_pairs={{0,12},{1,13},{2,14},{3,15},{4,8},{5,9},{6,10},{7,11},{8,4},{9,5},... | collective-permute-start | bytes 589832 | tf_op jit(solution)/shard_map/ppermute | solution.py:37
  122.6 16.9 %collective-permute-start.17 = (bf16[96,1024]{1,0:T(8,128)(2,1)}, bf16[96,1024]{1,0:T(8,128)(2,1)S(1)}, u32[]{:S(2)}, u32[]{:S(2)}) collective-permute-start(bf16[96,1024]{1,0:T(8,128)(2,1)} %get-tuple-element.42), channel_id=1, source_target_pairs={{0,4},{1,5},{2,6},{3,7},{4,0},{5,1},{6,2},{7,3},{8,12},{9,13},{10,... | collective-permute-start | bytes 589832 | tf_op jit(solution)/shard_map/ppermute | solution.py:37
  123.5 0.9 copy-start.10
  141.0 32.3 %copy-start.7 = (f32[256]{0:T(256)S(1)}, f32[256]{0:T(256)}, u32[]{:S(2)}) copy-start(f32[256]{0:T(256)} %param.19) | copy-start | bytes 3076
  141.0 32.3 %copy-start.8 = (s32[1,256]{1,0:T(1,128)S(1)}, s32[1,256]{1,0:T(1,128)}, u32[]{:S(2)}) copy-start(s32[1,256]{1,0:T(1,128)} %get-tuple-element.45.slot_ref) | copy-start | bytes 3076

commit v5 on v4

--- a/solution.py
+++ b/solution.py
@@ -39,11 +39,18 @@
     ]
 
 
-def in_plane(stack, groups):
-    stacks = [stack]
-    for bit in reversed(range(plane_of(groups).bit_length() - 1)):
-        stacks += [lax.ppermute(held, "expert", [(i, i ^ (1 << bit)) for i in range(groups)]) for held in stacks]
-    return stacks
+def cross(array, bit, groups):
+    return lax.ppermute(array, "expert", [(i, i ^ (1 << bit)) for i in range(groups)])
+
+
+def in_plane(column, groups):
+    bits = list(reversed(range(plane_of(groups).bit_length() - 1)))
+    across = [cross(piece, bits[0], groups) for piece in column] if bits else None
+    stack, token = stacked(column)
+    stacks = [stack] + ([stacked(across)[0]] if bits else [])
+    for bit in bits[1:]:
+        stacks += [cross(held, bit, groups) for held in stacks]
+    return stacks, token
 
 
 def plane_offsets(groups):
@@ -109,9 +116,10 @@
 
 
 def stack_kernel(order, *refs):
-    stack_ref = refs[-1]
+    stack_ref, token_ref = refs[-2:]
     for k, piece in zip(order, refs):
         stack_ref[k] = piece[...]
+    token_ref[...] = jnp.zeros_like(token_ref)
 
 
 def stacked(pieces):
@@ -119,9 +127,9 @@
     shape = (line,) + pieces[0].shape
     return pl.pallas_call(
         functools.partial(stack_kernel, line_order(line)),
-        out_shape=jax.ShapeDtypeStruct(shape, BF16),
+        out_shape=(jax.ShapeDtypeStruct(shape, BF16), jax.ShapeDtypeStruct((8, 128), F32)),
         in_specs=[VMEM] * line,
-        out_specs=VMEM,
+        out_specs=(VMEM, VMEM),
         compiler_params=pltpu.CompilerParams(vmem_limit_bytes=32 * MIB),
         cost_estimate=pl.CostEstimate(flops=0, bytes_accessed=4 * line * pieces[0].size, transcendentals=0),
         name="stack",
@@ -157,10 +165,6 @@
         cost_estimate=pl.CostEstimate(flops=0, bytes_accessed=4 * stacks[0].size, transcendentals=0),
         name="pick",
     )(me, perm, *stacks)
-
-
-def relocated(me, perm, stack, groups):
-    return along_line(pick(me, perm, in_plane(stack, groups), groups), groups)
 
 
 def assembled(plane, me_ref, pieces, held):
@@ -350,12 +354,12 @@
     packed, fwd_slot = pack_rows(
         live_rows, perm, grad_route, fwd_route, grad_hidden, grad_out, fwd_hidden, weight_pieces[0], groups, capacity
     )
-    moment_stack = stacked(along_line(moment_pieces, groups))
-    weight_stack = stacked(along_line(weight_pieces, groups))
-    packed = after(packed, moment_stack, weight_stack)
+    moment_stacks, moment_here = in_plane(along_line(moment_pieces, groups), groups)
+    weight_stacks, weight_here = in_plane(along_line(weight_pieces, groups), groups)
+    packed = after(packed, moment_here, weight_here)
     received = exchange(packed.reshape(groups, capacity, -1)).reshape(groups * capacity, -1)
-    moment_placed = relocated(me, perm, moment_stack, groups)
-    weight_placed = relocated(me, perm, weight_stack, groups)
+    moment_placed = along_line(pick(me, perm, moment_stacks, groups), groups)
+    weight_placed = along_line(pick(me, perm, weight_stacks, groups), groups)
     moment_new, ortho = orthogonal(me, received, moment_placed, groups)
     weight_new, produced = produce(me, received, ortho, weight_placed, groups)
     returned = exchange(produced.reshape(groups, capacity, d)).reshape(groups * capacity, d)

time: 175 us -> 176 us (level)
  waiting for transfers between devices: 92.9 us -> 84.1 us
  starting transfers between devices: 29.6 us -> 37.9 us
    ppermute x6 -> x12, waiting for transfers between devices: 53.9 us -> 44.9 us  [cross(): lax.ppermute(array, 'expert', [(i, i ^ 1 << bit) for i in range(groups)])]
    ppermute x6 -> x12, starting transfers between devices: 2.61 us -> 10.9 us  [cross(): lax.ppermute(array, 'expert', [(i, i ^ 1 << bit) for i in range(groups)])]
  transfers between devices with their start and end apart: 19 -> 25, of which waited for: 8 -> 13; matrix products, arithmetic and copies ran while one was open for 0% -> 0% of each run, Pallas kernels for 6% -> 7%
where the time goes in v5:
time: 176 us; the launch traced here: 175 us
  waiting for transfers between devices  84.1 us (48%)
  starting transfers between devices  37.9 us (22%)
  blocking collectives  32.3 us (18%)
  Pallas kernels  17 us (10%)
  local copies, waits for them, and re-layouts  2.26 us (1%)
    ppermute x12, waiting for transfers between devices, cross(): lax.ppermute(array, 'expert', [(i, i ^ 1 << bit) for i in range(groups)])  44.9 us
    ppermute x12, waiting for transfers between devices, along_line(): lax.ppermute(piece, 'expert', [(i, i ^ k * plane) for i in range(groups)])  39.2 us
    all_to_all x1, blocking collectives, exchange(): lax.all_to_all(array, 'expert', split_axis=0, concat_axis=0, tiled=True)  32.3 us
    ppermute x12, starting transfers between devices, along_line(): lax.ppermute(piece, 'expert', [(i, i ^ k * plane) for i in range(groups)])  18.5 us
    ppermute x12, starting transfers between devices, cross(): lax.ppermute(array, 'expert', [(i, i ^ 1 << bit) for i in range(groups)])  10.9 us
    all_to_all x1, starting transfers between devices, exchange(): lax.all_to_all(array, 'expert', split_axis=0, concat_axis=0, tiled=True)  8.43 us
    pallas_call x1, Pallas kernels, pack_rows(): pl.pallas_call(functools.partial(pack_kernel, groups), out_shape=(jax.Sha...  4.17 us
    pallas_call x1, Pallas kernels, orthogonal(): pl.pallas_call(functools.partial(orthogonal_kernel, plane_of(groups)), ou...  3.62 us
  transfers between devices with their start and end apart: 25, of which 13 were waited for; matrix products, arithmetic and copies ran while one was open for 0% of the time, Pallas kernels for 7%

profile of v5, /device:TPU:0, one launch (start us, length us, event | category | flops | bytes accessed | tf_op | source)
XLA Modules:
  0.0 175.0 jit_solution(13546345276441184891)
XLA Ops:
  0.6 2.7 %split.1 = (bf16[96,1024]{1,0:T(8,128)(2,1)}, bf16[96,1024]{1,0:T(8,128)(2,1)}, bf16[96,1024]{1,0:T(8,128)(2,1)}, bf16[96,1024]{1,0:T(8,128)(2,1)}, bf16[96,1024...) custom-call(s32[1]{0:T(128)} %bitcast.me_ref, ...), custom_call_target="tpu_custom_call" | custom-call | bytes 3145728 | tf_op jit(solution)/shard_map/split/pallas_call | solution.py:105
  3.3 4.1 %collective-permute-start.3 = (bf16[96,1024]{1,0:T(8,128)(2,1)}, bf16[96,1024]{1,0:T(8,128)(2,1)S(1)}, u32[]{:S(2)}, u32[]{:S(2)}) collective-permute-start(bf16[96,1024]{1,0:T(8,128)(2,1)} %get-tuple-element.38), channel_id=1, source_target_pairs={{0,8},{1,9},{2,10},{3,11},{4,12},{5,13},{6,14},{7,15},{8,0},{9,1},... | collective-permute-start | bytes 589832 | tf_op jit(solution)/shard_map/ppermute | solution.py:37
  7.4 1.3 collective-permute-start.4
  9.0 2.8 %collective-permute-start = (bf16[96,1024]{1,0:T(8,128)(2,1)}, bf16[96,1024]{1,0:T(8,128)(2,1)S(1)}, u32[]{:S(2)}, u32[]{:S(2)}) collective-permute-start(bf16[96,1024]{1,0:T(8,128)(2,1)} %get-tuple-element.34), channel_id=1, source_target_pairs={{0,8},{1,9},{2,10},{3,11},{4,12},{5,13},{6,14},{7,15},{8,0},{9,1},... | collective-permute-start | bytes 589832 | tf_op jit(solution)/shard_map/ppermute | solution.py:37
  11.8 1.3 collective-permute-start.1
  13.2 9.5 %collective-permute-done.3.refs_1_ = bf16[96,1024]{1,0:T(8,128)(2,1)S(1)} collective-permute-done((bf16[96,1024]{1,0:T(8,128)(2,1)}, bf16[96,1024]{1,0:T(8,128)(2,1)S(1)}, u32[]{:S(2)}, u32[]{:S(2)}) %collective-permute-start.3) | collective-permute-done | bytes 196640 | tf_op jit(solution)/shard_map/ppermute | solution.py:37
  23.5 4.2 %pack_rows.1 = (bf16[512,1792]{1,0:T(8,128)(2,1)}, s32[1,256]{1,0:T(1,128)}) custom-call(s32[1]{0:T(128)S(6)} %copy.15.live_ref, s32[16]{0:T(128)} %perm_ref.5, s32[1,256]{1,0:T(1,128)} %bitcast.17, s32[1,256]{1,0:T(1,128)} %bitcast.18, bf16[256,384]{1,0:T(8,128)(2,1)} %refs_2_.1, bf16[256,1024]{1,0:T(8,128)(2,1)} %refs_3_.1, bf16[256,384]{1,0:T(8,128)(2,1)} %refs_4_.1, ...), custom_call_target="tpu_custom_call" | custom-call | flops 469762048 | bytes 2752512 | tf_op jit(solution)/shard_map/pack_rows/pallas_call | solution.py:227
  28.4 10.3 %collective-permute-done.refs_1_ = bf16[96,1024]{1,0:T(8,128)(2,1)S(1)} collective-permute-done((bf16[96,1024]{1,0:T(8,128)(2,1)}, bf16[96,1024]{1,0:T(8,128)(2,1)S(1)}, u32[]{:S(2)}, u32[]{:S(2)}) %collective-permute-start) | collective-permute-done | bytes 196640 | tf_op jit(solution)/shard_map/ppermute | solution.py:37
  39.5 8.4 %all-to-all-start = ((bf16[16,32,1792]{2,1,0:T(8,128)(2,1)}), bf16[16,32,1792]{2,1,0:T(8,128)(2,1)S(1)}, u32[]{:S(2)}, u32[]{:S(2)}) async-start(bf16[16,32,1792]{2,1,0:T(8,128)(2,1)} %bitcast.15), calls=%async_computation | async-start | bytes 3670016 | tf_op jit(solution)/shard_map/all_to_all | solution.py:343
  47.9 1.9 %collective-permute-start.6 = (bf16[96,1024]{1,0:T(8,128)(2,1)}, bf16[96,1024]{1,0:T(8,128)(2,1)S(1)}, u32[]{:S(2)}, u32[]{:S(2)}) collective-permute-start(bf16[96,1024]{1,0:T(8,128)(2,1)} %get-tuple-element.33.refs_0_), channel_id=1, source_target_pairs={{0,2},{1,3},{2,0},{3,1},{4,6},{5,7},{6,4},{7,5},{8,10},{9,11},{10,... | collective-permute-start | bytes 589832 | tf_op jit(solution)/shard_map/ppermute | solution.py:43
  50.0 1.9 %collective-permute-start.8 = (bf16[96,1024]{1,0:T(8,128)(2,1)}, bf16[96,1024]{1,0:T(8,128)(2,1)S(1)}, u32[]{:S(2)}, u32[]{:S(2)}) collective-permute-start(bf16[96,1024]{1,0:T(8,128)(2,1)} %copy-done.5), channel_id=1, source_target_pairs={{0,2},{1,3},{2,0},{3,1},{4,6},{5,7},{6,4},{7,5},{8,10},{9,11},{10,... | collective-permute-start | bytes 589832 | tf_op jit(solution)/shard_map/ppermute | solution.py:43
  52.1 1.9 %collective-permute-start.15 = (bf16[96,1024]{1,0:T(8,128)(2,1)}, bf16[96,1024]{1,0:T(8,128)(2,1)S(1)}, u32[]{:S(2)}, u32[]{:S(2)}) collective-permute-start(bf16[96,1024]{1,0:T(8,128)(2,1)} %get-tuple-element.31.refs_5_.refs_0_), channel_id=1, source_target_pairs={{0,2},{1,3},{2,0},{3,1},{4,6},{5,7},{6,4},{7,5},{8,10},{9,11},{10,... | collective-permute-start | bytes 589832 | tf_op jit(solution)/shard_map/ppermute | solution.py:43
  53.9 16.1 %collective-permute-done.6.refs_0_ = bf16[96,1024]{1,0:T(8,128)(2,1)S(1)} collective-permute-done((bf16[96,1024]{1,0:T(8,128)(2,1)}, bf16[96,1024]{1,0:T(8,128)(2,1)S(1)}, u32[]{:S(2)}, u32[]{:S(2)}) %collective-permute-start.6) | collective-permute-done | bytes 196640 | tf_op jit(solution)/shard_map/ppermute | solution.py:43
  70.0 4.7 %collective-permute-done.7.refs_1_ = bf16[96,1024]{1,0:T(8,128)(2,1)S(1)} collective-permute-done((bf16[96,1024]{1,0:T(8,128)(2,1)}, bf16[96,1024]{1,0:T(8,128)(2,1)S(1)}, u32[]{:S(2)}, u32[]{:S(2)}) %collective-permute-start.7) | collective-permute-done | bytes 196640 | tf_op jit(solution)/shard_map/ppermute | solution.py:43
  74.7 2.6 %collective-permute-start.17 = (bf16[96,1024]{1,0:T(8,128)(2,1)}, bf16[96,1024]{1,0:T(8,128)(2,1)S(1)}, u32[]{:S(2)}, u32[]{:S(2)}) collective-permute-start(bf16[96,1024]{1,0:T(8,128)(2,1)} %copy-done), channel_id=1, source_target_pairs={{0,2},{1,3},{2,0},{3,1},{4,6},{5,7},{6,4},{7,5},{8,10},{9,11},{10,... | collective-permute-start | bytes 589832 | tf_op jit(solution)/shard_map/ppermute | solution.py:43
  77.3 1.8 %collective-permute-done.8.refs_2_ = bf16[96,1024]{1,0:T(8,128)(2,1)S(1)} collective-permute-done((bf16[96,1024]{1,0:T(8,128)(2,1)}, bf16[96,1024]{1,0:T(8,128)(2,1)S(1)}, u32[]{:S(2)}, u32[]{:S(2)}) %collective-permute-start.8) | collective-permute-done | bytes 196640 | tf_op jit(solution)/shard_map/ppermute | solution.py:43
  79.1 2.4 %collective-permute-start.18 = (bf16[96,1024]{1,0:T(8,128)(2,1)}, bf16[96,1024]{1,0:T(8,128)(2,1)S(1)}, u32[]{:S(2)}, u32[]{:S(2)}) collective-permute-start(bf16[96,1024]{1,0:T(8,128)(2,1)} %copy-done.1), channel_id=1, source_target_pairs={{0,2},{1,3},{2,0},{3,1},{4,6},{5,7},{6,4},{7,5},{8,10},{9,11},{10,... | collective-permute-start | bytes 589832 | tf_op jit(solution)/shard_map/ppermute | solution.py:43
  81.5 6.6 %collective-permute-done.9.refs_3_ = bf16[96,1024]{1,0:T(8,128)(2,1)S(1)} collective-permute-done((bf16[96,1024]{1,0:T(8,128)(2,1)}, bf16[96,1024]{1,0:T(8,128)(2,1)S(1)}, u32[]{:S(2)}, u32[]{:S(2)}) %collective-permute-start.9) | collective-permute-done | bytes 196640 | tf_op jit(solution)/shard_map/ppermute | solution.py:43
  88.7 3.6 %collective-permute-done.15.refs_0_ = bf16[96,1024]{1,0:T(8,128)(2,1)S(1)} collective-permute-done((bf16[96,1024]{1,0:T(8,128)(2,1)}, bf16[96,1024]{1,0:T(8,128)(2,1)S(1)}, u32[]{:S(2)}, u32[]{:S(2)}) %collective-permute-start.15) | collective-permute-done | bytes 196640 | tf_op jit(solution)/shard_map/ppermute | solution.py:43
  92.3 4.2 %collective-permute-done.16.refs_1_ = bf16[96,1024]{1,0:T(8,128)(2,1)S(1)} collective-permute-done((bf16[96,1024]{1,0:T(8,128)(2,1)}, bf16[96,1024]{1,0:T(8,128)(2,1)S(1)}, u32[]{:S(2)}, u32[]{:S(2)}) %collective-permute-start.16) | collective-permute-done | bytes 196640 | tf_op jit(solution)/shard_map/ppermute | solution.py:43
  96.5 4.2 %collective-permute-done.17.refs_2_ = bf16[96,1024]{1,0:T(8,128)(2,1)S(1)} collective-permute-done((bf16[96,1024]{1,0:T(8,128)(2,1)}, bf16[96,1024]{1,0:T(8,128)(2,1)S(1)}, u32[]{:S(2)}, u32[]{:S(2)}) %collective-permute-start.17) | collective-permute-done | bytes 196640 | tf_op jit(solution)/shard_map/ppermute | solution.py:43
  100.7 3.7 %collective-permute-done.18.refs_3_ = bf16[96,1024]{1,0:T(8,128)(2,1)S(1)} collective-permute-done((bf16[96,1024]{1,0:T(8,128)(2,1)}, bf16[96,1024]{1,0:T(8,128)(2,1)S(1)}, u32[]{:S(2)}, u32[]{:S(2)}) %collective-permute-start.18) | collective-permute-done | bytes 196640 | tf_op jit(solution)/shard_map/ppermute | solution.py:43
  105.9 2.4 %collective-permute-start.12 = (bf16[96,1024]{1,0:T(8,128)(2,1)S(1)}, bf16[96,1024]{1,0:T(8,128)(2,1)S(1)}, u32[]{:S(2)}, u32[]{:S(2)}) collective-permute-start(bf16[96,1024]{1,0:T(8,128)(2,1)S(1)} %get-tuple-element.45), channel_id=1, source_target_pairs={{0,8},{1,9},{2,10},{3,11},{4,12},{5,13},{6,14},{7,15},{8,0},{9,1},... | collective-permute-start | bytes 589832 | tf_op jit(solution)/shard_map/ppermute | solution.py:37
  108.3 1.5 collective-permute-start.13
  109.8 1.6 pick.3
  111.3 2.9 %collective-permute-start.21 = (bf16[96,1024]{1,0:T(8,128)(2,1)}, bf16[96,1024]{1,0:T(8,128)(2,1)S(1)}, u32[]{:S(2)}, u32[]{:S(2)}) collective-permute-start(bf16[96,1024]{1,0:T(8,128)(2,1)} %get-tuple-element.52), channel_id=1, source_target_pairs={{0,8},{1,9},{2,10},{3,11},{4,12},{5,13},{6,14},{7,15},{8,0},{9,1},... | collective-permute-start | bytes 589832 | tf_op jit(solution)/shard_map/ppermute | solution.py:37
  114.3 1.5 collective-permute-start.22
  115.7 7.3 %collective-permute-done.12.refs_1_ = bf16[96,1024]{1,0:T(8,128)(2,1)S(1)} collective-permute-done((bf16[96,1024]{1,0:T(8,128)(2,1)S(1)}, bf16[96,1024]{1,0:T(8,128)(2,1)S(1)}, u32[]{:S(2)}, u32[]{:S(2)}) %collective-permute-start.12) | collective-permute-done | bytes 196640 | tf_op jit(solution)/shard_map/ppermute | solution.py:37
  124.9 3.6 %orthogonal.1 = (bf16[384,1024]{1,0:T(8,128)(2,1)}, bf16[384,1024]{1,0:T(8,128)(2,1)S(1)}) custom-call(s32[1]{0:T(128)} %bitcast.me_ref, bf16[512,1792]{1,0:T(8,128)(2,1)S(1)} %bitcast.10, bf16[96,1024]{1,0:T(8,128)(2,1)S(1)} %copy-done.14, bf16[96,1024]{1,0:T(8,128)(2,1)S(1)} %collective-permute-done.12.refs_1_, ...), custom_call_target="tpu_custom_call" | custom-call | flops 1837105152 | bytes 4194304 | tf_op jit(solution)/shard_map/orthogonal/pallas_call | solution.py:272
  128.5 11.4 %collective-permute-done.21.refs_1_ = bf16[96,1024]{1,0:T(8,128)(2,1)S(1)} collective-permute-done((bf16[96,1024]{1,0:T(8,128)(2,1)}, bf16[96,1024]{1,0:T(8,128)(2,1)S(1)}, u32[]{:S(2)}, u32[]{:S(2)}) %collective-permute-start.21) | collective-permute-done | bytes 196640 | tf_op jit(solution)/shard_map/ppermute | solution.py:37
  139.9 1.6 produce.1
  141.4 32.3 %all_to_all.10 = bf16[16,32,1024]{2,1,0:T(8,128)(2,1)S(1)} all-to-all(bf16[16,32,1024]{2,1,0:T(8,128)(2,1)S(1)} %bitcast.13), channel_id=1, replica_groups=mesh['layer'=2,'expert'=16] {'expert'}, dimensions={0} | all-to-all | bytes 2097152 | tf_op jit(solution)/shard_map/all_to_all | solution.py:343
  (61 shorter events, 7.3 us)
Async XLA Ops:
  3.3 24.4 %copy-start.3 = (bf16[96,1024]{1,0:T(8,128)(2,1)S(1)}, bf16[96,1024]{1,0:T(8,128)(2,1)}, u32[]{:S(2)}) copy-start(bf16[96,1024]{1,0:T(8,128)(2,1)} %get-tuple-element.31.refs_5_.refs_0_) | copy-start | bytes 589828
  3.3 35.4 %copy-start.4 = (bf16[96,1024]{1,0:T(8,128)(2,1)S(1)}, bf16[96,1024]{1,0:T(8,128)(2,1)}, u32[]{:S(2)}) copy-start(bf16[96,1024]{1,0:T(8,128)(2,1)} %get-tuple-element.33.refs_0_) | copy-start | bytes 589828
  3.3 19.3 %collective-permute-start.3 = (bf16[96,1024]{1,0:T(8,128)(2,1)}, bf16[96,1024]{1,0:T(8,128)(2,1)S(1)}, u32[]{:S(2)}, u32[]{:S(2)}) collective-permute-start(bf16[96,1024]{1,0:T(8,128)(2,1)} %get-tuple-element.38), channel_id=1, source_target_pairs={{0,8},{1,9},{2,10},{3,11},{4,12},{5,13},{6,14},{7,15},{8,0},{9,1},... | collective-permute-start | bytes 589832 | tf_op jit(solution)/shard_map/ppermute | solution.py:37
  7.4 20.2 %collective-permute-start.4 = (bf16[96,1024]{1,0:T(8,128)(2,1)}, bf16[96,1024]{1,0:T(8,128)(2,1)S(1)}, u32[]{:S(2)}, u32[]{:S(2)}) collective-permute-start(bf16[96,1024]{1,0:T(8,128)(2,1)} %get-tuple-element.39), channel_id=1, source_target_pairs={{0,12},{1,13},{2,14},{3,15},{4,8},{5,9},{6,10},{7,11},{8,4},{9,5},... | collective-permute-start | bytes 589832 | tf_op jit(solution)/shard_map/ppermute | solution.py:37
  8.8 18.9 %collective-permute-start.5 = (bf16[96,1024]{1,0:T(8,128)(2,1)}, bf16[96,1024]{1,0:T(8,128)(2,1)S(1)}, u32[]{:S(2)}, u32[]{:S(2)}) collective-permute-start(bf16[96,1024]{1,0:T(8,128)(2,1)} %get-tuple-element.40), channel_id=1, source_target_pairs={{0,4},{1,5},{2,6},{3,7},{4,0},{5,1},{6,2},{7,3},{8,12},{9,13},{10,... | collective-permute-start | bytes 589832 | tf_op jit(solution)/shard_map/ppermute | solution.py:37
  9.0 29.7 %collective-permute-start = (bf16[96,1024]{1,0:T(8,128)(2,1)}, bf16[96,1024]{1,0:T(8,128)(2,1)S(1)}, u32[]{:S(2)}, u32[]{:S(2)}) collective-permute-start(bf16[96,1024]{1,0:T(8,128)(2,1)} %get-tuple-element.34), channel_id=1, source_target_pairs={{0,8},{1,9},{2,10},{3,11},{4,12},{5,13},{6,14},{7,15},{8,0},{9,1},... | collective-permute-start | bytes 589832 | tf_op jit(solution)/shard_map/ppermute | solution.py:37
  11.8 26.9 %collective-permute-start.1 = (bf16[96,1024]{1,0:T(8,128)(2,1)}, bf16[96,1024]{1,0:T(8,128)(2,1)S(1)}, u32[]{:S(2)}, u32[]{:S(2)}) collective-permute-start(bf16[96,1024]{1,0:T(8,128)(2,1)} %get-tuple-element.35), channel_id=1, source_target_pairs={{0,12},{1,13},{2,14},{3,15},{4,8},{5,9},{6,10},{7,11},{8,4},{9,5},... | collective-permute-start | bytes 589832 | tf_op jit(solution)/shard_map/ppermute | solution.py:37
  22.7 16.0 %copy-start.2 = (bf16[96,1024]{1,0:T(8,128)(2,1)}, bf16[96,1024]{1,0:T(8,128)(2,1)S(1)}, u32[]{:S(2)}) copy-start(bf16[96,1024]{1,0:T(8,128)(2,1)S(1)} %collective-permute-done.3.refs_1_) | copy-start | bytes 589828
  22.7 16.0 %collective-permute-start.2 = (bf16[96,1024]{1,0:T(8,128)(2,1)}, bf16[96,1024]{1,0:T(8,128)(2,1)S(1)}, u32[]{:S(2)}, u32[]{:S(2)}) collective-permute-start(bf16[96,1024]{1,0:T(8,128)(2,1)} %get-tuple-element.36), channel_id=1, source_target_pairs={{0,4},{1,5},{2,6},{3,7},{4,0},{5,1},{6,2},{7,3},{8,12},{9,13},{10,... | collective-permute-start | bytes 589832 | tf_op jit(solution)/shard_map/ppermute | solution.py:37
  39.5 65.6 %copy-start.10 = (s32[16]{0:T(128)S(1)}, s32[16]{0:T(128)}, u32[]{:S(2)}) copy-start(s32[16]{0:T(128)} %perm_ref.5) | copy-start | bytes 196
  39.5 84.4 %all-to-all-start = ((bf16[16,32,1792]{2,1,0:T(8,128)(2,1)}), bf16[16,32,1792]{2,1,0:T(8,128)(2,1)S(1)}, u32[]{:S(2)}, u32[]{:S(2)}) async-start(bf16[16,32,1792]{2,1,0:T(8,128)(2,1)} %bitcast.15), calls=%async_computation | async-start | bytes 3670016 | tf_op jit(solution)/shard_map/all_to_all | solution.py:343
  47.9 22.1 %collective-permute-start.6 = (bf16[96,1024]{1,0:T(8,128)(2,1)}, bf16[96,1024]{1,0:T(8,128)(2,1)S(1)}, u32[]{:S(2)}, u32[]{:S(2)}) collective-permute-start(bf16[96,1024]{1,0:T(8,128)(2,1)} %get-tuple-element.33.refs_0_), channel_id=1, source_target_pairs={{0,2},{1,3},{2,0},{3,1},{4,6},{5,7},{6,4},{7,5},{8,10},{9,11},{10,... | collective-permute-start | bytes 589832 | tf_op jit(solution)/shard_map/ppermute | solution.py:43
  49.9 24.8 %collective-permute-start.7 = (bf16[96,1024]{1,0:T(8,128)(2,1)}, bf16[96,1024]{1,0:T(8,128)(2,1)S(1)}, u32[]{:S(2)}, u32[]{:S(2)}) collective-permute-start(bf16[96,1024]{1,0:T(8,128)(2,1)} %copy-done.7), channel_id=1, source_target_pairs={{0,2},{1,3},{2,0},{3,1},{4,6},{5,7},{6,4},{7,5},{8,10},{9,11},{10,... | collective-permute-start | bytes 589832 | tf_op jit(solution)/shard_map/ppermute | solution.py:43
  50.0 29.1 %collective-permute-start.8 = (bf16[96,1024]{1,0:T(8,128)(2,1)}, bf16[96,1024]{1,0:T(8,128)(2,1)S(1)}, u32[]{:S(2)}, u32[]{:S(2)}) collective-permute-start(bf16[96,1024]{1,0:T(8,128)(2,1)} %copy-done.5), channel_id=1, source_target_pairs={{0,2},{1,3},{2,0},{3,1},{4,6},{5,7},{6,4},{7,5},{8,10},{9,11},{10,... | collective-permute-start | bytes 589832 | tf_op jit(solution)/shard_map/ppermute | solution.py:43
  51.9 36.2 %collective-permute-start.9 = (bf16[96,1024]{1,0:T(8,128)(2,1)}, bf16[96,1024]{1,0:T(8,128)(2,1)S(1)}, u32[]{:S(2)}, u32[]{:S(2)}) collective-permute-start(bf16[96,1024]{1,0:T(8,128)(2,1)} %copy-done.6), channel_id=1, source_target_pairs={{0,2},{1,3},{2,0},{3,1},{4,6},{5,7},{6,4},{7,5},{8,10},{9,11},{10,... | collective-permute-start | bytes 589832 | tf_op jit(solution)/shard_map/ppermute | solution.py:43
  52.1 40.2 %collective-permute-start.15 = (bf16[96,1024]{1,0:T(8,128)(2,1)}, bf16[96,1024]{1,0:T(8,128)(2,1)S(1)}, u32[]{:S(2)}, u32[]{:S(2)}) collective-permute-start(bf16[96,1024]{1,0:T(8,128)(2,1)} %get-tuple-element.31.refs_5_.refs_0_), channel_id=1, source_target_pairs={{0,2},{1,3},{2,0},{3,1},{4,6},{5,7},{6,4},{7,5},{8,10},{9,11},{10,... | collective-permute-start | bytes 589832 | tf_op jit(solution)/shard_map/ppermute | solution.py:43
  70.0 26.4 %collective-permute-start.16 = (bf16[96,1024]{1,0:T(8,128)(2,1)}, bf16[96,1024]{1,0:T(8,128)(2,1)S(1)}, u32[]{:S(2)}, u32[]{:S(2)}) collective-permute-start(bf16[96,1024]{1,0:T(8,128)(2,1)} %copy-done.2), channel_id=1, source_target_pairs={{0,2},{1,3},{2,0},{3,1},{4,6},{5,7},{6,4},{7,5},{8,10},{9,11},{10,... | collective-permute-start | bytes 589832 | tf_op jit(solution)/shard_map/ppermute | solution.py:43
  74.7 26.0 %collective-permute-start.17 = (bf16[96,1024]{1,0:T(8,128)(2,1)}, bf16[96,1024]{1,0:T(8,128)(2,1)S(1)}, u32[]{:S(2)}, u32[]{:S(2)}) collective-permute-start(bf16[96,1024]{1,0:T(8,128)(2,1)} %copy-done), channel_id=1, source_target_pairs={{0,2},{1,3},{2,0},{3,1},{4,6},{5,7},{6,4},{7,5},{8,10},{9,11},{10,... | collective-permute-start | bytes 589832 | tf_op jit(solution)/shard_map/ppermute | solution.py:43
  79.1 25.3 %collective-permute-start.18 = (bf16[96,1024]{1,0:T(8,128)(2,1)}, bf16[96,1024]{1,0:T(8,128)(2,1)S(1)}, u32[]{:S(2)}, u32[]{:S(2)}) collective-permute-start(bf16[96,1024]{1,0:T(8,128)(2,1)} %copy-done.1), channel_id=1, source_target_pairs={{0,2},{1,3},{2,0},{3,1},{4,6},{5,7},{6,4},{7,5},{8,10},{9,11},{10,... | collective-permute-start | bytes 589832 | tf_op jit(solution)/shard_map/ppermute | solution.py:43
  88.1 17.0 %collective-permute-start.10 = (bf16[4,96,1024]{2,1,0:T(8,128)(2,1)S(1)}, bf16[4,96,1024]{2,1,0:T(8,128)(2,1)S(1)}, u32[]{:S(2)}, u32[]{:S(2)}) collective-permute-start(bf16[4,96,1024]{2,1,0:T(8,128)(2,1)S(1)} %get-tuple-element.42.refs_0_), channel_id=1, source_target_pairs={{0,1},{1,0},{2,3},{3,2},{4,5},{5,4},{6,7},{7,6},{8,9},{9,8},{10,11... | collective-permute-start | bytes 2359304 | tf_op jit(solution)/shard_map/ppermute | solution.py:43
  92.3 12.8 %collective-permute-start.11 = (bf16[4,96,1024]{2,1,0:T(8,128)(2,1)S(1)}, bf16[4,96,1024]{2,1,0:T(8,128)(2,1)S(1)}, u32[]{:S(2)}, u32[]{:S(2)}) collective-permute-start(bf16[4,96,1024]{2,1,0:T(8,128)(2,1)S(1)} %get-tuple-element.43.refs_1_), channel_id=1, source_target_pairs={{0,1},{1,0},{2,3},{3,2},{4,5},{5,4},{6,7},{7,6},{8,9},{9,8},{10,11... | collective-permute-start | bytes 2359304 | tf_op jit(solution)/shard_map/ppermute | solution.py:43
  96.5 13.3 %collective-permute-start.19 = (bf16[4,96,1024]{2,1,0:T(8,128)(2,1)S(1)}, bf16[4,96,1024]{2,1,0:T(8,128)(2,1)S(1)}, u32[]{:S(2)}, u32[]{:S(2)}) collective-permute-start(bf16[4,96,1024]{2,1,0:T(8,128)(2,1)S(1)} %get-tuple-element.49.refs_0_), channel_id=1, source_target_pairs={{0,1},{1,0},{2,3},{3,2},{4,5},{5,4},{6,7},{7,6},{8,9},{9,8},{10,11... | collective-permute-start | bytes 2359304 | tf_op jit(solution)/shard_map/ppermute | solution.py:43
  105.1 4.7 %collective-permute-start.20 = (bf16[4,96,1024]{2,1,0:T(8,128)(2,1)S(1)}, bf16[4,96,1024]{2,1,0:T(8,128)(2,1)S(1)}, u32[]{:S(2)}, u32[]{:S(2)}) collective-permute-start(bf16[4,96,1024]{2,1,0:T(8,128)(2,1)S(1)} %get-tuple-element.50.refs_1_), channel_id=1, source_target_pairs={{0,1},{1,0},{2,3},{3,2},{4,5},{5,4},{6,7},{7,6},{8,9},{9,8},{10,11... | collective-permute-start | bytes 2359304 | tf_op jit(solution)/shard_map/ppermute | solution.py:43
  105.9 17.4 %copy-start.13 = (bf16[96,1024]{1,0:T(8,128)(2,1)}, bf16[96,1024]{1,0:T(8,128)(2,1)S(1)}, u32[]{:S(2)}) copy-start(bf16[96,1024]{1,0:T(8,128)(2,1)S(1)} %get-tuple-element.44.refs_0_) | copy-start | bytes 589828
  105.9 17.1 %collective-permute-start.12 = (bf16[96,1024]{1,0:T(8,128)(2,1)S(1)}, bf16[96,1024]{1,0:T(8,128)(2,1)S(1)}, u32[]{:S(2)}, u32[]{:S(2)}) collective-permute-start(bf16[96,1024]{1,0:T(8,128)(2,1)S(1)} %get-tuple-element.45), channel_id=1, source_target_pairs={{0,8},{1,9},{2,10},{3,11},{4,12},{5,13},{6,14},{7,15},{8,0},{9,1},... | collective-permute-start | bytes 589832 | tf_op jit(solution)/shard_map/ppermute | solution.py:37
  108.3 15.0 %collective-permute-start.13 = (bf16[96,1024]{1,0:T(8,128)(2,1)S(1)}, bf16[96,1024]{1,0:T(8,128)(2,1)S(1)}, u32[]{:S(2)}, u32[]{:S(2)}) collective-permute-start(bf16[96,1024]{1,0:T(8,128)(2,1)S(1)} %get-tuple-element.46), channel_id=1, source_target_pairs={{0,12},{1,13},{2,14},{3,15},{4,8},{5,9},{6,10},{7,11},{8,4},{9,5},... | collective-permute-start | bytes 589832 | tf_op jit(solution)/shard_map/ppermute | solution.py:37
  109.8 14.2 %collective-permute-start.14 = (bf16[96,1024]{1,0:T(8,128)(2,1)S(1)}, bf16[96,1024]{1,0:T(8,128)(2,1)S(1)}, u32[]{:S(2)}, u32[]{:S(2)}) collective-permute-start(bf16[96,1024]{1,0:T(8,128)(2,1)S(1)} %get-tuple-element.47), channel_id=1, source_target_pairs={{0,4},{1,5},{2,6},{3,7},{4,0},{5,1},{6,2},{7,3},{8,12},{9,13},{10,... | collective-permute-start | bytes 589832 | tf_op jit(solution)/shard_map/ppermute | solution.py:37
  111.3 28.5 %collective-permute-start.21 = (bf16[96,1024]{1,0:T(8,128)(2,1)}, bf16[96,1024]{1,0:T(8,128)(2,1)S(1)}, u32[]{:S(2)}, u32[]{:S(2)}) collective-permute-start(bf16[96,1024]{1,0:T(8,128)(2,1)} %get-tuple-element.52), channel_id=1, source_target_pairs={{0,8},{1,9},{2,10},{3,11},{4,12},{5,13},{6,14},{7,15},{8,0},{9,1},... | collective-permute-start | bytes 589832 | tf_op jit(solution)/shard_map/ppermute | solution.py:37
  114.3 25.6 %collective-permute-start.22 = (bf16[96,1024]{1,0:T(8,128)(2,1)}, bf16[96,1024]{1,0:T(8,128)(2,1)S(1)}, u32[]{:S(2)}, u32[]{:S(2)}) collective-permute-start(bf16[96,1024]{1,0:T(8,128)(2,1)} %get-tuple-element.53), channel_id=1, source_target_pairs={{0,12},{1,13},{2,14},{3,15},{4,8},{5,9},{6,10},{7,11},{8,4},{9,5},... | collective-permute-start | bytes 589832 | tf_op jit(solution)/shard_map/ppermute | solution.py:37
  123.0 16.9 %collective-permute-start.23 = (bf16[96,1024]{1,0:T(8,128)(2,1)}, bf16[96,1024]{1,0:T(8,128)(2,1)S(1)}, u32[]{:S(2)}, u32[]{:S(2)}) collective-permute-start(bf16[96,1024]{1,0:T(8,128)(2,1)} %get-tuple-element.54), channel_id=1, source_target_pairs={{0,4},{1,5},{2,6},{3,7},{4,0},{5,1},{6,2},{7,3},{8,12},{9,13},{10,... | collective-permute-start | bytes 589832 | tf_op jit(solution)/shard_map/ppermute | solution.py:37
  141.4 32.3 %copy-start.11 = (f32[256]{0:T(256)S(1)}, f32[256]{0:T(256)}, u32[]{:S(2)}) copy-start(f32[256]{0:T(256)} %param.19) | copy-start | bytes 3076
  141.4 32.3 %copy-start.12 = (s32[1,256]{1,0:T(1,128)S(1)}, s32[1,256]{1,0:T(1,128)}, u32[]{:S(2)}) copy-start(s32[1,256]{1,0:T(1,128)} %get-tuple-element.57.slot_ref) | copy-start | bytes 3076
  (8 other events, 26.6 us)

commit v6 on v5

--- a/solution.py
+++ b/solution.py
@@ -46,11 +46,10 @@
 def in_plane(column, groups):
     bits = list(reversed(range(plane_of(groups).bit_length() - 1)))
     across = [cross(piece, bits[0], groups) for piece in column] if bits else None
-    stack, token = stacked(column)
-    stacks = [stack] + ([stacked(across)[0]] if bits else [])
+    stacks, tokens = zip(*[stacked(pieces) for pieces in ([column, across] if bits else [column])])
     for bit in bits[1:]:
-        stacks += [cross(held, bit, groups) for held in stacks]
-    return stacks, token
+        stacks += tuple(cross(held, bit, groups) for held in stacks)
+    return stacks, tokens
 
 
 def plane_offsets(groups):
@@ -356,7 +355,7 @@
     )
     moment_stacks, moment_here = in_plane(along_line(moment_pieces, groups), groups)
     weight_stacks, weight_here = in_plane(along_line(weight_pieces, groups), groups)
-    packed = after(packed, moment_here, weight_here)
+    packed = after(packed, *moment_here, *weight_here)
     received = exchange(packed.reshape(groups, capacity, -1)).reshape(groups * capacity, -1)
     moment_placed = along_line(pick(me, perm, moment_stacks, groups), groups)
     weight_placed = along_line(pick(me, perm, weight_stacks, groups), groups)

time: 176 us -> 188 us (1.068)
  local copies, waits for them, and re-layouts: 2.26 us -> 15.9 us
    ppermute x12, waiting for transfers between devices: 39.2 us -> 69.6 us  [along_line(): lax.ppermute(piece, 'expert', [(i, i ^ k * plane) for i in range(groups)])]
    ppermute x12, waiting for transfers between devices: 44.9 us -> 15.1 us  [cross(): lax.ppermute(array, 'expert', [(i, i ^ 1 << bit) for i in range(groups)])]
    unnamed x30 -> x58, local copies, waits for them, and re-layouts: 2.26 us -> 15.9 us
  transfers between devices with their start and end apart: 25 -> 25, of which waited for: 13 -> 10; matrix products, arithmetic and copies ran while one was open for 0% -> 0% of each run, Pallas kernels for 7% -> 5%
where the time goes in v6:
time: 188 us; the launch traced here: 187 us
  waiting for transfers between devices  84.7 us (45%)
  starting transfers between devices  37.3 us (20%)
  blocking collectives  30.9 us (16%)
  Pallas kernels  16.9 us (9%)
  local copies, waits for them, and re-layouts  15.9 us (8%)
    ppermute x12, waiting for transfers between devices, along_line(): lax.ppermute(piece, 'expert', [(i, i ^ k * plane) for i in range(groups)])  69.6 us
    all_to_all x1, blocking collectives, exchange(): lax.all_to_all(array, 'expert', split_axis=0, concat_axis=0, tiled=True)  30.9 us
    ppermute x12, starting transfers between devices, along_line(): lax.ppermute(piece, 'expert', [(i, i ^ k * plane) for i in range(groups)])  17.6 us
    unnamed x58, local copies, waits for them, and re-layouts  15.9 us
    ppermute x12, waiting for transfers between devices, cross(): lax.ppermute(array, 'expert', [(i, i ^ 1 << bit) for i in range(groups)])  15.1 us
    ppermute x12, starting transfers between devices, cross(): lax.ppermute(array, 'expert', [(i, i ^ 1 << bit) for i in range(groups)])  10.6 us
    all_to_all x1, starting transfers between devices, exchange(): lax.all_to_all(array, 'expert', split_axis=0, concat_axis=0, tiled=True)  9.13 us
    pallas_call x1, Pallas kernels, pack_rows(): pl.pallas_call(functools.partial(pack_kernel, groups), out_shape=(jax.Sha...  4.15 us
  transfers between devices with their start and end apart: 25, of which 10 were waited for; matrix products, arithmetic and copies ran while one was open for 0% of the time, Pallas kernels for 5%

profile of v6, /device:TPU:0, one launch (start us, length us, event | category | flops | bytes accessed | tf_op | source)
XLA Modules:
  0.0 187.2 jit_solution(1655480762063944540)
XLA Ops:
  0.6 2.7 %split.1 = (bf16[96,1024]{1,0:T(8,128)(2,1)}, bf16[96,1024]{1,0:T(8,128)(2,1)}, bf16[96,1024]{1,0:T(8,128)(2,1)}, bf16[96,1024]{1,0:T(8,128)(2,1)}, bf16[96,1024...) custom-call(s32[1]{0:T(128)} %bitcast.me_ref, ...), custom_call_target="tpu_custom_call" | custom-call | bytes 3145728 | tf_op jit(solution)/shard_map/split/pallas_call | solution.py:104
  3.3 3.0 %collective-permute-start.10 = (bf16[96,1024]{1,0:T(8,128)(2,1)}, bf16[96,1024]{1,0:T(8,128)(2,1)S(1)}, u32[]{:S(2)}, u32[]{:S(2)}) collective-permute-start(bf16[96,1024]{1,0:T(8,128)(2,1)} %get-tuple-element.33.refs_5_.refs_0_), channel_id=1, source_target_pairs={{0,2},{1,3},{2,0},{3,1},{4,6},{5,7},{6,4},{7,5},{8,10},{9,11},{10,... | collective-permute-start | bytes 589832 | tf_op jit(solution)/shard_map/ppermute | solution.py:43
  6.4 2.6 %collective-permute-start.7 = (bf16[96,1024]{1,0:T(8,128)(2,1)}, bf16[96,1024]{1,0:T(8,128)(2,1)S(1)}, u32[]{:S(2)}, u32[]{:S(2)}) collective-permute-start(bf16[96,1024]{1,0:T(8,128)(2,1)} %get-tuple-element.41), channel_id=1, source_target_pairs={{0,8},{1,9},{2,10},{3,11},{4,12},{5,13},{6,14},{7,15},{8,0},{9,1},... | collective-permute-start | bytes 589832 | tf_op jit(solution)/shard_map/ppermute | solution.py:37
  9.0 1.3 collective-permute-start.8
  10.5 2.8 %collective-permute-start = (bf16[96,1024]{1,0:T(8,128)(2,1)}, bf16[96,1024]{1,0:T(8,128)(2,1)S(1)}, u32[]{:S(2)}, u32[]{:S(2)}) collective-permute-start(bf16[96,1024]{1,0:T(8,128)(2,1)} %get-tuple-element.36), channel_id=1, source_target_pairs={{0,8},{1,9},{2,10},{3,11},{4,12},{5,13},{6,14},{7,15},{8,0},{9,1},... | collective-permute-start | bytes 589832 | tf_op jit(solution)/shard_map/ppermute | solution.py:37
  13.4 2.0 %collective-permute-start.1 = (bf16[96,1024]{1,0:T(8,128)(2,1)}, bf16[96,1024]{1,0:T(8,128)(2,1)S(1)}, u32[]{:S(2)}, u32[]{:S(2)}) collective-permute-start(bf16[96,1024]{1,0:T(8,128)(2,1)} %get-tuple-element.37), channel_id=1, source_target_pairs={{0,12},{1,13},{2,14},{3,15},{4,8},{5,9},{6,10},{7,11},{8,4},{9,5},... | collective-permute-start | bytes 589832 | tf_op jit(solution)/shard_map/ppermute | solution.py:37
  15.3 15.3 %collective-permute-done.7.refs_1_ = bf16[96,1024]{1,0:T(8,128)(2,1)S(1)} collective-permute-done((bf16[96,1024]{1,0:T(8,128)(2,1)}, bf16[96,1024]{1,0:T(8,128)(2,1)S(1)}, u32[]{:S(2)}, u32[]{:S(2)}) %collective-permute-start.7) | collective-permute-done | bytes 196640 | tf_op jit(solution)/shard_map/ppermute | solution.py:37
  30.6 2.0 %collective-permute-start.12 = (bf16[96,1024]{1,0:T(8,128)(2,1)S(1)}, bf16[96,1024]{1,0:T(8,128)(2,1)S(1)}, u32[]{:S(2)}, u32[]{:S(2)}) collective-permute-start(bf16[96,1024]{1,0:T(8,128)(2,1)S(1)} %collective-permute-done.8.refs_2_), channel_id=1, source_target_pairs={{0,2},{1,3},{2,0},{3,1},{4,6},{5,7},{6,4},{7,5},{8,10},{9,11},{10,... | collective-permute-start | bytes 589832 | tf_op jit(solution)/shard_map/ppermute | solution.py:43
  32.6 7.8 %collective-permute-done.refs_1_ = bf16[96,1024]{1,0:T(8,128)(2,1)S(1)} collective-permute-done((bf16[96,1024]{1,0:T(8,128)(2,1)}, bf16[96,1024]{1,0:T(8,128)(2,1)S(1)}, u32[]{:S(2)}, u32[]{:S(2)}) %collective-permute-start) | collective-permute-done | bytes 196640 | tf_op jit(solution)/shard_map/ppermute | solution.py:37
  40.8 1.6 collective-permute-start.13
  42.8 1.6 collective-permute-start.5
  45.5 4.1 %pack_rows.1 = (bf16[512,1792]{1,0:T(8,128)(2,1)}, s32[1,256]{1,0:T(1,128)}) custom-call(s32[1]{0:T(128)S(6)} %copy.15.live_ref, s32[16]{0:T(128)} %perm_ref.5, s32[1,256]{1,0:T(1,128)} %bitcast.17, s32[1,256]{1,0:T(1,128)} %bitcast.18, bf16[256,384]{1,0:T(8,128)(2,1)} %refs_2_.1, bf16[256,1024]{1,0:T(8,128)(2,1)} %refs_3_.1, bf16[256,384]{1,0:T(8,128)(2,1)} %refs_4_.1, ...), custom_call_target="tpu_custom_call" | custom-call | flops 469762048 | bytes 2752512 | tf_op jit(solution)/shard_map/pack_rows/pallas_call | solution.py:226
  50.7 2.0 %collective-permute-done.13.refs_3_ = bf16[96,1024]{1,0:T(8,128)(2,1)S(1)} collective-permute-done((bf16[96,1024]{1,0:T(8,128)(2,1)S(1)}, bf16[96,1024]{1,0:T(8,128)(2,1)S(1)}, u32[]{:S(2)}, u32[]{:S(2)}) %collective-permute-start.13) | collective-permute-done | bytes 196640 | tf_op jit(solution)/shard_map/ppermute | solution.py:43
  52.7 4.2 %collective-permute-done.4.refs_1_ = bf16[96,1024]{1,0:T(8,128)(2,1)} collective-permute-done((bf16[96,1024]{1,0:T(8,128)(2,1)S(1)}, bf16[96,1024]{1,0:T(8,128)(2,1)}, u32[]{:S(2)}, u32[]{:S(2)}) %collective-permute-start.4) | collective-permute-done | bytes 196640 | tf_op jit(solution)/shard_map/ppermute | solution.py:43
  57.0 3.1 %collective-permute-done.5.refs_2_ = bf16[96,1024]{1,0:T(8,128)(2,1)} collective-permute-done((bf16[96,1024]{1,0:T(8,128)(2,1)S(1)}, bf16[96,1024]{1,0:T(8,128)(2,1)}, u32[]{:S(2)}, u32[]{:S(2)}) %collective-permute-start.5) | collective-permute-done | bytes 196640 | tf_op jit(solution)/shard_map/ppermute | solution.py:43
  60.0 2.1 %collective-permute-done.6.refs_3_ = bf16[96,1024]{1,0:T(8,128)(2,1)} collective-permute-done((bf16[96,1024]{1,0:T(8,128)(2,1)S(1)}, bf16[96,1024]{1,0:T(8,128)(2,1)}, u32[]{:S(2)}, u32[]{:S(2)}) %collective-permute-start.6) | collective-permute-done | bytes 196640 | tf_op jit(solution)/shard_map/ppermute | solution.py:43
  62.1 1.2 stack.5
  64.8 9.1 %all-to-all-start = ((bf16[16,32,1792]{2,1,0:T(8,128)(2,1)}), bf16[16,32,1792]{2,1,0:T(8,128)(2,1)S(1)}, u32[]{:S(2)}, u32[]{:S(2)}) async-start(bf16[16,32,1792]{2,1,0:T(8,128)(2,1)} %bitcast.15), calls=%async_computation | async-start | bytes 3670016 | tf_op jit(solution)/shard_map/all_to_all | solution.py:342
  75.0 1.5 collective-permute-done.14.refs_2_
  76.5 2.2 %collective-permute-done.15.refs_3_ = bf16[4,96,1024]{2,1,0:T(8,128)(2,1)S(1)} collective-permute-done((bf16[4,96,1024]{2,1,0:T(8,128)(2,1)}, bf16[4,96,1024]{2,1,0:T(8,128)(2,1)S(1)}, u32[]{:S(2)}, u32[]{:S(2)}) %collective-permute-start.15) | collective-permute-done | bytes 786464 | tf_op jit(solution)/shard_map/ppermute | solution.py:43
  78.7 1.1 copy-done.1
  79.9 1.1 copy-done.3
  81.8 2.8 %collective-permute-start.16 = (bf16[96,1024]{1,0:T(8,128)(2,1)S(1)}, bf16[96,1024]{1,0:T(8,128)(2,1)S(1)}, u32[]{:S(2)}, u32[]{:S(2)}) collective-permute-start(bf16[96,1024]{1,0:T(8,128)(2,1)S(1)} %get-tuple-element.49), channel_id=1, source_target_pairs={{0,8},{1,9},{2,10},{3,11},{4,12},{5,13},{6,14},{7,15},{8,0},{9,1},... | collective-permute-start | bytes 589832 | tf_op jit(solution)/shard_map/ppermute | solution.py:37
  84.6 1.5 collective-permute-start.17
  86.1 1.6 pick.3
  88.3 2.9 %collective-permute-start.21 = (bf16[96,1024]{1,0:T(8,128)(2,1)}, bf16[96,1024]{1,0:T(8,128)(2,1)S(1)}, u32[]{:S(2)}, u32[]{:S(2)}) collective-permute-start(bf16[96,1024]{1,0:T(8,128)(2,1)} %get-tuple-element.56), channel_id=1, source_target_pairs={{0,8},{1,9},{2,10},{3,11},{4,12},{5,13},{6,14},{7,15},{8,0},{9,1},... | collective-permute-start | bytes 589832 | tf_op jit(solution)/shard_map/ppermute | solution.py:37
  91.2 1.5 collective-permute-start.22
  92.7 46.2 %collective-permute-done.16.refs_1_ = bf16[96,1024]{1,0:T(8,128)(2,1)S(1)} collective-permute-done((bf16[96,1024]{1,0:T(8,128)(2,1)S(1)}, bf16[96,1024]{1,0:T(8,128)(2,1)S(1)}, u32[]{:S(2)}, u32[]{:S(2)}) %collective-permute-start.16) | collective-permute-done | bytes 196640 | tf_op jit(solution)/shard_map/ppermute | solution.py:37
  144.7 3.6 %orthogonal.1 = (bf16[384,1024]{1,0:T(8,128)(2,1)}, bf16[384,1024]{1,0:T(8,128)(2,1)S(1)}) custom-call(s32[1]{0:T(128)} %bitcast.me_ref, bf16[512,1792]{1,0:T(8,128)(2,1)S(1)} %bitcast.10, bf16[96,1024]{1,0:T(8,128)(2,1)S(1)} %copy-done.22, bf16[96,1024]{1,0:T(8,128)(2,1)S(1)} %copy-done.24, bf16[96,1024]{1,0:T(8,128)(2,1)S(1)} %copy-done.26, ...), custom_call_target="tpu_custom_call" | custom-call | flops 1837105152 | bytes 4194304 | tf_op jit(solution)/shard_map/orthogonal/pallas_call | solution.py:271
  153.4 1.6 produce.1
  155.0 30.9 %all_to_all.10 = bf16[16,32,1024]{2,1,0:T(8,128)(2,1)S(1)} all-to-all(bf16[16,32,1024]{2,1,0:T(8,128)(2,1)S(1)} %bitcast.13), channel_id=1, replica_groups=mesh['layer'=2,'expert'=16] {'expert'}, dimensions={0} | all-to-all | bytes 2097152 | tf_op jit(solution)/shard_map/all_to_all | solution.py:342
  185.9 1.3 finish.1
  (89 shorter events, 17.3 us)
Async XLA Ops:
  3.3 46.3 %copy-start.13 = (bf16[96,1024]{1,0:T(8,128)(2,1)S(1)}, bf16[96,1024]{1,0:T(8,128)(2,1)}, u32[]{:S(2)}) copy-start(bf16[96,1024]{1,0:T(8,128)(2,1)} %get-tuple-element.33.refs_5_.refs_0_) | copy-start | bytes 589828
  3.3 46.4 %copy-start.12 = (bf16[96,1024]{1,0:T(8,128)(2,1)S(1)}, bf16[96,1024]{1,0:T(8,128)(2,1)}, u32[]{:S(2)}) copy-start(bf16[96,1024]{1,0:T(8,128)(2,1)} %get-tuple-element.35.refs_0_) | copy-start | bytes 589828
  3.3 10.0 %collective-permute-start.10 = (bf16[96,1024]{1,0:T(8,128)(2,1)}, bf16[96,1024]{1,0:T(8,128)(2,1)S(1)}, u32[]{:S(2)}, u32[]{:S(2)}) collective-permute-start(bf16[96,1024]{1,0:T(8,128)(2,1)} %get-tuple-element.33.refs_5_.refs_0_), channel_id=1, source_target_pairs={{0,2},{1,3},{2,0},{3,1},{4,6},{5,7},{6,4},{7,5},{8,10},{9,11},{10,... | collective-permute-start | bytes 589832 | tf_op jit(solution)/shard_map/ppermute | solution.py:43
  6.4 24.2 %collective-permute-start.7 = (bf16[96,1024]{1,0:T(8,128)(2,1)}, bf16[96,1024]{1,0:T(8,128)(2,1)S(1)}, u32[]{:S(2)}, u32[]{:S(2)}) collective-permute-start(bf16[96,1024]{1,0:T(8,128)(2,1)} %get-tuple-element.41), channel_id=1, source_target_pairs={{0,8},{1,9},{2,10},{3,11},{4,12},{5,13},{6,14},{7,15},{8,0},{9,1},... | collective-permute-start | bytes 589832 | tf_op jit(solution)/shard_map/ppermute | solution.py:37
  9.0 21.6 %collective-permute-start.8 = (bf16[96,1024]{1,0:T(8,128)(2,1)}, bf16[96,1024]{1,0:T(8,128)(2,1)S(1)}, u32[]{:S(2)}, u32[]{:S(2)}) collective-permute-start(bf16[96,1024]{1,0:T(8,128)(2,1)} %get-tuple-element.42), channel_id=1, source_target_pairs={{0,12},{1,13},{2,14},{3,15},{4,8},{5,9},{6,10},{7,11},{8,4},{9,5},... | collective-permute-start | bytes 589832 | tf_op jit(solution)/shard_map/ppermute | solution.py:37
  10.3 20.3 %collective-permute-start.9 = (bf16[96,1024]{1,0:T(8,128)(2,1)}, bf16[96,1024]{1,0:T(8,128)(2,1)S(1)}, u32[]{:S(2)}, u32[]{:S(2)}) collective-permute-start(bf16[96,1024]{1,0:T(8,128)(2,1)} %get-tuple-element.43), channel_id=1, source_target_pairs={{0,4},{1,5},{2,6},{3,7},{4,0},{5,1},{6,2},{7,3},{8,12},{9,13},{10,... | collective-permute-start | bytes 589832 | tf_op jit(solution)/shard_map/ppermute | solution.py:37
  10.5 29.8 %collective-permute-start = (bf16[96,1024]{1,0:T(8,128)(2,1)}, bf16[96,1024]{1,0:T(8,128)(2,1)S(1)}, u32[]{:S(2)}, u32[]{:S(2)}) collective-permute-start(bf16[96,1024]{1,0:T(8,128)(2,1)} %get-tuple-element.36), channel_id=1, source_target_pairs={{0,8},{1,9},{2,10},{3,11},{4,12},{5,13},{6,14},{7,15},{8,0},{9,1},... | collective-permute-start | bytes 589832 | tf_op jit(solution)/shard_map/ppermute | solution.py:37
  13.4 27.4 %collective-permute-start.1 = (bf16[96,1024]{1,0:T(8,128)(2,1)}, bf16[96,1024]{1,0:T(8,128)(2,1)S(1)}, u32[]{:S(2)}, u32[]{:S(2)}) collective-permute-start(bf16[96,1024]{1,0:T(8,128)(2,1)} %get-tuple-element.37), channel_id=1, source_target_pairs={{0,12},{1,13},{2,14},{3,15},{4,8},{5,9},{6,10},{7,11},{8,4},{9,5},... | collective-permute-start | bytes 589832 | tf_op jit(solution)/shard_map/ppermute | solution.py:37
  30.6 11.8 %collective-permute-start.2 = (bf16[96,1024]{1,0:T(8,128)(2,1)}, bf16[96,1024]{1,0:T(8,128)(2,1)S(1)}, u32[]{:S(2)}, u32[]{:S(2)}) collective-permute-start(bf16[96,1024]{1,0:T(8,128)(2,1)} %get-tuple-element.38), channel_id=1, source_target_pairs={{0,4},{1,5},{2,6},{3,7},{4,0},{5,1},{6,2},{7,3},{8,12},{9,13},{10,... | collective-permute-start | bytes 589832 | tf_op jit(solution)/shard_map/ppermute | solution.py:37
  30.6 12.2 %collective-permute-start.11 = (bf16[96,1024]{1,0:T(8,128)(2,1)S(1)}, bf16[96,1024]{1,0:T(8,128)(2,1)S(1)}, u32[]{:S(2)}, u32[]{:S(2)}) collective-permute-start(bf16[96,1024]{1,0:T(8,128)(2,1)S(1)} %collective-permute-done.7.refs_1_), channel_id=1, source_target_pairs={{0,2},{1,3},{2,0},{3,1},{4,6},{5,7},{6,4},{7,5},{8,10},{9,11},{10,... | collective-permute-start | bytes 589832 | tf_op jit(solution)/shard_map/ppermute | solution.py:43
  30.6 13.8 %collective-permute-start.12 = (bf16[96,1024]{1,0:T(8,128)(2,1)S(1)}, bf16[96,1024]{1,0:T(8,128)(2,1)S(1)}, u32[]{:S(2)}, u32[]{:S(2)}) collective-permute-start(bf16[96,1024]{1,0:T(8,128)(2,1)S(1)} %collective-permute-done.8.refs_2_), channel_id=1, source_target_pairs={{0,2},{1,3},{2,0},{3,1},{4,6},{5,7},{6,4},{7,5},{8,10},{9,11},{10,... | collective-permute-start | bytes 589832 | tf_op jit(solution)/shard_map/ppermute | solution.py:43
  40.4 12.3 %collective-permute-start.3 = (bf16[96,1024]{1,0:T(8,128)(2,1)}, bf16[96,1024]{1,0:T(8,128)(2,1)S(1)}, u32[]{:S(2)}, u32[]{:S(2)}) collective-permute-start(bf16[96,1024]{1,0:T(8,128)(2,1)} %get-tuple-element.35.refs_0_), channel_id=1, source_target_pairs={{0,2},{1,3},{2,0},{3,1},{4,6},{5,7},{6,4},{7,5},{8,10},{9,11},{10,... | collective-permute-start | bytes 589832 | tf_op jit(solution)/shard_map/ppermute | solution.py:43
  40.8 11.9 %collective-permute-start.13 = (bf16[96,1024]{1,0:T(8,128)(2,1)S(1)}, bf16[96,1024]{1,0:T(8,128)(2,1)S(1)}, u32[]{:S(2)}, u32[]{:S(2)}) collective-permute-start(bf16[96,1024]{1,0:T(8,128)(2,1)S(1)} %collective-permute-done.9.refs_3_), channel_id=1, source_target_pairs={{0,2},{1,3},{2,0},{3,1},{4,6},{5,7},{6,4},{7,5},{8,10},{9,11},{10,... | collective-permute-start | bytes 589832 | tf_op jit(solution)/shard_map/ppermute | solution.py:43
  42.4 14.5 %collective-permute-start.4 = (bf16[96,1024]{1,0:T(8,128)(2,1)S(1)}, bf16[96,1024]{1,0:T(8,128)(2,1)}, u32[]{:S(2)}, u32[]{:S(2)}) collective-permute-start(bf16[96,1024]{1,0:T(8,128)(2,1)S(1)} %collective-permute-done.refs_1_), channel_id=1, source_target_pairs={{0,2},{1,3},{2,0},{3,1},{4,6},{5,7},{6,4},{7,5},{8,10},{9,11},{10,... | collective-permute-start | bytes 589832 | tf_op jit(solution)/shard_map/ppermute | solution.py:43
  42.8 17.2 %collective-permute-start.5 = (bf16[96,1024]{1,0:T(8,128)(2,1)S(1)}, bf16[96,1024]{1,0:T(8,128)(2,1)}, u32[]{:S(2)}, u32[]{:S(2)}) collective-permute-start(bf16[96,1024]{1,0:T(8,128)(2,1)S(1)} %collective-permute-done.1.refs_2_), channel_id=1, source_target_pairs={{0,2},{1,3},{2,0},{3,1},{4,6},{5,7},{6,4},{7,5},{8,10},{9,11},{10,... | collective-permute-start | bytes 589832 | tf_op jit(solution)/shard_map/ppermute | solution.py:43
  44.4 17.7 %collective-permute-start.6 = (bf16[96,1024]{1,0:T(8,128)(2,1)S(1)}, bf16[96,1024]{1,0:T(8,128)(2,1)}, u32[]{:S(2)}, u32[]{:S(2)}) collective-permute-start(bf16[96,1024]{1,0:T(8,128)(2,1)S(1)} %collective-permute-done.2.refs_3_), channel_id=1, source_target_pairs={{0,2},{1,3},{2,0},{3,1},{4,6},{5,7},{6,4},{7,5},{8,10},{9,11},{10,... | collective-permute-start | bytes 589832 | tf_op jit(solution)/shard_map/ppermute | solution.py:43
  50.7 13.2 %copy-start.15 = (f32[8,128]{1,0:T(8,128)}, f32[8,128]{1,0:T(8,128)S(1)}, u32[]{:S(2)}) copy-start(f32[8,128]{1,0:T(8,128)S(1)} %get-tuple-element.39.refs_1_) | copy-start | bytes 12292
  64.8 14.0 %copy-start.18 = (s32[16]{0:T(128)S(1)}, s32[16]{0:T(128)}, u32[]{:S(2)}) copy-start(s32[16]{0:T(128)} %perm_ref.5) | copy-start | bytes 196
  64.8 76.2 %all-to-all-start = ((bf16[16,32,1792]{2,1,0:T(8,128)(2,1)}), bf16[16,32,1792]{2,1,0:T(8,128)(2,1)S(1)}, u32[]{:S(2)}, u32[]{:S(2)}) async-start(bf16[16,32,1792]{2,1,0:T(8,128)(2,1)} %bitcast.15), calls=%async_computation | async-start | bytes 3670016 | tf_op jit(solution)/shard_map/all_to_all | solution.py:342
  73.9 2.6 %collective-permute-start.14 = (bf16[4,96,1024]{2,1,0:T(8,128)(2,1)}, bf16[4,96,1024]{2,1,0:T(8,128)(2,1)S(1)}, u32[]{:S(2)}, u32[]{:S(2)}) collective-permute-start(bf16[4,96,1024]{2,1,0:T(8,128)(2,1)} %copy-done), channel_id=1, source_target_pairs={{0,1},{1,0},{2,3},{3,2},{4,5},{5,4},{6,7},{7,6},{8,9},{9,8},{10,11... | collective-permute-start | bytes 2359304 | tf_op jit(solution)/shard_map/ppermute | solution.py:43
  74.3 4.4 %collective-permute-start.15 = (bf16[4,96,1024]{2,1,0:T(8,128)(2,1)}, bf16[4,96,1024]{2,1,0:T(8,128)(2,1)S(1)}, u32[]{:S(2)}, u32[]{:S(2)}) collective-permute-start(bf16[4,96,1024]{2,1,0:T(8,128)(2,1)} %copy-done.2), channel_id=1, source_target_pairs={{0,1},{1,0},{2,3},{3,2},{4,5},{5,4},{6,7},{7,6},{8,9},{9,8},{10,11... | collective-permute-start | bytes 2359304 | tf_op jit(solution)/shard_map/ppermute | solution.py:43
  74.5 11.6 %collective-permute-start.19 = (bf16[4,96,1024]{2,1,0:T(8,128)(2,1)S(1)}, bf16[4,96,1024]{2,1,0:T(8,128)(2,1)S(1)}, u32[]{:S(2)}, u32[]{:S(2)}) collective-permute-start(bf16[4,96,1024]{2,1,0:T(8,128)(2,1)S(1)} %get-tuple-element.53.refs_0_), channel_id=1, source_target_pairs={{0,1},{1,0},{2,3},{3,2},{4,5},{5,4},{6,7},{7,6},{8,9},{9,8},{10,11... | collective-permute-start | bytes 2359304 | tf_op jit(solution)/shard_map/ppermute | solution.py:43
  74.8 11.2 %collective-permute-start.20 = (bf16[4,96,1024]{2,1,0:T(8,128)(2,1)S(1)}, bf16[4,96,1024]{2,1,0:T(8,128)(2,1)S(1)}, u32[]{:S(2)}, u32[]{:S(2)}) collective-permute-start(bf16[4,96,1024]{2,1,0:T(8,128)(2,1)S(1)} %get-tuple-element.54.refs_1_), channel_id=1, source_target_pairs={{0,1},{1,0},{2,3},{3,2},{4,5},{5,4},{6,7},{7,6},{8,9},{9,8},{10,11... | collective-permute-start | bytes 2359304 | tf_op jit(solution)/shard_map/ppermute | solution.py:43
  81.7 57.8 %copy-start.21 = (bf16[96,1024]{1,0:T(8,128)(2,1)}, bf16[96,1024]{1,0:T(8,128)(2,1)S(1)}, u32[]{:S(2)}) copy-start(bf16[96,1024]{1,0:T(8,128)(2,1)S(1)} %get-tuple-element.48.refs_0_) | copy-start | bytes 589828
  81.8 57.1 %collective-permute-start.16 = (bf16[96,1024]{1,0:T(8,128)(2,1)S(1)}, bf16[96,1024]{1,0:T(8,128)(2,1)S(1)}, u32[]{:S(2)}, u32[]{:S(2)}) collective-permute-start(bf16[96,1024]{1,0:T(8,128)(2,1)S(1)} %get-tuple-element.49), channel_id=1, source_target_pairs={{0,8},{1,9},{2,10},{3,11},{4,12},{5,13},{6,14},{7,15},{8,0},{9,1},... | collective-permute-start | bytes 589832 | tf_op jit(solution)/shard_map/ppermute | solution.py:37
  84.6 55.0 %collective-permute-start.17 = (bf16[96,1024]{1,0:T(8,128)(2,1)S(1)}, bf16[96,1024]{1,0:T(8,128)(2,1)S(1)}, u32[]{:S(2)}, u32[]{:S(2)}) collective-permute-start(bf16[96,1024]{1,0:T(8,128)(2,1)S(1)} %get-tuple-element.50), channel_id=1, source_target_pairs={{0,12},{1,13},{2,14},{3,15},{4,8},{5,9},{6,10},{7,11},{8,4},{9,5},... | collective-permute-start | bytes 589832 | tf_op jit(solution)/shard_map/ppermute | solution.py:37
  86.0 54.2 %collective-permute-start.18 = (bf16[96,1024]{1,0:T(8,128)(2,1)S(1)}, bf16[96,1024]{1,0:T(8,128)(2,1)S(1)}, u32[]{:S(2)}, u32[]{:S(2)}) collective-permute-start(bf16[96,1024]{1,0:T(8,128)(2,1)S(1)} %get-tuple-element.51), channel_id=1, source_target_pairs={{0,4},{1,5},{2,6},{3,7},{4,0},{5,1},{6,2},{7,3},{8,12},{9,13},{10,... | collective-permute-start | bytes 589832 | tf_op jit(solution)/shard_map/ppermute | solution.py:37
  88.3 60.0 %collective-permute-start.21 = (bf16[96,1024]{1,0:T(8,128)(2,1)}, bf16[96,1024]{1,0:T(8,128)(2,1)S(1)}, u32[]{:S(2)}, u32[]{:S(2)}) collective-permute-start(bf16[96,1024]{1,0:T(8,128)(2,1)} %get-tuple-element.56), channel_id=1, source_target_pairs={{0,8},{1,9},{2,10},{3,11},{4,12},{5,13},{6,14},{7,15},{8,0},{9,1},... | collective-permute-start | bytes 589832 | tf_op jit(solution)/shard_map/ppermute | solution.py:37
  91.2 57.8 %collective-permute-start.22 = (bf16[96,1024]{1,0:T(8,128)(2,1)}, bf16[96,1024]{1,0:T(8,128)(2,1)S(1)}, u32[]{:S(2)}, u32[]{:S(2)}) collective-permute-start(bf16[96,1024]{1,0:T(8,128)(2,1)} %get-tuple-element.57), channel_id=1, source_target_pairs={{0,12},{1,13},{2,14},{3,15},{4,8},{5,9},{6,10},{7,11},{8,4},{9,5},... | collective-permute-start | bytes 589832 | tf_op jit(solution)/shard_map/ppermute | solution.py:37
  139.6 10.4 %collective-permute-start.23 = (bf16[96,1024]{1,0:T(8,128)(2,1)}, bf16[96,1024]{1,0:T(8,128)(2,1)S(1)}, u32[]{:S(2)}, u32[]{:S(2)}) collective-permute-start(bf16[96,1024]{1,0:T(8,128)(2,1)} %get-tuple-element.58), channel_id=1, source_target_pairs={{0,4},{1,5},{2,6},{3,7},{4,0},{5,1},{6,2},{7,3},{8,12},{9,13},{10,... | collective-permute-start | bytes 589832 | tf_op jit(solution)/shard_map/ppermute | solution.py:37
  155.0 30.9 %copy-start.19 = (f32[256]{0:T(256)S(1)}, f32[256]{0:T(256)}, u32[]{:S(2)}) copy-start(f32[256]{0:T(256)} %param.19) | copy-start | bytes 3076
  155.0 30.9 %copy-start.20 = (s32[1,256]{1,0:T(1,128)S(1)}, s32[1,256]{1,0:T(1,128)}, u32[]{:S(2)}) copy-start(s32[1,256]{1,0:T(1,128)} %get-tuple-element.61.slot_ref) | copy-start | bytes 3076
  (22 other events, 43.4 us)

commit v7 on v2

--- a/solution.py
+++ b/solution.py
@@ -43,7 +43,7 @@
     ]
 
 
-def slot_rows(route, live, groups, capacity, perm_ref):
+def slot_rows(route, live, groups, capacity, me_ref, perm_ref):
     rows = route.shape[1]
     experts = lax.broadcasted_iota(jnp.int32, (groups, rows), 0)
     onehot = jnp.where((experts == route) & live, 1.0, 0.0).astype(BF16)
@@ -52,10 +52,10 @@
     upto = jnp.where(before <= after, 1.0, 0.0).astype(BF16)
     ranks = jnp.dot(onehot, upto, preferred_element_type=F32)
     rank = jnp.sum(ranks * onehot.astype(F32), axis=0, keepdims=True).astype(jnp.int32) - 1
-    target = jnp.zeros_like(route)
+    partner = jnp.zeros_like(route)
     for e in range(groups):
-        target = jnp.where(route == e, perm_ref[e], target)
-    return jnp.where(live, target * capacity + rank, -1)
+        partner = jnp.where(route == e, perm_ref[e] ^ me_ref[0], partner)
+    return jnp.where(live, partner * capacity + rank, -1)
 
 
 def selector_of(slot, slots):
@@ -64,43 +64,56 @@
     return jnp.where(places == slot, 1.0, 0.0).astype(BF16)
 
 
-def pack_kernel(groups, live_ref, perm_ref, *refs):
-    sources, (packed_ref, slot_ref), held, sem = refs[:5], refs[5:7], refs[7:12], refs[12]
-    fetched(sources, held, sem)
+def pack_kernel(groups, live_ref, me_ref, perm_ref, *refs):
+    sources, pieces, slot_ref = refs[:5], refs[6 : 6 + groups], refs[6 + groups]
+    held, sem = refs[7 + groups : 12 + groups], refs[-1]
     route_ref, fwd_route_ref, hidden_ref, out_ref, fwd_ref = held
+    copies = [pltpu.make_async_copy(ref, room, sem.at[n]) for n, (ref, room) in enumerate(zip(sources, held))]
+    for copy in copies:
+        copy.start()
     rows, ff = hidden_ref.shape
     d = out_ref.shape[1]
-    capacity = packed_ref.shape[0] // groups
+    capacity = pieces[0].shape[0]
+    slots = groups * capacity
     place = lax.broadcasted_iota(jnp.int32, (1, rows), 1)
-    slot = slot_rows(route_ref[...], place < live_ref[0], groups, capacity, perm_ref)
-    selector = selector_of(slot, groups * capacity)
-    packed_ref[:, :ff] = jnp.dot(selector, hidden_ref[...], preferred_element_type=F32).astype(BF16)
-    packed_ref[:, ff : ff + d] = jnp.dot(selector, out_ref[...], preferred_element_type=F32).astype(BF16)
-    fwd_slot = slot_rows(fwd_route_ref[...], place >= 0, groups, capacity, perm_ref)
+
+    def fill(first, selector, source_ref):
+        chosen = jnp.dot(selector, source_ref[...], preferred_element_type=F32).astype(BF16)
+        for s, piece in zip(mixed_order(groups), pieces):
+            piece[:, first : first + source_ref.shape[1]] = chosen[s * capacity : (s + 1) * capacity]
+
+    copies[0].wait()
+    slot = slot_rows(route_ref[...], place < live_ref[0], groups, capacity, me_ref, perm_ref)
+    selector = selector_of(slot, slots)
+    copies[1].wait()
+    fwd_slot = slot_rows(fwd_route_ref[...], place >= 0, groups, capacity, me_ref, perm_ref)
     slot_ref[...] = fwd_slot
-    fwd_selector = selector_of(fwd_slot, groups * capacity)
-    packed_ref[:, ff + d :] = jnp.dot(fwd_selector, fwd_ref[...], preferred_element_type=F32).astype(BF16)
-
-
-def pack_rows(live_rows, perm, route, fwd_route, hidden, grad_out, fwd_hidden, groups, capacity):
+    copies[2].wait()
+    fill(0, selector, hidden_ref)
+    copies[3].wait()
+    fill(ff, selector, out_ref)
+    copies[4].wait()
+    fill(ff + d, selector_of(fwd_slot, slots), fwd_ref)
+
+
+def pack_rows(live_rows, me, perm, route, fwd_route, hidden, grad_out, fwd_hidden, earlier, groups, capacity):
     rows, ff = hidden.shape
     width = 2 * ff + grad_out.shape[1]
     sources = (route.reshape(1, rows), fwd_route.reshape(1, rows), hidden, grad_out, fwd_hidden)
-    return pl.pallas_call(
+    *pieces, slot = pl.pallas_call(
         functools.partial(pack_kernel, groups),
-        out_shape=(
-            jax.ShapeDtypeStruct((groups * capacity, width), BF16),
-            jax.ShapeDtypeStruct((1, rows), jnp.int32),
-        ),
-        in_specs=[SMEM, SMEM] + [HBM] * 5,
-        out_specs=(VMEM, VMEM),
-        scratch_shapes=rooms(sources),
-        compiler_params=pltpu.CompilerParams(vmem_limit_bytes=60 * MIB),
+        out_shape=(jax.ShapeDtypeStruct((capacity, width), BF16),) * groups
+        + (jax.ShapeDtypeStruct((1, rows), jnp.int32),),
+        in_specs=[SMEM] * 3 + [HBM] * 5 + [VMEM],
+        out_specs=(VMEM,) * (groups + 1),
+        scratch_shapes=[pltpu.VMEM(a.shape, a.dtype) for a in sources] + [pltpu.SemaphoreType.DMA((len(sources),))],
+        compiler_params=pltpu.CompilerParams(vmem_limit_bytes=32 * MIB),
         cost_estimate=pl.CostEstimate(
             flops=2 * groups * capacity * rows * width, bytes_accessed=6 * rows * width, transcendentals=0
         ),
         name="pack_rows",
-    )(live_rows, perm, *sources)
+    )(live_rows, me, perm, *sources, earlier)
+    return pieces, slot
 
 
 def split_kernel(me_ref, moment_ref, weight_ref, *refs):
@@ -128,8 +141,8 @@
 
 
 def reorder_kernel(me_ref, perm_ref, *refs):
-    groups = (len(refs) - 1) // 2
-    sources, targets, held = refs[:groups], refs[groups : 2 * groups], refs[-1]
+    groups = len(refs) // 2 - 1
+    sources, targets, held = refs[:groups], refs[groups + 1 : 2 * groups + 1], refs[-1]
     me, order = me_ref[0], mixed_order(groups)
     for s, source in zip(order, sources):
         held[me ^ perm_ref[me ^ s]] = source[...]
@@ -137,31 +150,35 @@
         target[...] = held[s]
 
 
-def reorder(me, perm, pieces):
+def reorder(me, perm, pieces, earlier):
     groups = len(pieces)
     piece = jax.ShapeDtypeStruct(pieces[0].shape, BF16)
     return pl.pallas_call(
         reorder_kernel,
         out_shape=(piece,) * groups,
-        in_specs=[SMEM, SMEM] + [VMEM] * groups,
+        in_specs=[SMEM, SMEM] + [VMEM] * (groups + 1),
         out_specs=(VMEM,) * groups,
         scratch_shapes=[pltpu.VMEM((groups,) + pieces[0].shape, BF16)],
         compiler_params=pltpu.CompilerParams(vmem_limit_bytes=32 * MIB),
         cost_estimate=pl.CostEstimate(flops=0, bytes_accessed=4 * groups * pieces[0].size, transcendentals=0),
         name="reorder",
-    )(me, perm, *pieces)
-
-
-def update_kernel(groups, me_ref, packed_ref, *refs):
-    pieces = refs[:groups]
-    weight_new_ref, moment_new_ref, produced_ref, held = refs[groups:]
+    )(me, perm, *pieces, earlier)
+
+
+def update_kernel(groups, me_ref, *refs):
+    packed, pieces, produced = refs[:groups], refs[groups : 2 * groups], refs[2 * groups + 2 : 3 * groups + 2]
+    weight_new_ref, moment_new_ref = refs[2 * groups : 2 * groups + 2]
+    held, rows_ref = refs[-2:]
     _, ff, d = held.shape
+    capacity = packed[0].shape[0]
+    for n, piece in enumerate(packed):
+        rows_ref[n * capacity : (n + 1) * capacity] = piece[...]
     for s, piece in zip(mixed_order(groups), pieces):
         rows, columns = piece.shape[1:]
         for lead in range(2):
             chunk_at(held, lead, me_ref[0] ^ s, rows, columns)[...] = piece[lead]
     grad = lax.dot_general(
-        packed_ref[:, :ff], packed_ref[:, ff : ff + d], (((0,), (0,)), ((), ())), preferred_element_type=F32
+        rows_ref[:, :ff], rows_ref[:, ff : ff + d], (((0,), (0,)), ((), ())), preferred_element_type=F32
     )
     moment_new = (moment_decay * held[0].astype(F32) + grad).astype(BF16)
     moment_new_ref[...] = moment_new
@@ -179,32 +196,40 @@
         ).astype(BF16)
     weight_new = (held[1].astype(F32) - step_scale * current.astype(F32)).astype(BF16)
     weight_new_ref[...] = weight_new
-    produced_ref[...] = jnp.dot(packed_ref[:, ff + d :], weight_new, preferred_element_type=F32).astype(BF16)
+    product = jnp.dot(rows_ref[:, ff + d :], weight_new, preferred_element_type=F32).astype(BF16)
+    for n, piece in enumerate(produced):
+        piece[...] = product[n * capacity : (n + 1) * capacity]
 
 
 def update(me, packed, pieces, ff, d):
     groups = len(pieces)
-    slots = packed.shape[0]
+    capacity, width = packed[0].shape
+    slots = groups * capacity
     shape = jax.ShapeDtypeStruct((ff, d), BF16)
-    return pl.pallas_call(
+    weight_new, moment_new, *produced = pl.pallas_call(
         functools.partial(update_kernel, groups),
-        out_shape=(shape, shape, jax.ShapeDtypeStruct((slots, d), BF16)),
-        in_specs=[SMEM] + [VMEM] * (1 + groups),
-        out_specs=(VMEM,) * 3,
-        scratch_shapes=[pltpu.VMEM((2, ff, d), BF16)],
-        compiler_params=pltpu.CompilerParams(vmem_limit_bytes=48 * MIB),
+        out_shape=(shape, shape) + (jax.ShapeDtypeStruct((capacity, d), BF16),) * groups,
+        in_specs=[SMEM] + [VMEM] * (2 * groups),
+        out_specs=(VMEM,) * (groups + 2),
+        scratch_shapes=[pltpu.VMEM((2, ff, d), BF16), pltpu.VMEM((slots, width), BF16)],
+        compiler_params=pltpu.CompilerParams(vmem_limit_bytes=40 * MIB),
         cost_estimate=pl.CostEstimate(
             flops=4 * ff * d * slots + 8 * ff * ff * d + 4 * ff**3,
-            bytes_accessed=8 * ff * d + 2 * packed.size + 2 * slots * d,
+            bytes_accessed=8 * ff * d + 2 * slots * (width + d),
             transcendentals=1,
         ),
         name="update",
-    )(me, packed, *pieces)
-
-
-def finish_kernel(slot_ref, gate_ref, returned_ref, out_ref):
+    )(me, *packed, *pieces)
+    return weight_new, moment_new, produced
+
+
+def finish_kernel(groups, slot_ref, gate_ref, *refs):
+    pieces, (out_ref, returned_ref) = refs[:groups], refs[groups:]
+    capacity = pieces[0].shape[0]
+    for s, piece in zip(mixed_order(groups), pieces):
+        returned_ref[s * capacity : (s + 1) * capacity] = piece[...]
     rows = slot_ref.shape[1]
-    selector = selector_of(slot_ref[...], returned_ref.shape[0])
+    selector = selector_of(slot_ref[...], groups * capacity)
     expert_out = lax.dot_general(
         selector, returned_ref[...], (((0,), (0,)), ((), ())), preferred_element_type=F32
     )
@@ -215,23 +240,22 @@
 
 
 def finish(slot, gate, returned):
+    groups = len(returned)
     rows = slot.shape[1]
-    slots, d = returned.shape
+    capacity, d = returned[0].shape
+    slots = groups * capacity
     return pl.pallas_call(
-        finish_kernel,
+        functools.partial(finish_kernel, groups),
         out_shape=jax.ShapeDtypeStruct((rows, d), BF16),
-        in_specs=[VMEM] * 3,
+        in_specs=[VMEM] * (2 + groups),
         out_specs=VMEM,
+        scratch_shapes=[pltpu.VMEM((slots, d), BF16)],
         compiler_params=pltpu.CompilerParams(vmem_limit_bytes=32 * MIB),
         cost_estimate=pl.CostEstimate(
             flops=2 * slots * rows * d, bytes_accessed=2 * d * (slots + rows), transcendentals=0
         ),
         name="finish",
-    )(slot, gate.reshape(1, rows), returned)
-
-
-def exchange(array):
-    return lax.all_to_all(array, "expert", split_axis=0, concat_axis=0, tiled=True)
+    )(slot, gate.reshape(1, rows), *returned)
 
 
 def mixed_order(groups):
@@ -256,13 +280,13 @@
     ff, d = w_down.shape[1:]
     spread = swap(split(me, w_moment, w_down, groups))
     packed, fwd_slot = pack_rows(
-        live_rows, perm, grad_route, fwd_route, grad_hidden, grad_out, fwd_hidden, groups, capacity
-    )
-    received = exchange(packed.reshape(groups, capacity, -1)).reshape(groups * capacity, -1)
-    placed = swap(reorder(me, perm, spread))
+        live_rows, me, perm, grad_route, fwd_route, grad_hidden, grad_out, fwd_hidden,
+        spread[2 * groups // 3], groups, capacity,
+    )
+    received = swap(packed)
+    placed = swap(reorder(me, perm, spread, received[groups // 3]))
     weight_new, moment_new, produced = update(me, received, placed, ff, d)
-    returned = exchange(produced.reshape(groups, capacity, d)).reshape(groups * capacity, d)
-    return weight_new[None], moment_new[None], finish(fwd_slot, fwd_gate, returned)
+    return weight_new[None], moment_new[None], finish(fwd_slot, fwd_gate, swap(produced))
 
 
 def lookup(route_ids, mapping):

time: 164 us -> 152 us (0.927)
  starting transfers between devices: 48.8 us -> 113 us
  waiting for transfers between devices: 67.4 us -> 23.8 us
  blocking collectives: 30.4 us -> 0 us
  Pallas kernels: 14.1 us -> 12.1 us
    ppermute x30 -> x60, starting transfers between devices: 41.4 us -> 113 us  [swap(): lax.ppermute(piece, 'expert', [(i, i ^ s) for i in range(groups)])]
    ppermute x30 -> x60, waiting for transfers between devices: 67.4 us -> 23.8 us  [swap(): lax.ppermute(piece, 'expert', [(i, i ^ s) for i in range(groups)])]
    all_to_all x1 -> x0, blocking collectives: 30.4 us -> none  [exchange(): lax.all_to_all(array, 'expert', split_axis=0, concat_axis=0, tiled=True)]
    all_to_all x1 -> x0, starting transfers between devices: 7.38 us -> none  [exchange(): lax.all_to_all(array, 'expert', split_axis=0, concat_axis=0, tiled=True)]
  transfers between devices with their start and end apart: 31 -> 60, of which waited for: 13 -> 17; matrix products, arithmetic and copies ran while one was open for 0% -> 0% of each run, Pallas kernels for 2% -> 2%
where the time goes in v7:
time: 152 us
  starting transfers between devices  113 us (74%)
  waiting for transfers between devices  23.8 us (16%)
  Pallas kernels  12.1 us (8%)
    ppermute x60, starting transfers between devices, swap(): lax.ppermute(piece, 'expert', [(i, i ^ s) for i in range(groups)])  113 us
    ppermute x60, waiting for transfers between devices, swap(): lax.ppermute(piece, 'expert', [(i, i ^ s) for i in range(groups)])  23.8 us
    pallas_call x1, Pallas kernels, update(): pl.pallas_call(functools.partial(update_kernel, groups), out_shape=(shape...  4.74 us
  transfers between devices with their start and end apart: 60, of which 17 were waited for; matrix products, arithmetic and copies ran while one was open for 0% of the time, Pallas kernels for 2%

profile of v7, /device:TPU:0, one launch (start us, length us, event | category | flops | bytes accessed | tf_op | source)
XLA Modules:
  0.0 151.9 jit_solution(4328806743957006762)
XLA Ops:
  0.7 2.7 %split.1 = (bf16[2,48,512]{2,1,0:T(8,128)(2,1)}, bf16[2,48,512]{2,1,0:T(8,128)(2,1)}, bf16[2,48,512]{2,1,0:T(8,128)(2,1)}, bf16[2,48,512]{2,1,0:T(8,128)(2,1)}, ...) custom-call(s32[1]{0:T(128)} %bitcast.me_ref, ...), custom_call_target="tpu_custom_call" | custom-call | bytes 3145728 | tf_op jit(solution)/shard_map/split/pallas_call | solution.py:131
  3.4 2.5 %collective-permute-start = (bf16[2,48,512]{2,1,0:T(8,128)(2,1)}, bf16[2,48,512]{2,1,0:T(8,128)(2,1)S(1)}, u32[]{:S(2)}, u32[]{:S(2)}) collective-permute-start(bf16[2,48,512]{2,1,0:T(8,128)(2,1)} %get-tuple-element.70), channel_id=1, source_target_pairs={{0,3},{1,2},{2,1},{3,0},{4,7},{5,6},{6,5},{7,4},{8,11},{9,10},{10,... | collective-permute-start | bytes 294920 | tf_op jit(solution)/shard_map/ppermute | solution.py:270
  5.9 2.6 %collective-permute-start.16 = (bf16[2,48,512]{2,1,0:T(8,128)(2,1)}, bf16[2,48,512]{2,1,0:T(8,128)(2,1)S(1)}, u32[]{:S(2)}, u32[]{:S(2)}) collective-permute-start(bf16[2,48,512]{2,1,0:T(8,128)(2,1)} %get-tuple-element.88), channel_id=1, source_target_pairs={{0,8},{1,9},{2,10},{3,11},{4,12},{5,13},{6,14},{7,15},{8,0},{9,1},... | collective-permute-start | bytes 294920 | tf_op jit(solution)/shard_map/ppermute | solution.py:270
  11.4 2.7 %collective-permute-start.20 = (bf16[2,48,512]{2,1,0:T(8,128)(2,1)}, bf16[2,48,512]{2,1,0:T(8,128)(2,1)S(1)}, u32[]{:S(2)}, u32[]{:S(2)}) collective-permute-start(bf16[2,48,512]{2,1,0:T(8,128)(2,1)} %get-tuple-element.92), channel_id=1, source_target_pairs={{0,10},{1,11},{2,8},{3,9},{4,14},{5,15},{6,12},{7,13},{8,2},{9,3},... | collective-permute-start | bytes 294920 | tf_op jit(solution)/shard_map/ppermute | solution.py:270
  14.8 2.0 %collective-permute-start.21 = (bf16[2,48,512]{2,1,0:T(8,128)(2,1)}, bf16[2,48,512]{2,1,0:T(8,128)(2,1)S(1)}, u32[]{:S(2)}, u32[]{:S(2)}) collective-permute-start(bf16[2,48,512]{2,1,0:T(8,128)(2,1)} %get-tuple-element.93), channel_id=1, source_target_pairs={{0,5},{1,4},{2,7},{3,6},{4,1},{5,0},{6,3},{7,2},{8,13},{9,12},{10,... | collective-permute-start | bytes 294920 | tf_op jit(solution)/shard_map/ppermute | solution.py:270
  23.8 2.7 %collective-permute-start.25 = (bf16[2,48,512]{2,1,0:T(8,128)(2,1)}, bf16[2,48,512]{2,1,0:T(8,128)(2,1)S(1)}, u32[]{:S(2)}, u32[]{:S(2)}) collective-permute-start(bf16[2,48,512]{2,1,0:T(8,128)(2,1)} %get-tuple-element.97), channel_id=1, source_target_pairs={{0,13},{1,12},{2,15},{3,14},{4,9},{5,8},{6,11},{7,10},{8,5},{9,4},... | collective-permute-start | bytes 294920 | tf_op jit(solution)/shard_map/ppermute | solution.py:270
  27.7 3.8 %collective-permute-start.27 = (bf16[2,48,512]{2,1,0:T(8,128)(2,1)}, bf16[2,48,512]{2,1,0:T(8,128)(2,1)S(1)}, u32[]{:S(2)}, u32[]{:S(2)}) collective-permute-start(bf16[2,48,512]{2,1,0:T(8,128)(2,1)} %get-tuple-element.99), channel_id=1, source_target_pairs={{0,14},{1,15},{2,12},{3,13},{4,10},{5,11},{6,8},{7,9},{8,6},{9,7},... | collective-permute-start | bytes 294920 | tf_op jit(solution)/shard_map/ppermute | solution.py:270
  33.9 2.7 %pack_rows.1 = (bf16[32,1792]{1,0:T(8,128)(2,1)S(1)}, bf16[32,1792]{1,0:T(8,128)(2,1)S(1)}, bf16[32,1792]{1,0:T(8,128)(2,1)S(1)}, bf16[32,1792]{1,0:T(8,128)(2,1...) custom-call(s32[1]{0:T(128)S(6)} %copy.13.live_ref, ...), custom_call_target="tpu_custom_call" | custom-call | flops 469762048 | bytes 2752512 | tf_op jit(solution)/shard_map/pack_rows/pallas_call | solution.py:103
  36.6 7.7 %collective-permute-start.1 = (bf16[32,1792]{1,0:T(8,128)(2,1)S(1)}, bf16[32,1792]{1,0:T(8,128)(2,1)S(1)}, u32[]{:S(2)}, u32[]{:S(2)}) collective-permute-start(bf16[32,1792]{1,0:T(8,128)(2,1)S(1)} %get-tuple-element.72), channel_id=1, source_target_pairs={{0,8},{1,9},{2,10},{3,11},{4,12},{5,13},{6,14},{7,15},{8,0},{9,1},... | collective-permute-start | bytes 344072 | tf_op jit(solution)/shard_map/ppermute | solution.py:270
  45.6 2.5 %collective-permute-start.3 = (bf16[32,1792]{1,0:T(8,128)(2,1)S(1)}, bf16[32,1792]{1,0:T(8,128)(2,1)S(1)}, u32[]{:S(2)}, u32[]{:S(2)}) collective-permute-start(bf16[32,1792]{1,0:T(8,128)(2,1)S(1)} %get-tuple-element.74), channel_id=1, source_target_pairs={{0,9},{1,8},{2,11},{3,10},{4,13},{5,12},{6,15},{7,14},{8,1},{9,0},... | collective-permute-start | bytes 344072 | tf_op jit(solution)/shard_map/ppermute | solution.py:270
  50.9 4.0 %collective-permute-start.7 = (bf16[32,1792]{1,0:T(8,128)(2,1)S(1)}, bf16[32,1792]{1,0:T(8,128)(2,1)S(1)}, u32[]{:S(2)}, u32[]{:S(2)}) collective-permute-start(bf16[32,1792]{1,0:T(8,128)(2,1)S(1)} %get-tuple-element.78), channel_id=1, source_target_pairs={{0,11},{1,10},{2,9},{3,8},{4,15},{5,14},{6,13},{7,12},{8,3},{9,2},... | collective-permute-start | bytes 344072 | tf_op jit(solution)/shard_map/ppermute | solution.py:270
  55.0 2.2 %collective-permute-start.8 = (bf16[32,1792]{1,0:T(8,128)(2,1)S(1)}, bf16[32,1792]{1,0:T(8,128)(2,1)S(1)}, u32[]{:S(2)}, u32[]{:S(2)}) collective-permute-start(bf16[32,1792]{1,0:T(8,128)(2,1)S(1)} %get-tuple-element.79), channel_id=1, source_target_pairs={{0,4},{1,5},{2,6},{3,7},{4,0},{5,1},{6,2},{7,3},{8,12},{9,13},{10,... | collective-permute-start | bytes 344072 | tf_op jit(solution)/shard_map/ppermute | solution.py:270
  57.2 3.1 %collective-permute-start.9 = (bf16[32,1792]{1,0:T(8,128)(2,1)S(1)}, bf16[32,1792]{1,0:T(8,128)(2,1)S(1)}, u32[]{:S(2)}, u32[]{:S(2)}) collective-permute-start(bf16[32,1792]{1,0:T(8,128)(2,1)S(1)} %get-tuple-element.80), channel_id=1, source_target_pairs={{0,12},{1,13},{2,14},{3,15},{4,8},{5,9},{6,10},{7,11},{8,4},{9,5},... | collective-permute-start | bytes 344072 | tf_op jit(solution)/shard_map/ppermute | solution.py:270
  61.2 4.2 %collective-permute-start.11 = (bf16[32,1792]{1,0:T(8,128)(2,1)S(1)}, bf16[32,1792]{1,0:T(8,128)(2,1)S(1)}, u32[]{:S(2)}, u32[]{:S(2)}) collective-permute-start(bf16[32,1792]{1,0:T(8,128)(2,1)S(1)} %get-tuple-element.82), channel_id=1, source_target_pairs={{0,13},{1,12},{2,15},{3,14},{4,9},{5,8},{6,11},{7,10},{8,5},{9,4},... | collective-permute-start | bytes 344072 | tf_op jit(solution)/shard_map/ppermute | solution.py:270
  66.7 3.5 %collective-permute-start.13 = (bf16[32,1792]{1,0:T(8,128)(2,1)S(1)}, bf16[32,1792]{1,0:T(8,128)(2,1)S(1)}, u32[]{:S(2)}, u32[]{:S(2)}) collective-permute-start(bf16[32,1792]{1,0:T(8,128)(2,1)S(1)} %get-tuple-element.84), channel_id=1, source_target_pairs={{0,14},{1,15},{2,12},{3,13},{4,10},{5,11},{6,8},{7,9},{8,6},{9,7},... | collective-permute-start | bytes 344072 | tf_op jit(solution)/shard_map/ppermute | solution.py:270
  73.1 8.4 %collective-permute-start.30 = (bf16[2,48,512]{2,1,0:T(8,128)(2,1)S(1)}, bf16[2,48,512]{2,1,0:T(8,128)(2,1)S(1)}, u32[]{:S(2)}, u32[]{:S(2)}) collective-permute-start(bf16[2,48,512]{2,1,0:T(8,128)(2,1)S(1)} %get-tuple-element.103), channel_id=1, source_target_pairs={{0,8},{1,9},{2,10},{3,11},{4,12},{5,13},{6,14},{7,15},{8,0},{9,1},... | collective-permute-start | bytes 294920 | tf_op jit(solution)/shard_map/ppermute | solution.py:270
  81.5 3.2 %collective-permute-start.32 = (bf16[2,48,512]{2,1,0:T(8,128)(2,1)S(1)}, bf16[2,48,512]{2,1,0:T(8,128)(2,1)S(1)}, u32[]{:S(2)}, u32[]{:S(2)}) collective-permute-start(bf16[2,48,512]{2,1,0:T(8,128)(2,1)S(1)} %get-tuple-element.105), channel_id=1, source_target_pairs={{0,9},{1,8},{2,11},{3,10},{4,13},{5,12},{6,15},{7,14},{8,1},{9,0},... | collective-permute-start | bytes 294920 | tf_op jit(solution)/shard_map/ppermute | solution.py:270
  84.7 5.1 %collective-permute-start.34 = (bf16[2,48,512]{2,1,0:T(8,128)(2,1)S(1)}, bf16[2,48,512]{2,1,0:T(8,128)(2,1)S(1)}, u32[]{:S(2)}, u32[]{:S(2)}) collective-permute-start(bf16[2,48,512]{2,1,0:T(8,128)(2,1)S(1)} %get-tuple-element.107), channel_id=1, source_target_pairs={{0,10},{1,11},{2,8},{3,9},{4,14},{5,15},{6,12},{7,13},{8,2},{9,3},... | collective-permute-start | bytes 294920 | tf_op jit(solution)/shard_map/ppermute | solution.py:270
  91.4 4.1 %collective-permute-start.36 = (bf16[2,48,512]{2,1,0:T(8,128)(2,1)S(1)}, bf16[2,48,512]{2,1,0:T(8,128)(2,1)S(1)}, u32[]{:S(2)}, u32[]{:S(2)}) collective-permute-start(bf16[2,48,512]{2,1,0:T(8,128)(2,1)S(1)} %get-tuple-element.109), channel_id=1, source_target_pairs={{0,11},{1,10},{2,9},{3,8},{4,15},{5,14},{6,13},{7,12},{8,3},{9,2},... | collective-permute-start | bytes 294920 | tf_op jit(solution)/shard_map/ppermute | solution.py:270
  95.5 2.5 %collective-permute-start.38 = (bf16[2,48,512]{2,1,0:T(8,128)(2,1)S(1)}, bf16[2,48,512]{2,1,0:T(8,128)(2,1)S(1)}, u32[]{:S(2)}, u32[]{:S(2)}) collective-permute-start(bf16[2,48,512]{2,1,0:T(8,128)(2,1)S(1)} %get-tuple-element.111), channel_id=1, source_target_pairs={{0,12},{1,13},{2,14},{3,15},{4,8},{5,9},{6,10},{7,11},{8,4},{9,5},... | collective-permute-start | bytes 294920 | tf_op jit(solution)/shard_map/ppermute | solution.py:270
  98.0 2.7 %collective-permute-done.34.refs_21_ = bf16[2,48,512]{2,1,0:T(8,128)(2,1)S(1)} collective-permute-done((bf16[2,48,512]{2,1,0:T(8,128)(2,1)S(1)}, bf16[2,48,512]{2,1,0:T(8,128)(2,1)S(1)}, u32[]{:S(2)}, u32[]{:S(2)}) %collective-permute-start.34) | collective-permute-done | bytes 98336 | tf_op jit(solution)/shard_map/ppermute | solution.py:270
  102.1 2.9 %collective-permute-done.36.refs_23_ = bf16[2,48,512]{2,1,0:T(8,128)(2,1)S(1)} collective-permute-done((bf16[2,48,512]{2,1,0:T(8,128)(2,1)S(1)}, bf16[2,48,512]{2,1,0:T(8,128)(2,1)S(1)}, u32[]{:S(2)}, u32[]{:S(2)}) %collective-permute-start.36) | collective-permute-done | bytes 98336 | tf_op jit(solution)/shard_map/ppermute | solution.py:270
  105.2 2.0 %collective-permute-start.42 = (bf16[2,48,512]{2,1,0:T(8,128)(2,1)S(1)}, bf16[2,48,512]{2,1,0:T(8,128)(2,1)S(1)}, u32[]{:S(2)}, u32[]{:S(2)}) collective-permute-start(bf16[2,48,512]{2,1,0:T(8,128)(2,1)S(1)} %get-tuple-element.115), channel_id=1, source_target_pairs={{0,14},{1,15},{2,12},{3,13},{4,10},{5,11},{6,8},{7,9},{8,6},{9,7},... | collective-permute-start | bytes 294920 | tf_op jit(solution)/shard_map/ppermute | solution.py:270
  107.3 2.8 %collective-permute-start.44 = (bf16[2,48,512]{2,1,0:T(8,128)(2,1)S(1)}, bf16[2,48,512]{2,1,0:T(8,128)(2,1)S(1)}, u32[]{:S(2)}, u32[]{:S(2)}) collective-permute-start(bf16[2,48,512]{2,1,0:T(8,128)(2,1)S(1)} %get-tuple-element.117), channel_id=1, source_target_pairs={{0,15},{1,14},{2,13},{3,12},{4,11},{5,10},{6,9},{7,8},{8,7},{9,6},... | collective-permute-start | bytes 294920 | tf_op jit(solution)/shard_map/ppermute | solution.py:270
  110.1 2.7 %collective-permute-done.42.refs_29_ = bf16[2,48,512]{2,1,0:T(8,128)(2,1)S(1)} collective-permute-done((bf16[2,48,512]{2,1,0:T(8,128)(2,1)S(1)}, bf16[2,48,512]{2,1,0:T(8,128)(2,1)S(1)}, u32[]{:S(2)}, u32[]{:S(2)}) %collective-permute-start.42) | collective-permute-done | bytes 98336 | tf_op jit(solution)/shard_map/ppermute | solution.py:270
  114.6 4.7 %update.1 = (bf16[384,1024]{1,0:T(8,128)(2,1)}, bf16[384,1024]{1,0:T(8,128)(2,1)}, bf16[32,1024]{1,0:T(8,128)(2,1)S(1)}, bf16[32,1024]{1,0:T(8,128)(2,1)S(1)}, b...) custom-call(s32[1]{0:T(128)} %bitcast.me_ref, ...), custom_call_target="tpu_custom_call" | custom-call | flops 2239758336 | bytes 6029312 | tf_op jit(solution)/shard_map/update/pallas_call | solution.py:209
  119.3 6.7 %collective-permute-start.45 = (bf16[32,1024]{1,0:T(8,128)(2,1)S(1)}, bf16[32,1024]{1,0:T(8,128)(2,1)S(1)}, u32[]{:S(2)}, u32[]{:S(2)}) collective-permute-start(bf16[32,1024]{1,0:T(8,128)(2,1)S(1)} %get-tuple-element.122), channel_id=1, source_target_pairs={{0,8},{1,9},{2,10},{3,11},{4,12},{5,13},{6,14},{7,15},{8,0},{9,1},... | collective-permute-start | bytes 196616 | tf_op jit(solution)/shard_map/ppermute | solution.py:270
  128.7 2.2 %collective-permute-start.49 = (bf16[32,1024]{1,0:T(8,128)(2,1)S(1)}, bf16[32,1024]{1,0:T(8,128)(2,1)S(1)}, u32[]{:S(2)}, u32[]{:S(2)}) collective-permute-start(bf16[32,1024]{1,0:T(8,128)(2,1)S(1)} %get-tuple-element.126), channel_id=1, source_target_pairs={{0,10},{1,11},{2,8},{3,9},{4,14},{5,15},{6,12},{7,13},{8,2},{9,3},... | collective-permute-start | bytes 196616 | tf_op jit(solution)/shard_map/ppermute | solution.py:270
  140.6 2.7 %collective-permute-start.57 = (bf16[32,1024]{1,0:T(8,128)(2,1)S(1)}, bf16[32,1024]{1,0:T(8,128)(2,1)S(1)}, u32[]{:S(2)}, u32[]{:S(2)}) collective-permute-start(bf16[32,1024]{1,0:T(8,128)(2,1)S(1)} %get-tuple-element.134), channel_id=1, source_target_pairs={{0,14},{1,15},{2,12},{3,13},{4,10},{5,11},{6,8},{7,9},{8,6},{9,7},... | collective-permute-start | bytes 196616 | tf_op jit(solution)/shard_map/ppermute | solution.py:270
  143.3 2.2 %collective-permute-start.59 = (bf16[32,1024]{1,0:T(8,128)(2,1)S(1)}, bf16[32,1024]{1,0:T(8,128)(2,1)S(1)}, u32[]{:S(2)}, u32[]{:S(2)}) collective-permute-start(bf16[32,1024]{1,0:T(8,128)(2,1)S(1)} %get-tuple-element.136), channel_id=1, source_target_pairs={{0,15},{1,14},{2,13},{3,12},{4,11},{5,10},{6,9},{7,8},{8,7},{9,6},... | collective-permute-start | bytes 196616 | tf_op jit(solution)/shard_map/ppermute | solution.py:270
  145.5 2.2 %collective-permute-done.57.refs_13_ = bf16[32,1024]{1,0:T(8,128)(2,1)S(1)} collective-permute-done((bf16[32,1024]{1,0:T(8,128)(2,1)S(1)}, bf16[32,1024]{1,0:T(8,128)(2,1)S(1)}, u32[]{:S(2)}, u32[]{:S(2)}) %collective-permute-start.57) | collective-permute-done | bytes 65568 | tf_op jit(solution)/shard_map/ppermute | solution.py:270
  147.7 2.3 %collective-permute-done.59.refs_15_ = bf16[32,1024]{1,0:T(8,128)(2,1)S(1)} collective-permute-done((bf16[32,1024]{1,0:T(8,128)(2,1)S(1)}, bf16[32,1024]{1,0:T(8,128)(2,1)S(1)}, u32[]{:S(2)}, u32[]{:S(2)}) %collective-permute-start.59) | collective-permute-done | bytes 65568 | tf_op jit(solution)/shard_map/ppermute | solution.py:270
  (109 shorter events, 42.1 us)
Async XLA Ops:
  10.2 10.5 %collective-permute-start.19 = (bf16[2,48,512]{2,1,0:T(8,128)(2,1)}, bf16[2,48,512]{2,1,0:T(8,128)(2,1)S(1)}, u32[]{:S(2)}, u32[]{:S(2)}) collective-permute-start(bf16[2,48,512]{2,1,0:T(8,128)(2,1)} %get-tuple-element.91), channel_id=1, source_target_pairs={{0,6},{1,7},{2,4},{3,5},{4,2},{5,3},{6,0},{7,1},{8,14},{9,15},{10,... | collective-permute-start | bytes 294920 | tf_op jit(solution)/shard_map/ppermute | solution.py:270
  11.4 12.4 %collective-permute-start.20 = (bf16[2,48,512]{2,1,0:T(8,128)(2,1)}, bf16[2,48,512]{2,1,0:T(8,128)(2,1)S(1)}, u32[]{:S(2)}, u32[]{:S(2)}) collective-permute-start(bf16[2,48,512]{2,1,0:T(8,128)(2,1)} %get-tuple-element.92), channel_id=1, source_target_pairs={{0,10},{1,11},{2,8},{3,9},{4,14},{5,15},{6,12},{7,13},{8,2},{9,3},... | collective-permute-start | bytes 294920 | tf_op jit(solution)/shard_map/ppermute | solution.py:270
  14.8 11.7 %collective-permute-start.21 = (bf16[2,48,512]{2,1,0:T(8,128)(2,1)}, bf16[2,48,512]{2,1,0:T(8,128)(2,1)S(1)}, u32[]{:S(2)}, u32[]{:S(2)}) collective-permute-start(bf16[2,48,512]{2,1,0:T(8,128)(2,1)} %get-tuple-element.93), channel_id=1, source_target_pairs={{0,5},{1,4},{2,7},{3,6},{4,1},{5,0},{6,3},{7,2},{8,13},{9,12},{10,... | collective-permute-start | bytes 294920 | tf_op jit(solution)/shard_map/ppermute | solution.py:270
  16.9 10.8 %collective-permute-start.22 = (bf16[2,48,512]{2,1,0:T(8,128)(2,1)}, bf16[2,48,512]{2,1,0:T(8,128)(2,1)S(1)}, u32[]{:S(2)}, u32[]{:S(2)}) collective-permute-start(bf16[2,48,512]{2,1,0:T(8,128)(2,1)} %get-tuple-element.94), channel_id=1, source_target_pairs={{0,11},{1,10},{2,9},{3,8},{4,15},{5,14},{6,13},{7,12},{8,3},{9,2},... | collective-permute-start | bytes 294920 | tf_op jit(solution)/shard_map/ppermute | solution.py:270
  18.7 12.8 %collective-permute-start.23 = (bf16[2,48,512]{2,1,0:T(8,128)(2,1)}, bf16[2,48,512]{2,1,0:T(8,128)(2,1)S(1)}, u32[]{:S(2)}, u32[]{:S(2)}) collective-permute-start(bf16[2,48,512]{2,1,0:T(8,128)(2,1)} %get-tuple-element.95), channel_id=1, source_target_pairs={{0,4},{1,5},{2,6},{3,7},{4,0},{5,1},{6,2},{7,3},{8,12},{9,13},{10,... | collective-permute-start | bytes 294920 | tf_op jit(solution)/shard_map/ppermute | solution.py:270
  20.7 10.9 %collective-permute-start.24 = (bf16[2,48,512]{2,1,0:T(8,128)(2,1)}, bf16[2,48,512]{2,1,0:T(8,128)(2,1)S(1)}, u32[]{:S(2)}, u32[]{:S(2)}) collective-permute-start(bf16[2,48,512]{2,1,0:T(8,128)(2,1)} %get-tuple-element.96), channel_id=1, source_target_pairs={{0,12},{1,13},{2,14},{3,15},{4,8},{5,9},{6,10},{7,11},{8,4},{9,5},... | collective-permute-start | bytes 294920 | tf_op jit(solution)/shard_map/ppermute | solution.py:270
  23.8 12.8 %collective-permute-start.25 = (bf16[2,48,512]{2,1,0:T(8,128)(2,1)}, bf16[2,48,512]{2,1,0:T(8,128)(2,1)S(1)}, u32[]{:S(2)}, u32[]{:S(2)}) collective-permute-start(bf16[2,48,512]{2,1,0:T(8,128)(2,1)} %get-tuple-element.97), channel_id=1, source_target_pairs={{0,13},{1,12},{2,15},{3,14},{4,9},{5,8},{6,11},{7,10},{8,5},{9,4},... | collective-permute-start | bytes 294920 | tf_op jit(solution)/shard_map/ppermute | solution.py:270
  26.6 17.8 %collective-permute-start.26 = (bf16[2,48,512]{2,1,0:T(8,128)(2,1)}, bf16[2,48,512]{2,1,0:T(8,128)(2,1)S(1)}, u32[]{:S(2)}, u32[]{:S(2)}) collective-permute-start(bf16[2,48,512]{2,1,0:T(8,128)(2,1)} %get-tuple-element.98), channel_id=1, source_target_pairs={{0,2},{1,3},{2,0},{3,1},{4,6},{5,7},{6,4},{7,5},{8,10},{9,11},{10,... | collective-permute-start | bytes 294920 | tf_op jit(solution)/shard_map/ppermute | solution.py:270
  27.7 17.9 %collective-permute-start.27 = (bf16[2,48,512]{2,1,0:T(8,128)(2,1)}, bf16[2,48,512]{2,1,0:T(8,128)(2,1)S(1)}, u32[]{:S(2)}, u32[]{:S(2)}) collective-permute-start(bf16[2,48,512]{2,1,0:T(8,128)(2,1)} %get-tuple-element.99), channel_id=1, source_target_pairs={{0,14},{1,15},{2,12},{3,13},{4,10},{5,11},{6,8},{7,9},{8,6},{9,7},... | collective-permute-start | bytes 294920 | tf_op jit(solution)/shard_map/ppermute | solution.py:270
  31.6 16.6 %collective-permute-start.28 = (bf16[2,48,512]{2,1,0:T(8,128)(2,1)}, bf16[2,48,512]{2,1,0:T(8,128)(2,1)S(1)}, u32[]{:S(2)}, u32[]{:S(2)}) collective-permute-start(bf16[2,48,512]{2,1,0:T(8,128)(2,1)} %get-tuple-element.100), channel_id=1, source_target_pairs={{0,1},{1,0},{2,3},{3,2},{4,5},{5,4},{6,7},{7,6},{8,9},{9,8},{10,11... | collective-permute-start | bytes 294920 | tf_op jit(solution)/shard_map/ppermute | solution.py:270
  31.6 16.7 %collective-permute-start.29 = (bf16[2,48,512]{2,1,0:T(8,128)(2,1)}, bf16[2,48,512]{2,1,0:T(8,128)(2,1)S(1)}, u32[]{:S(2)}, u32[]{:S(2)}) collective-permute-start(bf16[2,48,512]{2,1,0:T(8,128)(2,1)} %get-tuple-element.101), channel_id=1, source_target_pairs={{0,15},{1,14},{2,13},{3,12},{4,11},{5,10},{6,9},{7,8},{8,7},{9,6},... | collective-permute-start | bytes 294920 | tf_op jit(solution)/shard_map/ppermute | solution.py:270
  36.6 13.7 %collective-permute-start.1 = (bf16[32,1792]{1,0:T(8,128)(2,1)S(1)}, bf16[32,1792]{1,0:T(8,128)(2,1)S(1)}, u32[]{:S(2)}, u32[]{:S(2)}) collective-permute-start(bf16[32,1792]{1,0:T(8,128)(2,1)S(1)} %get-tuple-element.72), channel_id=1, source_target_pairs={{0,8},{1,9},{2,10},{3,11},{4,12},{5,13},{6,14},{7,15},{8,0},{9,1},... | collective-permute-start | bytes 344072 | tf_op jit(solution)/shard_map/ppermute | solution.py:270
  48.3 12.0 %collective-permute-start.5 = (bf16[32,1792]{1,0:T(8,128)(2,1)S(1)}, bf16[32,1792]{1,0:T(8,128)(2,1)S(1)}, u32[]{:S(2)}, u32[]{:S(2)}) collective-permute-start(bf16[32,1792]{1,0:T(8,128)(2,1)S(1)} %get-tuple-element.76), channel_id=1, source_target_pairs={{0,10},{1,11},{2,8},{3,9},{4,14},{5,15},{6,12},{7,13},{8,2},{9,3},... | collective-permute-start | bytes 344072 | tf_op jit(solution)/shard_map/ppermute | solution.py:270
  50.3 10.9 %collective-permute-start.6 = (bf16[32,1792]{1,0:T(8,128)(2,1)S(1)}, bf16[32,1792]{1,0:T(8,128)(2,1)S(1)}, u32[]{:S(2)}, u32[]{:S(2)}) collective-permute-start(bf16[32,1792]{1,0:T(8,128)(2,1)S(1)} %get-tuple-element.77), channel_id=1, source_target_pairs={{0,5},{1,4},{2,7},{3,6},{4,1},{5,0},{6,3},{7,2},{8,13},{9,12},{10,... | collective-permute-start | bytes 344072 | tf_op jit(solution)/shard_map/ppermute | solution.py:270
  50.9 14.5 %collective-permute-start.7 = (bf16[32,1792]{1,0:T(8,128)(2,1)S(1)}, bf16[32,1792]{1,0:T(8,128)(2,1)S(1)}, u32[]{:S(2)}, u32[]{:S(2)}) collective-permute-start(bf16[32,1792]{1,0:T(8,128)(2,1)S(1)} %get-tuple-element.78), channel_id=1, source_target_pairs={{0,11},{1,10},{2,9},{3,8},{4,15},{5,14},{6,13},{7,12},{8,3},{9,2},... | collective-permute-start | bytes 344072 | tf_op jit(solution)/shard_map/ppermute | solution.py:270
  55.0 11.8 %collective-permute-start.8 = (bf16[32,1792]{1,0:T(8,128)(2,1)S(1)}, bf16[32,1792]{1,0:T(8,128)(2,1)S(1)}, u32[]{:S(2)}, u32[]{:S(2)}) collective-permute-start(bf16[32,1792]{1,0:T(8,128)(2,1)S(1)} %get-tuple-element.79), channel_id=1, source_target_pairs={{0,4},{1,5},{2,6},{3,7},{4,0},{5,1},{6,2},{7,3},{8,12},{9,13},{10,... | collective-permute-start | bytes 344072 | tf_op jit(solution)/shard_map/ppermute | solution.py:270
  57.2 13.1 %collective-permute-start.9 = (bf16[32,1792]{1,0:T(8,128)(2,1)S(1)}, bf16[32,1792]{1,0:T(8,128)(2,1)S(1)}, u32[]{:S(2)}, u32[]{:S(2)}) collective-permute-start(bf16[32,1792]{1,0:T(8,128)(2,1)S(1)} %get-tuple-element.80), channel_id=1, source_target_pairs={{0,12},{1,13},{2,14},{3,15},{4,8},{5,9},{6,10},{7,11},{8,4},{9,5},... | collective-permute-start | bytes 344072 | tf_op jit(solution)/shard_map/ppermute | solution.py:270
  60.2 10.1 %collective-permute-start.10 = (bf16[32,1792]{1,0:T(8,128)(2,1)S(1)}, bf16[32,1792]{1,0:T(8,128)(2,1)S(1)}, u32[]{:S(2)}, u32[]{:S(2)}) collective-permute-start(bf16[32,1792]{1,0:T(8,128)(2,1)S(1)} %get-tuple-element.81), channel_id=1, source_target_pairs={{0,3},{1,2},{2,1},{3,0},{4,7},{5,6},{6,5},{7,4},{8,11},{9,10},{10,... | collective-permute-start | bytes 344072 | tf_op jit(solution)/shard_map/ppermute | solution.py:270
  61.2 11.9 %collective-permute-start.11 = (bf16[32,1792]{1,0:T(8,128)(2,1)S(1)}, bf16[32,1792]{1,0:T(8,128)(2,1)S(1)}, u32[]{:S(2)}, u32[]{:S(2)}) collective-permute-start(bf16[32,1792]{1,0:T(8,128)(2,1)S(1)} %get-tuple-element.82), channel_id=1, source_target_pairs={{0,13},{1,12},{2,15},{3,14},{4,9},{5,8},{6,11},{7,10},{8,5},{9,4},... | collective-permute-start | bytes 344072 | tf_op jit(solution)/shard_map/ppermute | solution.py:270
  65.4 16.2 %collective-permute-start.12 = (bf16[32,1792]{1,0:T(8,128)(2,1)S(1)}, bf16[32,1792]{1,0:T(8,128)(2,1)S(1)}, u32[]{:S(2)}, u32[]{:S(2)}) collective-permute-start(bf16[32,1792]{1,0:T(8,128)(2,1)S(1)} %get-tuple-element.83), channel_id=1, source_target_pairs={{0,2},{1,3},{2,0},{3,1},{4,6},{5,7},{6,4},{7,5},{8,10},{9,11},{10,... | collective-permute-start | bytes 344072 | tf_op jit(solution)/shard_map/ppermute | solution.py:270
  66.7 14.8 %collective-permute-start.13 = (bf16[32,1792]{1,0:T(8,128)(2,1)S(1)}, bf16[32,1792]{1,0:T(8,128)(2,1)S(1)}, u32[]{:S(2)}, u32[]{:S(2)}) collective-permute-start(bf16[32,1792]{1,0:T(8,128)(2,1)S(1)} %get-tuple-element.84), channel_id=1, source_target_pairs={{0,14},{1,15},{2,12},{3,13},{4,10},{5,11},{6,8},{7,9},{8,6},{9,7},... | collective-permute-start | bytes 344072 | tf_op jit(solution)/shard_map/ppermute | solution.py:270
  70.3 14.5 %collective-permute-start.14 = (bf16[32,1792]{1,0:T(8,128)(2,1)S(1)}, bf16[32,1792]{1,0:T(8,128)(2,1)S(1)}, u32[]{:S(2)}, u32[]{:S(2)}) collective-permute-start(bf16[32,1792]{1,0:T(8,128)(2,1)S(1)} %get-tuple-element.85), channel_id=1, source_target_pairs={{0,1},{1,0},{2,3},{3,2},{4,5},{5,4},{6,7},{7,6},{8,9},{9,8},{10,11... | collective-permute-start | bytes 344072 | tf_op jit(solution)/shard_map/ppermute | solution.py:270
  70.3 14.4 %collective-permute-start.15 = (bf16[32,1792]{1,0:T(8,128)(2,1)S(1)}, bf16[32,1792]{1,0:T(8,128)(2,1)S(1)}, u32[]{:S(2)}, u32[]{:S(2)}) collective-permute-start(bf16[32,1792]{1,0:T(8,128)(2,1)S(1)} %get-tuple-element.86), channel_id=1, source_target_pairs={{0,15},{1,14},{2,13},{3,12},{4,11},{5,10},{6,9},{7,8},{8,7},{9,6},... | collective-permute-start | bytes 344072 | tf_op jit(solution)/shard_map/ppermute | solution.py:270
  73.1 18.2 %collective-permute-start.30 = (bf16[2,48,512]{2,1,0:T(8,128)(2,1)S(1)}, bf16[2,48,512]{2,1,0:T(8,128)(2,1)S(1)}, u32[]{:S(2)}, u32[]{:S(2)}) collective-permute-start(bf16[2,48,512]{2,1,0:T(8,128)(2,1)S(1)} %get-tuple-element.103), channel_id=1, source_target_pairs={{0,8},{1,9},{2,10},{3,11},{4,12},{5,13},{6,14},{7,15},{8,0},{9,1},... | collective-permute-start | bytes 294920 | tf_op jit(solution)/shard_map/ppermute | solution.py:270
  81.5 9.8 %collective-permute-start.31 = (bf16[2,48,512]{2,1,0:T(8,128)(2,1)S(1)}, bf16[2,48,512]{2,1,0:T(8,128)(2,1)S(1)}, u32[]{:S(2)}, u32[]{:S(2)}) collective-permute-start(bf16[2,48,512]{2,1,0:T(8,128)(2,1)S(1)} %get-tuple-element.104), channel_id=1, source_target_pairs={{0,7},{1,6},{2,5},{3,4},{4,3},{5,2},{6,1},{7,0},{8,15},{9,14},{10,... | collective-permute-start | bytes 294920 | tf_op jit(solution)/shard_map/ppermute | solution.py:270
  81.5 13.9 %collective-permute-start.32 = (bf16[2,48,512]{2,1,0:T(8,128)(2,1)S(1)}, bf16[2,48,512]{2,1,0:T(8,128)(2,1)S(1)}, u32[]{:S(2)}, u32[]{:S(2)}) collective-permute-start(bf16[2,48,512]{2,1,0:T(8,128)(2,1)S(1)} %get-tuple-element.105), channel_id=1, source_target_pairs={{0,9},{1,8},{2,11},{3,10},{4,13},{5,12},{6,15},{7,14},{8,1},{9,0},... | collective-permute-start | bytes 294920 | tf_op jit(solution)/shard_map/ppermute | solution.py:270
  84.7 10.7 %collective-permute-start.33 = (bf16[2,48,512]{2,1,0:T(8,128)(2,1)S(1)}, bf16[2,48,512]{2,1,0:T(8,128)(2,1)S(1)}, u32[]{:S(2)}, u32[]{:S(2)}) collective-permute-start(bf16[2,48,512]{2,1,0:T(8,128)(2,1)S(1)} %get-tuple-element.106), channel_id=1, source_target_pairs={{0,6},{1,7},{2,4},{3,5},{4,2},{5,3},{6,0},{7,1},{8,14},{9,15},{10,... | collective-permute-start | bytes 294920 | tf_op jit(solution)/shard_map/ppermute | solution.py:270
  84.7 16.0 %collective-permute-start.34 = (bf16[2,48,512]{2,1,0:T(8,128)(2,1)S(1)}, bf16[2,48,512]{2,1,0:T(8,128)(2,1)S(1)}, u32[]{:S(2)}, u32[]{:S(2)}) collective-permute-start(bf16[2,48,512]{2,1,0:T(8,128)(2,1)S(1)} %get-tuple-element.107), channel_id=1, source_target_pairs={{0,10},{1,11},{2,8},{3,9},{4,14},{5,15},{6,12},{7,13},{8,2},{9,3},... | collective-permute-start | bytes 294920 | tf_op jit(solution)/shard_map/ppermute | solution.py:270
  91.4 13.6 %collective-permute-start.36 = (bf16[2,48,512]{2,1,0:T(8,128)(2,1)S(1)}, bf16[2,48,512]{2,1,0:T(8,128)(2,1)S(1)}, u32[]{:S(2)}, u32[]{:S(2)}) collective-permute-start(bf16[2,48,512]{2,1,0:T(8,128)(2,1)S(1)} %get-tuple-element.109), channel_id=1, source_target_pairs={{0,11},{1,10},{2,9},{3,8},{4,15},{5,14},{6,13},{7,12},{8,3},{9,2},... | collective-permute-start | bytes 294920 | tf_op jit(solution)/shard_map/ppermute | solution.py:270
  95.4 9.8 %collective-permute-start.37 = (bf16[2,48,512]{2,1,0:T(8,128)(2,1)S(1)}, bf16[2,48,512]{2,1,0:T(8,128)(2,1)S(1)}, u32[]{:S(2)}, u32[]{:S(2)}) collective-permute-start(bf16[2,48,512]{2,1,0:T(8,128)(2,1)S(1)} %get-tuple-element.110), channel_id=1, source_target_pairs={{0,4},{1,5},{2,6},{3,7},{4,0},{5,1},{6,2},{7,3},{8,12},{9,13},{10,... | collective-permute-start | bytes 294920 | tf_op jit(solution)/shard_map/ppermute | solution.py:270
  95.5 11.8 %collective-permute-start.38 = (bf16[2,48,512]{2,1,0:T(8,128)(2,1)S(1)}, bf16[2,48,512]{2,1,0:T(8,128)(2,1)S(1)}, u32[]{:S(2)}, u32[]{:S(2)}) collective-permute-start(bf16[2,48,512]{2,1,0:T(8,128)(2,1)S(1)} %get-tuple-element.111), channel_id=1, source_target_pairs={{0,12},{1,13},{2,14},{3,15},{4,8},{5,9},{6,10},{7,11},{8,4},{9,5},... | collective-permute-start | bytes 294920 | tf_op jit(solution)/shard_map/ppermute | solution.py:270
  119.3 11.6 %collective-permute-start.45 = (bf16[32,1024]{1,0:T(8,128)(2,1)S(1)}, bf16[32,1024]{1,0:T(8,128)(2,1)S(1)}, u32[]{:S(2)}, u32[]{:S(2)}) collective-permute-start(bf16[32,1024]{1,0:T(8,128)(2,1)S(1)} %get-tuple-element.122), channel_id=1, source_target_pairs={{0,8},{1,9},{2,10},{3,11},{4,12},{5,13},{6,14},{7,15},{8,0},{9,1},... | collective-permute-start | bytes 196616 | tf_op jit(solution)/shard_map/ppermute | solution.py:270
  (36 other events, 359.9 us)

commit v8 on v7

--- a/solution.py
+++ b/solution.py
@@ -65,9 +65,9 @@
 
 
 def pack_kernel(groups, live_ref, me_ref, perm_ref, *refs):
-    sources, pieces, slot_ref = refs[:5], refs[6 : 6 + groups], refs[6 + groups]
-    held, sem = refs[7 + groups : 12 + groups], refs[-1]
-    route_ref, fwd_route_ref, hidden_ref, out_ref, fwd_ref = held
+    sources, pieces, (slot_ref, gates_ref) = refs[:6], refs[7 : 7 + groups], refs[7 + groups : 9 + groups]
+    held, sem = refs[9 + groups : 15 + groups], refs[-1]
+    route_ref, fwd_route_ref, hidden_ref, out_ref, fwd_ref, gate_ref = held
     copies = [pltpu.make_async_copy(ref, room, sem.at[n]) for n, (ref, room) in enumerate(zip(sources, held))]
     for copy in copies:
         copy.start()
@@ -94,18 +94,22 @@
     fill(ff, selector, out_ref)
     copies[4].wait()
     fill(ff + d, selector_of(fwd_slot, slots), fwd_ref)
-
-
-def pack_rows(live_rows, me, perm, route, fwd_route, hidden, grad_out, fwd_hidden, earlier, groups, capacity):
+    copies[5].wait()
+    down = lax.broadcasted_iota(jnp.int32, (rows, rows), 0)
+    across = lax.broadcasted_iota(jnp.int32, (rows, rows), 1)
+    gates_ref[...] = jnp.sum(jnp.where(down == across, gate_ref[...], 0.0), axis=1, keepdims=True)
+
+
+def pack_rows(live_rows, me, perm, route, fwd_route, hidden, grad_out, fwd_hidden, gate, earlier, groups, capacity):
     rows, ff = hidden.shape
     width = 2 * ff + grad_out.shape[1]
-    sources = (route.reshape(1, rows), fwd_route.reshape(1, rows), hidden, grad_out, fwd_hidden)
-    *pieces, slot = pl.pallas_call(
+    sources = (route.reshape(1, rows), fwd_route.reshape(1, rows), hidden, grad_out, fwd_hidden, gate.reshape(1, rows))
+    *pieces, slot, gates = pl.pallas_call(
         functools.partial(pack_kernel, groups),
         out_shape=(jax.ShapeDtypeStruct((capacity, width), BF16),) * groups
-        + (jax.ShapeDtypeStruct((1, rows), jnp.int32),),
-        in_specs=[SMEM] * 3 + [HBM] * 5 + [VMEM],
-        out_specs=(VMEM,) * (groups + 1),
+        + (jax.ShapeDtypeStruct((1, rows), jnp.int32), jax.ShapeDtypeStruct((rows, 1), F32)),
+        in_specs=[SMEM] * 3 + [HBM] * 6 + [VMEM],
+        out_specs=(VMEM,) * (groups + 2),
         scratch_shapes=[pltpu.VMEM(a.shape, a.dtype) for a in sources] + [pltpu.SemaphoreType.DMA((len(sources),))],
         compiler_params=pltpu.CompilerParams(vmem_limit_bytes=32 * MIB),
         cost_estimate=pl.CostEstimate(
@@ -113,7 +117,7 @@
         ),
         name="pack_rows",
     )(live_rows, me, perm, *sources, earlier)
-    return pieces, slot
+    return pieces, slot, gates
 
 
 def split_kernel(me_ref, moment_ref, weight_ref, *refs):
@@ -146,7 +150,7 @@
     me, order = me_ref[0], mixed_order(groups)
     for s, source in zip(order, sources):
         held[me ^ perm_ref[me ^ s]] = source[...]
-    for s, target in zip(order, targets):
+    for s, target in zip(return_order(groups), targets):
         target[...] = held[s]
 
 
@@ -165,22 +169,43 @@
     )(me, perm, *pieces, earlier)
 
 
-def update_kernel(groups, me_ref, *refs):
-    packed, pieces, produced = refs[:groups], refs[groups : 2 * groups], refs[2 * groups + 2 : 3 * groups + 2]
-    weight_new_ref, moment_new_ref = refs[2 * groups : 2 * groups + 2]
-    held, rows_ref = refs[-2:]
-    _, ff, d = held.shape
-    capacity = packed[0].shape[0]
-    for n, piece in enumerate(packed):
-        rows_ref[n * capacity : (n + 1) * capacity] = piece[...]
-    for s, piece in zip(mixed_order(groups), pieces):
+def gradient_kernel(groups, *refs):
+    pieces, (grad_ref, fwd_ref, rows_ref) = refs[:groups], refs[groups:]
+    ff, d = grad_ref.shape
+    capacity = pieces[0].shape[0]
+    for n, piece in enumerate(pieces):
+        span = slice(n * capacity, (n + 1) * capacity)
+        rows_ref[span] = piece[:, : ff + d]
+        fwd_ref[span] = piece[:, ff + d :]
+    grad_ref[...] = lax.dot_general(
+        rows_ref[:, :ff], rows_ref[:, ff:], (((0,), (0,)), ((), ())), preferred_element_type=F32
+    )
+
+
+def gradient(pieces, ff, d):
+    groups = len(pieces)
+    slots = groups * pieces[0].shape[0]
+    return pl.pallas_call(
+        functools.partial(gradient_kernel, groups),
+        out_shape=(jax.ShapeDtypeStruct((ff, d), F32), jax.ShapeDtypeStruct((slots, ff), BF16)),
+        in_specs=[VMEM] * groups,
+        out_specs=(VMEM, VMEM),
+        scratch_shapes=[pltpu.VMEM((slots, ff + d), BF16)],
+        compiler_params=pltpu.CompilerParams(vmem_limit_bytes=32 * MIB),
+        cost_estimate=pl.CostEstimate(
+            flops=2 * ff * d * slots, bytes_accessed=4 * ff * d + 4 * slots * (ff + d), transcendentals=0
+        ),
+        name="gradient",
+    )(*pieces)
+
+
+def update_kernel(groups, me_ref, grad_ref, fwd_ref, *refs):
+    pieces, (weight_new_ref, moment_new_ref, *produced), held = refs[:groups], refs[groups:-1], refs[-1]
+    for s, piece in zip(return_order(groups), pieces):
         rows, columns = piece.shape[1:]
         for lead in range(2):
             chunk_at(held, lead, me_ref[0] ^ s, rows, columns)[...] = piece[lead]
-    grad = lax.dot_general(
-        rows_ref[:, :ff], rows_ref[:, ff : ff + d], (((0,), (0,)), ((), ())), preferred_element_type=F32
-    )
-    moment_new = (moment_decay * held[0].astype(F32) + grad).astype(BF16)
+    moment_new = (moment_decay * held[0].astype(F32) + grad_ref[...]).astype(BF16)
     moment_new_ref[...] = moment_new
     moment_f = moment_new.astype(F32)
     frobenius = jnp.sqrt(jnp.sum(moment_f * moment_f))
@@ -196,50 +221,48 @@
         ).astype(BF16)
     weight_new = (held[1].astype(F32) - step_scale * current.astype(F32)).astype(BF16)
     weight_new_ref[...] = weight_new
-    product = jnp.dot(rows_ref[:, ff + d :], weight_new, preferred_element_type=F32).astype(BF16)
-    for n, piece in enumerate(produced):
+    product = jnp.dot(fwd_ref[...], weight_new, preferred_element_type=F32).astype(BF16)
+    capacity, came = produced[0].shape[0], mixed_order(groups)
+    for s, piece in zip(return_order(groups), produced):
+        n = came.index(s)
         piece[...] = product[n * capacity : (n + 1) * capacity]
 
 
-def update(me, packed, pieces, ff, d):
+def update(me, grad, fwd_rows, pieces):
     groups = len(pieces)
-    capacity, width = packed[0].shape
-    slots = groups * capacity
+    ff, d = grad.shape
+    slots = fwd_rows.shape[0]
     shape = jax.ShapeDtypeStruct((ff, d), BF16)
     weight_new, moment_new, *produced = pl.pallas_call(
         functools.partial(update_kernel, groups),
-        out_shape=(shape, shape) + (jax.ShapeDtypeStruct((capacity, d), BF16),) * groups,
-        in_specs=[SMEM] + [VMEM] * (2 * groups),
+        out_shape=(shape, shape) + (jax.ShapeDtypeStruct((slots // groups, d), BF16),) * groups,
+        in_specs=[SMEM] + [VMEM] * (2 + groups),
         out_specs=(VMEM,) * (groups + 2),
-        scratch_shapes=[pltpu.VMEM((2, ff, d), BF16), pltpu.VMEM((slots, width), BF16)],
+        scratch_shapes=[pltpu.VMEM((2, ff, d), BF16)],
         compiler_params=pltpu.CompilerParams(vmem_limit_bytes=40 * MIB),
         cost_estimate=pl.CostEstimate(
-            flops=4 * ff * d * slots + 8 * ff * ff * d + 4 * ff**3,
-            bytes_accessed=8 * ff * d + 2 * slots * (width + d),
+            flops=2 * ff * d * slots + 8 * ff * ff * d + 4 * ff**3,
+            bytes_accessed=12 * ff * d + 2 * slots * (ff + d),
             transcendentals=1,
         ),
         name="update",
-    )(me, *packed, *pieces)
+    )(me, grad, fwd_rows, *pieces)
     return weight_new, moment_new, produced
 
 
-def finish_kernel(groups, slot_ref, gate_ref, *refs):
+def finish_kernel(groups, slot_ref, gates_ref, *refs):
     pieces, (out_ref, returned_ref) = refs[:groups], refs[groups:]
     capacity = pieces[0].shape[0]
-    for s, piece in zip(mixed_order(groups), pieces):
+    for s, piece in zip(return_order(groups), pieces):
         returned_ref[s * capacity : (s + 1) * capacity] = piece[...]
-    rows = slot_ref.shape[1]
     selector = selector_of(slot_ref[...], groups * capacity)
     expert_out = lax.dot_general(
         selector, returned_ref[...], (((0,), (0,)), ((), ())), preferred_element_type=F32
     )
-    down = lax.broadcasted_iota(jnp.int32, (rows, rows), 0)
-    across = lax.broadcasted_iota(jnp.int32, (rows, rows), 1)
-    gate = jnp.sum(jnp.where(down == across, gate_ref[...], 0.0), axis=1, keepdims=True)
-    out_ref[...] = (gate * expert_out).astype(BF16)
-
-
-def finish(slot, gate, returned):
+    out_ref[...] = (gates_ref[...] * expert_out).astype(BF16)
+
+
+def finish(slot, gates, returned):
     groups = len(returned)
     rows = slot.shape[1]
     capacity, d = returned[0].shape
@@ -255,7 +278,7 @@
             flops=2 * slots * rows * d, bytes_accessed=2 * d * (slots + rows), transcendentals=0
         ),
         name="finish",
-    )(slot, gate.reshape(1, rows), *returned)
+    )(slot, gates, *returned)
 
 
 def mixed_order(groups):
@@ -263,11 +286,20 @@
     return [0] + [s for pair in zip(far, near + [None]) for s in pair if s is not None]
 
 
-def swap(pieces):
-    groups = len(pieces)
-    order = mixed_order(groups)
-    return [pieces[0]] + [
-        lax.ppermute(piece, "expert", [(i, i ^ s) for i in range(groups)]) for s, piece in zip(order[1:], pieces[1:])
+def return_order(groups):
+    far, near = list(range(groups // 2, groups)), list(range(groups // 2 - 1, 0, -1))
+    order = [0]
+    while far or near:
+        order += far[:2] + near[:1]
+        far, near = far[2:], near[1:]
+    return order
+
+
+def swap(pieces, order):
+    groups = lax.axis_size("expert")
+    return [
+        lax.ppermute(piece, "expert", [(i, i ^ s) for i in range(groups)]) if s else piece
+        for s, piece in zip(order, pieces)
     ]
 
 
@@ -278,15 +310,17 @@
     me = lax.axis_index("expert").astype(jnp.int32).reshape(1)
     capacity = max(4, 2 * grad_hidden.shape[0] // groups)
     ff, d = w_down.shape[1:]
-    spread = swap(split(me, w_moment, w_down, groups))
-    packed, fwd_slot = pack_rows(
-        live_rows, me, perm, grad_route, fwd_route, grad_hidden, grad_out, fwd_hidden,
+    spread = swap(split(me, w_moment, w_down, groups), mixed_order(groups))
+    packed, fwd_slot, gates = pack_rows(
+        live_rows, me, perm, grad_route, fwd_route, grad_hidden, grad_out, fwd_hidden, fwd_gate,
         spread[2 * groups // 3], groups, capacity,
     )
-    received = swap(packed)
-    placed = swap(reorder(me, perm, spread, received[groups // 3]))
-    weight_new, moment_new, produced = update(me, received, placed, ff, d)
-    return weight_new[None], moment_new[None], finish(fwd_slot, fwd_gate, swap(produced))
+    received = swap(packed, mixed_order(groups))
+    placed = swap(reorder(me, perm, spread, received[groups // 3]), return_order(groups))
+    grad, fwd_rows = gradient(received, ff, d)
+    weight_new, moment_new, produced = update(me, grad, fwd_rows, placed)
+    returned = swap(produced, return_order(groups))
+    return weight_new[None], moment_new[None], finish(fwd_slot, gates, returned)
 
 
 def lookup(route_ids, mapping):

time: 152 us -> 157 us (1.033)
  waiting for transfers between devices: 23.8 us -> 26.6 us
  starting transfers between devices: 113 us -> 115 us
    ppermute x60, waiting for transfers between devices: 23.8 us -> 26.6 us  [swap(): lax.ppermute(piece, 'expert', [(i, i ^ s) for i in range(groups)])]
    ppermute x60, starting transfers between devices: 113 us -> 115 us  [swap(): lax.ppermute(piece, 'expert', [(i, i ^ s) for i in range(groups)])]
  transfers between devices with their start and end apart: 60 -> 60, of which waited for: 17 -> 18; matrix products, arithmetic and copies ran while one was open for 0% -> 0% of each run, Pallas kernels for 2% -> 3%
where the time goes in v8:
time: 157 us
  starting transfers between devices  115 us (73%)
  waiting for transfers between devices  26.6 us (17%)
  Pallas kernels  13.2 us (8%)
    ppermute x60, starting transfers between devices, swap(): lax.ppermute(piece, 'expert', [(i, i ^ s) for i in range(groups)])  115 us
    ppermute x60, waiting for transfers between devices, swap(): lax.ppermute(piece, 'expert', [(i, i ^ s) for i in range(groups)])  26.6 us
    pallas_call x1, Pallas kernels, update(): pl.pallas_call(functools.partial(update_kernel, groups), out_shape=(shape...  5.03 us
  transfers between devices with their start and end apart: 60, of which 18 were waited for; matrix products, arithmetic and copies ran while one was open for 0% of the time, Pallas kernels for 3%

profile of v8, /device:TPU:0, one launch (start us, length us, event | category | flops | bytes accessed | tf_op | source)
XLA Modules:
  0.0 156.8 jit_solution(8113339380956887053)
XLA Ops:
  0.7 2.7 %split.1 = (bf16[2,48,512]{2,1,0:T(8,128)(2,1)}, bf16[2,48,512]{2,1,0:T(8,128)(2,1)}, bf16[2,48,512]{2,1,0:T(8,128)(2,1)}, bf16[2,48,512]{2,1,0:T(8,128)(2,1)}, ...) custom-call(s32[1]{0:T(128)} %bitcast.me_ref, ...), custom_call_target="tpu_custom_call" | custom-call | bytes 3145728 | tf_op jit(solution)/shard_map/split/pallas_call | solution.py:135
  3.5 2.5 %collective-permute-start = (bf16[2,48,512]{2,1,0:T(8,128)(2,1)}, bf16[2,48,512]{2,1,0:T(8,128)(2,1)S(1)}, u32[]{:S(2)}, u32[]{:S(2)}) collective-permute-start(bf16[2,48,512]{2,1,0:T(8,128)(2,1)} %get-tuple-element.73), channel_id=1, source_target_pairs={{0,3},{1,2},{2,1},{3,0},{4,7},{5,6},{6,5},{7,4},{8,11},{9,10},{10,... | collective-permute-start | bytes 294920 | tf_op jit(solution)/shard_map/ppermute | solution.py:301
  5.9 2.6 %collective-permute-start.16 = (bf16[2,48,512]{2,1,0:T(8,128)(2,1)}, bf16[2,48,512]{2,1,0:T(8,128)(2,1)S(1)}, u32[]{:S(2)}, u32[]{:S(2)}) collective-permute-start(bf16[2,48,512]{2,1,0:T(8,128)(2,1)} %get-tuple-element.93), channel_id=1, source_target_pairs={{0,8},{1,9},{2,10},{3,11},{4,12},{5,13},{6,14},{7,15},{8,0},{9,1},... | collective-permute-start | bytes 294920 | tf_op jit(solution)/shard_map/ppermute | solution.py:301
  11.5 2.7 %collective-permute-start.20 = (bf16[2,48,512]{2,1,0:T(8,128)(2,1)}, bf16[2,48,512]{2,1,0:T(8,128)(2,1)S(1)}, u32[]{:S(2)}, u32[]{:S(2)}) collective-permute-start(bf16[2,48,512]{2,1,0:T(8,128)(2,1)} %get-tuple-element.97), channel_id=1, source_target_pairs={{0,10},{1,11},{2,8},{3,9},{4,14},{5,15},{6,12},{7,13},{8,2},{9,3},... | collective-permute-start | bytes 294920 | tf_op jit(solution)/shard_map/ppermute | solution.py:301
  23.9 2.7 %collective-permute-start.25 = (bf16[2,48,512]{2,1,0:T(8,128)(2,1)}, bf16[2,48,512]{2,1,0:T(8,128)(2,1)S(1)}, u32[]{:S(2)}, u32[]{:S(2)}) collective-permute-start(bf16[2,48,512]{2,1,0:T(8,128)(2,1)} %get-tuple-element.102), channel_id=1, source_target_pairs={{0,13},{1,12},{2,15},{3,14},{4,9},{5,8},{6,11},{7,10},{8,5},{9,4},... | collective-permute-start | bytes 294920 | tf_op jit(solution)/shard_map/ppermute | solution.py:301
  27.8 3.8 %collective-permute-start.27 = (bf16[2,48,512]{2,1,0:T(8,128)(2,1)}, bf16[2,48,512]{2,1,0:T(8,128)(2,1)S(1)}, u32[]{:S(2)}, u32[]{:S(2)}) collective-permute-start(bf16[2,48,512]{2,1,0:T(8,128)(2,1)} %get-tuple-element.104), channel_id=1, source_target_pairs={{0,14},{1,15},{2,12},{3,13},{4,10},{5,11},{6,8},{7,9},{8,6},{9,7},... | collective-permute-start | bytes 294920 | tf_op jit(solution)/shard_map/ppermute | solution.py:301
  33.4 2.8 %pack_rows.1 = (bf16[32,1792]{1,0:T(8,128)(2,1)S(1)}, bf16[32,1792]{1,0:T(8,128)(2,1)S(1)}, bf16[32,1792]{1,0:T(8,128)(2,1)S(1)}, bf16[32,1792]{1,0:T(8,128)(2,1...) custom-call(s32[1]{0:T(128)S(6)} %copy.13.live_ref, ...), custom_call_target="tpu_custom_call" | custom-call | flops 469762048 | bytes 2752512 | tf_op jit(solution)/shard_map/pack_rows/pallas_call | solution.py:107
  36.2 7.7 %collective-permute-start.1 = (bf16[32,1792]{1,0:T(8,128)(2,1)S(1)}, bf16[32,1792]{1,0:T(8,128)(2,1)S(1)}, u32[]{:S(2)}, u32[]{:S(2)}) collective-permute-start(bf16[32,1792]{1,0:T(8,128)(2,1)S(1)} %get-tuple-element.75), channel_id=1, source_target_pairs={{0,8},{1,9},{2,10},{3,11},{4,12},{5,13},{6,14},{7,15},{8,0},{9,1},... | collective-permute-start | bytes 344072 | tf_op jit(solution)/shard_map/ppermute | solution.py:301
  45.2 2.5 %collective-permute-start.3 = (bf16[32,1792]{1,0:T(8,128)(2,1)S(1)}, bf16[32,1792]{1,0:T(8,128)(2,1)S(1)}, u32[]{:S(2)}, u32[]{:S(2)}) collective-permute-start(bf16[32,1792]{1,0:T(8,128)(2,1)S(1)} %get-tuple-element.77), channel_id=1, source_target_pairs={{0,9},{1,8},{2,11},{3,10},{4,13},{5,12},{6,15},{7,14},{8,1},{9,0},... | collective-permute-start | bytes 344072 | tf_op jit(solution)/shard_map/ppermute | solution.py:301
  50.5 4.0 %collective-permute-start.7 = (bf16[32,1792]{1,0:T(8,128)(2,1)S(1)}, bf16[32,1792]{1,0:T(8,128)(2,1)S(1)}, u32[]{:S(2)}, u32[]{:S(2)}) collective-permute-start(bf16[32,1792]{1,0:T(8,128)(2,1)S(1)} %get-tuple-element.81), channel_id=1, source_target_pairs={{0,11},{1,10},{2,9},{3,8},{4,15},{5,14},{6,13},{7,12},{8,3},{9,2},... | collective-permute-start | bytes 344072 | tf_op jit(solution)/shard_map/ppermute | solution.py:301
  54.6 2.2 %collective-permute-start.8 = (bf16[32,1792]{1,0:T(8,128)(2,1)S(1)}, bf16[32,1792]{1,0:T(8,128)(2,1)S(1)}, u32[]{:S(2)}, u32[]{:S(2)}) collective-permute-start(bf16[32,1792]{1,0:T(8,128)(2,1)S(1)} %get-tuple-element.82), channel_id=1, source_target_pairs={{0,4},{1,5},{2,6},{3,7},{4,0},{5,1},{6,2},{7,3},{8,12},{9,13},{10,... | collective-permute-start | bytes 344072 | tf_op jit(solution)/shard_map/ppermute | solution.py:301
  56.7 3.1 %collective-permute-start.9 = (bf16[32,1792]{1,0:T(8,128)(2,1)S(1)}, bf16[32,1792]{1,0:T(8,128)(2,1)S(1)}, u32[]{:S(2)}, u32[]{:S(2)}) collective-permute-start(bf16[32,1792]{1,0:T(8,128)(2,1)S(1)} %get-tuple-element.83), channel_id=1, source_target_pairs={{0,12},{1,13},{2,14},{3,15},{4,8},{5,9},{6,10},{7,11},{8,4},{9,5},... | collective-permute-start | bytes 344072 | tf_op jit(solution)/shard_map/ppermute | solution.py:301
  60.9 4.1 %collective-permute-start.11 = (bf16[32,1792]{1,0:T(8,128)(2,1)S(1)}, bf16[32,1792]{1,0:T(8,128)(2,1)S(1)}, u32[]{:S(2)}, u32[]{:S(2)}) collective-permute-start(bf16[32,1792]{1,0:T(8,128)(2,1)S(1)} %get-tuple-element.85), channel_id=1, source_target_pairs={{0,13},{1,12},{2,15},{3,14},{4,9},{5,8},{6,11},{7,10},{8,5},{9,4},... | collective-permute-start | bytes 344072 | tf_op jit(solution)/shard_map/ppermute | solution.py:301
  66.3 3.5 %collective-permute-start.13 = (bf16[32,1792]{1,0:T(8,128)(2,1)S(1)}, bf16[32,1792]{1,0:T(8,128)(2,1)S(1)}, u32[]{:S(2)}, u32[]{:S(2)}) collective-permute-start(bf16[32,1792]{1,0:T(8,128)(2,1)S(1)} %get-tuple-element.87), channel_id=1, source_target_pairs={{0,14},{1,15},{2,12},{3,13},{4,10},{5,11},{6,8},{7,9},{8,6},{9,7},... | collective-permute-start | bytes 344072 | tf_op jit(solution)/shard_map/ppermute | solution.py:301
  69.9 2.1 %collective-permute-start.15 = (bf16[32,1792]{1,0:T(8,128)(2,1)S(1)}, bf16[32,1792]{1,0:T(8,128)(2,1)S(1)}, u32[]{:S(2)}, u32[]{:S(2)}) collective-permute-start(bf16[32,1792]{1,0:T(8,128)(2,1)S(1)} %get-tuple-element.89), channel_id=1, source_target_pairs={{0,15},{1,14},{2,13},{3,12},{4,11},{5,10},{6,9},{7,8},{8,7},{9,6},... | collective-permute-start | bytes 344072 | tf_op jit(solution)/shard_map/ppermute | solution.py:301
  72.7 8.9 %collective-permute-start.30 = (bf16[2,48,512]{2,1,0:T(8,128)(2,1)S(1)}, bf16[2,48,512]{2,1,0:T(8,128)(2,1)S(1)}, u32[]{:S(2)}, u32[]{:S(2)}) collective-permute-start(bf16[2,48,512]{2,1,0:T(8,128)(2,1)S(1)} %get-tuple-element.108), channel_id=1, source_target_pairs={{0,8},{1,9},{2,10},{3,11},{4,12},{5,13},{6,14},{7,15},{8,0},{9,1},... | collective-permute-start | bytes 294920 | tf_op jit(solution)/shard_map/ppermute | solution.py:301
  81.6 4.8 %collective-permute-start.32 = (bf16[2,48,512]{2,1,0:T(8,128)(2,1)S(1)}, bf16[2,48,512]{2,1,0:T(8,128)(2,1)S(1)}, u32[]{:S(2)}, u32[]{:S(2)}) collective-permute-start(bf16[2,48,512]{2,1,0:T(8,128)(2,1)S(1)} %get-tuple-element.110), channel_id=1, source_target_pairs={{0,7},{1,6},{2,5},{3,4},{4,3},{5,2},{6,1},{7,0},{8,15},{9,14},{10,... | collective-permute-start | bytes 294920 | tf_op jit(solution)/shard_map/ppermute | solution.py:301
  86.5 4.3 %collective-permute-start.34 = (bf16[2,48,512]{2,1,0:T(8,128)(2,1)S(1)}, bf16[2,48,512]{2,1,0:T(8,128)(2,1)S(1)}, u32[]{:S(2)}, u32[]{:S(2)}) collective-permute-start(bf16[2,48,512]{2,1,0:T(8,128)(2,1)S(1)} %get-tuple-element.112), channel_id=1, source_target_pairs={{0,11},{1,10},{2,9},{3,8},{4,15},{5,14},{6,13},{7,12},{8,3},{9,2},... | collective-permute-start | bytes 294920 | tf_op jit(solution)/shard_map/ppermute | solution.py:301
  90.8 2.1 %collective-permute-done.30.refs_1_ = bf16[2,48,512]{2,1,0:T(8,128)(2,1)S(1)} collective-permute-done((bf16[2,48,512]{2,1,0:T(8,128)(2,1)S(1)}, bf16[2,48,512]{2,1,0:T(8,128)(2,1)S(1)}, u32[]{:S(2)}, u32[]{:S(2)}) %collective-permute-start.30) | collective-permute-done | bytes 98336 | tf_op jit(solution)/shard_map/ppermute | solution.py:301
  92.9 4.3 %collective-permute-done.31.refs_2_ = bf16[2,48,512]{2,1,0:T(8,128)(2,1)S(1)} collective-permute-done((bf16[2,48,512]{2,1,0:T(8,128)(2,1)S(1)}, bf16[2,48,512]{2,1,0:T(8,128)(2,1)S(1)}, u32[]{:S(2)}, u32[]{:S(2)}) %collective-permute-start.31) | collective-permute-done | bytes 98336 | tf_op jit(solution)/shard_map/ppermute | solution.py:301
  97.2 3.0 %collective-permute-start.36 = (bf16[2,48,512]{2,1,0:T(8,128)(2,1)S(1)}, bf16[2,48,512]{2,1,0:T(8,128)(2,1)S(1)}, u32[]{:S(2)}, u32[]{:S(2)}) collective-permute-start(bf16[2,48,512]{2,1,0:T(8,128)(2,1)S(1)} %get-tuple-element.114), channel_id=1, source_target_pairs={{0,12},{1,13},{2,14},{3,15},{4,8},{5,9},{6,10},{7,11},{8,4},{9,5},... | collective-permute-start | bytes 294920 | tf_op jit(solution)/shard_map/ppermute | solution.py:301
  100.5 3.9 %collective-permute-done.34.refs_5_ = bf16[2,48,512]{2,1,0:T(8,128)(2,1)S(1)} collective-permute-done((bf16[2,48,512]{2,1,0:T(8,128)(2,1)S(1)}, bf16[2,48,512]{2,1,0:T(8,128)(2,1)S(1)}, u32[]{:S(2)}, u32[]{:S(2)}) %collective-permute-start.34) | collective-permute-done | bytes 98336 | tf_op jit(solution)/shard_map/ppermute | solution.py:301
  106.3 2.2 %collective-permute-start.40 = (bf16[2,48,512]{2,1,0:T(8,128)(2,1)S(1)}, bf16[2,48,512]{2,1,0:T(8,128)(2,1)S(1)}, u32[]{:S(2)}, u32[]{:S(2)}) collective-permute-start(bf16[2,48,512]{2,1,0:T(8,128)(2,1)S(1)} %get-tuple-element.118), channel_id=1, source_target_pairs={{0,15},{1,14},{2,13},{3,12},{4,11},{5,10},{6,9},{7,8},{8,7},{9,6},... | collective-permute-start | bytes 294920 | tf_op jit(solution)/shard_map/ppermute | solution.py:301
  109.2 2.8 %collective-permute-start.43 = (bf16[2,48,512]{2,1,0:T(8,128)(2,1)S(1)}, bf16[2,48,512]{2,1,0:T(8,128)(2,1)S(1)}, u32[]{:S(2)}, u32[]{:S(2)}) collective-permute-start(bf16[2,48,512]{2,1,0:T(8,128)(2,1)S(1)} %get-tuple-element.121), channel_id=1, source_target_pairs={{0,2},{1,3},{2,0},{3,1},{4,6},{5,7},{6,4},{7,5},{8,10},{9,11},{10,... | collective-permute-start | bytes 294920 | tf_op jit(solution)/shard_map/ppermute | solution.py:301
  116.2 2.2 %collective-permute-done.43.refs_14_ = bf16[2,48,512]{2,1,0:T(8,128)(2,1)S(1)} collective-permute-done((bf16[2,48,512]{2,1,0:T(8,128)(2,1)S(1)}, bf16[2,48,512]{2,1,0:T(8,128)(2,1)S(1)}, u32[]{:S(2)}, u32[]{:S(2)}) %collective-permute-start.43) | collective-permute-done | bytes 98336 | tf_op jit(solution)/shard_map/ppermute | solution.py:301
  118.4 5.0 %update.1 = (bf16[384,1024]{1,0:T(8,128)(2,1)}, bf16[384,1024]{1,0:T(8,128)(2,1)}, bf16[32,1024]{1,0:T(8,128)(2,1)S(1)}, bf16[32,1024]{1,0:T(8,128)(2,1)S(1)}, b...) custom-call(s32[1]{0:T(128)} %bitcast.me_ref, ...), custom_call_target="tpu_custom_call" | custom-call | flops 1837105152 | bytes 6160384 | tf_op jit(solution)/shard_map/update/pallas_call | solution.py:236
  123.5 6.8 %collective-permute-start.45 = (bf16[32,1024]{1,0:T(8,128)(2,1)S(1)}, bf16[32,1024]{1,0:T(8,128)(2,1)S(1)}, u32[]{:S(2)}, u32[]{:S(2)}) collective-permute-start(bf16[32,1024]{1,0:T(8,128)(2,1)S(1)} %get-tuple-element.128), channel_id=1, source_target_pairs={{0,8},{1,9},{2,10},{3,11},{4,12},{5,13},{6,14},{7,15},{8,0},{9,1},... | collective-permute-start | bytes 196616 | tf_op jit(solution)/shard_map/ppermute | solution.py:301
  132.5 2.1 %collective-permute-start.49 = (bf16[32,1024]{1,0:T(8,128)(2,1)S(1)}, bf16[32,1024]{1,0:T(8,128)(2,1)S(1)}, u32[]{:S(2)}, u32[]{:S(2)}) collective-permute-start(bf16[32,1024]{1,0:T(8,128)(2,1)S(1)} %get-tuple-element.132), channel_id=1, source_target_pairs={{0,11},{1,10},{2,9},{3,8},{4,15},{5,14},{6,13},{7,12},{8,3},{9,2},... | collective-permute-start | bytes 196616 | tf_op jit(solution)/shard_map/ppermute | solution.py:301
  136.4 3.2 %collective-permute-start.51 = (bf16[32,1024]{1,0:T(8,128)(2,1)S(1)}, bf16[32,1024]{1,0:T(8,128)(2,1)S(1)}, u32[]{:S(2)}, u32[]{:S(2)}) collective-permute-start(bf16[32,1024]{1,0:T(8,128)(2,1)S(1)} %get-tuple-element.134), channel_id=1, source_target_pairs={{0,12},{1,13},{2,14},{3,15},{4,8},{5,9},{6,10},{7,11},{8,4},{9,5},... | collective-permute-start | bytes 196616 | tf_op jit(solution)/shard_map/ppermute | solution.py:301
  139.6 3.5 %collective-permute-start.52 = (bf16[32,1024]{1,0:T(8,128)(2,1)S(1)}, bf16[32,1024]{1,0:T(8,128)(2,1)S(1)}, u32[]{:S(2)}, u32[]{:S(2)}) collective-permute-start(bf16[32,1024]{1,0:T(8,128)(2,1)S(1)} %get-tuple-element.135), channel_id=1, source_target_pairs={{0,13},{1,12},{2,15},{3,14},{4,9},{5,8},{6,11},{7,10},{8,5},{9,4},... | collective-permute-start | bytes 196616 | tf_op jit(solution)/shard_map/ppermute | solution.py:301
  143.1 2.3 %collective-permute-start.54 = (bf16[32,1024]{1,0:T(8,128)(2,1)S(1)}, bf16[32,1024]{1,0:T(8,128)(2,1)S(1)}, u32[]{:S(2)}, u32[]{:S(2)}) collective-permute-start(bf16[32,1024]{1,0:T(8,128)(2,1)S(1)} %get-tuple-element.137), channel_id=1, source_target_pairs={{0,14},{1,15},{2,12},{3,13},{4,10},{5,11},{6,8},{7,9},{8,6},{9,7},... | collective-permute-start | bytes 196616 | tf_op jit(solution)/shard_map/ppermute | solution.py:301
  145.5 3.2 %collective-permute-start.55 = (bf16[32,1024]{1,0:T(8,128)(2,1)S(1)}, bf16[32,1024]{1,0:T(8,128)(2,1)S(1)}, u32[]{:S(2)}, u32[]{:S(2)}) collective-permute-start(bf16[32,1024]{1,0:T(8,128)(2,1)S(1)} %get-tuple-element.138), channel_id=1, source_target_pairs={{0,15},{1,14},{2,13},{3,12},{4,11},{5,10},{6,9},{7,8},{8,7},{9,6},... | collective-permute-start | bytes 196616 | tf_op jit(solution)/shard_map/ppermute | solution.py:301
  (110 shorter events, 41.5 us)
Async XLA Ops:
  11.5 12.4 %collective-permute-start.20 = (bf16[2,48,512]{2,1,0:T(8,128)(2,1)}, bf16[2,48,512]{2,1,0:T(8,128)(2,1)S(1)}, u32[]{:S(2)}, u32[]{:S(2)}) collective-permute-start(bf16[2,48,512]{2,1,0:T(8,128)(2,1)} %get-tuple-element.97), channel_id=1, source_target_pairs={{0,10},{1,11},{2,8},{3,9},{4,14},{5,15},{6,12},{7,13},{8,2},{9,3},... | collective-permute-start | bytes 294920 | tf_op jit(solution)/shard_map/ppermute | solution.py:301
  14.9 11.7 %collective-permute-start.21 = (bf16[2,48,512]{2,1,0:T(8,128)(2,1)}, bf16[2,48,512]{2,1,0:T(8,128)(2,1)S(1)}, u32[]{:S(2)}, u32[]{:S(2)}) collective-permute-start(bf16[2,48,512]{2,1,0:T(8,128)(2,1)} %get-tuple-element.98), channel_id=1, source_target_pairs={{0,5},{1,4},{2,7},{3,6},{4,1},{5,0},{6,3},{7,2},{8,13},{9,12},{10,... | collective-permute-start | bytes 294920 | tf_op jit(solution)/shard_map/ppermute | solution.py:301
  16.9 10.8 %collective-permute-start.22 = (bf16[2,48,512]{2,1,0:T(8,128)(2,1)}, bf16[2,48,512]{2,1,0:T(8,128)(2,1)S(1)}, u32[]{:S(2)}, u32[]{:S(2)}) collective-permute-start(bf16[2,48,512]{2,1,0:T(8,128)(2,1)} %get-tuple-element.99), channel_id=1, source_target_pairs={{0,11},{1,10},{2,9},{3,8},{4,15},{5,14},{6,13},{7,12},{8,3},{9,2},... | collective-permute-start | bytes 294920 | tf_op jit(solution)/shard_map/ppermute | solution.py:301
  18.8 12.8 %collective-permute-start.23 = (bf16[2,48,512]{2,1,0:T(8,128)(2,1)}, bf16[2,48,512]{2,1,0:T(8,128)(2,1)S(1)}, u32[]{:S(2)}, u32[]{:S(2)}) collective-permute-start(bf16[2,48,512]{2,1,0:T(8,128)(2,1)} %get-tuple-element.100), channel_id=1, source_target_pairs={{0,4},{1,5},{2,6},{3,7},{4,0},{5,1},{6,2},{7,3},{8,12},{9,13},{10,... | collective-permute-start | bytes 294920 | tf_op jit(solution)/shard_map/ppermute | solution.py:301
  20.7 10.9 %collective-permute-start.24 = (bf16[2,48,512]{2,1,0:T(8,128)(2,1)}, bf16[2,48,512]{2,1,0:T(8,128)(2,1)S(1)}, u32[]{:S(2)}, u32[]{:S(2)}) collective-permute-start(bf16[2,48,512]{2,1,0:T(8,128)(2,1)} %get-tuple-element.101), channel_id=1, source_target_pairs={{0,12},{1,13},{2,14},{3,15},{4,8},{5,9},{6,10},{7,11},{8,4},{9,5},... | collective-permute-start | bytes 294920 | tf_op jit(solution)/shard_map/ppermute | solution.py:301
  23.9 12.3 %collective-permute-start.25 = (bf16[2,48,512]{2,1,0:T(8,128)(2,1)}, bf16[2,48,512]{2,1,0:T(8,128)(2,1)S(1)}, u32[]{:S(2)}, u32[]{:S(2)}) collective-permute-start(bf16[2,48,512]{2,1,0:T(8,128)(2,1)} %get-tuple-element.102), channel_id=1, source_target_pairs={{0,13},{1,12},{2,15},{3,14},{4,9},{5,8},{6,11},{7,10},{8,5},{9,4},... | collective-permute-start | bytes 294920 | tf_op jit(solution)/shard_map/ppermute | solution.py:301
  26.6 17.3 %collective-permute-start.26 = (bf16[2,48,512]{2,1,0:T(8,128)(2,1)}, bf16[2,48,512]{2,1,0:T(8,128)(2,1)S(1)}, u32[]{:S(2)}, u32[]{:S(2)}) collective-permute-start(bf16[2,48,512]{2,1,0:T(8,128)(2,1)} %get-tuple-element.103), channel_id=1, source_target_pairs={{0,2},{1,3},{2,0},{3,1},{4,6},{5,7},{6,4},{7,5},{8,10},{9,11},{10,... | collective-permute-start | bytes 294920 | tf_op jit(solution)/shard_map/ppermute | solution.py:301
  27.8 17.4 %collective-permute-start.27 = (bf16[2,48,512]{2,1,0:T(8,128)(2,1)}, bf16[2,48,512]{2,1,0:T(8,128)(2,1)S(1)}, u32[]{:S(2)}, u32[]{:S(2)}) collective-permute-start(bf16[2,48,512]{2,1,0:T(8,128)(2,1)} %get-tuple-element.104), channel_id=1, source_target_pairs={{0,14},{1,15},{2,12},{3,13},{4,10},{5,11},{6,8},{7,9},{8,6},{9,7},... | collective-permute-start | bytes 294920 | tf_op jit(solution)/shard_map/ppermute | solution.py:301
  31.6 16.1 %collective-permute-start.28 = (bf16[2,48,512]{2,1,0:T(8,128)(2,1)}, bf16[2,48,512]{2,1,0:T(8,128)(2,1)S(1)}, u32[]{:S(2)}, u32[]{:S(2)}) collective-permute-start(bf16[2,48,512]{2,1,0:T(8,128)(2,1)} %get-tuple-element.105), channel_id=1, source_target_pairs={{0,1},{1,0},{2,3},{3,2},{4,5},{5,4},{6,7},{7,6},{8,9},{9,8},{10,11... | collective-permute-start | bytes 294920 | tf_op jit(solution)/shard_map/ppermute | solution.py:301
  31.6 16.2 %collective-permute-start.29 = (bf16[2,48,512]{2,1,0:T(8,128)(2,1)}, bf16[2,48,512]{2,1,0:T(8,128)(2,1)S(1)}, u32[]{:S(2)}, u32[]{:S(2)}) collective-permute-start(bf16[2,48,512]{2,1,0:T(8,128)(2,1)} %get-tuple-element.106), channel_id=1, source_target_pairs={{0,15},{1,14},{2,13},{3,12},{4,11},{5,10},{6,9},{7,8},{8,7},{9,6},... | collective-permute-start | bytes 294920 | tf_op jit(solution)/shard_map/ppermute | solution.py:301
  36.2 13.6 %collective-permute-start.1 = (bf16[32,1792]{1,0:T(8,128)(2,1)S(1)}, bf16[32,1792]{1,0:T(8,128)(2,1)S(1)}, u32[]{:S(2)}, u32[]{:S(2)}) collective-permute-start(bf16[32,1792]{1,0:T(8,128)(2,1)S(1)} %get-tuple-element.75), channel_id=1, source_target_pairs={{0,8},{1,9},{2,10},{3,11},{4,12},{5,13},{6,14},{7,15},{8,0},{9,1},... | collective-permute-start | bytes 344072 | tf_op jit(solution)/shard_map/ppermute | solution.py:301
  47.8 12.0 %collective-permute-start.5 = (bf16[32,1792]{1,0:T(8,128)(2,1)S(1)}, bf16[32,1792]{1,0:T(8,128)(2,1)S(1)}, u32[]{:S(2)}, u32[]{:S(2)}) collective-permute-start(bf16[32,1792]{1,0:T(8,128)(2,1)S(1)} %get-tuple-element.79), channel_id=1, source_target_pairs={{0,10},{1,11},{2,8},{3,9},{4,14},{5,15},{6,12},{7,13},{8,2},{9,3},... | collective-permute-start | bytes 344072 | tf_op jit(solution)/shard_map/ppermute | solution.py:301
  49.8 11.0 %collective-permute-start.6 = (bf16[32,1792]{1,0:T(8,128)(2,1)S(1)}, bf16[32,1792]{1,0:T(8,128)(2,1)S(1)}, u32[]{:S(2)}, u32[]{:S(2)}) collective-permute-start(bf16[32,1792]{1,0:T(8,128)(2,1)S(1)} %get-tuple-element.80), channel_id=1, source_target_pairs={{0,5},{1,4},{2,7},{3,6},{4,1},{5,0},{6,3},{7,2},{8,13},{9,12},{10,... | collective-permute-start | bytes 344072 | tf_op jit(solution)/shard_map/ppermute | solution.py:301
  50.5 14.5 %collective-permute-start.7 = (bf16[32,1792]{1,0:T(8,128)(2,1)S(1)}, bf16[32,1792]{1,0:T(8,128)(2,1)S(1)}, u32[]{:S(2)}, u32[]{:S(2)}) collective-permute-start(bf16[32,1792]{1,0:T(8,128)(2,1)S(1)} %get-tuple-element.81), channel_id=1, source_target_pairs={{0,11},{1,10},{2,9},{3,8},{4,15},{5,14},{6,13},{7,12},{8,3},{9,2},... | collective-permute-start | bytes 344072 | tf_op jit(solution)/shard_map/ppermute | solution.py:301
  54.6 11.8 %collective-permute-start.8 = (bf16[32,1792]{1,0:T(8,128)(2,1)S(1)}, bf16[32,1792]{1,0:T(8,128)(2,1)S(1)}, u32[]{:S(2)}, u32[]{:S(2)}) collective-permute-start(bf16[32,1792]{1,0:T(8,128)(2,1)S(1)} %get-tuple-element.82), channel_id=1, source_target_pairs={{0,4},{1,5},{2,6},{3,7},{4,0},{5,1},{6,2},{7,3},{8,12},{9,13},{10,... | collective-permute-start | bytes 344072 | tf_op jit(solution)/shard_map/ppermute | solution.py:301
  56.7 13.1 %collective-permute-start.9 = (bf16[32,1792]{1,0:T(8,128)(2,1)S(1)}, bf16[32,1792]{1,0:T(8,128)(2,1)S(1)}, u32[]{:S(2)}, u32[]{:S(2)}) collective-permute-start(bf16[32,1792]{1,0:T(8,128)(2,1)S(1)} %get-tuple-element.83), channel_id=1, source_target_pairs={{0,12},{1,13},{2,14},{3,15},{4,8},{5,9},{6,10},{7,11},{8,4},{9,5},... | collective-permute-start | bytes 344072 | tf_op jit(solution)/shard_map/ppermute | solution.py:301
  60.9 11.9 %collective-permute-start.11 = (bf16[32,1792]{1,0:T(8,128)(2,1)S(1)}, bf16[32,1792]{1,0:T(8,128)(2,1)S(1)}, u32[]{:S(2)}, u32[]{:S(2)}) collective-permute-start(bf16[32,1792]{1,0:T(8,128)(2,1)S(1)} %get-tuple-element.85), channel_id=1, source_target_pairs={{0,13},{1,12},{2,15},{3,14},{4,9},{5,8},{6,11},{7,10},{8,5},{9,4},... | collective-permute-start | bytes 344072 | tf_op jit(solution)/shard_map/ppermute | solution.py:301
  65.0 16.6 %collective-permute-start.12 = (bf16[32,1792]{1,0:T(8,128)(2,1)S(1)}, bf16[32,1792]{1,0:T(8,128)(2,1)S(1)}, u32[]{:S(2)}, u32[]{:S(2)}) collective-permute-start(bf16[32,1792]{1,0:T(8,128)(2,1)S(1)} %get-tuple-element.86), channel_id=1, source_target_pairs={{0,2},{1,3},{2,0},{3,1},{4,6},{5,7},{6,4},{7,5},{8,10},{9,11},{10,... | collective-permute-start | bytes 344072 | tf_op jit(solution)/shard_map/ppermute | solution.py:301
  66.3 15.3 %collective-permute-start.13 = (bf16[32,1792]{1,0:T(8,128)(2,1)S(1)}, bf16[32,1792]{1,0:T(8,128)(2,1)S(1)}, u32[]{:S(2)}, u32[]{:S(2)}) collective-permute-start(bf16[32,1792]{1,0:T(8,128)(2,1)S(1)} %get-tuple-element.87), channel_id=1, source_target_pairs={{0,14},{1,15},{2,12},{3,13},{4,10},{5,11},{6,8},{7,9},{8,6},{9,7},... | collective-permute-start | bytes 344072 | tf_op jit(solution)/shard_map/ppermute | solution.py:301
  69.9 16.6 %collective-permute-start.14 = (bf16[32,1792]{1,0:T(8,128)(2,1)S(1)}, bf16[32,1792]{1,0:T(8,128)(2,1)S(1)}, u32[]{:S(2)}, u32[]{:S(2)}) collective-permute-start(bf16[32,1792]{1,0:T(8,128)(2,1)S(1)} %get-tuple-element.88), channel_id=1, source_target_pairs={{0,1},{1,0},{2,3},{3,2},{4,5},{5,4},{6,7},{7,6},{8,9},{9,8},{10,11... | collective-permute-start | bytes 344072 | tf_op jit(solution)/shard_map/ppermute | solution.py:301
  69.9 16.6 %collective-permute-start.15 = (bf16[32,1792]{1,0:T(8,128)(2,1)S(1)}, bf16[32,1792]{1,0:T(8,128)(2,1)S(1)}, u32[]{:S(2)}, u32[]{:S(2)}) collective-permute-start(bf16[32,1792]{1,0:T(8,128)(2,1)S(1)} %get-tuple-element.89), channel_id=1, source_target_pairs={{0,15},{1,14},{2,13},{3,12},{4,11},{5,10},{6,9},{7,8},{8,7},{9,6},... | collective-permute-start | bytes 344072 | tf_op jit(solution)/shard_map/ppermute | solution.py:301
  72.7 20.2 %collective-permute-start.30 = (bf16[2,48,512]{2,1,0:T(8,128)(2,1)S(1)}, bf16[2,48,512]{2,1,0:T(8,128)(2,1)S(1)}, u32[]{:S(2)}, u32[]{:S(2)}) collective-permute-start(bf16[2,48,512]{2,1,0:T(8,128)(2,1)S(1)} %get-tuple-element.108), channel_id=1, source_target_pairs={{0,8},{1,9},{2,10},{3,11},{4,12},{5,13},{6,14},{7,15},{8,0},{9,1},... | collective-permute-start | bytes 294920 | tf_op jit(solution)/shard_map/ppermute | solution.py:301
  81.6 15.6 %collective-permute-start.31 = (bf16[2,48,512]{2,1,0:T(8,128)(2,1)S(1)}, bf16[2,48,512]{2,1,0:T(8,128)(2,1)S(1)}, u32[]{:S(2)}, u32[]{:S(2)}) collective-permute-start(bf16[2,48,512]{2,1,0:T(8,128)(2,1)S(1)} %get-tuple-element.109), channel_id=1, source_target_pairs={{0,9},{1,8},{2,11},{3,10},{4,13},{5,12},{6,15},{7,14},{8,1},{9,0},... | collective-permute-start | bytes 294920 | tf_op jit(solution)/shard_map/ppermute | solution.py:301
  81.6 18.6 %collective-permute-start.32 = (bf16[2,48,512]{2,1,0:T(8,128)(2,1)S(1)}, bf16[2,48,512]{2,1,0:T(8,128)(2,1)S(1)}, u32[]{:S(2)}, u32[]{:S(2)}) collective-permute-start(bf16[2,48,512]{2,1,0:T(8,128)(2,1)S(1)} %get-tuple-element.110), channel_id=1, source_target_pairs={{0,7},{1,6},{2,5},{3,4},{4,3},{5,2},{6,1},{7,0},{8,15},{9,14},{10,... | collective-permute-start | bytes 294920 | tf_op jit(solution)/shard_map/ppermute | solution.py:301
  86.5 14.1 %collective-permute-start.33 = (bf16[2,48,512]{2,1,0:T(8,128)(2,1)S(1)}, bf16[2,48,512]{2,1,0:T(8,128)(2,1)S(1)}, u32[]{:S(2)}, u32[]{:S(2)}) collective-permute-start(bf16[2,48,512]{2,1,0:T(8,128)(2,1)S(1)} %get-tuple-element.111), channel_id=1, source_target_pairs={{0,10},{1,11},{2,8},{3,9},{4,14},{5,15},{6,12},{7,13},{8,2},{9,3},... | collective-permute-start | bytes 294920 | tf_op jit(solution)/shard_map/ppermute | solution.py:301
  86.5 18.0 %collective-permute-start.34 = (bf16[2,48,512]{2,1,0:T(8,128)(2,1)S(1)}, bf16[2,48,512]{2,1,0:T(8,128)(2,1)S(1)}, u32[]{:S(2)}, u32[]{:S(2)}) collective-permute-start(bf16[2,48,512]{2,1,0:T(8,128)(2,1)S(1)} %get-tuple-element.112), channel_id=1, source_target_pairs={{0,11},{1,10},{2,9},{3,8},{4,15},{5,14},{6,13},{7,12},{8,3},{9,2},... | collective-permute-start | bytes 294920 | tf_op jit(solution)/shard_map/ppermute | solution.py:301
  92.9 13.4 %collective-permute-start.35 = (bf16[2,48,512]{2,1,0:T(8,128)(2,1)S(1)}, bf16[2,48,512]{2,1,0:T(8,128)(2,1)S(1)}, u32[]{:S(2)}, u32[]{:S(2)}) collective-permute-start(bf16[2,48,512]{2,1,0:T(8,128)(2,1)S(1)} %get-tuple-element.113), channel_id=1, source_target_pairs={{0,6},{1,7},{2,4},{3,5},{4,2},{5,3},{6,0},{7,1},{8,14},{9,15},{10,... | collective-permute-start | bytes 294920 | tf_op jit(solution)/shard_map/ppermute | solution.py:301
  97.2 11.3 %collective-permute-start.36 = (bf16[2,48,512]{2,1,0:T(8,128)(2,1)S(1)}, bf16[2,48,512]{2,1,0:T(8,128)(2,1)S(1)}, u32[]{:S(2)}, u32[]{:S(2)}) collective-permute-start(bf16[2,48,512]{2,1,0:T(8,128)(2,1)S(1)} %get-tuple-element.114), channel_id=1, source_target_pairs={{0,12},{1,13},{2,14},{3,15},{4,8},{5,9},{6,10},{7,11},{8,4},{9,5},... | collective-permute-start | bytes 294920 | tf_op jit(solution)/shard_map/ppermute | solution.py:301
  123.5 12.4 %collective-permute-start.45 = (bf16[32,1024]{1,0:T(8,128)(2,1)S(1)}, bf16[32,1024]{1,0:T(8,128)(2,1)S(1)}, u32[]{:S(2)}, u32[]{:S(2)}) collective-permute-start(bf16[32,1024]{1,0:T(8,128)(2,1)S(1)} %get-tuple-element.128), channel_id=1, source_target_pairs={{0,8},{1,9},{2,10},{3,11},{4,12},{5,13},{6,14},{7,15},{8,0},{9,1},... | collective-permute-start | bytes 196616 | tf_op jit(solution)/shard_map/ppermute | solution.py:301
  131.6 11.5 %collective-permute-start.48 = (bf16[32,1024]{1,0:T(8,128)(2,1)S(1)}, bf16[32,1024]{1,0:T(8,128)(2,1)S(1)}, u32[]{:S(2)}, u32[]{:S(2)}) collective-permute-start(bf16[32,1024]{1,0:T(8,128)(2,1)S(1)} %get-tuple-element.131), channel_id=1, source_target_pairs={{0,10},{1,11},{2,8},{3,9},{4,14},{5,15},{6,12},{7,13},{8,2},{9,3},... | collective-permute-start | bytes 196616 | tf_op jit(solution)/shard_map/ppermute | solution.py:301
  132.5 10.6 %collective-permute-start.49 = (bf16[32,1024]{1,0:T(8,128)(2,1)S(1)}, bf16[32,1024]{1,0:T(8,128)(2,1)S(1)}, u32[]{:S(2)}, u32[]{:S(2)}) collective-permute-start(bf16[32,1024]{1,0:T(8,128)(2,1)S(1)} %get-tuple-element.132), channel_id=1, source_target_pairs={{0,11},{1,10},{2,9},{3,8},{4,15},{5,14},{6,13},{7,12},{8,3},{9,2},... | collective-permute-start | bytes 196616 | tf_op jit(solution)/shard_map/ppermute | solution.py:301
  136.4 12.3 %collective-permute-start.51 = (bf16[32,1024]{1,0:T(8,128)(2,1)S(1)}, bf16[32,1024]{1,0:T(8,128)(2,1)S(1)}, u32[]{:S(2)}, u32[]{:S(2)}) collective-permute-start(bf16[32,1024]{1,0:T(8,128)(2,1)S(1)} %get-tuple-element.134), channel_id=1, source_target_pairs={{0,12},{1,13},{2,14},{3,15},{4,8},{5,9},{6,10},{7,11},{8,4},{9,5},... | collective-permute-start | bytes 196616 | tf_op jit(solution)/shard_map/ppermute | solution.py:301
  (36 other events, 517.2 us)

commit v9 on v2

--- a/solution.py
+++ b/solution.py
@@ -65,42 +65,61 @@
 
 
 def pack_kernel(groups, live_ref, perm_ref, *refs):
-    sources, (packed_ref, slot_ref), held, sem = refs[:5], refs[5:7], refs[7:12], refs[12]
-    fetched(sources, held, sem)
-    route_ref, fwd_route_ref, hidden_ref, out_ref, fwd_ref = held
+    sources, (packed_ref, slot_ref, gates_ref), held, sem = refs[:6], refs[7:10], refs[10:16], refs[16]
+    route_ref, fwd_route_ref, hidden_ref, out_ref, fwd_ref, gate_ref = held
+    copies = [pltpu.make_async_copy(ref, room, sem.at[n]) for n, (ref, room) in enumerate(zip(sources, held))]
+    for copy in copies:
+        copy.start()
     rows, ff = hidden_ref.shape
     d = out_ref.shape[1]
-    capacity = packed_ref.shape[0] // groups
+    slots = packed_ref.shape[0]
+    capacity = slots // groups
     place = lax.broadcasted_iota(jnp.int32, (1, rows), 1)
+
+    def fill(first, selector, source_ref):
+        chosen = jnp.dot(selector, source_ref[...], preferred_element_type=F32)
+        packed_ref[:, first : first + source_ref.shape[1]] = chosen.astype(BF16)
+
+    copies[0].wait()
     slot = slot_rows(route_ref[...], place < live_ref[0], groups, capacity, perm_ref)
-    selector = selector_of(slot, groups * capacity)
-    packed_ref[:, :ff] = jnp.dot(selector, hidden_ref[...], preferred_element_type=F32).astype(BF16)
-    packed_ref[:, ff : ff + d] = jnp.dot(selector, out_ref[...], preferred_element_type=F32).astype(BF16)
+    selector = selector_of(slot, slots)
+    copies[1].wait()
     fwd_slot = slot_rows(fwd_route_ref[...], place >= 0, groups, capacity, perm_ref)
     slot_ref[...] = fwd_slot
-    fwd_selector = selector_of(fwd_slot, groups * capacity)
-    packed_ref[:, ff + d :] = jnp.dot(fwd_selector, fwd_ref[...], preferred_element_type=F32).astype(BF16)
-
-
-def pack_rows(live_rows, perm, route, fwd_route, hidden, grad_out, fwd_hidden, groups, capacity):
+    copies[2].wait()
+    fill(0, selector, hidden_ref)
+    copies[3].wait()
+    fill(ff, selector, out_ref)
+    copies[4].wait()
+    fill(ff + d, selector_of(fwd_slot, slots), fwd_ref)
+    copies[5].wait()
+    down = lax.broadcasted_iota(jnp.int32, (rows, rows), 0)
+    across = lax.broadcasted_iota(jnp.int32, (rows, rows), 1)
+    gates_ref[...] = jnp.sum(jnp.where(down == across, gate_ref[...], 0.0), axis=1, keepdims=True)
+
+
+def pack_rows(live_rows, perm, route, fwd_route, hidden, grad_out, fwd_hidden, gate, earlier, groups, capacity):
     rows, ff = hidden.shape
     width = 2 * ff + grad_out.shape[1]
-    sources = (route.reshape(1, rows), fwd_route.reshape(1, rows), hidden, grad_out, fwd_hidden)
+    sources = (
+        route.reshape(1, rows), fwd_route.reshape(1, rows), hidden, grad_out, fwd_hidden, gate.reshape(1, rows),
+    )
     return pl.pallas_call(
         functools.partial(pack_kernel, groups),
         out_shape=(
             jax.ShapeDtypeStruct((groups * capacity, width), BF16),
             jax.ShapeDtypeStruct((1, rows), jnp.int32),
+            jax.ShapeDtypeStruct((rows, 1), F32),
         ),
-        in_specs=[SMEM, SMEM] + [HBM] * 5,
-        out_specs=(VMEM, VMEM),
-        scratch_shapes=rooms(sources),
-        compiler_params=pltpu.CompilerParams(vmem_limit_bytes=60 * MIB),
+        in_specs=[SMEM] * 2 + [HBM] * 6 + [VMEM],
+        out_specs=(VMEM,) * 3,
+        scratch_shapes=[pltpu.VMEM(a.shape, a.dtype) for a in sources] + [pltpu.SemaphoreType.DMA((len(sources),))],
+        compiler_params=pltpu.CompilerParams(vmem_limit_bytes=32 * MIB),
         cost_estimate=pl.CostEstimate(
             flops=2 * groups * capacity * rows * width, bytes_accessed=6 * rows * width, transcendentals=0
         ),
         name="pack_rows",
-    )(live_rows, perm, *sources)
+    )(live_rows, perm, *sources, earlier)
 
 
 def split_kernel(me_ref, moment_ref, weight_ref, *refs):
@@ -128,42 +147,45 @@
 
 
 def reorder_kernel(me_ref, perm_ref, *refs):
-    groups = (len(refs) - 1) // 2
-    sources, targets, held = refs[:groups], refs[groups : 2 * groups], refs[-1]
+    groups = (len(refs) - 2) // 3
+    sources, targets, held = refs[:groups], refs[groups + 1 : -1], refs[-1]
     me, order = me_ref[0], mixed_order(groups)
     for s, source in zip(order, sources):
         held[me ^ perm_ref[me ^ s]] = source[...]
-    for s, target in zip(order, targets):
-        target[...] = held[s]
-
-
-def reorder(me, perm, pieces):
+    for n, target in enumerate(targets):
+        target[...] = held[order[n % groups], n // groups]
+
+
+def reorder(me, perm, pieces, earlier):
     groups = len(pieces)
-    piece = jax.ShapeDtypeStruct(pieces[0].shape, BF16)
-    return pl.pallas_call(
+    piece = jax.ShapeDtypeStruct(pieces[0].shape[1:], BF16)
+    targets = pl.pallas_call(
         reorder_kernel,
-        out_shape=(piece,) * groups,
-        in_specs=[SMEM, SMEM] + [VMEM] * groups,
-        out_specs=(VMEM,) * groups,
+        out_shape=(piece,) * (2 * groups),
+        in_specs=[SMEM, SMEM] + [VMEM] * (groups + 1),
+        out_specs=(VMEM,) * (2 * groups),
         scratch_shapes=[pltpu.VMEM((groups,) + pieces[0].shape, BF16)],
         compiler_params=pltpu.CompilerParams(vmem_limit_bytes=32 * MIB),
         cost_estimate=pl.CostEstimate(flops=0, bytes_accessed=4 * groups * pieces[0].size, transcendentals=0),
         name="reorder",
-    )(me, perm, *pieces)
-
-
-def update_kernel(groups, me_ref, packed_ref, *refs):
-    pieces = refs[:groups]
-    weight_new_ref, moment_new_ref, produced_ref, held = refs[groups:]
-    _, ff, d = held.shape
-    for s, piece in zip(mixed_order(groups), pieces):
-        rows, columns = piece.shape[1:]
-        for lead in range(2):
-            chunk_at(held, lead, me_ref[0] ^ s, rows, columns)[...] = piece[lead]
+    )(me, perm, *pieces, earlier)
+    return targets[:groups], targets[groups:]
+
+
+def assembled(me_ref, pieces, held):
+    rows, columns = pieces[0].shape
+    for s, piece in zip(mixed_order(len(pieces)), pieces):
+        chunk_at(held, 0, me_ref[0] ^ s, rows, columns)[...] = piece[...]
+    return held[0].astype(F32)
+
+
+def orthogonal_kernel(me_ref, packed_ref, *refs):
+    pieces, (moment_new_ref, ortho_ref, held) = refs[:-3], refs[-3:]
+    ff, d = ortho_ref.shape
     grad = lax.dot_general(
         packed_ref[:, :ff], packed_ref[:, ff : ff + d], (((0,), (0,)), ((), ())), preferred_element_type=F32
     )
-    moment_new = (moment_decay * held[0].astype(F32) + grad).astype(BF16)
+    moment_new = (moment_decay * assembled(me_ref, pieces, held) + grad).astype(BF16)
     moment_new_ref[...] = moment_new
     moment_f = moment_new.astype(F32)
     frobenius = jnp.sqrt(jnp.sum(moment_f * moment_f))
@@ -177,61 +199,90 @@
         current = (
             linear_term * current.astype(F32) + jnp.dot(poly, current, preferred_element_type=F32)
         ).astype(BF16)
-    weight_new = (held[1].astype(F32) - step_scale * current.astype(F32)).astype(BF16)
-    weight_new_ref[...] = weight_new
-    produced_ref[...] = jnp.dot(packed_ref[:, ff + d :], weight_new, preferred_element_type=F32).astype(BF16)
-
-
-def update(me, packed, pieces, ff, d):
-    groups = len(pieces)
-    slots = packed.shape[0]
+    ortho_ref[...] = current
+
+
+def orthogonal(me, packed, pieces, ff, d):
     shape = jax.ShapeDtypeStruct((ff, d), BF16)
     return pl.pallas_call(
-        functools.partial(update_kernel, groups),
-        out_shape=(shape, shape, jax.ShapeDtypeStruct((slots, d), BF16)),
-        in_specs=[SMEM] + [VMEM] * (1 + groups),
-        out_specs=(VMEM,) * 3,
-        scratch_shapes=[pltpu.VMEM((2, ff, d), BF16)],
-        compiler_params=pltpu.CompilerParams(vmem_limit_bytes=48 * MIB),
+        orthogonal_kernel,
+        out_shape=(shape, shape),
+        in_specs=[SMEM, VMEM] + [VMEM] * len(pieces),
+        out_specs=(VMEM, VMEM),
+        scratch_shapes=[pltpu.VMEM((1, ff, d), BF16)],
+        compiler_params=pltpu.CompilerParams(vmem_limit_bytes=40 * MIB),
         cost_estimate=pl.CostEstimate(
-            flops=4 * ff * d * slots + 8 * ff * ff * d + 4 * ff**3,
-            bytes_accessed=8 * ff * d + 2 * packed.size + 2 * slots * d,
+            flops=2 * ff * d * packed.shape[0] + 8 * ff * ff * d + 4 * ff**3,
+            bytes_accessed=6 * ff * d + 2 * packed.size,
             transcendentals=1,
         ),
-        name="update",
+        name="orthogonal",
     )(me, packed, *pieces)
 
 
-def finish_kernel(slot_ref, gate_ref, returned_ref, out_ref):
-    rows = slot_ref.shape[1]
-    selector = selector_of(slot_ref[...], returned_ref.shape[0])
+def produce_kernel(groups, me_ref, packed_ref, ortho_ref, *refs):
+    pieces, (weight_new_ref, *produced), (held, product_ref) = refs[:groups], refs[groups:-2], refs[-2:]
+    ff, d = ortho_ref.shape
+    weight = assembled(me_ref, pieces, held)
+    weight_new = (weight - step_scale * ortho_ref[...].astype(F32)).astype(BF16)
+    weight_new_ref[...] = weight_new
+    product = jnp.dot(packed_ref[:, ff + d :], weight_new, preferred_element_type=F32).astype(BF16)
+    capacity = produced[0].shape[0]
+    product_ref[...] = product.reshape(groups, capacity, d)
+    for s, piece in zip(mixed_order(groups), produced):
+        piece[...] = product_ref[me_ref[0] ^ s]
+
+
+def produce(me, packed, ortho, pieces):
+    groups = len(pieces)
+    ff, d = ortho.shape
+    slots = packed.shape[0]
+    weight_new, *produced = pl.pallas_call(
+        functools.partial(produce_kernel, groups),
+        out_shape=(jax.ShapeDtypeStruct((ff, d), BF16),)
+        + (jax.ShapeDtypeStruct((slots // groups, d), BF16),) * groups,
+        in_specs=[SMEM] + [VMEM] * (2 + groups),
+        out_specs=(VMEM,) * (groups + 1),
+        scratch_shapes=[pltpu.VMEM((1, ff, d), BF16), pltpu.VMEM((groups, slots // groups, d), BF16)],
+        compiler_params=pltpu.CompilerParams(vmem_limit_bytes=40 * MIB),
+        cost_estimate=pl.CostEstimate(
+            flops=2 * ff * d * slots, bytes_accessed=8 * ff * d + 2 * slots * (ff + d), transcendentals=0
+        ),
+        name="produce",
+    )(me, packed, ortho, *pieces)
+    return weight_new, produced
+
+
+def finish_kernel(groups, me_ref, slot_ref, gates_ref, *refs):
+    pieces, (out_ref, returned_ref) = refs[:groups], refs[groups:]
+    for s, piece in zip(mixed_order(groups), pieces):
+        returned_ref[me_ref[0] ^ s] = piece[...]
+    _, capacity, d = returned_ref.shape
+    slots = groups * capacity
+    selector = selector_of(slot_ref[...], slots)
     expert_out = lax.dot_general(
-        selector, returned_ref[...], (((0,), (0,)), ((), ())), preferred_element_type=F32
-    )
-    down = lax.broadcasted_iota(jnp.int32, (rows, rows), 0)
-    across = lax.broadcasted_iota(jnp.int32, (rows, rows), 1)
-    gate = jnp.sum(jnp.where(down == across, gate_ref[...], 0.0), axis=1, keepdims=True)
-    out_ref[...] = (gate * expert_out).astype(BF16)
-
-
-def finish(slot, gate, returned):
+        selector, returned_ref[...].reshape(slots, d), (((0,), (0,)), ((), ())), preferred_element_type=F32
+    )
+    out_ref[...] = (gates_ref[...] * expert_out).astype(BF16)
+
+
+def finish(me, slot, gates, returned):
+    groups = len(returned)
     rows = slot.shape[1]
-    slots, d = returned.shape
+    capacity, d = returned[0].shape
+    slots = groups * capacity
     return pl.pallas_call(
-        finish_kernel,
+        functools.partial(finish_kernel, groups),
         out_shape=jax.ShapeDtypeStruct((rows, d), BF16),
-        in_specs=[VMEM] * 3,
+        in_specs=[SMEM] + [VMEM] * (2 + groups),
         out_specs=VMEM,
+        scratch_shapes=[pltpu.VMEM((groups, capacity, d), BF16)],
         compiler_params=pltpu.CompilerParams(vmem_limit_bytes=32 * MIB),
         cost_estimate=pl.CostEstimate(
             flops=2 * slots * rows * d, bytes_accessed=2 * d * (slots + rows), transcendentals=0
         ),
         name="finish",
-    )(slot, gate.reshape(1, rows), returned)
-
-
-def exchange(array):
-    return lax.all_to_all(array, "expert", split_axis=0, concat_axis=0, tiled=True)
+    )(me, slot, gates, *returned)
 
 
 def mixed_order(groups):
@@ -239,11 +290,15 @@
     return [0] + [s for pair in zip(far, near + [None]) for s in pair if s is not None]
 
 
-def swap(pieces):
-    groups = len(pieces)
-    order = mixed_order(groups)
-    return [pieces[0]] + [
-        lax.ppermute(piece, "expert", [(i, i ^ s) for i in range(groups)]) for s, piece in zip(order[1:], pieces[1:])
+def exchange(array):
+    return lax.all_to_all(array, "expert", split_axis=0, concat_axis=0, tiled=True)
+
+
+def swap(pieces, order):
+    groups = lax.axis_size("expert")
+    return [
+        lax.ppermute(piece, "expert", [(i, i ^ s) for i in range(groups)]) if s else piece
+        for s, piece in zip(order, pieces)
     ]
 
 
@@ -254,15 +309,17 @@
     me = lax.axis_index("expert").astype(jnp.int32).reshape(1)
     capacity = max(4, 2 * grad_hidden.shape[0] // groups)
     ff, d = w_down.shape[1:]
-    spread = swap(split(me, w_moment, w_down, groups))
-    packed, fwd_slot = pack_rows(
-        live_rows, perm, grad_route, fwd_route, grad_hidden, grad_out, fwd_hidden, groups, capacity
+    order = mixed_order(groups)
+    spread = swap(split(me, w_moment, w_down, groups), order)
+    packed, fwd_slot, gates = pack_rows(
+        live_rows, perm, grad_route, fwd_route, grad_hidden, grad_out, fwd_hidden, fwd_gate,
+        spread[2 * groups // 3], groups, capacity,
     )
     received = exchange(packed.reshape(groups, capacity, -1)).reshape(groups * capacity, -1)
-    placed = swap(reorder(me, perm, spread))
-    weight_new, moment_new, produced = update(me, received, placed, ff, d)
-    returned = exchange(produced.reshape(groups, capacity, d)).reshape(groups * capacity, d)
-    return weight_new[None], moment_new[None], finish(fwd_slot, fwd_gate, returned)
+    moment_pieces, weight_pieces = reorder(me, perm, spread, fwd_slot)
+    moment_new, ortho = orthogonal(me, received, swap(moment_pieces, order), ff, d)
+    weight_new, produced = produce(me, received, ortho, swap(weight_pieces, order))
+    return weight_new[None], moment_new[None], finish(me, fwd_slot, gates, swap(produced, order))
 
 
 def lookup(route_ids, mapping):

time: 164 us -> 188 us (1.15)
  starting transfers between devices: 48.8 us -> 99.8 us
  blocking collectives: 30.4 us -> 0 us
  local copies, waits for them, and re-layouts: 0.91 us -> 13.9 us
  waiting for transfers between devices: 67.4 us -> 59.5 us
    ppermute x30 -> x60, starting transfers between devices: 41.4 us -> 92.9 us  [swap(): lax.ppermute(piece, 'expert', [(i, i ^ s) for i in range(groups)])]
    all_to_all x1 -> x0, blocking collectives: 30.4 us -> none  [exchange(): lax.all_to_all(array, 'expert', split_axis=0, concat_axis=0, tiled=True)]
    unnamed x8 -> x66, local copies, waits for them, and re-layouts: 0.91 us -> 13.9 us
    ppermute x30 -> x60, waiting for transfers between devices: 67.4 us -> 59.5 us  [swap(): lax.ppermute(piece, 'expert', [(i, i ^ s) for i in range(groups)])]
    pallas_call x3 -> x4, Pallas kernels: 7.23 us -> 7.41 us  [the longest x1 3.65 us: orthogonal(): pl.pallas_call(orthogonal_kernel, out_shape=(shape, shape), in_specs=[SME...]
  transfers between devices with their start and end apart: 31 -> 61, of which waited for: 13 -> 10; matrix products, arithmetic and copies ran while one was open for 0% -> 0% of each run, Pallas kernels for 2% -> 2%
where the time goes in v9:
time: 188 us
  starting transfers between devices  99.8 us (53%)
  waiting for transfers between devices  59.5 us (32%)
  local copies, waits for them, and re-layouts  13.9 us (7%)
  Pallas kernels  12.7 us (7%)
    ppermute x60, starting transfers between devices, swap(): lax.ppermute(piece, 'expert', [(i, i ^ s) for i in range(groups)])  92.9 us
    ppermute x60, waiting for transfers between devices, swap(): lax.ppermute(piece, 'expert', [(i, i ^ s) for i in range(groups)])  59.5 us
    unnamed x66, local copies, waits for them, and re-layouts  13.9 us
    all_to_all x1, starting transfers between devices, exchange(): lax.all_to_all(array, 'expert', split_axis=0, concat_axis=0, tiled=True)  6.91 us
  transfers between devices with their start and end apart: 61, of which 10 were waited for; matrix products, arithmetic and copies ran while one was open for 0% of the time, Pallas kernels for 2%

profile of v9, /device:TPU:0, one launch (start us, length us, event | category | flops | bytes accessed | tf_op | source)
XLA Modules:
  0.0 187.6 jit_solution(17213116616914982009)
XLA Ops:
  0.6 2.6 %split.1 = (bf16[2,48,512]{2,1,0:T(8,128)(2,1)}, bf16[2,48,512]{2,1,0:T(8,128)(2,1)}, bf16[2,48,512]{2,1,0:T(8,128)(2,1)}, bf16[2,48,512]{2,1,0:T(8,128)(2,1)}, ...) custom-call(s32[1]{0:T(128)} %bitcast.me_ref, ...), custom_call_target="tpu_custom_call" | custom-call | bytes 3145728 | tf_op jit(solution)/shard_map/split/pallas_call | solution.py:137
  3.3 2.5 %collective-permute-start = (bf16[2,48,512]{2,1,0:T(8,128)(2,1)}, bf16[2,48,512]{2,1,0:T(8,128)(2,1)S(1)}, u32[]{:S(2)}, u32[]{:S(2)}) collective-permute-start(bf16[2,48,512]{2,1,0:T(8,128)(2,1)} %get-tuple-element.73), channel_id=1, source_target_pairs={{0,3},{1,2},{2,1},{3,0},{4,7},{5,6},{6,5},{7,4},{8,11},{9,10},{10,... | collective-permute-start | bytes 294920 | tf_op jit(solution)/shard_map/ppermute | solution.py:300
  6.4 2.8 %collective-permute-done.refs_6_.refs_10_ = bf16[2,48,512]{2,1,0:T(8,128)(2,1)S(1)} collective-permute-done((bf16[2,48,512]{2,1,0:T(8,128)(2,1)}, bf16[2,48,512]{2,1,0:T(8,128)(2,1)S(1)}, u32[]{:S(2)}, u32[]{:S(2)}) %collective-permute-start) | collective-permute-done | bytes 98336 | tf_op jit(solution)/shard_map/ppermute | solution.py:300
  14.8 2.7 %pack_rows.1 = (bf16[512,1792]{1,0:T(8,128)(2,1)S(1)}, s32[1,256]{1,0:T(1,128)S(1)}, f32[256,1]{1,0:T(8,128)S(1)}) custom-call(s32[1]{0:T(128)S(6)} %copy.13.live_ref, s32[16]{0:T(128)S(1)} %copy-done.2, s32[1,256]{1,0:T(1,128)S(1)} %bitcast.11, s32[1,256]{1,0:T(1,128)S(1)} %bitcast.12, bf16[256,384]{1,0:T(8,128)(2,1)S(1)} %copy-done.5, ...), custom_call_target="tpu_custom_call" | custom-call | flops 469762048 | bytes 2752512 | tf_op jit(solution)/shard_map/pack_rows/pallas_call | solution.py:107
  18.9 6.9 %all-to-all-start = ((bf16[16,32,1792]{2,1,0:T(8,128)(2,1)}), bf16[16,32,1792]{2,1,0:T(8,128)(2,1)S(1)}, u32[]{:S(2)}, u32[]{:S(2)}) async-start(bf16[16,32,1792]{2,1,0:T(8,128)(2,1)} %bitcast.10), calls=%async_computation | async-start | bytes 3670016 | tf_op jit(solution)/shard_map/all_to_all | solution.py:294
  25.8 2.8 %collective-permute-start.1 = (bf16[2,48,512]{2,1,0:T(8,128)(2,1)}, bf16[2,48,512]{2,1,0:T(8,128)(2,1)S(1)}, u32[]{:S(2)}, u32[]{:S(2)}) collective-permute-start(bf16[2,48,512]{2,1,0:T(8,128)(2,1)} %get-tuple-element.76), channel_id=1, source_target_pairs={{0,8},{1,9},{2,10},{3,11},{4,12},{5,13},{6,14},{7,15},{8,0},{9,1},... | collective-permute-start | bytes 294920 | tf_op jit(solution)/shard_map/ppermute | solution.py:300
  31.4 3.7 %collective-permute-start.5 = (bf16[2,48,512]{2,1,0:T(8,128)(2,1)S(1)}, bf16[2,48,512]{2,1,0:T(8,128)(2,1)S(1)}, u32[]{:S(2)}, u32[]{:S(2)}) collective-permute-start(bf16[2,48,512]{2,1,0:T(8,128)(2,1)S(1)} %copy-done.29), channel_id=1, source_target_pairs={{0,10},{1,11},{2,8},{3,9},{4,14},{5,15},{6,12},{7,13},{8,2},{9,3},... | collective-permute-start | bytes 294920 | tf_op jit(solution)/shard_map/ppermute | solution.py:300
  35.1 43.0 %collective-permute-done.1.refs_1_ = bf16[2,48,512]{2,1,0:T(8,128)(2,1)S(1)} collective-permute-done((bf16[2,48,512]{2,1,0:T(8,128)(2,1)}, bf16[2,48,512]{2,1,0:T(8,128)(2,1)S(1)}, u32[]{:S(2)}, u32[]{:S(2)}) %collective-permute-start.1) | collective-permute-done | bytes 98336 | tf_op jit(solution)/shard_map/ppermute | solution.py:300
  78.1 2.6 %collective-permute-start.7 = (bf16[2,48,512]{2,1,0:T(8,128)(2,1)S(1)}, bf16[2,48,512]{2,1,0:T(8,128)(2,1)S(1)}, u32[]{:S(2)}, u32[]{:S(2)}) collective-permute-start(bf16[2,48,512]{2,1,0:T(8,128)(2,1)S(1)} %copy-done.27), channel_id=1, source_target_pairs={{0,11},{1,10},{2,9},{3,8},{4,15},{5,14},{6,13},{7,12},{8,3},{9,2},... | collective-permute-start | bytes 294920 | tf_op jit(solution)/shard_map/ppermute | solution.py:300
  80.8 2.5 %collective-permute-start.9 = (bf16[2,48,512]{2,1,0:T(8,128)(2,1)S(1)}, bf16[2,48,512]{2,1,0:T(8,128)(2,1)S(1)}, u32[]{:S(2)}, u32[]{:S(2)}) collective-permute-start(bf16[2,48,512]{2,1,0:T(8,128)(2,1)S(1)} %copy-done.25), channel_id=1, source_target_pairs={{0,12},{1,13},{2,14},{3,15},{4,8},{5,9},{6,10},{7,11},{8,4},{9,5},... | collective-permute-start | bytes 294920 | tf_op jit(solution)/shard_map/ppermute | solution.py:300
  84.1 2.0 %collective-permute-done.6.refs_6_ = bf16[2,48,512]{2,1,0:T(8,128)(2,1)S(1)} collective-permute-done((bf16[2,48,512]{2,1,0:T(8,128)(2,1)S(1)}, bf16[2,48,512]{2,1,0:T(8,128)(2,1)S(1)}, u32[]{:S(2)}, u32[]{:S(2)}) %collective-permute-start.6) | collective-permute-done | bytes 98336 | tf_op jit(solution)/shard_map/ppermute | solution.py:300
  86.9 3.1 %collective-permute-start.12 = (bf16[2,48,512]{2,1,0:T(8,128)(2,1)S(1)}, bf16[2,48,512]{2,1,0:T(8,128)(2,1)S(1)}, u32[]{:S(2)}, u32[]{:S(2)}) collective-permute-start(bf16[2,48,512]{2,1,0:T(8,128)(2,1)S(1)} %copy-done.22), channel_id=1, source_target_pairs={{0,14},{1,15},{2,12},{3,13},{4,10},{5,11},{6,8},{7,9},{8,6},{9,7},... | collective-permute-start | bytes 294920 | tf_op jit(solution)/shard_map/ppermute | solution.py:300
  94.7 4.5 %collective-permute-done.14.refs_15_ = bf16[2,48,512]{2,1,0:T(8,128)(2,1)S(1)} collective-permute-done((bf16[2,48,512]{2,1,0:T(8,128)(2,1)S(1)}, bf16[2,48,512]{2,1,0:T(8,128)(2,1)S(1)}, u32[]{:S(2)}, u32[]{:S(2)}) %collective-permute-start.14) | collective-permute-done | bytes 98336 | tf_op jit(solution)/shard_map/ppermute | solution.py:300
  99.9 7.1 %collective-permute-start.15 = (bf16[48,512]{1,0:T(8,128)(2,1)S(1)}, bf16[48,512]{1,0:T(8,128)(2,1)S(1)}, u32[]{:S(2)}, u32[]{:S(2)}) collective-permute-start(bf16[48,512]{1,0:T(8,128)(2,1)S(1)} %get-tuple-element.92), channel_id=1, source_target_pairs={{0,8},{1,9},{2,10},{3,11},{4,12},{5,13},{6,14},{7,15},{8,0},{9,1},... | collective-permute-start | bytes 147464 | tf_op jit(solution)/shard_map/ppermute | solution.py:300
  107.1 2.7 %collective-permute-start.18 = (bf16[48,512]{1,0:T(8,128)(2,1)S(1)}, bf16[48,512]{1,0:T(8,128)(2,1)S(1)}, u32[]{:S(2)}, u32[]{:S(2)}) collective-permute-start(bf16[48,512]{1,0:T(8,128)(2,1)S(1)} %get-tuple-element.95), channel_id=1, source_target_pairs={{0,6},{1,7},{2,4},{3,5},{4,2},{5,3},{6,0},{7,1},{8,14},{9,15},{10,... | collective-permute-start | bytes 147464 | tf_op jit(solution)/shard_map/ppermute | solution.py:300
  109.8 2.5 %collective-permute-start.19 = (bf16[48,512]{1,0:T(8,128)(2,1)S(1)}, bf16[48,512]{1,0:T(8,128)(2,1)S(1)}, u32[]{:S(2)}, u32[]{:S(2)}) collective-permute-start(bf16[48,512]{1,0:T(8,128)(2,1)S(1)} %get-tuple-element.96), channel_id=1, source_target_pairs={{0,10},{1,11},{2,8},{3,9},{4,14},{5,15},{6,12},{7,13},{8,2},{9,3},... | collective-permute-start | bytes 147464 | tf_op jit(solution)/shard_map/ppermute | solution.py:300
  115.4 2.4 %collective-permute-start.23 = (bf16[48,512]{1,0:T(8,128)(2,1)S(1)}, bf16[48,512]{1,0:T(8,128)(2,1)S(1)}, u32[]{:S(2)}, u32[]{:S(2)}) collective-permute-start(bf16[48,512]{1,0:T(8,128)(2,1)S(1)} %get-tuple-element.100), channel_id=1, source_target_pairs={{0,12},{1,13},{2,14},{3,15},{4,8},{5,9},{6,10},{7,11},{8,4},{9,5},... | collective-permute-start | bytes 147464 | tf_op jit(solution)/shard_map/ppermute | solution.py:300
  121.0 3.0 %collective-permute-start.27 = (bf16[48,512]{1,0:T(8,128)(2,1)S(1)}, bf16[48,512]{1,0:T(8,128)(2,1)S(1)}, u32[]{:S(2)}, u32[]{:S(2)}) collective-permute-start(bf16[48,512]{1,0:T(8,128)(2,1)S(1)} %get-tuple-element.104), channel_id=1, source_target_pairs={{0,14},{1,15},{2,12},{3,13},{4,10},{5,11},{6,8},{7,9},{8,6},{9,7},... | collective-permute-start | bytes 147464 | tf_op jit(solution)/shard_map/ppermute | solution.py:300
  127.1 3.0 %collective-permute-start.31 = (bf16[48,512]{1,0:T(8,128)(2,1)S(1)}, bf16[48,512]{1,0:T(8,128)(2,1)S(1)}, u32[]{:S(2)}, u32[]{:S(2)}) collective-permute-start(bf16[48,512]{1,0:T(8,128)(2,1)S(1)} %get-tuple-element.110), channel_id=1, source_target_pairs={{0,7},{1,6},{2,5},{3,4},{4,3},{5,2},{6,1},{7,0},{8,15},{9,14},{10,... | collective-permute-start | bytes 147464 | tf_op jit(solution)/shard_map/ppermute | solution.py:300
  131.6 2.3 %collective-permute-start.33 = (bf16[48,512]{1,0:T(8,128)(2,1)S(1)}, bf16[48,512]{1,0:T(8,128)(2,1)S(1)}, u32[]{:S(2)}, u32[]{:S(2)}) collective-permute-start(bf16[48,512]{1,0:T(8,128)(2,1)S(1)} %get-tuple-element.112), channel_id=1, source_target_pairs={{0,6},{1,7},{2,4},{3,5},{4,2},{5,3},{6,0},{7,1},{8,14},{9,15},{10,... | collective-permute-start | bytes 147464 | tf_op jit(solution)/shard_map/ppermute | solution.py:300
  138.1 2.0 %collective-permute-start.37 = (bf16[48,512]{1,0:T(8,128)(2,1)S(1)}, bf16[48,512]{1,0:T(8,128)(2,1)S(1)}, u32[]{:S(2)}, u32[]{:S(2)}) collective-permute-start(bf16[48,512]{1,0:T(8,128)(2,1)S(1)} %get-tuple-element.116), channel_id=1, source_target_pairs={{0,4},{1,5},{2,6},{3,7},{4,0},{5,1},{6,2},{7,3},{8,12},{9,13},{10,... | collective-permute-start | bytes 147464 | tf_op jit(solution)/shard_map/ppermute | solution.py:300
  140.1 2.4 %collective-permute-start.38 = (bf16[48,512]{1,0:T(8,128)(2,1)S(1)}, bf16[48,512]{1,0:T(8,128)(2,1)S(1)}, u32[]{:S(2)}, u32[]{:S(2)}) collective-permute-start(bf16[48,512]{1,0:T(8,128)(2,1)S(1)} %get-tuple-element.117), channel_id=1, source_target_pairs={{0,12},{1,13},{2,14},{3,15},{4,8},{5,9},{6,10},{7,11},{8,4},{9,5},... | collective-permute-start | bytes 147464 | tf_op jit(solution)/shard_map/ppermute | solution.py:300
  145.7 3.0 %collective-permute-start.42 = (bf16[48,512]{1,0:T(8,128)(2,1)S(1)}, bf16[48,512]{1,0:T(8,128)(2,1)S(1)}, u32[]{:S(2)}, u32[]{:S(2)}) collective-permute-start(bf16[48,512]{1,0:T(8,128)(2,1)S(1)} %get-tuple-element.121), channel_id=1, source_target_pairs={{0,14},{1,15},{2,12},{3,13},{4,10},{5,11},{6,8},{7,9},{8,6},{9,7},... | collective-permute-start | bytes 147464 | tf_op jit(solution)/shard_map/ppermute | solution.py:300
  154.5 3.7 %orthogonal.1 = (bf16[384,1024]{1,0:T(8,128)(2,1)}, bf16[384,1024]{1,0:T(8,128)(2,1)S(1)}) custom-call(s32[1]{0:T(128)} %bitcast.me_ref, bf16[512,1792]{1,0:T(8,128)(2,1)S(1)} %bitcast.8, bf16[48,512]{1,0:T(8,128)(2,1)S(1)} %get-tuple-element.91.refs_0_, bf16[48,512]{1,0:T(8,128)(2,1)S(1)} %collective-permute-done.15.refs_1_, ...), custom_call_target="tpu_custom_call" | custom-call | flops 1837105152 | bytes 4194304 | tf_op jit(solution)/shard_map/orthogonal/pallas_call | solution.py:207
  159.9 3.0 %collective-permute-start.46 = (bf16[32,1024]{1,0:T(8,128)(2,1)S(1)}, bf16[32,1024]{1,0:T(8,128)(2,1)S(1)}, u32[]{:S(2)}, u32[]{:S(2)}) collective-permute-start(bf16[32,1024]{1,0:T(8,128)(2,1)S(1)} %get-tuple-element.129), channel_id=1, source_target_pairs={{0,7},{1,6},{2,5},{3,4},{4,3},{5,2},{6,1},{7,0},{8,15},{9,14},{10,... | collective-permute-start | bytes 196616 | tf_op jit(solution)/shard_map/ppermute | solution.py:300
  163.2 2.3 %collective-permute-start.48 = (bf16[32,1024]{1,0:T(8,128)(2,1)S(1)}, bf16[32,1024]{1,0:T(8,128)(2,1)S(1)}, u32[]{:S(2)}, u32[]{:S(2)}) collective-permute-start(bf16[32,1024]{1,0:T(8,128)(2,1)S(1)} %get-tuple-element.131), channel_id=1, source_target_pairs={{0,6},{1,7},{2,4},{3,5},{4,2},{5,3},{6,0},{7,1},{8,14},{9,15},{10,... | collective-permute-start | bytes 196616 | tf_op jit(solution)/shard_map/ppermute | solution.py:300
  171.2 2.2 %collective-permute-start.53 = (bf16[32,1024]{1,0:T(8,128)(2,1)S(1)}, bf16[32,1024]{1,0:T(8,128)(2,1)S(1)}, u32[]{:S(2)}, u32[]{:S(2)}) collective-permute-start(bf16[32,1024]{1,0:T(8,128)(2,1)S(1)} %get-tuple-element.136), channel_id=1, source_target_pairs={{0,12},{1,13},{2,14},{3,15},{4,8},{5,9},{6,10},{7,11},{8,4},{9,5},... | collective-permute-start | bytes 196616 | tf_op jit(solution)/shard_map/ppermute | solution.py:300
  173.4 2.3 %collective-permute-start.55 = (bf16[32,1024]{1,0:T(8,128)(2,1)S(1)}, bf16[32,1024]{1,0:T(8,128)(2,1)S(1)}, u32[]{:S(2)}, u32[]{:S(2)}) collective-permute-start(bf16[32,1024]{1,0:T(8,128)(2,1)S(1)} %get-tuple-element.138), channel_id=1, source_target_pairs={{0,13},{1,12},{2,15},{3,14},{4,9},{5,8},{6,11},{7,10},{8,5},{9,4},... | collective-permute-start | bytes 196616 | tf_op jit(solution)/shard_map/ppermute | solution.py:300
  176.8 2.8 %collective-permute-start.57 = (bf16[32,1024]{1,0:T(8,128)(2,1)S(1)}, bf16[32,1024]{1,0:T(8,128)(2,1)S(1)}, u32[]{:S(2)}, u32[]{:S(2)}) collective-permute-start(bf16[32,1024]{1,0:T(8,128)(2,1)S(1)} %get-tuple-element.140), channel_id=1, source_target_pairs={{0,14},{1,15},{2,12},{3,13},{4,10},{5,11},{6,8},{7,9},{8,6},{9,7},... | collective-permute-start | bytes 196616 | tf_op jit(solution)/shard_map/ppermute | solution.py:300
  179.7 2.0 %collective-permute-start.59 = (bf16[32,1024]{1,0:T(8,128)(2,1)S(1)}, bf16[32,1024]{1,0:T(8,128)(2,1)S(1)}, u32[]{:S(2)}, u32[]{:S(2)}) collective-permute-start(bf16[32,1024]{1,0:T(8,128)(2,1)S(1)} %get-tuple-element.142), channel_id=1, source_target_pairs={{0,15},{1,14},{2,13},{3,12},{4,11},{5,10},{6,9},{7,8},{8,7},{9,6},... | collective-permute-start | bytes 196616 | tf_op jit(solution)/shard_map/ppermute | solution.py:300
  181.7 2.1 %collective-permute-done.57.refs_13_ = bf16[32,1024]{1,0:T(8,128)(2,1)S(1)} collective-permute-done((bf16[32,1024]{1,0:T(8,128)(2,1)S(1)}, bf16[32,1024]{1,0:T(8,128)(2,1)S(1)}, u32[]{:S(2)}, u32[]{:S(2)}) %collective-permute-start.57) | collective-permute-done | bytes 65568 | tf_op jit(solution)/shard_map/ppermute | solution.py:300
  183.8 2.5 %collective-permute-done.59.refs_15_ = bf16[32,1024]{1,0:T(8,128)(2,1)S(1)} collective-permute-done((bf16[32,1024]{1,0:T(8,128)(2,1)S(1)}, bf16[32,1024]{1,0:T(8,128)(2,1)S(1)}, u32[]{:S(2)}, u32[]{:S(2)}) %collective-permute-start.59) | collective-permute-done | bytes 65568 | tf_op jit(solution)/shard_map/ppermute | solution.py:300
  (162 shorter events, 51.2 us)
Async XLA Ops:
  18.9 131.7 %all-to-all-start = ((bf16[16,32,1792]{2,1,0:T(8,128)(2,1)}), bf16[16,32,1792]{2,1,0:T(8,128)(2,1)S(1)}, u32[]{:S(2)}, u32[]{:S(2)}) async-start(bf16[16,32,1792]{2,1,0:T(8,128)(2,1)} %bitcast.10), calls=%async_computation | async-start | bytes 3670016 | tf_op jit(solution)/shard_map/all_to_all | solution.py:294
  25.8 52.3 %collective-permute-start.1 = (bf16[2,48,512]{2,1,0:T(8,128)(2,1)}, bf16[2,48,512]{2,1,0:T(8,128)(2,1)S(1)}, u32[]{:S(2)}, u32[]{:S(2)}) collective-permute-start(bf16[2,48,512]{2,1,0:T(8,128)(2,1)} %get-tuple-element.76), channel_id=1, source_target_pairs={{0,8},{1,9},{2,10},{3,11},{4,12},{5,13},{6,14},{7,15},{8,0},{9,1},... | collective-permute-start | bytes 294920 | tf_op jit(solution)/shard_map/ppermute | solution.py:300
  28.6 49.5 %collective-permute-start.2 = (bf16[2,48,512]{2,1,0:T(8,128)(2,1)S(1)}, bf16[2,48,512]{2,1,0:T(8,128)(2,1)S(1)}, u32[]{:S(2)}, u32[]{:S(2)}) collective-permute-start(bf16[2,48,512]{2,1,0:T(8,128)(2,1)S(1)} %copy-done.32), channel_id=1, source_target_pairs={{0,7},{1,6},{2,5},{3,4},{4,3},{5,2},{6,1},{7,0},{8,15},{9,14},{10,... | collective-permute-start | bytes 294920 | tf_op jit(solution)/shard_map/ppermute | solution.py:300
  30.5 50.3 %collective-permute-start.3 = (bf16[2,48,512]{2,1,0:T(8,128)(2,1)S(1)}, bf16[2,48,512]{2,1,0:T(8,128)(2,1)S(1)}, u32[]{:S(2)}, u32[]{:S(2)}) collective-permute-start(bf16[2,48,512]{2,1,0:T(8,128)(2,1)S(1)} %copy-done.31), channel_id=1, source_target_pairs={{0,9},{1,8},{2,11},{3,10},{4,13},{5,12},{6,15},{7,14},{8,1},{9,0},... | collective-permute-start | bytes 294920 | tf_op jit(solution)/shard_map/ppermute | solution.py:300
  31.3 49.5 %collective-permute-start.4 = (bf16[2,48,512]{2,1,0:T(8,128)(2,1)S(1)}, bf16[2,48,512]{2,1,0:T(8,128)(2,1)S(1)}, u32[]{:S(2)}, u32[]{:S(2)}) collective-permute-start(bf16[2,48,512]{2,1,0:T(8,128)(2,1)S(1)} %copy-done.30), channel_id=1, source_target_pairs={{0,6},{1,7},{2,4},{3,5},{4,2},{5,3},{6,0},{7,1},{8,14},{9,15},{10,... | collective-permute-start | bytes 294920 | tf_op jit(solution)/shard_map/ppermute | solution.py:300
  31.4 51.9 %collective-permute-start.5 = (bf16[2,48,512]{2,1,0:T(8,128)(2,1)S(1)}, bf16[2,48,512]{2,1,0:T(8,128)(2,1)S(1)}, u32[]{:S(2)}, u32[]{:S(2)}) collective-permute-start(bf16[2,48,512]{2,1,0:T(8,128)(2,1)S(1)} %copy-done.29), channel_id=1, source_target_pairs={{0,10},{1,11},{2,8},{3,9},{4,14},{5,15},{6,12},{7,13},{8,2},{9,3},... | collective-permute-start | bytes 294920 | tf_op jit(solution)/shard_map/ppermute | solution.py:300
  78.1 8.0 %collective-permute-start.6 = (bf16[2,48,512]{2,1,0:T(8,128)(2,1)S(1)}, bf16[2,48,512]{2,1,0:T(8,128)(2,1)S(1)}, u32[]{:S(2)}, u32[]{:S(2)}) collective-permute-start(bf16[2,48,512]{2,1,0:T(8,128)(2,1)S(1)} %copy-done.28), channel_id=1, source_target_pairs={{0,5},{1,4},{2,7},{3,6},{4,1},{5,0},{6,3},{7,2},{8,13},{9,12},{10,... | collective-permute-start | bytes 294920 | tf_op jit(solution)/shard_map/ppermute | solution.py:300
  78.1 8.8 %collective-permute-start.7 = (bf16[2,48,512]{2,1,0:T(8,128)(2,1)S(1)}, bf16[2,48,512]{2,1,0:T(8,128)(2,1)S(1)}, u32[]{:S(2)}, u32[]{:S(2)}) collective-permute-start(bf16[2,48,512]{2,1,0:T(8,128)(2,1)S(1)} %copy-done.27), channel_id=1, source_target_pairs={{0,11},{1,10},{2,9},{3,8},{4,15},{5,14},{6,13},{7,12},{8,3},{9,2},... | collective-permute-start | bytes 294920 | tf_op jit(solution)/shard_map/ppermute | solution.py:300
  80.8 9.2 %collective-permute-start.8 = (bf16[2,48,512]{2,1,0:T(8,128)(2,1)S(1)}, bf16[2,48,512]{2,1,0:T(8,128)(2,1)S(1)}, u32[]{:S(2)}, u32[]{:S(2)}) collective-permute-start(bf16[2,48,512]{2,1,0:T(8,128)(2,1)S(1)} %copy-done.26), channel_id=1, source_target_pairs={{0,4},{1,5},{2,6},{3,7},{4,0},{5,1},{6,2},{7,3},{8,12},{9,13},{10,... | collective-permute-start | bytes 294920 | tf_op jit(solution)/shard_map/ppermute | solution.py:300
  80.8 10.6 %collective-permute-start.9 = (bf16[2,48,512]{2,1,0:T(8,128)(2,1)S(1)}, bf16[2,48,512]{2,1,0:T(8,128)(2,1)S(1)}, u32[]{:S(2)}, u32[]{:S(2)}) collective-permute-start(bf16[2,48,512]{2,1,0:T(8,128)(2,1)S(1)} %copy-done.25), channel_id=1, source_target_pairs={{0,12},{1,13},{2,14},{3,15},{4,8},{5,9},{6,10},{7,11},{8,4},{9,5},... | collective-permute-start | bytes 294920 | tf_op jit(solution)/shard_map/ppermute | solution.py:300
  83.3 9.5 %collective-permute-start.10 = (bf16[2,48,512]{2,1,0:T(8,128)(2,1)S(1)}, bf16[2,48,512]{2,1,0:T(8,128)(2,1)S(1)}, u32[]{:S(2)}, u32[]{:S(2)}) collective-permute-start(bf16[2,48,512]{2,1,0:T(8,128)(2,1)S(1)} %copy-done.24), channel_id=1, source_target_pairs={{0,13},{1,12},{2,15},{3,14},{4,9},{5,8},{6,11},{7,10},{8,5},{9,4},... | collective-permute-start | bytes 294920 | tf_op jit(solution)/shard_map/ppermute | solution.py:300
  99.9 12.3 %collective-permute-start.15 = (bf16[48,512]{1,0:T(8,128)(2,1)S(1)}, bf16[48,512]{1,0:T(8,128)(2,1)S(1)}, u32[]{:S(2)}, u32[]{:S(2)}) collective-permute-start(bf16[48,512]{1,0:T(8,128)(2,1)S(1)} %get-tuple-element.92), channel_id=1, source_target_pairs={{0,8},{1,9},{2,10},{3,11},{4,12},{5,13},{6,14},{7,15},{8,0},{9,1},... | collective-permute-start | bytes 147464 | tf_op jit(solution)/shard_map/ppermute | solution.py:300
  107.1 8.3 %collective-permute-start.18 = (bf16[48,512]{1,0:T(8,128)(2,1)S(1)}, bf16[48,512]{1,0:T(8,128)(2,1)S(1)}, u32[]{:S(2)}, u32[]{:S(2)}) collective-permute-start(bf16[48,512]{1,0:T(8,128)(2,1)S(1)} %get-tuple-element.95), channel_id=1, source_target_pairs={{0,6},{1,7},{2,4},{3,5},{4,2},{5,3},{6,0},{7,1},{8,14},{9,15},{10,... | collective-permute-start | bytes 147464 | tf_op jit(solution)/shard_map/ppermute | solution.py:300
  109.8 7.9 %collective-permute-start.19 = (bf16[48,512]{1,0:T(8,128)(2,1)S(1)}, bf16[48,512]{1,0:T(8,128)(2,1)S(1)}, u32[]{:S(2)}, u32[]{:S(2)}) collective-permute-start(bf16[48,512]{1,0:T(8,128)(2,1)S(1)} %get-tuple-element.96), channel_id=1, source_target_pairs={{0,10},{1,11},{2,8},{3,9},{4,14},{5,15},{6,12},{7,13},{8,2},{9,3},... | collective-permute-start | bytes 147464 | tf_op jit(solution)/shard_map/ppermute | solution.py:300
  115.4 8.6 %collective-permute-start.23 = (bf16[48,512]{1,0:T(8,128)(2,1)S(1)}, bf16[48,512]{1,0:T(8,128)(2,1)S(1)}, u32[]{:S(2)}, u32[]{:S(2)}) collective-permute-start(bf16[48,512]{1,0:T(8,128)(2,1)S(1)} %get-tuple-element.100), channel_id=1, source_target_pairs={{0,12},{1,13},{2,14},{3,15},{4,8},{5,9},{6,10},{7,11},{8,4},{9,5},... | collective-permute-start | bytes 147464 | tf_op jit(solution)/shard_map/ppermute | solution.py:300
  117.8 8.1 %collective-permute-start.25 = (bf16[48,512]{1,0:T(8,128)(2,1)S(1)}, bf16[48,512]{1,0:T(8,128)(2,1)S(1)}, u32[]{:S(2)}, u32[]{:S(2)}) collective-permute-start(bf16[48,512]{1,0:T(8,128)(2,1)S(1)} %get-tuple-element.102), channel_id=1, source_target_pairs={{0,13},{1,12},{2,15},{3,14},{4,9},{5,8},{6,11},{7,10},{8,5},{9,4},... | collective-permute-start | bytes 147464 | tf_op jit(solution)/shard_map/ppermute | solution.py:300
  121.0 9.1 %collective-permute-start.27 = (bf16[48,512]{1,0:T(8,128)(2,1)S(1)}, bf16[48,512]{1,0:T(8,128)(2,1)S(1)}, u32[]{:S(2)}, u32[]{:S(2)}) collective-permute-start(bf16[48,512]{1,0:T(8,128)(2,1)S(1)} %get-tuple-element.104), channel_id=1, source_target_pairs={{0,14},{1,15},{2,12},{3,13},{4,10},{5,11},{6,8},{7,9},{8,6},{9,7},... | collective-permute-start | bytes 147464 | tf_op jit(solution)/shard_map/ppermute | solution.py:300
  124.0 9.9 %collective-permute-start.29 = (bf16[48,512]{1,0:T(8,128)(2,1)S(1)}, bf16[48,512]{1,0:T(8,128)(2,1)S(1)}, u32[]{:S(2)}, u32[]{:S(2)}) collective-permute-start(bf16[48,512]{1,0:T(8,128)(2,1)S(1)} %get-tuple-element.106), channel_id=1, source_target_pairs={{0,15},{1,14},{2,13},{3,12},{4,11},{5,10},{6,9},{7,8},{8,7},{9,6},... | collective-permute-start | bytes 147464 | tf_op jit(solution)/shard_map/ppermute | solution.py:300
  126.4 9.0 %collective-permute-start.30 = (bf16[48,512]{1,0:T(8,128)(2,1)S(1)}, bf16[48,512]{1,0:T(8,128)(2,1)S(1)}, u32[]{:S(2)}, u32[]{:S(2)}) collective-permute-start(bf16[48,512]{1,0:T(8,128)(2,1)S(1)} %get-tuple-element.109), channel_id=1, source_target_pairs={{0,8},{1,9},{2,10},{3,11},{4,12},{5,13},{6,14},{7,15},{8,0},{9,1},... | collective-permute-start | bytes 147464 | tf_op jit(solution)/shard_map/ppermute | solution.py:300
  127.1 9.8 %collective-permute-start.31 = (bf16[48,512]{1,0:T(8,128)(2,1)S(1)}, bf16[48,512]{1,0:T(8,128)(2,1)S(1)}, u32[]{:S(2)}, u32[]{:S(2)}) collective-permute-start(bf16[48,512]{1,0:T(8,128)(2,1)S(1)} %get-tuple-element.110), channel_id=1, source_target_pairs={{0,7},{1,6},{2,5},{3,4},{4,3},{5,2},{6,1},{7,0},{8,15},{9,14},{10,... | collective-permute-start | bytes 147464 | tf_op jit(solution)/shard_map/ppermute | solution.py:300
  131.6 8.5 %collective-permute-start.33 = (bf16[48,512]{1,0:T(8,128)(2,1)S(1)}, bf16[48,512]{1,0:T(8,128)(2,1)S(1)}, u32[]{:S(2)}, u32[]{:S(2)}) collective-permute-start(bf16[48,512]{1,0:T(8,128)(2,1)S(1)} %get-tuple-element.112), channel_id=1, source_target_pairs={{0,6},{1,7},{2,4},{3,5},{4,2},{5,3},{6,0},{7,1},{8,14},{9,15},{10,... | collective-permute-start | bytes 147464 | tf_op jit(solution)/shard_map/ppermute | solution.py:300
  134.5 7.9 %collective-permute-start.34 = (bf16[48,512]{1,0:T(8,128)(2,1)S(1)}, bf16[48,512]{1,0:T(8,128)(2,1)S(1)}, u32[]{:S(2)}, u32[]{:S(2)}) collective-permute-start(bf16[48,512]{1,0:T(8,128)(2,1)S(1)} %get-tuple-element.113), channel_id=1, source_target_pairs={{0,10},{1,11},{2,8},{3,9},{4,14},{5,15},{6,12},{7,13},{8,2},{9,3},... | collective-permute-start | bytes 147464 | tf_op jit(solution)/shard_map/ppermute | solution.py:300
  140.1 8.6 %collective-permute-start.38 = (bf16[48,512]{1,0:T(8,128)(2,1)S(1)}, bf16[48,512]{1,0:T(8,128)(2,1)S(1)}, u32[]{:S(2)}, u32[]{:S(2)}) collective-permute-start(bf16[48,512]{1,0:T(8,128)(2,1)S(1)} %get-tuple-element.117), channel_id=1, source_target_pairs={{0,12},{1,13},{2,14},{3,15},{4,8},{5,9},{6,10},{7,11},{8,4},{9,5},... | collective-permute-start | bytes 147464 | tf_op jit(solution)/shard_map/ppermute | solution.py:300
  142.5 15.7 %collective-permute-start.40 = (bf16[48,512]{1,0:T(8,128)(2,1)S(1)}, bf16[48,512]{1,0:T(8,128)(2,1)S(1)}, u32[]{:S(2)}, u32[]{:S(2)}) collective-permute-start(bf16[48,512]{1,0:T(8,128)(2,1)S(1)} %get-tuple-element.119), channel_id=1, source_target_pairs={{0,13},{1,12},{2,15},{3,14},{4,9},{5,8},{6,11},{7,10},{8,5},{9,4},... | collective-permute-start | bytes 147464 | tf_op jit(solution)/shard_map/ppermute | solution.py:300
  144.1 14.1 %collective-permute-start.41 = (bf16[48,512]{1,0:T(8,128)(2,1)S(1)}, bf16[48,512]{1,0:T(8,128)(2,1)S(1)}, u32[]{:S(2)}, u32[]{:S(2)}) collective-permute-start(bf16[48,512]{1,0:T(8,128)(2,1)S(1)} %get-tuple-element.120), channel_id=1, source_target_pairs={{0,2},{1,3},{2,0},{3,1},{4,6},{5,7},{6,4},{7,5},{8,10},{9,11},{10,... | collective-permute-start | bytes 147464 | tf_op jit(solution)/shard_map/ppermute | solution.py:300
  145.7 12.5 %collective-permute-start.42 = (bf16[48,512]{1,0:T(8,128)(2,1)S(1)}, bf16[48,512]{1,0:T(8,128)(2,1)S(1)}, u32[]{:S(2)}, u32[]{:S(2)}) collective-permute-start(bf16[48,512]{1,0:T(8,128)(2,1)S(1)} %get-tuple-element.121), channel_id=1, source_target_pairs={{0,14},{1,15},{2,12},{3,13},{4,10},{5,11},{6,8},{7,9},{8,6},{9,7},... | collective-permute-start | bytes 147464 | tf_op jit(solution)/shard_map/ppermute | solution.py:300
  148.7 9.5 %collective-permute-start.43 = (bf16[48,512]{1,0:T(8,128)(2,1)S(1)}, bf16[48,512]{1,0:T(8,128)(2,1)S(1)}, u32[]{:S(2)}, u32[]{:S(2)}) collective-permute-start(bf16[48,512]{1,0:T(8,128)(2,1)S(1)} %get-tuple-element.122), channel_id=1, source_target_pairs={{0,1},{1,0},{2,3},{3,2},{4,5},{5,4},{6,7},{7,6},{8,9},{9,8},{10,11... | collective-permute-start | bytes 147464 | tf_op jit(solution)/shard_map/ppermute | solution.py:300
  148.7 9.5 %collective-permute-start.44 = (bf16[48,512]{1,0:T(8,128)(2,1)S(1)}, bf16[48,512]{1,0:T(8,128)(2,1)S(1)}, u32[]{:S(2)}, u32[]{:S(2)}) collective-permute-start(bf16[48,512]{1,0:T(8,128)(2,1)S(1)} %get-tuple-element.123), channel_id=1, source_target_pairs={{0,15},{1,14},{2,13},{3,12},{4,11},{5,10},{6,9},{7,8},{8,7},{9,6},... | collective-permute-start | bytes 147464 | tf_op jit(solution)/shard_map/ppermute | solution.py:300
  159.9 8.0 %collective-permute-start.46 = (bf16[32,1024]{1,0:T(8,128)(2,1)S(1)}, bf16[32,1024]{1,0:T(8,128)(2,1)S(1)}, u32[]{:S(2)}, u32[]{:S(2)}) collective-permute-start(bf16[32,1024]{1,0:T(8,128)(2,1)S(1)} %get-tuple-element.129), channel_id=1, source_target_pairs={{0,7},{1,6},{2,5},{3,4},{4,3},{5,2},{6,1},{7,0},{8,15},{9,14},{10,... | collective-permute-start | bytes 196616 | tf_op jit(solution)/shard_map/ppermute | solution.py:300
  163.2 8.0 %collective-permute-start.48 = (bf16[32,1024]{1,0:T(8,128)(2,1)S(1)}, bf16[32,1024]{1,0:T(8,128)(2,1)S(1)}, u32[]{:S(2)}, u32[]{:S(2)}) collective-permute-start(bf16[32,1024]{1,0:T(8,128)(2,1)S(1)} %get-tuple-element.131), channel_id=1, source_target_pairs={{0,6},{1,7},{2,4},{3,5},{4,2},{5,3},{6,0},{7,1},{8,14},{9,15},{10,... | collective-permute-start | bytes 196616 | tf_op jit(solution)/shard_map/ppermute | solution.py:300
  171.2 8.4 %collective-permute-start.53 = (bf16[32,1024]{1,0:T(8,128)(2,1)S(1)}, bf16[32,1024]{1,0:T(8,128)(2,1)S(1)}, u32[]{:S(2)}, u32[]{:S(2)}) collective-permute-start(bf16[32,1024]{1,0:T(8,128)(2,1)S(1)} %get-tuple-element.136), channel_id=1, source_target_pairs={{0,12},{1,13},{2,14},{3,15},{4,8},{5,9},{6,10},{7,11},{8,4},{9,5},... | collective-permute-start | bytes 196616 | tf_op jit(solution)/shard_map/ppermute | solution.py:300
  173.4 8.2 %collective-permute-start.55 = (bf16[32,1024]{1,0:T(8,128)(2,1)S(1)}, bf16[32,1024]{1,0:T(8,128)(2,1)S(1)}, u32[]{:S(2)}, u32[]{:S(2)}) collective-permute-start(bf16[32,1024]{1,0:T(8,128)(2,1)S(1)} %get-tuple-element.138), channel_id=1, source_target_pairs={{0,13},{1,12},{2,15},{3,14},{4,9},{5,8},{6,11},{7,10},{8,5},{9,4},... | collective-permute-start | bytes 196616 | tf_op jit(solution)/shard_map/ppermute | solution.py:300
  (62 other events, 1001.3 us)

commit v10 on v7

--- a/solution.py
+++ b/solution.py
@@ -65,9 +65,9 @@
 
 
 def pack_kernel(groups, live_ref, me_ref, perm_ref, *refs):
-    sources, pieces, slot_ref = refs[:5], refs[6 : 6 + groups], refs[6 + groups]
-    held, sem = refs[7 + groups : 12 + groups], refs[-1]
-    route_ref, fwd_route_ref, hidden_ref, out_ref, fwd_ref = held
+    sources, pieces, (slot_ref, gates_ref) = refs[:6], refs[7 : 7 + groups], refs[7 + groups : 9 + groups]
+    held, sem = refs[9 + groups : 15 + groups], refs[-1]
+    route_ref, fwd_route_ref, hidden_ref, out_ref, fwd_ref, gate_ref = held
     copies = [pltpu.make_async_copy(ref, room, sem.at[n]) for n, (ref, room) in enumerate(zip(sources, held))]
     for copy in copies:
         copy.start()
@@ -94,18 +94,22 @@
     fill(ff, selector, out_ref)
     copies[4].wait()
     fill(ff + d, selector_of(fwd_slot, slots), fwd_ref)
-
-
-def pack_rows(live_rows, me, perm, route, fwd_route, hidden, grad_out, fwd_hidden, earlier, groups, capacity):
+    copies[5].wait()
+    down = lax.broadcasted_iota(jnp.int32, (rows, rows), 0)
+    across = lax.broadcasted_iota(jnp.int32, (rows, rows), 1)
+    gates_ref[...] = jnp.sum(jnp.where(down == across, gate_ref[...], 0.0), axis=1, keepdims=True)
+
+
+def pack_rows(live_rows, me, perm, route, fwd_route, hidden, grad_out, fwd_hidden, gate, earlier, groups, capacity):
     rows, ff = hidden.shape
     width = 2 * ff + grad_out.shape[1]
-    sources = (route.reshape(1, rows), fwd_route.reshape(1, rows), hidden, grad_out, fwd_hidden)
-    *pieces, slot = pl.pallas_call(
+    sources = (route.reshape(1, rows), fwd_route.reshape(1, rows), hidden, grad_out, fwd_hidden, gate.reshape(1, rows))
+    *pieces, slot, gates = pl.pallas_call(
         functools.partial(pack_kernel, groups),
         out_shape=(jax.ShapeDtypeStruct((capacity, width), BF16),) * groups
-        + (jax.ShapeDtypeStruct((1, rows), jnp.int32),),
-        in_specs=[SMEM] * 3 + [HBM] * 5 + [VMEM],
-        out_specs=(VMEM,) * (groups + 1),
+        + (jax.ShapeDtypeStruct((1, rows), jnp.int32), jax.ShapeDtypeStruct((rows, 1), F32)),
+        in_specs=[SMEM] * 3 + [HBM] * 6 + [VMEM],
+        out_specs=(VMEM,) * (groups + 2),
         scratch_shapes=[pltpu.VMEM(a.shape, a.dtype) for a in sources] + [pltpu.SemaphoreType.DMA((len(sources),))],
         compiler_params=pltpu.CompilerParams(vmem_limit_bytes=32 * MIB),
         cost_estimate=pl.CostEstimate(
@@ -113,7 +117,7 @@
         ),
         name="pack_rows",
     )(live_rows, me, perm, *sources, earlier)
-    return pieces, slot
+    return pieces, slot, gates
 
 
 def split_kernel(me_ref, moment_ref, weight_ref, *refs):
@@ -223,23 +227,19 @@
     return weight_new, moment_new, produced
 
 
-def finish_kernel(groups, slot_ref, gate_ref, *refs):
+def finish_kernel(groups, slot_ref, gates_ref, *refs):
     pieces, (out_ref, returned_ref) = refs[:groups], refs[groups:]
     capacity = pieces[0].shape[0]
     for s, piece in zip(mixed_order(groups), pieces):
         returned_ref[s * capacity : (s + 1) * capacity] = piece[...]
-    rows = slot_ref.shape[1]
     selector = selector_of(slot_ref[...], groups * capacity)
     expert_out = lax.dot_general(
         selector, returned_ref[...], (((0,), (0,)), ((), ())), preferred_element_type=F32
     )
-    down = lax.broadcasted_iota(jnp.int32, (rows, rows), 0)
-    across = lax.broadcasted_iota(jnp.int32, (rows, rows), 1)
-    gate = jnp.sum(jnp.where(down == across, gate_ref[...], 0.0), axis=1, keepdims=True)
-    out_ref[...] = (gate * expert_out).astype(BF16)
-
-
-def finish(slot, gate, returned):
+    out_ref[...] = (gates_ref[...] * expert_out).astype(BF16)
+
+
+def finish(slot, gates, returned):
     groups = len(returned)
     rows = slot.shape[1]
     capacity, d = returned[0].shape
@@ -255,11 +255,17 @@
             flops=2 * slots * rows * d, bytes_accessed=2 * d * (slots + rows), transcendentals=0
         ),
         name="finish",
-    )(slot, gate.reshape(1, rows), *returned)
+    )(slot, gates, *returned)
 
 
 def mixed_order(groups):
-    far, near = list(range(groups // 2, groups)), list(range(groups // 2 - 1, 0, -1))
+    def both_ends(partners):
+        middle = (len(partners) + 1) // 2
+        first, second = partners[:middle], partners[middle:]
+        return [s for pair in zip(first, second + [None]) for s in pair if s is not None]
+
+    half = groups // 2
+    far, near = both_ends(list(range(half, groups))), both_ends(list(range(half - 1, 0, -1)))
     return [0] + [s for pair in zip(far, near + [None]) for s in pair if s is not None]
 
 
@@ -279,14 +285,14 @@
     capacity = max(4, 2 * grad_hidden.shape[0] // groups)
     ff, d = w_down.shape[1:]
     spread = swap(split(me, w_moment, w_down, groups))
-    packed, fwd_slot = pack_rows(
-        live_rows, me, perm, grad_route, fwd_route, grad_hidden, grad_out, fwd_hidden,
+    packed, fwd_slot, gates = pack_rows(
+        live_rows, me, perm, grad_route, fwd_route, grad_hidden, grad_out, fwd_hidden, fwd_gate,
         spread[2 * groups // 3], groups, capacity,
     )
     received = swap(packed)
     placed = swap(reorder(me, perm, spread, received[groups // 3]))
     weight_new, moment_new, produced = update(me, received, placed, ff, d)
-    return weight_new[None], moment_new[None], finish(fwd_slot, fwd_gate, swap(produced))
+    return weight_new[None], moment_new[None], finish(fwd_slot, gates, swap(produced))
 
 
 def lookup(route_ids, mapping):

time: 152 us -> 149 us (0.980)
  starting transfers between devices: 113 us -> 110 us
    ppermute x60, starting transfers between devices: 113 us -> 110 us  [swap(): lax.ppermute(piece, 'expert', [(i, i ^ s) for i in range(groups)])]
  transfers between devices with their start and end apart: 60 -> 60, of which waited for: 17 -> 12; matrix products, arithmetic and copies ran while one was open for 0% -> 0% of each run, Pallas kernels for 2% -> 2%
where the time goes in v10:
time: 149 us
  starting transfers between devices  110 us (74%)
  waiting for transfers between devices  24.5 us (16%)
  Pallas kernels  12.3 us (8%)
  between operations  1.49 us (1%)
    ppermute x60, starting transfers between devices, swap(): lax.ppermute(piece, 'expert', [(i, i ^ s) for i in range(groups)])  110 us
    ppermute x60, waiting for transfers between devices, swap(): lax.ppermute(piece, 'expert', [(i, i ^ s) for i in range(groups)])  24.5 us
    pallas_call x1, Pallas kernels, update(): pl.pallas_call(functools.partial(update_kernel, groups), out_shape=(shape...  4.73 us
  transfers between devices with their start and end apart: 60, of which 12 were waited for; matrix products, arithmetic and copies ran while one was open for 0% of the time, Pallas kernels for 2%

profile of v10, /device:TPU:0, one launch (start us, length us, event | category | flops | bytes accessed | tf_op | source)
XLA Modules:
  0.0 149.0 jit_solution(2630584417143970665)
XLA Ops:
  0.7 2.7 %split.1 = (bf16[2,48,512]{2,1,0:T(8,128)(2,1)}, bf16[2,48,512]{2,1,0:T(8,128)(2,1)}, bf16[2,48,512]{2,1,0:T(8,128)(2,1)}, bf16[2,48,512]{2,1,0:T(8,128)(2,1)}, ...) custom-call(s32[1]{0:T(128)} %bitcast.me_ref, ...), custom_call_target="tpu_custom_call" | custom-call | bytes 3145728 | tf_op jit(solution)/shard_map/split/pallas_call | solution.py:135
  3.4 2.5 %collective-permute-start = (bf16[2,48,512]{2,1,0:T(8,128)(2,1)}, bf16[2,48,512]{2,1,0:T(8,128)(2,1)S(1)}, u32[]{:S(2)}, u32[]{:S(2)}) collective-permute-start(bf16[2,48,512]{2,1,0:T(8,128)(2,1)} %get-tuple-element.71), channel_id=1, source_target_pairs={{0,5},{1,4},{2,7},{3,6},{4,1},{5,0},{6,3},{7,2},{8,13},{9,12},{10,... | collective-permute-start | bytes 294920 | tf_op jit(solution)/shard_map/ppermute | solution.py:276
  5.9 2.6 %collective-permute-start.16 = (bf16[2,48,512]{2,1,0:T(8,128)(2,1)}, bf16[2,48,512]{2,1,0:T(8,128)(2,1)S(1)}, u32[]{:S(2)}, u32[]{:S(2)}) collective-permute-start(bf16[2,48,512]{2,1,0:T(8,128)(2,1)} %get-tuple-element.89), channel_id=1, source_target_pairs={{0,8},{1,9},{2,10},{3,11},{4,12},{5,13},{6,14},{7,15},{8,0},{9,1},... | collective-permute-start | bytes 294920 | tf_op jit(solution)/shard_map/ppermute | solution.py:276
  16.1 2.8 %collective-permute-start.22 = (bf16[2,48,512]{2,1,0:T(8,128)(2,1)}, bf16[2,48,512]{2,1,0:T(8,128)(2,1)S(1)}, u32[]{:S(2)}, u32[]{:S(2)}) collective-permute-start(bf16[2,48,512]{2,1,0:T(8,128)(2,1)} %get-tuple-element.95), channel_id=1, source_target_pairs={{0,13},{1,12},{2,15},{3,14},{4,9},{5,8},{6,11},{7,10},{8,5},{9,4},... | collective-permute-start | bytes 294920 | tf_op jit(solution)/shard_map/ppermute | solution.py:276
  20.4 3.9 %collective-permute-start.24 = (bf16[2,48,512]{2,1,0:T(8,128)(2,1)}, bf16[2,48,512]{2,1,0:T(8,128)(2,1)S(1)}, u32[]{:S(2)}, u32[]{:S(2)}) collective-permute-start(bf16[2,48,512]{2,1,0:T(8,128)(2,1)} %get-tuple-element.97), channel_id=1, source_target_pairs={{0,10},{1,11},{2,8},{3,9},{4,14},{5,15},{6,12},{7,13},{8,2},{9,3},... | collective-permute-start | bytes 294920 | tf_op jit(solution)/shard_map/ppermute | solution.py:276
  24.3 3.8 %collective-permute-start.25 = (bf16[2,48,512]{2,1,0:T(8,128)(2,1)}, bf16[2,48,512]{2,1,0:T(8,128)(2,1)S(1)}, u32[]{:S(2)}, u32[]{:S(2)}) collective-permute-start(bf16[2,48,512]{2,1,0:T(8,128)(2,1)} %get-tuple-element.98), channel_id=1, source_target_pairs={{0,14},{1,15},{2,12},{3,13},{4,10},{5,11},{6,8},{7,9},{8,6},{9,7},... | collective-permute-start | bytes 294920 | tf_op jit(solution)/shard_map/ppermute | solution.py:276
  28.5 3.2 %collective-permute-start.27 = (bf16[2,48,512]{2,1,0:T(8,128)(2,1)}, bf16[2,48,512]{2,1,0:T(8,128)(2,1)S(1)}, u32[]{:S(2)}, u32[]{:S(2)}) collective-permute-start(bf16[2,48,512]{2,1,0:T(8,128)(2,1)} %get-tuple-element.100), channel_id=1, source_target_pairs={{0,11},{1,10},{2,9},{3,8},{4,15},{5,14},{6,13},{7,12},{8,3},{9,2},... | collective-permute-start | bytes 294920 | tf_op jit(solution)/shard_map/ppermute | solution.py:276
  31.7 2.8 %collective-permute-done.24.refs_9_ = bf16[2,48,512]{2,1,0:T(8,128)(2,1)S(1)} collective-permute-done((bf16[2,48,512]{2,1,0:T(8,128)(2,1)}, bf16[2,48,512]{2,1,0:T(8,128)(2,1)S(1)}, u32[]{:S(2)}, u32[]{:S(2)}) %collective-permute-start.24) | collective-permute-done | bytes 98336 | tf_op jit(solution)/shard_map/ppermute | solution.py:276
  37.5 2.8 %pack_rows.1 = (bf16[32,1792]{1,0:T(8,128)(2,1)S(1)}, bf16[32,1792]{1,0:T(8,128)(2,1)S(1)}, bf16[32,1792]{1,0:T(8,128)(2,1)S(1)}, bf16[32,1792]{1,0:T(8,128)(2,1...) custom-call(s32[1]{0:T(128)S(6)} %copy.13.live_ref, ...), custom_call_target="tpu_custom_call" | custom-call | flops 469762048 | bytes 2752512 | tf_op jit(solution)/shard_map/pack_rows/pallas_call | solution.py:107
  40.7 2.7 %collective-permute-start.2 = (bf16[32,1792]{1,0:T(8,128)(2,1)S(1)}, bf16[32,1792]{1,0:T(8,128)(2,1)S(1)}, u32[]{:S(2)}, u32[]{:S(2)}) collective-permute-start(bf16[32,1792]{1,0:T(8,128)(2,1)S(1)} %get-tuple-element.74), channel_id=1, source_target_pairs={{0,7},{1,6},{2,5},{3,4},{4,3},{5,2},{6,1},{7,0},{8,15},{9,14},{10,... | collective-permute-start | bytes 344072 | tf_op jit(solution)/shard_map/ppermute | solution.py:276
  43.4 5.0 %collective-permute-start.3 = (bf16[32,1792]{1,0:T(8,128)(2,1)S(1)}, bf16[32,1792]{1,0:T(8,128)(2,1)S(1)}, u32[]{:S(2)}, u32[]{:S(2)}) collective-permute-start(bf16[32,1792]{1,0:T(8,128)(2,1)S(1)} %get-tuple-element.75), channel_id=1, source_target_pairs={{0,12},{1,13},{2,14},{3,15},{4,8},{5,9},{6,10},{7,11},{8,4},{9,5},... | collective-permute-start | bytes 344072 | tf_op jit(solution)/shard_map/ppermute | solution.py:276
  50.4 5.6 %collective-permute-start.7 = (bf16[32,1792]{1,0:T(8,128)(2,1)S(1)}, bf16[32,1792]{1,0:T(8,128)(2,1)S(1)}, u32[]{:S(2)}, u32[]{:S(2)}) collective-permute-start(bf16[32,1792]{1,0:T(8,128)(2,1)S(1)} %get-tuple-element.79), channel_id=1, source_target_pairs={{0,13},{1,12},{2,15},{3,14},{4,9},{5,8},{6,11},{7,10},{8,5},{9,4},... | collective-permute-start | bytes 344072 | tf_op jit(solution)/shard_map/ppermute | solution.py:276
  56.1 4.4 %collective-permute-start.9 = (bf16[32,1792]{1,0:T(8,128)(2,1)S(1)}, bf16[32,1792]{1,0:T(8,128)(2,1)S(1)}, u32[]{:S(2)}, u32[]{:S(2)}) collective-permute-start(bf16[32,1792]{1,0:T(8,128)(2,1)S(1)} %get-tuple-element.81), channel_id=1, source_target_pairs={{0,10},{1,11},{2,8},{3,9},{4,14},{5,15},{6,12},{7,13},{8,2},{9,3},... | collective-permute-start | bytes 344072 | tf_op jit(solution)/shard_map/ppermute | solution.py:276
  60.5 3.8 %collective-permute-start.11 = (bf16[32,1792]{1,0:T(8,128)(2,1)S(1)}, bf16[32,1792]{1,0:T(8,128)(2,1)S(1)}, u32[]{:S(2)}, u32[]{:S(2)}) collective-permute-start(bf16[32,1792]{1,0:T(8,128)(2,1)S(1)} %get-tuple-element.83), channel_id=1, source_target_pairs={{0,14},{1,15},{2,12},{3,13},{4,10},{5,11},{6,8},{7,9},{8,6},{9,7},... | collective-permute-start | bytes 344072 | tf_op jit(solution)/shard_map/ppermute | solution.py:276
  64.6 4.3 %collective-permute-start.13 = (bf16[32,1792]{1,0:T(8,128)(2,1)S(1)}, bf16[32,1792]{1,0:T(8,128)(2,1)S(1)}, u32[]{:S(2)}, u32[]{:S(2)}) collective-permute-start(bf16[32,1792]{1,0:T(8,128)(2,1)S(1)} %get-tuple-element.85), channel_id=1, source_target_pairs={{0,11},{1,10},{2,9},{3,8},{4,15},{5,14},{6,13},{7,12},{8,3},{9,2},... | collective-permute-start | bytes 344072 | tf_op jit(solution)/shard_map/ppermute | solution.py:276
  69.0 2.2 %collective-permute-start.14 = (bf16[32,1792]{1,0:T(8,128)(2,1)S(1)}, bf16[32,1792]{1,0:T(8,128)(2,1)S(1)}, u32[]{:S(2)}, u32[]{:S(2)}) collective-permute-start(bf16[32,1792]{1,0:T(8,128)(2,1)S(1)} %get-tuple-element.86), channel_id=1, source_target_pairs={{0,4},{1,5},{2,6},{3,7},{4,0},{5,1},{6,2},{7,3},{8,12},{9,13},{10,... | collective-permute-start | bytes 344072 | tf_op jit(solution)/shard_map/ppermute | solution.py:276
  71.1 4.6 %collective-permute-start.15 = (bf16[32,1792]{1,0:T(8,128)(2,1)S(1)}, bf16[32,1792]{1,0:T(8,128)(2,1)S(1)}, u32[]{:S(2)}, u32[]{:S(2)}) collective-permute-start(bf16[32,1792]{1,0:T(8,128)(2,1)S(1)} %get-tuple-element.87), channel_id=1, source_target_pairs={{0,15},{1,14},{2,13},{3,12},{4,11},{5,10},{6,9},{7,8},{8,7},{9,6},... | collective-permute-start | bytes 344072 | tf_op jit(solution)/shard_map/ppermute | solution.py:276
  76.5 2.4 %collective-permute-start.30 = (bf16[2,48,512]{2,1,0:T(8,128)(2,1)S(1)}, bf16[2,48,512]{2,1,0:T(8,128)(2,1)S(1)}, u32[]{:S(2)}, u32[]{:S(2)}) collective-permute-start(bf16[2,48,512]{2,1,0:T(8,128)(2,1)S(1)} %get-tuple-element.104), channel_id=1, source_target_pairs={{0,8},{1,9},{2,10},{3,11},{4,12},{5,13},{6,14},{7,15},{8,0},{9,1},... | collective-permute-start | bytes 294920 | tf_op jit(solution)/shard_map/ppermute | solution.py:276
  82.9 3.5 %collective-permute-start.33 = (bf16[2,48,512]{2,1,0:T(8,128)(2,1)S(1)}, bf16[2,48,512]{2,1,0:T(8,128)(2,1)S(1)}, u32[]{:S(2)}, u32[]{:S(2)}) collective-permute-start(bf16[2,48,512]{2,1,0:T(8,128)(2,1)S(1)} %get-tuple-element.107), channel_id=1, source_target_pairs={{0,3},{1,2},{2,1},{3,0},{4,7},{5,6},{6,5},{7,4},{8,11},{9,10},{10,... | collective-permute-start | bytes 294920 | tf_op jit(solution)/shard_map/ppermute | solution.py:276
  87.7 3.1 %collective-permute-done.30.refs_17_ = bf16[2,48,512]{2,1,0:T(8,128)(2,1)S(1)} collective-permute-done((bf16[2,48,512]{2,1,0:T(8,128)(2,1)S(1)}, bf16[2,48,512]{2,1,0:T(8,128)(2,1)S(1)}, u32[]{:S(2)}, u32[]{:S(2)}) %collective-permute-start.30) | collective-permute-done | bytes 98336 | tf_op jit(solution)/shard_map/ppermute | solution.py:276
  94.0 3.7 %collective-permute-start.38 = (bf16[2,48,512]{2,1,0:T(8,128)(2,1)S(1)}, bf16[2,48,512]{2,1,0:T(8,128)(2,1)S(1)}, u32[]{:S(2)}, u32[]{:S(2)}) collective-permute-start(bf16[2,48,512]{2,1,0:T(8,128)(2,1)S(1)} %get-tuple-element.112), channel_id=1, source_target_pairs={{0,10},{1,11},{2,8},{3,9},{4,14},{5,15},{6,12},{7,13},{8,2},{9,3},... | collective-permute-start | bytes 294920 | tf_op jit(solution)/shard_map/ppermute | solution.py:276
  97.7 2.6 %collective-permute-done.35.refs_22_ = bf16[2,48,512]{2,1,0:T(8,128)(2,1)S(1)} collective-permute-done((bf16[2,48,512]{2,1,0:T(8,128)(2,1)S(1)}, bf16[2,48,512]{2,1,0:T(8,128)(2,1)S(1)}, u32[]{:S(2)}, u32[]{:S(2)}) %collective-permute-start.35) | collective-permute-done | bytes 98336 | tf_op jit(solution)/shard_map/ppermute | solution.py:276
  100.3 2.6 %collective-permute-start.40 = (bf16[2,48,512]{2,1,0:T(8,128)(2,1)S(1)}, bf16[2,48,512]{2,1,0:T(8,128)(2,1)S(1)}, u32[]{:S(2)}, u32[]{:S(2)}) collective-permute-start(bf16[2,48,512]{2,1,0:T(8,128)(2,1)S(1)} %get-tuple-element.114), channel_id=1, source_target_pairs={{0,14},{1,15},{2,12},{3,13},{4,10},{5,11},{6,8},{7,9},{8,6},{9,7},... | collective-permute-start | bytes 294920 | tf_op jit(solution)/shard_map/ppermute | solution.py:276
  102.9 3.0 %collective-permute-start.42 = (bf16[2,48,512]{2,1,0:T(8,128)(2,1)S(1)}, bf16[2,48,512]{2,1,0:T(8,128)(2,1)S(1)}, u32[]{:S(2)}, u32[]{:S(2)}) collective-permute-start(bf16[2,48,512]{2,1,0:T(8,128)(2,1)S(1)} %get-tuple-element.116), channel_id=1, source_target_pairs={{0,11},{1,10},{2,9},{3,8},{4,15},{5,14},{6,13},{7,12},{8,3},{9,2},... | collective-permute-start | bytes 294920 | tf_op jit(solution)/shard_map/ppermute | solution.py:276
  107.8 7.4 %collective-permute-done.42.refs_29_ = bf16[2,48,512]{2,1,0:T(8,128)(2,1)S(1)} collective-permute-done((bf16[2,48,512]{2,1,0:T(8,128)(2,1)S(1)}, bf16[2,48,512]{2,1,0:T(8,128)(2,1)S(1)}, u32[]{:S(2)}, u32[]{:S(2)}) %collective-permute-start.42) | collective-permute-done | bytes 98336 | tf_op jit(solution)/shard_map/ppermute | solution.py:276
  115.1 4.7 %update.1 = (bf16[384,1024]{1,0:T(8,128)(2,1)}, bf16[384,1024]{1,0:T(8,128)(2,1)}, bf16[32,1024]{1,0:T(8,128)(2,1)S(1)}, bf16[32,1024]{1,0:T(8,128)(2,1)S(1)}, b...) custom-call(s32[1]{0:T(128)} %bitcast.me_ref, ...), custom_call_target="tpu_custom_call" | custom-call | flops 2239758336 | bytes 6029312 | tf_op jit(solution)/shard_map/update/pallas_call | solution.py:213
  119.9 3.9 %collective-permute-start.45 = (bf16[32,1024]{1,0:T(8,128)(2,1)S(1)}, bf16[32,1024]{1,0:T(8,128)(2,1)S(1)}, u32[]{:S(2)}, u32[]{:S(2)}) collective-permute-start(bf16[32,1024]{1,0:T(8,128)(2,1)S(1)} %get-tuple-element.124), channel_id=1, source_target_pairs={{0,8},{1,9},{2,10},{3,11},{4,12},{5,13},{6,14},{7,15},{8,0},{9,1},... | collective-permute-start | bytes 196616 | tf_op jit(solution)/shard_map/ppermute | solution.py:276
  126.2 2.1 %collective-permute-start.49 = (bf16[32,1024]{1,0:T(8,128)(2,1)S(1)}, bf16[32,1024]{1,0:T(8,128)(2,1)S(1)}, u32[]{:S(2)}, u32[]{:S(2)}) collective-permute-start(bf16[32,1024]{1,0:T(8,128)(2,1)S(1)} %get-tuple-element.128), channel_id=1, source_target_pairs={{0,9},{1,8},{2,11},{3,10},{4,13},{5,12},{6,15},{7,14},{8,1},{9,0},... | collective-permute-start | bytes 196616 | tf_op jit(solution)/shard_map/ppermute | solution.py:276
  132.1 2.6 %collective-permute-start.53 = (bf16[32,1024]{1,0:T(8,128)(2,1)S(1)}, bf16[32,1024]{1,0:T(8,128)(2,1)S(1)}, u32[]{:S(2)}, u32[]{:S(2)}) collective-permute-start(bf16[32,1024]{1,0:T(8,128)(2,1)S(1)} %get-tuple-element.132), channel_id=1, source_target_pairs={{0,10},{1,11},{2,8},{3,9},{4,14},{5,15},{6,12},{7,13},{8,2},{9,3},... | collective-permute-start | bytes 196616 | tf_op jit(solution)/shard_map/ppermute | solution.py:276
  134.8 3.1 %collective-permute-start.55 = (bf16[32,1024]{1,0:T(8,128)(2,1)S(1)}, bf16[32,1024]{1,0:T(8,128)(2,1)S(1)}, u32[]{:S(2)}, u32[]{:S(2)}) collective-permute-start(bf16[32,1024]{1,0:T(8,128)(2,1)S(1)} %get-tuple-element.134), channel_id=1, source_target_pairs={{0,14},{1,15},{2,12},{3,13},{4,10},{5,11},{6,8},{7,9},{8,6},{9,7},... | collective-permute-start | bytes 196616 | tf_op jit(solution)/shard_map/ppermute | solution.py:276
  142.7 2.9 %collective-permute-done.57.refs_13_ = bf16[32,1024]{1,0:T(8,128)(2,1)S(1)} collective-permute-done((bf16[32,1024]{1,0:T(8,128)(2,1)S(1)}, bf16[32,1024]{1,0:T(8,128)(2,1)S(1)}, u32[]{:S(2)}, u32[]{:S(2)}) %collective-permute-start.57) | collective-permute-done | bytes 65568 | tf_op jit(solution)/shard_map/ppermute | solution.py:276
  145.6 2.1 %collective-permute-done.59.refs_15_ = bf16[32,1024]{1,0:T(8,128)(2,1)S(1)} collective-permute-done((bf16[32,1024]{1,0:T(8,128)(2,1)S(1)}, bf16[32,1024]{1,0:T(8,128)(2,1)S(1)}, u32[]{:S(2)}, u32[]{:S(2)}) %collective-permute-start.59) | collective-permute-done | bytes 65568 | tf_op jit(solution)/shard_map/ppermute | solution.py:276
  (109 shorter events, 38.1 us)
Async XLA Ops:
  11.3 13.0 %collective-permute-start.20 = (bf16[2,48,512]{2,1,0:T(8,128)(2,1)}, bf16[2,48,512]{2,1,0:T(8,128)(2,1)S(1)}, u32[]{:S(2)}, u32[]{:S(2)}) collective-permute-start(bf16[2,48,512]{2,1,0:T(8,128)(2,1)} %get-tuple-element.93), channel_id=1, source_target_pairs={{0,9},{1,8},{2,11},{3,10},{4,13},{5,12},{6,15},{7,14},{8,1},{9,0},... | collective-permute-start | bytes 294920 | tf_op jit(solution)/shard_map/ppermute | solution.py:276
  14.5 13.6 %collective-permute-start.21 = (bf16[2,48,512]{2,1,0:T(8,128)(2,1)}, bf16[2,48,512]{2,1,0:T(8,128)(2,1)S(1)}, u32[]{:S(2)}, u32[]{:S(2)}) collective-permute-start(bf16[2,48,512]{2,1,0:T(8,128)(2,1)} %get-tuple-element.94), channel_id=1, source_target_pairs={{0,6},{1,7},{2,4},{3,5},{4,2},{5,3},{6,0},{7,1},{8,14},{9,15},{10,... | collective-permute-start | bytes 294920 | tf_op jit(solution)/shard_map/ppermute | solution.py:276
  16.1 12.3 %collective-permute-start.22 = (bf16[2,48,512]{2,1,0:T(8,128)(2,1)}, bf16[2,48,512]{2,1,0:T(8,128)(2,1)S(1)}, u32[]{:S(2)}, u32[]{:S(2)}) collective-permute-start(bf16[2,48,512]{2,1,0:T(8,128)(2,1)} %get-tuple-element.95), channel_id=1, source_target_pairs={{0,13},{1,12},{2,15},{3,14},{4,9},{5,8},{6,11},{7,10},{8,5},{9,4},... | collective-permute-start | bytes 294920 | tf_op jit(solution)/shard_map/ppermute | solution.py:276
  18.9 12.7 %collective-permute-start.23 = (bf16[2,48,512]{2,1,0:T(8,128)(2,1)}, bf16[2,48,512]{2,1,0:T(8,128)(2,1)S(1)}, u32[]{:S(2)}, u32[]{:S(2)}) collective-permute-start(bf16[2,48,512]{2,1,0:T(8,128)(2,1)} %get-tuple-element.96), channel_id=1, source_target_pairs={{0,2},{1,3},{2,0},{3,1},{4,6},{5,7},{6,4},{7,5},{8,10},{9,11},{10,... | collective-permute-start | bytes 294920 | tf_op jit(solution)/shard_map/ppermute | solution.py:276
  20.4 14.1 %collective-permute-start.24 = (bf16[2,48,512]{2,1,0:T(8,128)(2,1)}, bf16[2,48,512]{2,1,0:T(8,128)(2,1)S(1)}, u32[]{:S(2)}, u32[]{:S(2)}) collective-permute-start(bf16[2,48,512]{2,1,0:T(8,128)(2,1)} %get-tuple-element.97), channel_id=1, source_target_pairs={{0,10},{1,11},{2,8},{3,9},{4,14},{5,15},{6,12},{7,13},{8,2},{9,3},... | collective-permute-start | bytes 294920 | tf_op jit(solution)/shard_map/ppermute | solution.py:276
  24.3 16.0 %collective-permute-start.25 = (bf16[2,48,512]{2,1,0:T(8,128)(2,1)}, bf16[2,48,512]{2,1,0:T(8,128)(2,1)S(1)}, u32[]{:S(2)}, u32[]{:S(2)}) collective-permute-start(bf16[2,48,512]{2,1,0:T(8,128)(2,1)} %get-tuple-element.98), channel_id=1, source_target_pairs={{0,14},{1,15},{2,12},{3,13},{4,10},{5,11},{6,8},{7,9},{8,6},{9,7},... | collective-permute-start | bytes 294920 | tf_op jit(solution)/shard_map/ppermute | solution.py:276
  28.1 12.6 %collective-permute-start.26 = (bf16[2,48,512]{2,1,0:T(8,128)(2,1)}, bf16[2,48,512]{2,1,0:T(8,128)(2,1)S(1)}, u32[]{:S(2)}, u32[]{:S(2)}) collective-permute-start(bf16[2,48,512]{2,1,0:T(8,128)(2,1)} %get-tuple-element.99), channel_id=1, source_target_pairs={{0,1},{1,0},{2,3},{3,2},{4,5},{5,4},{6,7},{7,6},{8,9},{9,8},{10,11... | collective-permute-start | bytes 294920 | tf_op jit(solution)/shard_map/ppermute | solution.py:276
  28.5 14.9 %collective-permute-start.27 = (bf16[2,48,512]{2,1,0:T(8,128)(2,1)}, bf16[2,48,512]{2,1,0:T(8,128)(2,1)S(1)}, u32[]{:S(2)}, u32[]{:S(2)}) collective-permute-start(bf16[2,48,512]{2,1,0:T(8,128)(2,1)} %get-tuple-element.100), channel_id=1, source_target_pairs={{0,11},{1,10},{2,9},{3,8},{4,15},{5,14},{6,13},{7,12},{8,3},{9,2},... | collective-permute-start | bytes 294920 | tf_op jit(solution)/shard_map/ppermute | solution.py:276
  31.7 16.8 %collective-permute-start.28 = (bf16[2,48,512]{2,1,0:T(8,128)(2,1)}, bf16[2,48,512]{2,1,0:T(8,128)(2,1)S(1)}, u32[]{:S(2)}, u32[]{:S(2)}) collective-permute-start(bf16[2,48,512]{2,1,0:T(8,128)(2,1)} %get-tuple-element.101), channel_id=1, source_target_pairs={{0,4},{1,5},{2,6},{3,7},{4,0},{5,1},{6,2},{7,3},{8,12},{9,13},{10,... | collective-permute-start | bytes 294920 | tf_op jit(solution)/shard_map/ppermute | solution.py:276
  34.4 14.0 %collective-permute-start.29 = (bf16[2,48,512]{2,1,0:T(8,128)(2,1)}, bf16[2,48,512]{2,1,0:T(8,128)(2,1)S(1)}, u32[]{:S(2)}, u32[]{:S(2)}) collective-permute-start(bf16[2,48,512]{2,1,0:T(8,128)(2,1)} %get-tuple-element.102), channel_id=1, source_target_pairs={{0,15},{1,14},{2,13},{3,12},{4,11},{5,10},{6,9},{7,8},{8,7},{9,6},... | collective-permute-start | bytes 294920 | tf_op jit(solution)/shard_map/ppermute | solution.py:276
  40.7 9.8 %collective-permute-start.2 = (bf16[32,1792]{1,0:T(8,128)(2,1)S(1)}, bf16[32,1792]{1,0:T(8,128)(2,1)S(1)}, u32[]{:S(2)}, u32[]{:S(2)}) collective-permute-start(bf16[32,1792]{1,0:T(8,128)(2,1)S(1)} %get-tuple-element.74), channel_id=1, source_target_pairs={{0,7},{1,6},{2,5},{3,4},{4,3},{5,2},{6,1},{7,0},{8,15},{9,14},{10,... | collective-permute-start | bytes 344072 | tf_op jit(solution)/shard_map/ppermute | solution.py:276
  43.4 12.7 %collective-permute-start.3 = (bf16[32,1792]{1,0:T(8,128)(2,1)S(1)}, bf16[32,1792]{1,0:T(8,128)(2,1)S(1)}, u32[]{:S(2)}, u32[]{:S(2)}) collective-permute-start(bf16[32,1792]{1,0:T(8,128)(2,1)S(1)} %get-tuple-element.75), channel_id=1, source_target_pairs={{0,12},{1,13},{2,14},{3,15},{4,8},{5,9},{6,10},{7,11},{8,4},{9,5},... | collective-permute-start | bytes 344072 | tf_op jit(solution)/shard_map/ppermute | solution.py:276
  48.4 12.1 %collective-permute-start.5 = (bf16[32,1792]{1,0:T(8,128)(2,1)S(1)}, bf16[32,1792]{1,0:T(8,128)(2,1)S(1)}, u32[]{:S(2)}, u32[]{:S(2)}) collective-permute-start(bf16[32,1792]{1,0:T(8,128)(2,1)S(1)} %get-tuple-element.77), channel_id=1, source_target_pairs={{0,9},{1,8},{2,11},{3,10},{4,13},{5,12},{6,15},{7,14},{8,1},{9,0},... | collective-permute-start | bytes 344072 | tf_op jit(solution)/shard_map/ppermute | solution.py:276
  49.0 11.5 %collective-permute-start.6 = (bf16[32,1792]{1,0:T(8,128)(2,1)S(1)}, bf16[32,1792]{1,0:T(8,128)(2,1)S(1)}, u32[]{:S(2)}, u32[]{:S(2)}) collective-permute-start(bf16[32,1792]{1,0:T(8,128)(2,1)S(1)} %get-tuple-element.78), channel_id=1, source_target_pairs={{0,6},{1,7},{2,4},{3,5},{4,2},{5,3},{6,0},{7,1},{8,14},{9,15},{10,... | collective-permute-start | bytes 344072 | tf_op jit(solution)/shard_map/ppermute | solution.py:276
  50.4 13.8 %collective-permute-start.7 = (bf16[32,1792]{1,0:T(8,128)(2,1)S(1)}, bf16[32,1792]{1,0:T(8,128)(2,1)S(1)}, u32[]{:S(2)}, u32[]{:S(2)}) collective-permute-start(bf16[32,1792]{1,0:T(8,128)(2,1)S(1)} %get-tuple-element.79), channel_id=1, source_target_pairs={{0,13},{1,12},{2,15},{3,14},{4,9},{5,8},{6,11},{7,10},{8,5},{9,4},... | collective-permute-start | bytes 344072 | tf_op jit(solution)/shard_map/ppermute | solution.py:276
  56.1 12.9 %collective-permute-start.9 = (bf16[32,1792]{1,0:T(8,128)(2,1)S(1)}, bf16[32,1792]{1,0:T(8,128)(2,1)S(1)}, u32[]{:S(2)}, u32[]{:S(2)}) collective-permute-start(bf16[32,1792]{1,0:T(8,128)(2,1)S(1)} %get-tuple-element.81), channel_id=1, source_target_pairs={{0,10},{1,11},{2,8},{3,9},{4,14},{5,15},{6,12},{7,13},{8,2},{9,3},... | collective-permute-start | bytes 344072 | tf_op jit(solution)/shard_map/ppermute | solution.py:276
  60.5 10.6 %collective-permute-start.10 = (bf16[32,1792]{1,0:T(8,128)(2,1)S(1)}, bf16[32,1792]{1,0:T(8,128)(2,1)S(1)}, u32[]{:S(2)}, u32[]{:S(2)}) collective-permute-start(bf16[32,1792]{1,0:T(8,128)(2,1)S(1)} %get-tuple-element.82), channel_id=1, source_target_pairs={{0,5},{1,4},{2,7},{3,6},{4,1},{5,0},{6,3},{7,2},{8,13},{9,12},{10,... | collective-permute-start | bytes 344072 | tf_op jit(solution)/shard_map/ppermute | solution.py:276
  60.5 16.0 %collective-permute-start.11 = (bf16[32,1792]{1,0:T(8,128)(2,1)S(1)}, bf16[32,1792]{1,0:T(8,128)(2,1)S(1)}, u32[]{:S(2)}, u32[]{:S(2)}) collective-permute-start(bf16[32,1792]{1,0:T(8,128)(2,1)S(1)} %get-tuple-element.83), channel_id=1, source_target_pairs={{0,14},{1,15},{2,12},{3,13},{4,10},{5,11},{6,8},{7,9},{8,6},{9,7},... | collective-permute-start | bytes 344072 | tf_op jit(solution)/shard_map/ppermute | solution.py:276
  64.3 14.7 %collective-permute-start.12 = (bf16[32,1792]{1,0:T(8,128)(2,1)S(1)}, bf16[32,1792]{1,0:T(8,128)(2,1)S(1)}, u32[]{:S(2)}, u32[]{:S(2)}) collective-permute-start(bf16[32,1792]{1,0:T(8,128)(2,1)S(1)} %get-tuple-element.84), channel_id=1, source_target_pairs={{0,1},{1,0},{2,3},{3,2},{4,5},{5,4},{6,7},{7,6},{8,9},{9,8},{10,11... | collective-permute-start | bytes 344072 | tf_op jit(solution)/shard_map/ppermute | solution.py:276
  64.6 16.2 %collective-permute-start.13 = (bf16[32,1792]{1,0:T(8,128)(2,1)S(1)}, bf16[32,1792]{1,0:T(8,128)(2,1)S(1)}, u32[]{:S(2)}, u32[]{:S(2)}) collective-permute-start(bf16[32,1792]{1,0:T(8,128)(2,1)S(1)} %get-tuple-element.85), channel_id=1, source_target_pairs={{0,11},{1,10},{2,9},{3,8},{4,15},{5,14},{6,13},{7,12},{8,3},{9,2},... | collective-permute-start | bytes 344072 | tf_op jit(solution)/shard_map/ppermute | solution.py:276
  69.0 14.0 %collective-permute-start.14 = (bf16[32,1792]{1,0:T(8,128)(2,1)S(1)}, bf16[32,1792]{1,0:T(8,128)(2,1)S(1)}, u32[]{:S(2)}, u32[]{:S(2)}) collective-permute-start(bf16[32,1792]{1,0:T(8,128)(2,1)S(1)} %get-tuple-element.86), channel_id=1, source_target_pairs={{0,4},{1,5},{2,6},{3,7},{4,0},{5,1},{6,2},{7,3},{8,12},{9,13},{10,... | collective-permute-start | bytes 344072 | tf_op jit(solution)/shard_map/ppermute | solution.py:276
  71.1 15.4 %collective-permute-start.15 = (bf16[32,1792]{1,0:T(8,128)(2,1)S(1)}, bf16[32,1792]{1,0:T(8,128)(2,1)S(1)}, u32[]{:S(2)}, u32[]{:S(2)}) collective-permute-start(bf16[32,1792]{1,0:T(8,128)(2,1)S(1)} %get-tuple-element.87), channel_id=1, source_target_pairs={{0,15},{1,14},{2,13},{3,12},{4,11},{5,10},{6,9},{7,8},{8,7},{9,6},... | collective-permute-start | bytes 344072 | tf_op jit(solution)/shard_map/ppermute | solution.py:276
  76.5 14.2 %collective-permute-start.30 = (bf16[2,48,512]{2,1,0:T(8,128)(2,1)S(1)}, bf16[2,48,512]{2,1,0:T(8,128)(2,1)S(1)}, u32[]{:S(2)}, u32[]{:S(2)}) collective-permute-start(bf16[2,48,512]{2,1,0:T(8,128)(2,1)S(1)} %get-tuple-element.104), channel_id=1, source_target_pairs={{0,8},{1,9},{2,10},{3,11},{4,12},{5,13},{6,14},{7,15},{8,0},{9,1},... | collective-permute-start | bytes 294920 | tf_op jit(solution)/shard_map/ppermute | solution.py:276
  78.9 11.8 %collective-permute-start.31 = (bf16[2,48,512]{2,1,0:T(8,128)(2,1)S(1)}, bf16[2,48,512]{2,1,0:T(8,128)(2,1)S(1)}, u32[]{:S(2)}, u32[]{:S(2)}) collective-permute-start(bf16[2,48,512]{2,1,0:T(8,128)(2,1)S(1)} %get-tuple-element.105), channel_id=1, source_target_pairs={{0,7},{1,6},{2,5},{3,4},{4,3},{5,2},{6,1},{7,0},{8,15},{9,14},{10,... | collective-permute-start | bytes 294920 | tf_op jit(solution)/shard_map/ppermute | solution.py:276
  80.8 11.7 %collective-permute-start.32 = (bf16[2,48,512]{2,1,0:T(8,128)(2,1)S(1)}, bf16[2,48,512]{2,1,0:T(8,128)(2,1)S(1)}, u32[]{:S(2)}, u32[]{:S(2)}) collective-permute-start(bf16[2,48,512]{2,1,0:T(8,128)(2,1)S(1)} %get-tuple-element.106), channel_id=1, source_target_pairs={{0,12},{1,13},{2,14},{3,15},{4,8},{5,9},{6,10},{7,11},{8,4},{9,5},... | collective-permute-start | bytes 294920 | tf_op jit(solution)/shard_map/ppermute | solution.py:276
  82.9 11.0 %collective-permute-start.33 = (bf16[2,48,512]{2,1,0:T(8,128)(2,1)S(1)}, bf16[2,48,512]{2,1,0:T(8,128)(2,1)S(1)}, u32[]{:S(2)}, u32[]{:S(2)}) collective-permute-start(bf16[2,48,512]{2,1,0:T(8,128)(2,1)S(1)} %get-tuple-element.107), channel_id=1, source_target_pairs={{0,3},{1,2},{2,1},{3,0},{4,7},{5,6},{6,5},{7,4},{8,11},{9,10},{10,... | collective-permute-start | bytes 294920 | tf_op jit(solution)/shard_map/ppermute | solution.py:276
  86.5 11.2 %collective-permute-start.34 = (bf16[2,48,512]{2,1,0:T(8,128)(2,1)S(1)}, bf16[2,48,512]{2,1,0:T(8,128)(2,1)S(1)}, u32[]{:S(2)}, u32[]{:S(2)}) collective-permute-start(bf16[2,48,512]{2,1,0:T(8,128)(2,1)S(1)} %get-tuple-element.108), channel_id=1, source_target_pairs={{0,9},{1,8},{2,11},{3,10},{4,13},{5,12},{6,15},{7,14},{8,1},{9,0},... | collective-permute-start | bytes 294920 | tf_op jit(solution)/shard_map/ppermute | solution.py:276
  90.7 9.5 %collective-permute-start.35 = (bf16[2,48,512]{2,1,0:T(8,128)(2,1)S(1)}, bf16[2,48,512]{2,1,0:T(8,128)(2,1)S(1)}, u32[]{:S(2)}, u32[]{:S(2)}) collective-permute-start(bf16[2,48,512]{2,1,0:T(8,128)(2,1)S(1)} %get-tuple-element.109), channel_id=1, source_target_pairs={{0,6},{1,7},{2,4},{3,5},{4,2},{5,3},{6,0},{7,1},{8,14},{9,15},{10,... | collective-permute-start | bytes 294920 | tf_op jit(solution)/shard_map/ppermute | solution.py:276
  90.8 12.1 %collective-permute-start.36 = (bf16[2,48,512]{2,1,0:T(8,128)(2,1)S(1)}, bf16[2,48,512]{2,1,0:T(8,128)(2,1)S(1)}, u32[]{:S(2)}, u32[]{:S(2)}) collective-permute-start(bf16[2,48,512]{2,1,0:T(8,128)(2,1)S(1)} %get-tuple-element.110), channel_id=1, source_target_pairs={{0,13},{1,12},{2,15},{3,14},{4,9},{5,8},{6,11},{7,10},{8,5},{9,4},... | collective-permute-start | bytes 294920 | tf_op jit(solution)/shard_map/ppermute | solution.py:276
  92.5 10.3 %collective-permute-start.37 = (bf16[2,48,512]{2,1,0:T(8,128)(2,1)S(1)}, bf16[2,48,512]{2,1,0:T(8,128)(2,1)S(1)}, u32[]{:S(2)}, u32[]{:S(2)}) collective-permute-start(bf16[2,48,512]{2,1,0:T(8,128)(2,1)S(1)} %get-tuple-element.111), channel_id=1, source_target_pairs={{0,2},{1,3},{2,0},{3,1},{4,6},{5,7},{6,4},{7,5},{8,10},{9,11},{10,... | collective-permute-start | bytes 294920 | tf_op jit(solution)/shard_map/ppermute | solution.py:276
  94.0 12.6 %collective-permute-start.38 = (bf16[2,48,512]{2,1,0:T(8,128)(2,1)S(1)}, bf16[2,48,512]{2,1,0:T(8,128)(2,1)S(1)}, u32[]{:S(2)}, u32[]{:S(2)}) collective-permute-start(bf16[2,48,512]{2,1,0:T(8,128)(2,1)S(1)} %get-tuple-element.112), channel_id=1, source_target_pairs={{0,10},{1,11},{2,8},{3,9},{4,14},{5,15},{6,12},{7,13},{8,2},{9,3},... | collective-permute-start | bytes 294920 | tf_op jit(solution)/shard_map/ppermute | solution.py:276
  102.9 12.3 %collective-permute-start.42 = (bf16[2,48,512]{2,1,0:T(8,128)(2,1)S(1)}, bf16[2,48,512]{2,1,0:T(8,128)(2,1)S(1)}, u32[]{:S(2)}, u32[]{:S(2)}) collective-permute-start(bf16[2,48,512]{2,1,0:T(8,128)(2,1)S(1)} %get-tuple-element.116), channel_id=1, source_target_pairs={{0,11},{1,10},{2,9},{3,8},{4,15},{5,14},{6,13},{7,12},{8,3},{9,2},... | collective-permute-start | bytes 294920 | tf_op jit(solution)/shard_map/ppermute | solution.py:276
  (36 other events, 391.5 us)

commit v11 on v10

--- a/solution.py
+++ b/solution.py
@@ -120,26 +120,33 @@
     return pieces, slot, gates
 
 
-def split_kernel(me_ref, moment_ref, weight_ref, *refs):
-    pieces, held, sem = refs[:-3], refs[-3:-1], refs[-1]
-    fetched((moment_ref, weight_ref), held, sem)
-    for s, piece in zip(mixed_order(len(pieces)), pieces):
+def split_kernel(partners, me_ref, moment_ref, weight_ref, *refs):
+    pieces, sem = refs[:-1], refs[-1]
+    copies = []
+    for s, piece in zip(partners, pieces):
         rows, columns = piece.shape[1:]
-        for lead, source in enumerate(held):
-            piece[lead] = chunk_at(source, 0, me_ref[0] ^ s, rows, columns)[...]
-
-
-def split(me, moment, weight, groups):
+        for lead, source in enumerate((moment_ref, weight_ref)):
+            chunk = chunk_at(source, 0, me_ref[0] ^ s, rows, columns)
+            copies.append(pltpu.make_async_copy(chunk, piece.at[lead], sem.at[len(copies)]))
+    for copy in copies:
+        copy.start()
+    for copy in copies:
+        copy.wait()
+
+
+def split(me, moment, weight, groups, partners):
     _, ff, d = weight.shape
     piece = jax.ShapeDtypeStruct((2, ff // (groups // 2), d // 2), BF16)
     return pl.pallas_call(
-        split_kernel,
-        out_shape=(piece,) * groups,
+        functools.partial(split_kernel, partners),
+        out_shape=(piece,) * len(partners),
         in_specs=[SMEM, HBM, HBM],
-        out_specs=(VMEM,) * groups,
-        scratch_shapes=rooms((moment, weight)),
+        out_specs=(VMEM,) * len(partners),
+        scratch_shapes=[pltpu.SemaphoreType.DMA((2 * len(partners),))],
         compiler_params=pltpu.CompilerParams(vmem_limit_bytes=60 * MIB),
-        cost_estimate=pl.CostEstimate(flops=0, bytes_accessed=8 * ff * d, transcendentals=0),
+        cost_estimate=pl.CostEstimate(
+            flops=0, bytes_accessed=8 * ff * d * len(partners) // groups, transcendentals=0
+        ),
         name="split",
     )(me, moment, weight)
 
@@ -150,7 +157,7 @@
     me, order = me_ref[0], mixed_order(groups)
     for s, source in zip(order, sources):
         held[me ^ perm_ref[me ^ s]] = source[...]
-    for s, target in zip(order, targets):
+    for s, target in zip(ending_near(groups), targets):
         target[...] = held[s]
 
 
@@ -177,7 +184,7 @@
     capacity = packed[0].shape[0]
     for n, piece in enumerate(packed):
         rows_ref[n * capacity : (n + 1) * capacity] = piece[...]
-    for s, piece in zip(mixed_order(groups), pieces):
+    for s, piece in zip(ending_near(groups), pieces):
         rows, columns = piece.shape[1:]
         for lead in range(2):
             chunk_at(held, lead, me_ref[0] ^ s, rows, columns)[...] = piece[lead]
@@ -201,7 +208,9 @@
     weight_new = (held[1].astype(F32) - step_scale * current.astype(F32)).astype(BF16)
     weight_new_ref[...] = weight_new
     product = jnp.dot(rows_ref[:, ff + d :], weight_new, preferred_element_type=F32).astype(BF16)
-    for n, piece in enumerate(produced):
+    came = mixed_order(groups)
+    for s, piece in zip(ending_near(groups), produced):
+        n = came.index(s)
         piece[...] = product[n * capacity : (n + 1) * capacity]
 
 
@@ -230,7 +239,7 @@
 def finish_kernel(groups, slot_ref, gates_ref, *refs):
     pieces, (out_ref, returned_ref) = refs[:groups], refs[groups:]
     capacity = pieces[0].shape[0]
-    for s, piece in zip(mixed_order(groups), pieces):
+    for s, piece in zip(ending_near(groups), pieces):
         returned_ref[s * capacity : (s + 1) * capacity] = piece[...]
     selector = selector_of(slot_ref[...], groups * capacity)
     expert_out = lax.dot_general(
@@ -269,11 +278,16 @@
     return [0] + [s for pair in zip(far, near + [None]) for s in pair if s is not None]
 
 
-def swap(pieces):
-    groups = len(pieces)
+def ending_near(groups):
     order = mixed_order(groups)
-    return [pieces[0]] + [
-        lax.ppermute(piece, "expert", [(i, i ^ s) for i in range(groups)]) for s, piece in zip(order[1:], pieces[1:])
+    return order[:-4] + [order[n] for n in (-3, -4, -1, -2)] if groups > 4 else order
+
+
+def swap(pieces, order):
+    groups = lax.axis_size("expert")
+    return [
+        lax.ppermute(piece, "expert", [(i, i ^ s) for i in range(groups)]) if s else piece
+        for s, piece in zip(order, pieces)
     ]
 
 
@@ -284,15 +298,20 @@
     me = lax.axis_index("expert").astype(jnp.int32).reshape(1)
     capacity = max(4, 2 * grad_hidden.shape[0] // groups)
     ff, d = w_down.shape[1:]
-    spread = swap(split(me, w_moment, w_down, groups))
+    order, last_order = mixed_order(groups), ending_near(groups)
+    first = order[1:6]
+    blocks = dict(zip(first, split(me, w_moment, w_down, groups, first)))
+    others = [s for s in order if s not in first]
+    blocks.update(zip(others, split(me, w_moment, w_down, groups, others)))
+    spread = swap([blocks[s] for s in order], order)
     packed, fwd_slot, gates = pack_rows(
         live_rows, me, perm, grad_route, fwd_route, grad_hidden, grad_out, fwd_hidden, fwd_gate,
-        spread[2 * groups // 3], groups, capacity,
-    )
-    received = swap(packed)
-    placed = swap(reorder(me, perm, spread, received[groups // 3]))
+        spread[1], groups, capacity,
+    )
+    received = swap(packed, order)
+    placed = swap(reorder(me, perm, spread, received[groups // 3]), last_order)
     weight_new, moment_new, produced = update(me, received, placed, ff, d)
-    return weight_new[None], moment_new[None], finish(fwd_slot, gates, swap(produced))
+    return weight_new[None], moment_new[None], finish(fwd_slot, gates, swap(produced, last_order))
 
 
 def lookup(route_ids, mapping):

time: 149 us -> 151 us (1.013)
  waiting for transfers between devices: 24.5 us -> 42 us
  starting transfers between devices: 110 us -> 92.7 us
  Pallas kernels: 12.3 us -> 14 us
    ppermute x60, waiting for transfers between devices: 24.5 us -> 42 us  [swap(): lax.ppermute(piece, 'expert', [(i, i ^ s) for i in range(groups)])]
    ppermute x60, starting transfers between devices: 110 us -> 92.7 us  [swap(): lax.ppermute(piece, 'expert', [(i, i ^ s) for i in range(groups)])]
    pallas_call x1 -> x2, Pallas kernels: 2.71 us -> 4.34 us  [split(): pl.pallas_call(functools.partial(split_kernel, partners), out_shape=(piec...]
  transfers between devices with their start and end apart: 60 -> 60, of which waited for: 12 -> 19; matrix products, arithmetic and copies ran while one was open for 0% -> 0% of each run, Pallas kernels for 2% -> 4%
where the time goes in v11:
time: 151 us
  starting transfers between devices  92.7 us (61%)
  waiting for transfers between devices  42 us (28%)
  Pallas kernels  14 us (9%)
    ppermute x60, starting transfers between devices, swap(): lax.ppermute(piece, 'expert', [(i, i ^ s) for i in range(groups)])  92.7 us
    ppermute x60, waiting for transfers between devices, swap(): lax.ppermute(piece, 'expert', [(i, i ^ s) for i in range(groups)])  42 us
    pallas_call x1, Pallas kernels, update(): pl.pallas_call(functools.partial(update_kernel, groups), out_shape=(shape...  4.82 us
    pallas_call x2, Pallas kernels, split(): pl.pallas_call(functools.partial(split_kernel, partners), out_shape=(piec...  4.34 us
  transfers between devices with their start and end apart: 60, of which 19 were waited for; matrix products, arithmetic and copies ran while one was open for 0% of the time, Pallas kernels for 4%

profile of v11, /device:TPU:0, one launch (start us, length us, event | category | flops | bytes accessed | tf_op | source)
XLA Modules:
  0.0 150.9 jit_solution(631603973679605544)
XLA Ops:
  0.6 1.9 %split.2 = (bf16[2,48,512]{2,1,0:T(8,128)(2,1)}, bf16[2,48,512]{2,1,0:T(8,128)(2,1)}, bf16[2,48,512]{2,1,0:T(8,128)(2,1)}, bf16[2,48,512]{2,1,0:T(8,128)(2,1)}, bf16[2,48,512]{2,1,0:T(8,128)(2,1)}) custom-call(s32[1]{0:T(128)} %bitcast.me_ref, bf16[1,384,1024]{2,1,0:T(8,128)(2,1)} %moment_ref.3, bf16[1,384,1024]{2,1,0:T(8,128)(2,1)} %weight_ref.3), custom_call_target="tpu_custom_call" | custom-call | bytes 983040 | tf_op jit(solution)/shard_map/split/pallas_call | solution.py:140
  2.5 4.1 %collective-permute-start = (bf16[2,48,512]{2,1,0:T(8,128)(2,1)}, bf16[2,48,512]{2,1,0:T(8,128)(2,1)S(1)}, u32[]{:S(2)}, u32[]{:S(2)}) collective-permute-start(bf16[2,48,512]{2,1,0:T(8,128)(2,1)} %get-tuple-element.71), channel_id=1, source_target_pairs={{0,8},{1,9},{2,10},{3,11},{4,12},{5,13},{6,14},{7,15},{8,0},{9,1},... | collective-permute-start | bytes 294920 | tf_op jit(solution)/shard_map/ppermute | solution.py:289
  10.9 2.5 %split.3 = (bf16[2,48,512]{2,1,0:T(8,128)(2,1)}, bf16[2,48,512]{2,1,0:T(8,128)(2,1)}, bf16[2,48,512]{2,1,0:T(8,128)(2,1)}, bf16[2,48,512]{2,1,0:T(8,128)(2,1)}, ...) custom-call(s32[1]{0:T(128)} %bitcast.me_ref, ...), custom_call_target="tpu_custom_call" | custom-call | bytes 2162688 | tf_op jit(solution)/shard_map/split/pallas_call | solution.py:140
  13.4 3.0 %collective-permute-start.20 = (bf16[2,48,512]{2,1,0:T(8,128)(2,1)}, bf16[2,48,512]{2,1,0:T(8,128)(2,1)S(1)}, u32[]{:S(2)}, u32[]{:S(2)}) collective-permute-start(bf16[2,48,512]{2,1,0:T(8,128)(2,1)} %get-tuple-element.93), channel_id=1, source_target_pairs={{0,6},{1,7},{2,4},{3,5},{4,2},{5,3},{6,0},{7,1},{8,14},{9,15},{10,... | collective-permute-start | bytes 294920 | tf_op jit(solution)/shard_map/ppermute | solution.py:289
  17.2 5.1 %collective-permute-start.23 = (bf16[2,48,512]{2,1,0:T(8,128)(2,1)}, bf16[2,48,512]{2,1,0:T(8,128)(2,1)S(1)}, u32[]{:S(2)}, u32[]{:S(2)}) collective-permute-start(bf16[2,48,512]{2,1,0:T(8,128)(2,1)} %get-tuple-element.96), channel_id=1, source_target_pairs={{0,10},{1,11},{2,8},{3,9},{4,14},{5,15},{6,12},{7,13},{8,2},{9,3},... | collective-permute-start | bytes 294920 | tf_op jit(solution)/shard_map/ppermute | solution.py:289
  22.3 2.2 %collective-permute-done.20.refs_6_ = bf16[2,48,512]{2,1,0:T(8,128)(2,1)S(1)} collective-permute-done((bf16[2,48,512]{2,1,0:T(8,128)(2,1)}, bf16[2,48,512]{2,1,0:T(8,128)(2,1)S(1)}, u32[]{:S(2)}, u32[]{:S(2)}) %collective-permute-start.20) | collective-permute-done | bytes 98336 | tf_op jit(solution)/shard_map/ppermute | solution.py:289
  24.5 2.2 %collective-permute-start.25 = (bf16[2,48,512]{2,1,0:T(8,128)(2,1)}, bf16[2,48,512]{2,1,0:T(8,128)(2,1)S(1)}, u32[]{:S(2)}, u32[]{:S(2)}) collective-permute-start(bf16[2,48,512]{2,1,0:T(8,128)(2,1)} %get-tuple-element.98), channel_id=1, source_target_pairs={{0,14},{1,15},{2,12},{3,13},{4,10},{5,11},{6,8},{7,9},{8,6},{9,7},... | collective-permute-start | bytes 294920 | tf_op jit(solution)/shard_map/ppermute | solution.py:289
  26.7 3.4 %collective-permute-start.27 = (bf16[2,48,512]{2,1,0:T(8,128)(2,1)}, bf16[2,48,512]{2,1,0:T(8,128)(2,1)S(1)}, u32[]{:S(2)}, u32[]{:S(2)}) collective-permute-start(bf16[2,48,512]{2,1,0:T(8,128)(2,1)} %get-tuple-element.100), channel_id=1, source_target_pairs={{0,11},{1,10},{2,9},{3,8},{4,15},{5,14},{6,13},{7,12},{8,3},{9,2},... | collective-permute-start | bytes 294920 | tf_op jit(solution)/shard_map/ppermute | solution.py:289
  31.7 3.9 %collective-permute-start.29 = (bf16[2,48,512]{2,1,0:T(8,128)(2,1)}, bf16[2,48,512]{2,1,0:T(8,128)(2,1)S(1)}, u32[]{:S(2)}, u32[]{:S(2)}) collective-permute-start(bf16[2,48,512]{2,1,0:T(8,128)(2,1)} %get-tuple-element.102), channel_id=1, source_target_pairs={{0,15},{1,14},{2,13},{3,12},{4,11},{5,10},{6,9},{7,8},{8,7},{9,6},... | collective-permute-start | bytes 294920 | tf_op jit(solution)/shard_map/ppermute | solution.py:289
  37.0 2.8 %pack_rows.1 = (bf16[32,1792]{1,0:T(8,128)(2,1)S(1)}, bf16[32,1792]{1,0:T(8,128)(2,1)S(1)}, bf16[32,1792]{1,0:T(8,128)(2,1)S(1)}, bf16[32,1792]{1,0:T(8,128)(2,1...) custom-call(s32[1]{0:T(128)S(6)} %copy.13.live_ref, ...), custom_call_target="tpu_custom_call" | custom-call | flops 469762048 | bytes 2752512 | tf_op jit(solution)/shard_map/pack_rows/pallas_call | solution.py:107
  41.4 2.9 %collective-permute-start.3 = (bf16[32,1792]{1,0:T(8,128)(2,1)S(1)}, bf16[32,1792]{1,0:T(8,128)(2,1)S(1)}, u32[]{:S(2)}, u32[]{:S(2)}) collective-permute-start(bf16[32,1792]{1,0:T(8,128)(2,1)S(1)} %get-tuple-element.75), channel_id=1, source_target_pairs={{0,12},{1,13},{2,14},{3,15},{4,8},{5,9},{6,10},{7,11},{8,4},{9,5},... | collective-permute-start | bytes 344072 | tf_op jit(solution)/shard_map/ppermute | solution.py:289
  45.2 1.8 %collective-permute-start.5 = (bf16[32,1792]{1,0:T(8,128)(2,1)S(1)}, bf16[32,1792]{1,0:T(8,128)(2,1)S(1)}, u32[]{:S(2)}, u32[]{:S(2)}) collective-permute-start(bf16[32,1792]{1,0:T(8,128)(2,1)S(1)} %get-tuple-element.77), channel_id=1, source_target_pairs={{0,9},{1,8},{2,11},{3,10},{4,13},{5,12},{6,15},{7,14},{8,1},{9,0},... | collective-permute-start | bytes 344072 | tf_op jit(solution)/shard_map/ppermute | solution.py:289
  48.7 4.1 %collective-permute-start.6 = (bf16[32,1792]{1,0:T(8,128)(2,1)S(1)}, bf16[32,1792]{1,0:T(8,128)(2,1)S(1)}, u32[]{:S(2)}, u32[]{:S(2)}) collective-permute-start(bf16[32,1792]{1,0:T(8,128)(2,1)S(1)} %get-tuple-element.78), channel_id=1, source_target_pairs={{0,6},{1,7},{2,4},{3,5},{4,2},{5,3},{6,0},{7,1},{8,14},{9,15},{10,... | collective-permute-start | bytes 344072 | tf_op jit(solution)/shard_map/ppermute | solution.py:289
  52.8 3.0 %collective-permute-start.8 = (bf16[32,1792]{1,0:T(8,128)(2,1)S(1)}, bf16[32,1792]{1,0:T(8,128)(2,1)S(1)}, u32[]{:S(2)}, u32[]{:S(2)}) collective-permute-start(bf16[32,1792]{1,0:T(8,128)(2,1)S(1)} %get-tuple-element.80), channel_id=1, source_target_pairs={{0,2},{1,3},{2,0},{3,1},{4,6},{5,7},{6,4},{7,5},{8,10},{9,11},{10,... | collective-permute-start | bytes 344072 | tf_op jit(solution)/shard_map/ppermute | solution.py:289
  55.9 3.2 %collective-permute-start.9 = (bf16[32,1792]{1,0:T(8,128)(2,1)S(1)}, bf16[32,1792]{1,0:T(8,128)(2,1)S(1)}, u32[]{:S(2)}, u32[]{:S(2)}) collective-permute-start(bf16[32,1792]{1,0:T(8,128)(2,1)S(1)} %get-tuple-element.81), channel_id=1, source_target_pairs={{0,10},{1,11},{2,8},{3,9},{4,14},{5,15},{6,12},{7,13},{8,2},{9,3},... | collective-permute-start | bytes 344072 | tf_op jit(solution)/shard_map/ppermute | solution.py:289
  60.8 4.5 %collective-permute-start.11 = (bf16[32,1792]{1,0:T(8,128)(2,1)S(1)}, bf16[32,1792]{1,0:T(8,128)(2,1)S(1)}, u32[]{:S(2)}, u32[]{:S(2)}) collective-permute-start(bf16[32,1792]{1,0:T(8,128)(2,1)S(1)} %get-tuple-element.83), channel_id=1, source_target_pairs={{0,14},{1,15},{2,12},{3,13},{4,10},{5,11},{6,8},{7,9},{8,6},{9,7},... | collective-permute-start | bytes 344072 | tf_op jit(solution)/shard_map/ppermute | solution.py:289
  65.4 2.1 %collective-permute-start.13 = (bf16[32,1792]{1,0:T(8,128)(2,1)S(1)}, bf16[32,1792]{1,0:T(8,128)(2,1)S(1)}, u32[]{:S(2)}, u32[]{:S(2)}) collective-permute-start(bf16[32,1792]{1,0:T(8,128)(2,1)S(1)} %get-tuple-element.85), channel_id=1, source_target_pairs={{0,11},{1,10},{2,9},{3,8},{4,15},{5,14},{6,13},{7,12},{8,3},{9,2},... | collective-permute-start | bytes 344072 | tf_op jit(solution)/shard_map/ppermute | solution.py:289
  67.5 6.3 %collective-permute-done.9.refs_9_ = bf16[32,1792]{1,0:T(8,128)(2,1)S(1)} collective-permute-done((bf16[32,1792]{1,0:T(8,128)(2,1)S(1)}, bf16[32,1792]{1,0:T(8,128)(2,1)S(1)}, u32[]{:S(2)}, u32[]{:S(2)}) %collective-permute-start.9) | collective-permute-done | bytes 114720 | tf_op jit(solution)/shard_map/ppermute | solution.py:289
  74.6 3.2 %collective-permute-start.30 = (bf16[2,48,512]{2,1,0:T(8,128)(2,1)S(1)}, bf16[2,48,512]{2,1,0:T(8,128)(2,1)S(1)}, u32[]{:S(2)}, u32[]{:S(2)}) collective-permute-start(bf16[2,48,512]{2,1,0:T(8,128)(2,1)S(1)} %get-tuple-element.104), channel_id=1, source_target_pairs={{0,8},{1,9},{2,10},{3,11},{4,12},{5,13},{6,14},{7,15},{8,0},{9,1},... | collective-permute-start | bytes 294920 | tf_op jit(solution)/shard_map/ppermute | solution.py:289
  83.6 3.6 %collective-permute-start.34 = (bf16[2,48,512]{2,1,0:T(8,128)(2,1)S(1)}, bf16[2,48,512]{2,1,0:T(8,128)(2,1)S(1)}, u32[]{:S(2)}, u32[]{:S(2)}) collective-permute-start(bf16[2,48,512]{2,1,0:T(8,128)(2,1)S(1)} %get-tuple-element.108), channel_id=1, source_target_pairs={{0,9},{1,8},{2,11},{3,10},{4,13},{5,12},{6,15},{7,14},{8,1},{9,0},... | collective-permute-start | bytes 294920 | tf_op jit(solution)/shard_map/ppermute | solution.py:289
  87.2 3.3 %collective-permute-done.30.refs_17_ = bf16[2,48,512]{2,1,0:T(8,128)(2,1)S(1)} collective-permute-done((bf16[2,48,512]{2,1,0:T(8,128)(2,1)S(1)}, bf16[2,48,512]{2,1,0:T(8,128)(2,1)S(1)}, u32[]{:S(2)}, u32[]{:S(2)}) %collective-permute-start.30) | collective-permute-done | bytes 98336 | tf_op jit(solution)/shard_map/ppermute | solution.py:289
  90.7 4.1 %collective-permute-start.37 = (bf16[2,48,512]{2,1,0:T(8,128)(2,1)S(1)}, bf16[2,48,512]{2,1,0:T(8,128)(2,1)S(1)}, u32[]{:S(2)}, u32[]{:S(2)}) collective-permute-start(bf16[2,48,512]{2,1,0:T(8,128)(2,1)S(1)} %get-tuple-element.111), channel_id=1, source_target_pairs={{0,2},{1,3},{2,0},{3,1},{4,6},{5,7},{6,4},{7,5},{8,10},{9,11},{10,... | collective-permute-start | bytes 294920 | tf_op jit(solution)/shard_map/ppermute | solution.py:289
  95.7 3.4 %collective-permute-done.34.refs_21_ = bf16[2,48,512]{2,1,0:T(8,128)(2,1)S(1)} collective-permute-done((bf16[2,48,512]{2,1,0:T(8,128)(2,1)S(1)}, bf16[2,48,512]{2,1,0:T(8,128)(2,1)S(1)}, u32[]{:S(2)}, u32[]{:S(2)}) %collective-permute-start.34) | collective-permute-done | bytes 98336 | tf_op jit(solution)/shard_map/ppermute | solution.py:289
  100.3 1.9 %collective-permute-start.40 = (bf16[2,48,512]{2,1,0:T(8,128)(2,1)S(1)}, bf16[2,48,512]{2,1,0:T(8,128)(2,1)S(1)}, u32[]{:S(2)}, u32[]{:S(2)}) collective-permute-start(bf16[2,48,512]{2,1,0:T(8,128)(2,1)S(1)} %get-tuple-element.114), channel_id=1, source_target_pairs={{0,14},{1,15},{2,12},{3,13},{4,10},{5,11},{6,8},{7,9},{8,6},{9,7},... | collective-permute-start | bytes 294920 | tf_op jit(solution)/shard_map/ppermute | solution.py:289
  104.5 2.0 %collective-permute-done.38.refs_25_ = bf16[2,48,512]{2,1,0:T(8,128)(2,1)S(1)} collective-permute-done((bf16[2,48,512]{2,1,0:T(8,128)(2,1)S(1)}, bf16[2,48,512]{2,1,0:T(8,128)(2,1)S(1)}, u32[]{:S(2)}, u32[]{:S(2)}) %collective-permute-start.38) | collective-permute-done | bytes 98336 | tf_op jit(solution)/shard_map/ppermute | solution.py:289
  107.6 7.8 %collective-permute-done.41.refs_28_ = bf16[2,48,512]{2,1,0:T(8,128)(2,1)S(1)} collective-permute-done((bf16[2,48,512]{2,1,0:T(8,128)(2,1)S(1)}, bf16[2,48,512]{2,1,0:T(8,128)(2,1)S(1)}, u32[]{:S(2)}, u32[]{:S(2)}) %collective-permute-start.41) | collective-permute-done | bytes 98336 | tf_op jit(solution)/shard_map/ppermute | solution.py:289
  115.4 4.8 %update.1 = (bf16[384,1024]{1,0:T(8,128)(2,1)}, bf16[384,1024]{1,0:T(8,128)(2,1)}, bf16[32,1024]{1,0:T(8,128)(2,1)S(1)}, bf16[32,1024]{1,0:T(8,128)(2,1)S(1)}, b...) custom-call(s32[1]{0:T(128)} %bitcast.me_ref, ...), custom_call_target="tpu_custom_call" | custom-call | flops 2239758336 | bytes 6029312 | tf_op jit(solution)/shard_map/update/pallas_call | solution.py:222
  120.2 4.6 %collective-permute-start.45 = (bf16[32,1024]{1,0:T(8,128)(2,1)S(1)}, bf16[32,1024]{1,0:T(8,128)(2,1)S(1)}, u32[]{:S(2)}, u32[]{:S(2)}) collective-permute-start(bf16[32,1024]{1,0:T(8,128)(2,1)S(1)} %get-tuple-element.124), channel_id=1, source_target_pairs={{0,8},{1,9},{2,10},{3,11},{4,12},{5,13},{6,14},{7,15},{8,0},{9,1},... | collective-permute-start | bytes 196616 | tf_op jit(solution)/shard_map/ppermute | solution.py:289
  124.8 2.1 %collective-permute-start.47 = (bf16[32,1024]{1,0:T(8,128)(2,1)S(1)}, bf16[32,1024]{1,0:T(8,128)(2,1)S(1)}, u32[]{:S(2)}, u32[]{:S(2)}) collective-permute-start(bf16[32,1024]{1,0:T(8,128)(2,1)S(1)} %get-tuple-element.126), channel_id=1, source_target_pairs={{0,12},{1,13},{2,14},{3,15},{4,8},{5,9},{6,10},{7,11},{8,4},{9,5},... | collective-permute-start | bytes 196616 | tf_op jit(solution)/shard_map/ppermute | solution.py:289
  132.5 2.0 %collective-permute-start.53 = (bf16[32,1024]{1,0:T(8,128)(2,1)S(1)}, bf16[32,1024]{1,0:T(8,128)(2,1)S(1)}, u32[]{:S(2)}, u32[]{:S(2)}) collective-permute-start(bf16[32,1024]{1,0:T(8,128)(2,1)S(1)} %get-tuple-element.132), channel_id=1, source_target_pairs={{0,10},{1,11},{2,8},{3,9},{4,14},{5,15},{6,12},{7,13},{8,2},{9,3},... | collective-permute-start | bytes 196616 | tf_op jit(solution)/shard_map/ppermute | solution.py:289
  138.8 2.4 %collective-permute-done.53.refs_9_ = bf16[32,1024]{1,0:T(8,128)(2,1)S(1)} collective-permute-done((bf16[32,1024]{1,0:T(8,128)(2,1)S(1)}, bf16[32,1024]{1,0:T(8,128)(2,1)S(1)}, u32[]{:S(2)}, u32[]{:S(2)}) %collective-permute-start.53) | collective-permute-done | bytes 65568 | tf_op jit(solution)/shard_map/ppermute | solution.py:289
  144.5 2.4 %collective-permute-done.56.refs_12_ = bf16[32,1024]{1,0:T(8,128)(2,1)S(1)} collective-permute-done((bf16[32,1024]{1,0:T(8,128)(2,1)S(1)}, bf16[32,1024]{1,0:T(8,128)(2,1)S(1)}, u32[]{:S(2)}, u32[]{:S(2)}) %collective-permute-start.56) | collective-permute-done | bytes 65568 | tf_op jit(solution)/shard_map/ppermute | solution.py:289
  (110 shorter events, 42.8 us)
Async XLA Ops:
  2.5 10.9 %collective-permute-start = (bf16[2,48,512]{2,1,0:T(8,128)(2,1)}, bf16[2,48,512]{2,1,0:T(8,128)(2,1)S(1)}, u32[]{:S(2)}, u32[]{:S(2)}) collective-permute-start(bf16[2,48,512]{2,1,0:T(8,128)(2,1)} %get-tuple-element.71), channel_id=1, source_target_pairs={{0,8},{1,9},{2,10},{3,11},{4,12},{5,13},{6,14},{7,15},{8,0},{9,1},... | collective-permute-start | bytes 294920 | tf_op jit(solution)/shard_map/ppermute | solution.py:289
  9.4 12.9 %collective-permute-start.19 = (bf16[2,48,512]{2,1,0:T(8,128)(2,1)}, bf16[2,48,512]{2,1,0:T(8,128)(2,1)S(1)}, u32[]{:S(2)}, u32[]{:S(2)}) collective-permute-start(bf16[2,48,512]{2,1,0:T(8,128)(2,1)} %get-tuple-element.92), channel_id=1, source_target_pairs={{0,9},{1,8},{2,11},{3,10},{4,13},{5,12},{6,15},{7,14},{8,1},{9,0},... | collective-permute-start | bytes 294920 | tf_op jit(solution)/shard_map/ppermute | solution.py:289
  13.4 11.1 %collective-permute-start.20 = (bf16[2,48,512]{2,1,0:T(8,128)(2,1)}, bf16[2,48,512]{2,1,0:T(8,128)(2,1)S(1)}, u32[]{:S(2)}, u32[]{:S(2)}) collective-permute-start(bf16[2,48,512]{2,1,0:T(8,128)(2,1)} %get-tuple-element.93), channel_id=1, source_target_pairs={{0,6},{1,7},{2,4},{3,5},{4,2},{5,3},{6,0},{7,1},{8,14},{9,15},{10,... | collective-permute-start | bytes 294920 | tf_op jit(solution)/shard_map/ppermute | solution.py:289
  16.4 10.2 %collective-permute-start.21 = (bf16[2,48,512]{2,1,0:T(8,128)(2,1)}, bf16[2,48,512]{2,1,0:T(8,128)(2,1)S(1)}, u32[]{:S(2)}, u32[]{:S(2)}) collective-permute-start(bf16[2,48,512]{2,1,0:T(8,128)(2,1)} %get-tuple-element.94), channel_id=1, source_target_pairs={{0,13},{1,12},{2,15},{3,14},{4,9},{5,8},{6,11},{7,10},{8,5},{9,4},... | collective-permute-start | bytes 294920 | tf_op jit(solution)/shard_map/ppermute | solution.py:289
  17.2 12.9 %collective-permute-start.23 = (bf16[2,48,512]{2,1,0:T(8,128)(2,1)}, bf16[2,48,512]{2,1,0:T(8,128)(2,1)S(1)}, u32[]{:S(2)}, u32[]{:S(2)}) collective-permute-start(bf16[2,48,512]{2,1,0:T(8,128)(2,1)} %get-tuple-element.96), channel_id=1, source_target_pairs={{0,10},{1,11},{2,8},{3,9},{4,14},{5,15},{6,12},{7,13},{8,2},{9,3},... | collective-permute-start | bytes 294920 | tf_op jit(solution)/shard_map/ppermute | solution.py:289
  24.5 15.3 %collective-permute-start.25 = (bf16[2,48,512]{2,1,0:T(8,128)(2,1)}, bf16[2,48,512]{2,1,0:T(8,128)(2,1)S(1)}, u32[]{:S(2)}, u32[]{:S(2)}) collective-permute-start(bf16[2,48,512]{2,1,0:T(8,128)(2,1)} %get-tuple-element.98), channel_id=1, source_target_pairs={{0,14},{1,15},{2,12},{3,13},{4,10},{5,11},{6,8},{7,9},{8,6},{9,7},... | collective-permute-start | bytes 294920 | tf_op jit(solution)/shard_map/ppermute | solution.py:289
  26.7 13.5 %collective-permute-start.26 = (bf16[2,48,512]{2,1,0:T(8,128)(2,1)}, bf16[2,48,512]{2,1,0:T(8,128)(2,1)S(1)}, u32[]{:S(2)}, u32[]{:S(2)}) collective-permute-start(bf16[2,48,512]{2,1,0:T(8,128)(2,1)} %get-tuple-element.99), channel_id=1, source_target_pairs={{0,1},{1,0},{2,3},{3,2},{4,5},{5,4},{6,7},{7,6},{8,9},{9,8},{10,11... | collective-permute-start | bytes 294920 | tf_op jit(solution)/shard_map/ppermute | solution.py:289
  26.7 14.7 %collective-permute-start.27 = (bf16[2,48,512]{2,1,0:T(8,128)(2,1)}, bf16[2,48,512]{2,1,0:T(8,128)(2,1)S(1)}, u32[]{:S(2)}, u32[]{:S(2)}) collective-permute-start(bf16[2,48,512]{2,1,0:T(8,128)(2,1)} %get-tuple-element.100), channel_id=1, source_target_pairs={{0,11},{1,10},{2,9},{3,8},{4,15},{5,14},{6,13},{7,12},{8,3},{9,2},... | collective-permute-start | bytes 294920 | tf_op jit(solution)/shard_map/ppermute | solution.py:289
  30.1 14.2 %collective-permute-start.28 = (bf16[2,48,512]{2,1,0:T(8,128)(2,1)}, bf16[2,48,512]{2,1,0:T(8,128)(2,1)S(1)}, u32[]{:S(2)}, u32[]{:S(2)}) collective-permute-start(bf16[2,48,512]{2,1,0:T(8,128)(2,1)} %get-tuple-element.101), channel_id=1, source_target_pairs={{0,4},{1,5},{2,6},{3,7},{4,0},{5,1},{6,2},{7,3},{8,12},{9,13},{10,... | collective-permute-start | bytes 294920 | tf_op jit(solution)/shard_map/ppermute | solution.py:289
  31.7 13.5 %collective-permute-start.29 = (bf16[2,48,512]{2,1,0:T(8,128)(2,1)}, bf16[2,48,512]{2,1,0:T(8,128)(2,1)S(1)}, u32[]{:S(2)}, u32[]{:S(2)}) collective-permute-start(bf16[2,48,512]{2,1,0:T(8,128)(2,1)} %get-tuple-element.102), channel_id=1, source_target_pairs={{0,15},{1,14},{2,13},{3,12},{4,11},{5,10},{6,9},{7,8},{8,7},{9,6},... | collective-permute-start | bytes 294920 | tf_op jit(solution)/shard_map/ppermute | solution.py:289
  40.2 12.7 %collective-permute-start.2 = (bf16[32,1792]{1,0:T(8,128)(2,1)S(1)}, bf16[32,1792]{1,0:T(8,128)(2,1)S(1)}, u32[]{:S(2)}, u32[]{:S(2)}) collective-permute-start(bf16[32,1792]{1,0:T(8,128)(2,1)S(1)} %get-tuple-element.74), channel_id=1, source_target_pairs={{0,7},{1,6},{2,5},{3,4},{4,3},{5,2},{6,1},{7,0},{8,15},{9,14},{10,... | collective-permute-start | bytes 344072 | tf_op jit(solution)/shard_map/ppermute | solution.py:289
  41.4 11.4 %collective-permute-start.3 = (bf16[32,1792]{1,0:T(8,128)(2,1)S(1)}, bf16[32,1792]{1,0:T(8,128)(2,1)S(1)}, u32[]{:S(2)}, u32[]{:S(2)}) collective-permute-start(bf16[32,1792]{1,0:T(8,128)(2,1)S(1)} %get-tuple-element.75), channel_id=1, source_target_pairs={{0,12},{1,13},{2,14},{3,15},{4,8},{5,9},{6,10},{7,11},{8,4},{9,5},... | collective-permute-start | bytes 344072 | tf_op jit(solution)/shard_map/ppermute | solution.py:289
  44.3 11.6 %collective-permute-start.4 = (bf16[32,1792]{1,0:T(8,128)(2,1)S(1)}, bf16[32,1792]{1,0:T(8,128)(2,1)S(1)}, u32[]{:S(2)}, u32[]{:S(2)}) collective-permute-start(bf16[32,1792]{1,0:T(8,128)(2,1)S(1)} %get-tuple-element.76), channel_id=1, source_target_pairs={{0,3},{1,2},{2,1},{3,0},{4,7},{5,6},{6,5},{7,4},{8,11},{9,10},{10,... | collective-permute-start | bytes 344072 | tf_op jit(solution)/shard_map/ppermute | solution.py:289
  45.2 15.7 %collective-permute-start.5 = (bf16[32,1792]{1,0:T(8,128)(2,1)S(1)}, bf16[32,1792]{1,0:T(8,128)(2,1)S(1)}, u32[]{:S(2)}, u32[]{:S(2)}) collective-permute-start(bf16[32,1792]{1,0:T(8,128)(2,1)S(1)} %get-tuple-element.77), channel_id=1, source_target_pairs={{0,9},{1,8},{2,11},{3,10},{4,13},{5,12},{6,15},{7,14},{8,1},{9,0},... | collective-permute-start | bytes 344072 | tf_op jit(solution)/shard_map/ppermute | solution.py:289
  48.7 12.2 %collective-permute-start.6 = (bf16[32,1792]{1,0:T(8,128)(2,1)S(1)}, bf16[32,1792]{1,0:T(8,128)(2,1)S(1)}, u32[]{:S(2)}, u32[]{:S(2)}) collective-permute-start(bf16[32,1792]{1,0:T(8,128)(2,1)S(1)} %get-tuple-element.78), channel_id=1, source_target_pairs={{0,6},{1,7},{2,4},{3,5},{4,2},{5,3},{6,0},{7,1},{8,14},{9,15},{10,... | collective-permute-start | bytes 344072 | tf_op jit(solution)/shard_map/ppermute | solution.py:289
  52.8 12.5 %collective-permute-start.7 = (bf16[32,1792]{1,0:T(8,128)(2,1)S(1)}, bf16[32,1792]{1,0:T(8,128)(2,1)S(1)}, u32[]{:S(2)}, u32[]{:S(2)}) collective-permute-start(bf16[32,1792]{1,0:T(8,128)(2,1)S(1)} %get-tuple-element.79), channel_id=1, source_target_pairs={{0,13},{1,12},{2,15},{3,14},{4,9},{5,8},{6,11},{7,10},{8,5},{9,4},... | collective-permute-start | bytes 344072 | tf_op jit(solution)/shard_map/ppermute | solution.py:289
  52.8 12.5 %collective-permute-start.8 = (bf16[32,1792]{1,0:T(8,128)(2,1)S(1)}, bf16[32,1792]{1,0:T(8,128)(2,1)S(1)}, u32[]{:S(2)}, u32[]{:S(2)}) collective-permute-start(bf16[32,1792]{1,0:T(8,128)(2,1)S(1)} %get-tuple-element.80), channel_id=1, source_target_pairs={{0,2},{1,3},{2,0},{3,1},{4,6},{5,7},{6,4},{7,5},{8,10},{9,11},{10,... | collective-permute-start | bytes 344072 | tf_op jit(solution)/shard_map/ppermute | solution.py:289
  55.9 17.9 %collective-permute-start.9 = (bf16[32,1792]{1,0:T(8,128)(2,1)S(1)}, bf16[32,1792]{1,0:T(8,128)(2,1)S(1)}, u32[]{:S(2)}, u32[]{:S(2)}) collective-permute-start(bf16[32,1792]{1,0:T(8,128)(2,1)S(1)} %get-tuple-element.81), channel_id=1, source_target_pairs={{0,10},{1,11},{2,8},{3,9},{4,14},{5,15},{6,12},{7,13},{8,2},{9,3},... | collective-permute-start | bytes 344072 | tf_op jit(solution)/shard_map/ppermute | solution.py:289
  60.8 13.0 %collective-permute-start.10 = (bf16[32,1792]{1,0:T(8,128)(2,1)S(1)}, bf16[32,1792]{1,0:T(8,128)(2,1)S(1)}, u32[]{:S(2)}, u32[]{:S(2)}) collective-permute-start(bf16[32,1792]{1,0:T(8,128)(2,1)S(1)} %get-tuple-element.82), channel_id=1, source_target_pairs={{0,5},{1,4},{2,7},{3,6},{4,1},{5,0},{6,3},{7,2},{8,13},{9,12},{10,... | collective-permute-start | bytes 344072 | tf_op jit(solution)/shard_map/ppermute | solution.py:289
  60.8 13.8 %collective-permute-start.11 = (bf16[32,1792]{1,0:T(8,128)(2,1)S(1)}, bf16[32,1792]{1,0:T(8,128)(2,1)S(1)}, u32[]{:S(2)}, u32[]{:S(2)}) collective-permute-start(bf16[32,1792]{1,0:T(8,128)(2,1)S(1)} %get-tuple-element.83), channel_id=1, source_target_pairs={{0,14},{1,15},{2,12},{3,13},{4,10},{5,11},{6,8},{7,9},{8,6},{9,7},... | collective-permute-start | bytes 344072 | tf_op jit(solution)/shard_map/ppermute | solution.py:289
  65.4 12.4 %collective-permute-start.12 = (bf16[32,1792]{1,0:T(8,128)(2,1)S(1)}, bf16[32,1792]{1,0:T(8,128)(2,1)S(1)}, u32[]{:S(2)}, u32[]{:S(2)}) collective-permute-start(bf16[32,1792]{1,0:T(8,128)(2,1)S(1)} %get-tuple-element.84), channel_id=1, source_target_pairs={{0,1},{1,0},{2,3},{3,2},{4,5},{5,4},{6,7},{7,6},{8,9},{9,8},{10,11... | collective-permute-start | bytes 344072 | tf_op jit(solution)/shard_map/ppermute | solution.py:289
  65.4 14.2 %collective-permute-start.13 = (bf16[32,1792]{1,0:T(8,128)(2,1)S(1)}, bf16[32,1792]{1,0:T(8,128)(2,1)S(1)}, u32[]{:S(2)}, u32[]{:S(2)}) collective-permute-start(bf16[32,1792]{1,0:T(8,128)(2,1)S(1)} %get-tuple-element.85), channel_id=1, source_target_pairs={{0,11},{1,10},{2,9},{3,8},{4,15},{5,14},{6,13},{7,12},{8,3},{9,2},... | collective-permute-start | bytes 344072 | tf_op jit(solution)/shard_map/ppermute | solution.py:289
  74.6 15.9 %collective-permute-start.30 = (bf16[2,48,512]{2,1,0:T(8,128)(2,1)S(1)}, bf16[2,48,512]{2,1,0:T(8,128)(2,1)S(1)}, u32[]{:S(2)}, u32[]{:S(2)}) collective-permute-start(bf16[2,48,512]{2,1,0:T(8,128)(2,1)S(1)} %get-tuple-element.104), channel_id=1, source_target_pairs={{0,8},{1,9},{2,10},{3,11},{4,12},{5,13},{6,14},{7,15},{8,0},{9,1},... | collective-permute-start | bytes 294920 | tf_op jit(solution)/shard_map/ppermute | solution.py:289
  77.8 12.7 %collective-permute-start.31 = (bf16[2,48,512]{2,1,0:T(8,128)(2,1)S(1)}, bf16[2,48,512]{2,1,0:T(8,128)(2,1)S(1)}, u32[]{:S(2)}, u32[]{:S(2)}) collective-permute-start(bf16[2,48,512]{2,1,0:T(8,128)(2,1)S(1)} %get-tuple-element.105), channel_id=1, source_target_pairs={{0,7},{1,6},{2,5},{3,4},{4,3},{5,2},{6,1},{7,0},{8,15},{9,14},{10,... | collective-permute-start | bytes 294920 | tf_op jit(solution)/shard_map/ppermute | solution.py:289
  79.5 11.2 %collective-permute-start.32 = (bf16[2,48,512]{2,1,0:T(8,128)(2,1)S(1)}, bf16[2,48,512]{2,1,0:T(8,128)(2,1)S(1)}, u32[]{:S(2)}, u32[]{:S(2)}) collective-permute-start(bf16[2,48,512]{2,1,0:T(8,128)(2,1)S(1)} %get-tuple-element.106), channel_id=1, source_target_pairs={{0,12},{1,13},{2,14},{3,15},{4,8},{5,9},{6,10},{7,11},{8,4},{9,5},... | collective-permute-start | bytes 294920 | tf_op jit(solution)/shard_map/ppermute | solution.py:289
  82.0 12.8 %collective-permute-start.33 = (bf16[2,48,512]{2,1,0:T(8,128)(2,1)S(1)}, bf16[2,48,512]{2,1,0:T(8,128)(2,1)S(1)}, u32[]{:S(2)}, u32[]{:S(2)}) collective-permute-start(bf16[2,48,512]{2,1,0:T(8,128)(2,1)S(1)} %get-tuple-element.107), channel_id=1, source_target_pairs={{0,3},{1,2},{2,1},{3,0},{4,7},{5,6},{6,5},{7,4},{8,11},{9,10},{10,... | collective-permute-start | bytes 294920 | tf_op jit(solution)/shard_map/ppermute | solution.py:289
  83.6 15.5 %collective-permute-start.34 = (bf16[2,48,512]{2,1,0:T(8,128)(2,1)S(1)}, bf16[2,48,512]{2,1,0:T(8,128)(2,1)S(1)}, u32[]{:S(2)}, u32[]{:S(2)}) collective-permute-start(bf16[2,48,512]{2,1,0:T(8,128)(2,1)S(1)} %get-tuple-element.108), channel_id=1, source_target_pairs={{0,9},{1,8},{2,11},{3,10},{4,13},{5,12},{6,15},{7,14},{8,1},{9,0},... | collective-permute-start | bytes 294920 | tf_op jit(solution)/shard_map/ppermute | solution.py:289
  90.5 11.7 %collective-permute-start.36 = (bf16[2,48,512]{2,1,0:T(8,128)(2,1)S(1)}, bf16[2,48,512]{2,1,0:T(8,128)(2,1)S(1)}, u32[]{:S(2)}, u32[]{:S(2)}) collective-permute-start(bf16[2,48,512]{2,1,0:T(8,128)(2,1)S(1)} %get-tuple-element.110), channel_id=1, source_target_pairs={{0,13},{1,12},{2,15},{3,14},{4,9},{5,8},{6,11},{7,10},{8,5},{9,4},... | collective-permute-start | bytes 294920 | tf_op jit(solution)/shard_map/ppermute | solution.py:289
  90.7 13.1 %collective-permute-start.37 = (bf16[2,48,512]{2,1,0:T(8,128)(2,1)S(1)}, bf16[2,48,512]{2,1,0:T(8,128)(2,1)S(1)}, u32[]{:S(2)}, u32[]{:S(2)}) collective-permute-start(bf16[2,48,512]{2,1,0:T(8,128)(2,1)S(1)} %get-tuple-element.111), channel_id=1, source_target_pairs={{0,2},{1,3},{2,0},{3,1},{4,6},{5,7},{6,4},{7,5},{8,10},{9,11},{10,... | collective-permute-start | bytes 294920 | tf_op jit(solution)/shard_map/ppermute | solution.py:289
  94.8 11.7 %collective-permute-start.38 = (bf16[2,48,512]{2,1,0:T(8,128)(2,1)S(1)}, bf16[2,48,512]{2,1,0:T(8,128)(2,1)S(1)}, u32[]{:S(2)}, u32[]{:S(2)}) collective-permute-start(bf16[2,48,512]{2,1,0:T(8,128)(2,1)S(1)} %get-tuple-element.112), channel_id=1, source_target_pairs={{0,10},{1,11},{2,8},{3,9},{4,14},{5,15},{6,12},{7,13},{8,2},{9,3},... | collective-permute-start | bytes 294920 | tf_op jit(solution)/shard_map/ppermute | solution.py:289
  102.2 13.2 %collective-permute-start.41 = (bf16[2,48,512]{2,1,0:T(8,128)(2,1)S(1)}, bf16[2,48,512]{2,1,0:T(8,128)(2,1)S(1)}, u32[]{:S(2)}, u32[]{:S(2)}) collective-permute-start(bf16[2,48,512]{2,1,0:T(8,128)(2,1)S(1)} %get-tuple-element.115), channel_id=1, source_target_pairs={{0,11},{1,10},{2,9},{3,8},{4,15},{5,14},{6,13},{7,12},{8,3},{9,2},... | collective-permute-start | bytes 294920 | tf_op jit(solution)/shard_map/ppermute | solution.py:289
  103.8 11.6 %collective-permute-start.42 = (bf16[2,48,512]{2,1,0:T(8,128)(2,1)S(1)}, bf16[2,48,512]{2,1,0:T(8,128)(2,1)S(1)}, u32[]{:S(2)}, u32[]{:S(2)}) collective-permute-start(bf16[2,48,512]{2,1,0:T(8,128)(2,1)S(1)} %get-tuple-element.116), channel_id=1, source_target_pairs={{0,1},{1,0},{2,3},{3,2},{4,5},{5,4},{6,7},{7,6},{8,9},{9,8},{10,11... | collective-permute-start | bytes 294920 | tf_op jit(solution)/shard_map/ppermute | solution.py:289
  (36 other events, 397.4 us)

commit v12 on v10

--- a/solution.py
+++ b/solution.py
@@ -43,19 +43,22 @@
     ]
 
 
-def slot_rows(route, live, groups, capacity, me_ref, perm_ref):
+def placed_rows(route, live, groups, me_ref, perm_ref):
     rows = route.shape[1]
     experts = lax.broadcasted_iota(jnp.int32, (groups, rows), 0)
     onehot = jnp.where((experts == route) & live, 1.0, 0.0).astype(BF16)
-    before = lax.broadcasted_iota(jnp.int32, (rows, rows), 0)
-    after = lax.broadcasted_iota(jnp.int32, (rows, rows), 1)
-    upto = jnp.where(before <= after, 1.0, 0.0).astype(BF16)
-    ranks = jnp.dot(onehot, upto, preferred_element_type=F32)
+    ranks = jnp.dot(onehot, upto(rows), preferred_element_type=F32)
     rank = jnp.sum(ranks * onehot.astype(F32), axis=0, keepdims=True).astype(jnp.int32) - 1
     partner = jnp.zeros_like(route)
     for e in range(groups):
         partner = jnp.where(route == e, perm_ref[e] ^ me_ref[0], partner)
-    return jnp.where(live, partner * capacity + rank, -1)
+    return partner, rank
+
+
+def upto(rows):
+    before = lax.broadcasted_iota(jnp.int32, (rows, rows), 0)
+    after = lax.broadcasted_iota(jnp.int32, (rows, rows), 1)
+    return jnp.where(before <= after, 1.0, 0.0).astype(BF16)
 
 
 def selector_of(slot, slots):
@@ -65,62 +68,122 @@
 
 
 def pack_kernel(groups, live_ref, me_ref, perm_ref, *refs):
-    sources, pieces, (slot_ref, gates_ref) = refs[:6], refs[7 : 7 + groups], refs[7 + groups : 9 + groups]
-    held, sem = refs[9 + groups : 15 + groups], refs[-1]
+    sources, (near_ref, *far_refs, info_ref, slot_ref, gates_ref) = refs[:6], refs[6:12]
+    held, sem = refs[12:18], refs[-1]
     route_ref, fwd_route_ref, hidden_ref, out_ref, fwd_ref, gate_ref = held
     copies = [pltpu.make_async_copy(ref, room, sem.at[n]) for n, (ref, room) in enumerate(zip(sources, held))]
     for copy in copies:
         copy.start()
     rows, ff = hidden_ref.shape
     d = out_ref.shape[1]
-    capacity = pieces[0].shape[0]
-    slots = groups * capacity
+    half = groups // 2
+    capacity = near_ref.shape[0] // half
     place = lax.broadcasted_iota(jnp.int32, (1, rows), 1)
 
-    def fill(first, selector, source_ref):
-        chosen = jnp.dot(selector, source_ref[...], preferred_element_type=F32).astype(BF16)
-        for s, piece in zip(mixed_order(groups), pieces):
-            piece[:, first : first + source_ref.shape[1]] = chosen[s * capacity : (s + 1) * capacity]
+    def fill(first, near, far, source_ref):
+        columns = slice(first, first + source_ref.shape[1])
+        near_ref[:, columns] = jnp.dot(near, source_ref[...], preferred_element_type=F32).astype(BF16)
+        chosen = jnp.dot(far, source_ref[...], preferred_element_type=F32).astype(BF16)
+        start = 0
+        for far_ref in far_refs:
+            far_ref[:, columns] = chosen[start : start + far_ref.shape[0]]
+            start += far_ref.shape[0]
+
+    def selectors(n, route, live):
+        partner, rank = placed_rows(route, live, groups, me_ref, perm_ref)
+        slot = (partner % half) * capacity + rank
+        is_far = live & (partner >= half)
+        near = selector_of(jnp.where(live & (partner < half), slot, -1), half * capacity)
+        order = jnp.dot(
+            jnp.broadcast_to(jnp.where(is_far, 1.0, 0.0), (8, rows)).astype(BF16), upto(rows),
+            preferred_element_type=F32,
+        )[:1].astype(jnp.int32) - 1
+        far = selector_of(jnp.where(is_far, order, -1), rows)
+        after = jnp.broadcast_to(jnp.where(is_far, slot + 1, 0), (8, rows)).astype(F32).astype(BF16)
+        info = lax.dot_general(after, far, (((1,), (1,)), ((), ())), preferred_element_type=F32)
+        info_ref[n : n + 1] = info[:1].astype(jnp.int32) - 1
+        return near, far, jnp.where(live, partner * capacity + rank, -1)
 
     copies[0].wait()
-    slot = slot_rows(route_ref[...], place < live_ref[0], groups, capacity, me_ref, perm_ref)
-    selector = selector_of(slot, slots)
+    near, far, _ = selectors(0, route_ref[...], place < live_ref[0])
     copies[1].wait()
-    fwd_slot = slot_rows(fwd_route_ref[...], place >= 0, groups, capacity, me_ref, perm_ref)
-    slot_ref[...] = fwd_slot
+    fwd_near, fwd_far, slot_ref[...] = selectors(1, fwd_route_ref[...], place >= 0)
     copies[2].wait()
-    fill(0, selector, hidden_ref)
+    fill(0, near, far, hidden_ref)
     copies[3].wait()
-    fill(ff, selector, out_ref)
+    fill(ff, near, far, out_ref)
     copies[4].wait()
-    fill(ff + d, selector_of(fwd_slot, slots), fwd_ref)
+    fill(ff + d, fwd_near, fwd_far, fwd_ref)
     copies[5].wait()
     down = lax.broadcasted_iota(jnp.int32, (rows, rows), 0)
     across = lax.broadcasted_iota(jnp.int32, (rows, rows), 1)
     gates_ref[...] = jnp.sum(jnp.where(down == across, gate_ref[...], 0.0), axis=1, keepdims=True)
 
 
-def pack_rows(live_rows, me, perm, route, fwd_route, hidden, grad_out, fwd_hidden, gate, earlier, groups, capacity):
+def pack_rows(live_rows, me, perm, route, fwd_route, hidden, grad_out, fwd_hidden, gate, groups, capacity):
     rows, ff = hidden.shape
     width = 2 * ff + grad_out.shape[1]
-    sources = (route.reshape(1, rows), fwd_route.reshape(1, rows), hidden, grad_out, fwd_hidden, gate.reshape(1, rows))
-    *pieces, slot, gates = pl.pallas_call(
+    sources = (
+        route.reshape(1, rows), fwd_route.reshape(1, rows), hidden, grad_out, fwd_hidden, gate.reshape(1, rows),
+    )
+    half = groups // 2
+    rest = rows // 4
+    return pl.pallas_call(
         functools.partial(pack_kernel, groups),
-        out_shape=(jax.ShapeDtypeStruct((capacity, width), BF16),) * groups
-        + (jax.ShapeDtypeStruct((1, rows), jnp.int32), jax.ShapeDtypeStruct((rows, 1), F32)),
-        in_specs=[SMEM] * 3 + [HBM] * 6 + [VMEM],
-        out_specs=(VMEM,) * (groups + 2),
+        out_shape=(
+            jax.ShapeDtypeStruct((half * capacity, width), BF16),
+            jax.ShapeDtypeStruct((rows - rest, width), BF16),
+            jax.ShapeDtypeStruct((rest, width), BF16),
+            jax.ShapeDtypeStruct((2, rows), jnp.int32),
+            jax.ShapeDtypeStruct((1, rows), jnp.int32),
+            jax.ShapeDtypeStruct((rows, 1), F32),
+        ),
+        in_specs=[SMEM] * 3 + [HBM] * 6,
+        out_specs=(VMEM,) * 6,
         scratch_shapes=[pltpu.VMEM(a.shape, a.dtype) for a in sources] + [pltpu.SemaphoreType.DMA((len(sources),))],
         compiler_params=pltpu.CompilerParams(vmem_limit_bytes=32 * MIB),
         cost_estimate=pl.CostEstimate(
             flops=2 * groups * capacity * rows * width, bytes_accessed=6 * rows * width, transcendentals=0
         ),
         name="pack_rows",
-    )(live_rows, me, perm, *sources, earlier)
-    return pieces, slot, gates
-
-
-def split_kernel(me_ref, moment_ref, weight_ref, *refs):
+    )(live_rows, me, perm, *sources)
+
+
+def repack_kernel(boundary, near_ref, first_ref, second_ref, info_ref, *refs):
+    pieces, far_ref = refs[:-1], refs[-1]
+    half = len(pieces)
+    slots = near_ref.shape[0]
+    capacity = slots // half
+    far_ref[: first_ref.shape[0]] = first_ref[...]
+    far_ref[first_ref.shape[0] :] = second_ref[...]
+    for n, columns in enumerate((slice(0, boundary), slice(boundary, None))):
+        selector = selector_of(info_ref[n : n + 1], slots)
+        chosen = jnp.dot(selector, far_ref[:, columns], preferred_element_type=F32).astype(BF16)
+        for s, piece in zip(mixed_order(half), pieces):
+            span = slice(s * capacity, (s + 1) * capacity)
+            piece[:capacity, columns] = near_ref[span, columns]
+            piece[capacity:, columns] = chosen[span]
+
+
+def repack(near, first, second, info, half, boundary):
+    slots, width = near.shape
+    rows = first.shape[0] + second.shape[0]
+    piece = jax.ShapeDtypeStruct((2 * slots // half, width), BF16)
+    return pl.pallas_call(
+        functools.partial(repack_kernel, boundary),
+        out_shape=(piece,) * half,
+        in_specs=[VMEM] * 4,
+        out_specs=(VMEM,) * half,
+        scratch_shapes=[pltpu.VMEM((rows, width), BF16)],
+        compiler_params=pltpu.CompilerParams(vmem_limit_bytes=32 * MIB),
+        cost_estimate=pl.CostEstimate(
+            flops=2 * slots * rows * width, bytes_accessed=8 * slots * width, transcendentals=0
+        ),
+        name="repack",
+    )(near, first, second, info)
+
+
+def split_kernel(me_ref, moment_ref, weight_ref, earlier_ref, *refs):
     pieces, held, sem = refs[:-3], refs[-3:-1], refs[-1]
     fetched((moment_ref, weight_ref), held, sem)
     for s, piece in zip(mixed_order(len(pieces)), pieces):
@@ -129,24 +192,24 @@
             piece[lead] = chunk_at(source, 0, me_ref[0] ^ s, rows, columns)[...]
 
 
-def split(me, moment, weight, groups):
+def split(me, moment, weight, earlier, groups):
     _, ff, d = weight.shape
     piece = jax.ShapeDtypeStruct((2, ff // (groups // 2), d // 2), BF16)
     return pl.pallas_call(
         split_kernel,
         out_shape=(piece,) * groups,
-        in_specs=[SMEM, HBM, HBM],
+        in_specs=[SMEM, HBM, HBM, VMEM],
         out_specs=(VMEM,) * groups,
         scratch_shapes=rooms((moment, weight)),
         compiler_params=pltpu.CompilerParams(vmem_limit_bytes=60 * MIB),
         cost_estimate=pl.CostEstimate(flops=0, bytes_accessed=8 * ff * d, transcendentals=0),
         name="split",
-    )(me, moment, weight)
+    )(me, moment, weight, earlier)
 
 
 def reorder_kernel(me_ref, perm_ref, *refs):
-    groups = len(refs) // 2 - 1
-    sources, targets, held = refs[:groups], refs[groups + 1 : 2 * groups + 1], refs[-1]
+    groups = len(refs) // 2
+    sources, targets, held = refs[:groups], refs[groups:-1], refs[-1]
     me, order = me_ref[0], mixed_order(groups)
     for s, source in zip(order, sources):
         held[me ^ perm_ref[me ^ s]] = source[...]
@@ -154,29 +217,29 @@
         target[...] = held[s]
 
 
-def reorder(me, perm, pieces, earlier):
+def reorder(me, perm, pieces):
     groups = len(pieces)
     piece = jax.ShapeDtypeStruct(pieces[0].shape, BF16)
     return pl.pallas_call(
         reorder_kernel,
         out_shape=(piece,) * groups,
-        in_specs=[SMEM, SMEM] + [VMEM] * (groups + 1),
+        in_specs=[SMEM, SMEM] + [VMEM] * groups,
         out_specs=(VMEM,) * groups,
         scratch_shapes=[pltpu.VMEM((groups,) + pieces[0].shape, BF16)],
         compiler_params=pltpu.CompilerParams(vmem_limit_bytes=32 * MIB),
         cost_estimate=pl.CostEstimate(flops=0, bytes_accessed=4 * groups * pieces[0].size, transcendentals=0),
         name="reorder",
-    )(me, perm, *pieces, earlier)
+    )(me, perm, *pieces)
 
 
 def update_kernel(groups, me_ref, *refs):
-    packed, pieces, produced = refs[:groups], refs[groups : 2 * groups], refs[2 * groups + 2 : 3 * groups + 2]
-    weight_new_ref, moment_new_ref = refs[2 * groups : 2 * groups + 2]
-    held, rows_ref = refs[-2:]
+    half = groups // 2
+    packed, pieces, refs = refs[:half], refs[half : half + groups], refs[half + groups :]
+    (weight_new_ref, moment_new_ref), produced, (held, rows_ref) = refs[:2], refs[2:-2], refs[-2:]
     _, ff, d = held.shape
-    capacity = packed[0].shape[0]
+    capacity = produced[0].shape[0]
     for n, piece in enumerate(packed):
-        rows_ref[n * capacity : (n + 1) * capacity] = piece[...]
+        rows_ref[2 * n * capacity : 2 * (n + 1) * capacity] = piece[...]
     for s, piece in zip(mixed_order(groups), pieces):
         rows, columns = piece.shape[1:]
         for lead in range(2):
@@ -201,19 +264,21 @@
     weight_new = (held[1].astype(F32) - step_scale * current.astype(F32)).astype(BF16)
     weight_new_ref[...] = weight_new
     product = jnp.dot(rows_ref[:, ff + d :], weight_new, preferred_element_type=F32).astype(BF16)
-    for n, piece in enumerate(produced):
+    came = mixed_order(half)
+    for s, piece in zip(mixed_order(groups), produced):
+        n = 2 * came.index(s % half) + s // half
         piece[...] = product[n * capacity : (n + 1) * capacity]
 
 
 def update(me, packed, pieces, ff, d):
-    groups = len(pieces)
-    capacity, width = packed[0].shape
-    slots = groups * capacity
+    groups, half = len(pieces), len(packed)
+    slots, width = half * packed[0].shape[0], packed[0].shape[1]
+    capacity = slots // groups
     shape = jax.ShapeDtypeStruct((ff, d), BF16)
     weight_new, moment_new, *produced = pl.pallas_call(
         functools.partial(update_kernel, groups),
         out_shape=(shape, shape) + (jax.ShapeDtypeStruct((capacity, d), BF16),) * groups,
-        in_specs=[SMEM] + [VMEM] * (2 * groups),
+        in_specs=[SMEM] + [VMEM] * (half + groups),
         out_specs=(VMEM,) * (groups + 2),
         scratch_shapes=[pltpu.VMEM((2, ff, d), BF16), pltpu.VMEM((slots, width), BF16)],
         compiler_params=pltpu.CompilerParams(vmem_limit_bytes=40 * MIB),
@@ -269,11 +334,11 @@
     return [0] + [s for pair in zip(far, near + [None]) for s in pair if s is not None]
 
 
-def swap(pieces):
-    groups = len(pieces)
-    order = mixed_order(groups)
-    return [pieces[0]] + [
-        lax.ppermute(piece, "expert", [(i, i ^ s) for i in range(groups)]) for s, piece in zip(order[1:], pieces[1:])
+def swap(pieces, order):
+    groups = lax.axis_size("expert")
+    return [
+        lax.ppermute(piece, "expert", [(i, i ^ s) for i in range(groups)]) if s else piece
+        for s, piece in zip(order, pieces)
     ]
 
 
@@ -284,15 +349,16 @@
     me = lax.axis_index("expert").astype(jnp.int32).reshape(1)
     capacity = max(4, 2 * grad_hidden.shape[0] // groups)
     ff, d = w_down.shape[1:]
-    spread = swap(split(me, w_moment, w_down, groups))
-    packed, fwd_slot, gates = pack_rows(
-        live_rows, me, perm, grad_route, fwd_route, grad_hidden, grad_out, fwd_hidden, fwd_gate,
-        spread[2 * groups // 3], groups, capacity,
-    )
-    received = swap(packed)
-    placed = swap(reorder(me, perm, spread, received[groups // 3]))
+    half, order = groups // 2, mixed_order(groups)
+    near, first, second, info, fwd_slot, gates = pack_rows(
+        live_rows, me, perm, grad_route, fwd_route, grad_hidden, grad_out, fwd_hidden, fwd_gate, groups, capacity
+    )
+    spread = swap(split(me, w_moment, w_down, fwd_slot, groups), order)
+    first, second, info = swap((first, second, info), (half,) * 3)
+    received = swap(repack(near, first, second, info, half, ff + d), mixed_order(half))
+    placed = swap(reorder(me, perm, spread), order)
     weight_new, moment_new, produced = update(me, received, placed, ff, d)
-    return weight_new[None], moment_new[None], finish(fwd_slot, gates, swap(produced))
+    return weight_new[None], moment_new[None], finish(fwd_slot, gates, swap(produced, order))
 
 
 def lookup(route_ids, mapping):

time: 149 us -> 179 us (1.20)
  waiting for transfers between devices: 24.5 us -> 75.4 us
  starting transfers between devices: 110 us -> 81.7 us
  local copies, waits for them, and re-layouts: 0.66 us -> 5.73 us
    ppermute x60 -> x55, waiting for transfers between devices: 24.5 us -> 75.4 us  [swap(): lax.ppermute(piece, 'expert', [(i, i ^ s) for i in range(groups)])]
    ppermute x60 -> x55, starting transfers between devices: 110 us -> 81.7 us  [swap(): lax.ppermute(piece, 'expert', [(i, i ^ s) for i in range(groups)])]
    unnamed x16 -> x20, local copies, waits for them, and re-layouts: 0.66 us -> 5.73 us
  transfers between devices with their start and end apart: 60 -> 55, of which waited for: 12 -> 25; matrix products, arithmetic and copies ran while one was open for 0% -> 0% of each run, Pallas kernels for 2% -> 3%
where the time goes in v12:
time: 179 us; the launch traced here: 178 us
  starting transfers between devices  81.7 us (46%)
  waiting for transfers between devices  75.4 us (42%)
  Pallas kernels  13.9 us (8%)
  local copies, waits for them, and re-layouts  5.73 us (3%)
    ppermute x55, starting transfers between devices, swap(): lax.ppermute(piece, 'expert', [(i, i ^ s) for i in range(groups)])  81.7 us
    ppermute x55, waiting for transfers between devices, swap(): lax.ppermute(piece, 'expert', [(i, i ^ s) for i in range(groups)])  75.4 us
    unnamed x20, local copies, waits for them, and re-layouts  5.73 us
    pallas_call x1, Pallas kernels, update(): pl.pallas_call(functools.partial(update_kernel, groups), out_shape=(shape...  5.11 us
  transfers between devices with their start and end apart: 55, of which 25 were waited for; matrix products, arithmetic and copies ran while one was open for 0% of the time, Pallas kernels for 3%

profile of v12, /device:TPU:0, one launch (start us, length us, event | category | flops | bytes accessed | tf_op | source)
XLA Modules:
  0.0 178.3 jit_solution(8287753308480773442)
XLA Ops:
  4.9 3.1 %pack_rows.1 = (bf16[256,1792]{1,0:T(8,128)(2,1)S(1)}, bf16[192,1792]{1,0:T(8,128)(2,1)S(1)}, bf16[64,1792]{1,0:T(8,128)(2,1)S(1)}, s32[2,256]{1,0:T(2,128)S(1)}...) custom-call(s32[1]{0:T(128)S(6)} %copy.13.live_ref, s32[1]{0:T(128)} %bitcast.me_ref, s32[16]{0:T(128)S(1)} %copy-done.3, ...), custom_call_target="tpu_custom_call" | custom-call | flops 469762048 | bytes 2752512 | tf_op jit(solution)/shard_map/pack_rows/pallas_call | solution.py:131
  8.6 4.0 %collective-permute-start = (bf16[192,1792]{1,0:T(8,128)(2,1)S(1)}, bf16[192,1792]{1,0:T(8,128)(2,1)S(1)}, u32[]{:S(2)}, u32[]{:S(2)}) collective-permute-start(bf16[192,1792]{1,0:T(8,128)(2,1)S(1)} %get-tuple-element.68), channel_id=1, source_target_pairs={{0,8},{1,9},{2,10},{3,11},{4,12},{5,13},{6,14},{7,15},{8,0},{9,1},... | collective-permute-start | bytes 2064392 | tf_op jit(solution)/shard_map/ppermute | solution.py:340
  12.6 3.3 %split.1 = (bf16[2,48,512]{2,1,0:T(8,128)(2,1)}, bf16[2,48,512]{2,1,0:T(8,128)(2,1)}, bf16[2,48,512]{2,1,0:T(8,128)(2,1)}, bf16[2,48,512]{2,1,0:T(8,128)(2,1)}, ...) custom-call(s32[1]{0:T(128)} %bitcast.me_ref, ...), custom_call_target="tpu_custom_call" | custom-call | bytes 3145728 | tf_op jit(solution)/shard_map/split/pallas_call | solution.py:198
  17.7 2.5 %collective-permute-start.12 = (bf16[2,48,512]{2,1,0:T(8,128)(2,1)}, bf16[2,48,512]{2,1,0:T(8,128)(2,1)S(1)}, u32[]{:S(2)}, u32[]{:S(2)}) collective-permute-start(bf16[2,48,512]{2,1,0:T(8,128)(2,1)} %get-tuple-element.83), channel_id=1, source_target_pairs={{0,12},{1,13},{2,14},{3,15},{4,8},{5,9},{6,10},{7,11},{8,4},{9,5},... | collective-permute-start | bytes 294920 | tf_op jit(solution)/shard_map/ppermute | solution.py:340
  21.3 28.7 %collective-permute-done.10.refs_1_ = bf16[2,48,512]{2,1,0:T(8,128)(2,1)S(1)} collective-permute-done((bf16[2,48,512]{2,1,0:T(8,128)(2,1)}, bf16[2,48,512]{2,1,0:T(8,128)(2,1)S(1)}, u32[]{:S(2)}, u32[]{:S(2)}) %collective-permute-start.10) | collective-permute-done | bytes 98336 | tf_op jit(solution)/shard_map/ppermute | solution.py:340
  49.9 3.9 %collective-permute-start.15 = (bf16[2,48,512]{2,1,0:T(8,128)(2,1)}, bf16[2,48,512]{2,1,0:T(8,128)(2,1)S(1)}, u32[]{:S(2)}, u32[]{:S(2)}) collective-permute-start(bf16[2,48,512]{2,1,0:T(8,128)(2,1)} %get-tuple-element.86), channel_id=1, source_target_pairs={{0,6},{1,7},{2,4},{3,5},{4,2},{5,3},{6,0},{7,1},{8,14},{9,15},{10,... | collective-permute-start | bytes 294920 | tf_op jit(solution)/shard_map/ppermute | solution.py:340
  60.6 2.4 %collective-permute-start.20 = (bf16[2,48,512]{2,1,0:T(8,128)(2,1)}, bf16[2,48,512]{2,1,0:T(8,128)(2,1)S(1)}, u32[]{:S(2)}, u32[]{:S(2)}) collective-permute-start(bf16[2,48,512]{2,1,0:T(8,128)(2,1)} %get-tuple-element.91), channel_id=1, source_target_pairs={{0,14},{1,15},{2,12},{3,13},{4,10},{5,11},{6,8},{7,9},{8,6},{9,7},... | collective-permute-start | bytes 294920 | tf_op jit(solution)/shard_map/ppermute | solution.py:340
  63.1 2.8 %collective-permute-done.18.refs_9_ = bf16[2,48,512]{2,1,0:T(8,128)(2,1)S(1)} collective-permute-done((bf16[2,48,512]{2,1,0:T(8,128)(2,1)}, bf16[2,48,512]{2,1,0:T(8,128)(2,1)S(1)}, u32[]{:S(2)}, u32[]{:S(2)}) %collective-permute-start.18) | collective-permute-done | bytes 98336 | tf_op jit(solution)/shard_map/ppermute | solution.py:340
  65.9 2.7 %collective-permute-start.23 = (bf16[2,48,512]{2,1,0:T(8,128)(2,1)}, bf16[2,48,512]{2,1,0:T(8,128)(2,1)S(1)}, u32[]{:S(2)}, u32[]{:S(2)}) collective-permute-start(bf16[2,48,512]{2,1,0:T(8,128)(2,1)} %get-tuple-element.94), channel_id=1, source_target_pairs={{0,4},{1,5},{2,6},{3,7},{4,0},{5,1},{6,2},{7,3},{8,12},{9,13},{10,... | collective-permute-start | bytes 294920 | tf_op jit(solution)/shard_map/ppermute | solution.py:340
  68.6 2.0 %collective-permute-start.24 = (bf16[2,48,512]{2,1,0:T(8,128)(2,1)}, bf16[2,48,512]{2,1,0:T(8,128)(2,1)S(1)}, u32[]{:S(2)}, u32[]{:S(2)}) collective-permute-start(bf16[2,48,512]{2,1,0:T(8,128)(2,1)} %get-tuple-element.95), channel_id=1, source_target_pairs={{0,15},{1,14},{2,13},{3,12},{4,11},{5,10},{6,9},{7,8},{8,7},{9,6},... | collective-permute-start | bytes 294920 | tf_op jit(solution)/shard_map/ppermute | solution.py:340
  70.6 3.4 %collective-permute-start.1 = (bf16[64,1792]{1,0:T(8,128)(2,1)S(1)}, bf16[64,1792]{1,0:T(8,128)(2,1)S(1)}, u32[]{:S(2)}, u32[]{:S(2)}) collective-permute-start(bf16[64,1792]{1,0:T(8,128)(2,1)S(1)} %get-tuple-element.69), channel_id=1, source_target_pairs={{0,8},{1,9},{2,10},{3,11},{4,12},{5,13},{6,14},{7,15},{8,0},{9,1},... | collective-permute-start | bytes 688136 | tf_op jit(solution)/shard_map/ppermute | solution.py:340
  78.5 8.5 %collective-permute-start.25 = (bf16[2,48,512]{2,1,0:T(8,128)(2,1)S(1)}, bf16[2,48,512]{2,1,0:T(8,128)(2,1)S(1)}, u32[]{:S(2)}, u32[]{:S(2)}) collective-permute-start(bf16[2,48,512]{2,1,0:T(8,128)(2,1)S(1)} %get-tuple-element.97), channel_id=1, source_target_pairs={{0,8},{1,9},{2,10},{3,11},{4,12},{5,13},{6,14},{7,15},{8,0},{9,1},... | collective-permute-start | bytes 294920 | tf_op jit(solution)/shard_map/ppermute | solution.py:340
  89.0 3.5 %collective-permute-done.2.info_ref = s32[2,256]{1,0:T(2,128)S(1)} collective-permute-done((s32[2,256]{1,0:T(2,128)S(1)}, s32[2,256]{1,0:T(2,128)S(1)}, u32[]{:S(2)}, u32[]{:S(2)}) %collective-permute-start.2) | collective-permute-done | bytes 2080 | tf_op jit(solution)/shard_map/ppermute | solution.py:340
  92.5 2.4 %collective-permute-start.27 = (bf16[2,48,512]{2,1,0:T(8,128)(2,1)S(1)}, bf16[2,48,512]{2,1,0:T(8,128)(2,1)S(1)}, u32[]{:S(2)}, u32[]{:S(2)}) collective-permute-start(bf16[2,48,512]{2,1,0:T(8,128)(2,1)S(1)} %get-tuple-element.99), channel_id=1, source_target_pairs={{0,12},{1,13},{2,14},{3,15},{4,8},{5,9},{6,10},{7,11},{8,4},{9,5},... | collective-permute-start | bytes 294920 | tf_op jit(solution)/shard_map/ppermute | solution.py:340
  95.3 3.9 %collective-permute-done.27.refs_11_ = bf16[2,48,512]{2,1,0:T(8,128)(2,1)S(1)} collective-permute-done((bf16[2,48,512]{2,1,0:T(8,128)(2,1)S(1)}, bf16[2,48,512]{2,1,0:T(8,128)(2,1)S(1)}, u32[]{:S(2)}, u32[]{:S(2)}) %collective-permute-start.27) | collective-permute-done | bytes 98336 | tf_op jit(solution)/shard_map/ppermute | solution.py:340
  102.3 2.5 %collective-permute-start.33 = (bf16[2,48,512]{2,1,0:T(8,128)(2,1)S(1)}, bf16[2,48,512]{2,1,0:T(8,128)(2,1)S(1)}, u32[]{:S(2)}, u32[]{:S(2)}) collective-permute-start(bf16[2,48,512]{2,1,0:T(8,128)(2,1)S(1)} %get-tuple-element.105), channel_id=1, source_target_pairs={{0,10},{1,11},{2,8},{3,9},{4,14},{5,15},{6,12},{7,13},{8,2},{9,3},... | collective-permute-start | bytes 294920 | tf_op jit(solution)/shard_map/ppermute | solution.py:340
  106.8 4.4 %collective-permute-start.34 = (bf16[2,48,512]{2,1,0:T(8,128)(2,1)S(1)}, bf16[2,48,512]{2,1,0:T(8,128)(2,1)S(1)}, u32[]{:S(2)}, u32[]{:S(2)}) collective-permute-start(bf16[2,48,512]{2,1,0:T(8,128)(2,1)S(1)} %get-tuple-element.106), channel_id=1, source_target_pairs={{0,5},{1,4},{2,7},{3,6},{4,1},{5,0},{6,3},{7,2},{8,13},{9,12},{10,... | collective-permute-start | bytes 294920 | tf_op jit(solution)/shard_map/ppermute | solution.py:340
  113.4 4.0 %collective-permute-done.34.refs_18_ = bf16[2,48,512]{2,1,0:T(8,128)(2,1)S(1)} collective-permute-done((bf16[2,48,512]{2,1,0:T(8,128)(2,1)S(1)}, bf16[2,48,512]{2,1,0:T(8,128)(2,1)S(1)}, u32[]{:S(2)}, u32[]{:S(2)}) %collective-permute-start.34) | collective-permute-done | bytes 98336 | tf_op jit(solution)/shard_map/ppermute | solution.py:340
  117.4 2.0 %collective-permute-start.37 = (bf16[2,48,512]{2,1,0:T(8,128)(2,1)S(1)}, bf16[2,48,512]{2,1,0:T(8,128)(2,1)S(1)}, u32[]{:S(2)}, u32[]{:S(2)}) collective-permute-start(bf16[2,48,512]{2,1,0:T(8,128)(2,1)S(1)} %get-tuple-element.109), channel_id=1, source_target_pairs={{0,11},{1,10},{2,9},{3,8},{4,15},{5,14},{6,13},{7,12},{8,3},{9,2},... | collective-permute-start | bytes 294920 | tf_op jit(solution)/shard_map/ppermute | solution.py:340
  119.4 2.2 %collective-permute-start.38 = (bf16[2,48,512]{2,1,0:T(8,128)(2,1)S(1)}, bf16[2,48,512]{2,1,0:T(8,128)(2,1)S(1)}, u32[]{:S(2)}, u32[]{:S(2)}) collective-permute-start(bf16[2,48,512]{2,1,0:T(8,128)(2,1)S(1)} %get-tuple-element.110), channel_id=1, source_target_pairs={{0,4},{1,5},{2,6},{3,7},{4,0},{5,1},{6,2},{7,3},{8,12},{9,13},{10,... | collective-permute-start | bytes 294920 | tf_op jit(solution)/shard_map/ppermute | solution.py:340
  122.3 3.1 %collective-permute-done.37.refs_21_ = bf16[2,48,512]{2,1,0:T(8,128)(2,1)S(1)} collective-permute-done((bf16[2,48,512]{2,1,0:T(8,128)(2,1)S(1)}, bf16[2,48,512]{2,1,0:T(8,128)(2,1)S(1)}, u32[]{:S(2)}, u32[]{:S(2)}) %collective-permute-start.37) | collective-permute-done | bytes 98336 | tf_op jit(solution)/shard_map/ppermute | solution.py:340
  129.2 2.5 %collective-permute-start.7 = (bf16[64,1792]{1,0:T(8,128)(2,1)S(1)}, bf16[64,1792]{1,0:T(8,128)(2,1)S(1)}, u32[]{:S(2)}, u32[]{:S(2)}) collective-permute-start(bf16[64,1792]{1,0:T(8,128)(2,1)S(1)} %get-tuple-element.76), channel_id=1, source_target_pairs={{0,5},{1,4},{2,7},{3,6},{4,1},{5,0},{6,3},{7,2},{8,13},{9,12},{10,... | collective-permute-start | bytes 688136 | tf_op jit(solution)/shard_map/ppermute | solution.py:340
  133.5 4.8 %collective-permute-done.7.refs_5_ = bf16[64,1792]{1,0:T(8,128)(2,1)S(1)} collective-permute-done((bf16[64,1792]{1,0:T(8,128)(2,1)S(1)}, bf16[64,1792]{1,0:T(8,128)(2,1)S(1)}, u32[]{:S(2)}, u32[]{:S(2)}) %collective-permute-start.7) | collective-permute-done | bytes 229408 | tf_op jit(solution)/shard_map/ppermute | solution.py:340
  138.3 2.7 %collective-permute-done.8.refs_6_ = bf16[64,1792]{1,0:T(8,128)(2,1)S(1)} collective-permute-done((bf16[64,1792]{1,0:T(8,128)(2,1)S(1)}, bf16[64,1792]{1,0:T(8,128)(2,1)S(1)}, u32[]{:S(2)}, u32[]{:S(2)}) %collective-permute-start.8) | collective-permute-done | bytes 229408 | tf_op jit(solution)/shard_map/ppermute | solution.py:340
  141.0 3.6 %collective-permute-done.9.refs_7_ = bf16[64,1792]{1,0:T(8,128)(2,1)S(1)} collective-permute-done((bf16[64,1792]{1,0:T(8,128)(2,1)S(1)}, bf16[64,1792]{1,0:T(8,128)(2,1)S(1)}, u32[]{:S(2)}, u32[]{:S(2)}) %collective-permute-start.9) | collective-permute-done | bytes 229408 | tf_op jit(solution)/shard_map/ppermute | solution.py:340
  144.6 5.1 %update.1 = (bf16[384,1024]{1,0:T(8,128)(2,1)}, bf16[384,1024]{1,0:T(8,128)(2,1)}, bf16[32,1024]{1,0:T(8,128)(2,1)S(1)}, bf16[32,1024]{1,0:T(8,128)(2,1)S(1)}, b...) custom-call(s32[1]{0:T(128)} %bitcast.me_ref, ...), custom_call_target="tpu_custom_call" | custom-call | flops 2239758336 | bytes 6029312 | tf_op jit(solution)/shard_map/update/pallas_call | solution.py:278
  149.7 2.4 %collective-permute-start.40 = (bf16[32,1024]{1,0:T(8,128)(2,1)S(1)}, bf16[32,1024]{1,0:T(8,128)(2,1)S(1)}, u32[]{:S(2)}, u32[]{:S(2)}) collective-permute-start(bf16[32,1024]{1,0:T(8,128)(2,1)S(1)} %get-tuple-element.116), channel_id=1, source_target_pairs={{0,8},{1,9},{2,10},{3,11},{4,12},{5,13},{6,14},{7,15},{8,0},{9,1},... | collective-permute-start | bytes 196616 | tf_op jit(solution)/shard_map/ppermute | solution.py:340
  156.3 2.6 %collective-permute-start.45 = (bf16[32,1024]{1,0:T(8,128)(2,1)S(1)}, bf16[32,1024]{1,0:T(8,128)(2,1)S(1)}, u32[]{:S(2)}, u32[]{:S(2)}) collective-permute-start(bf16[32,1024]{1,0:T(8,128)(2,1)S(1)} %get-tuple-element.121), channel_id=1, source_target_pairs={{0,6},{1,7},{2,4},{3,5},{4,2},{5,3},{6,0},{7,1},{8,14},{9,15},{10,... | collective-permute-start | bytes 196616 | tf_op jit(solution)/shard_map/ppermute | solution.py:340
  160.3 2.5 %collective-permute-start.48 = (bf16[32,1024]{1,0:T(8,128)(2,1)S(1)}, bf16[32,1024]{1,0:T(8,128)(2,1)S(1)}, u32[]{:S(2)}, u32[]{:S(2)}) collective-permute-start(bf16[32,1024]{1,0:T(8,128)(2,1)S(1)} %get-tuple-element.124), channel_id=1, source_target_pairs={{0,10},{1,11},{2,8},{3,9},{4,14},{5,15},{6,12},{7,13},{8,2},{9,3},... | collective-permute-start | bytes 196616 | tf_op jit(solution)/shard_map/ppermute | solution.py:340
  163.9 2.5 %collective-permute-start.50 = (bf16[32,1024]{1,0:T(8,128)(2,1)S(1)}, bf16[32,1024]{1,0:T(8,128)(2,1)S(1)}, u32[]{:S(2)}, u32[]{:S(2)}) collective-permute-start(bf16[32,1024]{1,0:T(8,128)(2,1)S(1)} %get-tuple-element.126), channel_id=1, source_target_pairs={{0,14},{1,15},{2,12},{3,13},{4,10},{5,11},{6,8},{7,9},{8,6},{9,7},... | collective-permute-start | bytes 196616 | tf_op jit(solution)/shard_map/ppermute | solution.py:340
  171.5 2.5 %collective-permute-done.52.refs_13_ = bf16[32,1024]{1,0:T(8,128)(2,1)S(1)} collective-permute-done((bf16[32,1024]{1,0:T(8,128)(2,1)S(1)}, bf16[32,1024]{1,0:T(8,128)(2,1)S(1)}, u32[]{:S(2)}, u32[]{:S(2)}) %collective-permute-start.52) | collective-permute-done | bytes 65568 | tf_op jit(solution)/shard_map/ppermute | solution.py:340
  174.0 2.3 %collective-permute-done.54.refs_15_ = bf16[32,1024]{1,0:T(8,128)(2,1)S(1)} collective-permute-done((bf16[32,1024]{1,0:T(8,128)(2,1)S(1)}, bf16[32,1024]{1,0:T(8,128)(2,1)S(1)}, u32[]{:S(2)}, u32[]{:S(2)}) %collective-permute-start.54) | collective-permute-done | bytes 65568 | tf_op jit(solution)/shard_map/ppermute | solution.py:340
  (104 shorter events, 48.1 us)
Async XLA Ops:
  8.6 93.7 %collective-permute-start = (bf16[192,1792]{1,0:T(8,128)(2,1)S(1)}, bf16[192,1792]{1,0:T(8,128)(2,1)S(1)}, u32[]{:S(2)}, u32[]{:S(2)}) collective-permute-start(bf16[192,1792]{1,0:T(8,128)(2,1)S(1)} %get-tuple-element.68), channel_id=1, source_target_pairs={{0,8},{1,9},{2,10},{3,11},{4,12},{5,13},{6,14},{7,15},{8,0},{9,1},... | collective-permute-start | bytes 2064392 | tf_op jit(solution)/shard_map/ppermute | solution.py:340
  15.9 34.0 %collective-permute-start.10 = (bf16[2,48,512]{2,1,0:T(8,128)(2,1)}, bf16[2,48,512]{2,1,0:T(8,128)(2,1)S(1)}, u32[]{:S(2)}, u32[]{:S(2)}) collective-permute-start(bf16[2,48,512]{2,1,0:T(8,128)(2,1)} %get-tuple-element.81), channel_id=1, source_target_pairs={{0,8},{1,9},{2,10},{3,11},{4,12},{5,13},{6,14},{7,15},{8,0},{9,1},... | collective-permute-start | bytes 294920 | tf_op jit(solution)/shard_map/ppermute | solution.py:340
  16.0 34.0 %collective-permute-start.11 = (bf16[2,48,512]{2,1,0:T(8,128)(2,1)}, bf16[2,48,512]{2,1,0:T(8,128)(2,1)S(1)}, u32[]{:S(2)}, u32[]{:S(2)}) collective-permute-start(bf16[2,48,512]{2,1,0:T(8,128)(2,1)} %get-tuple-element.82), channel_id=1, source_target_pairs={{0,7},{1,6},{2,5},{3,4},{4,3},{5,2},{6,1},{7,0},{8,15},{9,14},{10,... | collective-permute-start | bytes 294920 | tf_op jit(solution)/shard_map/ppermute | solution.py:340
  17.7 36.1 %collective-permute-start.12 = (bf16[2,48,512]{2,1,0:T(8,128)(2,1)}, bf16[2,48,512]{2,1,0:T(8,128)(2,1)S(1)}, u32[]{:S(2)}, u32[]{:S(2)}) collective-permute-start(bf16[2,48,512]{2,1,0:T(8,128)(2,1)} %get-tuple-element.83), channel_id=1, source_target_pairs={{0,12},{1,13},{2,14},{3,15},{4,8},{5,9},{6,10},{7,11},{8,4},{9,5},... | collective-permute-start | bytes 294920 | tf_op jit(solution)/shard_map/ppermute | solution.py:340
  20.2 34.8 %collective-permute-start.13 = (bf16[2,48,512]{2,1,0:T(8,128)(2,1)}, bf16[2,48,512]{2,1,0:T(8,128)(2,1)S(1)}, u32[]{:S(2)}, u32[]{:S(2)}) collective-permute-start(bf16[2,48,512]{2,1,0:T(8,128)(2,1)} %get-tuple-element.84), channel_id=1, source_target_pairs={{0,3},{1,2},{2,1},{3,0},{4,7},{5,6},{6,5},{7,4},{8,11},{9,10},{10,... | collective-permute-start | bytes 294920 | tf_op jit(solution)/shard_map/ppermute | solution.py:340
  49.9 8.7 %collective-permute-start.15 = (bf16[2,48,512]{2,1,0:T(8,128)(2,1)}, bf16[2,48,512]{2,1,0:T(8,128)(2,1)S(1)}, u32[]{:S(2)}, u32[]{:S(2)}) collective-permute-start(bf16[2,48,512]{2,1,0:T(8,128)(2,1)} %get-tuple-element.86), channel_id=1, source_target_pairs={{0,6},{1,7},{2,4},{3,5},{4,2},{5,3},{6,0},{7,1},{8,14},{9,15},{10,... | collective-permute-start | bytes 294920 | tf_op jit(solution)/shard_map/ppermute | solution.py:340
  55.0 7.9 %collective-permute-start.17 = (bf16[2,48,512]{2,1,0:T(8,128)(2,1)}, bf16[2,48,512]{2,1,0:T(8,128)(2,1)S(1)}, u32[]{:S(2)}, u32[]{:S(2)}) collective-permute-start(bf16[2,48,512]{2,1,0:T(8,128)(2,1)} %get-tuple-element.88), channel_id=1, source_target_pairs={{0,2},{1,3},{2,0},{3,1},{4,6},{5,7},{6,4},{7,5},{8,10},{9,11},{10,... | collective-permute-start | bytes 294920 | tf_op jit(solution)/shard_map/ppermute | solution.py:340
  57.0 8.9 %collective-permute-start.18 = (bf16[2,48,512]{2,1,0:T(8,128)(2,1)}, bf16[2,48,512]{2,1,0:T(8,128)(2,1)S(1)}, u32[]{:S(2)}, u32[]{:S(2)}) collective-permute-start(bf16[2,48,512]{2,1,0:T(8,128)(2,1)} %get-tuple-element.89), channel_id=1, source_target_pairs={{0,10},{1,11},{2,8},{3,9},{4,14},{5,15},{6,12},{7,13},{8,2},{9,3},... | collective-permute-start | bytes 294920 | tf_op jit(solution)/shard_map/ppermute | solution.py:340
  60.6 8.0 %collective-permute-start.20 = (bf16[2,48,512]{2,1,0:T(8,128)(2,1)}, bf16[2,48,512]{2,1,0:T(8,128)(2,1)S(1)}, u32[]{:S(2)}, u32[]{:S(2)}) collective-permute-start(bf16[2,48,512]{2,1,0:T(8,128)(2,1)} %get-tuple-element.91), channel_id=1, source_target_pairs={{0,14},{1,15},{2,12},{3,13},{4,10},{5,11},{6,8},{7,9},{8,6},{9,7},... | collective-permute-start | bytes 294920 | tf_op jit(solution)/shard_map/ppermute | solution.py:340
  62.9 7.7 %collective-permute-start.21 = (bf16[2,48,512]{2,1,0:T(8,128)(2,1)}, bf16[2,48,512]{2,1,0:T(8,128)(2,1)S(1)}, u32[]{:S(2)}, u32[]{:S(2)}) collective-permute-start(bf16[2,48,512]{2,1,0:T(8,128)(2,1)} %get-tuple-element.92), channel_id=1, source_target_pairs={{0,1},{1,0},{2,3},{3,2},{4,5},{5,4},{6,7},{7,6},{8,9},{9,8},{10,11... | collective-permute-start | bytes 294920 | tf_op jit(solution)/shard_map/ppermute | solution.py:340
  65.9 9.2 %collective-permute-start.22 = (bf16[2,48,512]{2,1,0:T(8,128)(2,1)}, bf16[2,48,512]{2,1,0:T(8,128)(2,1)S(1)}, u32[]{:S(2)}, u32[]{:S(2)}) collective-permute-start(bf16[2,48,512]{2,1,0:T(8,128)(2,1)} %get-tuple-element.93), channel_id=1, source_target_pairs={{0,11},{1,10},{2,9},{3,8},{4,15},{5,14},{6,13},{7,12},{8,3},{9,2},... | collective-permute-start | bytes 294920 | tf_op jit(solution)/shard_map/ppermute | solution.py:340
  65.9 9.2 %collective-permute-start.23 = (bf16[2,48,512]{2,1,0:T(8,128)(2,1)}, bf16[2,48,512]{2,1,0:T(8,128)(2,1)S(1)}, u32[]{:S(2)}, u32[]{:S(2)}) collective-permute-start(bf16[2,48,512]{2,1,0:T(8,128)(2,1)} %get-tuple-element.94), channel_id=1, source_target_pairs={{0,4},{1,5},{2,6},{3,7},{4,0},{5,1},{6,2},{7,3},{8,12},{9,13},{10,... | collective-permute-start | bytes 294920 | tf_op jit(solution)/shard_map/ppermute | solution.py:340
  68.6 8.2 %collective-permute-start.24 = (bf16[2,48,512]{2,1,0:T(8,128)(2,1)}, bf16[2,48,512]{2,1,0:T(8,128)(2,1)S(1)}, u32[]{:S(2)}, u32[]{:S(2)}) collective-permute-start(bf16[2,48,512]{2,1,0:T(8,128)(2,1)} %get-tuple-element.95), channel_id=1, source_target_pairs={{0,15},{1,14},{2,13},{3,12},{4,11},{5,10},{6,9},{7,8},{8,7},{9,6},... | collective-permute-start | bytes 294920 | tf_op jit(solution)/shard_map/ppermute | solution.py:340
  70.6 30.3 %collective-permute-start.1 = (bf16[64,1792]{1,0:T(8,128)(2,1)S(1)}, bf16[64,1792]{1,0:T(8,128)(2,1)S(1)}, u32[]{:S(2)}, u32[]{:S(2)}) collective-permute-start(bf16[64,1792]{1,0:T(8,128)(2,1)S(1)} %get-tuple-element.69), channel_id=1, source_target_pairs={{0,8},{1,9},{2,10},{3,11},{4,12},{5,13},{6,14},{7,15},{8,0},{9,1},... | collective-permute-start | bytes 688136 | tf_op jit(solution)/shard_map/ppermute | solution.py:340
  78.5 16.4 %collective-permute-start.25 = (bf16[2,48,512]{2,1,0:T(8,128)(2,1)S(1)}, bf16[2,48,512]{2,1,0:T(8,128)(2,1)S(1)}, u32[]{:S(2)}, u32[]{:S(2)}) collective-permute-start(bf16[2,48,512]{2,1,0:T(8,128)(2,1)S(1)} %get-tuple-element.97), channel_id=1, source_target_pairs={{0,8},{1,9},{2,10},{3,11},{4,12},{5,13},{6,14},{7,15},{8,0},{9,1},... | collective-permute-start | bytes 294920 | tf_op jit(solution)/shard_map/ppermute | solution.py:340
  87.1 8.2 %collective-permute-start.26 = (bf16[2,48,512]{2,1,0:T(8,128)(2,1)S(1)}, bf16[2,48,512]{2,1,0:T(8,128)(2,1)S(1)}, u32[]{:S(2)}, u32[]{:S(2)}) collective-permute-start(bf16[2,48,512]{2,1,0:T(8,128)(2,1)S(1)} %get-tuple-element.98), channel_id=1, source_target_pairs={{0,7},{1,6},{2,5},{3,4},{4,3},{5,2},{6,1},{7,0},{8,15},{9,14},{10,... | collective-permute-start | bytes 294920 | tf_op jit(solution)/shard_map/ppermute | solution.py:340
  95.3 10.0 %collective-permute-start.29 = (bf16[2,48,512]{2,1,0:T(8,128)(2,1)S(1)}, bf16[2,48,512]{2,1,0:T(8,128)(2,1)S(1)}, u32[]{:S(2)}, u32[]{:S(2)}) collective-permute-start(bf16[2,48,512]{2,1,0:T(8,128)(2,1)S(1)} %get-tuple-element.101), channel_id=1, source_target_pairs={{0,9},{1,8},{2,11},{3,10},{4,13},{5,12},{6,15},{7,14},{8,1},{9,0},... | collective-permute-start | bytes 294920 | tf_op jit(solution)/shard_map/ppermute | solution.py:340
  100.9 10.3 %collective-permute-start.32 = (bf16[2,48,512]{2,1,0:T(8,128)(2,1)S(1)}, bf16[2,48,512]{2,1,0:T(8,128)(2,1)S(1)}, u32[]{:S(2)}, u32[]{:S(2)}) collective-permute-start(bf16[2,48,512]{2,1,0:T(8,128)(2,1)S(1)} %get-tuple-element.104), channel_id=1, source_target_pairs={{0,2},{1,3},{2,0},{3,1},{4,6},{5,7},{6,4},{7,5},{8,10},{9,11},{10,... | collective-permute-start | bytes 294920 | tf_op jit(solution)/shard_map/ppermute | solution.py:340
  102.3 10.9 %collective-permute-start.33 = (bf16[2,48,512]{2,1,0:T(8,128)(2,1)S(1)}, bf16[2,48,512]{2,1,0:T(8,128)(2,1)S(1)}, u32[]{:S(2)}, u32[]{:S(2)}) collective-permute-start(bf16[2,48,512]{2,1,0:T(8,128)(2,1)S(1)} %get-tuple-element.105), channel_id=1, source_target_pairs={{0,10},{1,11},{2,8},{3,9},{4,14},{5,15},{6,12},{7,13},{8,2},{9,3},... | collective-permute-start | bytes 294920 | tf_op jit(solution)/shard_map/ppermute | solution.py:340
  105.3 26.4 %collective-permute-start.3 = (bf16[64,1792]{1,0:T(8,128)(2,1)S(1)}, bf16[64,1792]{1,0:T(8,128)(2,1)S(1)}, u32[]{:S(2)}, u32[]{:S(2)}) collective-permute-start(bf16[64,1792]{1,0:T(8,128)(2,1)S(1)} %get-tuple-element.72), channel_id=1, source_target_pairs={{0,4},{1,5},{2,6},{3,7},{4,0},{5,1},{6,2},{7,3},{8,12},{9,13},{10,... | collective-permute-start | bytes 688136 | tf_op jit(solution)/shard_map/ppermute | solution.py:340
  105.8 25.9 %collective-permute-start.4 = (bf16[64,1792]{1,0:T(8,128)(2,1)S(1)}, bf16[64,1792]{1,0:T(8,128)(2,1)S(1)}, u32[]{:S(2)}, u32[]{:S(2)}) collective-permute-start(bf16[64,1792]{1,0:T(8,128)(2,1)S(1)} %get-tuple-element.73), channel_id=1, source_target_pairs={{0,3},{1,2},{2,1},{3,0},{4,7},{5,6},{6,5},{7,4},{8,11},{9,10},{10,... | collective-permute-start | bytes 688136 | tf_op jit(solution)/shard_map/ppermute | solution.py:340
  106.8 10.6 %collective-permute-start.34 = (bf16[2,48,512]{2,1,0:T(8,128)(2,1)S(1)}, bf16[2,48,512]{2,1,0:T(8,128)(2,1)S(1)}, u32[]{:S(2)}, u32[]{:S(2)}) collective-permute-start(bf16[2,48,512]{2,1,0:T(8,128)(2,1)S(1)} %get-tuple-element.106), channel_id=1, source_target_pairs={{0,5},{1,4},{2,7},{3,6},{4,1},{5,0},{6,3},{7,2},{8,13},{9,12},{10,... | collective-permute-start | bytes 294920 | tf_op jit(solution)/shard_map/ppermute | solution.py:340
  111.2 8.2 %collective-permute-start.35 = (bf16[2,48,512]{2,1,0:T(8,128)(2,1)S(1)}, bf16[2,48,512]{2,1,0:T(8,128)(2,1)S(1)}, u32[]{:S(2)}, u32[]{:S(2)}) collective-permute-start(bf16[2,48,512]{2,1,0:T(8,128)(2,1)S(1)} %get-tuple-element.107), channel_id=1, source_target_pairs={{0,14},{1,15},{2,12},{3,13},{4,10},{5,11},{6,8},{7,9},{8,6},{9,7},... | collective-permute-start | bytes 294920 | tf_op jit(solution)/shard_map/ppermute | solution.py:340
  113.1 8.4 %collective-permute-start.36 = (bf16[2,48,512]{2,1,0:T(8,128)(2,1)S(1)}, bf16[2,48,512]{2,1,0:T(8,128)(2,1)S(1)}, u32[]{:S(2)}, u32[]{:S(2)}) collective-permute-start(bf16[2,48,512]{2,1,0:T(8,128)(2,1)S(1)} %get-tuple-element.108), channel_id=1, source_target_pairs={{0,1},{1,0},{2,3},{3,2},{4,5},{5,4},{6,7},{7,6},{8,9},{9,8},{10,11... | collective-permute-start | bytes 294920 | tf_op jit(solution)/shard_map/ppermute | solution.py:340
  117.4 8.0 %collective-permute-start.37 = (bf16[2,48,512]{2,1,0:T(8,128)(2,1)S(1)}, bf16[2,48,512]{2,1,0:T(8,128)(2,1)S(1)}, u32[]{:S(2)}, u32[]{:S(2)}) collective-permute-start(bf16[2,48,512]{2,1,0:T(8,128)(2,1)S(1)} %get-tuple-element.109), channel_id=1, source_target_pairs={{0,11},{1,10},{2,9},{3,8},{4,15},{5,14},{6,13},{7,12},{8,3},{9,2},... | collective-permute-start | bytes 294920 | tf_op jit(solution)/shard_map/ppermute | solution.py:340
  121.6 7.6 %collective-permute-start.39 = (bf16[2,48,512]{2,1,0:T(8,128)(2,1)S(1)}, bf16[2,48,512]{2,1,0:T(8,128)(2,1)S(1)}, u32[]{:S(2)}, u32[]{:S(2)}) collective-permute-start(bf16[2,48,512]{2,1,0:T(8,128)(2,1)S(1)} %get-tuple-element.111), channel_id=1, source_target_pairs={{0,15},{1,14},{2,13},{3,12},{4,11},{5,10},{6,9},{7,8},{8,7},{9,6},... | collective-permute-start | bytes 294920 | tf_op jit(solution)/shard_map/ppermute | solution.py:340
  125.4 8.1 %collective-permute-start.5 = (bf16[64,1792]{1,0:T(8,128)(2,1)S(1)}, bf16[64,1792]{1,0:T(8,128)(2,1)S(1)}, u32[]{:S(2)}, u32[]{:S(2)}) collective-permute-start(bf16[64,1792]{1,0:T(8,128)(2,1)S(1)} %get-tuple-element.74), channel_id=1, source_target_pairs={{0,6},{1,7},{2,4},{3,5},{4,2},{5,3},{6,0},{7,1},{8,14},{9,15},{10,... | collective-permute-start | bytes 688136 | tf_op jit(solution)/shard_map/ppermute | solution.py:340
  129.2 9.1 %collective-permute-start.7 = (bf16[64,1792]{1,0:T(8,128)(2,1)S(1)}, bf16[64,1792]{1,0:T(8,128)(2,1)S(1)}, u32[]{:S(2)}, u32[]{:S(2)}) collective-permute-start(bf16[64,1792]{1,0:T(8,128)(2,1)S(1)} %get-tuple-element.76), channel_id=1, source_target_pairs={{0,5},{1,4},{2,7},{3,6},{4,1},{5,0},{6,3},{7,2},{8,13},{9,12},{10,... | collective-permute-start | bytes 688136 | tf_op jit(solution)/shard_map/ppermute | solution.py:340
  131.6 9.4 %collective-permute-start.8 = (bf16[64,1792]{1,0:T(8,128)(2,1)S(1)}, bf16[64,1792]{1,0:T(8,128)(2,1)S(1)}, u32[]{:S(2)}, u32[]{:S(2)}) collective-permute-start(bf16[64,1792]{1,0:T(8,128)(2,1)S(1)} %get-tuple-element.77), channel_id=1, source_target_pairs={{0,2},{1,3},{2,0},{3,1},{4,6},{5,7},{6,4},{7,5},{8,10},{9,11},{10,... | collective-permute-start | bytes 688136 | tf_op jit(solution)/shard_map/ppermute | solution.py:340
  131.7 13.0 %collective-permute-start.9 = (bf16[64,1792]{1,0:T(8,128)(2,1)S(1)}, bf16[64,1792]{1,0:T(8,128)(2,1)S(1)}, u32[]{:S(2)}, u32[]{:S(2)}) collective-permute-start(bf16[64,1792]{1,0:T(8,128)(2,1)S(1)} %get-tuple-element.78), channel_id=1, source_target_pairs={{0,7},{1,6},{2,5},{3,4},{4,3},{5,2},{6,1},{7,0},{8,15},{9,14},{10,... | collective-permute-start | bytes 688136 | tf_op jit(solution)/shard_map/ppermute | solution.py:340
  155.0 7.8 %collective-permute-start.44 = (bf16[32,1024]{1,0:T(8,128)(2,1)S(1)}, bf16[32,1024]{1,0:T(8,128)(2,1)S(1)}, u32[]{:S(2)}, u32[]{:S(2)}) collective-permute-start(bf16[32,1024]{1,0:T(8,128)(2,1)S(1)} %get-tuple-element.120), channel_id=1, source_target_pairs={{0,9},{1,8},{2,11},{3,10},{4,13},{5,12},{6,15},{7,14},{8,1},{9,0},... | collective-permute-start | bytes 196616 | tf_op jit(solution)/shard_map/ppermute | solution.py:340
  156.3 7.7 %collective-permute-start.45 = (bf16[32,1024]{1,0:T(8,128)(2,1)S(1)}, bf16[32,1024]{1,0:T(8,128)(2,1)S(1)}, u32[]{:S(2)}, u32[]{:S(2)}) collective-permute-start(bf16[32,1024]{1,0:T(8,128)(2,1)S(1)} %get-tuple-element.121), channel_id=1, source_target_pairs={{0,6},{1,7},{2,4},{3,5},{4,2},{5,3},{6,0},{7,1},{8,14},{9,15},{10,... | collective-permute-start | bytes 196616 | tf_op jit(solution)/shard_map/ppermute | solution.py:340
  (33 other events, 161.9 us)

commit v13 on v10

--- a/solution.py
+++ b/solution.py
@@ -144,47 +144,62 @@
     )(me, moment, weight)
 
 
+def apart(groups):
+    return mixed_order(groups)[-(groups // 3) :]
+
+
 def reorder_kernel(me_ref, perm_ref, *refs):
-    groups = len(refs) // 2 - 1
-    sources, targets, held = refs[:groups], refs[groups + 1 : 2 * groups + 1], refs[-1]
-    me, order = me_ref[0], mixed_order(groups)
+    groups = perm_ref.shape[0]
+    sources, targets, held = refs[:groups], refs[groups + 1 : -1], refs[-1]
+    me, order, late = me_ref[0], mixed_order(groups), apart(groups)
     for s, source in zip(order, sources):
         held[me ^ perm_ref[me ^ s]] = source[...]
-    for s, target in zip(order, targets):
+    whole = [s for s in order if s not in late]
+    for s, target in zip(whole, targets):
         target[...] = held[s]
+    for n, target in enumerate(targets[len(whole) :]):
+        target[...] = held[late[n % len(late)], n // len(late)]
 
 
 def reorder(me, perm, pieces, earlier):
-    groups = len(pieces)
-    piece = jax.ShapeDtypeStruct(pieces[0].shape, BF16)
-    return pl.pallas_call(
+    groups, late = len(pieces), len(apart(len(pieces)))
+    shape = pieces[0].shape
+    whole, half = jax.ShapeDtypeStruct(shape, BF16), jax.ShapeDtypeStruct(shape[1:], BF16)
+    targets = pl.pallas_call(
         reorder_kernel,
-        out_shape=(piece,) * groups,
+        out_shape=(whole,) * (groups - late) + (half,) * (2 * late),
         in_specs=[SMEM, SMEM] + [VMEM] * (groups + 1),
-        out_specs=(VMEM,) * groups,
-        scratch_shapes=[pltpu.VMEM((groups,) + pieces[0].shape, BF16)],
+        out_specs=(VMEM,) * (groups + late),
+        scratch_shapes=[pltpu.VMEM((groups,) + shape, BF16)],
         compiler_params=pltpu.CompilerParams(vmem_limit_bytes=32 * MIB),
         cost_estimate=pl.CostEstimate(flops=0, bytes_accessed=4 * groups * pieces[0].size, transcendentals=0),
         name="reorder",
     )(me, perm, *pieces, earlier)
-
-
-def update_kernel(groups, me_ref, *refs):
-    packed, pieces, produced = refs[:groups], refs[groups : 2 * groups], refs[2 * groups + 2 : 3 * groups + 2]
-    weight_new_ref, moment_new_ref = refs[2 * groups : 2 * groups + 2]
-    held, rows_ref = refs[-2:]
-    _, ff, d = held.shape
+    return targets[: groups - late], targets[groups - late : groups], targets[groups:]
+
+
+def assembled(lead, me_ref, whole, pieces, held):
+    groups = len(whole) + len(pieces)
+    late = apart(groups)
+    rows, columns = pieces[0].shape
+    chunks = dict(zip([s for s in mixed_order(groups) if s not in late], [piece.at[lead] for piece in whole]))
+    chunks.update(zip(late, pieces))
+    for s, chunk in chunks.items():
+        chunk_at(held, 0, me_ref[0] ^ s, rows, columns)[...] = chunk[...]
+    return held[0].astype(F32)
+
+
+def orthogonal_kernel(groups, me_ref, *refs):
+    packed, whole, pieces = refs[:groups], refs[groups : -4 - len(apart(groups))], refs[-4 - len(apart(groups)) : -4]
+    moment_new_ref, ortho_ref, held, rows_ref = refs[-4:]
+    ff, d = ortho_ref.shape
     capacity = packed[0].shape[0]
     for n, piece in enumerate(packed):
-        rows_ref[n * capacity : (n + 1) * capacity] = piece[...]
-    for s, piece in zip(mixed_order(groups), pieces):
-        rows, columns = piece.shape[1:]
-        for lead in range(2):
-            chunk_at(held, lead, me_ref[0] ^ s, rows, columns)[...] = piece[lead]
+        rows_ref[n * capacity : (n + 1) * capacity] = piece[:, : ff + d]
     grad = lax.dot_general(
-        rows_ref[:, :ff], rows_ref[:, ff : ff + d], (((0,), (0,)), ((), ())), preferred_element_type=F32
-    )
-    moment_new = (moment_decay * held[0].astype(F32) + grad).astype(BF16)
+        rows_ref[:, :ff], rows_ref[:, ff:], (((0,), (0,)), ((), ())), preferred_element_type=F32
+    )
+    moment_new = (moment_decay * assembled(0, me_ref, whole, pieces, held) + grad).astype(BF16)
     moment_new_ref[...] = moment_new
     moment_f = moment_new.astype(F32)
     frobenius = jnp.sqrt(jnp.sum(moment_f * moment_f))
@@ -198,33 +213,64 @@
         current = (
             linear_term * current.astype(F32) + jnp.dot(poly, current, preferred_element_type=F32)
         ).astype(BF16)
-    weight_new = (held[1].astype(F32) - step_scale * current.astype(F32)).astype(BF16)
+    ortho_ref[...] = current
+
+
+def orthogonal(me, packed, whole, pieces, ff, d):
+    groups = len(packed)
+    slots = groups * packed[0].shape[0]
+    shape = jax.ShapeDtypeStruct((ff, d), BF16)
+    return pl.pallas_call(
+        functools.partial(orthogonal_kernel, groups),
+        out_shape=(shape, shape),
+        in_specs=[SMEM] + [VMEM] * (2 * groups),
+        out_specs=(VMEM, VMEM),
+        scratch_shapes=[pltpu.VMEM((1, ff, d), BF16), pltpu.VMEM((slots, ff + d), BF16)],
+        compiler_params=pltpu.CompilerParams(vmem_limit_bytes=40 * MIB),
+        cost_estimate=pl.CostEstimate(
+            flops=2 * ff * d * slots + 8 * ff * ff * d + 4 * ff**3,
+            bytes_accessed=6 * ff * d + 2 * slots * (ff + d),
+            transcendentals=1,
+        ),
+        name="orthogonal",
+    )(me, *packed, *whole, *pieces)
+
+
+def produce_kernel(groups, me_ref, ortho_ref, *refs):
+    late = len(apart(groups))
+    packed, whole, pieces, refs = refs[:groups], refs[groups : 2 * groups - late], refs[2 * groups - late : 2 * groups], refs[2 * groups :]
+    weight_new_ref, produced, (held, rows_ref) = refs[0], refs[1:-2], refs[-2:]
+    ff, d = ortho_ref.shape
+    capacity = packed[0].shape[0]
+    for n, piece in enumerate(packed):
+        rows_ref[n * capacity : (n + 1) * capacity] = piece[:, ff + d :]
+    weight = assembled(1, me_ref, whole, pieces, held)
+    weight_new = (weight - step_scale * ortho_ref[...].astype(F32)).astype(BF16)
     weight_new_ref[...] = weight_new
-    product = jnp.dot(rows_ref[:, ff + d :], weight_new, preferred_element_type=F32).astype(BF16)
+    product = jnp.dot(rows_ref[...], weight_new, preferred_element_type=F32).astype(BF16)
     for n, piece in enumerate(produced):
         piece[...] = product[n * capacity : (n + 1) * capacity]
 
 
-def update(me, packed, pieces, ff, d):
-    groups = len(pieces)
-    capacity, width = packed[0].shape
-    slots = groups * capacity
-    shape = jax.ShapeDtypeStruct((ff, d), BF16)
-    weight_new, moment_new, *produced = pl.pallas_call(
-        functools.partial(update_kernel, groups),
-        out_shape=(shape, shape) + (jax.ShapeDtypeStruct((capacity, d), BF16),) * groups,
-        in_specs=[SMEM] + [VMEM] * (2 * groups),
-        out_specs=(VMEM,) * (groups + 2),
-        scratch_shapes=[pltpu.VMEM((2, ff, d), BF16), pltpu.VMEM((slots, width), BF16)],
+def produce(me, ortho, packed, whole, pieces):
+    groups = len(packed)
+    ff, d = ortho.shape
+    capacity = packed[0].shape[0]
+    weight_new, *produced = pl.pallas_call(
+        functools.partial(produce_kernel, groups),
+        out_shape=(jax.ShapeDtypeStruct((ff, d), BF16),) + (jax.ShapeDtypeStruct((capacity, d), BF16),) * groups,
+        in_specs=[SMEM] + [VMEM] * (1 + 2 * groups),
+        out_specs=(VMEM,) * (groups + 1),
+        scratch_shapes=[pltpu.VMEM((1, ff, d), BF16), pltpu.VMEM((groups * capacity, ff), BF16)],
         compiler_params=pltpu.CompilerParams(vmem_limit_bytes=40 * MIB),
         cost_estimate=pl.CostEstimate(
-            flops=4 * ff * d * slots + 8 * ff * ff * d + 4 * ff**3,
-            bytes_accessed=8 * ff * d + 2 * slots * (width + d),
-            transcendentals=1,
+            flops=2 * ff * d * groups * capacity,
+            bytes_accessed=8 * ff * d + 2 * groups * capacity * (ff + d),
+            transcendentals=0,
         ),
-        name="update",
-    )(me, *packed, *pieces)
-    return weight_new, moment_new, produced
+        name="produce",
+    )(me, ortho, *packed, *whole, *pieces)
+    return weight_new, produced
 
 
 def finish_kernel(groups, slot_ref, gates_ref, *refs):
@@ -269,11 +315,11 @@
     return [0] + [s for pair in zip(far, near + [None]) for s in pair if s is not None]
 
 
-def swap(pieces):
-    groups = len(pieces)
-    order = mixed_order(groups)
-    return [pieces[0]] + [
-        lax.ppermute(piece, "expert", [(i, i ^ s) for i in range(groups)]) for s, piece in zip(order[1:], pieces[1:])
+def swap(pieces, order):
+    groups = lax.axis_size("expert")
+    return [
+        lax.ppermute(piece, "expert", [(i, i ^ s) for i in range(groups)]) if s else piece
+        for s, piece in zip(order, pieces)
     ]
 
 
@@ -284,15 +330,18 @@
     me = lax.axis_index("expert").astype(jnp.int32).reshape(1)
     capacity = max(4, 2 * grad_hidden.shape[0] // groups)
     ff, d = w_down.shape[1:]
-    spread = swap(split(me, w_moment, w_down, groups))
+    order, late = mixed_order(groups), apart(groups)
+    spread = swap(split(me, w_moment, w_down, groups), order)
     packed, fwd_slot, gates = pack_rows(
         live_rows, me, perm, grad_route, fwd_route, grad_hidden, grad_out, fwd_hidden, fwd_gate,
         spread[2 * groups // 3], groups, capacity,
     )
-    received = swap(packed)
-    placed = swap(reorder(me, perm, spread, received[groups // 3]))
-    weight_new, moment_new, produced = update(me, received, placed, ff, d)
-    return weight_new[None], moment_new[None], finish(fwd_slot, gates, swap(produced))
+    received = swap(packed, order)
+    whole, moment_pieces, weight_pieces = reorder(me, perm, spread, received[groups // 3])
+    whole = swap(whole, [s for s in order if s not in late])
+    moment_new, ortho = orthogonal(me, received, whole, swap(moment_pieces, late), ff, d)
+    weight_new, produced = produce(me, ortho, received, whole, swap(weight_pieces, late))
+    return weight_new[None], moment_new[None], finish(fwd_slot, gates, swap(produced, order))
 
 
 def lookup(route_ids, mapping):

time: 149 us -> 150 us (level)
  starting transfers between devices: 110 us -> 113 us
  waiting for transfers between devices: 24.5 us -> 21.7 us
    ppermute x60 -> x65, starting transfers between devices: 110 us -> 113 us  [swap(): lax.ppermute(piece, 'expert', [(i, i ^ s) for i in range(groups)])]
    ppermute x60 -> x65, waiting for transfers between devices: 24.5 us -> 21.7 us  [swap(): lax.ppermute(piece, 'expert', [(i, i ^ s) for i in range(groups)])]
    pallas_call x2 -> x3, Pallas kernels: 5.48 us -> 5.89 us  [the longest x1 3.72 us: orthogonal(): pl.pallas_call(functools.partial(orthogonal_kernel, groups), out_shape=(s...]
  transfers between devices with their start and end apart: 60 -> 65, of which waited for: 12 -> 15; matrix products, arithmetic and copies ran while one was open for 0% -> 0% of each run, Pallas kernels for 2% -> 5%
where the time goes in v13:
time: 150 us
  starting transfers between devices  113 us (75%)
  waiting for transfers between devices  21.7 us (14%)
  Pallas kernels  12.7 us (8%)
  between operations  1.53 us (1%)
    ppermute x65, starting transfers between devices, swap(): lax.ppermute(piece, 'expert', [(i, i ^ s) for i in range(groups)])  113 us
    ppermute x65, waiting for transfers between devices, swap(): lax.ppermute(piece, 'expert', [(i, i ^ s) for i in range(groups)])  21.7 us
    pallas_call x1, Pallas kernels, orthogonal(): pl.pallas_call(functools.partial(orthogonal_kernel, groups), out_shape=(s...  3.72 us
  transfers between devices with their start and end apart: 65, of which 15 were waited for; matrix products, arithmetic and copies ran while one was open for 0% of the time, Pallas kernels for 5%

profile of v13, /device:TPU:0, one launch (start us, length us, event | category | flops | bytes accessed | tf_op | source)
XLA Modules:
  0.0 149.8 jit_solution(5453837119484130908)
XLA Ops:
  0.7 2.7 %split.1 = (bf16[2,48,512]{2,1,0:T(8,128)(2,1)}, bf16[2,48,512]{2,1,0:T(8,128)(2,1)}, bf16[2,48,512]{2,1,0:T(8,128)(2,1)}, bf16[2,48,512]{2,1,0:T(8,128)(2,1)}, ...) custom-call(s32[1]{0:T(128)} %bitcast.me_ref, ...), custom_call_target="tpu_custom_call" | custom-call | bytes 3145728 | tf_op jit(solution)/shard_map/split/pallas_call | solution.py:135
  3.4 2.5 %collective-permute-start = (bf16[2,48,512]{2,1,0:T(8,128)(2,1)}, bf16[2,48,512]{2,1,0:T(8,128)(2,1)S(1)}, u32[]{:S(2)}, u32[]{:S(2)}) collective-permute-start(bf16[2,48,512]{2,1,0:T(8,128)(2,1)} %get-tuple-element.77), channel_id=1, source_target_pairs={{0,5},{1,4},{2,7},{3,6},{4,1},{5,0},{6,3},{7,2},{8,13},{9,12},{10,... | collective-permute-start | bytes 294920 | tf_op jit(solution)/shard_map/ppermute | solution.py:321
  5.9 2.6 %collective-permute-start.16 = (bf16[2,48,512]{2,1,0:T(8,128)(2,1)}, bf16[2,48,512]{2,1,0:T(8,128)(2,1)S(1)}, u32[]{:S(2)}, u32[]{:S(2)}) collective-permute-start(bf16[2,48,512]{2,1,0:T(8,128)(2,1)} %get-tuple-element.95), channel_id=1, source_target_pairs={{0,8},{1,9},{2,10},{3,11},{4,12},{5,13},{6,14},{7,15},{8,0},{9,1},... | collective-permute-start | bytes 294920 | tf_op jit(solution)/shard_map/ppermute | solution.py:321
  11.3 1.9 %collective-permute-start.20 = (bf16[2,48,512]{2,1,0:T(8,128)(2,1)}, bf16[2,48,512]{2,1,0:T(8,128)(2,1)S(1)}, u32[]{:S(2)}, u32[]{:S(2)}) collective-permute-start(bf16[2,48,512]{2,1,0:T(8,128)(2,1)} %get-tuple-element.99), channel_id=1, source_target_pairs={{0,9},{1,8},{2,11},{3,10},{4,13},{5,12},{6,15},{7,14},{8,1},{9,0},... | collective-permute-start | bytes 294920 | tf_op jit(solution)/shard_map/ppermute | solution.py:321
  16.1 2.8 %collective-permute-start.22 = (bf16[2,48,512]{2,1,0:T(8,128)(2,1)}, bf16[2,48,512]{2,1,0:T(8,128)(2,1)S(1)}, u32[]{:S(2)}, u32[]{:S(2)}) collective-permute-start(bf16[2,48,512]{2,1,0:T(8,128)(2,1)} %get-tuple-element.101), channel_id=1, source_target_pairs={{0,13},{1,12},{2,15},{3,14},{4,9},{5,8},{6,11},{7,10},{8,5},{9,4},... | collective-permute-start | bytes 294920 | tf_op jit(solution)/shard_map/ppermute | solution.py:321
  20.4 3.9 %collective-permute-start.24 = (bf16[2,48,512]{2,1,0:T(8,128)(2,1)}, bf16[2,48,512]{2,1,0:T(8,128)(2,1)S(1)}, u32[]{:S(2)}, u32[]{:S(2)}) collective-permute-start(bf16[2,48,512]{2,1,0:T(8,128)(2,1)} %get-tuple-element.103), channel_id=1, source_target_pairs={{0,10},{1,11},{2,8},{3,9},{4,14},{5,15},{6,12},{7,13},{8,2},{9,3},... | collective-permute-start | bytes 294920 | tf_op jit(solution)/shard_map/ppermute | solution.py:321
  24.3 3.8 %collective-permute-start.25 = (bf16[2,48,512]{2,1,0:T(8,128)(2,1)}, bf16[2,48,512]{2,1,0:T(8,128)(2,1)S(1)}, u32[]{:S(2)}, u32[]{:S(2)}) collective-permute-start(bf16[2,48,512]{2,1,0:T(8,128)(2,1)} %get-tuple-element.104), channel_id=1, source_target_pairs={{0,14},{1,15},{2,12},{3,13},{4,10},{5,11},{6,8},{7,9},{8,6},{9,7},... | collective-permute-start | bytes 294920 | tf_op jit(solution)/shard_map/ppermute | solution.py:321
  28.5 3.2 %collective-permute-start.27 = (bf16[2,48,512]{2,1,0:T(8,128)(2,1)}, bf16[2,48,512]{2,1,0:T(8,128)(2,1)S(1)}, u32[]{:S(2)}, u32[]{:S(2)}) collective-permute-start(bf16[2,48,512]{2,1,0:T(8,128)(2,1)} %get-tuple-element.106), channel_id=1, source_target_pairs={{0,11},{1,10},{2,9},{3,8},{4,15},{5,14},{6,13},{7,12},{8,3},{9,2},... | collective-permute-start | bytes 294920 | tf_op jit(solution)/shard_map/ppermute | solution.py:321
  31.7 2.8 %collective-permute-done.24.refs_9_ = bf16[2,48,512]{2,1,0:T(8,128)(2,1)S(1)} collective-permute-done((bf16[2,48,512]{2,1,0:T(8,128)(2,1)}, bf16[2,48,512]{2,1,0:T(8,128)(2,1)S(1)}, u32[]{:S(2)}, u32[]{:S(2)}) %collective-permute-start.24) | collective-permute-done | bytes 98336 | tf_op jit(solution)/shard_map/ppermute | solution.py:321
  37.5 2.8 %pack_rows.1 = (bf16[32,1792]{1,0:T(8,128)(2,1)S(1)}, bf16[32,1792]{1,0:T(8,128)(2,1)S(1)}, bf16[32,1792]{1,0:T(8,128)(2,1)S(1)}, bf16[32,1792]{1,0:T(8,128)(2,1...) custom-call(s32[1]{0:T(128)S(6)} %copy.13.live_ref, ...), custom_call_target="tpu_custom_call" | custom-call | flops 469762048 | bytes 2752512 | tf_op jit(solution)/shard_map/pack_rows/pallas_call | solution.py:107
  40.7 2.7 %collective-permute-start.2 = (bf16[32,1792]{1,0:T(8,128)(2,1)S(1)}, bf16[32,1792]{1,0:T(8,128)(2,1)S(1)}, u32[]{:S(2)}, u32[]{:S(2)}) collective-permute-start(bf16[32,1792]{1,0:T(8,128)(2,1)S(1)} %get-tuple-element.80), channel_id=1, source_target_pairs={{0,7},{1,6},{2,5},{3,4},{4,3},{5,2},{6,1},{7,0},{8,15},{9,14},{10,... | collective-permute-start | bytes 344072 | tf_op jit(solution)/shard_map/ppermute | solution.py:321
  43.4 5.0 %collective-permute-start.3 = (bf16[32,1792]{1,0:T(8,128)(2,1)S(1)}, bf16[32,1792]{1,0:T(8,128)(2,1)S(1)}, u32[]{:S(2)}, u32[]{:S(2)}) collective-permute-start(bf16[32,1792]{1,0:T(8,128)(2,1)S(1)} %get-tuple-element.81), channel_id=1, source_target_pairs={{0,12},{1,13},{2,14},{3,15},{4,8},{5,9},{6,10},{7,11},{8,4},{9,5},... | collective-permute-start | bytes 344072 | tf_op jit(solution)/shard_map/ppermute | solution.py:321
  50.5 5.6 %collective-permute-start.7 = (bf16[32,1792]{1,0:T(8,128)(2,1)S(1)}, bf16[32,1792]{1,0:T(8,128)(2,1)S(1)}, u32[]{:S(2)}, u32[]{:S(2)}) collective-permute-start(bf16[32,1792]{1,0:T(8,128)(2,1)S(1)} %get-tuple-element.85), channel_id=1, source_target_pairs={{0,13},{1,12},{2,15},{3,14},{4,9},{5,8},{6,11},{7,10},{8,5},{9,4},... | collective-permute-start | bytes 344072 | tf_op jit(solution)/shard_map/ppermute | solution.py:321
  56.1 4.4 %collective-permute-start.9 = (bf16[32,1792]{1,0:T(8,128)(2,1)S(1)}, bf16[32,1792]{1,0:T(8,128)(2,1)S(1)}, u32[]{:S(2)}, u32[]{:S(2)}) collective-permute-start(bf16[32,1792]{1,0:T(8,128)(2,1)S(1)} %get-tuple-element.87), channel_id=1, source_target_pairs={{0,10},{1,11},{2,8},{3,9},{4,14},{5,15},{6,12},{7,13},{8,2},{9,3},... | collective-permute-start | bytes 344072 | tf_op jit(solution)/shard_map/ppermute | solution.py:321
  60.5 3.8 %collective-permute-start.11 = (bf16[32,1792]{1,0:T(8,128)(2,1)S(1)}, bf16[32,1792]{1,0:T(8,128)(2,1)S(1)}, u32[]{:S(2)}, u32[]{:S(2)}) collective-permute-start(bf16[32,1792]{1,0:T(8,128)(2,1)S(1)} %get-tuple-element.89), channel_id=1, source_target_pairs={{0,14},{1,15},{2,12},{3,13},{4,10},{5,11},{6,8},{7,9},{8,6},{9,7},... | collective-permute-start | bytes 344072 | tf_op jit(solution)/shard_map/ppermute | solution.py:321
  64.6 4.3 %collective-permute-start.13 = (bf16[32,1792]{1,0:T(8,128)(2,1)S(1)}, bf16[32,1792]{1,0:T(8,128)(2,1)S(1)}, u32[]{:S(2)}, u32[]{:S(2)}) collective-permute-start(bf16[32,1792]{1,0:T(8,128)(2,1)S(1)} %get-tuple-element.91), channel_id=1, source_target_pairs={{0,11},{1,10},{2,9},{3,8},{4,15},{5,14},{6,13},{7,12},{8,3},{9,2},... | collective-permute-start | bytes 344072 | tf_op jit(solution)/shard_map/ppermute | solution.py:321
  69.0 2.2 %collective-permute-start.14 = (bf16[32,1792]{1,0:T(8,128)(2,1)S(1)}, bf16[32,1792]{1,0:T(8,128)(2,1)S(1)}, u32[]{:S(2)}, u32[]{:S(2)}) collective-permute-start(bf16[32,1792]{1,0:T(8,128)(2,1)S(1)} %get-tuple-element.92), channel_id=1, source_target_pairs={{0,4},{1,5},{2,6},{3,7},{4,0},{5,1},{6,2},{7,3},{8,12},{9,13},{10,... | collective-permute-start | bytes 344072 | tf_op jit(solution)/shard_map/ppermute | solution.py:321
  71.1 4.6 %collective-permute-start.15 = (bf16[32,1792]{1,0:T(8,128)(2,1)S(1)}, bf16[32,1792]{1,0:T(8,128)(2,1)S(1)}, u32[]{:S(2)}, u32[]{:S(2)}) collective-permute-start(bf16[32,1792]{1,0:T(8,128)(2,1)S(1)} %get-tuple-element.93), channel_id=1, source_target_pairs={{0,15},{1,14},{2,13},{3,12},{4,11},{5,10},{6,9},{7,8},{8,7},{9,6},... | collective-permute-start | bytes 344072 | tf_op jit(solution)/shard_map/ppermute | solution.py:321
  76.5 3.8 %collective-permute-start.40 = (bf16[48,512]{1,0:T(8,128)(2,1)S(1)}, bf16[48,512]{1,0:T(8,128)(2,1)S(1)}, u32[]{:S(2)}, u32[]{:S(2)}) collective-permute-start(bf16[48,512]{1,0:T(8,128)(2,1)S(1)} %get-tuple-element.120), channel_id=1, source_target_pairs={{0,14},{1,15},{2,12},{3,13},{4,10},{5,11},{6,8},{7,9},{8,6},{9,7},... | collective-permute-start | bytes 147464 | tf_op jit(solution)/shard_map/ppermute | solution.py:321
  80.8 4.4 %collective-permute-start.43 = (bf16[48,512]{1,0:T(8,128)(2,1)S(1)}, bf16[48,512]{1,0:T(8,128)(2,1)S(1)}, u32[]{:S(2)}, u32[]{:S(2)}) collective-permute-start(bf16[48,512]{1,0:T(8,128)(2,1)S(1)} %get-tuple-element.123), channel_id=1, source_target_pairs={{0,4},{1,5},{2,6},{3,7},{4,0},{5,1},{6,2},{7,3},{8,12},{9,13},{10,... | collective-permute-start | bytes 147464 | tf_op jit(solution)/shard_map/ppermute | solution.py:321
  85.6 3.3 %collective-permute-start.30 = (bf16[2,48,512]{2,1,0:T(8,128)(2,1)S(1)}, bf16[2,48,512]{2,1,0:T(8,128)(2,1)S(1)}, u32[]{:S(2)}, u32[]{:S(2)}) collective-permute-start(bf16[2,48,512]{2,1,0:T(8,128)(2,1)S(1)} %get-tuple-element.110), channel_id=1, source_target_pairs={{0,8},{1,9},{2,10},{3,11},{4,12},{5,13},{6,14},{7,15},{8,0},{9,1},... | collective-permute-start | bytes 294920 | tf_op jit(solution)/shard_map/ppermute | solution.py:321
  93.5 2.9 %collective-permute-done.30.refs_17_ = bf16[2,48,512]{2,1,0:T(8,128)(2,1)S(1)} collective-permute-done((bf16[2,48,512]{2,1,0:T(8,128)(2,1)S(1)}, bf16[2,48,512]{2,1,0:T(8,128)(2,1)S(1)}, u32[]{:S(2)}, u32[]{:S(2)}) %collective-permute-start.30) | collective-permute-done | bytes 98336 | tf_op jit(solution)/shard_map/ppermute | solution.py:321
  98.4 5.2 %collective-permute-start.37 = (bf16[2,48,512]{2,1,0:T(8,128)(2,1)S(1)}, bf16[2,48,512]{2,1,0:T(8,128)(2,1)S(1)}, u32[]{:S(2)}, u32[]{:S(2)}) collective-permute-start(bf16[2,48,512]{2,1,0:T(8,128)(2,1)S(1)} %get-tuple-element.117), channel_id=1, source_target_pairs={{0,2},{1,3},{2,0},{3,1},{4,6},{5,7},{6,4},{7,5},{8,10},{9,11},{10,... | collective-permute-start | bytes 294920 | tf_op jit(solution)/shard_map/ppermute | solution.py:321
  106.9 2.8 %collective-permute-start.45 = (bf16[48,512]{1,0:T(8,128)(2,1)S(1)}, bf16[48,512]{1,0:T(8,128)(2,1)S(1)}, u32[]{:S(2)}, u32[]{:S(2)}) collective-permute-start(bf16[48,512]{1,0:T(8,128)(2,1)S(1)} %get-tuple-element.126), channel_id=1, source_target_pairs={{0,14},{1,15},{2,12},{3,13},{4,10},{5,11},{6,8},{7,9},{8,6},{9,7},... | collective-permute-start | bytes 147464 | tf_op jit(solution)/shard_map/ppermute | solution.py:321
  109.7 3.4 %collective-permute-start.47 = (bf16[48,512]{1,0:T(8,128)(2,1)S(1)}, bf16[48,512]{1,0:T(8,128)(2,1)S(1)}, u32[]{:S(2)}, u32[]{:S(2)}) collective-permute-start(bf16[48,512]{1,0:T(8,128)(2,1)S(1)} %get-tuple-element.128), channel_id=1, source_target_pairs={{0,11},{1,10},{2,9},{3,8},{4,15},{5,14},{6,13},{7,12},{8,3},{9,2},... | collective-permute-start | bytes 147464 | tf_op jit(solution)/shard_map/ppermute | solution.py:321
  114.7 3.7 %orthogonal.1 = (bf16[384,1024]{1,0:T(8,128)(2,1)}, bf16[384,1024]{1,0:T(8,128)(2,1)S(1)}) custom-call(s32[1]{0:T(128)} %bitcast.me_ref, bf16[32,1792]{1,0:T(8,128)(2,1)S(1)} %get-tuple-element.78.refs_0_, bf16[32,1792]{1,0:T(8,128)(2,1)S(1)} %collective-permute-done.1.refs_1_, bf16[32,1792]{1,0:T(8,128)(2,1)S(1)} %collective-permute-done.2.refs_2_, ...), custom_call_target="tpu_custom_call" | custom-call | flops 1837105152 | bytes 3801088 | tf_op jit(solution)/shard_map/orthogonal/pallas_call | solution.py:223
  118.5 2.1 %collective-permute-done.49.refs_31_ = bf16[48,512]{1,0:T(8,128)(2,1)S(1)} collective-permute-done((bf16[48,512]{1,0:T(8,128)(2,1)S(1)}, bf16[48,512]{1,0:T(8,128)(2,1)S(1)}, u32[]{:S(2)}, u32[]{:S(2)}) %collective-permute-start.49) | collective-permute-done | bytes 49184 | tf_op jit(solution)/shard_map/ppermute | solution.py:321
  124.2 2.2 %collective-permute-start.52 = (bf16[32,1024]{1,0:T(8,128)(2,1)S(1)}, bf16[32,1024]{1,0:T(8,128)(2,1)S(1)}, u32[]{:S(2)}, u32[]{:S(2)}) collective-permute-start(bf16[32,1024]{1,0:T(8,128)(2,1)S(1)} %get-tuple-element.138), channel_id=1, source_target_pairs={{0,12},{1,13},{2,14},{3,15},{4,8},{5,9},{6,10},{7,11},{8,4},{9,5},... | collective-permute-start | bytes 196616 | tf_op jit(solution)/shard_map/ppermute | solution.py:321
  130.4 2.6 %collective-permute-start.56 = (bf16[32,1024]{1,0:T(8,128)(2,1)S(1)}, bf16[32,1024]{1,0:T(8,128)(2,1)S(1)}, u32[]{:S(2)}, u32[]{:S(2)}) collective-permute-start(bf16[32,1024]{1,0:T(8,128)(2,1)S(1)} %get-tuple-element.142), channel_id=1, source_target_pairs={{0,13},{1,12},{2,15},{3,14},{4,9},{5,8},{6,11},{7,10},{8,5},{9,4},... | collective-permute-start | bytes 196616 | tf_op jit(solution)/shard_map/ppermute | solution.py:321
  133.4 2.1 %collective-permute-start.58 = (bf16[32,1024]{1,0:T(8,128)(2,1)S(1)}, bf16[32,1024]{1,0:T(8,128)(2,1)S(1)}, u32[]{:S(2)}, u32[]{:S(2)}) collective-permute-start(bf16[32,1024]{1,0:T(8,128)(2,1)S(1)} %get-tuple-element.144), channel_id=1, source_target_pairs={{0,10},{1,11},{2,8},{3,9},{4,14},{5,15},{6,12},{7,13},{8,2},{9,3},... | collective-permute-start | bytes 196616 | tf_op jit(solution)/shard_map/ppermute | solution.py:321
  136.0 2.6 %collective-permute-start.60 = (bf16[32,1024]{1,0:T(8,128)(2,1)S(1)}, bf16[32,1024]{1,0:T(8,128)(2,1)S(1)}, u32[]{:S(2)}, u32[]{:S(2)}) collective-permute-start(bf16[32,1024]{1,0:T(8,128)(2,1)S(1)} %get-tuple-element.146), channel_id=1, source_target_pairs={{0,14},{1,15},{2,12},{3,13},{4,10},{5,11},{6,8},{7,9},{8,6},{9,7},... | collective-permute-start | bytes 196616 | tf_op jit(solution)/shard_map/ppermute | solution.py:321
  143.7 3.0 %collective-permute-done.62.refs_13_ = bf16[32,1024]{1,0:T(8,128)(2,1)S(1)} collective-permute-done((bf16[32,1024]{1,0:T(8,128)(2,1)S(1)}, bf16[32,1024]{1,0:T(8,128)(2,1)S(1)}, u32[]{:S(2)}, u32[]{:S(2)}) %collective-permute-start.62) | collective-permute-done | bytes 65568 | tf_op jit(solution)/shard_map/ppermute | solution.py:321
  (120 shorter events, 42.6 us)
Async XLA Ops:
  11.3 13.0 %collective-permute-start.20 = (bf16[2,48,512]{2,1,0:T(8,128)(2,1)}, bf16[2,48,512]{2,1,0:T(8,128)(2,1)S(1)}, u32[]{:S(2)}, u32[]{:S(2)}) collective-permute-start(bf16[2,48,512]{2,1,0:T(8,128)(2,1)} %get-tuple-element.99), channel_id=1, source_target_pairs={{0,9},{1,8},{2,11},{3,10},{4,13},{5,12},{6,15},{7,14},{8,1},{9,0},... | collective-permute-start | bytes 294920 | tf_op jit(solution)/shard_map/ppermute | solution.py:321
  14.5 13.6 %collective-permute-start.21 = (bf16[2,48,512]{2,1,0:T(8,128)(2,1)}, bf16[2,48,512]{2,1,0:T(8,128)(2,1)S(1)}, u32[]{:S(2)}, u32[]{:S(2)}) collective-permute-start(bf16[2,48,512]{2,1,0:T(8,128)(2,1)} %get-tuple-element.100), channel_id=1, source_target_pairs={{0,6},{1,7},{2,4},{3,5},{4,2},{5,3},{6,0},{7,1},{8,14},{9,15},{10,... | collective-permute-start | bytes 294920 | tf_op jit(solution)/shard_map/ppermute | solution.py:321
  16.1 12.3 %collective-permute-start.22 = (bf16[2,48,512]{2,1,0:T(8,128)(2,1)}, bf16[2,48,512]{2,1,0:T(8,128)(2,1)S(1)}, u32[]{:S(2)}, u32[]{:S(2)}) collective-permute-start(bf16[2,48,512]{2,1,0:T(8,128)(2,1)} %get-tuple-element.101), channel_id=1, source_target_pairs={{0,13},{1,12},{2,15},{3,14},{4,9},{5,8},{6,11},{7,10},{8,5},{9,4},... | collective-permute-start | bytes 294920 | tf_op jit(solution)/shard_map/ppermute | solution.py:321
  18.9 12.7 %collective-permute-start.23 = (bf16[2,48,512]{2,1,0:T(8,128)(2,1)}, bf16[2,48,512]{2,1,0:T(8,128)(2,1)S(1)}, u32[]{:S(2)}, u32[]{:S(2)}) collective-permute-start(bf16[2,48,512]{2,1,0:T(8,128)(2,1)} %get-tuple-element.102), channel_id=1, source_target_pairs={{0,2},{1,3},{2,0},{3,1},{4,6},{5,7},{6,4},{7,5},{8,10},{9,11},{10,... | collective-permute-start | bytes 294920 | tf_op jit(solution)/shard_map/ppermute | solution.py:321
  20.4 14.1 %collective-permute-start.24 = (bf16[2,48,512]{2,1,0:T(8,128)(2,1)}, bf16[2,48,512]{2,1,0:T(8,128)(2,1)S(1)}, u32[]{:S(2)}, u32[]{:S(2)}) collective-permute-start(bf16[2,48,512]{2,1,0:T(8,128)(2,1)} %get-tuple-element.103), channel_id=1, source_target_pairs={{0,10},{1,11},{2,8},{3,9},{4,14},{5,15},{6,12},{7,13},{8,2},{9,3},... | collective-permute-start | bytes 294920 | tf_op jit(solution)/shard_map/ppermute | solution.py:321
  24.3 16.0 %collective-permute-start.25 = (bf16[2,48,512]{2,1,0:T(8,128)(2,1)}, bf16[2,48,512]{2,1,0:T(8,128)(2,1)S(1)}, u32[]{:S(2)}, u32[]{:S(2)}) collective-permute-start(bf16[2,48,512]{2,1,0:T(8,128)(2,1)} %get-tuple-element.104), channel_id=1, source_target_pairs={{0,14},{1,15},{2,12},{3,13},{4,10},{5,11},{6,8},{7,9},{8,6},{9,7},... | collective-permute-start | bytes 294920 | tf_op jit(solution)/shard_map/ppermute | solution.py:321
  28.1 12.6 %collective-permute-start.26 = (bf16[2,48,512]{2,1,0:T(8,128)(2,1)}, bf16[2,48,512]{2,1,0:T(8,128)(2,1)S(1)}, u32[]{:S(2)}, u32[]{:S(2)}) collective-permute-start(bf16[2,48,512]{2,1,0:T(8,128)(2,1)} %get-tuple-element.105), channel_id=1, source_target_pairs={{0,1},{1,0},{2,3},{3,2},{4,5},{5,4},{6,7},{7,6},{8,9},{9,8},{10,11... | collective-permute-start | bytes 294920 | tf_op jit(solution)/shard_map/ppermute | solution.py:321
  28.5 14.9 %collective-permute-start.27 = (bf16[2,48,512]{2,1,0:T(8,128)(2,1)}, bf16[2,48,512]{2,1,0:T(8,128)(2,1)S(1)}, u32[]{:S(2)}, u32[]{:S(2)}) collective-permute-start(bf16[2,48,512]{2,1,0:T(8,128)(2,1)} %get-tuple-element.106), channel_id=1, source_target_pairs={{0,11},{1,10},{2,9},{3,8},{4,15},{5,14},{6,13},{7,12},{8,3},{9,2},... | collective-permute-start | bytes 294920 | tf_op jit(solution)/shard_map/ppermute | solution.py:321
  31.7 16.8 %collective-permute-start.28 = (bf16[2,48,512]{2,1,0:T(8,128)(2,1)}, bf16[2,48,512]{2,1,0:T(8,128)(2,1)S(1)}, u32[]{:S(2)}, u32[]{:S(2)}) collective-permute-start(bf16[2,48,512]{2,1,0:T(8,128)(2,1)} %get-tuple-element.107), channel_id=1, source_target_pairs={{0,4},{1,5},{2,6},{3,7},{4,0},{5,1},{6,2},{7,3},{8,12},{9,13},{10,... | collective-permute-start | bytes 294920 | tf_op jit(solution)/shard_map/ppermute | solution.py:321
  34.4 14.0 %collective-permute-start.29 = (bf16[2,48,512]{2,1,0:T(8,128)(2,1)}, bf16[2,48,512]{2,1,0:T(8,128)(2,1)S(1)}, u32[]{:S(2)}, u32[]{:S(2)}) collective-permute-start(bf16[2,48,512]{2,1,0:T(8,128)(2,1)} %get-tuple-element.108), channel_id=1, source_target_pairs={{0,15},{1,14},{2,13},{3,12},{4,11},{5,10},{6,9},{7,8},{8,7},{9,6},... | collective-permute-start | bytes 294920 | tf_op jit(solution)/shard_map/ppermute | solution.py:321
  40.7 9.8 %collective-permute-start.2 = (bf16[32,1792]{1,0:T(8,128)(2,1)S(1)}, bf16[32,1792]{1,0:T(8,128)(2,1)S(1)}, u32[]{:S(2)}, u32[]{:S(2)}) collective-permute-start(bf16[32,1792]{1,0:T(8,128)(2,1)S(1)} %get-tuple-element.80), channel_id=1, source_target_pairs={{0,7},{1,6},{2,5},{3,4},{4,3},{5,2},{6,1},{7,0},{8,15},{9,14},{10,... | collective-permute-start | bytes 344072 | tf_op jit(solution)/shard_map/ppermute | solution.py:321
  43.4 12.7 %collective-permute-start.3 = (bf16[32,1792]{1,0:T(8,128)(2,1)S(1)}, bf16[32,1792]{1,0:T(8,128)(2,1)S(1)}, u32[]{:S(2)}, u32[]{:S(2)}) collective-permute-start(bf16[32,1792]{1,0:T(8,128)(2,1)S(1)} %get-tuple-element.81), channel_id=1, source_target_pairs={{0,12},{1,13},{2,14},{3,15},{4,8},{5,9},{6,10},{7,11},{8,4},{9,5},... | collective-permute-start | bytes 344072 | tf_op jit(solution)/shard_map/ppermute | solution.py:321
  48.4 12.1 %collective-permute-start.5 = (bf16[32,1792]{1,0:T(8,128)(2,1)S(1)}, bf16[32,1792]{1,0:T(8,128)(2,1)S(1)}, u32[]{:S(2)}, u32[]{:S(2)}) collective-permute-start(bf16[32,1792]{1,0:T(8,128)(2,1)S(1)} %get-tuple-element.83), channel_id=1, source_target_pairs={{0,9},{1,8},{2,11},{3,10},{4,13},{5,12},{6,15},{7,14},{8,1},{9,0},... | collective-permute-start | bytes 344072 | tf_op jit(solution)/shard_map/ppermute | solution.py:321
  49.0 11.5 %collective-permute-start.6 = (bf16[32,1792]{1,0:T(8,128)(2,1)S(1)}, bf16[32,1792]{1,0:T(8,128)(2,1)S(1)}, u32[]{:S(2)}, u32[]{:S(2)}) collective-permute-start(bf16[32,1792]{1,0:T(8,128)(2,1)S(1)} %get-tuple-element.84), channel_id=1, source_target_pairs={{0,6},{1,7},{2,4},{3,5},{4,2},{5,3},{6,0},{7,1},{8,14},{9,15},{10,... | collective-permute-start | bytes 344072 | tf_op jit(solution)/shard_map/ppermute | solution.py:321
  50.5 13.8 %collective-permute-start.7 = (bf16[32,1792]{1,0:T(8,128)(2,1)S(1)}, bf16[32,1792]{1,0:T(8,128)(2,1)S(1)}, u32[]{:S(2)}, u32[]{:S(2)}) collective-permute-start(bf16[32,1792]{1,0:T(8,128)(2,1)S(1)} %get-tuple-element.85), channel_id=1, source_target_pairs={{0,13},{1,12},{2,15},{3,14},{4,9},{5,8},{6,11},{7,10},{8,5},{9,4},... | collective-permute-start | bytes 344072 | tf_op jit(solution)/shard_map/ppermute | solution.py:321
  56.1 12.9 %collective-permute-start.9 = (bf16[32,1792]{1,0:T(8,128)(2,1)S(1)}, bf16[32,1792]{1,0:T(8,128)(2,1)S(1)}, u32[]{:S(2)}, u32[]{:S(2)}) collective-permute-start(bf16[32,1792]{1,0:T(8,128)(2,1)S(1)} %get-tuple-element.87), channel_id=1, source_target_pairs={{0,10},{1,11},{2,8},{3,9},{4,14},{5,15},{6,12},{7,13},{8,2},{9,3},... | collective-permute-start | bytes 344072 | tf_op jit(solution)/shard_map/ppermute | solution.py:321
  60.5 10.6 %collective-permute-start.10 = (bf16[32,1792]{1,0:T(8,128)(2,1)S(1)}, bf16[32,1792]{1,0:T(8,128)(2,1)S(1)}, u32[]{:S(2)}, u32[]{:S(2)}) collective-permute-start(bf16[32,1792]{1,0:T(8,128)(2,1)S(1)} %get-tuple-element.88), channel_id=1, source_target_pairs={{0,5},{1,4},{2,7},{3,6},{4,1},{5,0},{6,3},{7,2},{8,13},{9,12},{10,... | collective-permute-start | bytes 344072 | tf_op jit(solution)/shard_map/ppermute | solution.py:321
  60.5 16.0 %collective-permute-start.11 = (bf16[32,1792]{1,0:T(8,128)(2,1)S(1)}, bf16[32,1792]{1,0:T(8,128)(2,1)S(1)}, u32[]{:S(2)}, u32[]{:S(2)}) collective-permute-start(bf16[32,1792]{1,0:T(8,128)(2,1)S(1)} %get-tuple-element.89), channel_id=1, source_target_pairs={{0,14},{1,15},{2,12},{3,13},{4,10},{5,11},{6,8},{7,9},{8,6},{9,7},... | collective-permute-start | bytes 344072 | tf_op jit(solution)/shard_map/ppermute | solution.py:321
  64.3 16.0 %collective-permute-start.12 = (bf16[32,1792]{1,0:T(8,128)(2,1)S(1)}, bf16[32,1792]{1,0:T(8,128)(2,1)S(1)}, u32[]{:S(2)}, u32[]{:S(2)}) collective-permute-start(bf16[32,1792]{1,0:T(8,128)(2,1)S(1)} %get-tuple-element.90), channel_id=1, source_target_pairs={{0,1},{1,0},{2,3},{3,2},{4,5},{5,4},{6,7},{7,6},{8,9},{9,8},{10,11... | collective-permute-start | bytes 344072 | tf_op jit(solution)/shard_map/ppermute | solution.py:321
  64.6 16.2 %collective-permute-start.13 = (bf16[32,1792]{1,0:T(8,128)(2,1)S(1)}, bf16[32,1792]{1,0:T(8,128)(2,1)S(1)}, u32[]{:S(2)}, u32[]{:S(2)}) collective-permute-start(bf16[32,1792]{1,0:T(8,128)(2,1)S(1)} %get-tuple-element.91), channel_id=1, source_target_pairs={{0,11},{1,10},{2,9},{3,8},{4,15},{5,14},{6,13},{7,12},{8,3},{9,2},... | collective-permute-start | bytes 344072 | tf_op jit(solution)/shard_map/ppermute | solution.py:321
  69.0 11.9 %collective-permute-start.14 = (bf16[32,1792]{1,0:T(8,128)(2,1)S(1)}, bf16[32,1792]{1,0:T(8,128)(2,1)S(1)}, u32[]{:S(2)}, u32[]{:S(2)}) collective-permute-start(bf16[32,1792]{1,0:T(8,128)(2,1)S(1)} %get-tuple-element.92), channel_id=1, source_target_pairs={{0,4},{1,5},{2,6},{3,7},{4,0},{5,1},{6,2},{7,3},{8,12},{9,13},{10,... | collective-permute-start | bytes 344072 | tf_op jit(solution)/shard_map/ppermute | solution.py:321
  71.1 14.1 %collective-permute-start.15 = (bf16[32,1792]{1,0:T(8,128)(2,1)S(1)}, bf16[32,1792]{1,0:T(8,128)(2,1)S(1)}, u32[]{:S(2)}, u32[]{:S(2)}) collective-permute-start(bf16[32,1792]{1,0:T(8,128)(2,1)S(1)} %get-tuple-element.93), channel_id=1, source_target_pairs={{0,15},{1,14},{2,13},{3,12},{4,11},{5,10},{6,9},{7,8},{8,7},{9,6},... | collective-permute-start | bytes 344072 | tf_op jit(solution)/shard_map/ppermute | solution.py:321
  80.8 9.3 %collective-permute-start.42 = (bf16[48,512]{1,0:T(8,128)(2,1)S(1)}, bf16[48,512]{1,0:T(8,128)(2,1)S(1)}, u32[]{:S(2)}, u32[]{:S(2)}) collective-permute-start(bf16[48,512]{1,0:T(8,128)(2,1)S(1)} %get-tuple-element.122), channel_id=1, source_target_pairs={{0,11},{1,10},{2,9},{3,8},{4,15},{5,14},{6,13},{7,12},{8,3},{9,2},... | collective-permute-start | bytes 147464 | tf_op jit(solution)/shard_map/ppermute | solution.py:321
  80.8 10.9 %collective-permute-start.43 = (bf16[48,512]{1,0:T(8,128)(2,1)S(1)}, bf16[48,512]{1,0:T(8,128)(2,1)S(1)}, u32[]{:S(2)}, u32[]{:S(2)}) collective-permute-start(bf16[48,512]{1,0:T(8,128)(2,1)S(1)} %get-tuple-element.123), channel_id=1, source_target_pairs={{0,4},{1,5},{2,6},{3,7},{4,0},{5,1},{6,2},{7,3},{8,12},{9,13},{10,... | collective-permute-start | bytes 147464 | tf_op jit(solution)/shard_map/ppermute | solution.py:321
  85.6 10.8 %collective-permute-start.30 = (bf16[2,48,512]{2,1,0:T(8,128)(2,1)S(1)}, bf16[2,48,512]{2,1,0:T(8,128)(2,1)S(1)}, u32[]{:S(2)}, u32[]{:S(2)}) collective-permute-start(bf16[2,48,512]{2,1,0:T(8,128)(2,1)S(1)} %get-tuple-element.110), channel_id=1, source_target_pairs={{0,8},{1,9},{2,10},{3,11},{4,12},{5,13},{6,14},{7,15},{8,0},{9,1},... | collective-permute-start | bytes 294920 | tf_op jit(solution)/shard_map/ppermute | solution.py:321
  91.7 11.9 %collective-permute-start.33 = (bf16[2,48,512]{2,1,0:T(8,128)(2,1)S(1)}, bf16[2,48,512]{2,1,0:T(8,128)(2,1)S(1)}, u32[]{:S(2)}, u32[]{:S(2)}) collective-permute-start(bf16[2,48,512]{2,1,0:T(8,128)(2,1)S(1)} %get-tuple-element.113), channel_id=1, source_target_pairs={{0,3},{1,2},{2,1},{3,0},{4,7},{5,6},{6,5},{7,4},{8,11},{9,10},{10,... | collective-permute-start | bytes 294920 | tf_op jit(solution)/shard_map/ppermute | solution.py:321
  92.5 13.0 %collective-permute-start.34 = (bf16[2,48,512]{2,1,0:T(8,128)(2,1)S(1)}, bf16[2,48,512]{2,1,0:T(8,128)(2,1)S(1)}, u32[]{:S(2)}, u32[]{:S(2)}) collective-permute-start(bf16[2,48,512]{2,1,0:T(8,128)(2,1)S(1)} %get-tuple-element.114), channel_id=1, source_target_pairs={{0,9},{1,8},{2,11},{3,10},{4,13},{5,12},{6,15},{7,14},{8,1},{9,0},... | collective-permute-start | bytes 294920 | tf_op jit(solution)/shard_map/ppermute | solution.py:321
  96.3 10.5 %collective-permute-start.35 = (bf16[2,48,512]{2,1,0:T(8,128)(2,1)S(1)}, bf16[2,48,512]{2,1,0:T(8,128)(2,1)S(1)}, u32[]{:S(2)}, u32[]{:S(2)}) collective-permute-start(bf16[2,48,512]{2,1,0:T(8,128)(2,1)S(1)} %get-tuple-element.115), channel_id=1, source_target_pairs={{0,6},{1,7},{2,4},{3,5},{4,2},{5,3},{6,0},{7,1},{8,14},{9,15},{10,... | collective-permute-start | bytes 294920 | tf_op jit(solution)/shard_map/ppermute | solution.py:321
  96.3 13.3 %collective-permute-start.36 = (bf16[2,48,512]{2,1,0:T(8,128)(2,1)S(1)}, bf16[2,48,512]{2,1,0:T(8,128)(2,1)S(1)}, u32[]{:S(2)}, u32[]{:S(2)}) collective-permute-start(bf16[2,48,512]{2,1,0:T(8,128)(2,1)S(1)} %get-tuple-element.116), channel_id=1, source_target_pairs={{0,13},{1,12},{2,15},{3,14},{4,9},{5,8},{6,11},{7,10},{8,5},{9,4},... | collective-permute-start | bytes 294920 | tf_op jit(solution)/shard_map/ppermute | solution.py:321
  98.4 11.2 %collective-permute-start.37 = (bf16[2,48,512]{2,1,0:T(8,128)(2,1)S(1)}, bf16[2,48,512]{2,1,0:T(8,128)(2,1)S(1)}, u32[]{:S(2)}, u32[]{:S(2)}) collective-permute-start(bf16[2,48,512]{2,1,0:T(8,128)(2,1)S(1)} %get-tuple-element.117), channel_id=1, source_target_pairs={{0,2},{1,3},{2,0},{3,1},{4,6},{5,7},{6,4},{7,5},{8,10},{9,11},{10,... | collective-permute-start | bytes 294920 | tf_op jit(solution)/shard_map/ppermute | solution.py:321
  103.6 10.5 %collective-permute-start.38 = (bf16[2,48,512]{2,1,0:T(8,128)(2,1)S(1)}, bf16[2,48,512]{2,1,0:T(8,128)(2,1)S(1)}, u32[]{:S(2)}, u32[]{:S(2)}) collective-permute-start(bf16[2,48,512]{2,1,0:T(8,128)(2,1)S(1)} %get-tuple-element.118), channel_id=1, source_target_pairs={{0,10},{1,11},{2,8},{3,9},{4,14},{5,15},{6,12},{7,13},{8,2},{9,3},... | collective-permute-start | bytes 294920 | tf_op jit(solution)/shard_map/ppermute | solution.py:321
  106.9 11.6 %collective-permute-start.45 = (bf16[48,512]{1,0:T(8,128)(2,1)S(1)}, bf16[48,512]{1,0:T(8,128)(2,1)S(1)}, u32[]{:S(2)}, u32[]{:S(2)}) collective-permute-start(bf16[48,512]{1,0:T(8,128)(2,1)S(1)} %get-tuple-element.126), channel_id=1, source_target_pairs={{0,14},{1,15},{2,12},{3,13},{4,10},{5,11},{6,8},{7,9},{8,6},{9,7},... | collective-permute-start | bytes 147464 | tf_op jit(solution)/shard_map/ppermute | solution.py:321
  (41 other events, 432.8 us)

commit v14 on v10

--- a/solution.py
+++ b/solution.py
@@ -171,8 +171,8 @@
 
 def update_kernel(groups, me_ref, *refs):
     packed, pieces, produced = refs[:groups], refs[groups : 2 * groups], refs[2 * groups + 2 : 3 * groups + 2]
-    weight_new_ref, moment_new_ref = refs[2 * groups : 2 * groups + 2]
-    held, rows_ref = refs[-2:]
+    results = refs[2 * groups : 2 * groups + 2]
+    held, rows_ref, sem = refs[-3:]
     _, ff, d = held.shape
     capacity = packed[0].shape[0]
     for n, piece in enumerate(packed):
@@ -185,7 +185,9 @@
         rows_ref[:, :ff], rows_ref[:, ff : ff + d], (((0,), (0,)), ((), ())), preferred_element_type=F32
     )
     moment_new = (moment_decay * held[0].astype(F32) + grad).astype(BF16)
-    moment_new_ref[...] = moment_new
+    held[0] = moment_new
+    leaving = [pltpu.make_async_copy(held.at[lead], results[lead], sem.at[lead]) for lead in range(2)]
+    leaving[0].start()
     moment_f = moment_new.astype(F32)
     frobenius = jnp.sqrt(jnp.sum(moment_f * moment_f))
     current = (moment_f / (frobenius + norm_floor)).astype(BF16)
@@ -199,10 +201,13 @@
             linear_term * current.astype(F32) + jnp.dot(poly, current, preferred_element_type=F32)
         ).astype(BF16)
     weight_new = (held[1].astype(F32) - step_scale * current.astype(F32)).astype(BF16)
-    weight_new_ref[...] = weight_new
+    held[1] = weight_new
+    leaving[1].start()
     product = jnp.dot(rows_ref[:, ff + d :], weight_new, preferred_element_type=F32).astype(BF16)
     for n, piece in enumerate(produced):
         piece[...] = product[n * capacity : (n + 1) * capacity]
+    for copy in leaving:
+        copy.wait()
 
 
 def update(me, packed, pieces, ff, d):
@@ -210,12 +215,16 @@
     capacity, width = packed[0].shape
     slots = groups * capacity
     shape = jax.ShapeDtypeStruct((ff, d), BF16)
-    weight_new, moment_new, *produced = pl.pallas_call(
+    moment_new, weight_new, *produced = pl.pallas_call(
         functools.partial(update_kernel, groups),
         out_shape=(shape, shape) + (jax.ShapeDtypeStruct((capacity, d), BF16),) * groups,
         in_specs=[SMEM] + [VMEM] * (2 * groups),
-        out_specs=(VMEM,) * (groups + 2),
-        scratch_shapes=[pltpu.VMEM((2, ff, d), BF16), pltpu.VMEM((slots, width), BF16)],
+        out_specs=(HBM, HBM) + (VMEM,) * groups,
+        scratch_shapes=[
+            pltpu.VMEM((2, ff, d), BF16),
+            pltpu.VMEM((slots, width), BF16),
+            pltpu.SemaphoreType.DMA((2,)),
+        ],
         compiler_params=pltpu.CompilerParams(vmem_limit_bytes=40 * MIB),
         cost_estimate=pl.CostEstimate(
             flops=4 * ff * d * slots + 8 * ff * ff * d + 4 * ff**3,
@@ -228,15 +237,22 @@
 
 
 def finish_kernel(groups, slot_ref, gates_ref, *refs):
-    pieces, (out_ref, returned_ref) = refs[:groups], refs[groups:]
+    pieces, (out_ref, returned_ref, held, sem) = refs[:groups], refs[groups:]
     capacity = pieces[0].shape[0]
     for s, piece in zip(mixed_order(groups), pieces):
         returned_ref[s * capacity : (s + 1) * capacity] = piece[...]
     selector = selector_of(slot_ref[...], groups * capacity)
-    expert_out = lax.dot_general(
-        selector, returned_ref[...], (((0,), (0,)), ((), ())), preferred_element_type=F32
-    )
-    out_ref[...] = (gates_ref[...] * expert_out).astype(BF16)
+    leaving = []
+    for n in range(2):
+        columns = slice(n * held.shape[1] // 2, (n + 1) * held.shape[1] // 2)
+        expert_out = lax.dot_general(
+            selector, returned_ref[:, columns], (((0,), (0,)), ((), ())), preferred_element_type=F32
+        )
+        held[:, columns] = (gates_ref[...] * expert_out).astype(BF16)
+        leaving.append(pltpu.make_async_copy(held.at[:, columns], out_ref.at[:, columns], sem.at[n]))
+        leaving[n].start()
+    for copy in leaving:
+        copy.wait()
 
 
 def finish(slot, gates, returned):
@@ -248,8 +264,12 @@
         functools.partial(finish_kernel, groups),
         out_shape=jax.ShapeDtypeStruct((rows, d), BF16),
         in_specs=[VMEM] * (2 + groups),
-        out_specs=VMEM,
-        scratch_shapes=[pltpu.VMEM((slots, d), BF16)],
+        out_specs=HBM,
+        scratch_shapes=[
+            pltpu.VMEM((slots, d), BF16),
+            pltpu.VMEM((rows, d), BF16),
+            pltpu.SemaphoreType.DMA((2,)),
+        ],
         compiler_params=pltpu.CompilerParams(vmem_limit_bytes=32 * MIB),
         cost_estimate=pl.CostEstimate(
             flops=2 * slots * rows * d, bytes_accessed=2 * d * (slots + rows), transcendentals=0

time: 149 us -> 149 us (level)
  transfers between devices with their start and end apart: 60 -> 60, of which waited for: 12 -> 10; matrix products, arithmetic and copies ran while one was open for 0% -> 0% of each run, Pallas kernels for 2% -> 2%
where the time goes in v14:
time: 149 us
  starting transfers between devices  110 us (74%)
  waiting for transfers between devices  24.2 us (16%)
  Pallas kernels  12.6 us (8%)
  between operations  1.5 us (1%)
    ppermute x60, starting transfers between devices, swap(): lax.ppermute(piece, 'expert', [(i, i ^ s) for i in range(groups)])  110 us
    ppermute x60, waiting for transfers between devices, swap(): lax.ppermute(piece, 'expert', [(i, i ^ s) for i in range(groups)])  24.2 us
    pallas_call x1, Pallas kernels, update(): pl.pallas_call(functools.partial(update_kernel, groups), out_shape=(shape...  5.14 us
  transfers between devices with their start and end apart: 60, of which 10 were waited for; matrix products, arithmetic and copies ran while one was open for 0% of the time, Pallas kernels for 2%

profile of v14, /device:TPU:0, one launch (start us, length us, event | category | flops | bytes accessed | tf_op | source)
XLA Modules:
  0.0 149.3 jit_solution(10359874477857554545)
XLA Ops:
  0.7 2.7 %split.1 = (bf16[2,48,512]{2,1,0:T(8,128)(2,1)}, bf16[2,48,512]{2,1,0:T(8,128)(2,1)}, bf16[2,48,512]{2,1,0:T(8,128)(2,1)}, bf16[2,48,512]{2,1,0:T(8,128)(2,1)}, ...) custom-call(s32[1]{0:T(128)} %bitcast.me_ref, ...), custom_call_target="tpu_custom_call" | custom-call | bytes 3145728 | tf_op jit(solution)/shard_map/split/pallas_call | solution.py:135
  3.4 2.5 %collective-permute-start = (bf16[2,48,512]{2,1,0:T(8,128)(2,1)}, bf16[2,48,512]{2,1,0:T(8,128)(2,1)S(1)}, u32[]{:S(2)}, u32[]{:S(2)}) collective-permute-start(bf16[2,48,512]{2,1,0:T(8,128)(2,1)} %get-tuple-element.71), channel_id=1, source_target_pairs={{0,5},{1,4},{2,7},{3,6},{4,1},{5,0},{6,3},{7,2},{8,13},{9,12},{10,... | collective-permute-start | bytes 294920 | tf_op jit(solution)/shard_map/ppermute | solution.py:296
  5.9 2.6 %collective-permute-start.16 = (bf16[2,48,512]{2,1,0:T(8,128)(2,1)}, bf16[2,48,512]{2,1,0:T(8,128)(2,1)S(1)}, u32[]{:S(2)}, u32[]{:S(2)}) collective-permute-start(bf16[2,48,512]{2,1,0:T(8,128)(2,1)} %get-tuple-element.89), channel_id=1, source_target_pairs={{0,8},{1,9},{2,10},{3,11},{4,12},{5,13},{6,14},{7,15},{8,0},{9,1},... | collective-permute-start | bytes 294920 | tf_op jit(solution)/shard_map/ppermute | solution.py:296
  16.1 2.8 %collective-permute-start.22 = (bf16[2,48,512]{2,1,0:T(8,128)(2,1)}, bf16[2,48,512]{2,1,0:T(8,128)(2,1)S(1)}, u32[]{:S(2)}, u32[]{:S(2)}) collective-permute-start(bf16[2,48,512]{2,1,0:T(8,128)(2,1)} %get-tuple-element.95), channel_id=1, source_target_pairs={{0,13},{1,12},{2,15},{3,14},{4,9},{5,8},{6,11},{7,10},{8,5},{9,4},... | collective-permute-start | bytes 294920 | tf_op jit(solution)/shard_map/ppermute | solution.py:296
  20.4 3.9 %collective-permute-start.24 = (bf16[2,48,512]{2,1,0:T(8,128)(2,1)}, bf16[2,48,512]{2,1,0:T(8,128)(2,1)S(1)}, u32[]{:S(2)}, u32[]{:S(2)}) collective-permute-start(bf16[2,48,512]{2,1,0:T(8,128)(2,1)} %get-tuple-element.97), channel_id=1, source_target_pairs={{0,10},{1,11},{2,8},{3,9},{4,14},{5,15},{6,12},{7,13},{8,2},{9,3},... | collective-permute-start | bytes 294920 | tf_op jit(solution)/shard_map/ppermute | solution.py:296
  24.3 3.8 %collective-permute-start.25 = (bf16[2,48,512]{2,1,0:T(8,128)(2,1)}, bf16[2,48,512]{2,1,0:T(8,128)(2,1)S(1)}, u32[]{:S(2)}, u32[]{:S(2)}) collective-permute-start(bf16[2,48,512]{2,1,0:T(8,128)(2,1)} %get-tuple-element.98), channel_id=1, source_target_pairs={{0,14},{1,15},{2,12},{3,13},{4,10},{5,11},{6,8},{7,9},{8,6},{9,7},... | collective-permute-start | bytes 294920 | tf_op jit(solution)/shard_map/ppermute | solution.py:296
  28.5 3.2 %collective-permute-start.27 = (bf16[2,48,512]{2,1,0:T(8,128)(2,1)}, bf16[2,48,512]{2,1,0:T(8,128)(2,1)S(1)}, u32[]{:S(2)}, u32[]{:S(2)}) collective-permute-start(bf16[2,48,512]{2,1,0:T(8,128)(2,1)} %get-tuple-element.100), channel_id=1, source_target_pairs={{0,11},{1,10},{2,9},{3,8},{4,15},{5,14},{6,13},{7,12},{8,3},{9,2},... | collective-permute-start | bytes 294920 | tf_op jit(solution)/shard_map/ppermute | solution.py:296
  31.7 2.8 %collective-permute-done.24.refs_9_ = bf16[2,48,512]{2,1,0:T(8,128)(2,1)S(1)} collective-permute-done((bf16[2,48,512]{2,1,0:T(8,128)(2,1)}, bf16[2,48,512]{2,1,0:T(8,128)(2,1)S(1)}, u32[]{:S(2)}, u32[]{:S(2)}) %collective-permute-start.24) | collective-permute-done | bytes 98336 | tf_op jit(solution)/shard_map/ppermute | solution.py:296
  37.5 2.8 %pack_rows.1 = (bf16[32,1792]{1,0:T(8,128)(2,1)S(1)}, bf16[32,1792]{1,0:T(8,128)(2,1)S(1)}, bf16[32,1792]{1,0:T(8,128)(2,1)S(1)}, bf16[32,1792]{1,0:T(8,128)(2,1...) custom-call(s32[1]{0:T(128)S(6)} %copy.13.live_ref, ...), custom_call_target="tpu_custom_call" | custom-call | flops 469762048 | bytes 2752512 | tf_op jit(solution)/shard_map/pack_rows/pallas_call | solution.py:107
  40.7 2.7 %collective-permute-start.2 = (bf16[32,1792]{1,0:T(8,128)(2,1)S(1)}, bf16[32,1792]{1,0:T(8,128)(2,1)S(1)}, u32[]{:S(2)}, u32[]{:S(2)}) collective-permute-start(bf16[32,1792]{1,0:T(8,128)(2,1)S(1)} %get-tuple-element.74), channel_id=1, source_target_pairs={{0,7},{1,6},{2,5},{3,4},{4,3},{5,2},{6,1},{7,0},{8,15},{9,14},{10,... | collective-permute-start | bytes 344072 | tf_op jit(solution)/shard_map/ppermute | solution.py:296
  43.4 5.0 %collective-permute-start.3 = (bf16[32,1792]{1,0:T(8,128)(2,1)S(1)}, bf16[32,1792]{1,0:T(8,128)(2,1)S(1)}, u32[]{:S(2)}, u32[]{:S(2)}) collective-permute-start(bf16[32,1792]{1,0:T(8,128)(2,1)S(1)} %get-tuple-element.75), channel_id=1, source_target_pairs={{0,12},{1,13},{2,14},{3,15},{4,8},{5,9},{6,10},{7,11},{8,4},{9,5},... | collective-permute-start | bytes 344072 | tf_op jit(solution)/shard_map/ppermute | solution.py:296
  50.4 5.6 %collective-permute-start.7 = (bf16[32,1792]{1,0:T(8,128)(2,1)S(1)}, bf16[32,1792]{1,0:T(8,128)(2,1)S(1)}, u32[]{:S(2)}, u32[]{:S(2)}) collective-permute-start(bf16[32,1792]{1,0:T(8,128)(2,1)S(1)} %get-tuple-element.79), channel_id=1, source_target_pairs={{0,13},{1,12},{2,15},{3,14},{4,9},{5,8},{6,11},{7,10},{8,5},{9,4},... | collective-permute-start | bytes 344072 | tf_op jit(solution)/shard_map/ppermute | solution.py:296
  56.1 4.4 %collective-permute-start.9 = (bf16[32,1792]{1,0:T(8,128)(2,1)S(1)}, bf16[32,1792]{1,0:T(8,128)(2,1)S(1)}, u32[]{:S(2)}, u32[]{:S(2)}) collective-permute-start(bf16[32,1792]{1,0:T(8,128)(2,1)S(1)} %get-tuple-element.81), channel_id=1, source_target_pairs={{0,10},{1,11},{2,8},{3,9},{4,14},{5,15},{6,12},{7,13},{8,2},{9,3},... | collective-permute-start | bytes 344072 | tf_op jit(solution)/shard_map/ppermute | solution.py:296
  60.5 3.8 %collective-permute-start.11 = (bf16[32,1792]{1,0:T(8,128)(2,1)S(1)}, bf16[32,1792]{1,0:T(8,128)(2,1)S(1)}, u32[]{:S(2)}, u32[]{:S(2)}) collective-permute-start(bf16[32,1792]{1,0:T(8,128)(2,1)S(1)} %get-tuple-element.83), channel_id=1, source_target_pairs={{0,14},{1,15},{2,12},{3,13},{4,10},{5,11},{6,8},{7,9},{8,6},{9,7},... | collective-permute-start | bytes 344072 | tf_op jit(solution)/shard_map/ppermute | solution.py:296
  64.6 4.3 %collective-permute-start.13 = (bf16[32,1792]{1,0:T(8,128)(2,1)S(1)}, bf16[32,1792]{1,0:T(8,128)(2,1)S(1)}, u32[]{:S(2)}, u32[]{:S(2)}) collective-permute-start(bf16[32,1792]{1,0:T(8,128)(2,1)S(1)} %get-tuple-element.85), channel_id=1, source_target_pairs={{0,11},{1,10},{2,9},{3,8},{4,15},{5,14},{6,13},{7,12},{8,3},{9,2},... | collective-permute-start | bytes 344072 | tf_op jit(solution)/shard_map/ppermute | solution.py:296
  69.0 2.2 %collective-permute-start.14 = (bf16[32,1792]{1,0:T(8,128)(2,1)S(1)}, bf16[32,1792]{1,0:T(8,128)(2,1)S(1)}, u32[]{:S(2)}, u32[]{:S(2)}) collective-permute-start(bf16[32,1792]{1,0:T(8,128)(2,1)S(1)} %get-tuple-element.86), channel_id=1, source_target_pairs={{0,4},{1,5},{2,6},{3,7},{4,0},{5,1},{6,2},{7,3},{8,12},{9,13},{10,... | collective-permute-start | bytes 344072 | tf_op jit(solution)/shard_map/ppermute | solution.py:296
  71.1 4.6 %collective-permute-start.15 = (bf16[32,1792]{1,0:T(8,128)(2,1)S(1)}, bf16[32,1792]{1,0:T(8,128)(2,1)S(1)}, u32[]{:S(2)}, u32[]{:S(2)}) collective-permute-start(bf16[32,1792]{1,0:T(8,128)(2,1)S(1)} %get-tuple-element.87), channel_id=1, source_target_pairs={{0,15},{1,14},{2,13},{3,12},{4,11},{5,10},{6,9},{7,8},{8,7},{9,6},... | collective-permute-start | bytes 344072 | tf_op jit(solution)/shard_map/ppermute | solution.py:296
  76.5 2.4 %collective-permute-start.30 = (bf16[2,48,512]{2,1,0:T(8,128)(2,1)S(1)}, bf16[2,48,512]{2,1,0:T(8,128)(2,1)S(1)}, u32[]{:S(2)}, u32[]{:S(2)}) collective-permute-start(bf16[2,48,512]{2,1,0:T(8,128)(2,1)S(1)} %get-tuple-element.104), channel_id=1, source_target_pairs={{0,8},{1,9},{2,10},{3,11},{4,12},{5,13},{6,14},{7,15},{8,0},{9,1},... | collective-permute-start | bytes 294920 | tf_op jit(solution)/shard_map/ppermute | solution.py:296
  80.8 2.1 %collective-permute-start.32 = (bf16[2,48,512]{2,1,0:T(8,128)(2,1)S(1)}, bf16[2,48,512]{2,1,0:T(8,128)(2,1)S(1)}, u32[]{:S(2)}, u32[]{:S(2)}) collective-permute-start(bf16[2,48,512]{2,1,0:T(8,128)(2,1)S(1)} %get-tuple-element.106), channel_id=1, source_target_pairs={{0,12},{1,13},{2,14},{3,15},{4,8},{5,9},{6,10},{7,11},{8,4},{9,5},... | collective-permute-start | bytes 294920 | tf_op jit(solution)/shard_map/ppermute | solution.py:296
  82.9 3.5 %collective-permute-start.33 = (bf16[2,48,512]{2,1,0:T(8,128)(2,1)S(1)}, bf16[2,48,512]{2,1,0:T(8,128)(2,1)S(1)}, u32[]{:S(2)}, u32[]{:S(2)}) collective-permute-start(bf16[2,48,512]{2,1,0:T(8,128)(2,1)S(1)} %get-tuple-element.107), channel_id=1, source_target_pairs={{0,3},{1,2},{2,1},{3,0},{4,7},{5,6},{6,5},{7,4},{8,11},{9,10},{10,... | collective-permute-start | bytes 294920 | tf_op jit(solution)/shard_map/ppermute | solution.py:296
  87.7 3.1 %collective-permute-done.30.refs_17_ = bf16[2,48,512]{2,1,0:T(8,128)(2,1)S(1)} collective-permute-done((bf16[2,48,512]{2,1,0:T(8,128)(2,1)S(1)}, bf16[2,48,512]{2,1,0:T(8,128)(2,1)S(1)}, u32[]{:S(2)}, u32[]{:S(2)}) %collective-permute-start.30) | collective-permute-done | bytes 98336 | tf_op jit(solution)/shard_map/ppermute | solution.py:296
  94.0 3.7 %collective-permute-start.38 = (bf16[2,48,512]{2,1,0:T(8,128)(2,1)S(1)}, bf16[2,48,512]{2,1,0:T(8,128)(2,1)S(1)}, u32[]{:S(2)}, u32[]{:S(2)}) collective-permute-start(bf16[2,48,512]{2,1,0:T(8,128)(2,1)S(1)} %get-tuple-element.112), channel_id=1, source_target_pairs={{0,10},{1,11},{2,8},{3,9},{4,14},{5,15},{6,12},{7,13},{8,2},{9,3},... | collective-permute-start | bytes 294920 | tf_op jit(solution)/shard_map/ppermute | solution.py:296
  97.7 2.6 %collective-permute-done.35.refs_22_ = bf16[2,48,512]{2,1,0:T(8,128)(2,1)S(1)} collective-permute-done((bf16[2,48,512]{2,1,0:T(8,128)(2,1)S(1)}, bf16[2,48,512]{2,1,0:T(8,128)(2,1)S(1)}, u32[]{:S(2)}, u32[]{:S(2)}) %collective-permute-start.35) | collective-permute-done | bytes 98336 | tf_op jit(solution)/shard_map/ppermute | solution.py:296
  100.3 2.6 %collective-permute-start.40 = (bf16[2,48,512]{2,1,0:T(8,128)(2,1)S(1)}, bf16[2,48,512]{2,1,0:T(8,128)(2,1)S(1)}, u32[]{:S(2)}, u32[]{:S(2)}) collective-permute-start(bf16[2,48,512]{2,1,0:T(8,128)(2,1)S(1)} %get-tuple-element.114), channel_id=1, source_target_pairs={{0,14},{1,15},{2,12},{3,13},{4,10},{5,11},{6,8},{7,9},{8,6},{9,7},... | collective-permute-start | bytes 294920 | tf_op jit(solution)/shard_map/ppermute | solution.py:296
  102.9 3.0 %collective-permute-start.42 = (bf16[2,48,512]{2,1,0:T(8,128)(2,1)S(1)}, bf16[2,48,512]{2,1,0:T(8,128)(2,1)S(1)}, u32[]{:S(2)}, u32[]{:S(2)}) collective-permute-start(bf16[2,48,512]{2,1,0:T(8,128)(2,1)S(1)} %get-tuple-element.116), channel_id=1, source_target_pairs={{0,11},{1,10},{2,9},{3,8},{4,15},{5,14},{6,13},{7,12},{8,3},{9,2},... | collective-permute-start | bytes 294920 | tf_op jit(solution)/shard_map/ppermute | solution.py:296
  107.8 7.4 %collective-permute-done.42.refs_29_ = bf16[2,48,512]{2,1,0:T(8,128)(2,1)S(1)} collective-permute-done((bf16[2,48,512]{2,1,0:T(8,128)(2,1)S(1)}, bf16[2,48,512]{2,1,0:T(8,128)(2,1)S(1)}, u32[]{:S(2)}, u32[]{:S(2)}) %collective-permute-start.42) | collective-permute-done | bytes 98336 | tf_op jit(solution)/shard_map/ppermute | solution.py:296
  115.1 5.1 %update.1 = (bf16[384,1024]{1,0:T(8,128)(2,1)}, bf16[384,1024]{1,0:T(8,128)(2,1)}, bf16[32,1024]{1,0:T(8,128)(2,1)S(1)}, bf16[32,1024]{1,0:T(8,128)(2,1)S(1)}, b...) custom-call(s32[1]{0:T(128)} %bitcast.me_ref, ...), custom_call_target="tpu_custom_call" | custom-call | flops 2239758336 | bytes 6029312 | tf_op jit(solution)/shard_map/update/pallas_call | solution.py:218
  120.3 4.0 %collective-permute-start.45 = (bf16[32,1024]{1,0:T(8,128)(2,1)S(1)}, bf16[32,1024]{1,0:T(8,128)(2,1)S(1)}, u32[]{:S(2)}, u32[]{:S(2)}) collective-permute-start(bf16[32,1024]{1,0:T(8,128)(2,1)S(1)} %get-tuple-element.124), channel_id=1, source_target_pairs={{0,8},{1,9},{2,10},{3,11},{4,12},{5,13},{6,14},{7,15},{8,0},{9,1},... | collective-permute-start | bytes 196616 | tf_op jit(solution)/shard_map/ppermute | solution.py:296
  124.3 2.1 %collective-permute-start.47 = (bf16[32,1024]{1,0:T(8,128)(2,1)S(1)}, bf16[32,1024]{1,0:T(8,128)(2,1)S(1)}, u32[]{:S(2)}, u32[]{:S(2)}) collective-permute-start(bf16[32,1024]{1,0:T(8,128)(2,1)S(1)} %get-tuple-element.126), channel_id=1, source_target_pairs={{0,12},{1,13},{2,14},{3,15},{4,8},{5,9},{6,10},{7,11},{8,4},{9,5},... | collective-permute-start | bytes 196616 | tf_op jit(solution)/shard_map/ppermute | solution.py:296
  132.5 2.7 %collective-permute-start.53 = (bf16[32,1024]{1,0:T(8,128)(2,1)S(1)}, bf16[32,1024]{1,0:T(8,128)(2,1)S(1)}, u32[]{:S(2)}, u32[]{:S(2)}) collective-permute-start(bf16[32,1024]{1,0:T(8,128)(2,1)S(1)} %get-tuple-element.132), channel_id=1, source_target_pairs={{0,10},{1,11},{2,8},{3,9},{4,14},{5,15},{6,12},{7,13},{8,2},{9,3},... | collective-permute-start | bytes 196616 | tf_op jit(solution)/shard_map/ppermute | solution.py:296
  135.3 3.1 %collective-permute-start.55 = (bf16[32,1024]{1,0:T(8,128)(2,1)S(1)}, bf16[32,1024]{1,0:T(8,128)(2,1)S(1)}, u32[]{:S(2)}, u32[]{:S(2)}) collective-permute-start(bf16[32,1024]{1,0:T(8,128)(2,1)S(1)} %get-tuple-element.134), channel_id=1, source_target_pairs={{0,14},{1,15},{2,12},{3,13},{4,10},{5,11},{6,8},{7,9},{8,6},{9,7},... | collective-permute-start | bytes 196616 | tf_op jit(solution)/shard_map/ppermute | solution.py:296
  143.2 3.0 %collective-permute-done.57.refs_13_ = bf16[32,1024]{1,0:T(8,128)(2,1)S(1)} collective-permute-done((bf16[32,1024]{1,0:T(8,128)(2,1)S(1)}, bf16[32,1024]{1,0:T(8,128)(2,1)S(1)}, u32[]{:S(2)}, u32[]{:S(2)}) %collective-permute-start.57) | collective-permute-done | bytes 65568 | tf_op jit(solution)/shard_map/ppermute | solution.py:296
  (109 shorter events, 37.8 us)
Async XLA Ops:
  11.3 13.0 %collective-permute-start.20 = (bf16[2,48,512]{2,1,0:T(8,128)(2,1)}, bf16[2,48,512]{2,1,0:T(8,128)(2,1)S(1)}, u32[]{:S(2)}, u32[]{:S(2)}) collective-permute-start(bf16[2,48,512]{2,1,0:T(8,128)(2,1)} %get-tuple-element.93), channel_id=1, source_target_pairs={{0,9},{1,8},{2,11},{3,10},{4,13},{5,12},{6,15},{7,14},{8,1},{9,0},... | collective-permute-start | bytes 294920 | tf_op jit(solution)/shard_map/ppermute | solution.py:296
  14.5 13.6 %collective-permute-start.21 = (bf16[2,48,512]{2,1,0:T(8,128)(2,1)}, bf16[2,48,512]{2,1,0:T(8,128)(2,1)S(1)}, u32[]{:S(2)}, u32[]{:S(2)}) collective-permute-start(bf16[2,48,512]{2,1,0:T(8,128)(2,1)} %get-tuple-element.94), channel_id=1, source_target_pairs={{0,6},{1,7},{2,4},{3,5},{4,2},{5,3},{6,0},{7,1},{8,14},{9,15},{10,... | collective-permute-start | bytes 294920 | tf_op jit(solution)/shard_map/ppermute | solution.py:296
  16.1 12.3 %collective-permute-start.22 = (bf16[2,48,512]{2,1,0:T(8,128)(2,1)}, bf16[2,48,512]{2,1,0:T(8,128)(2,1)S(1)}, u32[]{:S(2)}, u32[]{:S(2)}) collective-permute-start(bf16[2,48,512]{2,1,0:T(8,128)(2,1)} %get-tuple-element.95), channel_id=1, source_target_pairs={{0,13},{1,12},{2,15},{3,14},{4,9},{5,8},{6,11},{7,10},{8,5},{9,4},... | collective-permute-start | bytes 294920 | tf_op jit(solution)/shard_map/ppermute | solution.py:296
  18.9 12.7 %collective-permute-start.23 = (bf16[2,48,512]{2,1,0:T(8,128)(2,1)}, bf16[2,48,512]{2,1,0:T(8,128)(2,1)S(1)}, u32[]{:S(2)}, u32[]{:S(2)}) collective-permute-start(bf16[2,48,512]{2,1,0:T(8,128)(2,1)} %get-tuple-element.96), channel_id=1, source_target_pairs={{0,2},{1,3},{2,0},{3,1},{4,6},{5,7},{6,4},{7,5},{8,10},{9,11},{10,... | collective-permute-start | bytes 294920 | tf_op jit(solution)/shard_map/ppermute | solution.py:296
  20.4 14.1 %collective-permute-start.24 = (bf16[2,48,512]{2,1,0:T(8,128)(2,1)}, bf16[2,48,512]{2,1,0:T(8,128)(2,1)S(1)}, u32[]{:S(2)}, u32[]{:S(2)}) collective-permute-start(bf16[2,48,512]{2,1,0:T(8,128)(2,1)} %get-tuple-element.97), channel_id=1, source_target_pairs={{0,10},{1,11},{2,8},{3,9},{4,14},{5,15},{6,12},{7,13},{8,2},{9,3},... | collective-permute-start | bytes 294920 | tf_op jit(solution)/shard_map/ppermute | solution.py:296
  24.3 16.0 %collective-permute-start.25 = (bf16[2,48,512]{2,1,0:T(8,128)(2,1)}, bf16[2,48,512]{2,1,0:T(8,128)(2,1)S(1)}, u32[]{:S(2)}, u32[]{:S(2)}) collective-permute-start(bf16[2,48,512]{2,1,0:T(8,128)(2,1)} %get-tuple-element.98), channel_id=1, source_target_pairs={{0,14},{1,15},{2,12},{3,13},{4,10},{5,11},{6,8},{7,9},{8,6},{9,7},... | collective-permute-start | bytes 294920 | tf_op jit(solution)/shard_map/ppermute | solution.py:296
  28.1 12.6 %collective-permute-start.26 = (bf16[2,48,512]{2,1,0:T(8,128)(2,1)}, bf16[2,48,512]{2,1,0:T(8,128)(2,1)S(1)}, u32[]{:S(2)}, u32[]{:S(2)}) collective-permute-start(bf16[2,48,512]{2,1,0:T(8,128)(2,1)} %get-tuple-element.99), channel_id=1, source_target_pairs={{0,1},{1,0},{2,3},{3,2},{4,5},{5,4},{6,7},{7,6},{8,9},{9,8},{10,11... | collective-permute-start | bytes 294920 | tf_op jit(solution)/shard_map/ppermute | solution.py:296
  28.5 14.9 %collective-permute-start.27 = (bf16[2,48,512]{2,1,0:T(8,128)(2,1)}, bf16[2,48,512]{2,1,0:T(8,128)(2,1)S(1)}, u32[]{:S(2)}, u32[]{:S(2)}) collective-permute-start(bf16[2,48,512]{2,1,0:T(8,128)(2,1)} %get-tuple-element.100), channel_id=1, source_target_pairs={{0,11},{1,10},{2,9},{3,8},{4,15},{5,14},{6,13},{7,12},{8,3},{9,2},... | collective-permute-start | bytes 294920 | tf_op jit(solution)/shard_map/ppermute | solution.py:296
  31.7 16.8 %collective-permute-start.28 = (bf16[2,48,512]{2,1,0:T(8,128)(2,1)}, bf16[2,48,512]{2,1,0:T(8,128)(2,1)S(1)}, u32[]{:S(2)}, u32[]{:S(2)}) collective-permute-start(bf16[2,48,512]{2,1,0:T(8,128)(2,1)} %get-tuple-element.101), channel_id=1, source_target_pairs={{0,4},{1,5},{2,6},{3,7},{4,0},{5,1},{6,2},{7,3},{8,12},{9,13},{10,... | collective-permute-start | bytes 294920 | tf_op jit(solution)/shard_map/ppermute | solution.py:296
  34.4 14.0 %collective-permute-start.29 = (bf16[2,48,512]{2,1,0:T(8,128)(2,1)}, bf16[2,48,512]{2,1,0:T(8,128)(2,1)S(1)}, u32[]{:S(2)}, u32[]{:S(2)}) collective-permute-start(bf16[2,48,512]{2,1,0:T(8,128)(2,1)} %get-tuple-element.102), channel_id=1, source_target_pairs={{0,15},{1,14},{2,13},{3,12},{4,11},{5,10},{6,9},{7,8},{8,7},{9,6},... | collective-permute-start | bytes 294920 | tf_op jit(solution)/shard_map/ppermute | solution.py:296
  40.7 9.8 %collective-permute-start.2 = (bf16[32,1792]{1,0:T(8,128)(2,1)S(1)}, bf16[32,1792]{1,0:T(8,128)(2,1)S(1)}, u32[]{:S(2)}, u32[]{:S(2)}) collective-permute-start(bf16[32,1792]{1,0:T(8,128)(2,1)S(1)} %get-tuple-element.74), channel_id=1, source_target_pairs={{0,7},{1,6},{2,5},{3,4},{4,3},{5,2},{6,1},{7,0},{8,15},{9,14},{10,... | collective-permute-start | bytes 344072 | tf_op jit(solution)/shard_map/ppermute | solution.py:296
  43.4 12.7 %collective-permute-start.3 = (bf16[32,1792]{1,0:T(8,128)(2,1)S(1)}, bf16[32,1792]{1,0:T(8,128)(2,1)S(1)}, u32[]{:S(2)}, u32[]{:S(2)}) collective-permute-start(bf16[32,1792]{1,0:T(8,128)(2,1)S(1)} %get-tuple-element.75), channel_id=1, source_target_pairs={{0,12},{1,13},{2,14},{3,15},{4,8},{5,9},{6,10},{7,11},{8,4},{9,5},... | collective-permute-start | bytes 344072 | tf_op jit(solution)/shard_map/ppermute | solution.py:296
  48.4 12.1 %collective-permute-start.5 = (bf16[32,1792]{1,0:T(8,128)(2,1)S(1)}, bf16[32,1792]{1,0:T(8,128)(2,1)S(1)}, u32[]{:S(2)}, u32[]{:S(2)}) collective-permute-start(bf16[32,1792]{1,0:T(8,128)(2,1)S(1)} %get-tuple-element.77), channel_id=1, source_target_pairs={{0,9},{1,8},{2,11},{3,10},{4,13},{5,12},{6,15},{7,14},{8,1},{9,0},... | collective-permute-start | bytes 344072 | tf_op jit(solution)/shard_map/ppermute | solution.py:296
  49.0 11.5 %collective-permute-start.6 = (bf16[32,1792]{1,0:T(8,128)(2,1)S(1)}, bf16[32,1792]{1,0:T(8,128)(2,1)S(1)}, u32[]{:S(2)}, u32[]{:S(2)}) collective-permute-start(bf16[32,1792]{1,0:T(8,128)(2,1)S(1)} %get-tuple-element.78), channel_id=1, source_target_pairs={{0,6},{1,7},{2,4},{3,5},{4,2},{5,3},{6,0},{7,1},{8,14},{9,15},{10,... | collective-permute-start | bytes 344072 | tf_op jit(solution)/shard_map/ppermute | solution.py:296
  50.4 13.8 %collective-permute-start.7 = (bf16[32,1792]{1,0:T(8,128)(2,1)S(1)}, bf16[32,1792]{1,0:T(8,128)(2,1)S(1)}, u32[]{:S(2)}, u32[]{:S(2)}) collective-permute-start(bf16[32,1792]{1,0:T(8,128)(2,1)S(1)} %get-tuple-element.79), channel_id=1, source_target_pairs={{0,13},{1,12},{2,15},{3,14},{4,9},{5,8},{6,11},{7,10},{8,5},{9,4},... | collective-permute-start | bytes 344072 | tf_op jit(solution)/shard_map/ppermute | solution.py:296
  56.1 12.9 %collective-permute-start.9 = (bf16[32,1792]{1,0:T(8,128)(2,1)S(1)}, bf16[32,1792]{1,0:T(8,128)(2,1)S(1)}, u32[]{:S(2)}, u32[]{:S(2)}) collective-permute-start(bf16[32,1792]{1,0:T(8,128)(2,1)S(1)} %get-tuple-element.81), channel_id=1, source_target_pairs={{0,10},{1,11},{2,8},{3,9},{4,14},{5,15},{6,12},{7,13},{8,2},{9,3},... | collective-permute-start | bytes 344072 | tf_op jit(solution)/shard_map/ppermute | solution.py:296
  60.5 10.6 %collective-permute-start.10 = (bf16[32,1792]{1,0:T(8,128)(2,1)S(1)}, bf16[32,1792]{1,0:T(8,128)(2,1)S(1)}, u32[]{:S(2)}, u32[]{:S(2)}) collective-permute-start(bf16[32,1792]{1,0:T(8,128)(2,1)S(1)} %get-tuple-element.82), channel_id=1, source_target_pairs={{0,5},{1,4},{2,7},{3,6},{4,1},{5,0},{6,3},{7,2},{8,13},{9,12},{10,... | collective-permute-start | bytes 344072 | tf_op jit(solution)/shard_map/ppermute | solution.py:296
  60.5 16.0 %collective-permute-start.11 = (bf16[32,1792]{1,0:T(8,128)(2,1)S(1)}, bf16[32,1792]{1,0:T(8,128)(2,1)S(1)}, u32[]{:S(2)}, u32[]{:S(2)}) collective-permute-start(bf16[32,1792]{1,0:T(8,128)(2,1)S(1)} %get-tuple-element.83), channel_id=1, source_target_pairs={{0,14},{1,15},{2,12},{3,13},{4,10},{5,11},{6,8},{7,9},{8,6},{9,7},... | collective-permute-start | bytes 344072 | tf_op jit(solution)/shard_map/ppermute | solution.py:296
  64.3 14.7 %collective-permute-start.12 = (bf16[32,1792]{1,0:T(8,128)(2,1)S(1)}, bf16[32,1792]{1,0:T(8,128)(2,1)S(1)}, u32[]{:S(2)}, u32[]{:S(2)}) collective-permute-start(bf16[32,1792]{1,0:T(8,128)(2,1)S(1)} %get-tuple-element.84), channel_id=1, source_target_pairs={{0,1},{1,0},{2,3},{3,2},{4,5},{5,4},{6,7},{7,6},{8,9},{9,8},{10,11... | collective-permute-start | bytes 344072 | tf_op jit(solution)/shard_map/ppermute | solution.py:296
  64.6 16.2 %collective-permute-start.13 = (bf16[32,1792]{1,0:T(8,128)(2,1)S(1)}, bf16[32,1792]{1,0:T(8,128)(2,1)S(1)}, u32[]{:S(2)}, u32[]{:S(2)}) collective-permute-start(bf16[32,1792]{1,0:T(8,128)(2,1)S(1)} %get-tuple-element.85), channel_id=1, source_target_pairs={{0,11},{1,10},{2,9},{3,8},{4,15},{5,14},{6,13},{7,12},{8,3},{9,2},... | collective-permute-start | bytes 344072 | tf_op jit(solution)/shard_map/ppermute | solution.py:296
  69.0 14.0 %collective-permute-start.14 = (bf16[32,1792]{1,0:T(8,128)(2,1)S(1)}, bf16[32,1792]{1,0:T(8,128)(2,1)S(1)}, u32[]{:S(2)}, u32[]{:S(2)}) collective-permute-start(bf16[32,1792]{1,0:T(8,128)(2,1)S(1)} %get-tuple-element.86), channel_id=1, source_target_pairs={{0,4},{1,5},{2,6},{3,7},{4,0},{5,1},{6,2},{7,3},{8,12},{9,13},{10,... | collective-permute-start | bytes 344072 | tf_op jit(solution)/shard_map/ppermute | solution.py:296
  71.1 15.4 %collective-permute-start.15 = (bf16[32,1792]{1,0:T(8,128)(2,1)S(1)}, bf16[32,1792]{1,0:T(8,128)(2,1)S(1)}, u32[]{:S(2)}, u32[]{:S(2)}) collective-permute-start(bf16[32,1792]{1,0:T(8,128)(2,1)S(1)} %get-tuple-element.87), channel_id=1, source_target_pairs={{0,15},{1,14},{2,13},{3,12},{4,11},{5,10},{6,9},{7,8},{8,7},{9,6},... | collective-permute-start | bytes 344072 | tf_op jit(solution)/shard_map/ppermute | solution.py:296
  76.5 14.2 %collective-permute-start.30 = (bf16[2,48,512]{2,1,0:T(8,128)(2,1)S(1)}, bf16[2,48,512]{2,1,0:T(8,128)(2,1)S(1)}, u32[]{:S(2)}, u32[]{:S(2)}) collective-permute-start(bf16[2,48,512]{2,1,0:T(8,128)(2,1)S(1)} %get-tuple-element.104), channel_id=1, source_target_pairs={{0,8},{1,9},{2,10},{3,11},{4,12},{5,13},{6,14},{7,15},{8,0},{9,1},... | collective-permute-start | bytes 294920 | tf_op jit(solution)/shard_map/ppermute | solution.py:296
  78.9 11.8 %collective-permute-start.31 = (bf16[2,48,512]{2,1,0:T(8,128)(2,1)S(1)}, bf16[2,48,512]{2,1,0:T(8,128)(2,1)S(1)}, u32[]{:S(2)}, u32[]{:S(2)}) collective-permute-start(bf16[2,48,512]{2,1,0:T(8,128)(2,1)S(1)} %get-tuple-element.105), channel_id=1, source_target_pairs={{0,7},{1,6},{2,5},{3,4},{4,3},{5,2},{6,1},{7,0},{8,15},{9,14},{10,... | collective-permute-start | bytes 294920 | tf_op jit(solution)/shard_map/ppermute | solution.py:296
  80.8 11.7 %collective-permute-start.32 = (bf16[2,48,512]{2,1,0:T(8,128)(2,1)S(1)}, bf16[2,48,512]{2,1,0:T(8,128)(2,1)S(1)}, u32[]{:S(2)}, u32[]{:S(2)}) collective-permute-start(bf16[2,48,512]{2,1,0:T(8,128)(2,1)S(1)} %get-tuple-element.106), channel_id=1, source_target_pairs={{0,12},{1,13},{2,14},{3,15},{4,8},{5,9},{6,10},{7,11},{8,4},{9,5},... | collective-permute-start | bytes 294920 | tf_op jit(solution)/shard_map/ppermute | solution.py:296
  82.9 11.0 %collective-permute-start.33 = (bf16[2,48,512]{2,1,0:T(8,128)(2,1)S(1)}, bf16[2,48,512]{2,1,0:T(8,128)(2,1)S(1)}, u32[]{:S(2)}, u32[]{:S(2)}) collective-permute-start(bf16[2,48,512]{2,1,0:T(8,128)(2,1)S(1)} %get-tuple-element.107), channel_id=1, source_target_pairs={{0,3},{1,2},{2,1},{3,0},{4,7},{5,6},{6,5},{7,4},{8,11},{9,10},{10,... | collective-permute-start | bytes 294920 | tf_op jit(solution)/shard_map/ppermute | solution.py:296
  86.5 11.2 %collective-permute-start.34 = (bf16[2,48,512]{2,1,0:T(8,128)(2,1)S(1)}, bf16[2,48,512]{2,1,0:T(8,128)(2,1)S(1)}, u32[]{:S(2)}, u32[]{:S(2)}) collective-permute-start(bf16[2,48,512]{2,1,0:T(8,128)(2,1)S(1)} %get-tuple-element.108), channel_id=1, source_target_pairs={{0,9},{1,8},{2,11},{3,10},{4,13},{5,12},{6,15},{7,14},{8,1},{9,0},... | collective-permute-start | bytes 294920 | tf_op jit(solution)/shard_map/ppermute | solution.py:296
  90.7 9.5 %collective-permute-start.35 = (bf16[2,48,512]{2,1,0:T(8,128)(2,1)S(1)}, bf16[2,48,512]{2,1,0:T(8,128)(2,1)S(1)}, u32[]{:S(2)}, u32[]{:S(2)}) collective-permute-start(bf16[2,48,512]{2,1,0:T(8,128)(2,1)S(1)} %get-tuple-element.109), channel_id=1, source_target_pairs={{0,6},{1,7},{2,4},{3,5},{4,2},{5,3},{6,0},{7,1},{8,14},{9,15},{10,... | collective-permute-start | bytes 294920 | tf_op jit(solution)/shard_map/ppermute | solution.py:296
  90.8 12.1 %collective-permute-start.36 = (bf16[2,48,512]{2,1,0:T(8,128)(2,1)S(1)}, bf16[2,48,512]{2,1,0:T(8,128)(2,1)S(1)}, u32[]{:S(2)}, u32[]{:S(2)}) collective-permute-start(bf16[2,48,512]{2,1,0:T(8,128)(2,1)S(1)} %get-tuple-element.110), channel_id=1, source_target_pairs={{0,13},{1,12},{2,15},{3,14},{4,9},{5,8},{6,11},{7,10},{8,5},{9,4},... | collective-permute-start | bytes 294920 | tf_op jit(solution)/shard_map/ppermute | solution.py:296
  92.5 10.3 %collective-permute-start.37 = (bf16[2,48,512]{2,1,0:T(8,128)(2,1)S(1)}, bf16[2,48,512]{2,1,0:T(8,128)(2,1)S(1)}, u32[]{:S(2)}, u32[]{:S(2)}) collective-permute-start(bf16[2,48,512]{2,1,0:T(8,128)(2,1)S(1)} %get-tuple-element.111), channel_id=1, source_target_pairs={{0,2},{1,3},{2,0},{3,1},{4,6},{5,7},{6,4},{7,5},{8,10},{9,11},{10,... | collective-permute-start | bytes 294920 | tf_op jit(solution)/shard_map/ppermute | solution.py:296
  94.0 12.6 %collective-permute-start.38 = (bf16[2,48,512]{2,1,0:T(8,128)(2,1)S(1)}, bf16[2,48,512]{2,1,0:T(8,128)(2,1)S(1)}, u32[]{:S(2)}, u32[]{:S(2)}) collective-permute-start(bf16[2,48,512]{2,1,0:T(8,128)(2,1)S(1)} %get-tuple-element.112), channel_id=1, source_target_pairs={{0,10},{1,11},{2,8},{3,9},{4,14},{5,15},{6,12},{7,13},{8,2},{9,3},... | collective-permute-start | bytes 294920 | tf_op jit(solution)/shard_map/ppermute | solution.py:296
  102.9 12.3 %collective-permute-start.42 = (bf16[2,48,512]{2,1,0:T(8,128)(2,1)S(1)}, bf16[2,48,512]{2,1,0:T(8,128)(2,1)S(1)}, u32[]{:S(2)}, u32[]{:S(2)}) collective-permute-start(bf16[2,48,512]{2,1,0:T(8,128)(2,1)S(1)} %get-tuple-element.116), channel_id=1, source_target_pairs={{0,11},{1,10},{2,9},{3,8},{4,15},{5,14},{6,13},{7,12},{8,3},{9,2},... | collective-permute-start | bytes 294920 | tf_op jit(solution)/shard_map/ppermute | solution.py:296
  (36 other events, 391.8 us)

commit v15 on v10

--- a/solution.py
+++ b/solution.py
@@ -287,7 +287,7 @@
     spread = swap(split(me, w_moment, w_down, groups))
     packed, fwd_slot, gates = pack_rows(
         live_rows, me, perm, grad_route, fwd_route, grad_hidden, grad_out, fwd_hidden, fwd_gate,
-        spread[2 * groups // 3], groups, capacity,
+        spread[1], groups, capacity,
     )
     received = swap(packed)
     placed = swap(reorder(me, perm, spread, received[groups // 3]))

time: 149 us -> 150 us (level)
  waiting for transfers between devices: 24.5 us -> 36.1 us
  starting transfers between devices: 110 us -> 99.6 us
    ppermute x60, waiting for transfers between devices: 24.5 us -> 36.1 us  [swap(): lax.ppermute(piece, 'expert', [(i, i ^ s) for i in range(groups)])]
    ppermute x60, starting transfers between devices: 110 us -> 99.6 us  [swap(): lax.ppermute(piece, 'expert', [(i, i ^ s) for i in range(groups)])]
  transfers between devices with their start and end apart: 60 -> 60, of which waited for: 12 -> 17; matrix products, arithmetic and copies ran while one was open for 0% -> 0% of each run, Pallas kernels for 2% -> 2%
where the time goes in v15:
time: 150 us
  starting transfers between devices  99.6 us (66%)
  waiting for transfers between devices  36.1 us (24%)
  Pallas kernels  12.3 us (8%)
  between operations  1.52 us (1%)
    ppermute x60, starting transfers between devices, swap(): lax.ppermute(piece, 'expert', [(i, i ^ s) for i in range(groups)])  99.6 us
    ppermute x60, waiting for transfers between devices, swap(): lax.ppermute(piece, 'expert', [(i, i ^ s) for i in range(groups)])  36.1 us
    pallas_call x1, Pallas kernels, update(): pl.pallas_call(functools.partial(update_kernel, groups), out_shape=(shape...  4.74 us
  transfers between devices with their start and end apart: 60, of which 17 were waited for; matrix products, arithmetic and copies ran while one was open for 0% of the time, Pallas kernels for 2%

profile of v15, /device:TPU:0, one launch (start us, length us, event | category | flops | bytes accessed | tf_op | source)
XLA Modules:
  0.0 150.2 jit_solution(12024520451099506705)
XLA Ops:
  0.7 2.7 %split.1 = (bf16[2,48,512]{2,1,0:T(8,128)(2,1)}, bf16[2,48,512]{2,1,0:T(8,128)(2,1)}, bf16[2,48,512]{2,1,0:T(8,128)(2,1)}, bf16[2,48,512]{2,1,0:T(8,128)(2,1)}, ...) custom-call(s32[1]{0:T(128)} %bitcast.me_ref, ...), custom_call_target="tpu_custom_call" | custom-call | bytes 3145728 | tf_op jit(solution)/shard_map/split/pallas_call | solution.py:135
  3.4 4.1 %collective-permute-start = (bf16[2,48,512]{2,1,0:T(8,128)(2,1)}, bf16[2,48,512]{2,1,0:T(8,128)(2,1)S(1)}, u32[]{:S(2)}, u32[]{:S(2)}) collective-permute-start(bf16[2,48,512]{2,1,0:T(8,128)(2,1)} %get-tuple-element.71), channel_id=1, source_target_pairs={{0,8},{1,9},{2,10},{3,11},{4,12},{5,13},{6,14},{7,15},{8,0},{9,1},... | collective-permute-start | bytes 294920 | tf_op jit(solution)/shard_map/ppermute | solution.py:276
  12.6 2.2 %collective-permute-start.20 = (bf16[2,48,512]{2,1,0:T(8,128)(2,1)}, bf16[2,48,512]{2,1,0:T(8,128)(2,1)S(1)}, u32[]{:S(2)}, u32[]{:S(2)}) collective-permute-start(bf16[2,48,512]{2,1,0:T(8,128)(2,1)} %get-tuple-element.93), channel_id=1, source_target_pairs={{0,6},{1,7},{2,4},{3,5},{4,2},{5,3},{6,0},{7,1},{8,14},{9,15},{10,... | collective-permute-start | bytes 294920 | tf_op jit(solution)/shard_map/ppermute | solution.py:276
  17.9 5.3 %collective-permute-start.23 = (bf16[2,48,512]{2,1,0:T(8,128)(2,1)}, bf16[2,48,512]{2,1,0:T(8,128)(2,1)S(1)}, u32[]{:S(2)}, u32[]{:S(2)}) collective-permute-start(bf16[2,48,512]{2,1,0:T(8,128)(2,1)} %get-tuple-element.96), channel_id=1, source_target_pairs={{0,10},{1,11},{2,8},{3,9},{4,14},{5,15},{6,12},{7,13},{8,2},{9,3},... | collective-permute-start | bytes 294920 | tf_op jit(solution)/shard_map/ppermute | solution.py:276
  23.6 4.0 %collective-permute-start.25 = (bf16[2,48,512]{2,1,0:T(8,128)(2,1)}, bf16[2,48,512]{2,1,0:T(8,128)(2,1)S(1)}, u32[]{:S(2)}, u32[]{:S(2)}) collective-permute-start(bf16[2,48,512]{2,1,0:T(8,128)(2,1)} %get-tuple-element.98), channel_id=1, source_target_pairs={{0,14},{1,15},{2,12},{3,13},{4,10},{5,11},{6,8},{7,9},{8,6},{9,7},... | collective-permute-start | bytes 294920 | tf_op jit(solution)/shard_map/ppermute | solution.py:276
  27.6 3.3 %collective-permute-start.27 = (bf16[2,48,512]{2,1,0:T(8,128)(2,1)}, bf16[2,48,512]{2,1,0:T(8,128)(2,1)S(1)}, u32[]{:S(2)}, u32[]{:S(2)}) collective-permute-start(bf16[2,48,512]{2,1,0:T(8,128)(2,1)} %get-tuple-element.100), channel_id=1, source_target_pairs={{0,11},{1,10},{2,9},{3,8},{4,15},{5,14},{6,13},{7,12},{8,3},{9,2},... | collective-permute-start | bytes 294920 | tf_op jit(solution)/shard_map/ppermute | solution.py:276
  32.6 3.9 %collective-permute-start.29 = (bf16[2,48,512]{2,1,0:T(8,128)(2,1)}, bf16[2,48,512]{2,1,0:T(8,128)(2,1)S(1)}, u32[]{:S(2)}, u32[]{:S(2)}) collective-permute-start(bf16[2,48,512]{2,1,0:T(8,128)(2,1)} %get-tuple-element.102), channel_id=1, source_target_pairs={{0,15},{1,14},{2,13},{3,12},{4,11},{5,10},{6,9},{7,8},{8,7},{9,6},... | collective-permute-start | bytes 294920 | tf_op jit(solution)/shard_map/ppermute | solution.py:276
  37.8 2.8 %pack_rows.1 = (bf16[32,1792]{1,0:T(8,128)(2,1)S(1)}, bf16[32,1792]{1,0:T(8,128)(2,1)S(1)}, bf16[32,1792]{1,0:T(8,128)(2,1)S(1)}, bf16[32,1792]{1,0:T(8,128)(2,1...) custom-call(s32[1]{0:T(128)S(6)} %copy.13.live_ref, ...), custom_call_target="tpu_custom_call" | custom-call | flops 469762048 | bytes 2752512 | tf_op jit(solution)/shard_map/pack_rows/pallas_call | solution.py:107
  42.3 2.9 %collective-permute-start.3 = (bf16[32,1792]{1,0:T(8,128)(2,1)S(1)}, bf16[32,1792]{1,0:T(8,128)(2,1)S(1)}, u32[]{:S(2)}, u32[]{:S(2)}) collective-permute-start(bf16[32,1792]{1,0:T(8,128)(2,1)S(1)} %get-tuple-element.75), channel_id=1, source_target_pairs={{0,12},{1,13},{2,14},{3,15},{4,8},{5,9},{6,10},{7,11},{8,4},{9,5},... | collective-permute-start | bytes 344072 | tf_op jit(solution)/shard_map/ppermute | solution.py:276
  46.0 1.8 %collective-permute-start.5 = (bf16[32,1792]{1,0:T(8,128)(2,1)S(1)}, bf16[32,1792]{1,0:T(8,128)(2,1)S(1)}, u32[]{:S(2)}, u32[]{:S(2)}) collective-permute-start(bf16[32,1792]{1,0:T(8,128)(2,1)S(1)} %get-tuple-element.77), channel_id=1, source_target_pairs={{0,9},{1,8},{2,11},{3,10},{4,13},{5,12},{6,15},{7,14},{8,1},{9,0},... | collective-permute-start | bytes 344072 | tf_op jit(solution)/shard_map/ppermute | solution.py:276
  49.6 4.2 %collective-permute-start.6 = (bf16[32,1792]{1,0:T(8,128)(2,1)S(1)}, bf16[32,1792]{1,0:T(8,128)(2,1)S(1)}, u32[]{:S(2)}, u32[]{:S(2)}) collective-permute-start(bf16[32,1792]{1,0:T(8,128)(2,1)S(1)} %get-tuple-element.78), channel_id=1, source_target_pairs={{0,6},{1,7},{2,4},{3,5},{4,2},{5,3},{6,0},{7,1},{8,14},{9,15},{10,... | collective-permute-start | bytes 344072 | tf_op jit(solution)/shard_map/ppermute | solution.py:276
  53.8 3.0 %collective-permute-start.8 = (bf16[32,1792]{1,0:T(8,128)(2,1)S(1)}, bf16[32,1792]{1,0:T(8,128)(2,1)S(1)}, u32[]{:S(2)}, u32[]{:S(2)}) collective-permute-start(bf16[32,1792]{1,0:T(8,128)(2,1)S(1)} %get-tuple-element.80), channel_id=1, source_target_pairs={{0,2},{1,3},{2,0},{3,1},{4,6},{5,7},{6,4},{7,5},{8,10},{9,11},{10,... | collective-permute-start | bytes 344072 | tf_op jit(solution)/shard_map/ppermute | solution.py:276
  56.8 3.2 %collective-permute-start.9 = (bf16[32,1792]{1,0:T(8,128)(2,1)S(1)}, bf16[32,1792]{1,0:T(8,128)(2,1)S(1)}, u32[]{:S(2)}, u32[]{:S(2)}) collective-permute-start(bf16[32,1792]{1,0:T(8,128)(2,1)S(1)} %get-tuple-element.81), channel_id=1, source_target_pairs={{0,10},{1,11},{2,8},{3,9},{4,14},{5,15},{6,12},{7,13},{8,2},{9,3},... | collective-permute-start | bytes 344072 | tf_op jit(solution)/shard_map/ppermute | solution.py:276
  61.7 4.5 %collective-permute-start.11 = (bf16[32,1792]{1,0:T(8,128)(2,1)S(1)}, bf16[32,1792]{1,0:T(8,128)(2,1)S(1)}, u32[]{:S(2)}, u32[]{:S(2)}) collective-permute-start(bf16[32,1792]{1,0:T(8,128)(2,1)S(1)} %get-tuple-element.83), channel_id=1, source_target_pairs={{0,14},{1,15},{2,12},{3,13},{4,10},{5,11},{6,8},{7,9},{8,6},{9,7},... | collective-permute-start | bytes 344072 | tf_op jit(solution)/shard_map/ppermute | solution.py:276
  68.0 6.9 %collective-permute-done.9.refs_9_ = bf16[32,1792]{1,0:T(8,128)(2,1)S(1)} collective-permute-done((bf16[32,1792]{1,0:T(8,128)(2,1)S(1)}, bf16[32,1792]{1,0:T(8,128)(2,1)S(1)}, u32[]{:S(2)}, u32[]{:S(2)}) %collective-permute-start.9) | collective-permute-done | bytes 114720 | tf_op jit(solution)/shard_map/ppermute | solution.py:276
  75.7 2.2 %collective-permute-start.30 = (bf16[2,48,512]{2,1,0:T(8,128)(2,1)S(1)}, bf16[2,48,512]{2,1,0:T(8,128)(2,1)S(1)}, u32[]{:S(2)}, u32[]{:S(2)}) collective-permute-start(bf16[2,48,512]{2,1,0:T(8,128)(2,1)S(1)} %get-tuple-element.104), channel_id=1, source_target_pairs={{0,8},{1,9},{2,10},{3,11},{4,12},{5,13},{6,14},{7,15},{8,0},{9,1},... | collective-permute-start | bytes 294920 | tf_op jit(solution)/shard_map/ppermute | solution.py:276
  77.9 2.6 %collective-permute-start.31 = (bf16[2,48,512]{2,1,0:T(8,128)(2,1)S(1)}, bf16[2,48,512]{2,1,0:T(8,128)(2,1)S(1)}, u32[]{:S(2)}, u32[]{:S(2)}) collective-permute-start(bf16[2,48,512]{2,1,0:T(8,128)(2,1)S(1)} %get-tuple-element.105), channel_id=1, source_target_pairs={{0,7},{1,6},{2,5},{3,4},{4,3},{5,2},{6,1},{7,0},{8,15},{9,14},{10,... | collective-permute-start | bytes 294920 | tf_op jit(solution)/shard_map/ppermute | solution.py:276
  80.5 4.2 %collective-permute-start.32 = (bf16[2,48,512]{2,1,0:T(8,128)(2,1)S(1)}, bf16[2,48,512]{2,1,0:T(8,128)(2,1)S(1)}, u32[]{:S(2)}, u32[]{:S(2)}) collective-permute-start(bf16[2,48,512]{2,1,0:T(8,128)(2,1)S(1)} %get-tuple-element.106), channel_id=1, source_target_pairs={{0,12},{1,13},{2,14},{3,15},{4,8},{5,9},{6,10},{7,11},{8,4},{9,5},... | collective-permute-start | bytes 294920 | tf_op jit(solution)/shard_map/ppermute | solution.py:276
  84.7 5.1 %collective-permute-start.34 = (bf16[2,48,512]{2,1,0:T(8,128)(2,1)S(1)}, bf16[2,48,512]{2,1,0:T(8,128)(2,1)S(1)}, u32[]{:S(2)}, u32[]{:S(2)}) collective-permute-start(bf16[2,48,512]{2,1,0:T(8,128)(2,1)S(1)} %get-tuple-element.108), channel_id=1, source_target_pairs={{0,9},{1,8},{2,11},{3,10},{4,13},{5,12},{6,15},{7,14},{8,1},{9,0},... | collective-permute-start | bytes 294920 | tf_op jit(solution)/shard_map/ppermute | solution.py:276
  93.5 4.2 %collective-permute-start.38 = (bf16[2,48,512]{2,1,0:T(8,128)(2,1)S(1)}, bf16[2,48,512]{2,1,0:T(8,128)(2,1)S(1)}, u32[]{:S(2)}, u32[]{:S(2)}) collective-permute-start(bf16[2,48,512]{2,1,0:T(8,128)(2,1)S(1)} %get-tuple-element.112), channel_id=1, source_target_pairs={{0,10},{1,11},{2,8},{3,9},{4,14},{5,15},{6,12},{7,13},{8,2},{9,3},... | collective-permute-start | bytes 294920 | tf_op jit(solution)/shard_map/ppermute | solution.py:276
  100.9 2.2 %collective-permute-start.40 = (bf16[2,48,512]{2,1,0:T(8,128)(2,1)S(1)}, bf16[2,48,512]{2,1,0:T(8,128)(2,1)S(1)}, u32[]{:S(2)}, u32[]{:S(2)}) collective-permute-start(bf16[2,48,512]{2,1,0:T(8,128)(2,1)S(1)} %get-tuple-element.114), channel_id=1, source_target_pairs={{0,14},{1,15},{2,12},{3,13},{4,10},{5,11},{6,8},{7,9},{8,6},{9,7},... | collective-permute-start | bytes 294920 | tf_op jit(solution)/shard_map/ppermute | solution.py:276
  103.1 2.0 %collective-permute-start.42 = (bf16[2,48,512]{2,1,0:T(8,128)(2,1)S(1)}, bf16[2,48,512]{2,1,0:T(8,128)(2,1)S(1)}, u32[]{:S(2)}, u32[]{:S(2)}) collective-permute-start(bf16[2,48,512]{2,1,0:T(8,128)(2,1)S(1)} %get-tuple-element.116), channel_id=1, source_target_pairs={{0,11},{1,10},{2,9},{3,8},{4,15},{5,14},{6,13},{7,12},{8,3},{9,2},... | collective-permute-start | bytes 294920 | tf_op jit(solution)/shard_map/ppermute | solution.py:276
  105.1 5.7 %collective-permute-done.38.refs_25_ = bf16[2,48,512]{2,1,0:T(8,128)(2,1)S(1)} collective-permute-done((bf16[2,48,512]{2,1,0:T(8,128)(2,1)S(1)}, bf16[2,48,512]{2,1,0:T(8,128)(2,1)S(1)}, u32[]{:S(2)}, u32[]{:S(2)}) %collective-permute-start.38) | collective-permute-done | bytes 98336 | tf_op jit(solution)/shard_map/ppermute | solution.py:276
  110.9 4.1 %collective-permute-done.42.refs_29_ = bf16[2,48,512]{2,1,0:T(8,128)(2,1)S(1)} collective-permute-done((bf16[2,48,512]{2,1,0:T(8,128)(2,1)S(1)}, bf16[2,48,512]{2,1,0:T(8,128)(2,1)S(1)}, u32[]{:S(2)}, u32[]{:S(2)}) %collective-permute-start.42) | collective-permute-done | bytes 98336 | tf_op jit(solution)/shard_map/ppermute | solution.py:276
  114.9 2.6 %collective-permute-done.43.refs_30_ = bf16[2,48,512]{2,1,0:T(8,128)(2,1)S(1)} collective-permute-done((bf16[2,48,512]{2,1,0:T(8,128)(2,1)S(1)}, bf16[2,48,512]{2,1,0:T(8,128)(2,1)S(1)}, u32[]{:S(2)}, u32[]{:S(2)}) %collective-permute-start.43) | collective-permute-done | bytes 98336 | tf_op jit(solution)/shard_map/ppermute | solution.py:276
  117.7 4.7 %update.1 = (bf16[384,1024]{1,0:T(8,128)(2,1)}, bf16[384,1024]{1,0:T(8,128)(2,1)}, bf16[32,1024]{1,0:T(8,128)(2,1)S(1)}, bf16[32,1024]{1,0:T(8,128)(2,1)S(1)}, b...) custom-call(s32[1]{0:T(128)} %bitcast.me_ref, ...), custom_call_target="tpu_custom_call" | custom-call | flops 2239758336 | bytes 6029312 | tf_op jit(solution)/shard_map/update/pallas_call | solution.py:213
  122.5 2.1 %collective-permute-start.45 = (bf16[32,1024]{1,0:T(8,128)(2,1)S(1)}, bf16[32,1024]{1,0:T(8,128)(2,1)S(1)}, u32[]{:S(2)}, u32[]{:S(2)}) collective-permute-start(bf16[32,1024]{1,0:T(8,128)(2,1)S(1)} %get-tuple-element.124), channel_id=1, source_target_pairs={{0,8},{1,9},{2,10},{3,11},{4,12},{5,13},{6,14},{7,15},{8,0},{9,1},... | collective-permute-start | bytes 196616 | tf_op jit(solution)/shard_map/ppermute | solution.py:276
  124.6 2.3 %collective-permute-start.47 = (bf16[32,1024]{1,0:T(8,128)(2,1)S(1)}, bf16[32,1024]{1,0:T(8,128)(2,1)S(1)}, u32[]{:S(2)}, u32[]{:S(2)}) collective-permute-start(bf16[32,1024]{1,0:T(8,128)(2,1)S(1)} %get-tuple-element.126), channel_id=1, source_target_pairs={{0,12},{1,13},{2,14},{3,15},{4,8},{5,9},{6,10},{7,11},{8,4},{9,5},... | collective-permute-start | bytes 196616 | tf_op jit(solution)/shard_map/ppermute | solution.py:276
  133.1 3.2 %collective-permute-start.53 = (bf16[32,1024]{1,0:T(8,128)(2,1)S(1)}, bf16[32,1024]{1,0:T(8,128)(2,1)S(1)}, u32[]{:S(2)}, u32[]{:S(2)}) collective-permute-start(bf16[32,1024]{1,0:T(8,128)(2,1)S(1)} %get-tuple-element.132), channel_id=1, source_target_pairs={{0,10},{1,11},{2,8},{3,9},{4,14},{5,15},{6,12},{7,13},{8,2},{9,3},... | collective-permute-start | bytes 196616 | tf_op jit(solution)/shard_map/ppermute | solution.py:276
  136.3 2.3 %collective-permute-start.55 = (bf16[32,1024]{1,0:T(8,128)(2,1)S(1)}, bf16[32,1024]{1,0:T(8,128)(2,1)S(1)}, u32[]{:S(2)}, u32[]{:S(2)}) collective-permute-start(bf16[32,1024]{1,0:T(8,128)(2,1)S(1)} %get-tuple-element.134), channel_id=1, source_target_pairs={{0,14},{1,15},{2,12},{3,13},{4,10},{5,11},{6,8},{7,9},{8,6},{9,7},... | collective-permute-start | bytes 196616 | tf_op jit(solution)/shard_map/ppermute | solution.py:276
  143.4 3.2 %collective-permute-done.57.refs_13_ = bf16[32,1024]{1,0:T(8,128)(2,1)S(1)} collective-permute-done((bf16[32,1024]{1,0:T(8,128)(2,1)S(1)}, bf16[32,1024]{1,0:T(8,128)(2,1)S(1)}, u32[]{:S(2)}, u32[]{:S(2)}) %collective-permute-start.57) | collective-permute-done | bytes 65568 | tf_op jit(solution)/shard_map/ppermute | solution.py:276
  146.6 2.3 %collective-permute-done.59.refs_15_ = bf16[32,1024]{1,0:T(8,128)(2,1)S(1)} collective-permute-done((bf16[32,1024]{1,0:T(8,128)(2,1)S(1)}, bf16[32,1024]{1,0:T(8,128)(2,1)S(1)}, u32[]{:S(2)}, u32[]{:S(2)}) %collective-permute-start.59) | collective-permute-done | bytes 65568 | tf_op jit(solution)/shard_map/ppermute | solution.py:276
  (109 shorter events, 39.0 us)
Async XLA Ops:
  10.2 13.1 %collective-permute-start.19 = (bf16[2,48,512]{2,1,0:T(8,128)(2,1)}, bf16[2,48,512]{2,1,0:T(8,128)(2,1)S(1)}, u32[]{:S(2)}, u32[]{:S(2)}) collective-permute-start(bf16[2,48,512]{2,1,0:T(8,128)(2,1)} %get-tuple-element.92), channel_id=1, source_target_pairs={{0,9},{1,8},{2,11},{3,10},{4,13},{5,12},{6,15},{7,14},{8,1},{9,0},... | collective-permute-start | bytes 294920 | tf_op jit(solution)/shard_map/ppermute | solution.py:276
  12.6 11.0 %collective-permute-start.20 = (bf16[2,48,512]{2,1,0:T(8,128)(2,1)}, bf16[2,48,512]{2,1,0:T(8,128)(2,1)S(1)}, u32[]{:S(2)}, u32[]{:S(2)}) collective-permute-start(bf16[2,48,512]{2,1,0:T(8,128)(2,1)} %get-tuple-element.93), channel_id=1, source_target_pairs={{0,6},{1,7},{2,4},{3,5},{4,2},{5,3},{6,0},{7,1},{8,14},{9,15},{10,... | collective-permute-start | bytes 294920 | tf_op jit(solution)/shard_map/ppermute | solution.py:276
  14.8 12.9 %collective-permute-start.21 = (bf16[2,48,512]{2,1,0:T(8,128)(2,1)}, bf16[2,48,512]{2,1,0:T(8,128)(2,1)S(1)}, u32[]{:S(2)}, u32[]{:S(2)}) collective-permute-start(bf16[2,48,512]{2,1,0:T(8,128)(2,1)} %get-tuple-element.94), channel_id=1, source_target_pairs={{0,13},{1,12},{2,15},{3,14},{4,9},{5,8},{6,11},{7,10},{8,5},{9,4},... | collective-permute-start | bytes 294920 | tf_op jit(solution)/shard_map/ppermute | solution.py:276
  17.0 10.6 %collective-permute-start.22 = (bf16[2,48,512]{2,1,0:T(8,128)(2,1)}, bf16[2,48,512]{2,1,0:T(8,128)(2,1)S(1)}, u32[]{:S(2)}, u32[]{:S(2)}) collective-permute-start(bf16[2,48,512]{2,1,0:T(8,128)(2,1)} %get-tuple-element.95), channel_id=1, source_target_pairs={{0,2},{1,3},{2,0},{3,1},{4,6},{5,7},{6,4},{7,5},{8,10},{9,11},{10,... | collective-permute-start | bytes 294920 | tf_op jit(solution)/shard_map/ppermute | solution.py:276
  17.9 13.4 %collective-permute-start.23 = (bf16[2,48,512]{2,1,0:T(8,128)(2,1)}, bf16[2,48,512]{2,1,0:T(8,128)(2,1)S(1)}, u32[]{:S(2)}, u32[]{:S(2)}) collective-permute-start(bf16[2,48,512]{2,1,0:T(8,128)(2,1)} %get-tuple-element.96), channel_id=1, source_target_pairs={{0,10},{1,11},{2,8},{3,9},{4,14},{5,15},{6,12},{7,13},{8,2},{9,3},... | collective-permute-start | bytes 294920 | tf_op jit(solution)/shard_map/ppermute | solution.py:276
  23.6 17.0 %collective-permute-start.25 = (bf16[2,48,512]{2,1,0:T(8,128)(2,1)}, bf16[2,48,512]{2,1,0:T(8,128)(2,1)S(1)}, u32[]{:S(2)}, u32[]{:S(2)}) collective-permute-start(bf16[2,48,512]{2,1,0:T(8,128)(2,1)} %get-tuple-element.98), channel_id=1, source_target_pairs={{0,14},{1,15},{2,12},{3,13},{4,10},{5,11},{6,8},{7,9},{8,6},{9,7},... | collective-permute-start | bytes 294920 | tf_op jit(solution)/shard_map/ppermute | solution.py:276
  27.6 13.4 %collective-permute-start.26 = (bf16[2,48,512]{2,1,0:T(8,128)(2,1)}, bf16[2,48,512]{2,1,0:T(8,128)(2,1)S(1)}, u32[]{:S(2)}, u32[]{:S(2)}) collective-permute-start(bf16[2,48,512]{2,1,0:T(8,128)(2,1)} %get-tuple-element.99), channel_id=1, source_target_pairs={{0,1},{1,0},{2,3},{3,2},{4,5},{5,4},{6,7},{7,6},{8,9},{9,8},{10,11... | collective-permute-start | bytes 294920 | tf_op jit(solution)/shard_map/ppermute | solution.py:276
  27.6 14.7 %collective-permute-start.27 = (bf16[2,48,512]{2,1,0:T(8,128)(2,1)}, bf16[2,48,512]{2,1,0:T(8,128)(2,1)S(1)}, u32[]{:S(2)}, u32[]{:S(2)}) collective-permute-start(bf16[2,48,512]{2,1,0:T(8,128)(2,1)} %get-tuple-element.100), channel_id=1, source_target_pairs={{0,11},{1,10},{2,9},{3,8},{4,15},{5,14},{6,13},{7,12},{8,3},{9,2},... | collective-permute-start | bytes 294920 | tf_op jit(solution)/shard_map/ppermute | solution.py:276
  31.3 13.8 %collective-permute-start.28 = (bf16[2,48,512]{2,1,0:T(8,128)(2,1)}, bf16[2,48,512]{2,1,0:T(8,128)(2,1)S(1)}, u32[]{:S(2)}, u32[]{:S(2)}) collective-permute-start(bf16[2,48,512]{2,1,0:T(8,128)(2,1)} %get-tuple-element.101), channel_id=1, source_target_pairs={{0,4},{1,5},{2,6},{3,7},{4,0},{5,1},{6,2},{7,3},{8,12},{9,13},{10,... | collective-permute-start | bytes 294920 | tf_op jit(solution)/shard_map/ppermute | solution.py:276
  32.6 13.4 %collective-permute-start.29 = (bf16[2,48,512]{2,1,0:T(8,128)(2,1)}, bf16[2,48,512]{2,1,0:T(8,128)(2,1)S(1)}, u32[]{:S(2)}, u32[]{:S(2)}) collective-permute-start(bf16[2,48,512]{2,1,0:T(8,128)(2,1)} %get-tuple-element.102), channel_id=1, source_target_pairs={{0,15},{1,14},{2,13},{3,12},{4,11},{5,10},{6,9},{7,8},{8,7},{9,6},... | collective-permute-start | bytes 294920 | tf_op jit(solution)/shard_map/ppermute | solution.py:276
  41.0 12.8 %collective-permute-start.2 = (bf16[32,1792]{1,0:T(8,128)(2,1)S(1)}, bf16[32,1792]{1,0:T(8,128)(2,1)S(1)}, u32[]{:S(2)}, u32[]{:S(2)}) collective-permute-start(bf16[32,1792]{1,0:T(8,128)(2,1)S(1)} %get-tuple-element.74), channel_id=1, source_target_pairs={{0,7},{1,6},{2,5},{3,4},{4,3},{5,2},{6,1},{7,0},{8,15},{9,14},{10,... | collective-permute-start | bytes 344072 | tf_op jit(solution)/shard_map/ppermute | solution.py:276
  42.3 11.5 %collective-permute-start.3 = (bf16[32,1792]{1,0:T(8,128)(2,1)S(1)}, bf16[32,1792]{1,0:T(8,128)(2,1)S(1)}, u32[]{:S(2)}, u32[]{:S(2)}) collective-permute-start(bf16[32,1792]{1,0:T(8,128)(2,1)S(1)} %get-tuple-element.75), channel_id=1, source_target_pairs={{0,12},{1,13},{2,14},{3,15},{4,8},{5,9},{6,10},{7,11},{8,4},{9,5},... | collective-permute-start | bytes 344072 | tf_op jit(solution)/shard_map/ppermute | solution.py:276
  45.2 11.6 %collective-permute-start.4 = (bf16[32,1792]{1,0:T(8,128)(2,1)S(1)}, bf16[32,1792]{1,0:T(8,128)(2,1)S(1)}, u32[]{:S(2)}, u32[]{:S(2)}) collective-permute-start(bf16[32,1792]{1,0:T(8,128)(2,1)S(1)} %get-tuple-element.76), channel_id=1, source_target_pairs={{0,3},{1,2},{2,1},{3,0},{4,7},{5,6},{6,5},{7,4},{8,11},{9,10},{10,... | collective-permute-start | bytes 344072 | tf_op jit(solution)/shard_map/ppermute | solution.py:276
  46.0 15.7 %collective-permute-start.5 = (bf16[32,1792]{1,0:T(8,128)(2,1)S(1)}, bf16[32,1792]{1,0:T(8,128)(2,1)S(1)}, u32[]{:S(2)}, u32[]{:S(2)}) collective-permute-start(bf16[32,1792]{1,0:T(8,128)(2,1)S(1)} %get-tuple-element.77), channel_id=1, source_target_pairs={{0,9},{1,8},{2,11},{3,10},{4,13},{5,12},{6,15},{7,14},{8,1},{9,0},... | collective-permute-start | bytes 344072 | tf_op jit(solution)/shard_map/ppermute | solution.py:276
  49.6 12.1 %collective-permute-start.6 = (bf16[32,1792]{1,0:T(8,128)(2,1)S(1)}, bf16[32,1792]{1,0:T(8,128)(2,1)S(1)}, u32[]{:S(2)}, u32[]{:S(2)}) collective-permute-start(bf16[32,1792]{1,0:T(8,128)(2,1)S(1)} %get-tuple-element.78), channel_id=1, source_target_pairs={{0,6},{1,7},{2,4},{3,5},{4,2},{5,3},{6,0},{7,1},{8,14},{9,15},{10,... | collective-permute-start | bytes 344072 | tf_op jit(solution)/shard_map/ppermute | solution.py:276
  53.8 12.4 %collective-permute-start.7 = (bf16[32,1792]{1,0:T(8,128)(2,1)S(1)}, bf16[32,1792]{1,0:T(8,128)(2,1)S(1)}, u32[]{:S(2)}, u32[]{:S(2)}) collective-permute-start(bf16[32,1792]{1,0:T(8,128)(2,1)S(1)} %get-tuple-element.79), channel_id=1, source_target_pairs={{0,13},{1,12},{2,15},{3,14},{4,9},{5,8},{6,11},{7,10},{8,5},{9,4},... | collective-permute-start | bytes 344072 | tf_op jit(solution)/shard_map/ppermute | solution.py:276
  53.8 12.4 %collective-permute-start.8 = (bf16[32,1792]{1,0:T(8,128)(2,1)S(1)}, bf16[32,1792]{1,0:T(8,128)(2,1)S(1)}, u32[]{:S(2)}, u32[]{:S(2)}) collective-permute-start(bf16[32,1792]{1,0:T(8,128)(2,1)S(1)} %get-tuple-element.80), channel_id=1, source_target_pairs={{0,2},{1,3},{2,0},{3,1},{4,6},{5,7},{6,4},{7,5},{8,10},{9,11},{10,... | collective-permute-start | bytes 344072 | tf_op jit(solution)/shard_map/ppermute | solution.py:276
  56.8 18.2 %collective-permute-start.9 = (bf16[32,1792]{1,0:T(8,128)(2,1)S(1)}, bf16[32,1792]{1,0:T(8,128)(2,1)S(1)}, u32[]{:S(2)}, u32[]{:S(2)}) collective-permute-start(bf16[32,1792]{1,0:T(8,128)(2,1)S(1)} %get-tuple-element.81), channel_id=1, source_target_pairs={{0,10},{1,11},{2,8},{3,9},{4,14},{5,15},{6,12},{7,13},{8,2},{9,3},... | collective-permute-start | bytes 344072 | tf_op jit(solution)/shard_map/ppermute | solution.py:276
  61.7 13.2 %collective-permute-start.10 = (bf16[32,1792]{1,0:T(8,128)(2,1)S(1)}, bf16[32,1792]{1,0:T(8,128)(2,1)S(1)}, u32[]{:S(2)}, u32[]{:S(2)}) collective-permute-start(bf16[32,1792]{1,0:T(8,128)(2,1)S(1)} %get-tuple-element.82), channel_id=1, source_target_pairs={{0,5},{1,4},{2,7},{3,6},{4,1},{5,0},{6,3},{7,2},{8,13},{9,12},{10,... | collective-permute-start | bytes 344072 | tf_op jit(solution)/shard_map/ppermute | solution.py:276
  61.7 14.0 %collective-permute-start.11 = (bf16[32,1792]{1,0:T(8,128)(2,1)S(1)}, bf16[32,1792]{1,0:T(8,128)(2,1)S(1)}, u32[]{:S(2)}, u32[]{:S(2)}) collective-permute-start(bf16[32,1792]{1,0:T(8,128)(2,1)S(1)} %get-tuple-element.83), channel_id=1, source_target_pairs={{0,14},{1,15},{2,12},{3,13},{4,10},{5,11},{6,8},{7,9},{8,6},{9,7},... | collective-permute-start | bytes 344072 | tf_op jit(solution)/shard_map/ppermute | solution.py:276
  66.2 11.7 %collective-permute-start.12 = (bf16[32,1792]{1,0:T(8,128)(2,1)S(1)}, bf16[32,1792]{1,0:T(8,128)(2,1)S(1)}, u32[]{:S(2)}, u32[]{:S(2)}) collective-permute-start(bf16[32,1792]{1,0:T(8,128)(2,1)S(1)} %get-tuple-element.84), channel_id=1, source_target_pairs={{0,1},{1,0},{2,3},{3,2},{4,5},{5,4},{6,7},{7,6},{8,9},{9,8},{10,11... | collective-permute-start | bytes 344072 | tf_op jit(solution)/shard_map/ppermute | solution.py:276
  66.2 14.3 %collective-permute-start.13 = (bf16[32,1792]{1,0:T(8,128)(2,1)S(1)}, bf16[32,1792]{1,0:T(8,128)(2,1)S(1)}, u32[]{:S(2)}, u32[]{:S(2)}) collective-permute-start(bf16[32,1792]{1,0:T(8,128)(2,1)S(1)} %get-tuple-element.85), channel_id=1, source_target_pairs={{0,11},{1,10},{2,9},{3,8},{4,15},{5,14},{6,13},{7,12},{8,3},{9,2},... | collective-permute-start | bytes 344072 | tf_op jit(solution)/shard_map/ppermute | solution.py:276
  75.7 15.3 %collective-permute-start.30 = (bf16[2,48,512]{2,1,0:T(8,128)(2,1)S(1)}, bf16[2,48,512]{2,1,0:T(8,128)(2,1)S(1)}, u32[]{:S(2)}, u32[]{:S(2)}) collective-permute-start(bf16[2,48,512]{2,1,0:T(8,128)(2,1)S(1)} %get-tuple-element.104), channel_id=1, source_target_pairs={{0,8},{1,9},{2,10},{3,11},{4,12},{5,13},{6,14},{7,15},{8,0},{9,1},... | collective-permute-start | bytes 294920 | tf_op jit(solution)/shard_map/ppermute | solution.py:276
  77.9 13.2 %collective-permute-start.31 = (bf16[2,48,512]{2,1,0:T(8,128)(2,1)S(1)}, bf16[2,48,512]{2,1,0:T(8,128)(2,1)S(1)}, u32[]{:S(2)}, u32[]{:S(2)}) collective-permute-start(bf16[2,48,512]{2,1,0:T(8,128)(2,1)S(1)} %get-tuple-element.105), channel_id=1, source_target_pairs={{0,7},{1,6},{2,5},{3,4},{4,3},{5,2},{6,1},{7,0},{8,15},{9,14},{10,... | collective-permute-start | bytes 294920 | tf_op jit(solution)/shard_map/ppermute | solution.py:276
  80.5 12.2 %collective-permute-start.32 = (bf16[2,48,512]{2,1,0:T(8,128)(2,1)S(1)}, bf16[2,48,512]{2,1,0:T(8,128)(2,1)S(1)}, u32[]{:S(2)}, u32[]{:S(2)}) collective-permute-start(bf16[2,48,512]{2,1,0:T(8,128)(2,1)S(1)} %get-tuple-element.106), channel_id=1, source_target_pairs={{0,12},{1,13},{2,14},{3,15},{4,8},{5,9},{6,10},{7,11},{8,4},{9,5},... | collective-permute-start | bytes 294920 | tf_op jit(solution)/shard_map/ppermute | solution.py:276
  84.7 14.8 %collective-permute-start.34 = (bf16[2,48,512]{2,1,0:T(8,128)(2,1)S(1)}, bf16[2,48,512]{2,1,0:T(8,128)(2,1)S(1)}, u32[]{:S(2)}, u32[]{:S(2)}) collective-permute-start(bf16[2,48,512]{2,1,0:T(8,128)(2,1)S(1)} %get-tuple-element.108), channel_id=1, source_target_pairs={{0,9},{1,8},{2,11},{3,10},{4,13},{5,12},{6,15},{7,14},{8,1},{9,0},... | collective-permute-start | bytes 294920 | tf_op jit(solution)/shard_map/ppermute | solution.py:276
  91.1 12.1 %collective-permute-start.36 = (bf16[2,48,512]{2,1,0:T(8,128)(2,1)S(1)}, bf16[2,48,512]{2,1,0:T(8,128)(2,1)S(1)}, u32[]{:S(2)}, u32[]{:S(2)}) collective-permute-start(bf16[2,48,512]{2,1,0:T(8,128)(2,1)S(1)} %get-tuple-element.110), channel_id=1, source_target_pairs={{0,13},{1,12},{2,15},{3,14},{4,9},{5,8},{6,11},{7,10},{8,5},{9,4},... | collective-permute-start | bytes 294920 | tf_op jit(solution)/shard_map/ppermute | solution.py:276
  92.6 10.5 %collective-permute-start.37 = (bf16[2,48,512]{2,1,0:T(8,128)(2,1)S(1)}, bf16[2,48,512]{2,1,0:T(8,128)(2,1)S(1)}, u32[]{:S(2)}, u32[]{:S(2)}) collective-permute-start(bf16[2,48,512]{2,1,0:T(8,128)(2,1)S(1)} %get-tuple-element.111), channel_id=1, source_target_pairs={{0,2},{1,3},{2,0},{3,1},{4,6},{5,7},{6,4},{7,5},{8,10},{9,11},{10,... | collective-permute-start | bytes 294920 | tf_op jit(solution)/shard_map/ppermute | solution.py:276
  93.5 17.3 %collective-permute-start.38 = (bf16[2,48,512]{2,1,0:T(8,128)(2,1)S(1)}, bf16[2,48,512]{2,1,0:T(8,128)(2,1)S(1)}, u32[]{:S(2)}, u32[]{:S(2)}) collective-permute-start(bf16[2,48,512]{2,1,0:T(8,128)(2,1)S(1)} %get-tuple-element.112), channel_id=1, source_target_pairs={{0,10},{1,11},{2,8},{3,9},{4,14},{5,15},{6,12},{7,13},{8,2},{9,3},... | collective-permute-start | bytes 294920 | tf_op jit(solution)/shard_map/ppermute | solution.py:276
  99.5 11.3 %collective-permute-start.39 = (bf16[2,48,512]{2,1,0:T(8,128)(2,1)S(1)}, bf16[2,48,512]{2,1,0:T(8,128)(2,1)S(1)}, u32[]{:S(2)}, u32[]{:S(2)}) collective-permute-start(bf16[2,48,512]{2,1,0:T(8,128)(2,1)S(1)} %get-tuple-element.113), channel_id=1, source_target_pairs={{0,5},{1,4},{2,7},{3,6},{4,1},{5,0},{6,3},{7,2},{8,13},{9,12},{10,... | collective-permute-start | bytes 294920 | tf_op jit(solution)/shard_map/ppermute | solution.py:276
  100.9 9.9 %collective-permute-start.40 = (bf16[2,48,512]{2,1,0:T(8,128)(2,1)S(1)}, bf16[2,48,512]{2,1,0:T(8,128)(2,1)S(1)}, u32[]{:S(2)}, u32[]{:S(2)}) collective-permute-start(bf16[2,48,512]{2,1,0:T(8,128)(2,1)S(1)} %get-tuple-element.114), channel_id=1, source_target_pairs={{0,14},{1,15},{2,12},{3,13},{4,10},{5,11},{6,8},{7,9},{8,6},{9,7},... | collective-permute-start | bytes 294920 | tf_op jit(solution)/shard_map/ppermute | solution.py:276
  103.1 11.8 %collective-permute-start.42 = (bf16[2,48,512]{2,1,0:T(8,128)(2,1)S(1)}, bf16[2,48,512]{2,1,0:T(8,128)(2,1)S(1)}, u32[]{:S(2)}, u32[]{:S(2)}) collective-permute-start(bf16[2,48,512]{2,1,0:T(8,128)(2,1)S(1)} %get-tuple-element.116), channel_id=1, source_target_pairs={{0,11},{1,10},{2,9},{3,8},{4,15},{5,14},{6,13},{7,12},{8,3},{9,2},... | collective-permute-start | bytes 294920 | tf_op jit(solution)/shard_map/ppermute | solution.py:276
  (36 other events, 389.0 us)

commit v16 on v11

--- a/solution.py
+++ b/solution.py
@@ -157,7 +157,7 @@
     me, order = me_ref[0], mixed_order(groups)
     for s, source in zip(order, sources):
         held[me ^ perm_ref[me ^ s]] = source[...]
-    for s, target in zip(ending_near(groups), targets):
+    for s, target in zip(order, targets):
         target[...] = held[s]
 
 
@@ -184,7 +184,7 @@
     capacity = packed[0].shape[0]
     for n, piece in enumerate(packed):
         rows_ref[n * capacity : (n + 1) * capacity] = piece[...]
-    for s, piece in zip(ending_near(groups), pieces):
+    for s, piece in zip(mixed_order(groups), pieces):
         rows, columns = piece.shape[1:]
         for lead in range(2):
             chunk_at(held, lead, me_ref[0] ^ s, rows, columns)[...] = piece[lead]
@@ -208,9 +208,7 @@
     weight_new = (held[1].astype(F32) - step_scale * current.astype(F32)).astype(BF16)
     weight_new_ref[...] = weight_new
     product = jnp.dot(rows_ref[:, ff + d :], weight_new, preferred_element_type=F32).astype(BF16)
-    came = mixed_order(groups)
-    for s, piece in zip(ending_near(groups), produced):
-        n = came.index(s)
+    for n, piece in enumerate(produced):
         piece[...] = product[n * capacity : (n + 1) * capacity]
 
 
@@ -239,7 +237,7 @@
 def finish_kernel(groups, slot_ref, gates_ref, *refs):
     pieces, (out_ref, returned_ref) = refs[:groups], refs[groups:]
     capacity = pieces[0].shape[0]
-    for s, piece in zip(ending_near(groups), pieces):
+    for s, piece in zip(mixed_order(groups), pieces):
         returned_ref[s * capacity : (s + 1) * capacity] = piece[...]
     selector = selector_of(slot_ref[...], groups * capacity)
     expert_out = lax.dot_general(
@@ -278,16 +276,11 @@
     return [0] + [s for pair in zip(far, near + [None]) for s in pair if s is not None]
 
 
-def ending_near(groups):
+def swap(pieces):
+    groups = len(pieces)
     order = mixed_order(groups)
-    return order[:-4] + [order[n] for n in (-3, -4, -1, -2)] if groups > 4 else order
-
-
-def swap(pieces, order):
-    groups = lax.axis_size("expert")
-    return [
-        lax.ppermute(piece, "expert", [(i, i ^ s) for i in range(groups)]) if s else piece
-        for s, piece in zip(order, pieces)
+    return [pieces[0]] + [
+        lax.ppermute(piece, "expert", [(i, i ^ s) for i in range(groups)]) for s, piece in zip(order[1:], pieces[1:])
     ]
 
 
@@ -298,20 +291,20 @@
     me = lax.axis_index("expert").astype(jnp.int32).reshape(1)
     capacity = max(4, 2 * grad_hidden.shape[0] // groups)
     ff, d = w_down.shape[1:]
-    order, last_order = mixed_order(groups), ending_near(groups)
+    order = mixed_order(groups)
     first = order[1:6]
     blocks = dict(zip(first, split(me, w_moment, w_down, groups, first)))
     others = [s for s in order if s not in first]
     blocks.update(zip(others, split(me, w_moment, w_down, groups, others)))
-    spread = swap([blocks[s] for s in order], order)
+    spread = swap([blocks[s] for s in order])
     packed, fwd_slot, gates = pack_rows(
         live_rows, me, perm, grad_route, fwd_route, grad_hidden, grad_out, fwd_hidden, fwd_gate,
-        spread[1], groups, capacity,
-    )
-    received = swap(packed, order)
-    placed = swap(reorder(me, perm, spread, received[groups // 3]), last_order)
+        spread[2], groups, capacity,
+    )
+    received = swap(packed)
+    placed = swap(reorder(me, perm, spread, received[groups // 3]))
     weight_new, moment_new, produced = update(me, received, placed, ff, d)
-    return weight_new[None], moment_new[None], finish(fwd_slot, gates, swap(produced, last_order))
+    return weight_new[None], moment_new[None], finish(fwd_slot, gates, swap(produced))
 
 
 def lookup(route_ids, mapping):

time: 151 us -> 152 us (level)
  starting transfers between devices: 92.7 us -> 94.4 us
    ppermute x60, starting transfers between devices: 92.7 us -> 94.4 us  [swap(): lax.ppermute(piece, 'expert', [(i, i ^ s) for i in range(groups)])]
where the time goes in v16:
time: 152 us
  starting transfers between devices  94.4 us (62%)
  waiting for transfers between devices  41.6 us (27%)
  Pallas kernels  13.9 us (9%)
    ppermute x60, starting transfers between devices, swap(): lax.ppermute(piece, 'expert', [(i, i ^ s) for i in range(groups)])  94.4 us
    ppermute x60, waiting for transfers between devices, swap(): lax.ppermute(piece, 'expert', [(i, i ^ s) for i in range(groups)])  41.6 us
    pallas_call x1, Pallas kernels, update(): pl.pallas_call(functools.partial(update_kernel, groups), out_shape=(shape...  4.73 us
    pallas_call x2, Pallas kernels, split(): pl.pallas_call(functools.partial(split_kernel, partners), out_shape=(piec...  4.34 us
  transfers between devices with their start and end apart: 60, of which 19 were waited for; matrix products, arithmetic and copies ran while one was open for 0% of the time, Pallas kernels for 4%

profile of v16, /device:TPU:0, one launch (start us, length us, event | category | flops | bytes accessed | tf_op | source)
XLA Modules:
  0.0 152.1 jit_solution(15811544043293127067)
XLA Ops:
  2.5 3.5 %collective-permute-start = (bf16[2,48,512]{2,1,0:T(8,128)(2,1)}, bf16[2,48,512]{2,1,0:T(8,128)(2,1)S(1)}, u32[]{:S(2)}, u32[]{:S(2)}) collective-permute-start(bf16[2,48,512]{2,1,0:T(8,128)(2,1)} %get-tuple-element.71), channel_id=1, source_target_pairs={{0,7},{1,6},{2,5},{3,4},{4,3},{5,2},{6,1},{7,0},{8,15},{9,14},{10,... | collective-permute-start | bytes 294920 | tf_op jit(solution)/shard_map/ppermute | solution.py:283
  6.0 2.6 %collective-permute-start.16 = (bf16[2,48,512]{2,1,0:T(8,128)(2,1)}, bf16[2,48,512]{2,1,0:T(8,128)(2,1)S(1)}, u32[]{:S(2)}, u32[]{:S(2)}) collective-permute-start(bf16[2,48,512]{2,1,0:T(8,128)(2,1)} %get-tuple-element.89), channel_id=1, source_target_pairs={{0,8},{1,9},{2,10},{3,11},{4,12},{5,13},{6,14},{7,15},{8,0},{9,1},... | collective-permute-start | bytes 294920 | tf_op jit(solution)/shard_map/ppermute | solution.py:283
  11.0 2.5 %split.3 = (bf16[2,48,512]{2,1,0:T(8,128)(2,1)}, bf16[2,48,512]{2,1,0:T(8,128)(2,1)}, bf16[2,48,512]{2,1,0:T(8,128)(2,1)}, bf16[2,48,512]{2,1,0:T(8,128)(2,1)}, ...) custom-call(s32[1]{0:T(128)} %bitcast.me_ref, ...), custom_call_target="tpu_custom_call" | custom-call | bytes 2162688 | tf_op jit(solution)/shard_map/split/pallas_call | solution.py:140
  13.5 3.3 %collective-permute-start.20 = (bf16[2,48,512]{2,1,0:T(8,128)(2,1)}, bf16[2,48,512]{2,1,0:T(8,128)(2,1)S(1)}, u32[]{:S(2)}, u32[]{:S(2)}) collective-permute-start(bf16[2,48,512]{2,1,0:T(8,128)(2,1)} %get-tuple-element.93), channel_id=1, source_target_pairs={{0,6},{1,7},{2,4},{3,5},{4,2},{5,3},{6,0},{7,1},{8,14},{9,15},{10,... | collective-permute-start | bytes 294920 | tf_op jit(solution)/shard_map/ppermute | solution.py:283
  21.1 3.2 %collective-permute-start.23 = (bf16[2,48,512]{2,1,0:T(8,128)(2,1)}, bf16[2,48,512]{2,1,0:T(8,128)(2,1)S(1)}, u32[]{:S(2)}, u32[]{:S(2)}) collective-permute-start(bf16[2,48,512]{2,1,0:T(8,128)(2,1)} %get-tuple-element.96), channel_id=1, source_target_pairs={{0,10},{1,11},{2,8},{3,9},{4,14},{5,15},{6,12},{7,13},{8,2},{9,3},... | collective-permute-start | bytes 294920 | tf_op jit(solution)/shard_map/ppermute | solution.py:283
  24.3 2.4 %collective-permute-start.25 = (bf16[2,48,512]{2,1,0:T(8,128)(2,1)}, bf16[2,48,512]{2,1,0:T(8,128)(2,1)S(1)}, u32[]{:S(2)}, u32[]{:S(2)}) collective-permute-start(bf16[2,48,512]{2,1,0:T(8,128)(2,1)} %get-tuple-element.98), channel_id=1, source_target_pairs={{0,14},{1,15},{2,12},{3,13},{4,10},{5,11},{6,8},{7,9},{8,6},{9,7},... | collective-permute-start | bytes 294920 | tf_op jit(solution)/shard_map/ppermute | solution.py:283
  26.8 4.3 %collective-permute-start.27 = (bf16[2,48,512]{2,1,0:T(8,128)(2,1)}, bf16[2,48,512]{2,1,0:T(8,128)(2,1)S(1)}, u32[]{:S(2)}, u32[]{:S(2)}) collective-permute-start(bf16[2,48,512]{2,1,0:T(8,128)(2,1)} %get-tuple-element.100), channel_id=1, source_target_pairs={{0,11},{1,10},{2,9},{3,8},{4,15},{5,14},{6,13},{7,12},{8,3},{9,2},... | collective-permute-start | bytes 294920 | tf_op jit(solution)/shard_map/ppermute | solution.py:283
  31.1 2.7 %collective-permute-done.23.refs_9_ = bf16[2,48,512]{2,1,0:T(8,128)(2,1)S(1)} collective-permute-done((bf16[2,48,512]{2,1,0:T(8,128)(2,1)}, bf16[2,48,512]{2,1,0:T(8,128)(2,1)S(1)}, u32[]{:S(2)}, u32[]{:S(2)}) %collective-permute-start.23) | collective-permute-done | bytes 98336 | tf_op jit(solution)/shard_map/ppermute | solution.py:283
  33.8 2.6 %collective-permute-start.29 = (bf16[2,48,512]{2,1,0:T(8,128)(2,1)}, bf16[2,48,512]{2,1,0:T(8,128)(2,1)S(1)}, u32[]{:S(2)}, u32[]{:S(2)}) collective-permute-start(bf16[2,48,512]{2,1,0:T(8,128)(2,1)} %get-tuple-element.102), channel_id=1, source_target_pairs={{0,15},{1,14},{2,13},{3,12},{4,11},{5,10},{6,9},{7,8},{8,7},{9,6},... | collective-permute-start | bytes 294920 | tf_op jit(solution)/shard_map/ppermute | solution.py:283
  37.8 2.8 %pack_rows.1 = (bf16[32,1792]{1,0:T(8,128)(2,1)S(1)}, bf16[32,1792]{1,0:T(8,128)(2,1)S(1)}, bf16[32,1792]{1,0:T(8,128)(2,1)S(1)}, bf16[32,1792]{1,0:T(8,128)(2,1...) custom-call(s32[1]{0:T(128)S(6)} %copy.13.live_ref, ...), custom_call_target="tpu_custom_call" | custom-call | flops 469762048 | bytes 2752512 | tf_op jit(solution)/shard_map/pack_rows/pallas_call | solution.py:107
  42.8 2.7 %collective-permute-start.3 = (bf16[32,1792]{1,0:T(8,128)(2,1)S(1)}, bf16[32,1792]{1,0:T(8,128)(2,1)S(1)}, u32[]{:S(2)}, u32[]{:S(2)}) collective-permute-start(bf16[32,1792]{1,0:T(8,128)(2,1)S(1)} %get-tuple-element.75), channel_id=1, source_target_pairs={{0,12},{1,13},{2,14},{3,15},{4,8},{5,9},{6,10},{7,11},{8,4},{9,5},... | collective-permute-start | bytes 344072 | tf_op jit(solution)/shard_map/ppermute | solution.py:283
  46.6 3.4 %collective-permute-done.1.refs_1_ = bf16[32,1792]{1,0:T(8,128)(2,1)S(1)} collective-permute-done((bf16[32,1792]{1,0:T(8,128)(2,1)S(1)}, bf16[32,1792]{1,0:T(8,128)(2,1)S(1)}, u32[]{:S(2)}, u32[]{:S(2)}) %collective-permute-start.1) | collective-permute-done | bytes 114720 | tf_op jit(solution)/shard_map/ppermute | solution.py:283
  50.0 3.9 %collective-permute-start.7 = (bf16[32,1792]{1,0:T(8,128)(2,1)S(1)}, bf16[32,1792]{1,0:T(8,128)(2,1)S(1)}, u32[]{:S(2)}, u32[]{:S(2)}) collective-permute-start(bf16[32,1792]{1,0:T(8,128)(2,1)S(1)} %get-tuple-element.79), channel_id=1, source_target_pairs={{0,13},{1,12},{2,15},{3,14},{4,9},{5,8},{6,11},{7,10},{8,5},{9,4},... | collective-permute-start | bytes 344072 | tf_op jit(solution)/shard_map/ppermute | solution.py:283
  53.9 5.8 %collective-permute-start.9 = (bf16[32,1792]{1,0:T(8,128)(2,1)S(1)}, bf16[32,1792]{1,0:T(8,128)(2,1)S(1)}, u32[]{:S(2)}, u32[]{:S(2)}) collective-permute-start(bf16[32,1792]{1,0:T(8,128)(2,1)S(1)} %get-tuple-element.81), channel_id=1, source_target_pairs={{0,10},{1,11},{2,8},{3,9},{4,14},{5,15},{6,12},{7,13},{8,2},{9,3},... | collective-permute-start | bytes 344072 | tf_op jit(solution)/shard_map/ppermute | solution.py:283
  59.7 5.1 %collective-permute-done.5.refs_16_.refs_5_ = bf16[32,1792]{1,0:T(8,128)(2,1)S(1)} collective-permute-done((bf16[32,1792]{1,0:T(8,128)(2,1)S(1)}, bf16[32,1792]{1,0:T(8,128)(2,1)S(1)}, u32[]{:S(2)}, u32[]{:S(2)}) %collective-permute-start.5) | collective-permute-done | bytes 114720 | tf_op jit(solution)/shard_map/ppermute | solution.py:283
  65.0 4.0 %collective-permute-start.13 = (bf16[32,1792]{1,0:T(8,128)(2,1)S(1)}, bf16[32,1792]{1,0:T(8,128)(2,1)S(1)}, u32[]{:S(2)}, u32[]{:S(2)}) collective-permute-start(bf16[32,1792]{1,0:T(8,128)(2,1)S(1)} %get-tuple-element.85), channel_id=1, source_target_pairs={{0,11},{1,10},{2,9},{3,8},{4,15},{5,14},{6,13},{7,12},{8,3},{9,2},... | collective-permute-start | bytes 344072 | tf_op jit(solution)/shard_map/ppermute | solution.py:283
  70.2 3.7 %collective-permute-done.10.refs_10_ = bf16[32,1792]{1,0:T(8,128)(2,1)S(1)} collective-permute-done((bf16[32,1792]{1,0:T(8,128)(2,1)S(1)}, bf16[32,1792]{1,0:T(8,128)(2,1)S(1)}, u32[]{:S(2)}, u32[]{:S(2)}) %collective-permute-start.10) | collective-permute-done | bytes 114720 | tf_op jit(solution)/shard_map/ppermute | solution.py:283
  76.0 3.3 %collective-permute-start.30 = (bf16[2,48,512]{2,1,0:T(8,128)(2,1)S(1)}, bf16[2,48,512]{2,1,0:T(8,128)(2,1)S(1)}, u32[]{:S(2)}, u32[]{:S(2)}) collective-permute-start(bf16[2,48,512]{2,1,0:T(8,128)(2,1)S(1)} %get-tuple-element.104), channel_id=1, source_target_pairs={{0,8},{1,9},{2,10},{3,11},{4,12},{5,13},{6,14},{7,15},{8,0},{9,1},... | collective-permute-start | bytes 294920 | tf_op jit(solution)/shard_map/ppermute | solution.py:283
  81.1 3.7 %collective-permute-start.33 = (bf16[2,48,512]{2,1,0:T(8,128)(2,1)S(1)}, bf16[2,48,512]{2,1,0:T(8,128)(2,1)S(1)}, u32[]{:S(2)}, u32[]{:S(2)}) collective-permute-start(bf16[2,48,512]{2,1,0:T(8,128)(2,1)S(1)} %get-tuple-element.107), channel_id=1, source_target_pairs={{0,3},{1,2},{2,1},{3,0},{4,7},{5,6},{6,5},{7,4},{8,11},{9,10},{10,... | collective-permute-start | bytes 294920 | tf_op jit(solution)/shard_map/ppermute | solution.py:283
  84.8 2.5 %collective-permute-start.34 = (bf16[2,48,512]{2,1,0:T(8,128)(2,1)S(1)}, bf16[2,48,512]{2,1,0:T(8,128)(2,1)S(1)}, u32[]{:S(2)}, u32[]{:S(2)}) collective-permute-start(bf16[2,48,512]{2,1,0:T(8,128)(2,1)S(1)} %get-tuple-element.108), channel_id=1, source_target_pairs={{0,9},{1,8},{2,11},{3,10},{4,13},{5,12},{6,15},{7,14},{8,1},{9,0},... | collective-permute-start | bytes 294920 | tf_op jit(solution)/shard_map/ppermute | solution.py:283
  87.3 4.7 %collective-permute-done.30.refs_17_ = bf16[2,48,512]{2,1,0:T(8,128)(2,1)S(1)} collective-permute-done((bf16[2,48,512]{2,1,0:T(8,128)(2,1)S(1)}, bf16[2,48,512]{2,1,0:T(8,128)(2,1)S(1)}, u32[]{:S(2)}, u32[]{:S(2)}) %collective-permute-start.30) | collective-permute-done | bytes 98336 | tf_op jit(solution)/shard_map/ppermute | solution.py:283
  94.5 3.2 %collective-permute-start.38 = (bf16[2,48,512]{2,1,0:T(8,128)(2,1)S(1)}, bf16[2,48,512]{2,1,0:T(8,128)(2,1)S(1)}, u32[]{:S(2)}, u32[]{:S(2)}) collective-permute-start(bf16[2,48,512]{2,1,0:T(8,128)(2,1)S(1)} %get-tuple-element.112), channel_id=1, source_target_pairs={{0,10},{1,11},{2,8},{3,9},{4,14},{5,15},{6,12},{7,13},{8,2},{9,3},... | collective-permute-start | bytes 294920 | tf_op jit(solution)/shard_map/ppermute | solution.py:283
  97.7 2.9 %collective-permute-done.34.refs_21_ = bf16[2,48,512]{2,1,0:T(8,128)(2,1)S(1)} collective-permute-done((bf16[2,48,512]{2,1,0:T(8,128)(2,1)S(1)}, bf16[2,48,512]{2,1,0:T(8,128)(2,1)S(1)}, u32[]{:S(2)}, u32[]{:S(2)}) %collective-permute-start.34) | collective-permute-done | bytes 98336 | tf_op jit(solution)/shard_map/ppermute | solution.py:283
  101.9 3.2 %collective-permute-start.42 = (bf16[2,48,512]{2,1,0:T(8,128)(2,1)S(1)}, bf16[2,48,512]{2,1,0:T(8,128)(2,1)S(1)}, u32[]{:S(2)}, u32[]{:S(2)}) collective-permute-start(bf16[2,48,512]{2,1,0:T(8,128)(2,1)S(1)} %get-tuple-element.116), channel_id=1, source_target_pairs={{0,11},{1,10},{2,9},{3,8},{4,15},{5,14},{6,13},{7,12},{8,3},{9,2},... | collective-permute-start | bytes 294920 | tf_op jit(solution)/shard_map/ppermute | solution.py:283
  109.2 4.7 %collective-permute-done.42.refs_29_ = bf16[2,48,512]{2,1,0:T(8,128)(2,1)S(1)} collective-permute-done((bf16[2,48,512]{2,1,0:T(8,128)(2,1)S(1)}, bf16[2,48,512]{2,1,0:T(8,128)(2,1)S(1)}, u32[]{:S(2)}, u32[]{:S(2)}) %collective-permute-start.42) | collective-permute-done | bytes 98336 | tf_op jit(solution)/shard_map/ppermute | solution.py:283
  113.9 2.5 %collective-permute-done.44.refs_31_ = bf16[2,48,512]{2,1,0:T(8,128)(2,1)S(1)} collective-permute-done((bf16[2,48,512]{2,1,0:T(8,128)(2,1)S(1)}, bf16[2,48,512]{2,1,0:T(8,128)(2,1)S(1)}, u32[]{:S(2)}, u32[]{:S(2)}) %collective-permute-start.44) | collective-permute-done | bytes 98336 | tf_op jit(solution)/shard_map/ppermute | solution.py:283
  116.3 4.7 %update.1 = (bf16[384,1024]{1,0:T(8,128)(2,1)}, bf16[384,1024]{1,0:T(8,128)(2,1)}, bf16[32,1024]{1,0:T(8,128)(2,1)S(1)}, bf16[32,1024]{1,0:T(8,128)(2,1)S(1)}, b...) custom-call(s32[1]{0:T(128)} %bitcast.me_ref, ...), custom_call_target="tpu_custom_call" | custom-call | flops 2239758336 | bytes 6029312 | tf_op jit(solution)/shard_map/update/pallas_call | solution.py:220
  121.1 3.9 %collective-permute-start.45 = (bf16[32,1024]{1,0:T(8,128)(2,1)S(1)}, bf16[32,1024]{1,0:T(8,128)(2,1)S(1)}, u32[]{:S(2)}, u32[]{:S(2)}) collective-permute-start(bf16[32,1024]{1,0:T(8,128)(2,1)S(1)} %get-tuple-element.124), channel_id=1, source_target_pairs={{0,8},{1,9},{2,10},{3,11},{4,12},{5,13},{6,14},{7,15},{8,0},{9,1},... | collective-permute-start | bytes 196616 | tf_op jit(solution)/shard_map/ppermute | solution.py:283
  129.5 3.2 %collective-permute-start.50 = (bf16[32,1024]{1,0:T(8,128)(2,1)S(1)}, bf16[32,1024]{1,0:T(8,128)(2,1)S(1)}, u32[]{:S(2)}, u32[]{:S(2)}) collective-permute-start(bf16[32,1024]{1,0:T(8,128)(2,1)S(1)} %get-tuple-element.129), channel_id=1, source_target_pairs={{0,6},{1,7},{2,4},{3,5},{4,2},{5,3},{6,0},{7,1},{8,14},{9,15},{10,... | collective-permute-start | bytes 196616 | tf_op jit(solution)/shard_map/ppermute | solution.py:283
  133.6 2.6 %collective-permute-start.52 = (bf16[32,1024]{1,0:T(8,128)(2,1)S(1)}, bf16[32,1024]{1,0:T(8,128)(2,1)S(1)}, u32[]{:S(2)}, u32[]{:S(2)}) collective-permute-start(bf16[32,1024]{1,0:T(8,128)(2,1)S(1)} %get-tuple-element.131), channel_id=1, source_target_pairs={{0,2},{1,3},{2,0},{3,1},{4,6},{5,7},{6,4},{7,5},{8,10},{9,11},{10,... | collective-permute-start | bytes 196616 | tf_op jit(solution)/shard_map/ppermute | solution.py:283
  138.1 3.3 %collective-permute-start.55 = (bf16[32,1024]{1,0:T(8,128)(2,1)S(1)}, bf16[32,1024]{1,0:T(8,128)(2,1)S(1)}, u32[]{:S(2)}, u32[]{:S(2)}) collective-permute-start(bf16[32,1024]{1,0:T(8,128)(2,1)S(1)} %get-tuple-element.134), channel_id=1, source_target_pairs={{0,14},{1,15},{2,12},{3,13},{4,10},{5,11},{6,8},{7,9},{8,6},{9,7},... | collective-permute-start | bytes 196616 | tf_op jit(solution)/shard_map/ppermute | solution.py:283
  146.3 2.6 %collective-permute-done.57.refs_13_ = bf16[32,1024]{1,0:T(8,128)(2,1)S(1)} collective-permute-done((bf16[32,1024]{1,0:T(8,128)(2,1)S(1)}, bf16[32,1024]{1,0:T(8,128)(2,1)S(1)}, u32[]{:S(2)}, u32[]{:S(2)}) %collective-permute-start.57) | collective-permute-done | bytes 65568 | tf_op jit(solution)/shard_map/ppermute | solution.py:283
  (110 shorter events, 41.0 us)
Async XLA Ops:
  2.5 10.9 %collective-permute-start = (bf16[2,48,512]{2,1,0:T(8,128)(2,1)}, bf16[2,48,512]{2,1,0:T(8,128)(2,1)S(1)}, u32[]{:S(2)}, u32[]{:S(2)}) collective-permute-start(bf16[2,48,512]{2,1,0:T(8,128)(2,1)} %get-tuple-element.71), channel_id=1, source_target_pairs={{0,7},{1,6},{2,5},{3,4},{4,3},{5,2},{6,1},{7,0},{8,15},{9,14},{10,... | collective-permute-start | bytes 294920 | tf_op jit(solution)/shard_map/ppermute | solution.py:283
  6.0 13.1 %collective-permute-start.16 = (bf16[2,48,512]{2,1,0:T(8,128)(2,1)}, bf16[2,48,512]{2,1,0:T(8,128)(2,1)S(1)}, u32[]{:S(2)}, u32[]{:S(2)}) collective-permute-start(bf16[2,48,512]{2,1,0:T(8,128)(2,1)} %get-tuple-element.89), channel_id=1, source_target_pairs={{0,8},{1,9},{2,10},{3,11},{4,12},{5,13},{6,14},{7,15},{8,0},{9,1},... | collective-permute-start | bytes 294920 | tf_op jit(solution)/shard_map/ppermute | solution.py:283
  8.6 12.2 %collective-permute-start.17 = (bf16[2,48,512]{2,1,0:T(8,128)(2,1)}, bf16[2,48,512]{2,1,0:T(8,128)(2,1)S(1)}, u32[]{:S(2)}, u32[]{:S(2)}) collective-permute-start(bf16[2,48,512]{2,1,0:T(8,128)(2,1)} %get-tuple-element.90), channel_id=1, source_target_pairs={{0,12},{1,13},{2,14},{3,15},{4,8},{5,9},{6,10},{7,11},{8,4},{9,5},... | collective-permute-start | bytes 294920 | tf_op jit(solution)/shard_map/ppermute | solution.py:283
  8.8 12.3 %collective-permute-start.18 = (bf16[2,48,512]{2,1,0:T(8,128)(2,1)}, bf16[2,48,512]{2,1,0:T(8,128)(2,1)S(1)}, u32[]{:S(2)}, u32[]{:S(2)}) collective-permute-start(bf16[2,48,512]{2,1,0:T(8,128)(2,1)} %get-tuple-element.91), channel_id=1, source_target_pairs={{0,3},{1,2},{2,1},{3,0},{4,7},{5,6},{6,5},{7,4},{8,11},{9,10},{10,... | collective-permute-start | bytes 294920 | tf_op jit(solution)/shard_map/ppermute | solution.py:283
  9.1 15.2 %collective-permute-start.19 = (bf16[2,48,512]{2,1,0:T(8,128)(2,1)}, bf16[2,48,512]{2,1,0:T(8,128)(2,1)S(1)}, u32[]{:S(2)}, u32[]{:S(2)}) collective-permute-start(bf16[2,48,512]{2,1,0:T(8,128)(2,1)} %get-tuple-element.92), channel_id=1, source_target_pairs={{0,9},{1,8},{2,11},{3,10},{4,13},{5,12},{6,15},{7,14},{8,1},{9,0},... | collective-permute-start | bytes 294920 | tf_op jit(solution)/shard_map/ppermute | solution.py:283
  13.5 10.8 %collective-permute-start.20 = (bf16[2,48,512]{2,1,0:T(8,128)(2,1)}, bf16[2,48,512]{2,1,0:T(8,128)(2,1)S(1)}, u32[]{:S(2)}, u32[]{:S(2)}) collective-permute-start(bf16[2,48,512]{2,1,0:T(8,128)(2,1)} %get-tuple-element.93), channel_id=1, source_target_pairs={{0,6},{1,7},{2,4},{3,5},{4,2},{5,3},{6,0},{7,1},{8,14},{9,15},{10,... | collective-permute-start | bytes 294920 | tf_op jit(solution)/shard_map/ppermute | solution.py:283
  21.1 12.7 %collective-permute-start.23 = (bf16[2,48,512]{2,1,0:T(8,128)(2,1)}, bf16[2,48,512]{2,1,0:T(8,128)(2,1)S(1)}, u32[]{:S(2)}, u32[]{:S(2)}) collective-permute-start(bf16[2,48,512]{2,1,0:T(8,128)(2,1)} %get-tuple-element.96), channel_id=1, source_target_pairs={{0,10},{1,11},{2,8},{3,9},{4,14},{5,15},{6,12},{7,13},{8,2},{9,3},... | collective-permute-start | bytes 294920 | tf_op jit(solution)/shard_map/ppermute | solution.py:283
  24.3 16.3 %collective-permute-start.25 = (bf16[2,48,512]{2,1,0:T(8,128)(2,1)}, bf16[2,48,512]{2,1,0:T(8,128)(2,1)S(1)}, u32[]{:S(2)}, u32[]{:S(2)}) collective-permute-start(bf16[2,48,512]{2,1,0:T(8,128)(2,1)} %get-tuple-element.98), channel_id=1, source_target_pairs={{0,14},{1,15},{2,12},{3,13},{4,10},{5,11},{6,8},{7,9},{8,6},{9,7},... | collective-permute-start | bytes 294920 | tf_op jit(solution)/shard_map/ppermute | solution.py:283
  26.8 14.6 %collective-permute-start.26 = (bf16[2,48,512]{2,1,0:T(8,128)(2,1)}, bf16[2,48,512]{2,1,0:T(8,128)(2,1)S(1)}, u32[]{:S(2)}, u32[]{:S(2)}) collective-permute-start(bf16[2,48,512]{2,1,0:T(8,128)(2,1)} %get-tuple-element.99), channel_id=1, source_target_pairs={{0,1},{1,0},{2,3},{3,2},{4,5},{5,4},{6,7},{7,6},{8,9},{9,8},{10,11... | collective-permute-start | bytes 294920 | tf_op jit(solution)/shard_map/ppermute | solution.py:283
  26.8 16.0 %collective-permute-start.27 = (bf16[2,48,512]{2,1,0:T(8,128)(2,1)}, bf16[2,48,512]{2,1,0:T(8,128)(2,1)S(1)}, u32[]{:S(2)}, u32[]{:S(2)}) collective-permute-start(bf16[2,48,512]{2,1,0:T(8,128)(2,1)} %get-tuple-element.100), channel_id=1, source_target_pairs={{0,11},{1,10},{2,9},{3,8},{4,15},{5,14},{6,13},{7,12},{8,3},{9,2},... | collective-permute-start | bytes 294920 | tf_op jit(solution)/shard_map/ppermute | solution.py:283
  33.8 11.7 %collective-permute-start.28 = (bf16[2,48,512]{2,1,0:T(8,128)(2,1)}, bf16[2,48,512]{2,1,0:T(8,128)(2,1)S(1)}, u32[]{:S(2)}, u32[]{:S(2)}) collective-permute-start(bf16[2,48,512]{2,1,0:T(8,128)(2,1)} %get-tuple-element.101), channel_id=1, source_target_pairs={{0,4},{1,5},{2,6},{3,7},{4,0},{5,1},{6,2},{7,3},{8,12},{9,13},{10,... | collective-permute-start | bytes 294920 | tf_op jit(solution)/shard_map/ppermute | solution.py:283
  33.8 12.1 %collective-permute-start.29 = (bf16[2,48,512]{2,1,0:T(8,128)(2,1)}, bf16[2,48,512]{2,1,0:T(8,128)(2,1)S(1)}, u32[]{:S(2)}, u32[]{:S(2)}) collective-permute-start(bf16[2,48,512]{2,1,0:T(8,128)(2,1)} %get-tuple-element.102), channel_id=1, source_target_pairs={{0,15},{1,14},{2,13},{3,12},{4,11},{5,10},{6,9},{7,8},{8,7},{9,6},... | collective-permute-start | bytes 294920 | tf_op jit(solution)/shard_map/ppermute | solution.py:283
  42.8 11.1 %collective-permute-start.3 = (bf16[32,1792]{1,0:T(8,128)(2,1)S(1)}, bf16[32,1792]{1,0:T(8,128)(2,1)S(1)}, u32[]{:S(2)}, u32[]{:S(2)}) collective-permute-start(bf16[32,1792]{1,0:T(8,128)(2,1)S(1)} %get-tuple-element.75), channel_id=1, source_target_pairs={{0,12},{1,13},{2,14},{3,15},{4,8},{5,9},{6,10},{7,11},{8,4},{9,5},... | collective-permute-start | bytes 344072 | tf_op jit(solution)/shard_map/ppermute | solution.py:283
  46.0 18.8 %collective-permute-start.5 = (bf16[32,1792]{1,0:T(8,128)(2,1)S(1)}, bf16[32,1792]{1,0:T(8,128)(2,1)S(1)}, u32[]{:S(2)}, u32[]{:S(2)}) collective-permute-start(bf16[32,1792]{1,0:T(8,128)(2,1)S(1)} %get-tuple-element.77), channel_id=1, source_target_pairs={{0,9},{1,8},{2,11},{3,10},{4,13},{5,12},{6,15},{7,14},{8,1},{9,0},... | collective-permute-start | bytes 344072 | tf_op jit(solution)/shard_map/ppermute | solution.py:283
  50.0 14.8 %collective-permute-start.6 = (bf16[32,1792]{1,0:T(8,128)(2,1)S(1)}, bf16[32,1792]{1,0:T(8,128)(2,1)S(1)}, u32[]{:S(2)}, u32[]{:S(2)}) collective-permute-start(bf16[32,1792]{1,0:T(8,128)(2,1)S(1)} %get-tuple-element.78), channel_id=1, source_target_pairs={{0,6},{1,7},{2,4},{3,5},{4,2},{5,3},{6,0},{7,1},{8,14},{9,15},{10,... | collective-permute-start | bytes 344072 | tf_op jit(solution)/shard_map/ppermute | solution.py:283
  50.0 14.9 %collective-permute-start.7 = (bf16[32,1792]{1,0:T(8,128)(2,1)S(1)}, bf16[32,1792]{1,0:T(8,128)(2,1)S(1)}, u32[]{:S(2)}, u32[]{:S(2)}) collective-permute-start(bf16[32,1792]{1,0:T(8,128)(2,1)S(1)} %get-tuple-element.79), channel_id=1, source_target_pairs={{0,13},{1,12},{2,15},{3,14},{4,9},{5,8},{6,11},{7,10},{8,5},{9,4},... | collective-permute-start | bytes 344072 | tf_op jit(solution)/shard_map/ppermute | solution.py:283
  53.9 11.1 %collective-permute-start.8 = (bf16[32,1792]{1,0:T(8,128)(2,1)S(1)}, bf16[32,1792]{1,0:T(8,128)(2,1)S(1)}, u32[]{:S(2)}, u32[]{:S(2)}) collective-permute-start(bf16[32,1792]{1,0:T(8,128)(2,1)S(1)} %get-tuple-element.80), channel_id=1, source_target_pairs={{0,2},{1,3},{2,0},{3,1},{4,6},{5,7},{6,4},{7,5},{8,10},{9,11},{10,... | collective-permute-start | bytes 344072 | tf_op jit(solution)/shard_map/ppermute | solution.py:283
  53.9 15.3 %collective-permute-start.9 = (bf16[32,1792]{1,0:T(8,128)(2,1)S(1)}, bf16[32,1792]{1,0:T(8,128)(2,1)S(1)}, u32[]{:S(2)}, u32[]{:S(2)}) collective-permute-start(bf16[32,1792]{1,0:T(8,128)(2,1)S(1)} %get-tuple-element.81), channel_id=1, source_target_pairs={{0,10},{1,11},{2,8},{3,9},{4,14},{5,15},{6,12},{7,13},{8,2},{9,3},... | collective-permute-start | bytes 344072 | tf_op jit(solution)/shard_map/ppermute | solution.py:283
  64.8 11.2 %collective-permute-start.11 = (bf16[32,1792]{1,0:T(8,128)(2,1)S(1)}, bf16[32,1792]{1,0:T(8,128)(2,1)S(1)}, u32[]{:S(2)}, u32[]{:S(2)}) collective-permute-start(bf16[32,1792]{1,0:T(8,128)(2,1)S(1)} %get-tuple-element.83), channel_id=1, source_target_pairs={{0,14},{1,15},{2,12},{3,13},{4,10},{5,11},{6,8},{7,9},{8,6},{9,7},... | collective-permute-start | bytes 344072 | tf_op jit(solution)/shard_map/ppermute | solution.py:283
  64.9 14.4 %collective-permute-start.12 = (bf16[32,1792]{1,0:T(8,128)(2,1)S(1)}, bf16[32,1792]{1,0:T(8,128)(2,1)S(1)}, u32[]{:S(2)}, u32[]{:S(2)}) collective-permute-start(bf16[32,1792]{1,0:T(8,128)(2,1)S(1)} %get-tuple-element.84), channel_id=1, source_target_pairs={{0,1},{1,0},{2,3},{3,2},{4,5},{5,4},{6,7},{7,6},{8,9},{9,8},{10,11... | collective-permute-start | bytes 344072 | tf_op jit(solution)/shard_map/ppermute | solution.py:283
  65.0 14.6 %collective-permute-start.13 = (bf16[32,1792]{1,0:T(8,128)(2,1)S(1)}, bf16[32,1792]{1,0:T(8,128)(2,1)S(1)}, u32[]{:S(2)}, u32[]{:S(2)}) collective-permute-start(bf16[32,1792]{1,0:T(8,128)(2,1)S(1)} %get-tuple-element.85), channel_id=1, source_target_pairs={{0,11},{1,10},{2,9},{3,8},{4,15},{5,14},{6,13},{7,12},{8,3},{9,2},... | collective-permute-start | bytes 344072 | tf_op jit(solution)/shard_map/ppermute | solution.py:283
  69.2 11.8 %collective-permute-start.14 = (bf16[32,1792]{1,0:T(8,128)(2,1)S(1)}, bf16[32,1792]{1,0:T(8,128)(2,1)S(1)}, u32[]{:S(2)}, u32[]{:S(2)}) collective-permute-start(bf16[32,1792]{1,0:T(8,128)(2,1)S(1)} %get-tuple-element.86), channel_id=1, source_target_pairs={{0,4},{1,5},{2,6},{3,7},{4,0},{5,1},{6,2},{7,3},{8,12},{9,13},{10,... | collective-permute-start | bytes 344072 | tf_op jit(solution)/shard_map/ppermute | solution.py:283
  73.9 10.9 %collective-permute-start.15 = (bf16[32,1792]{1,0:T(8,128)(2,1)S(1)}, bf16[32,1792]{1,0:T(8,128)(2,1)S(1)}, u32[]{:S(2)}, u32[]{:S(2)}) collective-permute-start(bf16[32,1792]{1,0:T(8,128)(2,1)S(1)} %get-tuple-element.87), channel_id=1, source_target_pairs={{0,15},{1,14},{2,13},{3,12},{4,11},{5,10},{6,9},{7,8},{8,7},{9,6},... | collective-permute-start | bytes 344072 | tf_op jit(solution)/shard_map/ppermute | solution.py:283
  76.0 16.1 %collective-permute-start.30 = (bf16[2,48,512]{2,1,0:T(8,128)(2,1)S(1)}, bf16[2,48,512]{2,1,0:T(8,128)(2,1)S(1)}, u32[]{:S(2)}, u32[]{:S(2)}) collective-permute-start(bf16[2,48,512]{2,1,0:T(8,128)(2,1)S(1)} %get-tuple-element.104), channel_id=1, source_target_pairs={{0,8},{1,9},{2,10},{3,11},{4,12},{5,13},{6,14},{7,15},{8,0},{9,1},... | collective-permute-start | bytes 294920 | tf_op jit(solution)/shard_map/ppermute | solution.py:283
  79.3 12.8 %collective-permute-start.31 = (bf16[2,48,512]{2,1,0:T(8,128)(2,1)S(1)}, bf16[2,48,512]{2,1,0:T(8,128)(2,1)S(1)}, u32[]{:S(2)}, u32[]{:S(2)}) collective-permute-start(bf16[2,48,512]{2,1,0:T(8,128)(2,1)S(1)} %get-tuple-element.105), channel_id=1, source_target_pairs={{0,7},{1,6},{2,5},{3,4},{4,3},{5,2},{6,1},{7,0},{8,15},{9,14},{10,... | collective-permute-start | bytes 294920 | tf_op jit(solution)/shard_map/ppermute | solution.py:283
  79.5 14.9 %collective-permute-start.32 = (bf16[2,48,512]{2,1,0:T(8,128)(2,1)S(1)}, bf16[2,48,512]{2,1,0:T(8,128)(2,1)S(1)}, u32[]{:S(2)}, u32[]{:S(2)}) collective-permute-start(bf16[2,48,512]{2,1,0:T(8,128)(2,1)S(1)} %get-tuple-element.106), channel_id=1, source_target_pairs={{0,12},{1,13},{2,14},{3,15},{4,8},{5,9},{6,10},{7,11},{8,4},{9,5},... | collective-permute-start | bytes 294920 | tf_op jit(solution)/shard_map/ppermute | solution.py:283
  81.1 13.4 %collective-permute-start.33 = (bf16[2,48,512]{2,1,0:T(8,128)(2,1)S(1)}, bf16[2,48,512]{2,1,0:T(8,128)(2,1)S(1)}, u32[]{:S(2)}, u32[]{:S(2)}) collective-permute-start(bf16[2,48,512]{2,1,0:T(8,128)(2,1)S(1)} %get-tuple-element.107), channel_id=1, source_target_pairs={{0,3},{1,2},{2,1},{3,0},{4,7},{5,6},{6,5},{7,4},{8,11},{9,10},{10,... | collective-permute-start | bytes 294920 | tf_op jit(solution)/shard_map/ppermute | solution.py:283
  84.8 15.9 %collective-permute-start.34 = (bf16[2,48,512]{2,1,0:T(8,128)(2,1)S(1)}, bf16[2,48,512]{2,1,0:T(8,128)(2,1)S(1)}, u32[]{:S(2)}, u32[]{:S(2)}) collective-permute-start(bf16[2,48,512]{2,1,0:T(8,128)(2,1)S(1)} %get-tuple-element.108), channel_id=1, source_target_pairs={{0,9},{1,8},{2,11},{3,10},{4,13},{5,12},{6,15},{7,14},{8,1},{9,0},... | collective-permute-start | bytes 294920 | tf_op jit(solution)/shard_map/ppermute | solution.py:283
  92.1 9.6 %collective-permute-start.35 = (bf16[2,48,512]{2,1,0:T(8,128)(2,1)S(1)}, bf16[2,48,512]{2,1,0:T(8,128)(2,1)S(1)}, u32[]{:S(2)}, u32[]{:S(2)}) collective-permute-start(bf16[2,48,512]{2,1,0:T(8,128)(2,1)S(1)} %get-tuple-element.109), channel_id=1, source_target_pairs={{0,6},{1,7},{2,4},{3,5},{4,2},{5,3},{6,0},{7,1},{8,14},{9,15},{10,... | collective-permute-start | bytes 294920 | tf_op jit(solution)/shard_map/ppermute | solution.py:283
  92.1 9.6 %collective-permute-start.36 = (bf16[2,48,512]{2,1,0:T(8,128)(2,1)S(1)}, bf16[2,48,512]{2,1,0:T(8,128)(2,1)S(1)}, u32[]{:S(2)}, u32[]{:S(2)}) collective-permute-start(bf16[2,48,512]{2,1,0:T(8,128)(2,1)S(1)} %get-tuple-element.110), channel_id=1, source_target_pairs={{0,13},{1,12},{2,15},{3,14},{4,9},{5,8},{6,11},{7,10},{8,5},{9,4},... | collective-permute-start | bytes 294920 | tf_op jit(solution)/shard_map/ppermute | solution.py:283
  94.5 11.4 %collective-permute-start.38 = (bf16[2,48,512]{2,1,0:T(8,128)(2,1)S(1)}, bf16[2,48,512]{2,1,0:T(8,128)(2,1)S(1)}, u32[]{:S(2)}, u32[]{:S(2)}) collective-permute-start(bf16[2,48,512]{2,1,0:T(8,128)(2,1)S(1)} %get-tuple-element.112), channel_id=1, source_target_pairs={{0,10},{1,11},{2,8},{3,9},{4,14},{5,15},{6,12},{7,13},{8,2},{9,3},... | collective-permute-start | bytes 294920 | tf_op jit(solution)/shard_map/ppermute | solution.py:283
  101.9 12.0 %collective-permute-start.42 = (bf16[2,48,512]{2,1,0:T(8,128)(2,1)S(1)}, bf16[2,48,512]{2,1,0:T(8,128)(2,1)S(1)}, u32[]{:S(2)}, u32[]{:S(2)}) collective-permute-start(bf16[2,48,512]{2,1,0:T(8,128)(2,1)S(1)} %get-tuple-element.116), channel_id=1, source_target_pairs={{0,11},{1,10},{2,9},{3,8},{4,15},{5,14},{6,13},{7,12},{8,3},{9,2},... | collective-permute-start | bytes 294920 | tf_op jit(solution)/shard_map/ppermute | solution.py:283
  (36 other events, 391.4 us)

commit v17 on v10

--- a/solution.py
+++ b/solution.py
@@ -227,6 +227,30 @@
     return weight_new, moment_new, produced
 
 
+def emit_kernel(weight_ref, moment_ref, weight_out_ref, moment_out_ref, sem):
+    copies = [
+        pltpu.make_async_copy(source, target, sem.at[n])
+        for n, (source, target) in enumerate(((weight_ref, weight_out_ref), (moment_ref, moment_out_ref)))
+    ]
+    for copy in copies:
+        copy.start()
+    for copy in copies:
+        copy.wait()
+
+
+def emit(weight, moment):
+    shape = jax.ShapeDtypeStruct(weight.shape, BF16)
+    return pl.pallas_call(
+        emit_kernel,
+        out_shape=(shape, shape),
+        in_specs=[VMEM, VMEM],
+        out_specs=(HBM, HBM),
+        scratch_shapes=[pltpu.SemaphoreType.DMA((2,))],
+        cost_estimate=pl.CostEstimate(flops=0, bytes_accessed=8 * weight.size, transcendentals=0),
+        name="emit",
+    )(weight, moment)
+
+
 def finish_kernel(groups, slot_ref, gates_ref, *refs):
     pieces, (out_ref, returned_ref) = refs[:groups], refs[groups:]
     capacity = pieces[0].shape[0]
@@ -292,6 +316,7 @@
     received = swap(packed)
     placed = swap(reorder(me, perm, spread, received[groups // 3]))
     weight_new, moment_new, produced = update(me, received, placed, ff, d)
+    weight_new, moment_new = emit(weight_new, moment_new)
     return weight_new[None], moment_new[None], finish(fwd_slot, gates, swap(produced))
 
 

time: 149 us -> 151 us (1.013)
  waiting for transfers between devices: 24.5 us -> 21.6 us
  Pallas kernels: 12.3 us -> 14.4 us
  local copies, waits for them, and re-layouts: 0.66 us -> 2.48 us
    ppermute x60, waiting for transfers between devices: 24.5 us -> 21.6 us  [swap(): lax.ppermute(piece, 'expert', [(i, i ^ s) for i in range(groups)])]
    pallas_call x0 -> x1, Pallas kernels: none -> 2.52 us  [emit(): pl.pallas_call(emit_kernel, out_shape=(shape, shape), in_specs=[VMEM, VME...]
    unnamed x16 -> x20, local copies, waits for them, and re-layouts: 0.66 us -> 2.48 us
  transfers between devices with their start and end apart: 60 -> 60, of which waited for: 12 -> 11; matrix products, arithmetic and copies ran while one was open for 0% -> 0% of each run, Pallas kernels for 2% -> 4%
where the time goes in v17:
time: 151 us
  starting transfers between devices  111 us (74%)
  waiting for transfers between devices  21.6 us (14%)
  Pallas kernels  14.4 us (10%)
  local copies, waits for them, and re-layouts  2.48 us (2%)
  between operations  1.54 us (1%)
    ppermute x60, starting transfers between devices, swap(): lax.ppermute(piece, 'expert', [(i, i ^ s) for i in range(groups)])  111 us
    ppermute x60, waiting for transfers between devices, swap(): lax.ppermute(piece, 'expert', [(i, i ^ s) for i in range(groups)])  21.6 us
    pallas_call x1, Pallas kernels, update(): pl.pallas_call(functools.partial(update_kernel, groups), out_shape=(shape...  4.32 us
  transfers between devices with their start and end apart: 60, of which 11 were waited for; matrix products, arithmetic and copies ran while one was open for 0% of the time, Pallas kernels for 4%

profile of v17, /device:TPU:0, one launch (start us, length us, event | category | flops | bytes accessed | tf_op | source)
XLA Modules:
  0.0 150.8 jit_solution(16892578111000180828)
XLA Ops:
  0.7 2.7 %split.1 = (bf16[2,48,512]{2,1,0:T(8,128)(2,1)}, bf16[2,48,512]{2,1,0:T(8,128)(2,1)}, bf16[2,48,512]{2,1,0:T(8,128)(2,1)}, bf16[2,48,512]{2,1,0:T(8,128)(2,1)}, ...) custom-call(s32[1]{0:T(128)} %bitcast.me_ref, ...), custom_call_target="tpu_custom_call" | custom-call | bytes 3145728 | tf_op jit(solution)/shard_map/split/pallas_call | solution.py:135
  3.4 2.5 %collective-permute-start = (bf16[2,48,512]{2,1,0:T(8,128)(2,1)}, bf16[2,48,512]{2,1,0:T(8,128)(2,1)S(1)}, u32[]{:S(2)}, u32[]{:S(2)}) collective-permute-start(bf16[2,48,512]{2,1,0:T(8,128)(2,1)} %get-tuple-element.73), channel_id=1, source_target_pairs={{0,5},{1,4},{2,7},{3,6},{4,1},{5,0},{6,3},{7,2},{8,13},{9,12},{10,... | collective-permute-start | bytes 294920 | tf_op jit(solution)/shard_map/ppermute | solution.py:300
  5.9 2.6 %collective-permute-start.16 = (bf16[2,48,512]{2,1,0:T(8,128)(2,1)}, bf16[2,48,512]{2,1,0:T(8,128)(2,1)S(1)}, u32[]{:S(2)}, u32[]{:S(2)}) collective-permute-start(bf16[2,48,512]{2,1,0:T(8,128)(2,1)} %get-tuple-element.91), channel_id=1, source_target_pairs={{0,8},{1,9},{2,10},{3,11},{4,12},{5,13},{6,14},{7,15},{8,0},{9,1},... | collective-permute-start | bytes 294920 | tf_op jit(solution)/shard_map/ppermute | solution.py:300
  16.1 2.8 %collective-permute-start.22 = (bf16[2,48,512]{2,1,0:T(8,128)(2,1)}, bf16[2,48,512]{2,1,0:T(8,128)(2,1)S(1)}, u32[]{:S(2)}, u32[]{:S(2)}) collective-permute-start(bf16[2,48,512]{2,1,0:T(8,128)(2,1)} %get-tuple-element.97), channel_id=1, source_target_pairs={{0,13},{1,12},{2,15},{3,14},{4,9},{5,8},{6,11},{7,10},{8,5},{9,4},... | collective-permute-start | bytes 294920 | tf_op jit(solution)/shard_map/ppermute | solution.py:300
  20.4 3.9 %collective-permute-start.24 = (bf16[2,48,512]{2,1,0:T(8,128)(2,1)}, bf16[2,48,512]{2,1,0:T(8,128)(2,1)S(1)}, u32[]{:S(2)}, u32[]{:S(2)}) collective-permute-start(bf16[2,48,512]{2,1,0:T(8,128)(2,1)} %get-tuple-element.99), channel_id=1, source_target_pairs={{0,10},{1,11},{2,8},{3,9},{4,14},{5,15},{6,12},{7,13},{8,2},{9,3},... | collective-permute-start | bytes 294920 | tf_op jit(solution)/shard_map/ppermute | solution.py:300
  24.3 3.8 %collective-permute-start.25 = (bf16[2,48,512]{2,1,0:T(8,128)(2,1)}, bf16[2,48,512]{2,1,0:T(8,128)(2,1)S(1)}, u32[]{:S(2)}, u32[]{:S(2)}) collective-permute-start(bf16[2,48,512]{2,1,0:T(8,128)(2,1)} %get-tuple-element.100), channel_id=1, source_target_pairs={{0,14},{1,15},{2,12},{3,13},{4,10},{5,11},{6,8},{7,9},{8,6},{9,7},... | collective-permute-start | bytes 294920 | tf_op jit(solution)/shard_map/ppermute | solution.py:300
  28.5 3.2 %collective-permute-start.27 = (bf16[2,48,512]{2,1,0:T(8,128)(2,1)}, bf16[2,48,512]{2,1,0:T(8,128)(2,1)S(1)}, u32[]{:S(2)}, u32[]{:S(2)}) collective-permute-start(bf16[2,48,512]{2,1,0:T(8,128)(2,1)} %get-tuple-element.102), channel_id=1, source_target_pairs={{0,11},{1,10},{2,9},{3,8},{4,15},{5,14},{6,13},{7,12},{8,3},{9,2},... | collective-permute-start | bytes 294920 | tf_op jit(solution)/shard_map/ppermute | solution.py:300
  31.7 2.8 %collective-permute-done.24.refs_9_ = bf16[2,48,512]{2,1,0:T(8,128)(2,1)S(1)} collective-permute-done((bf16[2,48,512]{2,1,0:T(8,128)(2,1)}, bf16[2,48,512]{2,1,0:T(8,128)(2,1)S(1)}, u32[]{:S(2)}, u32[]{:S(2)}) %collective-permute-start.24) | collective-permute-done | bytes 98336 | tf_op jit(solution)/shard_map/ppermute | solution.py:300
  37.5 2.8 %pack_rows.1 = (bf16[32,1792]{1,0:T(8,128)(2,1)S(1)}, bf16[32,1792]{1,0:T(8,128)(2,1)S(1)}, bf16[32,1792]{1,0:T(8,128)(2,1)S(1)}, bf16[32,1792]{1,0:T(8,128)(2,1...) custom-call(s32[1]{0:T(128)S(6)} %copy.13.live_ref, ...), custom_call_target="tpu_custom_call" | custom-call | flops 469762048 | bytes 2752512 | tf_op jit(solution)/shard_map/pack_rows/pallas_call | solution.py:107
  40.7 2.7 %collective-permute-start.2 = (bf16[32,1792]{1,0:T(8,128)(2,1)S(1)}, bf16[32,1792]{1,0:T(8,128)(2,1)S(1)}, u32[]{:S(2)}, u32[]{:S(2)}) collective-permute-start(bf16[32,1792]{1,0:T(8,128)(2,1)S(1)} %get-tuple-element.76), channel_id=1, source_target_pairs={{0,7},{1,6},{2,5},{3,4},{4,3},{5,2},{6,1},{7,0},{8,15},{9,14},{10,... | collective-permute-start | bytes 344072 | tf_op jit(solution)/shard_map/ppermute | solution.py:300
  43.4 5.0 %collective-permute-start.3 = (bf16[32,1792]{1,0:T(8,128)(2,1)S(1)}, bf16[32,1792]{1,0:T(8,128)(2,1)S(1)}, u32[]{:S(2)}, u32[]{:S(2)}) collective-permute-start(bf16[32,1792]{1,0:T(8,128)(2,1)S(1)} %get-tuple-element.77), channel_id=1, source_target_pairs={{0,12},{1,13},{2,14},{3,15},{4,8},{5,9},{6,10},{7,11},{8,4},{9,5},... | collective-permute-start | bytes 344072 | tf_op jit(solution)/shard_map/ppermute | solution.py:300
  50.5 5.6 %collective-permute-start.7 = (bf16[32,1792]{1,0:T(8,128)(2,1)S(1)}, bf16[32,1792]{1,0:T(8,128)(2,1)S(1)}, u32[]{:S(2)}, u32[]{:S(2)}) collective-permute-start(bf16[32,1792]{1,0:T(8,128)(2,1)S(1)} %get-tuple-element.81), channel_id=1, source_target_pairs={{0,13},{1,12},{2,15},{3,14},{4,9},{5,8},{6,11},{7,10},{8,5},{9,4},... | collective-permute-start | bytes 344072 | tf_op jit(solution)/shard_map/ppermute | solution.py:300
  56.1 4.4 %collective-permute-start.9 = (bf16[32,1792]{1,0:T(8,128)(2,1)S(1)}, bf16[32,1792]{1,0:T(8,128)(2,1)S(1)}, u32[]{:S(2)}, u32[]{:S(2)}) collective-permute-start(bf16[32,1792]{1,0:T(8,128)(2,1)S(1)} %get-tuple-element.83), channel_id=1, source_target_pairs={{0,10},{1,11},{2,8},{3,9},{4,14},{5,15},{6,12},{7,13},{8,2},{9,3},... | collective-permute-start | bytes 344072 | tf_op jit(solution)/shard_map/ppermute | solution.py:300
  60.5 3.8 %collective-permute-start.11 = (bf16[32,1792]{1,0:T(8,128)(2,1)S(1)}, bf16[32,1792]{1,0:T(8,128)(2,1)S(1)}, u32[]{:S(2)}, u32[]{:S(2)}) collective-permute-start(bf16[32,1792]{1,0:T(8,128)(2,1)S(1)} %get-tuple-element.85), channel_id=1, source_target_pairs={{0,14},{1,15},{2,12},{3,13},{4,10},{5,11},{6,8},{7,9},{8,6},{9,7},... | collective-permute-start | bytes 344072 | tf_op jit(solution)/shard_map/ppermute | solution.py:300
  64.6 4.3 %collective-permute-start.13 = (bf16[32,1792]{1,0:T(8,128)(2,1)S(1)}, bf16[32,1792]{1,0:T(8,128)(2,1)S(1)}, u32[]{:S(2)}, u32[]{:S(2)}) collective-permute-start(bf16[32,1792]{1,0:T(8,128)(2,1)S(1)} %get-tuple-element.87), channel_id=1, source_target_pairs={{0,11},{1,10},{2,9},{3,8},{4,15},{5,14},{6,13},{7,12},{8,3},{9,2},... | collective-permute-start | bytes 344072 | tf_op jit(solution)/shard_map/ppermute | solution.py:300
  69.0 2.2 %collective-permute-start.14 = (bf16[32,1792]{1,0:T(8,128)(2,1)S(1)}, bf16[32,1792]{1,0:T(8,128)(2,1)S(1)}, u32[]{:S(2)}, u32[]{:S(2)}) collective-permute-start(bf16[32,1792]{1,0:T(8,128)(2,1)S(1)} %get-tuple-element.88), channel_id=1, source_target_pairs={{0,4},{1,5},{2,6},{3,7},{4,0},{5,1},{6,2},{7,3},{8,12},{9,13},{10,... | collective-permute-start | bytes 344072 | tf_op jit(solution)/shard_map/ppermute | solution.py:300
  71.1 4.6 %collective-permute-start.15 = (bf16[32,1792]{1,0:T(8,128)(2,1)S(1)}, bf16[32,1792]{1,0:T(8,128)(2,1)S(1)}, u32[]{:S(2)}, u32[]{:S(2)}) collective-permute-start(bf16[32,1792]{1,0:T(8,128)(2,1)S(1)} %get-tuple-element.89), channel_id=1, source_target_pairs={{0,15},{1,14},{2,13},{3,12},{4,11},{5,10},{6,9},{7,8},{8,7},{9,6},... | collective-permute-start | bytes 344072 | tf_op jit(solution)/shard_map/ppermute | solution.py:300
  76.5 2.4 %collective-permute-start.30 = (bf16[2,48,512]{2,1,0:T(8,128)(2,1)S(1)}, bf16[2,48,512]{2,1,0:T(8,128)(2,1)S(1)}, u32[]{:S(2)}, u32[]{:S(2)}) collective-permute-start(bf16[2,48,512]{2,1,0:T(8,128)(2,1)S(1)} %get-tuple-element.106), channel_id=1, source_target_pairs={{0,8},{1,9},{2,10},{3,11},{4,12},{5,13},{6,14},{7,15},{8,0},{9,1},... | collective-permute-start | bytes 294920 | tf_op jit(solution)/shard_map/ppermute | solution.py:300
  83.0 3.6 %collective-permute-start.33 = (bf16[2,48,512]{2,1,0:T(8,128)(2,1)S(1)}, bf16[2,48,512]{2,1,0:T(8,128)(2,1)S(1)}, u32[]{:S(2)}, u32[]{:S(2)}) collective-permute-start(bf16[2,48,512]{2,1,0:T(8,128)(2,1)S(1)} %get-tuple-element.109), channel_id=1, source_target_pairs={{0,3},{1,2},{2,1},{3,0},{4,7},{5,6},{6,5},{7,4},{8,11},{9,10},{10,... | collective-permute-start | bytes 294920 | tf_op jit(solution)/shard_map/ppermute | solution.py:300
  87.7 3.1 %collective-permute-done.30.refs_17_ = bf16[2,48,512]{2,1,0:T(8,128)(2,1)S(1)} collective-permute-done((bf16[2,48,512]{2,1,0:T(8,128)(2,1)S(1)}, bf16[2,48,512]{2,1,0:T(8,128)(2,1)S(1)}, u32[]{:S(2)}, u32[]{:S(2)}) %collective-permute-start.30) | collective-permute-done | bytes 98336 | tf_op jit(solution)/shard_map/ppermute | solution.py:300
  94.0 3.7 %collective-permute-start.38 = (bf16[2,48,512]{2,1,0:T(8,128)(2,1)S(1)}, bf16[2,48,512]{2,1,0:T(8,128)(2,1)S(1)}, u32[]{:S(2)}, u32[]{:S(2)}) collective-permute-start(bf16[2,48,512]{2,1,0:T(8,128)(2,1)S(1)} %get-tuple-element.114), channel_id=1, source_target_pairs={{0,10},{1,11},{2,8},{3,9},{4,14},{5,15},{6,12},{7,13},{8,2},{9,3},... | collective-permute-start | bytes 294920 | tf_op jit(solution)/shard_map/ppermute | solution.py:300
  97.7 2.6 %collective-permute-done.35.refs_22_ = bf16[2,48,512]{2,1,0:T(8,128)(2,1)S(1)} collective-permute-done((bf16[2,48,512]{2,1,0:T(8,128)(2,1)S(1)}, bf16[2,48,512]{2,1,0:T(8,128)(2,1)S(1)}, u32[]{:S(2)}, u32[]{:S(2)}) %collective-permute-start.35) | collective-permute-done | bytes 98336 | tf_op jit(solution)/shard_map/ppermute | solution.py:300
  100.3 2.6 %collective-permute-start.40 = (bf16[2,48,512]{2,1,0:T(8,128)(2,1)S(1)}, bf16[2,48,512]{2,1,0:T(8,128)(2,1)S(1)}, u32[]{:S(2)}, u32[]{:S(2)}) collective-permute-start(bf16[2,48,512]{2,1,0:T(8,128)(2,1)S(1)} %get-tuple-element.116), channel_id=1, source_target_pairs={{0,14},{1,15},{2,12},{3,13},{4,10},{5,11},{6,8},{7,9},{8,6},{9,7},... | collective-permute-start | bytes 294920 | tf_op jit(solution)/shard_map/ppermute | solution.py:300
  102.9 3.0 %collective-permute-start.42 = (bf16[2,48,512]{2,1,0:T(8,128)(2,1)S(1)}, bf16[2,48,512]{2,1,0:T(8,128)(2,1)S(1)}, u32[]{:S(2)}, u32[]{:S(2)}) collective-permute-start(bf16[2,48,512]{2,1,0:T(8,128)(2,1)S(1)} %get-tuple-element.118), channel_id=1, source_target_pairs={{0,11},{1,10},{2,9},{3,8},{4,15},{5,14},{6,13},{7,12},{8,3},{9,2},... | collective-permute-start | bytes 294920 | tf_op jit(solution)/shard_map/ppermute | solution.py:300
  107.8 7.4 %collective-permute-done.42.refs_29_ = bf16[2,48,512]{2,1,0:T(8,128)(2,1)S(1)} collective-permute-done((bf16[2,48,512]{2,1,0:T(8,128)(2,1)S(1)}, bf16[2,48,512]{2,1,0:T(8,128)(2,1)S(1)}, u32[]{:S(2)}, u32[]{:S(2)}) %collective-permute-start.42) | collective-permute-done | bytes 98336 | tf_op jit(solution)/shard_map/ppermute | solution.py:300
  115.2 4.3 %update.1 = (bf16[384,1024]{1,0:T(8,128)(2,1)S(1)}, bf16[384,1024]{1,0:T(8,128)(2,1)S(1)}, bf16[32,1024]{1,0:T(8,128)(2,1)S(1)}, bf16[32,1024]{1,0:T(8,128)(2,1)...) custom-call(s32[1]{0:T(128)} %bitcast.me_ref, ...), custom_call_target="tpu_custom_call" | custom-call | flops 2239758336 | bytes 6029312 | tf_op jit(solution)/shard_map/update/pallas_call | solution.py:213
  121.3 3.9 %collective-permute-start.45 = (bf16[32,1024]{1,0:T(8,128)(2,1)S(1)}, bf16[32,1024]{1,0:T(8,128)(2,1)S(1)}, u32[]{:S(2)}, u32[]{:S(2)}) collective-permute-start(bf16[32,1024]{1,0:T(8,128)(2,1)S(1)} %get-tuple-element.128), channel_id=1, source_target_pairs={{0,8},{1,9},{2,10},{3,11},{4,12},{5,13},{6,14},{7,15},{8,0},{9,1},... | collective-permute-start | bytes 196616 | tf_op jit(solution)/shard_map/ppermute | solution.py:300
  133.6 2.7 %collective-permute-start.53 = (bf16[32,1024]{1,0:T(8,128)(2,1)S(1)}, bf16[32,1024]{1,0:T(8,128)(2,1)S(1)}, u32[]{:S(2)}, u32[]{:S(2)}) collective-permute-start(bf16[32,1024]{1,0:T(8,128)(2,1)S(1)} %get-tuple-element.136), channel_id=1, source_target_pairs={{0,10},{1,11},{2,8},{3,9},{4,14},{5,15},{6,12},{7,13},{8,2},{9,3},... | collective-permute-start | bytes 196616 | tf_op jit(solution)/shard_map/ppermute | solution.py:300
  136.4 2.9 %collective-permute-start.55 = (bf16[32,1024]{1,0:T(8,128)(2,1)S(1)}, bf16[32,1024]{1,0:T(8,128)(2,1)S(1)}, u32[]{:S(2)}, u32[]{:S(2)}) collective-permute-start(bf16[32,1024]{1,0:T(8,128)(2,1)S(1)} %get-tuple-element.138), channel_id=1, source_target_pairs={{0,14},{1,15},{2,12},{3,13},{4,10},{5,11},{6,8},{7,9},{8,6},{9,7},... | collective-permute-start | bytes 196616 | tf_op jit(solution)/shard_map/ppermute | solution.py:300
  139.5 2.7 %collective-permute-start.57 = (bf16[32,1024]{1,0:T(8,128)(2,1)S(1)}, bf16[32,1024]{1,0:T(8,128)(2,1)S(1)}, u32[]{:S(2)}, u32[]{:S(2)}) collective-permute-start(bf16[32,1024]{1,0:T(8,128)(2,1)S(1)} %get-tuple-element.140), channel_id=1, source_target_pairs={{0,11},{1,10},{2,9},{3,8},{4,15},{5,14},{6,13},{7,12},{8,3},{9,2},... | collective-permute-start | bytes 196616 | tf_op jit(solution)/shard_map/ppermute | solution.py:300
  142.7 2.2 %collective-permute-start.59 = (bf16[32,1024]{1,0:T(8,128)(2,1)S(1)}, bf16[32,1024]{1,0:T(8,128)(2,1)S(1)}, u32[]{:S(2)}, u32[]{:S(2)}) collective-permute-start(bf16[32,1024]{1,0:T(8,128)(2,1)S(1)} %get-tuple-element.142), channel_id=1, source_target_pairs={{0,15},{1,14},{2,13},{3,12},{4,11},{5,10},{6,9},{7,8},{8,7},{9,6},... | collective-permute-start | bytes 196616 | tf_op jit(solution)/shard_map/ppermute | solution.py:300
  144.9 2.5 %emit.1 = (bf16[384,1024]{1,0:T(8,128)(2,1)}, bf16[384,1024]{1,0:T(8,128)(2,1)}) custom-call(bf16[384,1024]{1,0:T(8,128)(2,1)} %copy-done, bf16[384,1024]{1,0:T(8,128)(2,1)} %copy-done.1), custom_call_target="tpu_custom_call" | custom-call | bytes 3145728 | tf_op jit(solution)/shard_map/emit/pallas_call | solution.py:243
  (114 shorter events, 40.1 us)
Async XLA Ops:
  11.3 13.0 %collective-permute-start.20 = (bf16[2,48,512]{2,1,0:T(8,128)(2,1)}, bf16[2,48,512]{2,1,0:T(8,128)(2,1)S(1)}, u32[]{:S(2)}, u32[]{:S(2)}) collective-permute-start(bf16[2,48,512]{2,1,0:T(8,128)(2,1)} %get-tuple-element.95), channel_id=1, source_target_pairs={{0,9},{1,8},{2,11},{3,10},{4,13},{5,12},{6,15},{7,14},{8,1},{9,0},... | collective-permute-start | bytes 294920 | tf_op jit(solution)/shard_map/ppermute | solution.py:300
  14.5 13.6 %collective-permute-start.21 = (bf16[2,48,512]{2,1,0:T(8,128)(2,1)}, bf16[2,48,512]{2,1,0:T(8,128)(2,1)S(1)}, u32[]{:S(2)}, u32[]{:S(2)}) collective-permute-start(bf16[2,48,512]{2,1,0:T(8,128)(2,1)} %get-tuple-element.96), channel_id=1, source_target_pairs={{0,6},{1,7},{2,4},{3,5},{4,2},{5,3},{6,0},{7,1},{8,14},{9,15},{10,... | collective-permute-start | bytes 294920 | tf_op jit(solution)/shard_map/ppermute | solution.py:300
  16.1 12.3 %collective-permute-start.22 = (bf16[2,48,512]{2,1,0:T(8,128)(2,1)}, bf16[2,48,512]{2,1,0:T(8,128)(2,1)S(1)}, u32[]{:S(2)}, u32[]{:S(2)}) collective-permute-start(bf16[2,48,512]{2,1,0:T(8,128)(2,1)} %get-tuple-element.97), channel_id=1, source_target_pairs={{0,13},{1,12},{2,15},{3,14},{4,9},{5,8},{6,11},{7,10},{8,5},{9,4},... | collective-permute-start | bytes 294920 | tf_op jit(solution)/shard_map/ppermute | solution.py:300
  18.9 12.7 %collective-permute-start.23 = (bf16[2,48,512]{2,1,0:T(8,128)(2,1)}, bf16[2,48,512]{2,1,0:T(8,128)(2,1)S(1)}, u32[]{:S(2)}, u32[]{:S(2)}) collective-permute-start(bf16[2,48,512]{2,1,0:T(8,128)(2,1)} %get-tuple-element.98), channel_id=1, source_target_pairs={{0,2},{1,3},{2,0},{3,1},{4,6},{5,7},{6,4},{7,5},{8,10},{9,11},{10,... | collective-permute-start | bytes 294920 | tf_op jit(solution)/shard_map/ppermute | solution.py:300
  20.4 14.1 %collective-permute-start.24 = (bf16[2,48,512]{2,1,0:T(8,128)(2,1)}, bf16[2,48,512]{2,1,0:T(8,128)(2,1)S(1)}, u32[]{:S(2)}, u32[]{:S(2)}) collective-permute-start(bf16[2,48,512]{2,1,0:T(8,128)(2,1)} %get-tuple-element.99), channel_id=1, source_target_pairs={{0,10},{1,11},{2,8},{3,9},{4,14},{5,15},{6,12},{7,13},{8,2},{9,3},... | collective-permute-start | bytes 294920 | tf_op jit(solution)/shard_map/ppermute | solution.py:300
  24.3 16.0 %collective-permute-start.25 = (bf16[2,48,512]{2,1,0:T(8,128)(2,1)}, bf16[2,48,512]{2,1,0:T(8,128)(2,1)S(1)}, u32[]{:S(2)}, u32[]{:S(2)}) collective-permute-start(bf16[2,48,512]{2,1,0:T(8,128)(2,1)} %get-tuple-element.100), channel_id=1, source_target_pairs={{0,14},{1,15},{2,12},{3,13},{4,10},{5,11},{6,8},{7,9},{8,6},{9,7},... | collective-permute-start | bytes 294920 | tf_op jit(solution)/shard_map/ppermute | solution.py:300
  28.1 12.6 %collective-permute-start.26 = (bf16[2,48,512]{2,1,0:T(8,128)(2,1)}, bf16[2,48,512]{2,1,0:T(8,128)(2,1)S(1)}, u32[]{:S(2)}, u32[]{:S(2)}) collective-permute-start(bf16[2,48,512]{2,1,0:T(8,128)(2,1)} %get-tuple-element.101), channel_id=1, source_target_pairs={{0,1},{1,0},{2,3},{3,2},{4,5},{5,4},{6,7},{7,6},{8,9},{9,8},{10,11... | collective-permute-start | bytes 294920 | tf_op jit(solution)/shard_map/ppermute | solution.py:300
  28.5 14.9 %collective-permute-start.27 = (bf16[2,48,512]{2,1,0:T(8,128)(2,1)}, bf16[2,48,512]{2,1,0:T(8,128)(2,1)S(1)}, u32[]{:S(2)}, u32[]{:S(2)}) collective-permute-start(bf16[2,48,512]{2,1,0:T(8,128)(2,1)} %get-tuple-element.102), channel_id=1, source_target_pairs={{0,11},{1,10},{2,9},{3,8},{4,15},{5,14},{6,13},{7,12},{8,3},{9,2},... | collective-permute-start | bytes 294920 | tf_op jit(solution)/shard_map/ppermute | solution.py:300
  31.7 16.8 %collective-permute-start.28 = (bf16[2,48,512]{2,1,0:T(8,128)(2,1)}, bf16[2,48,512]{2,1,0:T(8,128)(2,1)S(1)}, u32[]{:S(2)}, u32[]{:S(2)}) collective-permute-start(bf16[2,48,512]{2,1,0:T(8,128)(2,1)} %get-tuple-element.103), channel_id=1, source_target_pairs={{0,4},{1,5},{2,6},{3,7},{4,0},{5,1},{6,2},{7,3},{8,12},{9,13},{10,... | collective-permute-start | bytes 294920 | tf_op jit(solution)/shard_map/ppermute | solution.py:300
  34.4 14.0 %collective-permute-start.29 = (bf16[2,48,512]{2,1,0:T(8,128)(2,1)}, bf16[2,48,512]{2,1,0:T(8,128)(2,1)S(1)}, u32[]{:S(2)}, u32[]{:S(2)}) collective-permute-start(bf16[2,48,512]{2,1,0:T(8,128)(2,1)} %get-tuple-element.104), channel_id=1, source_target_pairs={{0,15},{1,14},{2,13},{3,12},{4,11},{5,10},{6,9},{7,8},{8,7},{9,6},... | collective-permute-start | bytes 294920 | tf_op jit(solution)/shard_map/ppermute | solution.py:300
  40.7 9.8 %collective-permute-start.2 = (bf16[32,1792]{1,0:T(8,128)(2,1)S(1)}, bf16[32,1792]{1,0:T(8,128)(2,1)S(1)}, u32[]{:S(2)}, u32[]{:S(2)}) collective-permute-start(bf16[32,1792]{1,0:T(8,128)(2,1)S(1)} %get-tuple-element.76), channel_id=1, source_target_pairs={{0,7},{1,6},{2,5},{3,4},{4,3},{5,2},{6,1},{7,0},{8,15},{9,14},{10,... | collective-permute-start | bytes 344072 | tf_op jit(solution)/shard_map/ppermute | solution.py:300
  43.4 12.7 %collective-permute-start.3 = (bf16[32,1792]{1,0:T(8,128)(2,1)S(1)}, bf16[32,1792]{1,0:T(8,128)(2,1)S(1)}, u32[]{:S(2)}, u32[]{:S(2)}) collective-permute-start(bf16[32,1792]{1,0:T(8,128)(2,1)S(1)} %get-tuple-element.77), channel_id=1, source_target_pairs={{0,12},{1,13},{2,14},{3,15},{4,8},{5,9},{6,10},{7,11},{8,4},{9,5},... | collective-permute-start | bytes 344072 | tf_op jit(solution)/shard_map/ppermute | solution.py:300
  48.4 12.1 %collective-permute-start.5 = (bf16[32,1792]{1,0:T(8,128)(2,1)S(1)}, bf16[32,1792]{1,0:T(8,128)(2,1)S(1)}, u32[]{:S(2)}, u32[]{:S(2)}) collective-permute-start(bf16[32,1792]{1,0:T(8,128)(2,1)S(1)} %get-tuple-element.79), channel_id=1, source_target_pairs={{0,9},{1,8},{2,11},{3,10},{4,13},{5,12},{6,15},{7,14},{8,1},{9,0},... | collective-permute-start | bytes 344072 | tf_op jit(solution)/shard_map/ppermute | solution.py:300
  49.0 11.5 %collective-permute-start.6 = (bf16[32,1792]{1,0:T(8,128)(2,1)S(1)}, bf16[32,1792]{1,0:T(8,128)(2,1)S(1)}, u32[]{:S(2)}, u32[]{:S(2)}) collective-permute-start(bf16[32,1792]{1,0:T(8,128)(2,1)S(1)} %get-tuple-element.80), channel_id=1, source_target_pairs={{0,6},{1,7},{2,4},{3,5},{4,2},{5,3},{6,0},{7,1},{8,14},{9,15},{10,... | collective-permute-start | bytes 344072 | tf_op jit(solution)/shard_map/ppermute | solution.py:300
  50.5 13.8 %collective-permute-start.7 = (bf16[32,1792]{1,0:T(8,128)(2,1)S(1)}, bf16[32,1792]{1,0:T(8,128)(2,1)S(1)}, u32[]{:S(2)}, u32[]{:S(2)}) collective-permute-start(bf16[32,1792]{1,0:T(8,128)(2,1)S(1)} %get-tuple-element.81), channel_id=1, source_target_pairs={{0,13},{1,12},{2,15},{3,14},{4,9},{5,8},{6,11},{7,10},{8,5},{9,4},... | collective-permute-start | bytes 344072 | tf_op jit(solution)/shard_map/ppermute | solution.py:300
  56.1 12.9 %collective-permute-start.9 = (bf16[32,1792]{1,0:T(8,128)(2,1)S(1)}, bf16[32,1792]{1,0:T(8,128)(2,1)S(1)}, u32[]{:S(2)}, u32[]{:S(2)}) collective-permute-start(bf16[32,1792]{1,0:T(8,128)(2,1)S(1)} %get-tuple-element.83), channel_id=1, source_target_pairs={{0,10},{1,11},{2,8},{3,9},{4,14},{5,15},{6,12},{7,13},{8,2},{9,3},... | collective-permute-start | bytes 344072 | tf_op jit(solution)/shard_map/ppermute | solution.py:300
  60.5 10.6 %collective-permute-start.10 = (bf16[32,1792]{1,0:T(8,128)(2,1)S(1)}, bf16[32,1792]{1,0:T(8,128)(2,1)S(1)}, u32[]{:S(2)}, u32[]{:S(2)}) collective-permute-start(bf16[32,1792]{1,0:T(8,128)(2,1)S(1)} %get-tuple-element.84), channel_id=1, source_target_pairs={{0,5},{1,4},{2,7},{3,6},{4,1},{5,0},{6,3},{7,2},{8,13},{9,12},{10,... | collective-permute-start | bytes 344072 | tf_op jit(solution)/shard_map/ppermute | solution.py:300
  60.5 16.0 %collective-permute-start.11 = (bf16[32,1792]{1,0:T(8,128)(2,1)S(1)}, bf16[32,1792]{1,0:T(8,128)(2,1)S(1)}, u32[]{:S(2)}, u32[]{:S(2)}) collective-permute-start(bf16[32,1792]{1,0:T(8,128)(2,1)S(1)} %get-tuple-element.85), channel_id=1, source_target_pairs={{0,14},{1,15},{2,12},{3,13},{4,10},{5,11},{6,8},{7,9},{8,6},{9,7},... | collective-permute-start | bytes 344072 | tf_op jit(solution)/shard_map/ppermute | solution.py:300
  64.3 14.7 %collective-permute-start.12 = (bf16[32,1792]{1,0:T(8,128)(2,1)S(1)}, bf16[32,1792]{1,0:T(8,128)(2,1)S(1)}, u32[]{:S(2)}, u32[]{:S(2)}) collective-permute-start(bf16[32,1792]{1,0:T(8,128)(2,1)S(1)} %get-tuple-element.86), channel_id=1, source_target_pairs={{0,1},{1,0},{2,3},{3,2},{4,5},{5,4},{6,7},{7,6},{8,9},{9,8},{10,11... | collective-permute-start | bytes 344072 | tf_op jit(solution)/shard_map/ppermute | solution.py:300
  64.6 16.2 %collective-permute-start.13 = (bf16[32,1792]{1,0:T(8,128)(2,1)S(1)}, bf16[32,1792]{1,0:T(8,128)(2,1)S(1)}, u32[]{:S(2)}, u32[]{:S(2)}) collective-permute-start(bf16[32,1792]{1,0:T(8,128)(2,1)S(1)} %get-tuple-element.87), channel_id=1, source_target_pairs={{0,11},{1,10},{2,9},{3,8},{4,15},{5,14},{6,13},{7,12},{8,3},{9,2},... | collective-permute-start | bytes 344072 | tf_op jit(solution)/shard_map/ppermute | solution.py:300
  69.0 14.0 %collective-permute-start.14 = (bf16[32,1792]{1,0:T(8,128)(2,1)S(1)}, bf16[32,1792]{1,0:T(8,128)(2,1)S(1)}, u32[]{:S(2)}, u32[]{:S(2)}) collective-permute-start(bf16[32,1792]{1,0:T(8,128)(2,1)S(1)} %get-tuple-element.88), channel_id=1, source_target_pairs={{0,4},{1,5},{2,6},{3,7},{4,0},{5,1},{6,2},{7,3},{8,12},{9,13},{10,... | collective-permute-start | bytes 344072 | tf_op jit(solution)/shard_map/ppermute | solution.py:300
  71.1 15.4 %collective-permute-start.15 = (bf16[32,1792]{1,0:T(8,128)(2,1)S(1)}, bf16[32,1792]{1,0:T(8,128)(2,1)S(1)}, u32[]{:S(2)}, u32[]{:S(2)}) collective-permute-start(bf16[32,1792]{1,0:T(8,128)(2,1)S(1)} %get-tuple-element.89), channel_id=1, source_target_pairs={{0,15},{1,14},{2,13},{3,12},{4,11},{5,10},{6,9},{7,8},{8,7},{9,6},... | collective-permute-start | bytes 344072 | tf_op jit(solution)/shard_map/ppermute | solution.py:300
  76.5 14.2 %collective-permute-start.30 = (bf16[2,48,512]{2,1,0:T(8,128)(2,1)S(1)}, bf16[2,48,512]{2,1,0:T(8,128)(2,1)S(1)}, u32[]{:S(2)}, u32[]{:S(2)}) collective-permute-start(bf16[2,48,512]{2,1,0:T(8,128)(2,1)S(1)} %get-tuple-element.106), channel_id=1, source_target_pairs={{0,8},{1,9},{2,10},{3,11},{4,12},{5,13},{6,14},{7,15},{8,0},{9,1},... | collective-permute-start | bytes 294920 | tf_op jit(solution)/shard_map/ppermute | solution.py:300
  78.9 11.8 %collective-permute-start.31 = (bf16[2,48,512]{2,1,0:T(8,128)(2,1)S(1)}, bf16[2,48,512]{2,1,0:T(8,128)(2,1)S(1)}, u32[]{:S(2)}, u32[]{:S(2)}) collective-permute-start(bf16[2,48,512]{2,1,0:T(8,128)(2,1)S(1)} %get-tuple-element.107), channel_id=1, source_target_pairs={{0,7},{1,6},{2,5},{3,4},{4,3},{5,2},{6,1},{7,0},{8,15},{9,14},{10,... | collective-permute-start | bytes 294920 | tf_op jit(solution)/shard_map/ppermute | solution.py:300
  80.8 11.7 %collective-permute-start.32 = (bf16[2,48,512]{2,1,0:T(8,128)(2,1)S(1)}, bf16[2,48,512]{2,1,0:T(8,128)(2,1)S(1)}, u32[]{:S(2)}, u32[]{:S(2)}) collective-permute-start(bf16[2,48,512]{2,1,0:T(8,128)(2,1)S(1)} %get-tuple-element.108), channel_id=1, source_target_pairs={{0,12},{1,13},{2,14},{3,15},{4,8},{5,9},{6,10},{7,11},{8,4},{9,5},... | collective-permute-start | bytes 294920 | tf_op jit(solution)/shard_map/ppermute | solution.py:300
  83.0 11.0 %collective-permute-start.33 = (bf16[2,48,512]{2,1,0:T(8,128)(2,1)S(1)}, bf16[2,48,512]{2,1,0:T(8,128)(2,1)S(1)}, u32[]{:S(2)}, u32[]{:S(2)}) collective-permute-start(bf16[2,48,512]{2,1,0:T(8,128)(2,1)S(1)} %get-tuple-element.109), channel_id=1, source_target_pairs={{0,3},{1,2},{2,1},{3,0},{4,7},{5,6},{6,5},{7,4},{8,11},{9,10},{10,... | collective-permute-start | bytes 294920 | tf_op jit(solution)/shard_map/ppermute | solution.py:300
  86.5 11.2 %collective-permute-start.34 = (bf16[2,48,512]{2,1,0:T(8,128)(2,1)S(1)}, bf16[2,48,512]{2,1,0:T(8,128)(2,1)S(1)}, u32[]{:S(2)}, u32[]{:S(2)}) collective-permute-start(bf16[2,48,512]{2,1,0:T(8,128)(2,1)S(1)} %get-tuple-element.110), channel_id=1, source_target_pairs={{0,9},{1,8},{2,11},{3,10},{4,13},{5,12},{6,15},{7,14},{8,1},{9,0},... | collective-permute-start | bytes 294920 | tf_op jit(solution)/shard_map/ppermute | solution.py:300
  90.8 12.1 %collective-permute-start.36 = (bf16[2,48,512]{2,1,0:T(8,128)(2,1)S(1)}, bf16[2,48,512]{2,1,0:T(8,128)(2,1)S(1)}, u32[]{:S(2)}, u32[]{:S(2)}) collective-permute-start(bf16[2,48,512]{2,1,0:T(8,128)(2,1)S(1)} %get-tuple-element.112), channel_id=1, source_target_pairs={{0,13},{1,12},{2,15},{3,14},{4,9},{5,8},{6,11},{7,10},{8,5},{9,4},... | collective-permute-start | bytes 294920 | tf_op jit(solution)/shard_map/ppermute | solution.py:300
  92.6 10.3 %collective-permute-start.37 = (bf16[2,48,512]{2,1,0:T(8,128)(2,1)S(1)}, bf16[2,48,512]{2,1,0:T(8,128)(2,1)S(1)}, u32[]{:S(2)}, u32[]{:S(2)}) collective-permute-start(bf16[2,48,512]{2,1,0:T(8,128)(2,1)S(1)} %get-tuple-element.113), channel_id=1, source_target_pairs={{0,2},{1,3},{2,0},{3,1},{4,6},{5,7},{6,4},{7,5},{8,10},{9,11},{10,... | collective-permute-start | bytes 294920 | tf_op jit(solution)/shard_map/ppermute | solution.py:300
  94.0 12.6 %collective-permute-start.38 = (bf16[2,48,512]{2,1,0:T(8,128)(2,1)S(1)}, bf16[2,48,512]{2,1,0:T(8,128)(2,1)S(1)}, u32[]{:S(2)}, u32[]{:S(2)}) collective-permute-start(bf16[2,48,512]{2,1,0:T(8,128)(2,1)S(1)} %get-tuple-element.114), channel_id=1, source_target_pairs={{0,10},{1,11},{2,8},{3,9},{4,14},{5,15},{6,12},{7,13},{8,2},{9,3},... | collective-permute-start | bytes 294920 | tf_op jit(solution)/shard_map/ppermute | solution.py:300
  102.9 12.3 %collective-permute-start.42 = (bf16[2,48,512]{2,1,0:T(8,128)(2,1)S(1)}, bf16[2,48,512]{2,1,0:T(8,128)(2,1)S(1)}, u32[]{:S(2)}, u32[]{:S(2)}) collective-permute-start(bf16[2,48,512]{2,1,0:T(8,128)(2,1)S(1)} %get-tuple-element.118), channel_id=1, source_target_pairs={{0,11},{1,10},{2,9},{3,8},{4,15},{5,14},{6,13},{7,12},{8,3},{9,2},... | collective-permute-start | bytes 294920 | tf_op jit(solution)/shard_map/ppermute | solution.py:300
  136.4 11.1 %collective-permute-start.55 = (bf16[32,1024]{1,0:T(8,128)(2,1)S(1)}, bf16[32,1024]{1,0:T(8,128)(2,1)S(1)}, u32[]{:S(2)}, u32[]{:S(2)}) collective-permute-start(bf16[32,1024]{1,0:T(8,128)(2,1)S(1)} %get-tuple-element.138), channel_id=1, source_target_pairs={{0,14},{1,15},{2,12},{3,13},{4,10},{5,11},{6,8},{7,9},{8,6},{9,7},... | collective-permute-start | bytes 196616 | tf_op jit(solution)/shard_map/ppermute | solution.py:300
  (38 other events, 400.0 us)

commit v18 on v17

--- a/solution.py
+++ b/solution.py
@@ -111,7 +111,7 @@
         in_specs=[SMEM] * 3 + [HBM] * 6 + [VMEM],
         out_specs=(VMEM,) * (groups + 2),
         scratch_shapes=[pltpu.VMEM(a.shape, a.dtype) for a in sources] + [pltpu.SemaphoreType.DMA((len(sources),))],
-        compiler_params=pltpu.CompilerParams(vmem_limit_bytes=32 * MIB),
+        compiler_params=pltpu.CompilerParams(vmem_limit_bytes=24 * MIB),
         cost_estimate=pl.CostEstimate(
             flops=2 * groups * capacity * rows * width, bytes_accessed=6 * rows * width, transcendentals=0
         ),
@@ -163,7 +163,7 @@
         in_specs=[SMEM, SMEM] + [VMEM] * (groups + 1),
         out_specs=(VMEM,) * groups,
         scratch_shapes=[pltpu.VMEM((groups,) + pieces[0].shape, BF16)],
-        compiler_params=pltpu.CompilerParams(vmem_limit_bytes=32 * MIB),
+        compiler_params=pltpu.CompilerParams(vmem_limit_bytes=12 * MIB),
         cost_estimate=pl.CostEstimate(flops=0, bytes_accessed=4 * groups * pieces[0].size, transcendentals=0),
         name="reorder",
     )(me, perm, *pieces, earlier)
@@ -216,7 +216,7 @@
         in_specs=[SMEM] + [VMEM] * (2 * groups),
         out_specs=(VMEM,) * (groups + 2),
         scratch_shapes=[pltpu.VMEM((2, ff, d), BF16), pltpu.VMEM((slots, width), BF16)],
-        compiler_params=pltpu.CompilerParams(vmem_limit_bytes=40 * MIB),
+        compiler_params=pltpu.CompilerParams(vmem_limit_bytes=24 * MIB),
         cost_estimate=pl.CostEstimate(
             flops=4 * ff * d * slots + 8 * ff * ff * d + 4 * ff**3,
             bytes_accessed=8 * ff * d + 2 * slots * (width + d),
@@ -274,7 +274,7 @@
         in_specs=[VMEM] * (2 + groups),
         out_specs=VMEM,
         scratch_shapes=[pltpu.VMEM((slots, d), BF16)],
-        compiler_params=pltpu.CompilerParams(vmem_limit_bytes=32 * MIB),
+        compiler_params=pltpu.CompilerParams(vmem_limit_bytes=12 * MIB),
         cost_estimate=pl.CostEstimate(
             flops=2 * slots * rows * d, bytes_accessed=2 * d * (slots + rows), transcendentals=0
         ),

time: 151 us -> 151 us (level)
  transfers between devices with their start and end apart: 60 -> 60, of which waited for: 11 -> 12; matrix products, arithmetic and copies ran while one was open for 0% -> 0% of each run, Pallas kernels for 4% -> 4%
where the time goes in v18:
time: 151 us
  starting transfers between devices  110 us (73%)
  waiting for transfers between devices  22.4 us (15%)
  Pallas kernels  14.4 us (10%)
  local copies, waits for them, and re-layouts  2.48 us (2%)
  between operations  1.53 us (1%)
    ppermute x60, starting transfers between devices, swap(): lax.ppermute(piece, 'expert', [(i, i ^ s) for i in range(groups)])  110 us
    ppermute x60, waiting for transfers between devices, swap(): lax.ppermute(piece, 'expert', [(i, i ^ s) for i in range(groups)])  22.4 us
    pallas_call x1, Pallas kernels, update(): pl.pallas_call(functools.partial(update_kernel, groups), out_shape=(shape...  4.32 us
  transfers between devices with their start and end apart: 60, of which 12 were waited for; matrix products, arithmetic and copies ran while one was open for 0% of the time, Pallas kernels for 4%

profile of v18, /device:TPU:0, one launch (start us, length us, event | category | flops | bytes accessed | tf_op | source)
XLA Modules:
  0.0 150.8 jit_solution(11470872709859140992)
XLA Ops:
  0.7 2.7 %split.1 = (bf16[2,48,512]{2,1,0:T(8,128)(2,1)}, bf16[2,48,512]{2,1,0:T(8,128)(2,1)}, bf16[2,48,512]{2,1,0:T(8,128)(2,1)}, bf16[2,48,512]{2,1,0:T(8,128)(2,1)}, ...) custom-call(s32[1]{0:T(128)} %bitcast.me_ref, ...), custom_call_target="tpu_custom_call" | custom-call | bytes 3145728 | tf_op jit(solution)/shard_map/split/pallas_call | solution.py:135
  3.4 2.5 %collective-permute-start = (bf16[2,48,512]{2,1,0:T(8,128)(2,1)}, bf16[2,48,512]{2,1,0:T(8,128)(2,1)S(1)}, u32[]{:S(2)}, u32[]{:S(2)}) collective-permute-start(bf16[2,48,512]{2,1,0:T(8,128)(2,1)} %get-tuple-element.73), channel_id=1, source_target_pairs={{0,5},{1,4},{2,7},{3,6},{4,1},{5,0},{6,3},{7,2},{8,13},{9,12},{10,... | collective-permute-start | bytes 294920 | tf_op jit(solution)/shard_map/ppermute | solution.py:300
  5.9 2.6 %collective-permute-start.16 = (bf16[2,48,512]{2,1,0:T(8,128)(2,1)}, bf16[2,48,512]{2,1,0:T(8,128)(2,1)S(1)}, u32[]{:S(2)}, u32[]{:S(2)}) collective-permute-start(bf16[2,48,512]{2,1,0:T(8,128)(2,1)} %get-tuple-element.91), channel_id=1, source_target_pairs={{0,8},{1,9},{2,10},{3,11},{4,12},{5,13},{6,14},{7,15},{8,0},{9,1},... | collective-permute-start | bytes 294920 | tf_op jit(solution)/shard_map/ppermute | solution.py:300
  16.1 2.8 %collective-permute-start.22 = (bf16[2,48,512]{2,1,0:T(8,128)(2,1)}, bf16[2,48,512]{2,1,0:T(8,128)(2,1)S(1)}, u32[]{:S(2)}, u32[]{:S(2)}) collective-permute-start(bf16[2,48,512]{2,1,0:T(8,128)(2,1)} %get-tuple-element.97), channel_id=1, source_target_pairs={{0,13},{1,12},{2,15},{3,14},{4,9},{5,8},{6,11},{7,10},{8,5},{9,4},... | collective-permute-start | bytes 294920 | tf_op jit(solution)/shard_map/ppermute | solution.py:300
  20.4 3.9 %collective-permute-start.24 = (bf16[2,48,512]{2,1,0:T(8,128)(2,1)}, bf16[2,48,512]{2,1,0:T(8,128)(2,1)S(1)}, u32[]{:S(2)}, u32[]{:S(2)}) collective-permute-start(bf16[2,48,512]{2,1,0:T(8,128)(2,1)} %get-tuple-element.99), channel_id=1, source_target_pairs={{0,10},{1,11},{2,8},{3,9},{4,14},{5,15},{6,12},{7,13},{8,2},{9,3},... | collective-permute-start | bytes 294920 | tf_op jit(solution)/shard_map/ppermute | solution.py:300
  24.3 3.8 %collective-permute-start.25 = (bf16[2,48,512]{2,1,0:T(8,128)(2,1)}, bf16[2,48,512]{2,1,0:T(8,128)(2,1)S(1)}, u32[]{:S(2)}, u32[]{:S(2)}) collective-permute-start(bf16[2,48,512]{2,1,0:T(8,128)(2,1)} %get-tuple-element.100), channel_id=1, source_target_pairs={{0,14},{1,15},{2,12},{3,13},{4,10},{5,11},{6,8},{7,9},{8,6},{9,7},... | collective-permute-start | bytes 294920 | tf_op jit(solution)/shard_map/ppermute | solution.py:300
  28.5 3.2 %collective-permute-start.27 = (bf16[2,48,512]{2,1,0:T(8,128)(2,1)}, bf16[2,48,512]{2,1,0:T(8,128)(2,1)S(1)}, u32[]{:S(2)}, u32[]{:S(2)}) collective-permute-start(bf16[2,48,512]{2,1,0:T(8,128)(2,1)} %get-tuple-element.102), channel_id=1, source_target_pairs={{0,11},{1,10},{2,9},{3,8},{4,15},{5,14},{6,13},{7,12},{8,3},{9,2},... | collective-permute-start | bytes 294920 | tf_op jit(solution)/shard_map/ppermute | solution.py:300
  31.7 2.8 %collective-permute-done.24.refs_9_ = bf16[2,48,512]{2,1,0:T(8,128)(2,1)S(1)} collective-permute-done((bf16[2,48,512]{2,1,0:T(8,128)(2,1)}, bf16[2,48,512]{2,1,0:T(8,128)(2,1)S(1)}, u32[]{:S(2)}, u32[]{:S(2)}) %collective-permute-start.24) | collective-permute-done | bytes 98336 | tf_op jit(solution)/shard_map/ppermute | solution.py:300
  37.5 2.8 %pack_rows.1 = (bf16[32,1792]{1,0:T(8,128)(2,1)S(1)}, bf16[32,1792]{1,0:T(8,128)(2,1)S(1)}, bf16[32,1792]{1,0:T(8,128)(2,1)S(1)}, bf16[32,1792]{1,0:T(8,128)(2,1...) custom-call(s32[1]{0:T(128)S(6)} %copy.13.live_ref, ...), custom_call_target="tpu_custom_call" | custom-call | flops 469762048 | bytes 2752512 | tf_op jit(solution)/shard_map/pack_rows/pallas_call | solution.py:107
  40.7 2.7 %collective-permute-start.2 = (bf16[32,1792]{1,0:T(8,128)(2,1)S(1)}, bf16[32,1792]{1,0:T(8,128)(2,1)S(1)}, u32[]{:S(2)}, u32[]{:S(2)}) collective-permute-start(bf16[32,1792]{1,0:T(8,128)(2,1)S(1)} %get-tuple-element.76), channel_id=1, source_target_pairs={{0,7},{1,6},{2,5},{3,4},{4,3},{5,2},{6,1},{7,0},{8,15},{9,14},{10,... | collective-permute-start | bytes 344072 | tf_op jit(solution)/shard_map/ppermute | solution.py:300
  43.4 5.0 %collective-permute-start.3 = (bf16[32,1792]{1,0:T(8,128)(2,1)S(1)}, bf16[32,1792]{1,0:T(8,128)(2,1)S(1)}, u32[]{:S(2)}, u32[]{:S(2)}) collective-permute-start(bf16[32,1792]{1,0:T(8,128)(2,1)S(1)} %get-tuple-element.77), channel_id=1, source_target_pairs={{0,12},{1,13},{2,14},{3,15},{4,8},{5,9},{6,10},{7,11},{8,4},{9,5},... | collective-permute-start | bytes 344072 | tf_op jit(solution)/shard_map/ppermute | solution.py:300
  50.5 5.6 %collective-permute-start.7 = (bf16[32,1792]{1,0:T(8,128)(2,1)S(1)}, bf16[32,1792]{1,0:T(8,128)(2,1)S(1)}, u32[]{:S(2)}, u32[]{:S(2)}) collective-permute-start(bf16[32,1792]{1,0:T(8,128)(2,1)S(1)} %get-tuple-element.81), channel_id=1, source_target_pairs={{0,13},{1,12},{2,15},{3,14},{4,9},{5,8},{6,11},{7,10},{8,5},{9,4},... | collective-permute-start | bytes 344072 | tf_op jit(solution)/shard_map/ppermute | solution.py:300
  56.1 4.4 %collective-permute-start.9 = (bf16[32,1792]{1,0:T(8,128)(2,1)S(1)}, bf16[32,1792]{1,0:T(8,128)(2,1)S(1)}, u32[]{:S(2)}, u32[]{:S(2)}) collective-permute-start(bf16[32,1792]{1,0:T(8,128)(2,1)S(1)} %get-tuple-element.83), channel_id=1, source_target_pairs={{0,10},{1,11},{2,8},{3,9},{4,14},{5,15},{6,12},{7,13},{8,2},{9,3},... | collective-permute-start | bytes 344072 | tf_op jit(solution)/shard_map/ppermute | solution.py:300
  60.5 3.8 %collective-permute-start.11 = (bf16[32,1792]{1,0:T(8,128)(2,1)S(1)}, bf16[32,1792]{1,0:T(8,128)(2,1)S(1)}, u32[]{:S(2)}, u32[]{:S(2)}) collective-permute-start(bf16[32,1792]{1,0:T(8,128)(2,1)S(1)} %get-tuple-element.85), channel_id=1, source_target_pairs={{0,14},{1,15},{2,12},{3,13},{4,10},{5,11},{6,8},{7,9},{8,6},{9,7},... | collective-permute-start | bytes 344072 | tf_op jit(solution)/shard_map/ppermute | solution.py:300
  64.6 4.3 %collective-permute-start.13 = (bf16[32,1792]{1,0:T(8,128)(2,1)S(1)}, bf16[32,1792]{1,0:T(8,128)(2,1)S(1)}, u32[]{:S(2)}, u32[]{:S(2)}) collective-permute-start(bf16[32,1792]{1,0:T(8,128)(2,1)S(1)} %get-tuple-element.87), channel_id=1, source_target_pairs={{0,11},{1,10},{2,9},{3,8},{4,15},{5,14},{6,13},{7,12},{8,3},{9,2},... | collective-permute-start | bytes 344072 | tf_op jit(solution)/shard_map/ppermute | solution.py:300
  69.0 2.2 %collective-permute-start.14 = (bf16[32,1792]{1,0:T(8,128)(2,1)S(1)}, bf16[32,1792]{1,0:T(8,128)(2,1)S(1)}, u32[]{:S(2)}, u32[]{:S(2)}) collective-permute-start(bf16[32,1792]{1,0:T(8,128)(2,1)S(1)} %get-tuple-element.88), channel_id=1, source_target_pairs={{0,4},{1,5},{2,6},{3,7},{4,0},{5,1},{6,2},{7,3},{8,12},{9,13},{10,... | collective-permute-start | bytes 344072 | tf_op jit(solution)/shard_map/ppermute | solution.py:300
  71.1 4.6 %collective-permute-start.15 = (bf16[32,1792]{1,0:T(8,128)(2,1)S(1)}, bf16[32,1792]{1,0:T(8,128)(2,1)S(1)}, u32[]{:S(2)}, u32[]{:S(2)}) collective-permute-start(bf16[32,1792]{1,0:T(8,128)(2,1)S(1)} %get-tuple-element.89), channel_id=1, source_target_pairs={{0,15},{1,14},{2,13},{3,12},{4,11},{5,10},{6,9},{7,8},{8,7},{9,6},... | collective-permute-start | bytes 344072 | tf_op jit(solution)/shard_map/ppermute | solution.py:300
  76.5 2.4 %collective-permute-start.30 = (bf16[2,48,512]{2,1,0:T(8,128)(2,1)S(1)}, bf16[2,48,512]{2,1,0:T(8,128)(2,1)S(1)}, u32[]{:S(2)}, u32[]{:S(2)}) collective-permute-start(bf16[2,48,512]{2,1,0:T(8,128)(2,1)S(1)} %get-tuple-element.106), channel_id=1, source_target_pairs={{0,8},{1,9},{2,10},{3,11},{4,12},{5,13},{6,14},{7,15},{8,0},{9,1},... | collective-permute-start | bytes 294920 | tf_op jit(solution)/shard_map/ppermute | solution.py:300
  80.8 2.1 %collective-permute-start.32 = (bf16[2,48,512]{2,1,0:T(8,128)(2,1)S(1)}, bf16[2,48,512]{2,1,0:T(8,128)(2,1)S(1)}, u32[]{:S(2)}, u32[]{:S(2)}) collective-permute-start(bf16[2,48,512]{2,1,0:T(8,128)(2,1)S(1)} %get-tuple-element.108), channel_id=1, source_target_pairs={{0,12},{1,13},{2,14},{3,15},{4,8},{5,9},{6,10},{7,11},{8,4},{9,5},... | collective-permute-start | bytes 294920 | tf_op jit(solution)/shard_map/ppermute | solution.py:300
  83.0 3.6 %collective-permute-start.33 = (bf16[2,48,512]{2,1,0:T(8,128)(2,1)S(1)}, bf16[2,48,512]{2,1,0:T(8,128)(2,1)S(1)}, u32[]{:S(2)}, u32[]{:S(2)}) collective-permute-start(bf16[2,48,512]{2,1,0:T(8,128)(2,1)S(1)} %get-tuple-element.109), channel_id=1, source_target_pairs={{0,3},{1,2},{2,1},{3,0},{4,7},{5,6},{6,5},{7,4},{8,11},{9,10},{10,... | collective-permute-start | bytes 294920 | tf_op jit(solution)/shard_map/ppermute | solution.py:300
  87.7 3.1 %collective-permute-done.30.refs_17_ = bf16[2,48,512]{2,1,0:T(8,128)(2,1)S(1)} collective-permute-done((bf16[2,48,512]{2,1,0:T(8,128)(2,1)S(1)}, bf16[2,48,512]{2,1,0:T(8,128)(2,1)S(1)}, u32[]{:S(2)}, u32[]{:S(2)}) %collective-permute-start.30) | collective-permute-done | bytes 98336 | tf_op jit(solution)/shard_map/ppermute | solution.py:300
  94.0 3.7 %collective-permute-start.38 = (bf16[2,48,512]{2,1,0:T(8,128)(2,1)S(1)}, bf16[2,48,512]{2,1,0:T(8,128)(2,1)S(1)}, u32[]{:S(2)}, u32[]{:S(2)}) collective-permute-start(bf16[2,48,512]{2,1,0:T(8,128)(2,1)S(1)} %get-tuple-element.114), channel_id=1, source_target_pairs={{0,10},{1,11},{2,8},{3,9},{4,14},{5,15},{6,12},{7,13},{8,2},{9,3},... | collective-permute-start | bytes 294920 | tf_op jit(solution)/shard_map/ppermute | solution.py:300
  97.7 2.6 %collective-permute-done.35.refs_22_ = bf16[2,48,512]{2,1,0:T(8,128)(2,1)S(1)} collective-permute-done((bf16[2,48,512]{2,1,0:T(8,128)(2,1)S(1)}, bf16[2,48,512]{2,1,0:T(8,128)(2,1)S(1)}, u32[]{:S(2)}, u32[]{:S(2)}) %collective-permute-start.35) | collective-permute-done | bytes 98336 | tf_op jit(solution)/shard_map/ppermute | solution.py:300
  100.3 2.6 %collective-permute-start.40 = (bf16[2,48,512]{2,1,0:T(8,128)(2,1)S(1)}, bf16[2,48,512]{2,1,0:T(8,128)(2,1)S(1)}, u32[]{:S(2)}, u32[]{:S(2)}) collective-permute-start(bf16[2,48,512]{2,1,0:T(8,128)(2,1)S(1)} %get-tuple-element.116), channel_id=1, source_target_pairs={{0,14},{1,15},{2,12},{3,13},{4,10},{5,11},{6,8},{7,9},{8,6},{9,7},... | collective-permute-start | bytes 294920 | tf_op jit(solution)/shard_map/ppermute | solution.py:300
  102.9 3.0 %collective-permute-start.42 = (bf16[2,48,512]{2,1,0:T(8,128)(2,1)S(1)}, bf16[2,48,512]{2,1,0:T(8,128)(2,1)S(1)}, u32[]{:S(2)}, u32[]{:S(2)}) collective-permute-start(bf16[2,48,512]{2,1,0:T(8,128)(2,1)S(1)} %get-tuple-element.118), channel_id=1, source_target_pairs={{0,11},{1,10},{2,9},{3,8},{4,15},{5,14},{6,13},{7,12},{8,3},{9,2},... | collective-permute-start | bytes 294920 | tf_op jit(solution)/shard_map/ppermute | solution.py:300
  107.8 7.4 %collective-permute-done.42.refs_29_ = bf16[2,48,512]{2,1,0:T(8,128)(2,1)S(1)} collective-permute-done((bf16[2,48,512]{2,1,0:T(8,128)(2,1)S(1)}, bf16[2,48,512]{2,1,0:T(8,128)(2,1)S(1)}, u32[]{:S(2)}, u32[]{:S(2)}) %collective-permute-start.42) | collective-permute-done | bytes 98336 | tf_op jit(solution)/shard_map/ppermute | solution.py:300
  115.2 4.3 %update.1 = (bf16[384,1024]{1,0:T(8,128)(2,1)S(1)}, bf16[384,1024]{1,0:T(8,128)(2,1)S(1)}, bf16[32,1024]{1,0:T(8,128)(2,1)S(1)}, bf16[32,1024]{1,0:T(8,128)(2,1)...) custom-call(s32[1]{0:T(128)} %bitcast.me_ref, ...), custom_call_target="tpu_custom_call" | custom-call | flops 2239758336 | bytes 6029312 | tf_op jit(solution)/shard_map/update/pallas_call | solution.py:213
  121.3 3.9 %collective-permute-start.45 = (bf16[32,1024]{1,0:T(8,128)(2,1)S(1)}, bf16[32,1024]{1,0:T(8,128)(2,1)S(1)}, u32[]{:S(2)}, u32[]{:S(2)}) collective-permute-start(bf16[32,1024]{1,0:T(8,128)(2,1)S(1)} %get-tuple-element.128), channel_id=1, source_target_pairs={{0,8},{1,9},{2,10},{3,11},{4,12},{5,13},{6,14},{7,15},{8,0},{9,1},... | collective-permute-start | bytes 196616 | tf_op jit(solution)/shard_map/ppermute | solution.py:300
  133.5 2.7 %collective-permute-start.53 = (bf16[32,1024]{1,0:T(8,128)(2,1)S(1)}, bf16[32,1024]{1,0:T(8,128)(2,1)S(1)}, u32[]{:S(2)}, u32[]{:S(2)}) collective-permute-start(bf16[32,1024]{1,0:T(8,128)(2,1)S(1)} %get-tuple-element.136), channel_id=1, source_target_pairs={{0,10},{1,11},{2,8},{3,9},{4,14},{5,15},{6,12},{7,13},{8,2},{9,3},... | collective-permute-start | bytes 196616 | tf_op jit(solution)/shard_map/ppermute | solution.py:300
  136.4 2.9 %collective-permute-start.55 = (bf16[32,1024]{1,0:T(8,128)(2,1)S(1)}, bf16[32,1024]{1,0:T(8,128)(2,1)S(1)}, u32[]{:S(2)}, u32[]{:S(2)}) collective-permute-start(bf16[32,1024]{1,0:T(8,128)(2,1)S(1)} %get-tuple-element.138), channel_id=1, source_target_pairs={{0,14},{1,15},{2,12},{3,13},{4,10},{5,11},{6,8},{7,9},{8,6},{9,7},... | collective-permute-start | bytes 196616 | tf_op jit(solution)/shard_map/ppermute | solution.py:300
  139.3 2.8 %collective-permute-start.57 = (bf16[32,1024]{1,0:T(8,128)(2,1)S(1)}, bf16[32,1024]{1,0:T(8,128)(2,1)S(1)}, u32[]{:S(2)}, u32[]{:S(2)}) collective-permute-start(bf16[32,1024]{1,0:T(8,128)(2,1)S(1)} %get-tuple-element.140), channel_id=1, source_target_pairs={{0,11},{1,10},{2,9},{3,8},{4,15},{5,14},{6,13},{7,12},{8,3},{9,2},... | collective-permute-start | bytes 196616 | tf_op jit(solution)/shard_map/ppermute | solution.py:300
  144.1 2.5 %emit.1 = (bf16[384,1024]{1,0:T(8,128)(2,1)}, bf16[384,1024]{1,0:T(8,128)(2,1)}) custom-call(bf16[384,1024]{1,0:T(8,128)(2,1)} %copy-done, bf16[384,1024]{1,0:T(8,128)(2,1)} %copy-done.1), custom_call_target="tpu_custom_call" | custom-call | bytes 3145728 | tf_op jit(solution)/shard_map/emit/pallas_call | solution.py:243
  (114 shorter events, 40.1 us)
Async XLA Ops:
  11.3 13.0 %collective-permute-start.20 = (bf16[2,48,512]{2,1,0:T(8,128)(2,1)}, bf16[2,48,512]{2,1,0:T(8,128)(2,1)S(1)}, u32[]{:S(2)}, u32[]{:S(2)}) collective-permute-start(bf16[2,48,512]{2,1,0:T(8,128)(2,1)} %get-tuple-element.95), channel_id=1, source_target_pairs={{0,9},{1,8},{2,11},{3,10},{4,13},{5,12},{6,15},{7,14},{8,1},{9,0},... | collective-permute-start | bytes 294920 | tf_op jit(solution)/shard_map/ppermute | solution.py:300
  14.5 13.6 %collective-permute-start.21 = (bf16[2,48,512]{2,1,0:T(8,128)(2,1)}, bf16[2,48,512]{2,1,0:T(8,128)(2,1)S(1)}, u32[]{:S(2)}, u32[]{:S(2)}) collective-permute-start(bf16[2,48,512]{2,1,0:T(8,128)(2,1)} %get-tuple-element.96), channel_id=1, source_target_pairs={{0,6},{1,7},{2,4},{3,5},{4,2},{5,3},{6,0},{7,1},{8,14},{9,15},{10,... | collective-permute-start | bytes 294920 | tf_op jit(solution)/shard_map/ppermute | solution.py:300
  16.1 12.3 %collective-permute-start.22 = (bf16[2,48,512]{2,1,0:T(8,128)(2,1)}, bf16[2,48,512]{2,1,0:T(8,128)(2,1)S(1)}, u32[]{:S(2)}, u32[]{:S(2)}) collective-permute-start(bf16[2,48,512]{2,1,0:T(8,128)(2,1)} %get-tuple-element.97), channel_id=1, source_target_pairs={{0,13},{1,12},{2,15},{3,14},{4,9},{5,8},{6,11},{7,10},{8,5},{9,4},... | collective-permute-start | bytes 294920 | tf_op jit(solution)/shard_map/ppermute | solution.py:300
  18.9 12.7 %collective-permute-start.23 = (bf16[2,48,512]{2,1,0:T(8,128)(2,1)}, bf16[2,48,512]{2,1,0:T(8,128)(2,1)S(1)}, u32[]{:S(2)}, u32[]{:S(2)}) collective-permute-start(bf16[2,48,512]{2,1,0:T(8,128)(2,1)} %get-tuple-element.98), channel_id=1, source_target_pairs={{0,2},{1,3},{2,0},{3,1},{4,6},{5,7},{6,4},{7,5},{8,10},{9,11},{10,... | collective-permute-start | bytes 294920 | tf_op jit(solution)/shard_map/ppermute | solution.py:300
  20.4 14.1 %collective-permute-start.24 = (bf16[2,48,512]{2,1,0:T(8,128)(2,1)}, bf16[2,48,512]{2,1,0:T(8,128)(2,1)S(1)}, u32[]{:S(2)}, u32[]{:S(2)}) collective-permute-start(bf16[2,48,512]{2,1,0:T(8,128)(2,1)} %get-tuple-element.99), channel_id=1, source_target_pairs={{0,10},{1,11},{2,8},{3,9},{4,14},{5,15},{6,12},{7,13},{8,2},{9,3},... | collective-permute-start | bytes 294920 | tf_op jit(solution)/shard_map/ppermute | solution.py:300
  24.3 16.0 %collective-permute-start.25 = (bf16[2,48,512]{2,1,0:T(8,128)(2,1)}, bf16[2,48,512]{2,1,0:T(8,128)(2,1)S(1)}, u32[]{:S(2)}, u32[]{:S(2)}) collective-permute-start(bf16[2,48,512]{2,1,0:T(8,128)(2,1)} %get-tuple-element.100), channel_id=1, source_target_pairs={{0,14},{1,15},{2,12},{3,13},{4,10},{5,11},{6,8},{7,9},{8,6},{9,7},... | collective-permute-start | bytes 294920 | tf_op jit(solution)/shard_map/ppermute | solution.py:300
  28.1 12.6 %collective-permute-start.26 = (bf16[2,48,512]{2,1,0:T(8,128)(2,1)}, bf16[2,48,512]{2,1,0:T(8,128)(2,1)S(1)}, u32[]{:S(2)}, u32[]{:S(2)}) collective-permute-start(bf16[2,48,512]{2,1,0:T(8,128)(2,1)} %get-tuple-element.101), channel_id=1, source_target_pairs={{0,1},{1,0},{2,3},{3,2},{4,5},{5,4},{6,7},{7,6},{8,9},{9,8},{10,11... | collective-permute-start | bytes 294920 | tf_op jit(solution)/shard_map/ppermute | solution.py:300
  28.5 14.9 %collective-permute-start.27 = (bf16[2,48,512]{2,1,0:T(8,128)(2,1)}, bf16[2,48,512]{2,1,0:T(8,128)(2,1)S(1)}, u32[]{:S(2)}, u32[]{:S(2)}) collective-permute-start(bf16[2,48,512]{2,1,0:T(8,128)(2,1)} %get-tuple-element.102), channel_id=1, source_target_pairs={{0,11},{1,10},{2,9},{3,8},{4,15},{5,14},{6,13},{7,12},{8,3},{9,2},... | collective-permute-start | bytes 294920 | tf_op jit(solution)/shard_map/ppermute | solution.py:300
  31.7 16.8 %collective-permute-start.28 = (bf16[2,48,512]{2,1,0:T(8,128)(2,1)}, bf16[2,48,512]{2,1,0:T(8,128)(2,1)S(1)}, u32[]{:S(2)}, u32[]{:S(2)}) collective-permute-start(bf16[2,48,512]{2,1,0:T(8,128)(2,1)} %get-tuple-element.103), channel_id=1, source_target_pairs={{0,4},{1,5},{2,6},{3,7},{4,0},{5,1},{6,2},{7,3},{8,12},{9,13},{10,... | collective-permute-start | bytes 294920 | tf_op jit(solution)/shard_map/ppermute | solution.py:300
  34.4 14.0 %collective-permute-start.29 = (bf16[2,48,512]{2,1,0:T(8,128)(2,1)}, bf16[2,48,512]{2,1,0:T(8,128)(2,1)S(1)}, u32[]{:S(2)}, u32[]{:S(2)}) collective-permute-start(bf16[2,48,512]{2,1,0:T(8,128)(2,1)} %get-tuple-element.104), channel_id=1, source_target_pairs={{0,15},{1,14},{2,13},{3,12},{4,11},{5,10},{6,9},{7,8},{8,7},{9,6},... | collective-permute-start | bytes 294920 | tf_op jit(solution)/shard_map/ppermute | solution.py:300
  40.7 9.8 %collective-permute-start.2 = (bf16[32,1792]{1,0:T(8,128)(2,1)S(1)}, bf16[32,1792]{1,0:T(8,128)(2,1)S(1)}, u32[]{:S(2)}, u32[]{:S(2)}) collective-permute-start(bf16[32,1792]{1,0:T(8,128)(2,1)S(1)} %get-tuple-element.76), channel_id=1, source_target_pairs={{0,7},{1,6},{2,5},{3,4},{4,3},{5,2},{6,1},{7,0},{8,15},{9,14},{10,... | collective-permute-start | bytes 344072 | tf_op jit(solution)/shard_map/ppermute | solution.py:300
  43.4 12.7 %collective-permute-start.3 = (bf16[32,1792]{1,0:T(8,128)(2,1)S(1)}, bf16[32,1792]{1,0:T(8,128)(2,1)S(1)}, u32[]{:S(2)}, u32[]{:S(2)}) collective-permute-start(bf16[32,1792]{1,0:T(8,128)(2,1)S(1)} %get-tuple-element.77), channel_id=1, source_target_pairs={{0,12},{1,13},{2,14},{3,15},{4,8},{5,9},{6,10},{7,11},{8,4},{9,5},... | collective-permute-start | bytes 344072 | tf_op jit(solution)/shard_map/ppermute | solution.py:300
  48.4 12.1 %collective-permute-start.5 = (bf16[32,1792]{1,0:T(8,128)(2,1)S(1)}, bf16[32,1792]{1,0:T(8,128)(2,1)S(1)}, u32[]{:S(2)}, u32[]{:S(2)}) collective-permute-start(bf16[32,1792]{1,0:T(8,128)(2,1)S(1)} %get-tuple-element.79), channel_id=1, source_target_pairs={{0,9},{1,8},{2,11},{3,10},{4,13},{5,12},{6,15},{7,14},{8,1},{9,0},... | collective-permute-start | bytes 344072 | tf_op jit(solution)/shard_map/ppermute | solution.py:300
  49.0 11.5 %collective-permute-start.6 = (bf16[32,1792]{1,0:T(8,128)(2,1)S(1)}, bf16[32,1792]{1,0:T(8,128)(2,1)S(1)}, u32[]{:S(2)}, u32[]{:S(2)}) collective-permute-start(bf16[32,1792]{1,0:T(8,128)(2,1)S(1)} %get-tuple-element.80), channel_id=1, source_target_pairs={{0,6},{1,7},{2,4},{3,5},{4,2},{5,3},{6,0},{7,1},{8,14},{9,15},{10,... | collective-permute-start | bytes 344072 | tf_op jit(solution)/shard_map/ppermute | solution.py:300
  50.5 13.8 %collective-permute-start.7 = (bf16[32,1792]{1,0:T(8,128)(2,1)S(1)}, bf16[32,1792]{1,0:T(8,128)(2,1)S(1)}, u32[]{:S(2)}, u32[]{:S(2)}) collective-permute-start(bf16[32,1792]{1,0:T(8,128)(2,1)S(1)} %get-tuple-element.81), channel_id=1, source_target_pairs={{0,13},{1,12},{2,15},{3,14},{4,9},{5,8},{6,11},{7,10},{8,5},{9,4},... | collective-permute-start | bytes 344072 | tf_op jit(solution)/shard_map/ppermute | solution.py:300
  56.1 12.9 %collective-permute-start.9 = (bf16[32,1792]{1,0:T(8,128)(2,1)S(1)}, bf16[32,1792]{1,0:T(8,128)(2,1)S(1)}, u32[]{:S(2)}, u32[]{:S(2)}) collective-permute-start(bf16[32,1792]{1,0:T(8,128)(2,1)S(1)} %get-tuple-element.83), channel_id=1, source_target_pairs={{0,10},{1,11},{2,8},{3,9},{4,14},{5,15},{6,12},{7,13},{8,2},{9,3},... | collective-permute-start | bytes 344072 | tf_op jit(solution)/shard_map/ppermute | solution.py:300
  60.5 10.6 %collective-permute-start.10 = (bf16[32,1792]{1,0:T(8,128)(2,1)S(1)}, bf16[32,1792]{1,0:T(8,128)(2,1)S(1)}, u32[]{:S(2)}, u32[]{:S(2)}) collective-permute-start(bf16[32,1792]{1,0:T(8,128)(2,1)S(1)} %get-tuple-element.84), channel_id=1, source_target_pairs={{0,5},{1,4},{2,7},{3,6},{4,1},{5,0},{6,3},{7,2},{8,13},{9,12},{10,... | collective-permute-start | bytes 344072 | tf_op jit(solution)/shard_map/ppermute | solution.py:300
  60.5 16.0 %collective-permute-start.11 = (bf16[32,1792]{1,0:T(8,128)(2,1)S(1)}, bf16[32,1792]{1,0:T(8,128)(2,1)S(1)}, u32[]{:S(2)}, u32[]{:S(2)}) collective-permute-start(bf16[32,1792]{1,0:T(8,128)(2,1)S(1)} %get-tuple-element.85), channel_id=1, source_target_pairs={{0,14},{1,15},{2,12},{3,13},{4,10},{5,11},{6,8},{7,9},{8,6},{9,7},... | collective-permute-start | bytes 344072 | tf_op jit(solution)/shard_map/ppermute | solution.py:300
  64.3 14.7 %collective-permute-start.12 = (bf16[32,1792]{1,0:T(8,128)(2,1)S(1)}, bf16[32,1792]{1,0:T(8,128)(2,1)S(1)}, u32[]{:S(2)}, u32[]{:S(2)}) collective-permute-start(bf16[32,1792]{1,0:T(8,128)(2,1)S(1)} %get-tuple-element.86), channel_id=1, source_target_pairs={{0,1},{1,0},{2,3},{3,2},{4,5},{5,4},{6,7},{7,6},{8,9},{9,8},{10,11... | collective-permute-start | bytes 344072 | tf_op jit(solution)/shard_map/ppermute | solution.py:300
  64.6 16.2 %collective-permute-start.13 = (bf16[32,1792]{1,0:T(8,128)(2,1)S(1)}, bf16[32,1792]{1,0:T(8,128)(2,1)S(1)}, u32[]{:S(2)}, u32[]{:S(2)}) collective-permute-start(bf16[32,1792]{1,0:T(8,128)(2,1)S(1)} %get-tuple-element.87), channel_id=1, source_target_pairs={{0,11},{1,10},{2,9},{3,8},{4,15},{5,14},{6,13},{7,12},{8,3},{9,2},... | collective-permute-start | bytes 344072 | tf_op jit(solution)/shard_map/ppermute | solution.py:300
  69.0 14.0 %collective-permute-start.14 = (bf16[32,1792]{1,0:T(8,128)(2,1)S(1)}, bf16[32,1792]{1,0:T(8,128)(2,1)S(1)}, u32[]{:S(2)}, u32[]{:S(2)}) collective-permute-start(bf16[32,1792]{1,0:T(8,128)(2,1)S(1)} %get-tuple-element.88), channel_id=1, source_target_pairs={{0,4},{1,5},{2,6},{3,7},{4,0},{5,1},{6,2},{7,3},{8,12},{9,13},{10,... | collective-permute-start | bytes 344072 | tf_op jit(solution)/shard_map/ppermute | solution.py:300
  71.1 15.4 %collective-permute-start.15 = (bf16[32,1792]{1,0:T(8,128)(2,1)S(1)}, bf16[32,1792]{1,0:T(8,128)(2,1)S(1)}, u32[]{:S(2)}, u32[]{:S(2)}) collective-permute-start(bf16[32,1792]{1,0:T(8,128)(2,1)S(1)} %get-tuple-element.89), channel_id=1, source_target_pairs={{0,15},{1,14},{2,13},{3,12},{4,11},{5,10},{6,9},{7,8},{8,7},{9,6},... | collective-permute-start | bytes 344072 | tf_op jit(solution)/shard_map/ppermute | solution.py:300
  76.5 14.2 %collective-permute-start.30 = (bf16[2,48,512]{2,1,0:T(8,128)(2,1)S(1)}, bf16[2,48,512]{2,1,0:T(8,128)(2,1)S(1)}, u32[]{:S(2)}, u32[]{:S(2)}) collective-permute-start(bf16[2,48,512]{2,1,0:T(8,128)(2,1)S(1)} %get-tuple-element.106), channel_id=1, source_target_pairs={{0,8},{1,9},{2,10},{3,11},{4,12},{5,13},{6,14},{7,15},{8,0},{9,1},... | collective-permute-start | bytes 294920 | tf_op jit(solution)/shard_map/ppermute | solution.py:300
  78.9 11.8 %collective-permute-start.31 = (bf16[2,48,512]{2,1,0:T(8,128)(2,1)S(1)}, bf16[2,48,512]{2,1,0:T(8,128)(2,1)S(1)}, u32[]{:S(2)}, u32[]{:S(2)}) collective-permute-start(bf16[2,48,512]{2,1,0:T(8,128)(2,1)S(1)} %get-tuple-element.107), channel_id=1, source_target_pairs={{0,7},{1,6},{2,5},{3,4},{4,3},{5,2},{6,1},{7,0},{8,15},{9,14},{10,... | collective-permute-start | bytes 294920 | tf_op jit(solution)/shard_map/ppermute | solution.py:300
  80.8 11.7 %collective-permute-start.32 = (bf16[2,48,512]{2,1,0:T(8,128)(2,1)S(1)}, bf16[2,48,512]{2,1,0:T(8,128)(2,1)S(1)}, u32[]{:S(2)}, u32[]{:S(2)}) collective-permute-start(bf16[2,48,512]{2,1,0:T(8,128)(2,1)S(1)} %get-tuple-element.108), channel_id=1, source_target_pairs={{0,12},{1,13},{2,14},{3,15},{4,8},{5,9},{6,10},{7,11},{8,4},{9,5},... | collective-permute-start | bytes 294920 | tf_op jit(solution)/shard_map/ppermute | solution.py:300
  83.0 11.0 %collective-permute-start.33 = (bf16[2,48,512]{2,1,0:T(8,128)(2,1)S(1)}, bf16[2,48,512]{2,1,0:T(8,128)(2,1)S(1)}, u32[]{:S(2)}, u32[]{:S(2)}) collective-permute-start(bf16[2,48,512]{2,1,0:T(8,128)(2,1)S(1)} %get-tuple-element.109), channel_id=1, source_target_pairs={{0,3},{1,2},{2,1},{3,0},{4,7},{5,6},{6,5},{7,4},{8,11},{9,10},{10,... | collective-permute-start | bytes 294920 | tf_op jit(solution)/shard_map/ppermute | solution.py:300
  86.5 11.2 %collective-permute-start.34 = (bf16[2,48,512]{2,1,0:T(8,128)(2,1)S(1)}, bf16[2,48,512]{2,1,0:T(8,128)(2,1)S(1)}, u32[]{:S(2)}, u32[]{:S(2)}) collective-permute-start(bf16[2,48,512]{2,1,0:T(8,128)(2,1)S(1)} %get-tuple-element.110), channel_id=1, source_target_pairs={{0,9},{1,8},{2,11},{3,10},{4,13},{5,12},{6,15},{7,14},{8,1},{9,0},... | collective-permute-start | bytes 294920 | tf_op jit(solution)/shard_map/ppermute | solution.py:300
  90.8 12.1 %collective-permute-start.36 = (bf16[2,48,512]{2,1,0:T(8,128)(2,1)S(1)}, bf16[2,48,512]{2,1,0:T(8,128)(2,1)S(1)}, u32[]{:S(2)}, u32[]{:S(2)}) collective-permute-start(bf16[2,48,512]{2,1,0:T(8,128)(2,1)S(1)} %get-tuple-element.112), channel_id=1, source_target_pairs={{0,13},{1,12},{2,15},{3,14},{4,9},{5,8},{6,11},{7,10},{8,5},{9,4},... | collective-permute-start | bytes 294920 | tf_op jit(solution)/shard_map/ppermute | solution.py:300
  92.6 10.3 %collective-permute-start.37 = (bf16[2,48,512]{2,1,0:T(8,128)(2,1)S(1)}, bf16[2,48,512]{2,1,0:T(8,128)(2,1)S(1)}, u32[]{:S(2)}, u32[]{:S(2)}) collective-permute-start(bf16[2,48,512]{2,1,0:T(8,128)(2,1)S(1)} %get-tuple-element.113), channel_id=1, source_target_pairs={{0,2},{1,3},{2,0},{3,1},{4,6},{5,7},{6,4},{7,5},{8,10},{9,11},{10,... | collective-permute-start | bytes 294920 | tf_op jit(solution)/shard_map/ppermute | solution.py:300
  94.0 12.6 %collective-permute-start.38 = (bf16[2,48,512]{2,1,0:T(8,128)(2,1)S(1)}, bf16[2,48,512]{2,1,0:T(8,128)(2,1)S(1)}, u32[]{:S(2)}, u32[]{:S(2)}) collective-permute-start(bf16[2,48,512]{2,1,0:T(8,128)(2,1)S(1)} %get-tuple-element.114), channel_id=1, source_target_pairs={{0,10},{1,11},{2,8},{3,9},{4,14},{5,15},{6,12},{7,13},{8,2},{9,3},... | collective-permute-start | bytes 294920 | tf_op jit(solution)/shard_map/ppermute | solution.py:300
  102.9 12.3 %collective-permute-start.42 = (bf16[2,48,512]{2,1,0:T(8,128)(2,1)S(1)}, bf16[2,48,512]{2,1,0:T(8,128)(2,1)S(1)}, u32[]{:S(2)}, u32[]{:S(2)}) collective-permute-start(bf16[2,48,512]{2,1,0:T(8,128)(2,1)S(1)} %get-tuple-element.118), channel_id=1, source_target_pairs={{0,11},{1,10},{2,9},{3,8},{4,15},{5,14},{6,13},{7,12},{8,3},{9,2},... | collective-permute-start | bytes 294920 | tf_op jit(solution)/shard_map/ppermute | solution.py:300
  136.4 10.2 %collective-permute-start.55 = (bf16[32,1024]{1,0:T(8,128)(2,1)S(1)}, bf16[32,1024]{1,0:T(8,128)(2,1)S(1)}, u32[]{:S(2)}, u32[]{:S(2)}) collective-permute-start(bf16[32,1024]{1,0:T(8,128)(2,1)S(1)} %get-tuple-element.138), channel_id=1, source_target_pairs={{0,14},{1,15},{2,12},{3,13},{4,10},{5,11},{6,8},{7,9},{8,6},{9,7},... | collective-permute-start | bytes 196616 | tf_op jit(solution)/shard_map/ppermute | solution.py:300
  (38 other events, 398.6 us)

commit v19 on v10

--- a/solution.py
+++ b/solution.py
@@ -259,13 +259,13 @@
 
 
 def mixed_order(groups):
-    def both_ends(partners):
-        middle = (len(partners) + 1) // 2
-        first, second = partners[:middle], partners[middle:]
+    def in_turn(first, second):
         return [s for pair in zip(first, second + [None]) for s in pair if s is not None]
 
-    half = groups // 2
-    far, near = both_ends(list(range(half, groups))), both_ends(list(range(half - 1, 0, -1)))
+    half, plane = groups // 2, groups // 4
+    far = in_turn(list(range(half, half + plane)), list(range(half + plane, groups)))
+    near = in_turn(list(range(half - 1, plane - 1, -1)), list(range(plane - 1, 0, -1)))
+    near = in_turn(near[1::2], near[::2][:-1]) + near[-1:] if plane > 1 else near
     return [0] + [s for pair in zip(far, near + [None]) for s in pair if s is not None]
 
 
@@ -445,7 +445,7 @@
     )
 
     def per_device(*args):
-        few = groups & (groups - 1) == 0 and groups <= 2 * args[0].shape[0] // groups
+        few = groups >= 8 and groups & (groups - 1) == 0 and groups <= 2 * args[0].shape[0] // groups
         return (partner_plan if few else routed_plan)(*args)
 
     return jax.shard_map(

time: 149 us -> 151 us (1.013)
  waiting for transfers between devices: 24.5 us -> 36.6 us
  starting transfers between devices: 110 us -> 99.5 us
    ppermute x60, waiting for transfers between devices: 24.5 us -> 36.6 us  [swap(): lax.ppermute(piece, 'expert', [(i, i ^ s) for i in range(groups)])]
    ppermute x60, starting transfers between devices: 110 us -> 99.5 us  [swap(): lax.ppermute(piece, 'expert', [(i, i ^ s) for i in range(groups)])]
  transfers between devices with their start and end apart: 60 -> 60, of which waited for: 12 -> 18; matrix products, arithmetic and copies ran while one was open for 0% -> 0% of each run, Pallas kernels for 2% -> 2%
where the time goes in v19:
time: 151 us
  starting transfers between devices  99.5 us (66%)
  waiting for transfers between devices  36.6 us (24%)
  Pallas kernels  12.3 us (8%)
    ppermute x60, starting transfers between devices, swap(): lax.ppermute(piece, 'expert', [(i, i ^ s) for i in range(groups)])  99.5 us
    ppermute x60, waiting for transfers between devices, swap(): lax.ppermute(piece, 'expert', [(i, i ^ s) for i in range(groups)])  36.6 us
    pallas_call x1, Pallas kernels, update(): pl.pallas_call(functools.partial(update_kernel, groups), out_shape=(shape...  4.74 us
  transfers between devices with their start and end apart: 60, of which 18 were waited for; matrix products, arithmetic and copies ran while one was open for 0% of the time, Pallas kernels for 2%

profile of v19, /device:TPU:0, one launch (start us, length us, event | category | flops | bytes accessed | tf_op | source)
XLA Modules:
  0.0 150.6 jit_solution(2297562365530028914)
XLA Ops:
  0.7 2.7 %split.1 = (bf16[2,48,512]{2,1,0:T(8,128)(2,1)}, bf16[2,48,512]{2,1,0:T(8,128)(2,1)}, bf16[2,48,512]{2,1,0:T(8,128)(2,1)}, bf16[2,48,512]{2,1,0:T(8,128)(2,1)}, ...) custom-call(s32[1]{0:T(128)} %bitcast.me_ref, ...), custom_call_target="tpu_custom_call" | custom-call | bytes 3145728 | tf_op jit(solution)/shard_map/split/pallas_call | solution.py:135
  3.9 3.7 %collective-permute-start.16 = (bf16[2,48,512]{2,1,0:T(8,128)(2,1)}, bf16[2,48,512]{2,1,0:T(8,128)(2,1)S(1)}, u32[]{:S(2)}, u32[]{:S(2)}) collective-permute-start(bf16[2,48,512]{2,1,0:T(8,128)(2,1)} %get-tuple-element.89), channel_id=1, source_target_pairs={{0,8},{1,9},{2,10},{3,11},{4,12},{5,13},{6,14},{7,15},{8,0},{9,1},... | collective-permute-start | bytes 294920 | tf_op jit(solution)/shard_map/ppermute | solution.py:276
  10.3 2.6 %collective-permute-start.20 = (bf16[2,48,512]{2,1,0:T(8,128)(2,1)}, bf16[2,48,512]{2,1,0:T(8,128)(2,1)S(1)}, u32[]{:S(2)}, u32[]{:S(2)}) collective-permute-start(bf16[2,48,512]{2,1,0:T(8,128)(2,1)} %get-tuple-element.93), channel_id=1, source_target_pairs={{0,9},{1,8},{2,11},{3,10},{4,13},{5,12},{6,15},{7,14},{8,1},{9,0},... | collective-permute-start | bytes 294920 | tf_op jit(solution)/shard_map/ppermute | solution.py:276
  13.5 4.0 %collective-permute-start.21 = (bf16[2,48,512]{2,1,0:T(8,128)(2,1)}, bf16[2,48,512]{2,1,0:T(8,128)(2,1)S(1)}, u32[]{:S(2)}, u32[]{:S(2)}) collective-permute-start(bf16[2,48,512]{2,1,0:T(8,128)(2,1)} %get-tuple-element.94), channel_id=1, source_target_pairs={{0,2},{1,3},{2,0},{3,1},{4,6},{5,7},{6,4},{7,5},{8,10},{9,11},{10,... | collective-permute-start | bytes 294920 | tf_op jit(solution)/shard_map/ppermute | solution.py:276
  17.4 2.9 %collective-permute-start.22 = (bf16[2,48,512]{2,1,0:T(8,128)(2,1)}, bf16[2,48,512]{2,1,0:T(8,128)(2,1)S(1)}, u32[]{:S(2)}, u32[]{:S(2)}) collective-permute-start(bf16[2,48,512]{2,1,0:T(8,128)(2,1)} %get-tuple-element.95), channel_id=1, source_target_pairs={{0,13},{1,12},{2,15},{3,14},{4,9},{5,8},{6,11},{7,10},{8,5},{9,4},... | collective-permute-start | bytes 294920 | tf_op jit(solution)/shard_map/ppermute | solution.py:276
  23.4 5.0 %collective-permute-start.25 = (bf16[2,48,512]{2,1,0:T(8,128)(2,1)}, bf16[2,48,512]{2,1,0:T(8,128)(2,1)S(1)}, u32[]{:S(2)}, u32[]{:S(2)}) collective-permute-start(bf16[2,48,512]{2,1,0:T(8,128)(2,1)} %get-tuple-element.98), channel_id=1, source_target_pairs={{0,14},{1,15},{2,12},{3,13},{4,10},{5,11},{6,8},{7,9},{8,6},{9,7},... | collective-permute-start | bytes 294920 | tf_op jit(solution)/shard_map/ppermute | solution.py:276
  28.4 5.2 %collective-permute-start.27 = (bf16[2,48,512]{2,1,0:T(8,128)(2,1)}, bf16[2,48,512]{2,1,0:T(8,128)(2,1)S(1)}, u32[]{:S(2)}, u32[]{:S(2)}) collective-permute-start(bf16[2,48,512]{2,1,0:T(8,128)(2,1)} %get-tuple-element.100), channel_id=1, source_target_pairs={{0,11},{1,10},{2,9},{3,8},{4,15},{5,14},{6,13},{7,12},{8,3},{9,2},... | collective-permute-start | bytes 294920 | tf_op jit(solution)/shard_map/ppermute | solution.py:276
  33.7 2.4 %collective-permute-start.29 = (bf16[2,48,512]{2,1,0:T(8,128)(2,1)}, bf16[2,48,512]{2,1,0:T(8,128)(2,1)S(1)}, u32[]{:S(2)}, u32[]{:S(2)}) collective-permute-start(bf16[2,48,512]{2,1,0:T(8,128)(2,1)} %get-tuple-element.102), channel_id=1, source_target_pairs={{0,15},{1,14},{2,13},{3,12},{4,11},{5,10},{6,9},{7,8},{8,7},{9,6},... | collective-permute-start | bytes 294920 | tf_op jit(solution)/shard_map/ppermute | solution.py:276
  37.5 2.8 %pack_rows.1 = (bf16[32,1792]{1,0:T(8,128)(2,1)S(1)}, bf16[32,1792]{1,0:T(8,128)(2,1)S(1)}, bf16[32,1792]{1,0:T(8,128)(2,1)S(1)}, bf16[32,1792]{1,0:T(8,128)(2,1...) custom-call(s32[1]{0:T(128)S(6)} %copy.13.live_ref, ...), custom_call_target="tpu_custom_call" | custom-call | flops 469762048 | bytes 2752512 | tf_op jit(solution)/shard_map/pack_rows/pallas_call | solution.py:107
  41.4 3.1 %collective-permute-start.2 = (bf16[32,1792]{1,0:T(8,128)(2,1)S(1)}, bf16[32,1792]{1,0:T(8,128)(2,1)S(1)}, u32[]{:S(2)}, u32[]{:S(2)}) collective-permute-start(bf16[32,1792]{1,0:T(8,128)(2,1)S(1)} %get-tuple-element.74), channel_id=1, source_target_pairs={{0,3},{1,2},{2,1},{3,0},{4,7},{5,6},{6,5},{7,4},{8,11},{9,10},{10,... | collective-permute-start | bytes 344072 | tf_op jit(solution)/shard_map/ppermute | solution.py:276
  44.6 2.3 %collective-permute-start.4 = (bf16[32,1792]{1,0:T(8,128)(2,1)S(1)}, bf16[32,1792]{1,0:T(8,128)(2,1)S(1)}, u32[]{:S(2)}, u32[]{:S(2)}) collective-permute-start(bf16[32,1792]{1,0:T(8,128)(2,1)S(1)} %get-tuple-element.76), channel_id=1, source_target_pairs={{0,7},{1,6},{2,5},{3,4},{4,3},{5,2},{6,1},{7,0},{8,15},{9,14},{10,... | collective-permute-start | bytes 344072 | tf_op jit(solution)/shard_map/ppermute | solution.py:276
  48.0 2.6 %collective-permute-done.1.refs_1_ = bf16[32,1792]{1,0:T(8,128)(2,1)S(1)} collective-permute-done((bf16[32,1792]{1,0:T(8,128)(2,1)S(1)}, bf16[32,1792]{1,0:T(8,128)(2,1)S(1)}, u32[]{:S(2)}, u32[]{:S(2)}) %collective-permute-start.1) | collective-permute-done | bytes 114720 | tf_op jit(solution)/shard_map/ppermute | solution.py:276
  50.7 3.0 %collective-permute-start.6 = (bf16[32,1792]{1,0:T(8,128)(2,1)S(1)}, bf16[32,1792]{1,0:T(8,128)(2,1)S(1)}, u32[]{:S(2)}, u32[]{:S(2)}) collective-permute-start(bf16[32,1792]{1,0:T(8,128)(2,1)S(1)} %get-tuple-element.78), channel_id=1, source_target_pairs={{0,2},{1,3},{2,0},{3,1},{4,6},{5,7},{6,4},{7,5},{8,10},{9,11},{10,... | collective-permute-start | bytes 344072 | tf_op jit(solution)/shard_map/ppermute | solution.py:276
  54.7 6.3 %collective-permute-start.8 = (bf16[32,1792]{1,0:T(8,128)(2,1)S(1)}, bf16[32,1792]{1,0:T(8,128)(2,1)S(1)}, u32[]{:S(2)}, u32[]{:S(2)}) collective-permute-start(bf16[32,1792]{1,0:T(8,128)(2,1)S(1)} %get-tuple-element.80), channel_id=1, source_target_pairs={{0,6},{1,7},{2,4},{3,5},{4,2},{5,3},{6,0},{7,1},{8,14},{9,15},{10,... | collective-permute-start | bytes 344072 | tf_op jit(solution)/shard_map/ppermute | solution.py:276
  61.4 3.4 %collective-permute-start.11 = (bf16[32,1792]{1,0:T(8,128)(2,1)S(1)}, bf16[32,1792]{1,0:T(8,128)(2,1)S(1)}, u32[]{:S(2)}, u32[]{:S(2)}) collective-permute-start(bf16[32,1792]{1,0:T(8,128)(2,1)S(1)} %get-tuple-element.83), channel_id=1, source_target_pairs={{0,14},{1,15},{2,12},{3,13},{4,10},{5,11},{6,8},{7,9},{8,6},{9,7},... | collective-permute-start | bytes 344072 | tf_op jit(solution)/shard_map/ppermute | solution.py:276
  68.4 4.3 %collective-permute-done.9.refs_9_ = bf16[32,1792]{1,0:T(8,128)(2,1)S(1)} collective-permute-done((bf16[32,1792]{1,0:T(8,128)(2,1)S(1)}, bf16[32,1792]{1,0:T(8,128)(2,1)S(1)}, u32[]{:S(2)}, u32[]{:S(2)}) %collective-permute-start.9) | collective-permute-done | bytes 114720 | tf_op jit(solution)/shard_map/ppermute | solution.py:276
  74.9 3.7 %collective-permute-start.30 = (bf16[2,48,512]{2,1,0:T(8,128)(2,1)S(1)}, bf16[2,48,512]{2,1,0:T(8,128)(2,1)S(1)}, u32[]{:S(2)}, u32[]{:S(2)}) collective-permute-start(bf16[2,48,512]{2,1,0:T(8,128)(2,1)S(1)} %get-tuple-element.104), channel_id=1, source_target_pairs={{0,8},{1,9},{2,10},{3,11},{4,12},{5,13},{6,14},{7,15},{8,0},{9,1},... | collective-permute-start | bytes 294920 | tf_op jit(solution)/shard_map/ppermute | solution.py:276
  78.6 5.4 %collective-permute-done.13.refs_13_ = bf16[32,1792]{1,0:T(8,128)(2,1)S(1)} collective-permute-done((bf16[32,1792]{1,0:T(8,128)(2,1)S(1)}, bf16[32,1792]{1,0:T(8,128)(2,1)S(1)}, u32[]{:S(2)}, u32[]{:S(2)}) %collective-permute-start.13) | collective-permute-done | bytes 114720 | tf_op jit(solution)/shard_map/ppermute | solution.py:276
  84.0 2.5 %collective-permute-start.32 = (bf16[2,48,512]{2,1,0:T(8,128)(2,1)S(1)}, bf16[2,48,512]{2,1,0:T(8,128)(2,1)S(1)}, u32[]{:S(2)}, u32[]{:S(2)}) collective-permute-start(bf16[2,48,512]{2,1,0:T(8,128)(2,1)S(1)} %get-tuple-element.106), channel_id=1, source_target_pairs={{0,12},{1,13},{2,14},{3,15},{4,8},{5,9},{6,10},{7,11},{8,4},{9,5},... | collective-permute-start | bytes 294920 | tf_op jit(solution)/shard_map/ppermute | solution.py:276
  87.8 4.1 %collective-permute-start.35 = (bf16[2,48,512]{2,1,0:T(8,128)(2,1)S(1)}, bf16[2,48,512]{2,1,0:T(8,128)(2,1)S(1)}, u32[]{:S(2)}, u32[]{:S(2)}) collective-permute-start(bf16[2,48,512]{2,1,0:T(8,128)(2,1)S(1)} %get-tuple-element.109), channel_id=1, source_target_pairs={{0,2},{1,3},{2,0},{3,1},{4,6},{5,7},{6,4},{7,5},{8,10},{9,11},{10,... | collective-permute-start | bytes 294920 | tf_op jit(solution)/shard_map/ppermute | solution.py:276
  92.3 3.9 %collective-permute-start.37 = (bf16[2,48,512]{2,1,0:T(8,128)(2,1)S(1)}, bf16[2,48,512]{2,1,0:T(8,128)(2,1)S(1)}, u32[]{:S(2)}, u32[]{:S(2)}) collective-permute-start(bf16[2,48,512]{2,1,0:T(8,128)(2,1)S(1)} %get-tuple-element.111), channel_id=1, source_target_pairs={{0,6},{1,7},{2,4},{3,5},{4,2},{5,3},{6,0},{7,1},{8,14},{9,15},{10,... | collective-permute-start | bytes 294920 | tf_op jit(solution)/shard_map/ppermute | solution.py:276
  96.1 2.5 %collective-permute-start.38 = (bf16[2,48,512]{2,1,0:T(8,128)(2,1)S(1)}, bf16[2,48,512]{2,1,0:T(8,128)(2,1)S(1)}, u32[]{:S(2)}, u32[]{:S(2)}) collective-permute-start(bf16[2,48,512]{2,1,0:T(8,128)(2,1)S(1)} %get-tuple-element.112), channel_id=1, source_target_pairs={{0,10},{1,11},{2,8},{3,9},{4,14},{5,15},{6,12},{7,13},{8,2},{9,3},... | collective-permute-start | bytes 294920 | tf_op jit(solution)/shard_map/ppermute | solution.py:276
  98.7 5.2 %collective-permute-start.40 = (bf16[2,48,512]{2,1,0:T(8,128)(2,1)S(1)}, bf16[2,48,512]{2,1,0:T(8,128)(2,1)S(1)}, u32[]{:S(2)}, u32[]{:S(2)}) collective-permute-start(bf16[2,48,512]{2,1,0:T(8,128)(2,1)S(1)} %get-tuple-element.114), channel_id=1, source_target_pairs={{0,14},{1,15},{2,12},{3,13},{4,10},{5,11},{6,8},{7,9},{8,6},{9,7},... | collective-permute-start | bytes 294920 | tf_op jit(solution)/shard_map/ppermute | solution.py:276
  104.7 3.6 %collective-permute-done.38.refs_25_ = bf16[2,48,512]{2,1,0:T(8,128)(2,1)S(1)} collective-permute-done((bf16[2,48,512]{2,1,0:T(8,128)(2,1)S(1)}, bf16[2,48,512]{2,1,0:T(8,128)(2,1)S(1)}, u32[]{:S(2)}, u32[]{:S(2)}) %collective-permute-start.38) | collective-permute-done | bytes 98336 | tf_op jit(solution)/shard_map/ppermute | solution.py:276
  109.3 6.8 %collective-permute-done.42.refs_29_ = bf16[2,48,512]{2,1,0:T(8,128)(2,1)S(1)} collective-permute-done((bf16[2,48,512]{2,1,0:T(8,128)(2,1)S(1)}, bf16[2,48,512]{2,1,0:T(8,128)(2,1)S(1)}, u32[]{:S(2)}, u32[]{:S(2)}) %collective-permute-start.42) | collective-permute-done | bytes 98336 | tf_op jit(solution)/shard_map/ppermute | solution.py:276
  116.5 4.7 %update.1 = (bf16[384,1024]{1,0:T(8,128)(2,1)}, bf16[384,1024]{1,0:T(8,128)(2,1)}, bf16[32,1024]{1,0:T(8,128)(2,1)S(1)}, bf16[32,1024]{1,0:T(8,128)(2,1)S(1)}, b...) custom-call(s32[1]{0:T(128)} %bitcast.me_ref, ...), custom_call_target="tpu_custom_call" | custom-call | flops 2239758336 | bytes 6029312 | tf_op jit(solution)/shard_map/update/pallas_call | solution.py:213
  121.2 3.2 %collective-permute-start.45 = (bf16[32,1024]{1,0:T(8,128)(2,1)S(1)}, bf16[32,1024]{1,0:T(8,128)(2,1)S(1)}, u32[]{:S(2)}, u32[]{:S(2)}) collective-permute-start(bf16[32,1024]{1,0:T(8,128)(2,1)S(1)} %get-tuple-element.124), channel_id=1, source_target_pairs={{0,8},{1,9},{2,10},{3,11},{4,12},{5,13},{6,14},{7,15},{8,0},{9,1},... | collective-permute-start | bytes 196616 | tf_op jit(solution)/shard_map/ppermute | solution.py:276
  126.1 3.3 %collective-permute-start.49 = (bf16[32,1024]{1,0:T(8,128)(2,1)S(1)}, bf16[32,1024]{1,0:T(8,128)(2,1)S(1)}, u32[]{:S(2)}, u32[]{:S(2)}) collective-permute-start(bf16[32,1024]{1,0:T(8,128)(2,1)S(1)} %get-tuple-element.128), channel_id=1, source_target_pairs={{0,9},{1,8},{2,11},{3,10},{4,13},{5,12},{6,15},{7,14},{8,1},{9,0},... | collective-permute-start | bytes 196616 | tf_op jit(solution)/shard_map/ppermute | solution.py:276
  131.4 2.4 %collective-permute-done.48.refs_4_ = bf16[32,1024]{1,0:T(8,128)(2,1)S(1)} collective-permute-done((bf16[32,1024]{1,0:T(8,128)(2,1)S(1)}, bf16[32,1024]{1,0:T(8,128)(2,1)S(1)}, u32[]{:S(2)}, u32[]{:S(2)}) %collective-permute-start.48) | collective-permute-done | bytes 65568 | tf_op jit(solution)/shard_map/ppermute | solution.py:276
  135.0 2.5 %collective-permute-start.55 = (bf16[32,1024]{1,0:T(8,128)(2,1)S(1)}, bf16[32,1024]{1,0:T(8,128)(2,1)S(1)}, u32[]{:S(2)}, u32[]{:S(2)}) collective-permute-start(bf16[32,1024]{1,0:T(8,128)(2,1)S(1)} %get-tuple-element.134), channel_id=1, source_target_pairs={{0,14},{1,15},{2,12},{3,13},{4,10},{5,11},{6,8},{7,9},{8,6},{9,7},... | collective-permute-start | bytes 196616 | tf_op jit(solution)/shard_map/ppermute | solution.py:276
  140.0 2.8 %collective-permute-done.53.refs_9_ = bf16[32,1024]{1,0:T(8,128)(2,1)S(1)} collective-permute-done((bf16[32,1024]{1,0:T(8,128)(2,1)S(1)}, bf16[32,1024]{1,0:T(8,128)(2,1)S(1)}, u32[]{:S(2)}, u32[]{:S(2)}) %collective-permute-start.53) | collective-permute-done | bytes 65568 | tf_op jit(solution)/shard_map/ppermute | solution.py:276
  143.0 3.6 %collective-permute-done.57.refs_13_ = bf16[32,1024]{1,0:T(8,128)(2,1)S(1)} collective-permute-done((bf16[32,1024]{1,0:T(8,128)(2,1)S(1)}, bf16[32,1024]{1,0:T(8,128)(2,1)S(1)}, u32[]{:S(2)}, u32[]{:S(2)}) %collective-permute-start.57) | collective-permute-done | bytes 65568 | tf_op jit(solution)/shard_map/ppermute | solution.py:276
  (109 shorter events, 32.8 us)
Async XLA Ops:
  8.9 11.4 %collective-permute-start.18 = (bf16[2,48,512]{2,1,0:T(8,128)(2,1)}, bf16[2,48,512]{2,1,0:T(8,128)(2,1)S(1)}, u32[]{:S(2)}, u32[]{:S(2)}) collective-permute-start(bf16[2,48,512]{2,1,0:T(8,128)(2,1)} %get-tuple-element.91), channel_id=1, source_target_pairs={{0,12},{1,13},{2,14},{3,15},{4,8},{5,9},{6,10},{7,11},{8,4},{9,5},... | collective-permute-start | bytes 294920 | tf_op jit(solution)/shard_map/ppermute | solution.py:276
  10.2 11.4 %collective-permute-start.19 = (bf16[2,48,512]{2,1,0:T(8,128)(2,1)}, bf16[2,48,512]{2,1,0:T(8,128)(2,1)S(1)}, u32[]{:S(2)}, u32[]{:S(2)}) collective-permute-start(bf16[2,48,512]{2,1,0:T(8,128)(2,1)} %get-tuple-element.92), channel_id=1, source_target_pairs={{0,7},{1,6},{2,5},{3,4},{4,3},{5,2},{6,1},{7,0},{8,15},{9,14},{10,... | collective-permute-start | bytes 294920 | tf_op jit(solution)/shard_map/ppermute | solution.py:276
  10.3 13.1 %collective-permute-start.20 = (bf16[2,48,512]{2,1,0:T(8,128)(2,1)}, bf16[2,48,512]{2,1,0:T(8,128)(2,1)S(1)}, u32[]{:S(2)}, u32[]{:S(2)}) collective-permute-start(bf16[2,48,512]{2,1,0:T(8,128)(2,1)} %get-tuple-element.93), channel_id=1, source_target_pairs={{0,9},{1,8},{2,11},{3,10},{4,13},{5,12},{6,15},{7,14},{8,1},{9,0},... | collective-permute-start | bytes 294920 | tf_op jit(solution)/shard_map/ppermute | solution.py:276
  13.5 15.0 %collective-permute-start.21 = (bf16[2,48,512]{2,1,0:T(8,128)(2,1)}, bf16[2,48,512]{2,1,0:T(8,128)(2,1)S(1)}, u32[]{:S(2)}, u32[]{:S(2)}) collective-permute-start(bf16[2,48,512]{2,1,0:T(8,128)(2,1)} %get-tuple-element.94), channel_id=1, source_target_pairs={{0,2},{1,3},{2,0},{3,1},{4,6},{5,7},{6,4},{7,5},{8,10},{9,11},{10,... | collective-permute-start | bytes 294920 | tf_op jit(solution)/shard_map/ppermute | solution.py:276
  17.4 11.0 %collective-permute-start.22 = (bf16[2,48,512]{2,1,0:T(8,128)(2,1)}, bf16[2,48,512]{2,1,0:T(8,128)(2,1)S(1)}, u32[]{:S(2)}, u32[]{:S(2)}) collective-permute-start(bf16[2,48,512]{2,1,0:T(8,128)(2,1)} %get-tuple-element.95), channel_id=1, source_target_pairs={{0,13},{1,12},{2,15},{3,14},{4,9},{5,8},{6,11},{7,10},{8,5},{9,4},... | collective-permute-start | bytes 294920 | tf_op jit(solution)/shard_map/ppermute | solution.py:276
  20.3 13.3 %collective-permute-start.23 = (bf16[2,48,512]{2,1,0:T(8,128)(2,1)}, bf16[2,48,512]{2,1,0:T(8,128)(2,1)S(1)}, u32[]{:S(2)}, u32[]{:S(2)}) collective-permute-start(bf16[2,48,512]{2,1,0:T(8,128)(2,1)} %get-tuple-element.96), channel_id=1, source_target_pairs={{0,6},{1,7},{2,4},{3,5},{4,2},{5,3},{6,0},{7,1},{8,14},{9,15},{10,... | collective-permute-start | bytes 294920 | tf_op jit(solution)/shard_map/ppermute | solution.py:276
  21.6 12.1 %collective-permute-start.24 = (bf16[2,48,512]{2,1,0:T(8,128)(2,1)}, bf16[2,48,512]{2,1,0:T(8,128)(2,1)S(1)}, u32[]{:S(2)}, u32[]{:S(2)}) collective-permute-start(bf16[2,48,512]{2,1,0:T(8,128)(2,1)} %get-tuple-element.97), channel_id=1, source_target_pairs={{0,10},{1,11},{2,8},{3,9},{4,14},{5,15},{6,12},{7,13},{8,2},{9,3},... | collective-permute-start | bytes 294920 | tf_op jit(solution)/shard_map/ppermute | solution.py:276
  23.4 16.9 %collective-permute-start.25 = (bf16[2,48,512]{2,1,0:T(8,128)(2,1)}, bf16[2,48,512]{2,1,0:T(8,128)(2,1)S(1)}, u32[]{:S(2)}, u32[]{:S(2)}) collective-permute-start(bf16[2,48,512]{2,1,0:T(8,128)(2,1)} %get-tuple-element.98), channel_id=1, source_target_pairs={{0,14},{1,15},{2,12},{3,13},{4,10},{5,11},{6,8},{7,9},{8,6},{9,7},... | collective-permute-start | bytes 294920 | tf_op jit(solution)/shard_map/ppermute | solution.py:276
  28.4 13.0 %collective-permute-start.26 = (bf16[2,48,512]{2,1,0:T(8,128)(2,1)}, bf16[2,48,512]{2,1,0:T(8,128)(2,1)S(1)}, u32[]{:S(2)}, u32[]{:S(2)}) collective-permute-start(bf16[2,48,512]{2,1,0:T(8,128)(2,1)} %get-tuple-element.99), channel_id=1, source_target_pairs={{0,5},{1,4},{2,7},{3,6},{4,1},{5,0},{6,3},{7,2},{8,13},{9,12},{10,... | collective-permute-start | bytes 294920 | tf_op jit(solution)/shard_map/ppermute | solution.py:276
  28.4 16.1 %collective-permute-start.27 = (bf16[2,48,512]{2,1,0:T(8,128)(2,1)}, bf16[2,48,512]{2,1,0:T(8,128)(2,1)S(1)}, u32[]{:S(2)}, u32[]{:S(2)}) collective-permute-start(bf16[2,48,512]{2,1,0:T(8,128)(2,1)} %get-tuple-element.100), channel_id=1, source_target_pairs={{0,11},{1,10},{2,9},{3,8},{4,15},{5,14},{6,13},{7,12},{8,3},{9,2},... | collective-permute-start | bytes 294920 | tf_op jit(solution)/shard_map/ppermute | solution.py:276
  33.6 11.0 %collective-permute-start.28 = (bf16[2,48,512]{2,1,0:T(8,128)(2,1)}, bf16[2,48,512]{2,1,0:T(8,128)(2,1)S(1)}, u32[]{:S(2)}, u32[]{:S(2)}) collective-permute-start(bf16[2,48,512]{2,1,0:T(8,128)(2,1)} %get-tuple-element.101), channel_id=1, source_target_pairs={{0,4},{1,5},{2,6},{3,7},{4,0},{5,1},{6,2},{7,3},{8,12},{9,13},{10,... | collective-permute-start | bytes 294920 | tf_op jit(solution)/shard_map/ppermute | solution.py:276
  33.7 13.2 %collective-permute-start.29 = (bf16[2,48,512]{2,1,0:T(8,128)(2,1)}, bf16[2,48,512]{2,1,0:T(8,128)(2,1)S(1)}, u32[]{:S(2)}, u32[]{:S(2)}) collective-permute-start(bf16[2,48,512]{2,1,0:T(8,128)(2,1)} %get-tuple-element.102), channel_id=1, source_target_pairs={{0,15},{1,14},{2,13},{3,12},{4,11},{5,10},{6,9},{7,8},{8,7},{9,6},... | collective-permute-start | bytes 294920 | tf_op jit(solution)/shard_map/ppermute | solution.py:276
  41.4 12.2 %collective-permute-start.2 = (bf16[32,1792]{1,0:T(8,128)(2,1)S(1)}, bf16[32,1792]{1,0:T(8,128)(2,1)S(1)}, u32[]{:S(2)}, u32[]{:S(2)}) collective-permute-start(bf16[32,1792]{1,0:T(8,128)(2,1)S(1)} %get-tuple-element.74), channel_id=1, source_target_pairs={{0,3},{1,2},{2,1},{3,0},{4,7},{5,6},{6,5},{7,4},{8,11},{9,10},{10,... | collective-permute-start | bytes 344072 | tf_op jit(solution)/shard_map/ppermute | solution.py:276
  44.6 16.5 %collective-permute-start.4 = (bf16[32,1792]{1,0:T(8,128)(2,1)S(1)}, bf16[32,1792]{1,0:T(8,128)(2,1)S(1)}, u32[]{:S(2)}, u32[]{:S(2)}) collective-permute-start(bf16[32,1792]{1,0:T(8,128)(2,1)S(1)} %get-tuple-element.76), channel_id=1, source_target_pairs={{0,7},{1,6},{2,5},{3,4},{4,3},{5,2},{6,1},{7,0},{8,15},{9,14},{10,... | collective-permute-start | bytes 344072 | tf_op jit(solution)/shard_map/ppermute | solution.py:276
  46.9 14.5 %collective-permute-start.5 = (bf16[32,1792]{1,0:T(8,128)(2,1)S(1)}, bf16[32,1792]{1,0:T(8,128)(2,1)S(1)}, u32[]{:S(2)}, u32[]{:S(2)}) collective-permute-start(bf16[32,1792]{1,0:T(8,128)(2,1)S(1)} %get-tuple-element.77), channel_id=1, source_target_pairs={{0,9},{1,8},{2,11},{3,10},{4,13},{5,12},{6,15},{7,14},{8,1},{9,0},... | collective-permute-start | bytes 344072 | tf_op jit(solution)/shard_map/ppermute | solution.py:276
  53.6 11.2 %collective-permute-start.7 = (bf16[32,1792]{1,0:T(8,128)(2,1)S(1)}, bf16[32,1792]{1,0:T(8,128)(2,1)S(1)}, u32[]{:S(2)}, u32[]{:S(2)}) collective-permute-start(bf16[32,1792]{1,0:T(8,128)(2,1)S(1)} %get-tuple-element.79), channel_id=1, source_target_pairs={{0,13},{1,12},{2,15},{3,14},{4,9},{5,8},{6,11},{7,10},{8,5},{9,4},... | collective-permute-start | bytes 344072 | tf_op jit(solution)/shard_map/ppermute | solution.py:276
  54.7 11.4 %collective-permute-start.8 = (bf16[32,1792]{1,0:T(8,128)(2,1)S(1)}, bf16[32,1792]{1,0:T(8,128)(2,1)S(1)}, u32[]{:S(2)}, u32[]{:S(2)}) collective-permute-start(bf16[32,1792]{1,0:T(8,128)(2,1)S(1)} %get-tuple-element.80), channel_id=1, source_target_pairs={{0,6},{1,7},{2,4},{3,5},{4,2},{5,3},{6,0},{7,1},{8,14},{9,15},{10,... | collective-permute-start | bytes 344072 | tf_op jit(solution)/shard_map/ppermute | solution.py:276
  61.0 11.7 %collective-permute-start.9 = (bf16[32,1792]{1,0:T(8,128)(2,1)S(1)}, bf16[32,1792]{1,0:T(8,128)(2,1)S(1)}, u32[]{:S(2)}, u32[]{:S(2)}) collective-permute-start(bf16[32,1792]{1,0:T(8,128)(2,1)S(1)} %get-tuple-element.81), channel_id=1, source_target_pairs={{0,10},{1,11},{2,8},{3,9},{4,14},{5,15},{6,12},{7,13},{8,2},{9,3},... | collective-permute-start | bytes 344072 | tf_op jit(solution)/shard_map/ppermute | solution.py:276
  61.4 11.4 %collective-permute-start.10 = (bf16[32,1792]{1,0:T(8,128)(2,1)S(1)}, bf16[32,1792]{1,0:T(8,128)(2,1)S(1)}, u32[]{:S(2)}, u32[]{:S(2)}) collective-permute-start(bf16[32,1792]{1,0:T(8,128)(2,1)S(1)} %get-tuple-element.82), channel_id=1, source_target_pairs={{0,1},{1,0},{2,3},{3,2},{4,5},{5,4},{6,7},{7,6},{8,9},{9,8},{10,11... | collective-permute-start | bytes 344072 | tf_op jit(solution)/shard_map/ppermute | solution.py:276
  61.4 13.5 %collective-permute-start.11 = (bf16[32,1792]{1,0:T(8,128)(2,1)S(1)}, bf16[32,1792]{1,0:T(8,128)(2,1)S(1)}, u32[]{:S(2)}, u32[]{:S(2)}) collective-permute-start(bf16[32,1792]{1,0:T(8,128)(2,1)S(1)} %get-tuple-element.83), channel_id=1, source_target_pairs={{0,14},{1,15},{2,12},{3,13},{4,10},{5,11},{6,8},{7,9},{8,6},{9,7},... | collective-permute-start | bytes 344072 | tf_op jit(solution)/shard_map/ppermute | solution.py:276
  64.8 13.8 %collective-permute-start.12 = (bf16[32,1792]{1,0:T(8,128)(2,1)S(1)}, bf16[32,1792]{1,0:T(8,128)(2,1)S(1)}, u32[]{:S(2)}, u32[]{:S(2)}) collective-permute-start(bf16[32,1792]{1,0:T(8,128)(2,1)S(1)} %get-tuple-element.84), channel_id=1, source_target_pairs={{0,5},{1,4},{2,7},{3,6},{4,1},{5,0},{6,3},{7,2},{8,13},{9,12},{10,... | collective-permute-start | bytes 344072 | tf_op jit(solution)/shard_map/ppermute | solution.py:276
  66.2 17.8 %collective-permute-start.13 = (bf16[32,1792]{1,0:T(8,128)(2,1)S(1)}, bf16[32,1792]{1,0:T(8,128)(2,1)S(1)}, u32[]{:S(2)}, u32[]{:S(2)}) collective-permute-start(bf16[32,1792]{1,0:T(8,128)(2,1)S(1)} %get-tuple-element.85), channel_id=1, source_target_pairs={{0,11},{1,10},{2,9},{3,8},{4,15},{5,14},{6,13},{7,12},{8,3},{9,2},... | collective-permute-start | bytes 344072 | tf_op jit(solution)/shard_map/ppermute | solution.py:276
  72.7 13.8 %collective-permute-start.14 = (bf16[32,1792]{1,0:T(8,128)(2,1)S(1)}, bf16[32,1792]{1,0:T(8,128)(2,1)S(1)}, u32[]{:S(2)}, u32[]{:S(2)}) collective-permute-start(bf16[32,1792]{1,0:T(8,128)(2,1)S(1)} %get-tuple-element.86), channel_id=1, source_target_pairs={{0,4},{1,5},{2,6},{3,7},{4,0},{5,1},{6,2},{7,3},{8,12},{9,13},{10,... | collective-permute-start | bytes 344072 | tf_op jit(solution)/shard_map/ppermute | solution.py:276
  72.7 13.8 %collective-permute-start.15 = (bf16[32,1792]{1,0:T(8,128)(2,1)S(1)}, bf16[32,1792]{1,0:T(8,128)(2,1)S(1)}, u32[]{:S(2)}, u32[]{:S(2)}) collective-permute-start(bf16[32,1792]{1,0:T(8,128)(2,1)S(1)} %get-tuple-element.87), channel_id=1, source_target_pairs={{0,15},{1,14},{2,13},{3,12},{4,11},{5,10},{6,9},{7,8},{8,7},{9,6},... | collective-permute-start | bytes 344072 | tf_op jit(solution)/shard_map/ppermute | solution.py:276
  74.9 12.9 %collective-permute-start.30 = (bf16[2,48,512]{2,1,0:T(8,128)(2,1)S(1)}, bf16[2,48,512]{2,1,0:T(8,128)(2,1)S(1)}, u32[]{:S(2)}, u32[]{:S(2)}) collective-permute-start(bf16[2,48,512]{2,1,0:T(8,128)(2,1)S(1)} %get-tuple-element.104), channel_id=1, source_target_pairs={{0,8},{1,9},{2,10},{3,11},{4,12},{5,13},{6,14},{7,15},{8,0},{9,1},... | collective-permute-start | bytes 294920 | tf_op jit(solution)/shard_map/ppermute | solution.py:276
  78.6 13.3 %collective-permute-start.31 = (bf16[2,48,512]{2,1,0:T(8,128)(2,1)S(1)}, bf16[2,48,512]{2,1,0:T(8,128)(2,1)S(1)}, u32[]{:S(2)}, u32[]{:S(2)}) collective-permute-start(bf16[2,48,512]{2,1,0:T(8,128)(2,1)S(1)} %get-tuple-element.105), channel_id=1, source_target_pairs={{0,3},{1,2},{2,1},{3,0},{4,7},{5,6},{6,5},{7,4},{8,11},{9,10},{10,... | collective-permute-start | bytes 294920 | tf_op jit(solution)/shard_map/ppermute | solution.py:276
  86.5 12.1 %collective-permute-start.34 = (bf16[2,48,512]{2,1,0:T(8,128)(2,1)S(1)}, bf16[2,48,512]{2,1,0:T(8,128)(2,1)S(1)}, u32[]{:S(2)}, u32[]{:S(2)}) collective-permute-start(bf16[2,48,512]{2,1,0:T(8,128)(2,1)S(1)} %get-tuple-element.108), channel_id=1, source_target_pairs={{0,9},{1,8},{2,11},{3,10},{4,13},{5,12},{6,15},{7,14},{8,1},{9,0},... | collective-permute-start | bytes 294920 | tf_op jit(solution)/shard_map/ppermute | solution.py:276
  87.8 10.9 %collective-permute-start.35 = (bf16[2,48,512]{2,1,0:T(8,128)(2,1)S(1)}, bf16[2,48,512]{2,1,0:T(8,128)(2,1)S(1)}, u32[]{:S(2)}, u32[]{:S(2)}) collective-permute-start(bf16[2,48,512]{2,1,0:T(8,128)(2,1)S(1)} %get-tuple-element.109), channel_id=1, source_target_pairs={{0,2},{1,3},{2,0},{3,1},{4,6},{5,7},{6,4},{7,5},{8,10},{9,11},{10,... | collective-permute-start | bytes 294920 | tf_op jit(solution)/shard_map/ppermute | solution.py:276
  91.9 11.9 %collective-permute-start.36 = (bf16[2,48,512]{2,1,0:T(8,128)(2,1)S(1)}, bf16[2,48,512]{2,1,0:T(8,128)(2,1)S(1)}, u32[]{:S(2)}, u32[]{:S(2)}) collective-permute-start(bf16[2,48,512]{2,1,0:T(8,128)(2,1)S(1)} %get-tuple-element.110), channel_id=1, source_target_pairs={{0,13},{1,12},{2,15},{3,14},{4,9},{5,8},{6,11},{7,10},{8,5},{9,4},... | collective-permute-start | bytes 294920 | tf_op jit(solution)/shard_map/ppermute | solution.py:276
  92.3 11.6 %collective-permute-start.37 = (bf16[2,48,512]{2,1,0:T(8,128)(2,1)S(1)}, bf16[2,48,512]{2,1,0:T(8,128)(2,1)S(1)}, u32[]{:S(2)}, u32[]{:S(2)}) collective-permute-start(bf16[2,48,512]{2,1,0:T(8,128)(2,1)S(1)} %get-tuple-element.111), channel_id=1, source_target_pairs={{0,6},{1,7},{2,4},{3,5},{4,2},{5,3},{6,0},{7,1},{8,14},{9,15},{10,... | collective-permute-start | bytes 294920 | tf_op jit(solution)/shard_map/ppermute | solution.py:276
  96.1 12.2 %collective-permute-start.38 = (bf16[2,48,512]{2,1,0:T(8,128)(2,1)S(1)}, bf16[2,48,512]{2,1,0:T(8,128)(2,1)S(1)}, u32[]{:S(2)}, u32[]{:S(2)}) collective-permute-start(bf16[2,48,512]{2,1,0:T(8,128)(2,1)S(1)} %get-tuple-element.112), channel_id=1, source_target_pairs={{0,10},{1,11},{2,8},{3,9},{4,14},{5,15},{6,12},{7,13},{8,2},{9,3},... | collective-permute-start | bytes 294920 | tf_op jit(solution)/shard_map/ppermute | solution.py:276
  103.9 12.2 %collective-permute-start.42 = (bf16[2,48,512]{2,1,0:T(8,128)(2,1)S(1)}, bf16[2,48,512]{2,1,0:T(8,128)(2,1)S(1)}, u32[]{:S(2)}, u32[]{:S(2)}) collective-permute-start(bf16[2,48,512]{2,1,0:T(8,128)(2,1)S(1)} %get-tuple-element.116), channel_id=1, source_target_pairs={{0,11},{1,10},{2,9},{3,8},{4,15},{5,14},{6,13},{7,12},{8,3},{9,2},... | collective-permute-start | bytes 294920 | tf_op jit(solution)/shard_map/ppermute | solution.py:276
  (36 other events, 400.9 us)

commit v20 on v10

--- a/solution.py
+++ b/solution.py
@@ -266,7 +266,7 @@
 
     half = groups // 2
     far, near = both_ends(list(range(half, groups))), both_ends(list(range(half - 1, 0, -1)))
-    return [0] + [s for pair in zip(far, near + [None]) for s in pair if s is not None]
+    return [0] + [s for pair in zip(far, near + [None]) for s in pair if s is not None][::-1]
 
 
 def swap(pieces):
@@ -445,7 +445,7 @@
     )
 
     def per_device(*args):
-        few = groups & (groups - 1) == 0 and groups <= 2 * args[0].shape[0] // groups
+        few = groups >= 8 and groups & (groups - 1) == 0 and groups <= 2 * args[0].shape[0] // groups
         return (partner_plan if few else routed_plan)(*args)
 
     return jax.shard_map(

time: 149 us -> 152 us (1.020)
  waiting for transfers between devices: 24.5 us -> 39.9 us
  starting transfers between devices: 110 us -> 97.4 us
    ppermute x60, waiting for transfers between devices: 24.5 us -> 39.9 us  [swap(): lax.ppermute(piece, 'expert', [(i, i ^ s) for i in range(groups)])]
    ppermute x60, starting transfers between devices: 110 us -> 97.4 us  [swap(): lax.ppermute(piece, 'expert', [(i, i ^ s) for i in range(groups)])]
  transfers between devices with their start and end apart: 60 -> 60, of which waited for: 12 -> 19; matrix products, arithmetic and copies ran while one was open for 0% -> 0% of each run, Pallas kernels for 2% -> 2%
where the time goes in v20:
time: 152 us
  starting transfers between devices  97.4 us (64%)
  waiting for transfers between devices  39.9 us (26%)
  Pallas kernels  12.3 us (8%)
    ppermute x60, starting transfers between devices, swap(): lax.ppermute(piece, 'expert', [(i, i ^ s) for i in range(groups)])  97.4 us
    ppermute x60, waiting for transfers between devices, swap(): lax.ppermute(piece, 'expert', [(i, i ^ s) for i in range(groups)])  39.9 us
    pallas_call x1, Pallas kernels, update(): pl.pallas_call(functools.partial(update_kernel, groups), out_shape=(shape...  4.74 us
  transfers between devices with their start and end apart: 60, of which 19 were waited for; matrix products, arithmetic and copies ran while one was open for 0% of the time, Pallas kernels for 2%

profile of v20, /device:TPU:0, one launch (start us, length us, event | category | flops | bytes accessed | tf_op | source)
XLA Modules:
  0.0 151.7 jit_solution(12667223758532076953)
XLA Ops:
  0.7 2.7 %split.1 = (bf16[2,48,512]{2,1,0:T(8,128)(2,1)}, bf16[2,48,512]{2,1,0:T(8,128)(2,1)}, bf16[2,48,512]{2,1,0:T(8,128)(2,1)}, bf16[2,48,512]{2,1,0:T(8,128)(2,1)}, ...) custom-call(s32[1]{0:T(128)} %bitcast.me_ref, ...), custom_call_target="tpu_custom_call" | custom-call | bytes 3145728 | tf_op jit(solution)/shard_map/split/pallas_call | solution.py:135
  3.4 4.0 %collective-permute-start = (bf16[2,48,512]{2,1,0:T(8,128)(2,1)}, bf16[2,48,512]{2,1,0:T(8,128)(2,1)S(1)}, u32[]{:S(2)}, u32[]{:S(2)}) collective-permute-start(bf16[2,48,512]{2,1,0:T(8,128)(2,1)} %get-tuple-element.71), channel_id=1, source_target_pairs={{0,6},{1,7},{2,4},{3,5},{4,2},{5,3},{6,0},{7,1},{8,14},{9,15},{10,... | collective-permute-start | bytes 294920 | tf_op jit(solution)/shard_map/ppermute | solution.py:276
  9.7 2.5 %collective-permute-start.18 = (bf16[2,48,512]{2,1,0:T(8,128)(2,1)}, bf16[2,48,512]{2,1,0:T(8,128)(2,1)S(1)}, u32[]{:S(2)}, u32[]{:S(2)}) collective-permute-start(bf16[2,48,512]{2,1,0:T(8,128)(2,1)} %get-tuple-element.91), channel_id=1, source_target_pairs={{0,11},{1,10},{2,9},{3,8},{4,15},{5,14},{6,13},{7,12},{8,3},{9,2},... | collective-permute-start | bytes 294920 | tf_op jit(solution)/shard_map/ppermute | solution.py:276
  12.2 3.2 %collective-permute-start.20 = (bf16[2,48,512]{2,1,0:T(8,128)(2,1)}, bf16[2,48,512]{2,1,0:T(8,128)(2,1)S(1)}, u32[]{:S(2)}, u32[]{:S(2)}) collective-permute-start(bf16[2,48,512]{2,1,0:T(8,128)(2,1)} %get-tuple-element.93), channel_id=1, source_target_pairs={{0,14},{1,15},{2,12},{3,13},{4,10},{5,11},{6,8},{7,9},{8,6},{9,7},... | collective-permute-start | bytes 294920 | tf_op jit(solution)/shard_map/ppermute | solution.py:276
  16.1 2.4 %collective-permute-done.17.refs_2_ = bf16[2,48,512]{2,1,0:T(8,128)(2,1)S(1)} collective-permute-done((bf16[2,48,512]{2,1,0:T(8,128)(2,1)}, bf16[2,48,512]{2,1,0:T(8,128)(2,1)S(1)}, u32[]{:S(2)}, u32[]{:S(2)}) %collective-permute-start.17) | collective-permute-done | bytes 98336 | tf_op jit(solution)/shard_map/ppermute | solution.py:276
  18.5 3.4 %collective-permute-done.18.refs_3_ = bf16[2,48,512]{2,1,0:T(8,128)(2,1)S(1)} collective-permute-done((bf16[2,48,512]{2,1,0:T(8,128)(2,1)}, bf16[2,48,512]{2,1,0:T(8,128)(2,1)S(1)}, u32[]{:S(2)}, u32[]{:S(2)}) %collective-permute-start.18) | collective-permute-done | bytes 98336 | tf_op jit(solution)/shard_map/ppermute | solution.py:276
  21.9 3.1 %collective-permute-start.24 = (bf16[2,48,512]{2,1,0:T(8,128)(2,1)}, bf16[2,48,512]{2,1,0:T(8,128)(2,1)S(1)}, u32[]{:S(2)}, u32[]{:S(2)}) collective-permute-start(bf16[2,48,512]{2,1,0:T(8,128)(2,1)} %get-tuple-element.97), channel_id=1, source_target_pairs={{0,13},{1,12},{2,15},{3,14},{4,9},{5,8},{6,11},{7,10},{8,5},{9,4},... | collective-permute-start | bytes 294920 | tf_op jit(solution)/shard_map/ppermute | solution.py:276
  25.0 3.4 %collective-permute-start.25 = (bf16[2,48,512]{2,1,0:T(8,128)(2,1)}, bf16[2,48,512]{2,1,0:T(8,128)(2,1)S(1)}, u32[]{:S(2)}, u32[]{:S(2)}) collective-permute-start(bf16[2,48,512]{2,1,0:T(8,128)(2,1)} %get-tuple-element.98), channel_id=1, source_target_pairs={{0,9},{1,8},{2,11},{3,10},{4,13},{5,12},{6,15},{7,14},{8,1},{9,0},... | collective-permute-start | bytes 294920 | tf_op jit(solution)/shard_map/ppermute | solution.py:276
  31.5 5.9 %collective-permute-start.29 = (bf16[2,48,512]{2,1,0:T(8,128)(2,1)}, bf16[2,48,512]{2,1,0:T(8,128)(2,1)S(1)}, u32[]{:S(2)}, u32[]{:S(2)}) collective-permute-start(bf16[2,48,512]{2,1,0:T(8,128)(2,1)} %get-tuple-element.102), channel_id=1, source_target_pairs={{0,8},{1,9},{2,10},{3,11},{4,12},{5,13},{6,14},{7,15},{8,0},{9,1},... | collective-permute-start | bytes 294920 | tf_op jit(solution)/shard_map/ppermute | solution.py:276
  38.8 2.8 %pack_rows.1 = (bf16[32,1792]{1,0:T(8,128)(2,1)S(1)}, bf16[32,1792]{1,0:T(8,128)(2,1)S(1)}, bf16[32,1792]{1,0:T(8,128)(2,1)S(1)}, bf16[32,1792]{1,0:T(8,128)(2,1...) custom-call(s32[1]{0:T(128)S(6)} %copy.13.live_ref, ...), custom_call_target="tpu_custom_call" | custom-call | flops 469762048 | bytes 2752512 | tf_op jit(solution)/shard_map/pack_rows/pallas_call | solution.py:107
  43.0 3.4 %collective-permute-start.3 = (bf16[32,1792]{1,0:T(8,128)(2,1)S(1)}, bf16[32,1792]{1,0:T(8,128)(2,1)S(1)}, u32[]{:S(2)}, u32[]{:S(2)}) collective-permute-start(bf16[32,1792]{1,0:T(8,128)(2,1)S(1)} %get-tuple-element.75), channel_id=1, source_target_pairs={{0,11},{1,10},{2,9},{3,8},{4,15},{5,14},{6,13},{7,12},{8,3},{9,2},... | collective-permute-start | bytes 344072 | tf_op jit(solution)/shard_map/ppermute | solution.py:276
  46.5 3.5 %collective-permute-start.5 = (bf16[32,1792]{1,0:T(8,128)(2,1)S(1)}, bf16[32,1792]{1,0:T(8,128)(2,1)S(1)}, u32[]{:S(2)}, u32[]{:S(2)}) collective-permute-start(bf16[32,1792]{1,0:T(8,128)(2,1)S(1)} %get-tuple-element.77), channel_id=1, source_target_pairs={{0,14},{1,15},{2,12},{3,13},{4,10},{5,11},{6,8},{7,9},{8,6},{9,7},... | collective-permute-start | bytes 344072 | tf_op jit(solution)/shard_map/ppermute | solution.py:276
  53.5 4.0 %collective-permute-done.3.refs_3_ = bf16[32,1792]{1,0:T(8,128)(2,1)S(1)} collective-permute-done((bf16[32,1792]{1,0:T(8,128)(2,1)S(1)}, bf16[32,1792]{1,0:T(8,128)(2,1)S(1)}, u32[]{:S(2)}, u32[]{:S(2)}) %collective-permute-start.3) | collective-permute-done | bytes 114720 | tf_op jit(solution)/shard_map/ppermute | solution.py:276
  60.9 3.7 %collective-permute-start.11 = (bf16[32,1792]{1,0:T(8,128)(2,1)S(1)}, bf16[32,1792]{1,0:T(8,128)(2,1)S(1)}, u32[]{:S(2)}, u32[]{:S(2)}) collective-permute-start(bf16[32,1792]{1,0:T(8,128)(2,1)S(1)} %get-tuple-element.83), channel_id=1, source_target_pairs={{0,9},{1,8},{2,11},{3,10},{4,13},{5,12},{6,15},{7,14},{8,1},{9,0},... | collective-permute-start | bytes 344072 | tf_op jit(solution)/shard_map/ppermute | solution.py:276
  64.6 3.2 %collective-permute-done.7.refs_7_ = bf16[32,1792]{1,0:T(8,128)(2,1)S(1)} collective-permute-done((bf16[32,1792]{1,0:T(8,128)(2,1)S(1)}, bf16[32,1792]{1,0:T(8,128)(2,1)S(1)}, u32[]{:S(2)}, u32[]{:S(2)}) %collective-permute-start.7) | collective-permute-done | bytes 114720 | tf_op jit(solution)/shard_map/ppermute | solution.py:276
  67.9 3.1 %collective-permute-start.13 = (bf16[32,1792]{1,0:T(8,128)(2,1)S(1)}, bf16[32,1792]{1,0:T(8,128)(2,1)S(1)}, u32[]{:S(2)}, u32[]{:S(2)}) collective-permute-start(bf16[32,1792]{1,0:T(8,128)(2,1)S(1)} %get-tuple-element.85), channel_id=1, source_target_pairs={{0,12},{1,13},{2,14},{3,15},{4,8},{5,9},{6,10},{7,11},{8,4},{9,5},... | collective-permute-start | bytes 344072 | tf_op jit(solution)/shard_map/ppermute | solution.py:276
  74.8 2.3 %collective-permute-done.11.refs_11_ = bf16[32,1792]{1,0:T(8,128)(2,1)S(1)} collective-permute-done((bf16[32,1792]{1,0:T(8,128)(2,1)S(1)}, bf16[32,1792]{1,0:T(8,128)(2,1)S(1)}, u32[]{:S(2)}, u32[]{:S(2)}) %collective-permute-start.11) | collective-permute-done | bytes 114720 | tf_op jit(solution)/shard_map/ppermute | solution.py:276
  77.2 2.9 %collective-permute-start.30 = (bf16[2,48,512]{2,1,0:T(8,128)(2,1)S(1)}, bf16[2,48,512]{2,1,0:T(8,128)(2,1)S(1)}, u32[]{:S(2)}, u32[]{:S(2)}) collective-permute-start(bf16[2,48,512]{2,1,0:T(8,128)(2,1)S(1)} %get-tuple-element.104), channel_id=1, source_target_pairs={{0,15},{1,14},{2,13},{3,12},{4,11},{5,10},{6,9},{7,8},{8,7},{9,6},... | collective-permute-start | bytes 294920 | tf_op jit(solution)/shard_map/ppermute | solution.py:276
  80.1 6.6 %collective-permute-start.32 = (bf16[2,48,512]{2,1,0:T(8,128)(2,1)S(1)}, bf16[2,48,512]{2,1,0:T(8,128)(2,1)S(1)}, u32[]{:S(2)}, u32[]{:S(2)}) collective-permute-start(bf16[2,48,512]{2,1,0:T(8,128)(2,1)S(1)} %get-tuple-element.106), channel_id=1, source_target_pairs={{0,11},{1,10},{2,9},{3,8},{4,15},{5,14},{6,13},{7,12},{8,3},{9,2},... | collective-permute-start | bytes 294920 | tf_op jit(solution)/shard_map/ppermute | solution.py:276
  87.9 4.1 %collective-permute-start.34 = (bf16[2,48,512]{2,1,0:T(8,128)(2,1)S(1)}, bf16[2,48,512]{2,1,0:T(8,128)(2,1)S(1)}, u32[]{:S(2)}, u32[]{:S(2)}) collective-permute-start(bf16[2,48,512]{2,1,0:T(8,128)(2,1)S(1)} %get-tuple-element.108), channel_id=1, source_target_pairs={{0,14},{1,15},{2,12},{3,13},{4,10},{5,11},{6,8},{7,9},{8,6},{9,7},... | collective-permute-start | bytes 294920 | tf_op jit(solution)/shard_map/ppermute | solution.py:276
  95.5 2.6 %collective-permute-start.38 = (bf16[2,48,512]{2,1,0:T(8,128)(2,1)S(1)}, bf16[2,48,512]{2,1,0:T(8,128)(2,1)S(1)}, u32[]{:S(2)}, u32[]{:S(2)}) collective-permute-start(bf16[2,48,512]{2,1,0:T(8,128)(2,1)S(1)} %get-tuple-element.112), channel_id=1, source_target_pairs={{0,13},{1,12},{2,15},{3,14},{4,9},{5,8},{6,11},{7,10},{8,5},{9,4},... | collective-permute-start | bytes 294920 | tf_op jit(solution)/shard_map/ppermute | solution.py:276
  101.7 2.5 %collective-permute-done.36.refs_23_ = bf16[2,48,512]{2,1,0:T(8,128)(2,1)S(1)} collective-permute-done((bf16[2,48,512]{2,1,0:T(8,128)(2,1)S(1)}, bf16[2,48,512]{2,1,0:T(8,128)(2,1)S(1)}, u32[]{:S(2)}, u32[]{:S(2)}) %collective-permute-start.36) | collective-permute-done | bytes 98336 | tf_op jit(solution)/shard_map/ppermute | solution.py:276
  104.7 2.8 %collective-permute-start.42 = (bf16[2,48,512]{2,1,0:T(8,128)(2,1)S(1)}, bf16[2,48,512]{2,1,0:T(8,128)(2,1)S(1)}, u32[]{:S(2)}, u32[]{:S(2)}) collective-permute-start(bf16[2,48,512]{2,1,0:T(8,128)(2,1)S(1)} %get-tuple-element.116), channel_id=1, source_target_pairs={{0,12},{1,13},{2,14},{3,15},{4,8},{5,9},{6,10},{7,11},{8,4},{9,5},... | collective-permute-start | bytes 294920 | tf_op jit(solution)/shard_map/ppermute | solution.py:276
  109.6 2.4 %collective-permute-done.40.refs_27_ = bf16[2,48,512]{2,1,0:T(8,128)(2,1)S(1)} collective-permute-done((bf16[2,48,512]{2,1,0:T(8,128)(2,1)S(1)}, bf16[2,48,512]{2,1,0:T(8,128)(2,1)S(1)}, u32[]{:S(2)}, u32[]{:S(2)}) %collective-permute-start.40) | collective-permute-done | bytes 98336 | tf_op jit(solution)/shard_map/ppermute | solution.py:276
  112.0 2.9 %collective-permute-done.43.refs_30_ = bf16[2,48,512]{2,1,0:T(8,128)(2,1)S(1)} collective-permute-done((bf16[2,48,512]{2,1,0:T(8,128)(2,1)S(1)}, bf16[2,48,512]{2,1,0:T(8,128)(2,1)S(1)}, u32[]{:S(2)}, u32[]{:S(2)}) %collective-permute-start.43) | collective-permute-done | bytes 98336 | tf_op jit(solution)/shard_map/ppermute | solution.py:276
  114.9 3.4 %collective-permute-done.44.refs_31_ = bf16[2,48,512]{2,1,0:T(8,128)(2,1)S(1)} collective-permute-done((bf16[2,48,512]{2,1,0:T(8,128)(2,1)S(1)}, bf16[2,48,512]{2,1,0:T(8,128)(2,1)S(1)}, u32[]{:S(2)}, u32[]{:S(2)}) %collective-permute-start.44) | collective-permute-done | bytes 98336 | tf_op jit(solution)/shard_map/ppermute | solution.py:276
  118.3 4.7 %update.1 = (bf16[384,1024]{1,0:T(8,128)(2,1)}, bf16[384,1024]{1,0:T(8,128)(2,1)}, bf16[32,1024]{1,0:T(8,128)(2,1)S(1)}, bf16[32,1024]{1,0:T(8,128)(2,1)S(1)}, b...) custom-call(s32[1]{0:T(128)} %bitcast.me_ref, ...), custom_call_target="tpu_custom_call" | custom-call | flops 2239758336 | bytes 6029312 | tf_op jit(solution)/shard_map/update/pallas_call | solution.py:213
  123.0 3.1 %collective-permute-start.45 = (bf16[32,1024]{1,0:T(8,128)(2,1)S(1)}, bf16[32,1024]{1,0:T(8,128)(2,1)S(1)}, u32[]{:S(2)}, u32[]{:S(2)}) collective-permute-start(bf16[32,1024]{1,0:T(8,128)(2,1)S(1)} %get-tuple-element.124), channel_id=1, source_target_pairs={{0,15},{1,14},{2,13},{3,12},{4,11},{5,10},{6,9},{7,8},{8,7},{9,6},... | collective-permute-start | bytes 196616 | tf_op jit(solution)/shard_map/ppermute | solution.py:276
  128.1 3.4 %collective-permute-start.49 = (bf16[32,1024]{1,0:T(8,128)(2,1)S(1)}, bf16[32,1024]{1,0:T(8,128)(2,1)S(1)}, u32[]{:S(2)}, u32[]{:S(2)}) collective-permute-start(bf16[32,1024]{1,0:T(8,128)(2,1)S(1)} %get-tuple-element.128), channel_id=1, source_target_pairs={{0,14},{1,15},{2,12},{3,13},{4,10},{5,11},{6,8},{7,9},{8,6},{9,7},... | collective-permute-start | bytes 196616 | tf_op jit(solution)/shard_map/ppermute | solution.py:276
  134.2 2.4 %collective-permute-start.53 = (bf16[32,1024]{1,0:T(8,128)(2,1)S(1)}, bf16[32,1024]{1,0:T(8,128)(2,1)S(1)}, u32[]{:S(2)}, u32[]{:S(2)}) collective-permute-start(bf16[32,1024]{1,0:T(8,128)(2,1)S(1)} %get-tuple-element.132), channel_id=1, source_target_pairs={{0,13},{1,12},{2,15},{3,14},{4,9},{5,8},{6,11},{7,10},{8,5},{9,4},... | collective-permute-start | bytes 196616 | tf_op jit(solution)/shard_map/ppermute | solution.py:276
  136.9 2.3 %collective-permute-start.55 = (bf16[32,1024]{1,0:T(8,128)(2,1)S(1)}, bf16[32,1024]{1,0:T(8,128)(2,1)S(1)}, u32[]{:S(2)}, u32[]{:S(2)}) collective-permute-start(bf16[32,1024]{1,0:T(8,128)(2,1)S(1)} %get-tuple-element.134), channel_id=1, source_target_pairs={{0,9},{1,8},{2,11},{3,10},{4,13},{5,12},{6,15},{7,14},{8,1},{9,0},... | collective-permute-start | bytes 196616 | tf_op jit(solution)/shard_map/ppermute | solution.py:276
  145.5 2.2 %collective-permute-done.57.refs_13_ = bf16[32,1024]{1,0:T(8,128)(2,1)S(1)} collective-permute-done((bf16[32,1024]{1,0:T(8,128)(2,1)S(1)}, bf16[32,1024]{1,0:T(8,128)(2,1)S(1)}, u32[]{:S(2)}, u32[]{:S(2)}) %collective-permute-start.57) | collective-permute-done | bytes 65568 | tf_op jit(solution)/shard_map/ppermute | solution.py:276
  (109 shorter events, 45.1 us)
Async XLA Ops:
  9.7 12.2 %collective-permute-start.18 = (bf16[2,48,512]{2,1,0:T(8,128)(2,1)}, bf16[2,48,512]{2,1,0:T(8,128)(2,1)S(1)}, u32[]{:S(2)}, u32[]{:S(2)}) collective-permute-start(bf16[2,48,512]{2,1,0:T(8,128)(2,1)} %get-tuple-element.91), channel_id=1, source_target_pairs={{0,11},{1,10},{2,9},{3,8},{4,15},{5,14},{6,13},{7,12},{8,3},{9,2},... | collective-permute-start | bytes 294920 | tf_op jit(solution)/shard_map/ppermute | solution.py:276
  12.2 12.9 %collective-permute-start.20 = (bf16[2,48,512]{2,1,0:T(8,128)(2,1)}, bf16[2,48,512]{2,1,0:T(8,128)(2,1)S(1)}, u32[]{:S(2)}, u32[]{:S(2)}) collective-permute-start(bf16[2,48,512]{2,1,0:T(8,128)(2,1)} %get-tuple-element.93), channel_id=1, source_target_pairs={{0,14},{1,15},{2,12},{3,13},{4,10},{5,11},{6,8},{7,9},{8,6},{9,7},... | collective-permute-start | bytes 294920 | tf_op jit(solution)/shard_map/ppermute | solution.py:276
  15.5 12.9 %collective-permute-start.21 = (bf16[2,48,512]{2,1,0:T(8,128)(2,1)}, bf16[2,48,512]{2,1,0:T(8,128)(2,1)S(1)}, u32[]{:S(2)}, u32[]{:S(2)}) collective-permute-start(bf16[2,48,512]{2,1,0:T(8,128)(2,1)} %get-tuple-element.94), channel_id=1, source_target_pairs={{0,5},{1,4},{2,7},{3,6},{4,1},{5,0},{6,3},{7,2},{8,13},{9,12},{10,... | collective-permute-start | bytes 294920 | tf_op jit(solution)/shard_map/ppermute | solution.py:276
  18.5 12.4 %collective-permute-start.22 = (bf16[2,48,512]{2,1,0:T(8,128)(2,1)}, bf16[2,48,512]{2,1,0:T(8,128)(2,1)S(1)}, u32[]{:S(2)}, u32[]{:S(2)}) collective-permute-start(bf16[2,48,512]{2,1,0:T(8,128)(2,1)} %get-tuple-element.95), channel_id=1, source_target_pairs={{0,10},{1,11},{2,8},{3,9},{4,14},{5,15},{6,12},{7,13},{8,2},{9,3},... | collective-permute-start | bytes 294920 | tf_op jit(solution)/shard_map/ppermute | solution.py:276
  25.0 16.6 %collective-permute-start.25 = (bf16[2,48,512]{2,1,0:T(8,128)(2,1)}, bf16[2,48,512]{2,1,0:T(8,128)(2,1)S(1)}, u32[]{:S(2)}, u32[]{:S(2)}) collective-permute-start(bf16[2,48,512]{2,1,0:T(8,128)(2,1)} %get-tuple-element.98), channel_id=1, source_target_pairs={{0,9},{1,8},{2,11},{3,10},{4,13},{5,12},{6,15},{7,14},{8,1},{9,0},... | collective-permute-start | bytes 294920 | tf_op jit(solution)/shard_map/ppermute | solution.py:276
  28.4 14.6 %collective-permute-start.26 = (bf16[2,48,512]{2,1,0:T(8,128)(2,1)}, bf16[2,48,512]{2,1,0:T(8,128)(2,1)S(1)}, u32[]{:S(2)}, u32[]{:S(2)}) collective-permute-start(bf16[2,48,512]{2,1,0:T(8,128)(2,1)} %get-tuple-element.99), channel_id=1, source_target_pairs={{0,3},{1,2},{2,1},{3,0},{4,7},{5,6},{6,5},{7,4},{8,11},{9,10},{10,... | collective-permute-start | bytes 294920 | tf_op jit(solution)/shard_map/ppermute | solution.py:276
  30.9 12.1 %collective-permute-start.27 = (bf16[2,48,512]{2,1,0:T(8,128)(2,1)}, bf16[2,48,512]{2,1,0:T(8,128)(2,1)S(1)}, u32[]{:S(2)}, u32[]{:S(2)}) collective-permute-start(bf16[2,48,512]{2,1,0:T(8,128)(2,1)} %get-tuple-element.100), channel_id=1, source_target_pairs={{0,12},{1,13},{2,14},{3,15},{4,8},{5,9},{6,10},{7,11},{8,4},{9,5},... | collective-permute-start | bytes 294920 | tf_op jit(solution)/shard_map/ppermute | solution.py:276
  31.5 14.9 %collective-permute-start.28 = (bf16[2,48,512]{2,1,0:T(8,128)(2,1)}, bf16[2,48,512]{2,1,0:T(8,128)(2,1)S(1)}, u32[]{:S(2)}, u32[]{:S(2)}) collective-permute-start(bf16[2,48,512]{2,1,0:T(8,128)(2,1)} %get-tuple-element.101), channel_id=1, source_target_pairs={{0,7},{1,6},{2,5},{3,4},{4,3},{5,2},{6,1},{7,0},{8,15},{9,14},{10,... | collective-permute-start | bytes 294920 | tf_op jit(solution)/shard_map/ppermute | solution.py:276
  31.5 14.9 %collective-permute-start.29 = (bf16[2,48,512]{2,1,0:T(8,128)(2,1)}, bf16[2,48,512]{2,1,0:T(8,128)(2,1)S(1)}, u32[]{:S(2)}, u32[]{:S(2)}) collective-permute-start(bf16[2,48,512]{2,1,0:T(8,128)(2,1)} %get-tuple-element.102), channel_id=1, source_target_pairs={{0,8},{1,9},{2,10},{3,11},{4,12},{5,13},{6,14},{7,15},{8,0},{9,1},... | collective-permute-start | bytes 294920 | tf_op jit(solution)/shard_map/ppermute | solution.py:276
  43.0 14.4 %collective-permute-start.3 = (bf16[32,1792]{1,0:T(8,128)(2,1)S(1)}, bf16[32,1792]{1,0:T(8,128)(2,1)S(1)}, u32[]{:S(2)}, u32[]{:S(2)}) collective-permute-start(bf16[32,1792]{1,0:T(8,128)(2,1)S(1)} %get-tuple-element.75), channel_id=1, source_target_pairs={{0,11},{1,10},{2,9},{3,8},{4,15},{5,14},{6,13},{7,12},{8,3},{9,2},... | collective-permute-start | bytes 344072 | tf_op jit(solution)/shard_map/ppermute | solution.py:276
  46.4 12.8 %collective-permute-start.4 = (bf16[32,1792]{1,0:T(8,128)(2,1)S(1)}, bf16[32,1792]{1,0:T(8,128)(2,1)S(1)}, u32[]{:S(2)}, u32[]{:S(2)}) collective-permute-start(bf16[32,1792]{1,0:T(8,128)(2,1)S(1)} %get-tuple-element.76), channel_id=1, source_target_pairs={{0,1},{1,0},{2,3},{3,2},{4,5},{5,4},{6,7},{7,6},{8,9},{9,8},{10,11... | collective-permute-start | bytes 344072 | tf_op jit(solution)/shard_map/ppermute | solution.py:276
  46.5 14.1 %collective-permute-start.5 = (bf16[32,1792]{1,0:T(8,128)(2,1)S(1)}, bf16[32,1792]{1,0:T(8,128)(2,1)S(1)}, u32[]{:S(2)}, u32[]{:S(2)}) collective-permute-start(bf16[32,1792]{1,0:T(8,128)(2,1)S(1)} %get-tuple-element.77), channel_id=1, source_target_pairs={{0,14},{1,15},{2,12},{3,13},{4,10},{5,11},{6,8},{7,9},{8,6},{9,7},... | collective-permute-start | bytes 344072 | tf_op jit(solution)/shard_map/ppermute | solution.py:276
  50.0 11.0 %collective-permute-start.6 = (bf16[32,1792]{1,0:T(8,128)(2,1)S(1)}, bf16[32,1792]{1,0:T(8,128)(2,1)S(1)}, u32[]{:S(2)}, u32[]{:S(2)}) collective-permute-start(bf16[32,1792]{1,0:T(8,128)(2,1)S(1)} %get-tuple-element.78), channel_id=1, source_target_pairs={{0,5},{1,4},{2,7},{3,6},{4,1},{5,0},{6,3},{7,2},{8,13},{9,12},{10,... | collective-permute-start | bytes 344072 | tf_op jit(solution)/shard_map/ppermute | solution.py:276
  52.8 15.1 %collective-permute-start.7 = (bf16[32,1792]{1,0:T(8,128)(2,1)S(1)}, bf16[32,1792]{1,0:T(8,128)(2,1)S(1)}, u32[]{:S(2)}, u32[]{:S(2)}) collective-permute-start(bf16[32,1792]{1,0:T(8,128)(2,1)S(1)} %get-tuple-element.79), channel_id=1, source_target_pairs={{0,10},{1,11},{2,8},{3,9},{4,14},{5,15},{6,12},{7,13},{8,2},{9,3},... | collective-permute-start | bytes 344072 | tf_op jit(solution)/shard_map/ppermute | solution.py:276
  57.5 10.4 %collective-permute-start.8 = (bf16[32,1792]{1,0:T(8,128)(2,1)S(1)}, bf16[32,1792]{1,0:T(8,128)(2,1)S(1)}, u32[]{:S(2)}, u32[]{:S(2)}) collective-permute-start(bf16[32,1792]{1,0:T(8,128)(2,1)S(1)} %get-tuple-element.80), channel_id=1, source_target_pairs={{0,2},{1,3},{2,0},{3,1},{4,6},{5,7},{6,4},{7,5},{8,10},{9,11},{10,... | collective-permute-start | bytes 344072 | tf_op jit(solution)/shard_map/ppermute | solution.py:276
  59.2 11.7 %collective-permute-start.9 = (bf16[32,1792]{1,0:T(8,128)(2,1)S(1)}, bf16[32,1792]{1,0:T(8,128)(2,1)S(1)}, u32[]{:S(2)}, u32[]{:S(2)}) collective-permute-start(bf16[32,1792]{1,0:T(8,128)(2,1)S(1)} %get-tuple-element.81), channel_id=1, source_target_pairs={{0,13},{1,12},{2,15},{3,14},{4,9},{5,8},{6,11},{7,10},{8,5},{9,4},... | collective-permute-start | bytes 344072 | tf_op jit(solution)/shard_map/ppermute | solution.py:276
  60.5 12.4 %collective-permute-start.10 = (bf16[32,1792]{1,0:T(8,128)(2,1)S(1)}, bf16[32,1792]{1,0:T(8,128)(2,1)S(1)}, u32[]{:S(2)}, u32[]{:S(2)}) collective-permute-start(bf16[32,1792]{1,0:T(8,128)(2,1)S(1)} %get-tuple-element.82), channel_id=1, source_target_pairs={{0,6},{1,7},{2,4},{3,5},{4,2},{5,3},{6,0},{7,1},{8,14},{9,15},{10,... | collective-permute-start | bytes 344072 | tf_op jit(solution)/shard_map/ppermute | solution.py:276
  60.9 16.3 %collective-permute-start.11 = (bf16[32,1792]{1,0:T(8,128)(2,1)S(1)}, bf16[32,1792]{1,0:T(8,128)(2,1)S(1)}, u32[]{:S(2)}, u32[]{:S(2)}) collective-permute-start(bf16[32,1792]{1,0:T(8,128)(2,1)S(1)} %get-tuple-element.83), channel_id=1, source_target_pairs={{0,9},{1,8},{2,11},{3,10},{4,13},{5,12},{6,15},{7,14},{8,1},{9,0},... | collective-permute-start | bytes 344072 | tf_op jit(solution)/shard_map/ppermute | solution.py:276
  67.9 12.3 %collective-permute-start.12 = (bf16[32,1792]{1,0:T(8,128)(2,1)S(1)}, bf16[32,1792]{1,0:T(8,128)(2,1)S(1)}, u32[]{:S(2)}, u32[]{:S(2)}) collective-permute-start(bf16[32,1792]{1,0:T(8,128)(2,1)S(1)} %get-tuple-element.84), channel_id=1, source_target_pairs={{0,3},{1,2},{2,1},{3,0},{4,7},{5,6},{6,5},{7,4},{8,11},{9,10},{10,... | collective-permute-start | bytes 344072 | tf_op jit(solution)/shard_map/ppermute | solution.py:276
  67.9 12.3 %collective-permute-start.13 = (bf16[32,1792]{1,0:T(8,128)(2,1)S(1)}, bf16[32,1792]{1,0:T(8,128)(2,1)S(1)}, u32[]{:S(2)}, u32[]{:S(2)}) collective-permute-start(bf16[32,1792]{1,0:T(8,128)(2,1)S(1)} %get-tuple-element.85), channel_id=1, source_target_pairs={{0,12},{1,13},{2,14},{3,15},{4,8},{5,9},{6,10},{7,11},{8,4},{9,5},... | collective-permute-start | bytes 344072 | tf_op jit(solution)/shard_map/ppermute | solution.py:276
  70.9 15.8 %collective-permute-start.14 = (bf16[32,1792]{1,0:T(8,128)(2,1)S(1)}, bf16[32,1792]{1,0:T(8,128)(2,1)S(1)}, u32[]{:S(2)}, u32[]{:S(2)}) collective-permute-start(bf16[32,1792]{1,0:T(8,128)(2,1)S(1)} %get-tuple-element.86), channel_id=1, source_target_pairs={{0,7},{1,6},{2,5},{3,4},{4,3},{5,2},{6,1},{7,0},{8,15},{9,14},{10,... | collective-permute-start | bytes 344072 | tf_op jit(solution)/shard_map/ppermute | solution.py:276
  72.9 15.0 %collective-permute-start.15 = (bf16[32,1792]{1,0:T(8,128)(2,1)S(1)}, bf16[32,1792]{1,0:T(8,128)(2,1)S(1)}, u32[]{:S(2)}, u32[]{:S(2)}) collective-permute-start(bf16[32,1792]{1,0:T(8,128)(2,1)S(1)} %get-tuple-element.87), channel_id=1, source_target_pairs={{0,8},{1,9},{2,10},{3,11},{4,12},{5,13},{6,14},{7,15},{8,0},{9,1},... | collective-permute-start | bytes 344072 | tf_op jit(solution)/shard_map/ppermute | solution.py:276
  77.2 14.8 %collective-permute-start.30 = (bf16[2,48,512]{2,1,0:T(8,128)(2,1)S(1)}, bf16[2,48,512]{2,1,0:T(8,128)(2,1)S(1)}, u32[]{:S(2)}, u32[]{:S(2)}) collective-permute-start(bf16[2,48,512]{2,1,0:T(8,128)(2,1)S(1)} %get-tuple-element.104), channel_id=1, source_target_pairs={{0,15},{1,14},{2,13},{3,12},{4,11},{5,10},{6,9},{7,8},{8,7},{9,6},... | collective-permute-start | bytes 294920 | tf_op jit(solution)/shard_map/ppermute | solution.py:276
  80.1 11.9 %collective-permute-start.31 = (bf16[2,48,512]{2,1,0:T(8,128)(2,1)S(1)}, bf16[2,48,512]{2,1,0:T(8,128)(2,1)S(1)}, u32[]{:S(2)}, u32[]{:S(2)}) collective-permute-start(bf16[2,48,512]{2,1,0:T(8,128)(2,1)S(1)} %get-tuple-element.105), channel_id=1, source_target_pairs={{0,4},{1,5},{2,6},{3,7},{4,0},{5,1},{6,2},{7,3},{8,12},{9,13},{10,... | collective-permute-start | bytes 294920 | tf_op jit(solution)/shard_map/ppermute | solution.py:276
  80.1 13.5 %collective-permute-start.32 = (bf16[2,48,512]{2,1,0:T(8,128)(2,1)S(1)}, bf16[2,48,512]{2,1,0:T(8,128)(2,1)S(1)}, u32[]{:S(2)}, u32[]{:S(2)}) collective-permute-start(bf16[2,48,512]{2,1,0:T(8,128)(2,1)S(1)} %get-tuple-element.106), channel_id=1, source_target_pairs={{0,11},{1,10},{2,9},{3,8},{4,15},{5,14},{6,13},{7,12},{8,3},{9,2},... | collective-permute-start | bytes 294920 | tf_op jit(solution)/shard_map/ppermute | solution.py:276
  87.9 10.2 %collective-permute-start.34 = (bf16[2,48,512]{2,1,0:T(8,128)(2,1)S(1)}, bf16[2,48,512]{2,1,0:T(8,128)(2,1)S(1)}, u32[]{:S(2)}, u32[]{:S(2)}) collective-permute-start(bf16[2,48,512]{2,1,0:T(8,128)(2,1)S(1)} %get-tuple-element.108), channel_id=1, source_target_pairs={{0,14},{1,15},{2,12},{3,13},{4,10},{5,11},{6,8},{7,9},{8,6},{9,7},... | collective-permute-start | bytes 294920 | tf_op jit(solution)/shard_map/ppermute | solution.py:276
  92.0 12.1 %collective-permute-start.36 = (bf16[2,48,512]{2,1,0:T(8,128)(2,1)S(1)}, bf16[2,48,512]{2,1,0:T(8,128)(2,1)S(1)}, u32[]{:S(2)}, u32[]{:S(2)}) collective-permute-start(bf16[2,48,512]{2,1,0:T(8,128)(2,1)S(1)} %get-tuple-element.110), channel_id=1, source_target_pairs={{0,10},{1,11},{2,8},{3,9},{4,14},{5,15},{6,12},{7,13},{8,2},{9,3},... | collective-permute-start | bytes 294920 | tf_op jit(solution)/shard_map/ppermute | solution.py:276
  93.7 11.0 %collective-permute-start.37 = (bf16[2,48,512]{2,1,0:T(8,128)(2,1)S(1)}, bf16[2,48,512]{2,1,0:T(8,128)(2,1)S(1)}, u32[]{:S(2)}, u32[]{:S(2)}) collective-permute-start(bf16[2,48,512]{2,1,0:T(8,128)(2,1)S(1)} %get-tuple-element.111), channel_id=1, source_target_pairs={{0,2},{1,3},{2,0},{3,1},{4,6},{5,7},{6,4},{7,5},{8,10},{9,11},{10,... | collective-permute-start | bytes 294920 | tf_op jit(solution)/shard_map/ppermute | solution.py:276
  95.5 12.0 %collective-permute-start.38 = (bf16[2,48,512]{2,1,0:T(8,128)(2,1)S(1)}, bf16[2,48,512]{2,1,0:T(8,128)(2,1)S(1)}, u32[]{:S(2)}, u32[]{:S(2)}) collective-permute-start(bf16[2,48,512]{2,1,0:T(8,128)(2,1)S(1)} %get-tuple-element.112), channel_id=1, source_target_pairs={{0,13},{1,12},{2,15},{3,14},{4,9},{5,8},{6,11},{7,10},{8,5},{9,4},... | collective-permute-start | bytes 294920 | tf_op jit(solution)/shard_map/ppermute | solution.py:276
  98.1 10.3 %collective-permute-start.39 = (bf16[2,48,512]{2,1,0:T(8,128)(2,1)S(1)}, bf16[2,48,512]{2,1,0:T(8,128)(2,1)S(1)}, u32[]{:S(2)}, u32[]{:S(2)}) collective-permute-start(bf16[2,48,512]{2,1,0:T(8,128)(2,1)S(1)} %get-tuple-element.113), channel_id=1, source_target_pairs={{0,6},{1,7},{2,4},{3,5},{4,2},{5,3},{6,0},{7,1},{8,14},{9,15},{10,... | collective-permute-start | bytes 294920 | tf_op jit(solution)/shard_map/ppermute | solution.py:276
  99.8 12.2 %collective-permute-start.40 = (bf16[2,48,512]{2,1,0:T(8,128)(2,1)S(1)}, bf16[2,48,512]{2,1,0:T(8,128)(2,1)S(1)}, u32[]{:S(2)}, u32[]{:S(2)}) collective-permute-start(bf16[2,48,512]{2,1,0:T(8,128)(2,1)S(1)} %get-tuple-element.114), channel_id=1, source_target_pairs={{0,9},{1,8},{2,11},{3,10},{4,13},{5,12},{6,15},{7,14},{8,1},{9,0},... | collective-permute-start | bytes 294920 | tf_op jit(solution)/shard_map/ppermute | solution.py:276
  108.4 9.9 %collective-permute-start.44 = (bf16[2,48,512]{2,1,0:T(8,128)(2,1)S(1)}, bf16[2,48,512]{2,1,0:T(8,128)(2,1)S(1)}, u32[]{:S(2)}, u32[]{:S(2)}) collective-permute-start(bf16[2,48,512]{2,1,0:T(8,128)(2,1)S(1)} %get-tuple-element.118), channel_id=1, source_target_pairs={{0,8},{1,9},{2,10},{3,11},{4,12},{5,13},{6,14},{7,15},{8,0},{9,1},... | collective-permute-start | bytes 294920 | tf_op jit(solution)/shard_map/ppermute | solution.py:276
  (36 other events, 400.9 us)

commit v21 on v11

--- a/solution.py
+++ b/solution.py
@@ -108,7 +108,7 @@
         functools.partial(pack_kernel, groups),
         out_shape=(jax.ShapeDtypeStruct((capacity, width), BF16),) * groups
         + (jax.ShapeDtypeStruct((1, rows), jnp.int32), jax.ShapeDtypeStruct((rows, 1), F32)),
-        in_specs=[SMEM] * 3 + [HBM] * 6 + [VMEM],
+        in_specs=[SMEM] * 3 + [HBM] * 6 + [ANY],
         out_specs=(VMEM,) * (groups + 2),
         scratch_shapes=[pltpu.VMEM(a.shape, a.dtype) for a in sources] + [pltpu.SemaphoreType.DMA((len(sources),))],
         compiler_params=pltpu.CompilerParams(vmem_limit_bytes=32 * MIB),
@@ -120,7 +120,7 @@
     return pieces, slot, gates
 
 
-def split_kernel(partners, me_ref, moment_ref, weight_ref, *refs):
+def split_kernel(partners, me_ref, moment_ref, weight_ref, earlier_ref, *refs):
     pieces, sem = refs[:-1], refs[-1]
     copies = []
     for s, piece in zip(partners, pieces):
@@ -134,13 +134,13 @@
         copy.wait()
 
 
-def split(me, moment, weight, groups, partners):
+def split(me, moment, weight, earlier, groups, partners):
     _, ff, d = weight.shape
     piece = jax.ShapeDtypeStruct((2, ff // (groups // 2), d // 2), BF16)
     return pl.pallas_call(
         functools.partial(split_kernel, partners),
         out_shape=(piece,) * len(partners),
-        in_specs=[SMEM, HBM, HBM],
+        in_specs=[SMEM, HBM, HBM, ANY],
         out_specs=(VMEM,) * len(partners),
         scratch_shapes=[pltpu.SemaphoreType.DMA((2 * len(partners),))],
         compiler_params=pltpu.CompilerParams(vmem_limit_bytes=60 * MIB),
@@ -148,16 +148,16 @@
             flops=0, bytes_accessed=8 * ff * d * len(partners) // groups, transcendentals=0
         ),
         name="split",
-    )(me, moment, weight)
+    )(me, moment, weight, earlier)
 
 
 def reorder_kernel(me_ref, perm_ref, *refs):
     groups = len(refs) // 2 - 1
     sources, targets, held = refs[:groups], refs[groups + 1 : 2 * groups + 1], refs[-1]
-    me, order = me_ref[0], mixed_order(groups)
-    for s, source in zip(order, sources):
+    me = me_ref[0]
+    for s, source in zip(spread_order(groups), sources):
         held[me ^ perm_ref[me ^ s]] = source[...]
-    for s, target in zip(ending_near(groups), targets):
+    for s, target in zip(mixed_order(groups), targets):
         target[...] = held[s]
 
 
@@ -184,7 +184,7 @@
     capacity = packed[0].shape[0]
     for n, piece in enumerate(packed):
         rows_ref[n * capacity : (n + 1) * capacity] = piece[...]
-    for s, piece in zip(ending_near(groups), pieces):
+    for s, piece in zip(mixed_order(groups), pieces):
         rows, columns = piece.shape[1:]
         for lead in range(2):
             chunk_at(held, lead, me_ref[0] ^ s, rows, columns)[...] = piece[lead]
@@ -208,9 +208,7 @@
     weight_new = (held[1].astype(F32) - step_scale * current.astype(F32)).astype(BF16)
     weight_new_ref[...] = weight_new
     product = jnp.dot(rows_ref[:, ff + d :], weight_new, preferred_element_type=F32).astype(BF16)
-    came = mixed_order(groups)
-    for s, piece in zip(ending_near(groups), produced):
-        n = came.index(s)
+    for n, piece in enumerate(produced):
         piece[...] = product[n * capacity : (n + 1) * capacity]
 
 
@@ -239,7 +237,7 @@
 def finish_kernel(groups, slot_ref, gates_ref, *refs):
     pieces, (out_ref, returned_ref) = refs[:groups], refs[groups:]
     capacity = pieces[0].shape[0]
-    for s, piece in zip(ending_near(groups), pieces):
+    for s, piece in zip(mixed_order(groups), pieces):
         returned_ref[s * capacity : (s + 1) * capacity] = piece[...]
     selector = selector_of(slot_ref[...], groups * capacity)
     expert_out = lax.dot_general(
@@ -278,9 +276,9 @@
     return [0] + [s for pair in zip(far, near + [None]) for s in pair if s is not None]
 
 
-def ending_near(groups):
+def spread_order(groups):
     order = mixed_order(groups)
-    return order[:-4] + [order[n] for n in (-3, -4, -1, -2)] if groups > 4 else order
+    return [0, order[-6]] + [s for s in order[1:] if s != order[-6]]
 
 
 def swap(pieces, order):
@@ -298,20 +296,18 @@
     me = lax.axis_index("expert").astype(jnp.int32).reshape(1)
     capacity = max(4, 2 * grad_hidden.shape[0] // groups)
     ff, d = w_down.shape[1:]
-    order, last_order = mixed_order(groups), ending_near(groups)
-    first = order[1:6]
-    blocks = dict(zip(first, split(me, w_moment, w_down, groups, first)))
-    others = [s for s in order if s not in first]
-    blocks.update(zip(others, split(me, w_moment, w_down, groups, others)))
-    spread = swap([blocks[s] for s in order], order)
+    order, early = mixed_order(groups), spread_order(groups)
+    first = split(me, w_moment, w_down, live_rows, groups, early[1:6])
     packed, fwd_slot, gates = pack_rows(
         live_rows, me, perm, grad_route, fwd_route, grad_hidden, grad_out, fwd_hidden, fwd_gate,
-        spread[1], groups, capacity,
-    )
+        first[-1], groups, capacity,
+    )
+    own, *others = split(me, w_moment, w_down, fwd_slot, groups, early[:1] + early[6:])
+    spread = swap([own, *first, *others], early)
     received = swap(packed, order)
-    placed = swap(reorder(me, perm, spread, received[groups // 3]), last_order)
+    placed = swap(reorder(me, perm, spread, received[groups // 3]), order)
     weight_new, moment_new, produced = update(me, received, placed, ff, d)
-    return weight_new[None], moment_new[None], finish(fwd_slot, gates, swap(produced, last_order))
+    return weight_new[None], moment_new[None], finish(fwd_slot, gates, swap(produced, order))
 
 
 def lookup(route_ids, mapping):
@@ -464,7 +460,7 @@
     )
 
     def per_device(*args):
-        few = groups & (groups - 1) == 0 and groups <= 2 * args[0].shape[0] // groups
+        few = groups >= 8 and groups & (groups - 1) == 0 and groups <= 2 * args[0].shape[0] // groups
         return (partner_plan if few else routed_plan)(*args)
 
     return jax.shard_map(

time: 151 us -> 157 us (1.040)
  starting transfers between devices: 92.7 us -> 98.5 us
  local copies, waits for them, and re-layouts: 0.65 us -> 3.61 us
  waiting for transfers between devices: 42 us -> 39.3 us
    ppermute x60, starting transfers between devices: 92.7 us -> 98.5 us  [swap(): lax.ppermute(piece, 'expert', [(i, i ^ s) for i in range(groups)])]
    unnamed x16 -> x22, local copies, waits for them, and re-layouts: 0.65 us -> 3.61 us
    ppermute x60, waiting for transfers between devices: 42 us -> 39.3 us  [swap(): lax.ppermute(piece, 'expert', [(i, i ^ s) for i in range(groups)])]
  transfers between devices with their start and end apart: 60 -> 60, of which waited for: 19 -> 20; matrix products, arithmetic and copies ran while one was open for 0% -> 0% of each run, Pallas kernels for 4% -> 4%
where the time goes in v21:
time: 157 us
  starting transfers between devices  98.5 us (63%)
  waiting for transfers between devices  39.3 us (25%)
  Pallas kernels  13.9 us (9%)
  local copies, waits for them, and re-layouts  3.61 us (2%)
    ppermute x60, starting transfers between devices, swap(): lax.ppermute(piece, 'expert', [(i, i ^ s) for i in range(groups)])  98.5 us
    ppermute x60, waiting for transfers between devices, swap(): lax.ppermute(piece, 'expert', [(i, i ^ s) for i in range(groups)])  39.3 us
    pallas_call x1, Pallas kernels, update(): pl.pallas_call(functools.partial(update_kernel, groups), out_shape=(shape...  4.74 us
    pallas_call x2, Pallas kernels, split(): pl.pallas_call(functools.partial(split_kernel, partners), out_shape=(piec...  4.37 us
    unnamed x22, local copies, waits for them, and re-layouts  3.61 us
  transfers between devices with their start and end apart: 60, of which 20 were waited for; matrix products, arithmetic and copies ran while one was open for 0% of the time, Pallas kernels for 4%

profile of v21, /device:TPU:0, one launch (start us, length us, event | category | flops | bytes accessed | tf_op | source)
XLA Modules:
  0.0 156.8 jit_solution(4843121267044382556)
XLA Ops:
  3.3 2.5 %collective-permute-start.15 = (bf16[2,48,512]{2,1,0:T(8,128)(2,1)}, bf16[2,48,512]{2,1,0:T(8,128)(2,1)S(1)}, u32[]{:S(2)}, u32[]{:S(2)}) collective-permute-start(bf16[2,48,512]{2,1,0:T(8,128)(2,1)} %get-tuple-element.90), channel_id=1, source_target_pairs={{0,5},{1,4},{2,7},{3,6},{4,1},{5,0},{6,3},{7,2},{8,13},{9,12},{10,... | collective-permute-start | bytes 294920 | tf_op jit(solution)/shard_map/ppermute | solution.py:287
  5.8 2.6 %collective-permute-start.16 = (bf16[2,48,512]{2,1,0:T(8,128)(2,1)}, bf16[2,48,512]{2,1,0:T(8,128)(2,1)S(1)}, u32[]{:S(2)}, u32[]{:S(2)}) collective-permute-start(bf16[2,48,512]{2,1,0:T(8,128)(2,1)} %get-tuple-element.91), channel_id=1, source_target_pairs={{0,8},{1,9},{2,10},{3,11},{4,12},{5,13},{6,14},{7,15},{8,0},{9,1},... | collective-permute-start | bytes 294920 | tf_op jit(solution)/shard_map/ppermute | solution.py:287
  12.8 2.8 %pack_rows.1 = (bf16[32,1792]{1,0:T(8,128)(2,1)S(1)}, bf16[32,1792]{1,0:T(8,128)(2,1)S(1)}, bf16[32,1792]{1,0:T(8,128)(2,1)S(1)}, bf16[32,1792]{1,0:T(8,128)(2,1...) custom-call(s32[1]{0:T(128)S(6)} %copy.13.earlier_ref.live_ref, ...), custom_call_target="tpu_custom_call" | custom-call | flops 469762048 | bytes 2752512 | tf_op jit(solution)/shard_map/pack_rows/pallas_call | solution.py:107
  16.1 2.4 %split.3 = (bf16[2,48,512]{2,1,0:T(8,128)(2,1)}, bf16[2,48,512]{2,1,0:T(8,128)(2,1)}, bf16[2,48,512]{2,1,0:T(8,128)(2,1)}, bf16[2,48,512]{2,1,0:T(8,128)(2,1)}, ...) custom-call(s32[1]{0:T(128)} %bitcast.me_ref, ...), custom_call_target="tpu_custom_call" | custom-call | bytes 2162688 | tf_op jit(solution)/shard_map/split/pallas_call | solution.py:140
  18.6 2.0 %collective-permute-start.20 = (bf16[2,48,512]{2,1,0:T(8,128)(2,1)}, bf16[2,48,512]{2,1,0:T(8,128)(2,1)S(1)}, u32[]{:S(2)}, u32[]{:S(2)}) collective-permute-start(bf16[2,48,512]{2,1,0:T(8,128)(2,1)} %get-tuple-element.94), channel_id=1, source_target_pairs={{0,9},{1,8},{2,11},{3,10},{4,13},{5,12},{6,15},{7,14},{8,1},{9,0},... | collective-permute-start | bytes 294920 | tf_op jit(solution)/shard_map/ppermute | solution.py:287
  20.5 2.3 %collective-permute-start.21 = (bf16[2,48,512]{2,1,0:T(8,128)(2,1)}, bf16[2,48,512]{2,1,0:T(8,128)(2,1)S(1)}, u32[]{:S(2)}, u32[]{:S(2)}) collective-permute-start(bf16[2,48,512]{2,1,0:T(8,128)(2,1)} %get-tuple-element.95), channel_id=1, source_target_pairs={{0,6},{1,7},{2,4},{3,5},{4,2},{5,3},{6,0},{7,1},{8,14},{9,15},{10,... | collective-permute-start | bytes 294920 | tf_op jit(solution)/shard_map/ppermute | solution.py:287
  26.9 4.2 %collective-permute-start.25 = (bf16[2,48,512]{2,1,0:T(8,128)(2,1)}, bf16[2,48,512]{2,1,0:T(8,128)(2,1)S(1)}, u32[]{:S(2)}, u32[]{:S(2)}) collective-permute-start(bf16[2,48,512]{2,1,0:T(8,128)(2,1)} %get-tuple-element.99), channel_id=1, source_target_pairs={{0,14},{1,15},{2,12},{3,13},{4,10},{5,11},{6,8},{7,9},{8,6},{9,7},... | collective-permute-start | bytes 294920 | tf_op jit(solution)/shard_map/ppermute | solution.py:287
  31.1 3.1 %collective-permute-start.26 = (bf16[2,48,512]{2,1,0:T(8,128)(2,1)}, bf16[2,48,512]{2,1,0:T(8,128)(2,1)S(1)}, u32[]{:S(2)}, u32[]{:S(2)}) collective-permute-start(bf16[2,48,512]{2,1,0:T(8,128)(2,1)} %get-tuple-element.100), channel_id=1, source_target_pairs={{0,1},{1,0},{2,3},{3,2},{4,5},{5,4},{6,7},{7,6},{8,9},{9,8},{10,11... | collective-permute-start | bytes 294920 | tf_op jit(solution)/shard_map/ppermute | solution.py:287
  34.2 2.3 %collective-permute-start.27 = (bf16[2,48,512]{2,1,0:T(8,128)(2,1)}, bf16[2,48,512]{2,1,0:T(8,128)(2,1)S(1)}, u32[]{:S(2)}, u32[]{:S(2)}) collective-permute-start(bf16[2,48,512]{2,1,0:T(8,128)(2,1)} %get-tuple-element.101), channel_id=1, source_target_pairs={{0,11},{1,10},{2,9},{3,8},{4,15},{5,14},{6,13},{7,12},{8,3},{9,2},... | collective-permute-start | bytes 294920 | tf_op jit(solution)/shard_map/ppermute | solution.py:287
  36.5 4.2 %collective-permute-done.24.refs_10_ = bf16[2,48,512]{2,1,0:T(8,128)(2,1)S(1)} collective-permute-done((bf16[2,48,512]{2,1,0:T(8,128)(2,1)}, bf16[2,48,512]{2,1,0:T(8,128)(2,1)S(1)}, u32[]{:S(2)}, u32[]{:S(2)}) %collective-permute-start.24) | collective-permute-done | bytes 98336 | tf_op jit(solution)/shard_map/ppermute | solution.py:287
  40.7 3.6 %collective-permute-start = (bf16[32,1792]{1,0:T(8,128)(2,1)S(1)}, bf16[32,1792]{1,0:T(8,128)(2,1)S(1)}, u32[]{:S(2)}, u32[]{:S(2)}) collective-permute-start(bf16[32,1792]{1,0:T(8,128)(2,1)S(1)} %get-tuple-element.73), channel_id=1, source_target_pairs={{0,8},{1,9},{2,10},{3,11},{4,12},{5,13},{6,14},{7,15},{8,0},{9,1},... | collective-permute-start | bytes 344072 | tf_op jit(solution)/shard_map/ppermute | solution.py:287
  45.5 2.2 %collective-permute-start.2 = (bf16[32,1792]{1,0:T(8,128)(2,1)S(1)}, bf16[32,1792]{1,0:T(8,128)(2,1)S(1)}, u32[]{:S(2)}, u32[]{:S(2)}) collective-permute-start(bf16[32,1792]{1,0:T(8,128)(2,1)S(1)} %get-tuple-element.75), channel_id=1, source_target_pairs={{0,12},{1,13},{2,14},{3,15},{4,8},{5,9},{6,10},{7,11},{8,4},{9,5},... | collective-permute-start | bytes 344072 | tf_op jit(solution)/shard_map/ppermute | solution.py:287
  49.3 3.5 %collective-permute-start.4 = (bf16[32,1792]{1,0:T(8,128)(2,1)S(1)}, bf16[32,1792]{1,0:T(8,128)(2,1)S(1)}, u32[]{:S(2)}, u32[]{:S(2)}) collective-permute-start(bf16[32,1792]{1,0:T(8,128)(2,1)S(1)} %get-tuple-element.77), channel_id=1, source_target_pairs={{0,9},{1,8},{2,11},{3,10},{4,13},{5,12},{6,15},{7,14},{8,1},{9,0},... | collective-permute-start | bytes 344072 | tf_op jit(solution)/shard_map/ppermute | solution.py:287
  52.8 5.7 %collective-permute-done.refs_1_ = bf16[32,1792]{1,0:T(8,128)(2,1)S(1)} collective-permute-done((bf16[32,1792]{1,0:T(8,128)(2,1)S(1)}, bf16[32,1792]{1,0:T(8,128)(2,1)S(1)}, u32[]{:S(2)}, u32[]{:S(2)}) %collective-permute-start) | collective-permute-done | bytes 114720 | tf_op jit(solution)/shard_map/ppermute | solution.py:287
  60.2 3.5 %collective-permute-start.8 = (bf16[32,1792]{1,0:T(8,128)(2,1)S(1)}, bf16[32,1792]{1,0:T(8,128)(2,1)S(1)}, u32[]{:S(2)}, u32[]{:S(2)}) collective-permute-start(bf16[32,1792]{1,0:T(8,128)(2,1)S(1)} %get-tuple-element.81), channel_id=1, source_target_pairs={{0,10},{1,11},{2,8},{3,9},{4,14},{5,15},{6,12},{7,13},{8,2},{9,3},... | collective-permute-start | bytes 344072 | tf_op jit(solution)/shard_map/ppermute | solution.py:287
  63.8 4.8 %collective-permute-done.5.refs_6_ = bf16[32,1792]{1,0:T(8,128)(2,1)S(1)} collective-permute-done((bf16[32,1792]{1,0:T(8,128)(2,1)S(1)}, bf16[32,1792]{1,0:T(8,128)(2,1)S(1)}, u32[]{:S(2)}, u32[]{:S(2)}) %collective-permute-start.5) | collective-permute-done | bytes 114720 | tf_op jit(solution)/shard_map/ppermute | solution.py:287
  70.7 2.1 %collective-permute-start.12 = (bf16[32,1792]{1,0:T(8,128)(2,1)S(1)}, bf16[32,1792]{1,0:T(8,128)(2,1)S(1)}, u32[]{:S(2)}, u32[]{:S(2)}) collective-permute-start(bf16[32,1792]{1,0:T(8,128)(2,1)S(1)} %get-tuple-element.85), channel_id=1, source_target_pairs={{0,11},{1,10},{2,9},{3,8},{4,15},{5,14},{6,13},{7,12},{8,3},{9,2},... | collective-permute-start | bytes 344072 | tf_op jit(solution)/shard_map/ppermute | solution.py:287
  73.8 3.4 %collective-permute-start.13 = (bf16[32,1792]{1,0:T(8,128)(2,1)S(1)}, bf16[32,1792]{1,0:T(8,128)(2,1)S(1)}, u32[]{:S(2)}, u32[]{:S(2)}) collective-permute-start(bf16[32,1792]{1,0:T(8,128)(2,1)S(1)} %get-tuple-element.86), channel_id=1, source_target_pairs={{0,4},{1,5},{2,6},{3,7},{4,0},{5,1},{6,2},{7,3},{8,12},{9,13},{10,... | collective-permute-start | bytes 344072 | tf_op jit(solution)/shard_map/ppermute | solution.py:287
  77.2 3.3 %collective-permute-start.14 = (bf16[32,1792]{1,0:T(8,128)(2,1)S(1)}, bf16[32,1792]{1,0:T(8,128)(2,1)S(1)}, u32[]{:S(2)}, u32[]{:S(2)}) collective-permute-start(bf16[32,1792]{1,0:T(8,128)(2,1)S(1)} %get-tuple-element.87), channel_id=1, source_target_pairs={{0,15},{1,14},{2,13},{3,12},{4,11},{5,10},{6,9},{7,8},{8,7},{9,6},... | collective-permute-start | bytes 344072 | tf_op jit(solution)/shard_map/ppermute | solution.py:287
  83.7 2.9 %collective-permute-start.32 = (bf16[2,48,512]{2,1,0:T(8,128)(2,1)S(1)}, bf16[2,48,512]{2,1,0:T(8,128)(2,1)S(1)}, u32[]{:S(2)}, u32[]{:S(2)}) collective-permute-start(bf16[2,48,512]{2,1,0:T(8,128)(2,1)S(1)} %get-tuple-element.107), channel_id=1, source_target_pairs={{0,12},{1,13},{2,14},{3,15},{4,8},{5,9},{6,10},{7,11},{8,4},{9,5},... | collective-permute-start | bytes 294920 | tf_op jit(solution)/shard_map/ppermute | solution.py:287
  88.5 6.0 %collective-permute-start.34 = (bf16[2,48,512]{2,1,0:T(8,128)(2,1)S(1)}, bf16[2,48,512]{2,1,0:T(8,128)(2,1)S(1)}, u32[]{:S(2)}, u32[]{:S(2)}) collective-permute-start(bf16[2,48,512]{2,1,0:T(8,128)(2,1)S(1)} %get-tuple-element.109), channel_id=1, source_target_pairs={{0,9},{1,8},{2,11},{3,10},{4,13},{5,12},{6,15},{7,14},{8,1},{9,0},... | collective-permute-start | bytes 294920 | tf_op jit(solution)/shard_map/ppermute | solution.py:287
  98.1 3.1 %collective-permute-start.38 = (bf16[2,48,512]{2,1,0:T(8,128)(2,1)S(1)}, bf16[2,48,512]{2,1,0:T(8,128)(2,1)S(1)}, u32[]{:S(2)}, u32[]{:S(2)}) collective-permute-start(bf16[2,48,512]{2,1,0:T(8,128)(2,1)S(1)} %get-tuple-element.113), channel_id=1, source_target_pairs={{0,10},{1,11},{2,8},{3,9},{4,14},{5,15},{6,12},{7,13},{8,2},{9,3},... | collective-permute-start | bytes 294920 | tf_op jit(solution)/shard_map/ppermute | solution.py:287
  101.3 2.0 %collective-permute-done.34.refs_21_ = bf16[2,48,512]{2,1,0:T(8,128)(2,1)S(1)} collective-permute-done((bf16[2,48,512]{2,1,0:T(8,128)(2,1)S(1)}, bf16[2,48,512]{2,1,0:T(8,128)(2,1)S(1)}, u32[]{:S(2)}, u32[]{:S(2)}) %collective-permute-start.34) | collective-permute-done | bytes 98336 | tf_op jit(solution)/shard_map/ppermute | solution.py:287
  106.3 3.4 %collective-permute-start.42 = (bf16[2,48,512]{2,1,0:T(8,128)(2,1)S(1)}, bf16[2,48,512]{2,1,0:T(8,128)(2,1)S(1)}, u32[]{:S(2)}, u32[]{:S(2)}) collective-permute-start(bf16[2,48,512]{2,1,0:T(8,128)(2,1)S(1)} %get-tuple-element.117), channel_id=1, source_target_pairs={{0,11},{1,10},{2,9},{3,8},{4,15},{5,14},{6,13},{7,12},{8,3},{9,2},... | collective-permute-start | bytes 294920 | tf_op jit(solution)/shard_map/ppermute | solution.py:287
  109.7 2.5 %collective-permute-done.38.refs_25_ = bf16[2,48,512]{2,1,0:T(8,128)(2,1)S(1)} collective-permute-done((bf16[2,48,512]{2,1,0:T(8,128)(2,1)S(1)}, bf16[2,48,512]{2,1,0:T(8,128)(2,1)S(1)}, u32[]{:S(2)}, u32[]{:S(2)}) %collective-permute-start.38) | collective-permute-done | bytes 98336 | tf_op jit(solution)/shard_map/ppermute | solution.py:287
  112.4 2.3 %collective-permute-start.44 = (bf16[2,48,512]{2,1,0:T(8,128)(2,1)S(1)}, bf16[2,48,512]{2,1,0:T(8,128)(2,1)S(1)}, u32[]{:S(2)}, u32[]{:S(2)}) collective-permute-start(bf16[2,48,512]{2,1,0:T(8,128)(2,1)S(1)} %get-tuple-element.119), channel_id=1, source_target_pairs={{0,15},{1,14},{2,13},{3,12},{4,11},{5,10},{6,9},{7,8},{8,7},{9,6},... | collective-permute-start | bytes 294920 | tf_op jit(solution)/shard_map/ppermute | solution.py:287
  114.7 3.5 %collective-permute-done.42.refs_29_ = bf16[2,48,512]{2,1,0:T(8,128)(2,1)S(1)} collective-permute-done((bf16[2,48,512]{2,1,0:T(8,128)(2,1)S(1)}, bf16[2,48,512]{2,1,0:T(8,128)(2,1)S(1)}, u32[]{:S(2)}, u32[]{:S(2)}) %collective-permute-start.42) | collective-permute-done | bytes 98336 | tf_op jit(solution)/shard_map/ppermute | solution.py:287
  120.2 4.7 %update.1 = (bf16[384,1024]{1,0:T(8,128)(2,1)}, bf16[384,1024]{1,0:T(8,128)(2,1)}, bf16[32,1024]{1,0:T(8,128)(2,1)S(1)}, bf16[32,1024]{1,0:T(8,128)(2,1)S(1)}, b...) custom-call(s32[1]{0:T(128)} %bitcast.me_ref, ...), custom_call_target="tpu_custom_call" | custom-call | flops 2239758336 | bytes 6029312 | tf_op jit(solution)/shard_map/update/pallas_call | solution.py:220
  125.0 5.3 %collective-permute-start.45 = (bf16[32,1024]{1,0:T(8,128)(2,1)S(1)}, bf16[32,1024]{1,0:T(8,128)(2,1)S(1)}, u32[]{:S(2)}, u32[]{:S(2)}) collective-permute-start(bf16[32,1024]{1,0:T(8,128)(2,1)S(1)} %get-tuple-element.124), channel_id=1, source_target_pairs={{0,8},{1,9},{2,10},{3,11},{4,12},{5,13},{6,14},{7,15},{8,0},{9,1},... | collective-permute-start | bytes 196616 | tf_op jit(solution)/shard_map/ppermute | solution.py:287
  144.5 2.7 %collective-permute-done.53.refs_9_ = bf16[32,1024]{1,0:T(8,128)(2,1)S(1)} collective-permute-done((bf16[32,1024]{1,0:T(8,128)(2,1)S(1)}, bf16[32,1024]{1,0:T(8,128)(2,1)S(1)}, u32[]{:S(2)}, u32[]{:S(2)}) %collective-permute-start.53) | collective-permute-done | bytes 65568 | tf_op jit(solution)/shard_map/ppermute | solution.py:287
  149.5 2.7 %collective-permute-done.57.refs_13_ = bf16[32,1024]{1,0:T(8,128)(2,1)S(1)} collective-permute-done((bf16[32,1024]{1,0:T(8,128)(2,1)S(1)}, bf16[32,1024]{1,0:T(8,128)(2,1)S(1)}, u32[]{:S(2)}, u32[]{:S(2)}) %collective-permute-start.57) | collective-permute-done | bytes 65568 | tf_op jit(solution)/shard_map/ppermute | solution.py:287
  152.7 2.3 %collective-permute-done.59.refs_15_ = bf16[32,1024]{1,0:T(8,128)(2,1)S(1)} collective-permute-done((bf16[32,1024]{1,0:T(8,128)(2,1)S(1)}, bf16[32,1024]{1,0:T(8,128)(2,1)S(1)}, u32[]{:S(2)}, u32[]{:S(2)}) %collective-permute-start.59) | collective-permute-done | bytes 65568 | tf_op jit(solution)/shard_map/ppermute | solution.py:287
  (116 shorter events, 51.3 us)
Async XLA Ops:
  3.3 15.3 %collective-permute-start.15 = (bf16[2,48,512]{2,1,0:T(8,128)(2,1)}, bf16[2,48,512]{2,1,0:T(8,128)(2,1)S(1)}, u32[]{:S(2)}, u32[]{:S(2)}) collective-permute-start(bf16[2,48,512]{2,1,0:T(8,128)(2,1)} %get-tuple-element.90), channel_id=1, source_target_pairs={{0,5},{1,4},{2,7},{3,6},{4,1},{5,0},{6,3},{7,2},{8,13},{9,12},{10,... | collective-permute-start | bytes 294920 | tf_op jit(solution)/shard_map/ppermute | solution.py:287
  5.8 14.7 %collective-permute-start.16 = (bf16[2,48,512]{2,1,0:T(8,128)(2,1)}, bf16[2,48,512]{2,1,0:T(8,128)(2,1)S(1)}, u32[]{:S(2)}, u32[]{:S(2)}) collective-permute-start(bf16[2,48,512]{2,1,0:T(8,128)(2,1)} %get-tuple-element.91), channel_id=1, source_target_pairs={{0,8},{1,9},{2,10},{3,11},{4,12},{5,13},{6,14},{7,15},{8,0},{9,1},... | collective-permute-start | bytes 294920 | tf_op jit(solution)/shard_map/ppermute | solution.py:287
  8.4 14.4 %collective-permute-start.17 = (bf16[2,48,512]{2,1,0:T(8,128)(2,1)}, bf16[2,48,512]{2,1,0:T(8,128)(2,1)S(1)}, u32[]{:S(2)}, u32[]{:S(2)}) collective-permute-start(bf16[2,48,512]{2,1,0:T(8,128)(2,1)} %get-tuple-element.92), channel_id=1, source_target_pairs={{0,7},{1,6},{2,5},{3,4},{4,3},{5,2},{6,1},{7,0},{8,15},{9,14},{10,... | collective-permute-start | bytes 294920 | tf_op jit(solution)/shard_map/ppermute | solution.py:287
  9.8 13.5 %collective-permute-start.18 = (bf16[2,48,512]{2,1,0:T(8,128)(2,1)}, bf16[2,48,512]{2,1,0:T(8,128)(2,1)S(1)}, u32[]{:S(2)}, u32[]{:S(2)}) collective-permute-start(bf16[2,48,512]{2,1,0:T(8,128)(2,1)} %get-tuple-element.93), channel_id=1, source_target_pairs={{0,12},{1,13},{2,14},{3,15},{4,8},{5,9},{6,10},{7,11},{8,4},{9,5},... | collective-permute-start | bytes 294920 | tf_op jit(solution)/shard_map/ppermute | solution.py:287
  11.2 12.7 %collective-permute-start.19 = (bf16[2,48,512]{2,1,0:T(8,128)(2,1)}, bf16[2,48,512]{2,1,0:T(8,128)(2,1)S(1)}, u32[]{:S(2)}, u32[]{:S(2)}) collective-permute-start(bf16[2,48,512]{2,1,0:T(8,128)(2,1)} %get-tuple-element.71.refs_6_), channel_id=1, source_target_pairs={{0,3},{1,2},{2,1},{3,0},{4,7},{5,6},{6,5},{7,4},{8,11},{9,10},{10,... | collective-permute-start | bytes 294920 | tf_op jit(solution)/shard_map/ppermute | solution.py:287
  22.8 11.4 %collective-permute-start.22 = (bf16[2,48,512]{2,1,0:T(8,128)(2,1)}, bf16[2,48,512]{2,1,0:T(8,128)(2,1)S(1)}, u32[]{:S(2)}, u32[]{:S(2)}) collective-permute-start(bf16[2,48,512]{2,1,0:T(8,128)(2,1)} %get-tuple-element.96), channel_id=1, source_target_pairs={{0,13},{1,12},{2,15},{3,14},{4,9},{5,8},{6,11},{7,10},{8,5},{9,4},... | collective-permute-start | bytes 294920 | tf_op jit(solution)/shard_map/ppermute | solution.py:287
  23.3 13.2 %collective-permute-start.23 = (bf16[2,48,512]{2,1,0:T(8,128)(2,1)}, bf16[2,48,512]{2,1,0:T(8,128)(2,1)S(1)}, u32[]{:S(2)}, u32[]{:S(2)}) collective-permute-start(bf16[2,48,512]{2,1,0:T(8,128)(2,1)} %get-tuple-element.97), channel_id=1, source_target_pairs={{0,2},{1,3},{2,0},{3,1},{4,6},{5,7},{6,4},{7,5},{8,10},{9,11},{10,... | collective-permute-start | bytes 294920 | tf_op jit(solution)/shard_map/ppermute | solution.py:287
  23.9 16.8 %collective-permute-start.24 = (bf16[2,48,512]{2,1,0:T(8,128)(2,1)}, bf16[2,48,512]{2,1,0:T(8,128)(2,1)S(1)}, u32[]{:S(2)}, u32[]{:S(2)}) collective-permute-start(bf16[2,48,512]{2,1,0:T(8,128)(2,1)} %get-tuple-element.98), channel_id=1, source_target_pairs={{0,10},{1,11},{2,8},{3,9},{4,14},{5,15},{6,12},{7,13},{8,2},{9,3},... | collective-permute-start | bytes 294920 | tf_op jit(solution)/shard_map/ppermute | solution.py:287
  26.9 13.8 %collective-permute-start.25 = (bf16[2,48,512]{2,1,0:T(8,128)(2,1)}, bf16[2,48,512]{2,1,0:T(8,128)(2,1)S(1)}, u32[]{:S(2)}, u32[]{:S(2)}) collective-permute-start(bf16[2,48,512]{2,1,0:T(8,128)(2,1)} %get-tuple-element.99), channel_id=1, source_target_pairs={{0,14},{1,15},{2,12},{3,13},{4,10},{5,11},{6,8},{7,9},{8,6},{9,7},... | collective-permute-start | bytes 294920 | tf_op jit(solution)/shard_map/ppermute | solution.py:287
  31.1 13.2 %collective-permute-start.26 = (bf16[2,48,512]{2,1,0:T(8,128)(2,1)}, bf16[2,48,512]{2,1,0:T(8,128)(2,1)S(1)}, u32[]{:S(2)}, u32[]{:S(2)}) collective-permute-start(bf16[2,48,512]{2,1,0:T(8,128)(2,1)} %get-tuple-element.100), channel_id=1, source_target_pairs={{0,1},{1,0},{2,3},{3,2},{4,5},{5,4},{6,7},{7,6},{8,9},{9,8},{10,11... | collective-permute-start | bytes 294920 | tf_op jit(solution)/shard_map/ppermute | solution.py:287
  34.2 11.3 %collective-permute-start.27 = (bf16[2,48,512]{2,1,0:T(8,128)(2,1)}, bf16[2,48,512]{2,1,0:T(8,128)(2,1)S(1)}, u32[]{:S(2)}, u32[]{:S(2)}) collective-permute-start(bf16[2,48,512]{2,1,0:T(8,128)(2,1)} %get-tuple-element.101), channel_id=1, source_target_pairs={{0,11},{1,10},{2,9},{3,8},{4,15},{5,14},{6,13},{7,12},{8,3},{9,2},... | collective-permute-start | bytes 294920 | tf_op jit(solution)/shard_map/ppermute | solution.py:287
  36.5 11.2 %collective-permute-start.28 = (bf16[2,48,512]{2,1,0:T(8,128)(2,1)}, bf16[2,48,512]{2,1,0:T(8,128)(2,1)S(1)}, u32[]{:S(2)}, u32[]{:S(2)}) collective-permute-start(bf16[2,48,512]{2,1,0:T(8,128)(2,1)} %get-tuple-element.102), channel_id=1, source_target_pairs={{0,4},{1,5},{2,6},{3,7},{4,0},{5,1},{6,2},{7,3},{8,12},{9,13},{10,... | collective-permute-start | bytes 294920 | tf_op jit(solution)/shard_map/ppermute | solution.py:287
  40.7 17.8 %collective-permute-start = (bf16[32,1792]{1,0:T(8,128)(2,1)S(1)}, bf16[32,1792]{1,0:T(8,128)(2,1)S(1)}, u32[]{:S(2)}, u32[]{:S(2)}) collective-permute-start(bf16[32,1792]{1,0:T(8,128)(2,1)S(1)} %get-tuple-element.73), channel_id=1, source_target_pairs={{0,8},{1,9},{2,10},{3,11},{4,12},{5,13},{6,14},{7,15},{8,0},{9,1},... | collective-permute-start | bytes 344072 | tf_op jit(solution)/shard_map/ppermute | solution.py:287
  44.3 14.2 %collective-permute-start.1 = (bf16[32,1792]{1,0:T(8,128)(2,1)S(1)}, bf16[32,1792]{1,0:T(8,128)(2,1)S(1)}, u32[]{:S(2)}, u32[]{:S(2)}) collective-permute-start(bf16[32,1792]{1,0:T(8,128)(2,1)S(1)} %get-tuple-element.74), channel_id=1, source_target_pairs={{0,7},{1,6},{2,5},{3,4},{4,3},{5,2},{6,1},{7,0},{8,15},{9,14},{10,... | collective-permute-start | bytes 344072 | tf_op jit(solution)/shard_map/ppermute | solution.py:287
  45.5 14.7 %collective-permute-start.2 = (bf16[32,1792]{1,0:T(8,128)(2,1)S(1)}, bf16[32,1792]{1,0:T(8,128)(2,1)S(1)}, u32[]{:S(2)}, u32[]{:S(2)}) collective-permute-start(bf16[32,1792]{1,0:T(8,128)(2,1)S(1)} %get-tuple-element.75), channel_id=1, source_target_pairs={{0,12},{1,13},{2,14},{3,15},{4,8},{5,9},{6,10},{7,11},{8,4},{9,5},... | collective-permute-start | bytes 344072 | tf_op jit(solution)/shard_map/ppermute | solution.py:287
  47.8 12.4 %collective-permute-start.3 = (bf16[32,1792]{1,0:T(8,128)(2,1)S(1)}, bf16[32,1792]{1,0:T(8,128)(2,1)S(1)}, u32[]{:S(2)}, u32[]{:S(2)}) collective-permute-start(bf16[32,1792]{1,0:T(8,128)(2,1)S(1)} %get-tuple-element.76), channel_id=1, source_target_pairs={{0,3},{1,2},{2,1},{3,0},{4,7},{5,6},{6,5},{7,4},{8,11},{9,10},{10,... | collective-permute-start | bytes 344072 | tf_op jit(solution)/shard_map/ppermute | solution.py:287
  49.3 14.4 %collective-permute-start.4 = (bf16[32,1792]{1,0:T(8,128)(2,1)S(1)}, bf16[32,1792]{1,0:T(8,128)(2,1)S(1)}, u32[]{:S(2)}, u32[]{:S(2)}) collective-permute-start(bf16[32,1792]{1,0:T(8,128)(2,1)S(1)} %get-tuple-element.77), channel_id=1, source_target_pairs={{0,9},{1,8},{2,11},{3,10},{4,13},{5,12},{6,15},{7,14},{8,1},{9,0},... | collective-permute-start | bytes 344072 | tf_op jit(solution)/shard_map/ppermute | solution.py:287
  60.2 13.6 %collective-permute-start.8 = (bf16[32,1792]{1,0:T(8,128)(2,1)S(1)}, bf16[32,1792]{1,0:T(8,128)(2,1)S(1)}, u32[]{:S(2)}, u32[]{:S(2)}) collective-permute-start(bf16[32,1792]{1,0:T(8,128)(2,1)S(1)} %get-tuple-element.81), channel_id=1, source_target_pairs={{0,10},{1,11},{2,8},{3,9},{4,14},{5,15},{6,12},{7,13},{8,2},{9,3},... | collective-permute-start | bytes 344072 | tf_op jit(solution)/shard_map/ppermute | solution.py:287
  63.8 13.5 %collective-permute-start.9 = (bf16[32,1792]{1,0:T(8,128)(2,1)S(1)}, bf16[32,1792]{1,0:T(8,128)(2,1)S(1)}, u32[]{:S(2)}, u32[]{:S(2)}) collective-permute-start(bf16[32,1792]{1,0:T(8,128)(2,1)S(1)} %get-tuple-element.82), channel_id=1, source_target_pairs={{0,5},{1,4},{2,7},{3,6},{4,1},{5,0},{6,3},{7,2},{8,13},{9,12},{10,... | collective-permute-start | bytes 344072 | tf_op jit(solution)/shard_map/ppermute | solution.py:287
  68.6 13.6 %collective-permute-start.10 = (bf16[32,1792]{1,0:T(8,128)(2,1)S(1)}, bf16[32,1792]{1,0:T(8,128)(2,1)S(1)}, u32[]{:S(2)}, u32[]{:S(2)}) collective-permute-start(bf16[32,1792]{1,0:T(8,128)(2,1)S(1)} %get-tuple-element.83), channel_id=1, source_target_pairs={{0,14},{1,15},{2,12},{3,13},{4,10},{5,11},{6,8},{7,9},{8,6},{9,7},... | collective-permute-start | bytes 344072 | tf_op jit(solution)/shard_map/ppermute | solution.py:287
  69.5 14.0 %collective-permute-start.11 = (bf16[32,1792]{1,0:T(8,128)(2,1)S(1)}, bf16[32,1792]{1,0:T(8,128)(2,1)S(1)}, u32[]{:S(2)}, u32[]{:S(2)}) collective-permute-start(bf16[32,1792]{1,0:T(8,128)(2,1)S(1)} %get-tuple-element.84), channel_id=1, source_target_pairs={{0,1},{1,0},{2,3},{3,2},{4,5},{5,4},{6,7},{7,6},{8,9},{9,8},{10,11... | collective-permute-start | bytes 344072 | tf_op jit(solution)/shard_map/ppermute | solution.py:287
  70.7 13.0 %collective-permute-start.12 = (bf16[32,1792]{1,0:T(8,128)(2,1)S(1)}, bf16[32,1792]{1,0:T(8,128)(2,1)S(1)}, u32[]{:S(2)}, u32[]{:S(2)}) collective-permute-start(bf16[32,1792]{1,0:T(8,128)(2,1)S(1)} %get-tuple-element.85), channel_id=1, source_target_pairs={{0,11},{1,10},{2,9},{3,8},{4,15},{5,14},{6,13},{7,12},{8,3},{9,2},... | collective-permute-start | bytes 344072 | tf_op jit(solution)/shard_map/ppermute | solution.py:287
  73.8 12.8 %collective-permute-start.13 = (bf16[32,1792]{1,0:T(8,128)(2,1)S(1)}, bf16[32,1792]{1,0:T(8,128)(2,1)S(1)}, u32[]{:S(2)}, u32[]{:S(2)}) collective-permute-start(bf16[32,1792]{1,0:T(8,128)(2,1)S(1)} %get-tuple-element.86), channel_id=1, source_target_pairs={{0,4},{1,5},{2,6},{3,7},{4,0},{5,1},{6,2},{7,3},{8,12},{9,13},{10,... | collective-permute-start | bytes 344072 | tf_op jit(solution)/shard_map/ppermute | solution.py:287
  77.2 11.3 %collective-permute-start.14 = (bf16[32,1792]{1,0:T(8,128)(2,1)S(1)}, bf16[32,1792]{1,0:T(8,128)(2,1)S(1)}, u32[]{:S(2)}, u32[]{:S(2)}) collective-permute-start(bf16[32,1792]{1,0:T(8,128)(2,1)S(1)} %get-tuple-element.87), channel_id=1, source_target_pairs={{0,15},{1,14},{2,13},{3,12},{4,11},{5,10},{6,9},{7,8},{8,7},{9,6},... | collective-permute-start | bytes 344072 | tf_op jit(solution)/shard_map/ppermute | solution.py:287
  82.2 12.3 %collective-permute-start.30 = (bf16[2,48,512]{2,1,0:T(8,128)(2,1)S(1)}, bf16[2,48,512]{2,1,0:T(8,128)(2,1)S(1)}, u32[]{:S(2)}, u32[]{:S(2)}) collective-permute-start(bf16[2,48,512]{2,1,0:T(8,128)(2,1)S(1)} %get-tuple-element.105), channel_id=1, source_target_pairs={{0,8},{1,9},{2,10},{3,11},{4,12},{5,13},{6,14},{7,15},{8,0},{9,1},... | collective-permute-start | bytes 294920 | tf_op jit(solution)/shard_map/ppermute | solution.py:287
  83.5 11.7 %collective-permute-start.31 = (bf16[2,48,512]{2,1,0:T(8,128)(2,1)S(1)}, bf16[2,48,512]{2,1,0:T(8,128)(2,1)S(1)}, u32[]{:S(2)}, u32[]{:S(2)}) collective-permute-start(bf16[2,48,512]{2,1,0:T(8,128)(2,1)S(1)} %get-tuple-element.106), channel_id=1, source_target_pairs={{0,7},{1,6},{2,5},{3,4},{4,3},{5,2},{6,1},{7,0},{8,15},{9,14},{10,... | collective-permute-start | bytes 294920 | tf_op jit(solution)/shard_map/ppermute | solution.py:287
  83.7 12.7 %collective-permute-start.32 = (bf16[2,48,512]{2,1,0:T(8,128)(2,1)S(1)}, bf16[2,48,512]{2,1,0:T(8,128)(2,1)S(1)}, u32[]{:S(2)}, u32[]{:S(2)}) collective-permute-start(bf16[2,48,512]{2,1,0:T(8,128)(2,1)S(1)} %get-tuple-element.107), channel_id=1, source_target_pairs={{0,12},{1,13},{2,14},{3,15},{4,8},{5,9},{6,10},{7,11},{8,4},{9,5},... | collective-permute-start | bytes 294920 | tf_op jit(solution)/shard_map/ppermute | solution.py:287
  86.6 11.5 %collective-permute-start.33 = (bf16[2,48,512]{2,1,0:T(8,128)(2,1)S(1)}, bf16[2,48,512]{2,1,0:T(8,128)(2,1)S(1)}, u32[]{:S(2)}, u32[]{:S(2)}) collective-permute-start(bf16[2,48,512]{2,1,0:T(8,128)(2,1)S(1)} %get-tuple-element.108), channel_id=1, source_target_pairs={{0,3},{1,2},{2,1},{3,0},{4,7},{5,6},{6,5},{7,4},{8,11},{9,10},{10,... | collective-permute-start | bytes 294920 | tf_op jit(solution)/shard_map/ppermute | solution.py:287
  88.5 14.8 %collective-permute-start.34 = (bf16[2,48,512]{2,1,0:T(8,128)(2,1)S(1)}, bf16[2,48,512]{2,1,0:T(8,128)(2,1)S(1)}, u32[]{:S(2)}, u32[]{:S(2)}) collective-permute-start(bf16[2,48,512]{2,1,0:T(8,128)(2,1)S(1)} %get-tuple-element.109), channel_id=1, source_target_pairs={{0,9},{1,8},{2,11},{3,10},{4,13},{5,12},{6,15},{7,14},{8,1},{9,0},... | collective-permute-start | bytes 294920 | tf_op jit(solution)/shard_map/ppermute | solution.py:287
  95.2 11.1 %collective-permute-start.36 = (bf16[2,48,512]{2,1,0:T(8,128)(2,1)S(1)}, bf16[2,48,512]{2,1,0:T(8,128)(2,1)S(1)}, u32[]{:S(2)}, u32[]{:S(2)}) collective-permute-start(bf16[2,48,512]{2,1,0:T(8,128)(2,1)S(1)} %get-tuple-element.111), channel_id=1, source_target_pairs={{0,13},{1,12},{2,15},{3,14},{4,9},{5,8},{6,11},{7,10},{8,5},{9,4},... | collective-permute-start | bytes 294920 | tf_op jit(solution)/shard_map/ppermute | solution.py:287
  98.1 14.1 %collective-permute-start.38 = (bf16[2,48,512]{2,1,0:T(8,128)(2,1)S(1)}, bf16[2,48,512]{2,1,0:T(8,128)(2,1)S(1)}, u32[]{:S(2)}, u32[]{:S(2)}) collective-permute-start(bf16[2,48,512]{2,1,0:T(8,128)(2,1)S(1)} %get-tuple-element.113), channel_id=1, source_target_pairs={{0,10},{1,11},{2,8},{3,9},{4,14},{5,15},{6,12},{7,13},{8,2},{9,3},... | collective-permute-start | bytes 294920 | tf_op jit(solution)/shard_map/ppermute | solution.py:287
  106.3 11.9 %collective-permute-start.42 = (bf16[2,48,512]{2,1,0:T(8,128)(2,1)S(1)}, bf16[2,48,512]{2,1,0:T(8,128)(2,1)S(1)}, u32[]{:S(2)}, u32[]{:S(2)}) collective-permute-start(bf16[2,48,512]{2,1,0:T(8,128)(2,1)S(1)} %get-tuple-element.117), channel_id=1, source_target_pairs={{0,11},{1,10},{2,9},{3,8},{4,15},{5,14},{6,13},{7,12},{8,3},{9,2},... | collective-permute-start | bytes 294920 | tf_op jit(solution)/shard_map/ppermute | solution.py:287
  (39 other events, 284.5 us)

commit v22 on v20

--- a/solution.py
+++ b/solution.py
@@ -266,7 +266,7 @@
 
     half = groups // 2
     far, near = both_ends(list(range(half, groups))), both_ends(list(range(half - 1, 0, -1)))
-    return [0] + [s for pair in zip(far, near + [None]) for s in pair if s is not None][::-1]
+    return [0] + [s for pair in zip(far, near + [None]) for s in pair if s is not None]
 
 
 def swap(pieces):
@@ -287,7 +287,7 @@
     spread = swap(split(me, w_moment, w_down, groups))
     packed, fwd_slot, gates = pack_rows(
         live_rows, me, perm, grad_route, fwd_route, grad_hidden, grad_out, fwd_hidden, fwd_gate,
-        spread[2 * groups // 3], groups, capacity,
+        spread[mixed_order(groups).index(1)], groups, capacity,
     )
     received = swap(packed)
     placed = swap(reorder(me, perm, spread, received[groups // 3]))

time: 152 us -> 153 us (level)
  starting transfers between devices: 97.4 us -> 101 us
  waiting for transfers between devices: 39.9 us -> 36.8 us
    ppermute x60, starting transfers between devices: 97.4 us -> 101 us  [swap(): lax.ppermute(piece, 'expert', [(i, i ^ s) for i in range(groups)])]
    ppermute x60, waiting for transfers between devices: 39.9 us -> 36.8 us  [swap(): lax.ppermute(piece, 'expert', [(i, i ^ s) for i in range(groups)])]
  transfers between devices with their start and end apart: 60 -> 60, of which waited for: 19 -> 23; matrix products, arithmetic and copies ran while one was open for 0% -> 0% of each run, Pallas kernels for 2% -> 2%
where the time goes in v22:
time: 153 us
  starting transfers between devices  101 us (66%)
  waiting for transfers between devices  36.8 us (24%)
  Pallas kernels  12.3 us (8%)
  between operations  1.54 us (1%)
    ppermute x60, starting transfers between devices, swap(): lax.ppermute(piece, 'expert', [(i, i ^ s) for i in range(groups)])  101 us
    ppermute x60, waiting for transfers between devices, swap(): lax.ppermute(piece, 'expert', [(i, i ^ s) for i in range(groups)])  36.8 us
    pallas_call x1, Pallas kernels, update(): pl.pallas_call(functools.partial(update_kernel, groups), out_shape=(shape...  4.73 us
  transfers between devices with their start and end apart: 60, of which 23 were waited for; matrix products, arithmetic and copies ran while one was open for 0% of the time, Pallas kernels for 2%

profile of v22, /device:TPU:0, one launch (start us, length us, event | category | flops | bytes accessed | tf_op | source)
XLA Modules:
  0.0 152.6 jit_solution(13859004916337946712)
XLA Ops:
  0.7 2.7 %split.1 = (bf16[2,48,512]{2,1,0:T(8,128)(2,1)}, bf16[2,48,512]{2,1,0:T(8,128)(2,1)}, bf16[2,48,512]{2,1,0:T(8,128)(2,1)}, bf16[2,48,512]{2,1,0:T(8,128)(2,1)}, ...) custom-call(s32[1]{0:T(128)} %bitcast.me_ref, ...), custom_call_target="tpu_custom_call" | custom-call | bytes 3145728 | tf_op jit(solution)/shard_map/split/pallas_call | solution.py:135
  3.9 3.7 %collective-permute-start.16 = (bf16[2,48,512]{2,1,0:T(8,128)(2,1)}, bf16[2,48,512]{2,1,0:T(8,128)(2,1)S(1)}, u32[]{:S(2)}, u32[]{:S(2)}) collective-permute-start(bf16[2,48,512]{2,1,0:T(8,128)(2,1)} %get-tuple-element.89), channel_id=1, source_target_pairs={{0,8},{1,9},{2,10},{3,11},{4,12},{5,13},{6,14},{7,15},{8,0},{9,1},... | collective-permute-start | bytes 294920 | tf_op jit(solution)/shard_map/ppermute | solution.py:276
  7.6 2.3 %collective-permute-start.17 = (bf16[2,48,512]{2,1,0:T(8,128)(2,1)}, bf16[2,48,512]{2,1,0:T(8,128)(2,1)S(1)}, u32[]{:S(2)}, u32[]{:S(2)}) collective-permute-start(bf16[2,48,512]{2,1,0:T(8,128)(2,1)} %get-tuple-element.90), channel_id=1, source_target_pairs={{0,7},{1,6},{2,5},{3,4},{4,3},{5,2},{6,1},{7,0},{8,15},{9,14},{10,... | collective-permute-start | bytes 294920 | tf_op jit(solution)/shard_map/ppermute | solution.py:276
  13.5 1.9 %collective-permute-start.21 = (bf16[2,48,512]{2,1,0:T(8,128)(2,1)}, bf16[2,48,512]{2,1,0:T(8,128)(2,1)S(1)}, u32[]{:S(2)}, u32[]{:S(2)}) collective-permute-start(bf16[2,48,512]{2,1,0:T(8,128)(2,1)} %get-tuple-element.94), channel_id=1, source_target_pairs={{0,6},{1,7},{2,4},{3,5},{4,2},{5,3},{6,0},{7,1},{8,14},{9,15},{10,... | collective-permute-start | bytes 294920 | tf_op jit(solution)/shard_map/ppermute | solution.py:276
  18.7 5.1 %collective-permute-start.24 = (bf16[2,48,512]{2,1,0:T(8,128)(2,1)}, bf16[2,48,512]{2,1,0:T(8,128)(2,1)S(1)}, u32[]{:S(2)}, u32[]{:S(2)}) collective-permute-start(bf16[2,48,512]{2,1,0:T(8,128)(2,1)} %get-tuple-element.97), channel_id=1, source_target_pairs={{0,10},{1,11},{2,8},{3,9},{4,14},{5,15},{6,12},{7,13},{8,2},{9,3},... | collective-permute-start | bytes 294920 | tf_op jit(solution)/shard_map/ppermute | solution.py:276
  24.4 3.9 %collective-permute-start.26 = (bf16[2,48,512]{2,1,0:T(8,128)(2,1)}, bf16[2,48,512]{2,1,0:T(8,128)(2,1)S(1)}, u32[]{:S(2)}, u32[]{:S(2)}) collective-permute-start(bf16[2,48,512]{2,1,0:T(8,128)(2,1)} %get-tuple-element.99), channel_id=1, source_target_pairs={{0,14},{1,15},{2,12},{3,13},{4,10},{5,11},{6,8},{7,9},{8,6},{9,7},... | collective-permute-start | bytes 294920 | tf_op jit(solution)/shard_map/ppermute | solution.py:276
  28.3 2.9 %collective-permute-start.27 = (bf16[2,48,512]{2,1,0:T(8,128)(2,1)}, bf16[2,48,512]{2,1,0:T(8,128)(2,1)S(1)}, u32[]{:S(2)}, u32[]{:S(2)}) collective-permute-start(bf16[2,48,512]{2,1,0:T(8,128)(2,1)} %get-tuple-element.100), channel_id=1, source_target_pairs={{0,11},{1,10},{2,9},{3,8},{4,15},{5,14},{6,13},{7,12},{8,3},{9,2},... | collective-permute-start | bytes 294920 | tf_op jit(solution)/shard_map/ppermute | solution.py:276
  32.2 4.3 %collective-permute-start.29 = (bf16[2,48,512]{2,1,0:T(8,128)(2,1)}, bf16[2,48,512]{2,1,0:T(8,128)(2,1)S(1)}, u32[]{:S(2)}, u32[]{:S(2)}) collective-permute-start(bf16[2,48,512]{2,1,0:T(8,128)(2,1)} %get-tuple-element.102), channel_id=1, source_target_pairs={{0,15},{1,14},{2,13},{3,12},{4,11},{5,10},{6,9},{7,8},{8,7},{9,6},... | collective-permute-start | bytes 294920 | tf_op jit(solution)/shard_map/ppermute | solution.py:276
  37.8 2.8 %pack_rows.1 = (bf16[32,1792]{1,0:T(8,128)(2,1)S(1)}, bf16[32,1792]{1,0:T(8,128)(2,1)S(1)}, bf16[32,1792]{1,0:T(8,128)(2,1)S(1)}, bf16[32,1792]{1,0:T(8,128)(2,1...) custom-call(s32[1]{0:T(128)S(6)} %copy.13.live_ref, ...), custom_call_target="tpu_custom_call" | custom-call | flops 469762048 | bytes 2752512 | tf_op jit(solution)/shard_map/pack_rows/pallas_call | solution.py:107
  41.3 6.6 %collective-permute-start.3 = (bf16[32,1792]{1,0:T(8,128)(2,1)S(1)}, bf16[32,1792]{1,0:T(8,128)(2,1)S(1)}, u32[]{:S(2)}, u32[]{:S(2)}) collective-permute-start(bf16[32,1792]{1,0:T(8,128)(2,1)S(1)} %get-tuple-element.75), channel_id=1, source_target_pairs={{0,12},{1,13},{2,14},{3,15},{4,8},{5,9},{6,10},{7,11},{8,4},{9,5},... | collective-permute-start | bytes 344072 | tf_op jit(solution)/shard_map/ppermute | solution.py:276
  49.7 3.0 %collective-permute-start.7 = (bf16[32,1792]{1,0:T(8,128)(2,1)S(1)}, bf16[32,1792]{1,0:T(8,128)(2,1)S(1)}, u32[]{:S(2)}, u32[]{:S(2)}) collective-permute-start(bf16[32,1792]{1,0:T(8,128)(2,1)S(1)} %get-tuple-element.79), channel_id=1, source_target_pairs={{0,13},{1,12},{2,15},{3,14},{4,9},{5,8},{6,11},{7,10},{8,5},{9,4},... | collective-permute-start | bytes 344072 | tf_op jit(solution)/shard_map/ppermute | solution.py:276
  55.9 3.4 %collective-permute-start.9 = (bf16[32,1792]{1,0:T(8,128)(2,1)S(1)}, bf16[32,1792]{1,0:T(8,128)(2,1)S(1)}, u32[]{:S(2)}, u32[]{:S(2)}) collective-permute-start(bf16[32,1792]{1,0:T(8,128)(2,1)S(1)} %get-tuple-element.81), channel_id=1, source_target_pairs={{0,10},{1,11},{2,8},{3,9},{4,14},{5,15},{6,12},{7,13},{8,2},{9,3},... | collective-permute-start | bytes 344072 | tf_op jit(solution)/shard_map/ppermute | solution.py:276
  60.5 2.8 %collective-permute-start.11 = (bf16[32,1792]{1,0:T(8,128)(2,1)S(1)}, bf16[32,1792]{1,0:T(8,128)(2,1)S(1)}, u32[]{:S(2)}, u32[]{:S(2)}) collective-permute-start(bf16[32,1792]{1,0:T(8,128)(2,1)S(1)} %get-tuple-element.83), channel_id=1, source_target_pairs={{0,14},{1,15},{2,12},{3,13},{4,10},{5,11},{6,8},{7,9},{8,6},{9,7},... | collective-permute-start | bytes 344072 | tf_op jit(solution)/shard_map/ppermute | solution.py:276
  63.2 3.4 %collective-permute-start.12 = (bf16[32,1792]{1,0:T(8,128)(2,1)S(1)}, bf16[32,1792]{1,0:T(8,128)(2,1)S(1)}, u32[]{:S(2)}, u32[]{:S(2)}) collective-permute-start(bf16[32,1792]{1,0:T(8,128)(2,1)S(1)} %get-tuple-element.84), channel_id=1, source_target_pairs={{0,1},{1,0},{2,3},{3,2},{4,5},{5,4},{6,7},{7,6},{8,9},{9,8},{10,11... | collective-permute-start | bytes 344072 | tf_op jit(solution)/shard_map/ppermute | solution.py:276
  66.6 2.0 %collective-permute-start.13 = (bf16[32,1792]{1,0:T(8,128)(2,1)S(1)}, bf16[32,1792]{1,0:T(8,128)(2,1)S(1)}, u32[]{:S(2)}, u32[]{:S(2)}) collective-permute-start(bf16[32,1792]{1,0:T(8,128)(2,1)S(1)} %get-tuple-element.85), channel_id=1, source_target_pairs={{0,11},{1,10},{2,9},{3,8},{4,15},{5,14},{6,13},{7,12},{8,3},{9,2},... | collective-permute-start | bytes 344072 | tf_op jit(solution)/shard_map/ppermute | solution.py:276
  68.6 6.3 %collective-permute-done.9.refs_9_ = bf16[32,1792]{1,0:T(8,128)(2,1)S(1)} collective-permute-done((bf16[32,1792]{1,0:T(8,128)(2,1)S(1)}, bf16[32,1792]{1,0:T(8,128)(2,1)S(1)}, u32[]{:S(2)}, u32[]{:S(2)}) %collective-permute-start.9) | collective-permute-done | bytes 114720 | tf_op jit(solution)/shard_map/ppermute | solution.py:276
  75.8 2.7 %collective-permute-start.30 = (bf16[2,48,512]{2,1,0:T(8,128)(2,1)S(1)}, bf16[2,48,512]{2,1,0:T(8,128)(2,1)S(1)}, u32[]{:S(2)}, u32[]{:S(2)}) collective-permute-start(bf16[2,48,512]{2,1,0:T(8,128)(2,1)S(1)} %get-tuple-element.104), channel_id=1, source_target_pairs={{0,8},{1,9},{2,10},{3,11},{4,12},{5,13},{6,14},{7,15},{8,0},{9,1},... | collective-permute-start | bytes 294920 | tf_op jit(solution)/shard_map/ppermute | solution.py:276
  78.5 2.0 %collective-permute-start.31 = (bf16[2,48,512]{2,1,0:T(8,128)(2,1)S(1)}, bf16[2,48,512]{2,1,0:T(8,128)(2,1)S(1)}, u32[]{:S(2)}, u32[]{:S(2)}) collective-permute-start(bf16[2,48,512]{2,1,0:T(8,128)(2,1)S(1)} %get-tuple-element.105), channel_id=1, source_target_pairs={{0,7},{1,6},{2,5},{3,4},{4,3},{5,2},{6,1},{7,0},{8,15},{9,14},{10,... | collective-permute-start | bytes 294920 | tf_op jit(solution)/shard_map/ppermute | solution.py:276
  82.5 6.5 %collective-permute-start.34 = (bf16[2,48,512]{2,1,0:T(8,128)(2,1)S(1)}, bf16[2,48,512]{2,1,0:T(8,128)(2,1)S(1)}, u32[]{:S(2)}, u32[]{:S(2)}) collective-permute-start(bf16[2,48,512]{2,1,0:T(8,128)(2,1)S(1)} %get-tuple-element.108), channel_id=1, source_target_pairs={{0,9},{1,8},{2,11},{3,10},{4,13},{5,12},{6,15},{7,14},{8,1},{9,0},... | collective-permute-start | bytes 294920 | tf_op jit(solution)/shard_map/ppermute | solution.py:276
  91.8 4.8 %collective-permute-start.37 = (bf16[2,48,512]{2,1,0:T(8,128)(2,1)S(1)}, bf16[2,48,512]{2,1,0:T(8,128)(2,1)S(1)}, u32[]{:S(2)}, u32[]{:S(2)}) collective-permute-start(bf16[2,48,512]{2,1,0:T(8,128)(2,1)S(1)} %get-tuple-element.111), channel_id=1, source_target_pairs={{0,2},{1,3},{2,0},{3,1},{4,6},{5,7},{6,4},{7,5},{8,10},{9,11},{10,... | collective-permute-start | bytes 294920 | tf_op jit(solution)/shard_map/ppermute | solution.py:276
  96.6 1.9 %collective-permute-start.38 = (bf16[2,48,512]{2,1,0:T(8,128)(2,1)S(1)}, bf16[2,48,512]{2,1,0:T(8,128)(2,1)S(1)}, u32[]{:S(2)}, u32[]{:S(2)}) collective-permute-start(bf16[2,48,512]{2,1,0:T(8,128)(2,1)S(1)} %get-tuple-element.112), channel_id=1, source_target_pairs={{0,10},{1,11},{2,8},{3,9},{4,14},{5,15},{6,12},{7,13},{8,2},{9,3},... | collective-permute-start | bytes 294920 | tf_op jit(solution)/shard_map/ppermute | solution.py:276
  98.7 5.1 %collective-permute-start.40 = (bf16[2,48,512]{2,1,0:T(8,128)(2,1)S(1)}, bf16[2,48,512]{2,1,0:T(8,128)(2,1)S(1)}, u32[]{:S(2)}, u32[]{:S(2)}) collective-permute-start(bf16[2,48,512]{2,1,0:T(8,128)(2,1)S(1)} %get-tuple-element.114), channel_id=1, source_target_pairs={{0,14},{1,15},{2,12},{3,13},{4,10},{5,11},{6,8},{7,9},{8,6},{9,7},... | collective-permute-start | bytes 294920 | tf_op jit(solution)/shard_map/ppermute | solution.py:276
  103.9 2.7 %collective-permute-start.42 = (bf16[2,48,512]{2,1,0:T(8,128)(2,1)S(1)}, bf16[2,48,512]{2,1,0:T(8,128)(2,1)S(1)}, u32[]{:S(2)}, u32[]{:S(2)}) collective-permute-start(bf16[2,48,512]{2,1,0:T(8,128)(2,1)S(1)} %get-tuple-element.116), channel_id=1, source_target_pairs={{0,11},{1,10},{2,9},{3,8},{4,15},{5,14},{6,13},{7,12},{8,3},{9,2},... | collective-permute-start | bytes 294920 | tf_op jit(solution)/shard_map/ppermute | solution.py:276
  106.6 3.7 %collective-permute-done.38.refs_25_ = bf16[2,48,512]{2,1,0:T(8,128)(2,1)S(1)} collective-permute-done((bf16[2,48,512]{2,1,0:T(8,128)(2,1)S(1)}, bf16[2,48,512]{2,1,0:T(8,128)(2,1)S(1)}, u32[]{:S(2)}, u32[]{:S(2)}) %collective-permute-start.38) | collective-permute-done | bytes 98336 | tf_op jit(solution)/shard_map/ppermute | solution.py:276
  110.3 4.1 %collective-permute-done.42.refs_29_ = bf16[2,48,512]{2,1,0:T(8,128)(2,1)S(1)} collective-permute-done((bf16[2,48,512]{2,1,0:T(8,128)(2,1)S(1)}, bf16[2,48,512]{2,1,0:T(8,128)(2,1)S(1)}, u32[]{:S(2)}, u32[]{:S(2)}) %collective-permute-start.42) | collective-permute-done | bytes 98336 | tf_op jit(solution)/shard_map/ppermute | solution.py:276
  114.4 1.9 %collective-permute-done.43.refs_30_ = bf16[2,48,512]{2,1,0:T(8,128)(2,1)S(1)} collective-permute-done((bf16[2,48,512]{2,1,0:T(8,128)(2,1)S(1)}, bf16[2,48,512]{2,1,0:T(8,128)(2,1)S(1)}, u32[]{:S(2)}, u32[]{:S(2)}) %collective-permute-start.43) | collective-permute-done | bytes 98336 | tf_op jit(solution)/shard_map/ppermute | solution.py:276
  118.1 4.7 %update.1 = (bf16[384,1024]{1,0:T(8,128)(2,1)}, bf16[384,1024]{1,0:T(8,128)(2,1)}, bf16[32,1024]{1,0:T(8,128)(2,1)S(1)}, bf16[32,1024]{1,0:T(8,128)(2,1)S(1)}, b...) custom-call(s32[1]{0:T(128)} %bitcast.me_ref, ...), custom_call_target="tpu_custom_call" | custom-call | flops 2239758336 | bytes 6029312 | tf_op jit(solution)/shard_map/update/pallas_call | solution.py:213
  122.8 3.7 %collective-permute-start.45 = (bf16[32,1024]{1,0:T(8,128)(2,1)S(1)}, bf16[32,1024]{1,0:T(8,128)(2,1)S(1)}, u32[]{:S(2)}, u32[]{:S(2)}) collective-permute-start(bf16[32,1024]{1,0:T(8,128)(2,1)S(1)} %get-tuple-element.124), channel_id=1, source_target_pairs={{0,8},{1,9},{2,10},{3,11},{4,12},{5,13},{6,14},{7,15},{8,0},{9,1},... | collective-permute-start | bytes 196616 | tf_op jit(solution)/shard_map/ppermute | solution.py:276
  136.0 2.0 %collective-permute-start.54 = (bf16[32,1024]{1,0:T(8,128)(2,1)S(1)}, bf16[32,1024]{1,0:T(8,128)(2,1)S(1)}, u32[]{:S(2)}, u32[]{:S(2)}) collective-permute-start(bf16[32,1024]{1,0:T(8,128)(2,1)S(1)} %get-tuple-element.133), channel_id=1, source_target_pairs={{0,5},{1,4},{2,7},{3,6},{4,1},{5,0},{6,3},{7,2},{8,13},{9,12},{10,... | collective-permute-start | bytes 196616 | tf_op jit(solution)/shard_map/ppermute | solution.py:276
  140.8 2.6 %collective-permute-done.53.refs_9_ = bf16[32,1024]{1,0:T(8,128)(2,1)S(1)} collective-permute-done((bf16[32,1024]{1,0:T(8,128)(2,1)S(1)}, bf16[32,1024]{1,0:T(8,128)(2,1)S(1)}, u32[]{:S(2)}, u32[]{:S(2)}) %collective-permute-start.53) | collective-permute-done | bytes 65568 | tf_op jit(solution)/shard_map/ppermute | solution.py:276
  146.0 2.5 %collective-permute-done.57.refs_13_ = bf16[32,1024]{1,0:T(8,128)(2,1)S(1)} collective-permute-done((bf16[32,1024]{1,0:T(8,128)(2,1)S(1)}, bf16[32,1024]{1,0:T(8,128)(2,1)S(1)}, u32[]{:S(2)}, u32[]{:S(2)}) %collective-permute-start.57) | collective-permute-done | bytes 65568 | tf_op jit(solution)/shard_map/ppermute | solution.py:276
  148.9 2.4 %collective-permute-done.59.refs_15_ = bf16[32,1024]{1,0:T(8,128)(2,1)S(1)} collective-permute-done((bf16[32,1024]{1,0:T(8,128)(2,1)S(1)}, bf16[32,1024]{1,0:T(8,128)(2,1)S(1)}, u32[]{:S(2)}, u32[]{:S(2)}) %collective-permute-start.59) | collective-permute-done | bytes 65568 | tf_op jit(solution)/shard_map/ppermute | solution.py:276
  (109 shorter events, 40.7 us)
Async XLA Ops:
  3.9 9.6 %collective-permute-start.16 = (bf16[2,48,512]{2,1,0:T(8,128)(2,1)}, bf16[2,48,512]{2,1,0:T(8,128)(2,1)S(1)}, u32[]{:S(2)}, u32[]{:S(2)}) collective-permute-start(bf16[2,48,512]{2,1,0:T(8,128)(2,1)} %get-tuple-element.89), channel_id=1, source_target_pairs={{0,8},{1,9},{2,10},{3,11},{4,12},{5,13},{6,14},{7,15},{8,0},{9,1},... | collective-permute-start | bytes 294920 | tf_op jit(solution)/shard_map/ppermute | solution.py:276
  10.3 13.5 %collective-permute-start.20 = (bf16[2,48,512]{2,1,0:T(8,128)(2,1)}, bf16[2,48,512]{2,1,0:T(8,128)(2,1)S(1)}, u32[]{:S(2)}, u32[]{:S(2)}) collective-permute-start(bf16[2,48,512]{2,1,0:T(8,128)(2,1)} %get-tuple-element.93), channel_id=1, source_target_pairs={{0,9},{1,8},{2,11},{3,10},{4,13},{5,12},{6,15},{7,14},{8,1},{9,0},... | collective-permute-start | bytes 294920 | tf_op jit(solution)/shard_map/ppermute | solution.py:276
  13.5 10.8 %collective-permute-start.21 = (bf16[2,48,512]{2,1,0:T(8,128)(2,1)}, bf16[2,48,512]{2,1,0:T(8,128)(2,1)S(1)}, u32[]{:S(2)}, u32[]{:S(2)}) collective-permute-start(bf16[2,48,512]{2,1,0:T(8,128)(2,1)} %get-tuple-element.94), channel_id=1, source_target_pairs={{0,6},{1,7},{2,4},{3,5},{4,2},{5,3},{6,0},{7,1},{8,14},{9,15},{10,... | collective-permute-start | bytes 294920 | tf_op jit(solution)/shard_map/ppermute | solution.py:276
  15.4 12.8 %collective-permute-start.22 = (bf16[2,48,512]{2,1,0:T(8,128)(2,1)}, bf16[2,48,512]{2,1,0:T(8,128)(2,1)S(1)}, u32[]{:S(2)}, u32[]{:S(2)}) collective-permute-start(bf16[2,48,512]{2,1,0:T(8,128)(2,1)} %get-tuple-element.95), channel_id=1, source_target_pairs={{0,13},{1,12},{2,15},{3,14},{4,9},{5,8},{6,11},{7,10},{8,5},{9,4},... | collective-permute-start | bytes 294920 | tf_op jit(solution)/shard_map/ppermute | solution.py:276
  17.6 13.6 %collective-permute-start.23 = (bf16[2,48,512]{2,1,0:T(8,128)(2,1)}, bf16[2,48,512]{2,1,0:T(8,128)(2,1)S(1)}, u32[]{:S(2)}, u32[]{:S(2)}) collective-permute-start(bf16[2,48,512]{2,1,0:T(8,128)(2,1)} %get-tuple-element.96), channel_id=1, source_target_pairs={{0,2},{1,3},{2,0},{3,1},{4,6},{5,7},{6,4},{7,5},{8,10},{9,11},{10,... | collective-permute-start | bytes 294920 | tf_op jit(solution)/shard_map/ppermute | solution.py:276
  18.7 13.5 %collective-permute-start.24 = (bf16[2,48,512]{2,1,0:T(8,128)(2,1)}, bf16[2,48,512]{2,1,0:T(8,128)(2,1)S(1)}, u32[]{:S(2)}, u32[]{:S(2)}) collective-permute-start(bf16[2,48,512]{2,1,0:T(8,128)(2,1)} %get-tuple-element.97), channel_id=1, source_target_pairs={{0,10},{1,11},{2,8},{3,9},{4,14},{5,15},{6,12},{7,13},{8,2},{9,3},... | collective-permute-start | bytes 294920 | tf_op jit(solution)/shard_map/ppermute | solution.py:276
  23.8 16.8 %collective-permute-start.25 = (bf16[2,48,512]{2,1,0:T(8,128)(2,1)}, bf16[2,48,512]{2,1,0:T(8,128)(2,1)S(1)}, u32[]{:S(2)}, u32[]{:S(2)}) collective-permute-start(bf16[2,48,512]{2,1,0:T(8,128)(2,1)} %get-tuple-element.98), channel_id=1, source_target_pairs={{0,5},{1,4},{2,7},{3,6},{4,1},{5,0},{6,3},{7,2},{8,13},{9,12},{10,... | collective-permute-start | bytes 294920 | tf_op jit(solution)/shard_map/ppermute | solution.py:276
  24.4 16.3 %collective-permute-start.26 = (bf16[2,48,512]{2,1,0:T(8,128)(2,1)}, bf16[2,48,512]{2,1,0:T(8,128)(2,1)S(1)}, u32[]{:S(2)}, u32[]{:S(2)}) collective-permute-start(bf16[2,48,512]{2,1,0:T(8,128)(2,1)} %get-tuple-element.99), channel_id=1, source_target_pairs={{0,14},{1,15},{2,12},{3,13},{4,10},{5,11},{6,8},{7,9},{8,6},{9,7},... | collective-permute-start | bytes 294920 | tf_op jit(solution)/shard_map/ppermute | solution.py:276
  28.3 13.0 %collective-permute-start.27 = (bf16[2,48,512]{2,1,0:T(8,128)(2,1)}, bf16[2,48,512]{2,1,0:T(8,128)(2,1)S(1)}, u32[]{:S(2)}, u32[]{:S(2)}) collective-permute-start(bf16[2,48,512]{2,1,0:T(8,128)(2,1)} %get-tuple-element.100), channel_id=1, source_target_pairs={{0,11},{1,10},{2,9},{3,8},{4,15},{5,14},{6,13},{7,12},{8,3},{9,2},... | collective-permute-start | bytes 294920 | tf_op jit(solution)/shard_map/ppermute | solution.py:276
  31.2 16.7 %collective-permute-start.28 = (bf16[2,48,512]{2,1,0:T(8,128)(2,1)}, bf16[2,48,512]{2,1,0:T(8,128)(2,1)S(1)}, u32[]{:S(2)}, u32[]{:S(2)}) collective-permute-start(bf16[2,48,512]{2,1,0:T(8,128)(2,1)} %get-tuple-element.101), channel_id=1, source_target_pairs={{0,4},{1,5},{2,6},{3,7},{4,0},{5,1},{6,2},{7,3},{8,12},{9,13},{10,... | collective-permute-start | bytes 294920 | tf_op jit(solution)/shard_map/ppermute | solution.py:276
  32.2 15.7 %collective-permute-start.29 = (bf16[2,48,512]{2,1,0:T(8,128)(2,1)}, bf16[2,48,512]{2,1,0:T(8,128)(2,1)S(1)}, u32[]{:S(2)}, u32[]{:S(2)}) collective-permute-start(bf16[2,48,512]{2,1,0:T(8,128)(2,1)} %get-tuple-element.102), channel_id=1, source_target_pairs={{0,15},{1,14},{2,13},{3,12},{4,11},{5,10},{6,9},{7,8},{8,7},{9,6},... | collective-permute-start | bytes 294920 | tf_op jit(solution)/shard_map/ppermute | solution.py:276
  41.3 13.1 %collective-permute-start.3 = (bf16[32,1792]{1,0:T(8,128)(2,1)S(1)}, bf16[32,1792]{1,0:T(8,128)(2,1)S(1)}, u32[]{:S(2)}, u32[]{:S(2)}) collective-permute-start(bf16[32,1792]{1,0:T(8,128)(2,1)S(1)} %get-tuple-element.75), channel_id=1, source_target_pairs={{0,12},{1,13},{2,14},{3,15},{4,8},{5,9},{6,10},{7,11},{8,4},{9,5},... | collective-permute-start | bytes 344072 | tf_op jit(solution)/shard_map/ppermute | solution.py:276
  47.8 12.1 %collective-permute-start.5 = (bf16[32,1792]{1,0:T(8,128)(2,1)S(1)}, bf16[32,1792]{1,0:T(8,128)(2,1)S(1)}, u32[]{:S(2)}, u32[]{:S(2)}) collective-permute-start(bf16[32,1792]{1,0:T(8,128)(2,1)S(1)} %get-tuple-element.77), channel_id=1, source_target_pairs={{0,9},{1,8},{2,11},{3,10},{4,13},{5,12},{6,15},{7,14},{8,1},{9,0},... | collective-permute-start | bytes 344072 | tf_op jit(solution)/shard_map/ppermute | solution.py:276
  48.9 11.6 %collective-permute-start.6 = (bf16[32,1792]{1,0:T(8,128)(2,1)S(1)}, bf16[32,1792]{1,0:T(8,128)(2,1)S(1)}, u32[]{:S(2)}, u32[]{:S(2)}) collective-permute-start(bf16[32,1792]{1,0:T(8,128)(2,1)S(1)} %get-tuple-element.78), channel_id=1, source_target_pairs={{0,6},{1,7},{2,4},{3,5},{4,2},{5,3},{6,0},{7,1},{8,14},{9,15},{10,... | collective-permute-start | bytes 344072 | tf_op jit(solution)/shard_map/ppermute | solution.py:276
  49.7 13.6 %collective-permute-start.7 = (bf16[32,1792]{1,0:T(8,128)(2,1)S(1)}, bf16[32,1792]{1,0:T(8,128)(2,1)S(1)}, u32[]{:S(2)}, u32[]{:S(2)}) collective-permute-start(bf16[32,1792]{1,0:T(8,128)(2,1)S(1)} %get-tuple-element.79), channel_id=1, source_target_pairs={{0,13},{1,12},{2,15},{3,14},{4,9},{5,8},{6,11},{7,10},{8,5},{9,4},... | collective-permute-start | bytes 344072 | tf_op jit(solution)/shard_map/ppermute | solution.py:276
  54.4 12.2 %collective-permute-start.8 = (bf16[32,1792]{1,0:T(8,128)(2,1)S(1)}, bf16[32,1792]{1,0:T(8,128)(2,1)S(1)}, u32[]{:S(2)}, u32[]{:S(2)}) collective-permute-start(bf16[32,1792]{1,0:T(8,128)(2,1)S(1)} %get-tuple-element.80), channel_id=1, source_target_pairs={{0,2},{1,3},{2,0},{3,1},{4,6},{5,7},{6,4},{7,5},{8,10},{9,11},{10,... | collective-permute-start | bytes 344072 | tf_op jit(solution)/shard_map/ppermute | solution.py:276
  55.9 19.0 %collective-permute-start.9 = (bf16[32,1792]{1,0:T(8,128)(2,1)S(1)}, bf16[32,1792]{1,0:T(8,128)(2,1)S(1)}, u32[]{:S(2)}, u32[]{:S(2)}) collective-permute-start(bf16[32,1792]{1,0:T(8,128)(2,1)S(1)} %get-tuple-element.81), channel_id=1, source_target_pairs={{0,10},{1,11},{2,8},{3,9},{4,14},{5,15},{6,12},{7,13},{8,2},{9,3},... | collective-permute-start | bytes 344072 | tf_op jit(solution)/shard_map/ppermute | solution.py:276
  60.0 14.9 %collective-permute-start.10 = (bf16[32,1792]{1,0:T(8,128)(2,1)S(1)}, bf16[32,1792]{1,0:T(8,128)(2,1)S(1)}, u32[]{:S(2)}, u32[]{:S(2)}) collective-permute-start(bf16[32,1792]{1,0:T(8,128)(2,1)S(1)} %get-tuple-element.82), channel_id=1, source_target_pairs={{0,5},{1,4},{2,7},{3,6},{4,1},{5,0},{6,3},{7,2},{8,13},{9,12},{10,... | collective-permute-start | bytes 344072 | tf_op jit(solution)/shard_map/ppermute | solution.py:276
  60.5 15.3 %collective-permute-start.11 = (bf16[32,1792]{1,0:T(8,128)(2,1)S(1)}, bf16[32,1792]{1,0:T(8,128)(2,1)S(1)}, u32[]{:S(2)}, u32[]{:S(2)}) collective-permute-start(bf16[32,1792]{1,0:T(8,128)(2,1)S(1)} %get-tuple-element.83), channel_id=1, source_target_pairs={{0,14},{1,15},{2,12},{3,13},{4,10},{5,11},{6,8},{7,9},{8,6},{9,7},... | collective-permute-start | bytes 344072 | tf_op jit(solution)/shard_map/ppermute | solution.py:276
  63.2 15.2 %collective-permute-start.12 = (bf16[32,1792]{1,0:T(8,128)(2,1)S(1)}, bf16[32,1792]{1,0:T(8,128)(2,1)S(1)}, u32[]{:S(2)}, u32[]{:S(2)}) collective-permute-start(bf16[32,1792]{1,0:T(8,128)(2,1)S(1)} %get-tuple-element.84), channel_id=1, source_target_pairs={{0,1},{1,0},{2,3},{3,2},{4,5},{5,4},{6,7},{7,6},{8,9},{9,8},{10,11... | collective-permute-start | bytes 344072 | tf_op jit(solution)/shard_map/ppermute | solution.py:276
  66.6 14.0 %collective-permute-start.13 = (bf16[32,1792]{1,0:T(8,128)(2,1)S(1)}, bf16[32,1792]{1,0:T(8,128)(2,1)S(1)}, u32[]{:S(2)}, u32[]{:S(2)}) collective-permute-start(bf16[32,1792]{1,0:T(8,128)(2,1)S(1)} %get-tuple-element.85), channel_id=1, source_target_pairs={{0,11},{1,10},{2,9},{3,8},{4,15},{5,14},{6,13},{7,12},{8,3},{9,2},... | collective-permute-start | bytes 344072 | tf_op jit(solution)/shard_map/ppermute | solution.py:276
  75.8 14.5 %collective-permute-start.30 = (bf16[2,48,512]{2,1,0:T(8,128)(2,1)S(1)}, bf16[2,48,512]{2,1,0:T(8,128)(2,1)S(1)}, u32[]{:S(2)}, u32[]{:S(2)}) collective-permute-start(bf16[2,48,512]{2,1,0:T(8,128)(2,1)S(1)} %get-tuple-element.104), channel_id=1, source_target_pairs={{0,8},{1,9},{2,10},{3,11},{4,12},{5,13},{6,14},{7,15},{8,0},{9,1},... | collective-permute-start | bytes 294920 | tf_op jit(solution)/shard_map/ppermute | solution.py:276
  78.5 12.8 %collective-permute-start.31 = (bf16[2,48,512]{2,1,0:T(8,128)(2,1)S(1)}, bf16[2,48,512]{2,1,0:T(8,128)(2,1)S(1)}, u32[]{:S(2)}, u32[]{:S(2)}) collective-permute-start(bf16[2,48,512]{2,1,0:T(8,128)(2,1)S(1)} %get-tuple-element.105), channel_id=1, source_target_pairs={{0,7},{1,6},{2,5},{3,4},{4,3},{5,2},{6,1},{7,0},{8,15},{9,14},{10,... | collective-permute-start | bytes 294920 | tf_op jit(solution)/shard_map/ppermute | solution.py:276
  80.6 11.2 %collective-permute-start.32 = (bf16[2,48,512]{2,1,0:T(8,128)(2,1)S(1)}, bf16[2,48,512]{2,1,0:T(8,128)(2,1)S(1)}, u32[]{:S(2)}, u32[]{:S(2)}) collective-permute-start(bf16[2,48,512]{2,1,0:T(8,128)(2,1)S(1)} %get-tuple-element.106), channel_id=1, source_target_pairs={{0,12},{1,13},{2,14},{3,15},{4,8},{5,9},{6,10},{7,11},{8,4},{9,5},... | collective-permute-start | bytes 294920 | tf_op jit(solution)/shard_map/ppermute | solution.py:276
  82.5 14.1 %collective-permute-start.33 = (bf16[2,48,512]{2,1,0:T(8,128)(2,1)S(1)}, bf16[2,48,512]{2,1,0:T(8,128)(2,1)S(1)}, u32[]{:S(2)}, u32[]{:S(2)}) collective-permute-start(bf16[2,48,512]{2,1,0:T(8,128)(2,1)S(1)} %get-tuple-element.107), channel_id=1, source_target_pairs={{0,3},{1,2},{2,1},{3,0},{4,7},{5,6},{6,5},{7,4},{8,11},{9,10},{10,... | collective-permute-start | bytes 294920 | tf_op jit(solution)/shard_map/ppermute | solution.py:276
  82.5 16.0 %collective-permute-start.34 = (bf16[2,48,512]{2,1,0:T(8,128)(2,1)S(1)}, bf16[2,48,512]{2,1,0:T(8,128)(2,1)S(1)}, u32[]{:S(2)}, u32[]{:S(2)}) collective-permute-start(bf16[2,48,512]{2,1,0:T(8,128)(2,1)S(1)} %get-tuple-element.108), channel_id=1, source_target_pairs={{0,9},{1,8},{2,11},{3,10},{4,13},{5,12},{6,15},{7,14},{8,1},{9,0},... | collective-permute-start | bytes 294920 | tf_op jit(solution)/shard_map/ppermute | solution.py:276
  91.3 12.6 %collective-permute-start.36 = (bf16[2,48,512]{2,1,0:T(8,128)(2,1)S(1)}, bf16[2,48,512]{2,1,0:T(8,128)(2,1)S(1)}, u32[]{:S(2)}, u32[]{:S(2)}) collective-permute-start(bf16[2,48,512]{2,1,0:T(8,128)(2,1)S(1)} %get-tuple-element.110), channel_id=1, source_target_pairs={{0,13},{1,12},{2,15},{3,14},{4,9},{5,8},{6,11},{7,10},{8,5},{9,4},... | collective-permute-start | bytes 294920 | tf_op jit(solution)/shard_map/ppermute | solution.py:276
  91.8 12.1 %collective-permute-start.37 = (bf16[2,48,512]{2,1,0:T(8,128)(2,1)S(1)}, bf16[2,48,512]{2,1,0:T(8,128)(2,1)S(1)}, u32[]{:S(2)}, u32[]{:S(2)}) collective-permute-start(bf16[2,48,512]{2,1,0:T(8,128)(2,1)S(1)} %get-tuple-element.111), channel_id=1, source_target_pairs={{0,2},{1,3},{2,0},{3,1},{4,6},{5,7},{6,4},{7,5},{8,10},{9,11},{10,... | collective-permute-start | bytes 294920 | tf_op jit(solution)/shard_map/ppermute | solution.py:276
  96.6 13.7 %collective-permute-start.38 = (bf16[2,48,512]{2,1,0:T(8,128)(2,1)S(1)}, bf16[2,48,512]{2,1,0:T(8,128)(2,1)S(1)}, u32[]{:S(2)}, u32[]{:S(2)}) collective-permute-start(bf16[2,48,512]{2,1,0:T(8,128)(2,1)S(1)} %get-tuple-element.112), channel_id=1, source_target_pairs={{0,10},{1,11},{2,8},{3,9},{4,14},{5,15},{6,12},{7,13},{8,2},{9,3},... | collective-permute-start | bytes 294920 | tf_op jit(solution)/shard_map/ppermute | solution.py:276
  98.5 11.8 %collective-permute-start.39 = (bf16[2,48,512]{2,1,0:T(8,128)(2,1)S(1)}, bf16[2,48,512]{2,1,0:T(8,128)(2,1)S(1)}, u32[]{:S(2)}, u32[]{:S(2)}) collective-permute-start(bf16[2,48,512]{2,1,0:T(8,128)(2,1)S(1)} %get-tuple-element.113), channel_id=1, source_target_pairs={{0,5},{1,4},{2,7},{3,6},{4,1},{5,0},{6,3},{7,2},{8,13},{9,12},{10,... | collective-permute-start | bytes 294920 | tf_op jit(solution)/shard_map/ppermute | solution.py:276
  98.7 11.6 %collective-permute-start.40 = (bf16[2,48,512]{2,1,0:T(8,128)(2,1)S(1)}, bf16[2,48,512]{2,1,0:T(8,128)(2,1)S(1)}, u32[]{:S(2)}, u32[]{:S(2)}) collective-permute-start(bf16[2,48,512]{2,1,0:T(8,128)(2,1)S(1)} %get-tuple-element.114), channel_id=1, source_target_pairs={{0,14},{1,15},{2,12},{3,13},{4,10},{5,11},{6,8},{7,9},{8,6},{9,7},... | collective-permute-start | bytes 294920 | tf_op jit(solution)/shard_map/ppermute | solution.py:276
  103.9 10.5 %collective-permute-start.42 = (bf16[2,48,512]{2,1,0:T(8,128)(2,1)S(1)}, bf16[2,48,512]{2,1,0:T(8,128)(2,1)S(1)}, u32[]{:S(2)}, u32[]{:S(2)}) collective-permute-start(bf16[2,48,512]{2,1,0:T(8,128)(2,1)S(1)} %get-tuple-element.116), channel_id=1, source_target_pairs={{0,11},{1,10},{2,9},{3,8},{4,15},{5,14},{6,13},{7,12},{8,3},{9,2},... | collective-permute-start | bytes 294920 | tf_op jit(solution)/shard_map/ppermute | solution.py:276
  (36 other events, 393.4 us)

commit v23 on v22

--- a/solution.py
+++ b/solution.py
@@ -287,7 +287,7 @@
     spread = swap(split(me, w_moment, w_down, groups))
     packed, fwd_slot, gates = pack_rows(
         live_rows, me, perm, grad_route, fwd_route, grad_hidden, grad_out, fwd_hidden, fwd_gate,
-        spread[mixed_order(groups).index(1)], groups, capacity,
+        spread[mixed_order(groups).index(groups // 4)], groups, capacity,
     )
     received = swap(packed)
     placed = swap(reorder(me, perm, spread, received[groups // 3]))

time: 153 us -> 149 us (0.974)
  waiting for transfers between devices: 36.8 us -> 21.8 us
  starting transfers between devices: 101 us -> 113 us
    ppermute x60, waiting for transfers between devices: 36.8 us -> 21.8 us  [swap(): lax.ppermute(piece, 'expert', [(i, i ^ s) for i in range(groups)])]
    ppermute x60, starting transfers between devices: 101 us -> 113 us  [swap(): lax.ppermute(piece, 'expert', [(i, i ^ s) for i in range(groups)])]
  transfers between devices with their start and end apart: 60 -> 60, of which waited for: 23 -> 14; matrix products, arithmetic and copies ran while one was open for 0% -> 0% of each run, Pallas kernels for 2% -> 2%
where the time goes in v23:
time: 149 us
  starting transfers between devices  113 us (76%)
  waiting for transfers between devices  21.8 us (15%)
  Pallas kernels  12.3 us (8%)
  between operations  1.51 us (1%)
    ppermute x60, starting transfers between devices, swap(): lax.ppermute(piece, 'expert', [(i, i ^ s) for i in range(groups)])  113 us
    ppermute x60, waiting for transfers between devices, swap(): lax.ppermute(piece, 'expert', [(i, i ^ s) for i in range(groups)])  21.8 us
    pallas_call x1, Pallas kernels, update(): pl.pallas_call(functools.partial(update_kernel, groups), out_shape=(shape...  4.74 us
  transfers between devices with their start and end apart: 60, of which 14 were waited for; matrix products, arithmetic and copies ran while one was open for 0% of the time, Pallas kernels for 2%

profile of v23, /device:TPU:0, one launch (start us, length us, event | category | flops | bytes accessed | tf_op | source)
XLA Modules:
  0.0 148.9 jit_solution(13991344885218416483)
XLA Ops:
  0.7 2.7 %split.1 = (bf16[2,48,512]{2,1,0:T(8,128)(2,1)}, bf16[2,48,512]{2,1,0:T(8,128)(2,1)}, bf16[2,48,512]{2,1,0:T(8,128)(2,1)}, bf16[2,48,512]{2,1,0:T(8,128)(2,1)}, ...) custom-call(s32[1]{0:T(128)} %bitcast.me_ref, ...), custom_call_target="tpu_custom_call" | custom-call | bytes 3145728 | tf_op jit(solution)/shard_map/split/pallas_call | solution.py:135
  3.4 3.1 %collective-permute-start = (bf16[2,48,512]{2,1,0:T(8,128)(2,1)}, bf16[2,48,512]{2,1,0:T(8,128)(2,1)S(1)}, u32[]{:S(2)}, u32[]{:S(2)}) collective-permute-start(bf16[2,48,512]{2,1,0:T(8,128)(2,1)} %get-tuple-element.71), channel_id=1, source_target_pairs={{0,4},{1,5},{2,6},{3,7},{4,0},{5,1},{6,2},{7,3},{8,12},{9,13},{10,... | collective-permute-start | bytes 294920 | tf_op jit(solution)/shard_map/ppermute | solution.py:276
  6.5 2.6 %collective-permute-start.16 = (bf16[2,48,512]{2,1,0:T(8,128)(2,1)}, bf16[2,48,512]{2,1,0:T(8,128)(2,1)S(1)}, u32[]{:S(2)}, u32[]{:S(2)}) collective-permute-start(bf16[2,48,512]{2,1,0:T(8,128)(2,1)} %get-tuple-element.89), channel_id=1, source_target_pairs={{0,8},{1,9},{2,10},{3,11},{4,12},{5,13},{6,14},{7,15},{8,0},{9,1},... | collective-permute-start | bytes 294920 | tf_op jit(solution)/shard_map/ppermute | solution.py:276
  13.5 3.0 %collective-permute-start.21 = (bf16[2,48,512]{2,1,0:T(8,128)(2,1)}, bf16[2,48,512]{2,1,0:T(8,128)(2,1)S(1)}, u32[]{:S(2)}, u32[]{:S(2)}) collective-permute-start(bf16[2,48,512]{2,1,0:T(8,128)(2,1)} %get-tuple-element.94), channel_id=1, source_target_pairs={{0,6},{1,7},{2,4},{3,5},{4,2},{5,3},{6,0},{7,1},{8,14},{9,15},{10,... | collective-permute-start | bytes 294920 | tf_op jit(solution)/shard_map/ppermute | solution.py:276
  16.5 3.5 %collective-permute-start.22 = (bf16[2,48,512]{2,1,0:T(8,128)(2,1)}, bf16[2,48,512]{2,1,0:T(8,128)(2,1)S(1)}, u32[]{:S(2)}, u32[]{:S(2)}) collective-permute-start(bf16[2,48,512]{2,1,0:T(8,128)(2,1)} %get-tuple-element.95), channel_id=1, source_target_pairs={{0,13},{1,12},{2,15},{3,14},{4,9},{5,8},{6,11},{7,10},{8,5},{9,4},... | collective-permute-start | bytes 294920 | tf_op jit(solution)/shard_map/ppermute | solution.py:276
  20.7 3.3 %collective-permute-start.24 = (bf16[2,48,512]{2,1,0:T(8,128)(2,1)}, bf16[2,48,512]{2,1,0:T(8,128)(2,1)S(1)}, u32[]{:S(2)}, u32[]{:S(2)}) collective-permute-start(bf16[2,48,512]{2,1,0:T(8,128)(2,1)} %get-tuple-element.97), channel_id=1, source_target_pairs={{0,10},{1,11},{2,8},{3,9},{4,14},{5,15},{6,12},{7,13},{8,2},{9,3},... | collective-permute-start | bytes 294920 | tf_op jit(solution)/shard_map/ppermute | solution.py:276
  25.0 3.3 %collective-permute-start.26 = (bf16[2,48,512]{2,1,0:T(8,128)(2,1)}, bf16[2,48,512]{2,1,0:T(8,128)(2,1)S(1)}, u32[]{:S(2)}, u32[]{:S(2)}) collective-permute-start(bf16[2,48,512]{2,1,0:T(8,128)(2,1)} %get-tuple-element.99), channel_id=1, source_target_pairs={{0,14},{1,15},{2,12},{3,13},{4,10},{5,11},{6,8},{7,9},{8,6},{9,7},... | collective-permute-start | bytes 294920 | tf_op jit(solution)/shard_map/ppermute | solution.py:276
  29.4 2.4 %collective-permute-start.28 = (bf16[2,48,512]{2,1,0:T(8,128)(2,1)}, bf16[2,48,512]{2,1,0:T(8,128)(2,1)S(1)}, u32[]{:S(2)}, u32[]{:S(2)}) collective-permute-start(bf16[2,48,512]{2,1,0:T(8,128)(2,1)} %get-tuple-element.101), channel_id=1, source_target_pairs={{0,11},{1,10},{2,9},{3,8},{4,15},{5,14},{6,13},{7,12},{8,3},{9,2},... | collective-permute-start | bytes 294920 | tf_op jit(solution)/shard_map/ppermute | solution.py:276
  34.8 2.8 %pack_rows.1 = (bf16[32,1792]{1,0:T(8,128)(2,1)S(1)}, bf16[32,1792]{1,0:T(8,128)(2,1)S(1)}, bf16[32,1792]{1,0:T(8,128)(2,1)S(1)}, bf16[32,1792]{1,0:T(8,128)(2,1...) custom-call(s32[1]{0:T(128)S(6)} %copy.13.live_ref, ...), custom_call_target="tpu_custom_call" | custom-call | flops 469762048 | bytes 2752512 | tf_op jit(solution)/shard_map/pack_rows/pallas_call | solution.py:107
  37.7 3.4 %collective-permute-start.2 = (bf16[32,1792]{1,0:T(8,128)(2,1)S(1)}, bf16[32,1792]{1,0:T(8,128)(2,1)S(1)}, u32[]{:S(2)}, u32[]{:S(2)}) collective-permute-start(bf16[32,1792]{1,0:T(8,128)(2,1)S(1)} %get-tuple-element.74), channel_id=1, source_target_pairs={{0,7},{1,6},{2,5},{3,4},{4,3},{5,2},{6,1},{7,0},{8,15},{9,14},{10,... | collective-permute-start | bytes 344072 | tf_op jit(solution)/shard_map/ppermute | solution.py:276
  41.1 7.2 %collective-permute-start.3 = (bf16[32,1792]{1,0:T(8,128)(2,1)S(1)}, bf16[32,1792]{1,0:T(8,128)(2,1)S(1)}, u32[]{:S(2)}, u32[]{:S(2)}) collective-permute-start(bf16[32,1792]{1,0:T(8,128)(2,1)S(1)} %get-tuple-element.75), channel_id=1, source_target_pairs={{0,12},{1,13},{2,14},{3,15},{4,8},{5,9},{6,10},{7,11},{8,4},{9,5},... | collective-permute-start | bytes 344072 | tf_op jit(solution)/shard_map/ppermute | solution.py:276
  50.0 4.7 %collective-permute-start.6 = (bf16[32,1792]{1,0:T(8,128)(2,1)S(1)}, bf16[32,1792]{1,0:T(8,128)(2,1)S(1)}, u32[]{:S(2)}, u32[]{:S(2)}) collective-permute-start(bf16[32,1792]{1,0:T(8,128)(2,1)S(1)} %get-tuple-element.78), channel_id=1, source_target_pairs={{0,6},{1,7},{2,4},{3,5},{4,2},{5,3},{6,0},{7,1},{8,14},{9,15},{10,... | collective-permute-start | bytes 344072 | tf_op jit(solution)/shard_map/ppermute | solution.py:276
  56.0 4.4 %collective-permute-start.9 = (bf16[32,1792]{1,0:T(8,128)(2,1)S(1)}, bf16[32,1792]{1,0:T(8,128)(2,1)S(1)}, u32[]{:S(2)}, u32[]{:S(2)}) collective-permute-start(bf16[32,1792]{1,0:T(8,128)(2,1)S(1)} %get-tuple-element.81), channel_id=1, source_target_pairs={{0,10},{1,11},{2,8},{3,9},{4,14},{5,15},{6,12},{7,13},{8,2},{9,3},... | collective-permute-start | bytes 344072 | tf_op jit(solution)/shard_map/ppermute | solution.py:276
  60.4 5.4 %collective-permute-start.11 = (bf16[32,1792]{1,0:T(8,128)(2,1)S(1)}, bf16[32,1792]{1,0:T(8,128)(2,1)S(1)}, u32[]{:S(2)}, u32[]{:S(2)}) collective-permute-start(bf16[32,1792]{1,0:T(8,128)(2,1)S(1)} %get-tuple-element.83), channel_id=1, source_target_pairs={{0,14},{1,15},{2,12},{3,13},{4,10},{5,11},{6,8},{7,9},{8,6},{9,7},... | collective-permute-start | bytes 344072 | tf_op jit(solution)/shard_map/ppermute | solution.py:276
  65.8 2.9 %collective-permute-start.13 = (bf16[32,1792]{1,0:T(8,128)(2,1)S(1)}, bf16[32,1792]{1,0:T(8,128)(2,1)S(1)}, u32[]{:S(2)}, u32[]{:S(2)}) collective-permute-start(bf16[32,1792]{1,0:T(8,128)(2,1)S(1)} %get-tuple-element.85), channel_id=1, source_target_pairs={{0,11},{1,10},{2,9},{3,8},{4,15},{5,14},{6,13},{7,12},{8,3},{9,2},... | collective-permute-start | bytes 344072 | tf_op jit(solution)/shard_map/ppermute | solution.py:276
  68.7 6.9 %collective-permute-start.15 = (bf16[32,1792]{1,0:T(8,128)(2,1)S(1)}, bf16[32,1792]{1,0:T(8,128)(2,1)S(1)}, u32[]{:S(2)}, u32[]{:S(2)}) collective-permute-start(bf16[32,1792]{1,0:T(8,128)(2,1)S(1)} %get-tuple-element.87), channel_id=1, source_target_pairs={{0,15},{1,14},{2,13},{3,12},{4,11},{5,10},{6,9},{7,8},{8,7},{9,6},... | collective-permute-start | bytes 344072 | tf_op jit(solution)/shard_map/ppermute | solution.py:276
  76.4 2.5 %collective-permute-start.30 = (bf16[2,48,512]{2,1,0:T(8,128)(2,1)S(1)}, bf16[2,48,512]{2,1,0:T(8,128)(2,1)S(1)}, u32[]{:S(2)}, u32[]{:S(2)}) collective-permute-start(bf16[2,48,512]{2,1,0:T(8,128)(2,1)S(1)} %get-tuple-element.104), channel_id=1, source_target_pairs={{0,8},{1,9},{2,10},{3,11},{4,12},{5,13},{6,14},{7,15},{8,0},{9,1},... | collective-permute-start | bytes 294920 | tf_op jit(solution)/shard_map/ppermute | solution.py:276
  80.3 2.6 %collective-permute-start.32 = (bf16[2,48,512]{2,1,0:T(8,128)(2,1)S(1)}, bf16[2,48,512]{2,1,0:T(8,128)(2,1)S(1)}, u32[]{:S(2)}, u32[]{:S(2)}) collective-permute-start(bf16[2,48,512]{2,1,0:T(8,128)(2,1)S(1)} %get-tuple-element.106), channel_id=1, source_target_pairs={{0,12},{1,13},{2,14},{3,15},{4,8},{5,9},{6,10},{7,11},{8,4},{9,5},... | collective-permute-start | bytes 294920 | tf_op jit(solution)/shard_map/ppermute | solution.py:276
  82.9 4.9 %collective-permute-start.34 = (bf16[2,48,512]{2,1,0:T(8,128)(2,1)S(1)}, bf16[2,48,512]{2,1,0:T(8,128)(2,1)S(1)}, u32[]{:S(2)}, u32[]{:S(2)}) collective-permute-start(bf16[2,48,512]{2,1,0:T(8,128)(2,1)S(1)} %get-tuple-element.108), channel_id=1, source_target_pairs={{0,9},{1,8},{2,11},{3,10},{4,13},{5,12},{6,15},{7,14},{8,1},{9,0},... | collective-permute-start | bytes 294920 | tf_op jit(solution)/shard_map/ppermute | solution.py:276
  87.8 2.9 %collective-permute-done.30.refs_17_ = bf16[2,48,512]{2,1,0:T(8,128)(2,1)S(1)} collective-permute-done((bf16[2,48,512]{2,1,0:T(8,128)(2,1)S(1)}, bf16[2,48,512]{2,1,0:T(8,128)(2,1)S(1)}, u32[]{:S(2)}, u32[]{:S(2)}) %collective-permute-start.30) | collective-permute-done | bytes 98336 | tf_op jit(solution)/shard_map/ppermute | solution.py:276
  92.8 4.1 %collective-permute-start.38 = (bf16[2,48,512]{2,1,0:T(8,128)(2,1)S(1)}, bf16[2,48,512]{2,1,0:T(8,128)(2,1)S(1)}, u32[]{:S(2)}, u32[]{:S(2)}) collective-permute-start(bf16[2,48,512]{2,1,0:T(8,128)(2,1)S(1)} %get-tuple-element.112), channel_id=1, source_target_pairs={{0,10},{1,11},{2,8},{3,9},{4,14},{5,15},{6,12},{7,13},{8,2},{9,3},... | collective-permute-start | bytes 294920 | tf_op jit(solution)/shard_map/ppermute | solution.py:276
  97.4 2.3 %collective-permute-done.35.refs_22_ = bf16[2,48,512]{2,1,0:T(8,128)(2,1)S(1)} collective-permute-done((bf16[2,48,512]{2,1,0:T(8,128)(2,1)S(1)}, bf16[2,48,512]{2,1,0:T(8,128)(2,1)S(1)}, u32[]{:S(2)}, u32[]{:S(2)}) %collective-permute-start.35) | collective-permute-done | bytes 98336 | tf_op jit(solution)/shard_map/ppermute | solution.py:276
  99.7 2.7 %collective-permute-start.40 = (bf16[2,48,512]{2,1,0:T(8,128)(2,1)S(1)}, bf16[2,48,512]{2,1,0:T(8,128)(2,1)S(1)}, u32[]{:S(2)}, u32[]{:S(2)}) collective-permute-start(bf16[2,48,512]{2,1,0:T(8,128)(2,1)S(1)} %get-tuple-element.114), channel_id=1, source_target_pairs={{0,14},{1,15},{2,12},{3,13},{4,10},{5,11},{6,8},{7,9},{8,6},{9,7},... | collective-permute-start | bytes 294920 | tf_op jit(solution)/shard_map/ppermute | solution.py:276
  102.4 2.2 %collective-permute-start.42 = (bf16[2,48,512]{2,1,0:T(8,128)(2,1)S(1)}, bf16[2,48,512]{2,1,0:T(8,128)(2,1)S(1)}, u32[]{:S(2)}, u32[]{:S(2)}) collective-permute-start(bf16[2,48,512]{2,1,0:T(8,128)(2,1)S(1)} %get-tuple-element.116), channel_id=1, source_target_pairs={{0,11},{1,10},{2,9},{3,8},{4,15},{5,14},{6,13},{7,12},{8,3},{9,2},... | collective-permute-start | bytes 294920 | tf_op jit(solution)/shard_map/ppermute | solution.py:276
  105.2 5.0 %collective-permute-start.44 = (bf16[2,48,512]{2,1,0:T(8,128)(2,1)S(1)}, bf16[2,48,512]{2,1,0:T(8,128)(2,1)S(1)}, u32[]{:S(2)}, u32[]{:S(2)}) collective-permute-start(bf16[2,48,512]{2,1,0:T(8,128)(2,1)S(1)} %get-tuple-element.118), channel_id=1, source_target_pairs={{0,15},{1,14},{2,13},{3,12},{4,11},{5,10},{6,9},{7,8},{8,7},{9,6},... | collective-permute-start | bytes 294920 | tf_op jit(solution)/shard_map/ppermute | solution.py:276
  110.2 5.3 %collective-permute-done.42.refs_29_ = bf16[2,48,512]{2,1,0:T(8,128)(2,1)S(1)} collective-permute-done((bf16[2,48,512]{2,1,0:T(8,128)(2,1)S(1)}, bf16[2,48,512]{2,1,0:T(8,128)(2,1)S(1)}, u32[]{:S(2)}, u32[]{:S(2)}) %collective-permute-start.42) | collective-permute-done | bytes 98336 | tf_op jit(solution)/shard_map/ppermute | solution.py:276
  115.5 4.7 %update.1 = (bf16[384,1024]{1,0:T(8,128)(2,1)}, bf16[384,1024]{1,0:T(8,128)(2,1)}, bf16[32,1024]{1,0:T(8,128)(2,1)S(1)}, bf16[32,1024]{1,0:T(8,128)(2,1)S(1)}, b...) custom-call(s32[1]{0:T(128)} %bitcast.me_ref, ...), custom_call_target="tpu_custom_call" | custom-call | flops 2239758336 | bytes 6029312 | tf_op jit(solution)/shard_map/update/pallas_call | solution.py:213
  120.2 3.8 %collective-permute-start.45 = (bf16[32,1024]{1,0:T(8,128)(2,1)S(1)}, bf16[32,1024]{1,0:T(8,128)(2,1)S(1)}, u32[]{:S(2)}, u32[]{:S(2)}) collective-permute-start(bf16[32,1024]{1,0:T(8,128)(2,1)S(1)} %get-tuple-element.124), channel_id=1, source_target_pairs={{0,8},{1,9},{2,10},{3,11},{4,12},{5,13},{6,14},{7,15},{8,0},{9,1},... | collective-permute-start | bytes 196616 | tf_op jit(solution)/shard_map/ppermute | solution.py:276
  131.6 2.3 %collective-permute-start.53 = (bf16[32,1024]{1,0:T(8,128)(2,1)S(1)}, bf16[32,1024]{1,0:T(8,128)(2,1)S(1)}, u32[]{:S(2)}, u32[]{:S(2)}) collective-permute-start(bf16[32,1024]{1,0:T(8,128)(2,1)S(1)} %get-tuple-element.132), channel_id=1, source_target_pairs={{0,10},{1,11},{2,8},{3,9},{4,14},{5,15},{6,12},{7,13},{8,2},{9,3},... | collective-permute-start | bytes 196616 | tf_op jit(solution)/shard_map/ppermute | solution.py:276
  134.7 3.2 %collective-permute-start.55 = (bf16[32,1024]{1,0:T(8,128)(2,1)S(1)}, bf16[32,1024]{1,0:T(8,128)(2,1)S(1)}, u32[]{:S(2)}, u32[]{:S(2)}) collective-permute-start(bf16[32,1024]{1,0:T(8,128)(2,1)S(1)} %get-tuple-element.134), channel_id=1, source_target_pairs={{0,14},{1,15},{2,12},{3,13},{4,10},{5,11},{6,8},{7,9},{8,6},{9,7},... | collective-permute-start | bytes 196616 | tf_op jit(solution)/shard_map/ppermute | solution.py:276
  140.7 1.9 %collective-permute-start.59 = (bf16[32,1024]{1,0:T(8,128)(2,1)S(1)}, bf16[32,1024]{1,0:T(8,128)(2,1)S(1)}, u32[]{:S(2)}, u32[]{:S(2)}) collective-permute-start(bf16[32,1024]{1,0:T(8,128)(2,1)S(1)} %get-tuple-element.138), channel_id=1, source_target_pairs={{0,15},{1,14},{2,13},{3,12},{4,11},{5,10},{6,9},{7,8},{8,7},{9,6},... | collective-permute-start | bytes 196616 | tf_op jit(solution)/shard_map/ppermute | solution.py:276
  142.7 3.1 %collective-permute-done.57.refs_13_ = bf16[32,1024]{1,0:T(8,128)(2,1)S(1)} collective-permute-done((bf16[32,1024]{1,0:T(8,128)(2,1)S(1)}, bf16[32,1024]{1,0:T(8,128)(2,1)S(1)}, u32[]{:S(2)}, u32[]{:S(2)}) %collective-permute-start.57) | collective-permute-done | bytes 65568 | tf_op jit(solution)/shard_map/ppermute | solution.py:276
  (109 shorter events, 32.4 us)
Async XLA Ops:
  9.3 10.6 %collective-permute-start.18 = (bf16[2,48,512]{2,1,0:T(8,128)(2,1)}, bf16[2,48,512]{2,1,0:T(8,128)(2,1)S(1)}, u32[]{:S(2)}, u32[]{:S(2)}) collective-permute-start(bf16[2,48,512]{2,1,0:T(8,128)(2,1)} %get-tuple-element.91), channel_id=1, source_target_pairs={{0,12},{1,13},{2,14},{3,15},{4,8},{5,9},{6,10},{7,11},{8,4},{9,5},... | collective-permute-start | bytes 294920 | tf_op jit(solution)/shard_map/ppermute | solution.py:276
  11.8 13.2 %collective-permute-start.20 = (bf16[2,48,512]{2,1,0:T(8,128)(2,1)}, bf16[2,48,512]{2,1,0:T(8,128)(2,1)S(1)}, u32[]{:S(2)}, u32[]{:S(2)}) collective-permute-start(bf16[2,48,512]{2,1,0:T(8,128)(2,1)} %get-tuple-element.93), channel_id=1, source_target_pairs={{0,9},{1,8},{2,11},{3,10},{4,13},{5,12},{6,15},{7,14},{8,1},{9,0},... | collective-permute-start | bytes 294920 | tf_op jit(solution)/shard_map/ppermute | solution.py:276
  13.5 11.5 %collective-permute-start.21 = (bf16[2,48,512]{2,1,0:T(8,128)(2,1)}, bf16[2,48,512]{2,1,0:T(8,128)(2,1)S(1)}, u32[]{:S(2)}, u32[]{:S(2)}) collective-permute-start(bf16[2,48,512]{2,1,0:T(8,128)(2,1)} %get-tuple-element.94), channel_id=1, source_target_pairs={{0,6},{1,7},{2,4},{3,5},{4,2},{5,3},{6,0},{7,1},{8,14},{9,15},{10,... | collective-permute-start | bytes 294920 | tf_op jit(solution)/shard_map/ppermute | solution.py:276
  16.5 11.8 %collective-permute-start.22 = (bf16[2,48,512]{2,1,0:T(8,128)(2,1)}, bf16[2,48,512]{2,1,0:T(8,128)(2,1)S(1)}, u32[]{:S(2)}, u32[]{:S(2)}) collective-permute-start(bf16[2,48,512]{2,1,0:T(8,128)(2,1)} %get-tuple-element.95), channel_id=1, source_target_pairs={{0,13},{1,12},{2,15},{3,14},{4,9},{5,8},{6,11},{7,10},{8,5},{9,4},... | collective-permute-start | bytes 294920 | tf_op jit(solution)/shard_map/ppermute | solution.py:276
  20.7 11.4 %collective-permute-start.24 = (bf16[2,48,512]{2,1,0:T(8,128)(2,1)}, bf16[2,48,512]{2,1,0:T(8,128)(2,1)S(1)}, u32[]{:S(2)}, u32[]{:S(2)}) collective-permute-start(bf16[2,48,512]{2,1,0:T(8,128)(2,1)} %get-tuple-element.97), channel_id=1, source_target_pairs={{0,10},{1,11},{2,8},{3,9},{4,14},{5,15},{6,12},{7,13},{8,2},{9,3},... | collective-permute-start | bytes 294920 | tf_op jit(solution)/shard_map/ppermute | solution.py:276
  25.0 12.6 %collective-permute-start.25 = (bf16[2,48,512]{2,1,0:T(8,128)(2,1)}, bf16[2,48,512]{2,1,0:T(8,128)(2,1)S(1)}, u32[]{:S(2)}, u32[]{:S(2)}) collective-permute-start(bf16[2,48,512]{2,1,0:T(8,128)(2,1)} %get-tuple-element.98), channel_id=1, source_target_pairs={{0,5},{1,4},{2,7},{3,6},{4,1},{5,0},{6,3},{7,2},{8,13},{9,12},{10,... | collective-permute-start | bytes 294920 | tf_op jit(solution)/shard_map/ppermute | solution.py:276
  25.0 12.7 %collective-permute-start.26 = (bf16[2,48,512]{2,1,0:T(8,128)(2,1)}, bf16[2,48,512]{2,1,0:T(8,128)(2,1)S(1)}, u32[]{:S(2)}, u32[]{:S(2)}) collective-permute-start(bf16[2,48,512]{2,1,0:T(8,128)(2,1)} %get-tuple-element.99), channel_id=1, source_target_pairs={{0,14},{1,15},{2,12},{3,13},{4,10},{5,11},{6,8},{7,9},{8,6},{9,7},... | collective-permute-start | bytes 294920 | tf_op jit(solution)/shard_map/ppermute | solution.py:276
  28.3 12.8 %collective-permute-start.27 = (bf16[2,48,512]{2,1,0:T(8,128)(2,1)}, bf16[2,48,512]{2,1,0:T(8,128)(2,1)S(1)}, u32[]{:S(2)}, u32[]{:S(2)}) collective-permute-start(bf16[2,48,512]{2,1,0:T(8,128)(2,1)} %get-tuple-element.100), channel_id=1, source_target_pairs={{0,1},{1,0},{2,3},{3,2},{4,5},{5,4},{6,7},{7,6},{8,9},{9,8},{10,11... | collective-permute-start | bytes 294920 | tf_op jit(solution)/shard_map/ppermute | solution.py:276
  29.4 18.9 %collective-permute-start.28 = (bf16[2,48,512]{2,1,0:T(8,128)(2,1)}, bf16[2,48,512]{2,1,0:T(8,128)(2,1)S(1)}, u32[]{:S(2)}, u32[]{:S(2)}) collective-permute-start(bf16[2,48,512]{2,1,0:T(8,128)(2,1)} %get-tuple-element.101), channel_id=1, source_target_pairs={{0,11},{1,10},{2,9},{3,8},{4,15},{5,14},{6,13},{7,12},{8,3},{9,2},... | collective-permute-start | bytes 294920 | tf_op jit(solution)/shard_map/ppermute | solution.py:276
  32.1 16.2 %collective-permute-start.29 = (bf16[2,48,512]{2,1,0:T(8,128)(2,1)}, bf16[2,48,512]{2,1,0:T(8,128)(2,1)S(1)}, u32[]{:S(2)}, u32[]{:S(2)}) collective-permute-start(bf16[2,48,512]{2,1,0:T(8,128)(2,1)} %get-tuple-element.102), channel_id=1, source_target_pairs={{0,15},{1,14},{2,13},{3,12},{4,11},{5,10},{6,9},{7,8},{8,7},{9,6},... | collective-permute-start | bytes 294920 | tf_op jit(solution)/shard_map/ppermute | solution.py:276
  37.6 12.3 %collective-permute-start.1 = (bf16[32,1792]{1,0:T(8,128)(2,1)S(1)}, bf16[32,1792]{1,0:T(8,128)(2,1)S(1)}, u32[]{:S(2)}, u32[]{:S(2)}) collective-permute-start(bf16[32,1792]{1,0:T(8,128)(2,1)S(1)} %get-tuple-element.73), channel_id=1, source_target_pairs={{0,8},{1,9},{2,10},{3,11},{4,12},{5,13},{6,14},{7,15},{8,0},{9,1},... | collective-permute-start | bytes 344072 | tf_op jit(solution)/shard_map/ppermute | solution.py:276
  37.7 16.9 %collective-permute-start.2 = (bf16[32,1792]{1,0:T(8,128)(2,1)S(1)}, bf16[32,1792]{1,0:T(8,128)(2,1)S(1)}, u32[]{:S(2)}, u32[]{:S(2)}) collective-permute-start(bf16[32,1792]{1,0:T(8,128)(2,1)S(1)} %get-tuple-element.74), channel_id=1, source_target_pairs={{0,7},{1,6},{2,5},{3,4},{4,3},{5,2},{6,1},{7,0},{8,15},{9,14},{10,... | collective-permute-start | bytes 344072 | tf_op jit(solution)/shard_map/ppermute | solution.py:276
  41.1 14.9 %collective-permute-start.3 = (bf16[32,1792]{1,0:T(8,128)(2,1)S(1)}, bf16[32,1792]{1,0:T(8,128)(2,1)S(1)}, u32[]{:S(2)}, u32[]{:S(2)}) collective-permute-start(bf16[32,1792]{1,0:T(8,128)(2,1)S(1)} %get-tuple-element.75), channel_id=1, source_target_pairs={{0,12},{1,13},{2,14},{3,15},{4,8},{5,9},{6,10},{7,11},{8,4},{9,5},... | collective-permute-start | bytes 344072 | tf_op jit(solution)/shard_map/ppermute | solution.py:276
  48.3 12.1 %collective-permute-start.5 = (bf16[32,1792]{1,0:T(8,128)(2,1)S(1)}, bf16[32,1792]{1,0:T(8,128)(2,1)S(1)}, u32[]{:S(2)}, u32[]{:S(2)}) collective-permute-start(bf16[32,1792]{1,0:T(8,128)(2,1)S(1)} %get-tuple-element.77), channel_id=1, source_target_pairs={{0,9},{1,8},{2,11},{3,10},{4,13},{5,12},{6,15},{7,14},{8,1},{9,0},... | collective-permute-start | bytes 344072 | tf_op jit(solution)/shard_map/ppermute | solution.py:276
  50.0 10.4 %collective-permute-start.6 = (bf16[32,1792]{1,0:T(8,128)(2,1)S(1)}, bf16[32,1792]{1,0:T(8,128)(2,1)S(1)}, u32[]{:S(2)}, u32[]{:S(2)}) collective-permute-start(bf16[32,1792]{1,0:T(8,128)(2,1)S(1)} %get-tuple-element.78), channel_id=1, source_target_pairs={{0,6},{1,7},{2,4},{3,5},{4,2},{5,3},{6,0},{7,1},{8,14},{9,15},{10,... | collective-permute-start | bytes 344072 | tf_op jit(solution)/shard_map/ppermute | solution.py:276
  54.6 11.2 %collective-permute-start.7 = (bf16[32,1792]{1,0:T(8,128)(2,1)S(1)}, bf16[32,1792]{1,0:T(8,128)(2,1)S(1)}, u32[]{:S(2)}, u32[]{:S(2)}) collective-permute-start(bf16[32,1792]{1,0:T(8,128)(2,1)S(1)} %get-tuple-element.79), channel_id=1, source_target_pairs={{0,13},{1,12},{2,15},{3,14},{4,9},{5,8},{6,11},{7,10},{8,5},{9,4},... | collective-permute-start | bytes 344072 | tf_op jit(solution)/shard_map/ppermute | solution.py:276
  56.0 12.7 %collective-permute-start.9 = (bf16[32,1792]{1,0:T(8,128)(2,1)S(1)}, bf16[32,1792]{1,0:T(8,128)(2,1)S(1)}, u32[]{:S(2)}, u32[]{:S(2)}) collective-permute-start(bf16[32,1792]{1,0:T(8,128)(2,1)S(1)} %get-tuple-element.81), channel_id=1, source_target_pairs={{0,10},{1,11},{2,8},{3,9},{4,14},{5,15},{6,12},{7,13},{8,2},{9,3},... | collective-permute-start | bytes 344072 | tf_op jit(solution)/shard_map/ppermute | solution.py:276
  60.4 16.0 %collective-permute-start.11 = (bf16[32,1792]{1,0:T(8,128)(2,1)S(1)}, bf16[32,1792]{1,0:T(8,128)(2,1)S(1)}, u32[]{:S(2)}, u32[]{:S(2)}) collective-permute-start(bf16[32,1792]{1,0:T(8,128)(2,1)S(1)} %get-tuple-element.83), channel_id=1, source_target_pairs={{0,14},{1,15},{2,12},{3,13},{4,10},{5,11},{6,8},{7,9},{8,6},{9,7},... | collective-permute-start | bytes 344072 | tf_op jit(solution)/shard_map/ppermute | solution.py:276
  65.8 13.1 %collective-permute-start.12 = (bf16[32,1792]{1,0:T(8,128)(2,1)S(1)}, bf16[32,1792]{1,0:T(8,128)(2,1)S(1)}, u32[]{:S(2)}, u32[]{:S(2)}) collective-permute-start(bf16[32,1792]{1,0:T(8,128)(2,1)S(1)} %get-tuple-element.84), channel_id=1, source_target_pairs={{0,1},{1,0},{2,3},{3,2},{4,5},{5,4},{6,7},{7,6},{8,9},{9,8},{10,11... | collective-permute-start | bytes 344072 | tf_op jit(solution)/shard_map/ppermute | solution.py:276
  65.8 14.5 %collective-permute-start.13 = (bf16[32,1792]{1,0:T(8,128)(2,1)S(1)}, bf16[32,1792]{1,0:T(8,128)(2,1)S(1)}, u32[]{:S(2)}, u32[]{:S(2)}) collective-permute-start(bf16[32,1792]{1,0:T(8,128)(2,1)S(1)} %get-tuple-element.85), channel_id=1, source_target_pairs={{0,11},{1,10},{2,9},{3,8},{4,15},{5,14},{6,13},{7,12},{8,3},{9,2},... | collective-permute-start | bytes 344072 | tf_op jit(solution)/shard_map/ppermute | solution.py:276
  68.7 14.2 %collective-permute-start.14 = (bf16[32,1792]{1,0:T(8,128)(2,1)S(1)}, bf16[32,1792]{1,0:T(8,128)(2,1)S(1)}, u32[]{:S(2)}, u32[]{:S(2)}) collective-permute-start(bf16[32,1792]{1,0:T(8,128)(2,1)S(1)} %get-tuple-element.86), channel_id=1, source_target_pairs={{0,4},{1,5},{2,6},{3,7},{4,0},{5,1},{6,2},{7,3},{8,12},{9,13},{10,... | collective-permute-start | bytes 344072 | tf_op jit(solution)/shard_map/ppermute | solution.py:276
  68.7 14.2 %collective-permute-start.15 = (bf16[32,1792]{1,0:T(8,128)(2,1)S(1)}, bf16[32,1792]{1,0:T(8,128)(2,1)S(1)}, u32[]{:S(2)}, u32[]{:S(2)}) collective-permute-start(bf16[32,1792]{1,0:T(8,128)(2,1)S(1)} %get-tuple-element.87), channel_id=1, source_target_pairs={{0,15},{1,14},{2,13},{3,12},{4,11},{5,10},{6,9},{7,8},{8,7},{9,6},... | collective-permute-start | bytes 344072 | tf_op jit(solution)/shard_map/ppermute | solution.py:276
  76.4 14.3 %collective-permute-start.30 = (bf16[2,48,512]{2,1,0:T(8,128)(2,1)S(1)}, bf16[2,48,512]{2,1,0:T(8,128)(2,1)S(1)}, u32[]{:S(2)}, u32[]{:S(2)}) collective-permute-start(bf16[2,48,512]{2,1,0:T(8,128)(2,1)S(1)} %get-tuple-element.104), channel_id=1, source_target_pairs={{0,8},{1,9},{2,10},{3,11},{4,12},{5,13},{6,14},{7,15},{8,0},{9,1},... | collective-permute-start | bytes 294920 | tf_op jit(solution)/shard_map/ppermute | solution.py:276
  78.8 11.8 %collective-permute-start.31 = (bf16[2,48,512]{2,1,0:T(8,128)(2,1)S(1)}, bf16[2,48,512]{2,1,0:T(8,128)(2,1)S(1)}, u32[]{:S(2)}, u32[]{:S(2)}) collective-permute-start(bf16[2,48,512]{2,1,0:T(8,128)(2,1)S(1)} %get-tuple-element.105), channel_id=1, source_target_pairs={{0,7},{1,6},{2,5},{3,4},{4,3},{5,2},{6,1},{7,0},{8,15},{9,14},{10,... | collective-permute-start | bytes 294920 | tf_op jit(solution)/shard_map/ppermute | solution.py:276
  80.3 11.5 %collective-permute-start.32 = (bf16[2,48,512]{2,1,0:T(8,128)(2,1)S(1)}, bf16[2,48,512]{2,1,0:T(8,128)(2,1)S(1)}, u32[]{:S(2)}, u32[]{:S(2)}) collective-permute-start(bf16[2,48,512]{2,1,0:T(8,128)(2,1)S(1)} %get-tuple-element.106), channel_id=1, source_target_pairs={{0,12},{1,13},{2,14},{3,15},{4,8},{5,9},{6,10},{7,11},{8,4},{9,5},... | collective-permute-start | bytes 294920 | tf_op jit(solution)/shard_map/ppermute | solution.py:276
  82.9 14.0 %collective-permute-start.34 = (bf16[2,48,512]{2,1,0:T(8,128)(2,1)S(1)}, bf16[2,48,512]{2,1,0:T(8,128)(2,1)S(1)}, u32[]{:S(2)}, u32[]{:S(2)}) collective-permute-start(bf16[2,48,512]{2,1,0:T(8,128)(2,1)S(1)} %get-tuple-element.108), channel_id=1, source_target_pairs={{0,9},{1,8},{2,11},{3,10},{4,13},{5,12},{6,15},{7,14},{8,1},{9,0},... | collective-permute-start | bytes 294920 | tf_op jit(solution)/shard_map/ppermute | solution.py:276
  90.7 11.7 %collective-permute-start.36 = (bf16[2,48,512]{2,1,0:T(8,128)(2,1)S(1)}, bf16[2,48,512]{2,1,0:T(8,128)(2,1)S(1)}, u32[]{:S(2)}, u32[]{:S(2)}) collective-permute-start(bf16[2,48,512]{2,1,0:T(8,128)(2,1)S(1)} %get-tuple-element.110), channel_id=1, source_target_pairs={{0,13},{1,12},{2,15},{3,14},{4,9},{5,8},{6,11},{7,10},{8,5},{9,4},... | collective-permute-start | bytes 294920 | tf_op jit(solution)/shard_map/ppermute | solution.py:276
  91.7 10.7 %collective-permute-start.37 = (bf16[2,48,512]{2,1,0:T(8,128)(2,1)S(1)}, bf16[2,48,512]{2,1,0:T(8,128)(2,1)S(1)}, u32[]{:S(2)}, u32[]{:S(2)}) collective-permute-start(bf16[2,48,512]{2,1,0:T(8,128)(2,1)S(1)} %get-tuple-element.111), channel_id=1, source_target_pairs={{0,2},{1,3},{2,0},{3,1},{4,6},{5,7},{6,4},{7,5},{8,10},{9,11},{10,... | collective-permute-start | bytes 294920 | tf_op jit(solution)/shard_map/ppermute | solution.py:276
  92.8 12.4 %collective-permute-start.38 = (bf16[2,48,512]{2,1,0:T(8,128)(2,1)S(1)}, bf16[2,48,512]{2,1,0:T(8,128)(2,1)S(1)}, u32[]{:S(2)}, u32[]{:S(2)}) collective-permute-start(bf16[2,48,512]{2,1,0:T(8,128)(2,1)S(1)} %get-tuple-element.112), channel_id=1, source_target_pairs={{0,10},{1,11},{2,8},{3,9},{4,14},{5,15},{6,12},{7,13},{8,2},{9,3},... | collective-permute-start | bytes 294920 | tf_op jit(solution)/shard_map/ppermute | solution.py:276
  99.7 10.5 %collective-permute-start.40 = (bf16[2,48,512]{2,1,0:T(8,128)(2,1)S(1)}, bf16[2,48,512]{2,1,0:T(8,128)(2,1)S(1)}, u32[]{:S(2)}, u32[]{:S(2)}) collective-permute-start(bf16[2,48,512]{2,1,0:T(8,128)(2,1)S(1)} %get-tuple-element.114), channel_id=1, source_target_pairs={{0,14},{1,15},{2,12},{3,13},{4,10},{5,11},{6,8},{7,9},{8,6},{9,7},... | collective-permute-start | bytes 294920 | tf_op jit(solution)/shard_map/ppermute | solution.py:276
  102.4 13.0 %collective-permute-start.42 = (bf16[2,48,512]{2,1,0:T(8,128)(2,1)S(1)}, bf16[2,48,512]{2,1,0:T(8,128)(2,1)S(1)}, u32[]{:S(2)}, u32[]{:S(2)}) collective-permute-start(bf16[2,48,512]{2,1,0:T(8,128)(2,1)S(1)} %get-tuple-element.116), channel_id=1, source_target_pairs={{0,11},{1,10},{2,9},{3,8},{4,15},{5,14},{6,13},{7,12},{8,3},{9,2},... | collective-permute-start | bytes 294920 | tf_op jit(solution)/shard_map/ppermute | solution.py:276
  105.2 10.3 %collective-permute-start.43 = (bf16[2,48,512]{2,1,0:T(8,128)(2,1)S(1)}, bf16[2,48,512]{2,1,0:T(8,128)(2,1)S(1)}, u32[]{:S(2)}, u32[]{:S(2)}) collective-permute-start(bf16[2,48,512]{2,1,0:T(8,128)(2,1)S(1)} %get-tuple-element.117), channel_id=1, source_target_pairs={{0,4},{1,5},{2,6},{3,7},{4,0},{5,1},{6,2},{7,3},{8,12},{9,13},{10,... | collective-permute-start | bytes 294920 | tf_op jit(solution)/shard_map/ppermute | solution.py:276
  (36 other events, 389.3 us)

commit v24 on v10

--- a/solution.py
+++ b/solution.py
@@ -172,15 +172,18 @@
 def update_kernel(groups, me_ref, *refs):
     packed, pieces, produced = refs[:groups], refs[groups : 2 * groups], refs[2 * groups + 2 : 3 * groups + 2]
     weight_new_ref, moment_new_ref = refs[2 * groups : 2 * groups + 2]
-    held, rows_ref = refs[-2:]
+    held, weight_held, rows_ref, fwd_ref = refs[-4:]
     _, ff, d = held.shape
     capacity = packed[0].shape[0]
     for n, piece in enumerate(packed):
-        rows_ref[n * capacity : (n + 1) * capacity] = piece[...]
-    for s, piece in zip(mixed_order(groups), pieces):
-        rows, columns = piece.shape[1:]
-        for lead in range(2):
-            chunk_at(held, lead, me_ref[0] ^ s, rows, columns)[...] = piece[lead]
+        rows_ref[n * capacity : (n + 1) * capacity] = piece[:, : ff + d]
+
+    def assemble(lead, target):
+        for s, piece in zip(mixed_order(groups), pieces):
+            rows, columns = piece.shape[1:]
+            chunk_at(target, 0, me_ref[0] ^ s, rows, columns)[...] = piece[lead]
+
+    assemble(0, held)
     grad = lax.dot_general(
         rows_ref[:, :ff], rows_ref[:, ff : ff + d], (((0,), (0,)), ((), ())), preferred_element_type=F32
     )
@@ -189,18 +192,22 @@
     moment_f = moment_new.astype(F32)
     frobenius = jnp.sqrt(jnp.sum(moment_f * moment_f))
     current = (moment_f / (frobenius + norm_floor)).astype(BF16)
-    for _ in range(2):
+    for sweep in range(2):
         gramian = lax.dot_general(
             current, current, (((1,), (1,)), ((), ())), preferred_element_type=F32
         ).astype(BF16)
+        if sweep == 0:
+            assemble(1, weight_held)
+            for n, piece in enumerate(packed):
+                fwd_ref[n * capacity : (n + 1) * capacity] = piece[:, ff + d :]
         squared = jnp.dot(gramian, gramian, preferred_element_type=F32)
         poly = (cubic_term * gramian.astype(F32) + quintic_term * squared).astype(BF16)
         current = (
             linear_term * current.astype(F32) + jnp.dot(poly, current, preferred_element_type=F32)
         ).astype(BF16)
-    weight_new = (held[1].astype(F32) - step_scale * current.astype(F32)).astype(BF16)
+    weight_new = (weight_held[0].astype(F32) - step_scale * current.astype(F32)).astype(BF16)
     weight_new_ref[...] = weight_new
-    product = jnp.dot(rows_ref[:, ff + d :], weight_new, preferred_element_type=F32).astype(BF16)
+    product = jnp.dot(fwd_ref[...], weight_new, preferred_element_type=F32).astype(BF16)
     for n, piece in enumerate(produced):
         piece[...] = product[n * capacity : (n + 1) * capacity]
 
@@ -215,7 +222,12 @@
         out_shape=(shape, shape) + (jax.ShapeDtypeStruct((capacity, d), BF16),) * groups,
         in_specs=[SMEM] + [VMEM] * (2 * groups),
         out_specs=(VMEM,) * (groups + 2),
-        scratch_shapes=[pltpu.VMEM((2, ff, d), BF16), pltpu.VMEM((slots, width), BF16)],
+        scratch_shapes=[
+            pltpu.VMEM((1, ff, d), BF16),
+            pltpu.VMEM((1, ff, d), BF16),
+            pltpu.VMEM((slots, width - ff), BF16),
+            pltpu.VMEM((slots, ff), BF16),
+        ],
         compiler_params=pltpu.CompilerParams(vmem_limit_bytes=40 * MIB),
         cost_estimate=pl.CostEstimate(
             flops=4 * ff * d * slots + 8 * ff * ff * d + 4 * ff**3,

time: 149 us -> 149 us (level)
  no operation moved by 1% of the time
where the time goes in v24:
time: 149 us
  starting transfers between devices  110 us (74%)
  waiting for transfers between devices  24.5 us (16%)
  Pallas kernels  12.5 us (8%)
  between operations  1.49 us (1%)
    ppermute x60, starting transfers between devices, swap(): lax.ppermute(piece, 'expert', [(i, i ^ s) for i in range(groups)])  110 us
    ppermute x60, waiting for transfers between devices, swap(): lax.ppermute(piece, 'expert', [(i, i ^ s) for i in range(groups)])  24.5 us
    pallas_call x1, Pallas kernels, update(): pl.pallas_call(functools.partial(update_kernel, groups), out_shape=(shape...  4.94 us
  transfers between devices with their start and end apart: 60, of which 12 were waited for; matrix products, arithmetic and copies ran while one was open for 0% of the time, Pallas kernels for 2%

profile of v24, /device:TPU:0, one launch (start us, length us, event | category | flops | bytes accessed | tf_op | source)
XLA Modules:
  0.0 149.1 jit_solution(8708864879195716711)
XLA Ops:
  0.7 2.7 %split.1 = (bf16[2,48,512]{2,1,0:T(8,128)(2,1)}, bf16[2,48,512]{2,1,0:T(8,128)(2,1)}, bf16[2,48,512]{2,1,0:T(8,128)(2,1)}, bf16[2,48,512]{2,1,0:T(8,128)(2,1)}, ...) custom-call(s32[1]{0:T(128)} %bitcast.me_ref, ...), custom_call_target="tpu_custom_call" | custom-call | bytes 3145728 | tf_op jit(solution)/shard_map/split/pallas_call | solution.py:135
  3.4 2.5 %collective-permute-start = (bf16[2,48,512]{2,1,0:T(8,128)(2,1)}, bf16[2,48,512]{2,1,0:T(8,128)(2,1)S(1)}, u32[]{:S(2)}, u32[]{:S(2)}) collective-permute-start(bf16[2,48,512]{2,1,0:T(8,128)(2,1)} %get-tuple-element.71), channel_id=1, source_target_pairs={{0,5},{1,4},{2,7},{3,6},{4,1},{5,0},{6,3},{7,2},{8,13},{9,12},{10,... | collective-permute-start | bytes 294920 | tf_op jit(solution)/shard_map/ppermute | solution.py:288
  5.9 2.6 %collective-permute-start.16 = (bf16[2,48,512]{2,1,0:T(8,128)(2,1)}, bf16[2,48,512]{2,1,0:T(8,128)(2,1)S(1)}, u32[]{:S(2)}, u32[]{:S(2)}) collective-permute-start(bf16[2,48,512]{2,1,0:T(8,128)(2,1)} %get-tuple-element.89), channel_id=1, source_target_pairs={{0,8},{1,9},{2,10},{3,11},{4,12},{5,13},{6,14},{7,15},{8,0},{9,1},... | collective-permute-start | bytes 294920 | tf_op jit(solution)/shard_map/ppermute | solution.py:288
  16.1 2.8 %collective-permute-start.22 = (bf16[2,48,512]{2,1,0:T(8,128)(2,1)}, bf16[2,48,512]{2,1,0:T(8,128)(2,1)S(1)}, u32[]{:S(2)}, u32[]{:S(2)}) collective-permute-start(bf16[2,48,512]{2,1,0:T(8,128)(2,1)} %get-tuple-element.95), channel_id=1, source_target_pairs={{0,13},{1,12},{2,15},{3,14},{4,9},{5,8},{6,11},{7,10},{8,5},{9,4},... | collective-permute-start | bytes 294920 | tf_op jit(solution)/shard_map/ppermute | solution.py:288
  20.4 3.9 %collective-permute-start.24 = (bf16[2,48,512]{2,1,0:T(8,128)(2,1)}, bf16[2,48,512]{2,1,0:T(8,128)(2,1)S(1)}, u32[]{:S(2)}, u32[]{:S(2)}) collective-permute-start(bf16[2,48,512]{2,1,0:T(8,128)(2,1)} %get-tuple-element.97), channel_id=1, source_target_pairs={{0,10},{1,11},{2,8},{3,9},{4,14},{5,15},{6,12},{7,13},{8,2},{9,3},... | collective-permute-start | bytes 294920 | tf_op jit(solution)/shard_map/ppermute | solution.py:288
  24.3 3.8 %collective-permute-start.25 = (bf16[2,48,512]{2,1,0:T(8,128)(2,1)}, bf16[2,48,512]{2,1,0:T(8,128)(2,1)S(1)}, u32[]{:S(2)}, u32[]{:S(2)}) collective-permute-start(bf16[2,48,512]{2,1,0:T(8,128)(2,1)} %get-tuple-element.98), channel_id=1, source_target_pairs={{0,14},{1,15},{2,12},{3,13},{4,10},{5,11},{6,8},{7,9},{8,6},{9,7},... | collective-permute-start | bytes 294920 | tf_op jit(solution)/shard_map/ppermute | solution.py:288
  28.5 3.2 %collective-permute-start.27 = (bf16[2,48,512]{2,1,0:T(8,128)(2,1)}, bf16[2,48,512]{2,1,0:T(8,128)(2,1)S(1)}, u32[]{:S(2)}, u32[]{:S(2)}) collective-permute-start(bf16[2,48,512]{2,1,0:T(8,128)(2,1)} %get-tuple-element.100), channel_id=1, source_target_pairs={{0,11},{1,10},{2,9},{3,8},{4,15},{5,14},{6,13},{7,12},{8,3},{9,2},... | collective-permute-start | bytes 294920 | tf_op jit(solution)/shard_map/ppermute | solution.py:288
  31.7 2.8 %collective-permute-done.24.refs_9_ = bf16[2,48,512]{2,1,0:T(8,128)(2,1)S(1)} collective-permute-done((bf16[2,48,512]{2,1,0:T(8,128)(2,1)}, bf16[2,48,512]{2,1,0:T(8,128)(2,1)S(1)}, u32[]{:S(2)}, u32[]{:S(2)}) %collective-permute-start.24) | collective-permute-done | bytes 98336 | tf_op jit(solution)/shard_map/ppermute | solution.py:288
  37.5 2.8 %pack_rows.1 = (bf16[32,1792]{1,0:T(8,128)(2,1)S(1)}, bf16[32,1792]{1,0:T(8,128)(2,1)S(1)}, bf16[32,1792]{1,0:T(8,128)(2,1)S(1)}, bf16[32,1792]{1,0:T(8,128)(2,1...) custom-call(s32[1]{0:T(128)S(6)} %copy.13.live_ref, ...), custom_call_target="tpu_custom_call" | custom-call | flops 469762048 | bytes 2752512 | tf_op jit(solution)/shard_map/pack_rows/pallas_call | solution.py:107
  40.7 2.7 %collective-permute-start.2 = (bf16[32,1792]{1,0:T(8,128)(2,1)S(1)}, bf16[32,1792]{1,0:T(8,128)(2,1)S(1)}, u32[]{:S(2)}, u32[]{:S(2)}) collective-permute-start(bf16[32,1792]{1,0:T(8,128)(2,1)S(1)} %get-tuple-element.74), channel_id=1, source_target_pairs={{0,7},{1,6},{2,5},{3,4},{4,3},{5,2},{6,1},{7,0},{8,15},{9,14},{10,... | collective-permute-start | bytes 344072 | tf_op jit(solution)/shard_map/ppermute | solution.py:288
  43.4 5.0 %collective-permute-start.3 = (bf16[32,1792]{1,0:T(8,128)(2,1)S(1)}, bf16[32,1792]{1,0:T(8,128)(2,1)S(1)}, u32[]{:S(2)}, u32[]{:S(2)}) collective-permute-start(bf16[32,1792]{1,0:T(8,128)(2,1)S(1)} %get-tuple-element.75), channel_id=1, source_target_pairs={{0,12},{1,13},{2,14},{3,15},{4,8},{5,9},{6,10},{7,11},{8,4},{9,5},... | collective-permute-start | bytes 344072 | tf_op jit(solution)/shard_map/ppermute | solution.py:288
  50.4 5.6 %collective-permute-start.7 = (bf16[32,1792]{1,0:T(8,128)(2,1)S(1)}, bf16[32,1792]{1,0:T(8,128)(2,1)S(1)}, u32[]{:S(2)}, u32[]{:S(2)}) collective-permute-start(bf16[32,1792]{1,0:T(8,128)(2,1)S(1)} %get-tuple-element.79), channel_id=1, source_target_pairs={{0,13},{1,12},{2,15},{3,14},{4,9},{5,8},{6,11},{7,10},{8,5},{9,4},... | collective-permute-start | bytes 344072 | tf_op jit(solution)/shard_map/ppermute | solution.py:288
  56.1 4.4 %collective-permute-start.9 = (bf16[32,1792]{1,0:T(8,128)(2,1)S(1)}, bf16[32,1792]{1,0:T(8,128)(2,1)S(1)}, u32[]{:S(2)}, u32[]{:S(2)}) collective-permute-start(bf16[32,1792]{1,0:T(8,128)(2,1)S(1)} %get-tuple-element.81), channel_id=1, source_target_pairs={{0,10},{1,11},{2,8},{3,9},{4,14},{5,15},{6,12},{7,13},{8,2},{9,3},... | collective-permute-start | bytes 344072 | tf_op jit(solution)/shard_map/ppermute | solution.py:288
  60.5 3.8 %collective-permute-start.11 = (bf16[32,1792]{1,0:T(8,128)(2,1)S(1)}, bf16[32,1792]{1,0:T(8,128)(2,1)S(1)}, u32[]{:S(2)}, u32[]{:S(2)}) collective-permute-start(bf16[32,1792]{1,0:T(8,128)(2,1)S(1)} %get-tuple-element.83), channel_id=1, source_target_pairs={{0,14},{1,15},{2,12},{3,13},{4,10},{5,11},{6,8},{7,9},{8,6},{9,7},... | collective-permute-start | bytes 344072 | tf_op jit(solution)/shard_map/ppermute | solution.py:288
  64.6 4.3 %collective-permute-start.13 = (bf16[32,1792]{1,0:T(8,128)(2,1)S(1)}, bf16[32,1792]{1,0:T(8,128)(2,1)S(1)}, u32[]{:S(2)}, u32[]{:S(2)}) collective-permute-start(bf16[32,1792]{1,0:T(8,128)(2,1)S(1)} %get-tuple-element.85), channel_id=1, source_target_pairs={{0,11},{1,10},{2,9},{3,8},{4,15},{5,14},{6,13},{7,12},{8,3},{9,2},... | collective-permute-start | bytes 344072 | tf_op jit(solution)/shard_map/ppermute | solution.py:288
  69.0 2.2 %collective-permute-start.14 = (bf16[32,1792]{1,0:T(8,128)(2,1)S(1)}, bf16[32,1792]{1,0:T(8,128)(2,1)S(1)}, u32[]{:S(2)}, u32[]{:S(2)}) collective-permute-start(bf16[32,1792]{1,0:T(8,128)(2,1)S(1)} %get-tuple-element.86), channel_id=1, source_target_pairs={{0,4},{1,5},{2,6},{3,7},{4,0},{5,1},{6,2},{7,3},{8,12},{9,13},{10,... | collective-permute-start | bytes 344072 | tf_op jit(solution)/shard_map/ppermute | solution.py:288
  71.1 4.6 %collective-permute-start.15 = (bf16[32,1792]{1,0:T(8,128)(2,1)S(1)}, bf16[32,1792]{1,0:T(8,128)(2,1)S(1)}, u32[]{:S(2)}, u32[]{:S(2)}) collective-permute-start(bf16[32,1792]{1,0:T(8,128)(2,1)S(1)} %get-tuple-element.87), channel_id=1, source_target_pairs={{0,15},{1,14},{2,13},{3,12},{4,11},{5,10},{6,9},{7,8},{8,7},{9,6},... | collective-permute-start | bytes 344072 | tf_op jit(solution)/shard_map/ppermute | solution.py:288
  76.5 2.4 %collective-permute-start.30 = (bf16[2,48,512]{2,1,0:T(8,128)(2,1)S(1)}, bf16[2,48,512]{2,1,0:T(8,128)(2,1)S(1)}, u32[]{:S(2)}, u32[]{:S(2)}) collective-permute-start(bf16[2,48,512]{2,1,0:T(8,128)(2,1)S(1)} %get-tuple-element.104), channel_id=1, source_target_pairs={{0,8},{1,9},{2,10},{3,11},{4,12},{5,13},{6,14},{7,15},{8,0},{9,1},... | collective-permute-start | bytes 294920 | tf_op jit(solution)/shard_map/ppermute | solution.py:288
  80.8 2.1 %collective-permute-start.32 = (bf16[2,48,512]{2,1,0:T(8,128)(2,1)S(1)}, bf16[2,48,512]{2,1,0:T(8,128)(2,1)S(1)}, u32[]{:S(2)}, u32[]{:S(2)}) collective-permute-start(bf16[2,48,512]{2,1,0:T(8,128)(2,1)S(1)} %get-tuple-element.106), channel_id=1, source_target_pairs={{0,12},{1,13},{2,14},{3,15},{4,8},{5,9},{6,10},{7,11},{8,4},{9,5},... | collective-permute-start | bytes 294920 | tf_op jit(solution)/shard_map/ppermute | solution.py:288
  82.9 3.5 %collective-permute-start.33 = (bf16[2,48,512]{2,1,0:T(8,128)(2,1)S(1)}, bf16[2,48,512]{2,1,0:T(8,128)(2,1)S(1)}, u32[]{:S(2)}, u32[]{:S(2)}) collective-permute-start(bf16[2,48,512]{2,1,0:T(8,128)(2,1)S(1)} %get-tuple-element.107), channel_id=1, source_target_pairs={{0,3},{1,2},{2,1},{3,0},{4,7},{5,6},{6,5},{7,4},{8,11},{9,10},{10,... | collective-permute-start | bytes 294920 | tf_op jit(solution)/shard_map/ppermute | solution.py:288
  87.7 3.1 %collective-permute-done.30.refs_17_ = bf16[2,48,512]{2,1,0:T(8,128)(2,1)S(1)} collective-permute-done((bf16[2,48,512]{2,1,0:T(8,128)(2,1)S(1)}, bf16[2,48,512]{2,1,0:T(8,128)(2,1)S(1)}, u32[]{:S(2)}, u32[]{:S(2)}) %collective-permute-start.30) | collective-permute-done | bytes 98336 | tf_op jit(solution)/shard_map/ppermute | solution.py:288
  94.0 3.7 %collective-permute-start.38 = (bf16[2,48,512]{2,1,0:T(8,128)(2,1)S(1)}, bf16[2,48,512]{2,1,0:T(8,128)(2,1)S(1)}, u32[]{:S(2)}, u32[]{:S(2)}) collective-permute-start(bf16[2,48,512]{2,1,0:T(8,128)(2,1)S(1)} %get-tuple-element.112), channel_id=1, source_target_pairs={{0,10},{1,11},{2,8},{3,9},{4,14},{5,15},{6,12},{7,13},{8,2},{9,3},... | collective-permute-start | bytes 294920 | tf_op jit(solution)/shard_map/ppermute | solution.py:288
  97.7 2.6 %collective-permute-done.35.refs_22_ = bf16[2,48,512]{2,1,0:T(8,128)(2,1)S(1)} collective-permute-done((bf16[2,48,512]{2,1,0:T(8,128)(2,1)S(1)}, bf16[2,48,512]{2,1,0:T(8,128)(2,1)S(1)}, u32[]{:S(2)}, u32[]{:S(2)}) %collective-permute-start.35) | collective-permute-done | bytes 98336 | tf_op jit(solution)/shard_map/ppermute | solution.py:288
  100.3 2.6 %collective-permute-start.40 = (bf16[2,48,512]{2,1,0:T(8,128)(2,1)S(1)}, bf16[2,48,512]{2,1,0:T(8,128)(2,1)S(1)}, u32[]{:S(2)}, u32[]{:S(2)}) collective-permute-start(bf16[2,48,512]{2,1,0:T(8,128)(2,1)S(1)} %get-tuple-element.114), channel_id=1, source_target_pairs={{0,14},{1,15},{2,12},{3,13},{4,10},{5,11},{6,8},{7,9},{8,6},{9,7},... | collective-permute-start | bytes 294920 | tf_op jit(solution)/shard_map/ppermute | solution.py:288
  102.9 3.0 %collective-permute-start.42 = (bf16[2,48,512]{2,1,0:T(8,128)(2,1)S(1)}, bf16[2,48,512]{2,1,0:T(8,128)(2,1)S(1)}, u32[]{:S(2)}, u32[]{:S(2)}) collective-permute-start(bf16[2,48,512]{2,1,0:T(8,128)(2,1)S(1)} %get-tuple-element.116), channel_id=1, source_target_pairs={{0,11},{1,10},{2,9},{3,8},{4,15},{5,14},{6,13},{7,12},{8,3},{9,2},... | collective-permute-start | bytes 294920 | tf_op jit(solution)/shard_map/ppermute | solution.py:288
  107.8 7.4 %collective-permute-done.42.refs_29_ = bf16[2,48,512]{2,1,0:T(8,128)(2,1)S(1)} collective-permute-done((bf16[2,48,512]{2,1,0:T(8,128)(2,1)S(1)}, bf16[2,48,512]{2,1,0:T(8,128)(2,1)S(1)}, u32[]{:S(2)}, u32[]{:S(2)}) %collective-permute-start.42) | collective-permute-done | bytes 98336 | tf_op jit(solution)/shard_map/ppermute | solution.py:288
  115.1 4.9 %update.1 = (bf16[384,1024]{1,0:T(8,128)(2,1)}, bf16[384,1024]{1,0:T(8,128)(2,1)}, bf16[32,1024]{1,0:T(8,128)(2,1)S(1)}, bf16[32,1024]{1,0:T(8,128)(2,1)S(1)}, b...) custom-call(s32[1]{0:T(128)} %bitcast.me_ref, ...), custom_call_target="tpu_custom_call" | custom-call | flops 2239758336 | bytes 6029312 | tf_op jit(solution)/shard_map/update/pallas_call | solution.py:220
  120.1 3.9 %collective-permute-start.45 = (bf16[32,1024]{1,0:T(8,128)(2,1)S(1)}, bf16[32,1024]{1,0:T(8,128)(2,1)S(1)}, u32[]{:S(2)}, u32[]{:S(2)}) collective-permute-start(bf16[32,1024]{1,0:T(8,128)(2,1)S(1)} %get-tuple-element.124), channel_id=1, source_target_pairs={{0,8},{1,9},{2,10},{3,11},{4,12},{5,13},{6,14},{7,15},{8,0},{9,1},... | collective-permute-start | bytes 196616 | tf_op jit(solution)/shard_map/ppermute | solution.py:288
  126.4 2.1 %collective-permute-start.49 = (bf16[32,1024]{1,0:T(8,128)(2,1)S(1)}, bf16[32,1024]{1,0:T(8,128)(2,1)S(1)}, u32[]{:S(2)}, u32[]{:S(2)}) collective-permute-start(bf16[32,1024]{1,0:T(8,128)(2,1)S(1)} %get-tuple-element.128), channel_id=1, source_target_pairs={{0,9},{1,8},{2,11},{3,10},{4,13},{5,12},{6,15},{7,14},{8,1},{9,0},... | collective-permute-start | bytes 196616 | tf_op jit(solution)/shard_map/ppermute | solution.py:288
  132.3 2.6 %collective-permute-start.53 = (bf16[32,1024]{1,0:T(8,128)(2,1)S(1)}, bf16[32,1024]{1,0:T(8,128)(2,1)S(1)}, u32[]{:S(2)}, u32[]{:S(2)}) collective-permute-start(bf16[32,1024]{1,0:T(8,128)(2,1)S(1)} %get-tuple-element.132), channel_id=1, source_target_pairs={{0,10},{1,11},{2,8},{3,9},{4,14},{5,15},{6,12},{7,13},{8,2},{9,3},... | collective-permute-start | bytes 196616 | tf_op jit(solution)/shard_map/ppermute | solution.py:288
  135.0 3.1 %collective-permute-start.55 = (bf16[32,1024]{1,0:T(8,128)(2,1)S(1)}, bf16[32,1024]{1,0:T(8,128)(2,1)S(1)}, u32[]{:S(2)}, u32[]{:S(2)}) collective-permute-start(bf16[32,1024]{1,0:T(8,128)(2,1)S(1)} %get-tuple-element.134), channel_id=1, source_target_pairs={{0,14},{1,15},{2,12},{3,13},{4,10},{5,11},{6,8},{7,9},{8,6},{9,7},... | collective-permute-start | bytes 196616 | tf_op jit(solution)/shard_map/ppermute | solution.py:288
  142.9 3.0 %collective-permute-done.57.refs_13_ = bf16[32,1024]{1,0:T(8,128)(2,1)S(1)} collective-permute-done((bf16[32,1024]{1,0:T(8,128)(2,1)S(1)}, bf16[32,1024]{1,0:T(8,128)(2,1)S(1)}, u32[]{:S(2)}, u32[]{:S(2)}) %collective-permute-start.57) | collective-permute-done | bytes 65568 | tf_op jit(solution)/shard_map/ppermute | solution.py:288
  (109 shorter events, 37.9 us)
Async XLA Ops:
  11.3 13.0 %collective-permute-start.20 = (bf16[2,48,512]{2,1,0:T(8,128)(2,1)}, bf16[2,48,512]{2,1,0:T(8,128)(2,1)S(1)}, u32[]{:S(2)}, u32[]{:S(2)}) collective-permute-start(bf16[2,48,512]{2,1,0:T(8,128)(2,1)} %get-tuple-element.93), channel_id=1, source_target_pairs={{0,9},{1,8},{2,11},{3,10},{4,13},{5,12},{6,15},{7,14},{8,1},{9,0},... | collective-permute-start | bytes 294920 | tf_op jit(solution)/shard_map/ppermute | solution.py:288
  14.5 13.6 %collective-permute-start.21 = (bf16[2,48,512]{2,1,0:T(8,128)(2,1)}, bf16[2,48,512]{2,1,0:T(8,128)(2,1)S(1)}, u32[]{:S(2)}, u32[]{:S(2)}) collective-permute-start(bf16[2,48,512]{2,1,0:T(8,128)(2,1)} %get-tuple-element.94), channel_id=1, source_target_pairs={{0,6},{1,7},{2,4},{3,5},{4,2},{5,3},{6,0},{7,1},{8,14},{9,15},{10,... | collective-permute-start | bytes 294920 | tf_op jit(solution)/shard_map/ppermute | solution.py:288
  16.1 12.3 %collective-permute-start.22 = (bf16[2,48,512]{2,1,0:T(8,128)(2,1)}, bf16[2,48,512]{2,1,0:T(8,128)(2,1)S(1)}, u32[]{:S(2)}, u32[]{:S(2)}) collective-permute-start(bf16[2,48,512]{2,1,0:T(8,128)(2,1)} %get-tuple-element.95), channel_id=1, source_target_pairs={{0,13},{1,12},{2,15},{3,14},{4,9},{5,8},{6,11},{7,10},{8,5},{9,4},... | collective-permute-start | bytes 294920 | tf_op jit(solution)/shard_map/ppermute | solution.py:288
  18.9 12.7 %collective-permute-start.23 = (bf16[2,48,512]{2,1,0:T(8,128)(2,1)}, bf16[2,48,512]{2,1,0:T(8,128)(2,1)S(1)}, u32[]{:S(2)}, u32[]{:S(2)}) collective-permute-start(bf16[2,48,512]{2,1,0:T(8,128)(2,1)} %get-tuple-element.96), channel_id=1, source_target_pairs={{0,2},{1,3},{2,0},{3,1},{4,6},{5,7},{6,4},{7,5},{8,10},{9,11},{10,... | collective-permute-start | bytes 294920 | tf_op jit(solution)/shard_map/ppermute | solution.py:288
  20.4 14.1 %collective-permute-start.24 = (bf16[2,48,512]{2,1,0:T(8,128)(2,1)}, bf16[2,48,512]{2,1,0:T(8,128)(2,1)S(1)}, u32[]{:S(2)}, u32[]{:S(2)}) collective-permute-start(bf16[2,48,512]{2,1,0:T(8,128)(2,1)} %get-tuple-element.97), channel_id=1, source_target_pairs={{0,10},{1,11},{2,8},{3,9},{4,14},{5,15},{6,12},{7,13},{8,2},{9,3},... | collective-permute-start | bytes 294920 | tf_op jit(solution)/shard_map/ppermute | solution.py:288
  24.3 16.0 %collective-permute-start.25 = (bf16[2,48,512]{2,1,0:T(8,128)(2,1)}, bf16[2,48,512]{2,1,0:T(8,128)(2,1)S(1)}, u32[]{:S(2)}, u32[]{:S(2)}) collective-permute-start(bf16[2,48,512]{2,1,0:T(8,128)(2,1)} %get-tuple-element.98), channel_id=1, source_target_pairs={{0,14},{1,15},{2,12},{3,13},{4,10},{5,11},{6,8},{7,9},{8,6},{9,7},... | collective-permute-start | bytes 294920 | tf_op jit(solution)/shard_map/ppermute | solution.py:288
  28.1 12.6 %collective-permute-start.26 = (bf16[2,48,512]{2,1,0:T(8,128)(2,1)}, bf16[2,48,512]{2,1,0:T(8,128)(2,1)S(1)}, u32[]{:S(2)}, u32[]{:S(2)}) collective-permute-start(bf16[2,48,512]{2,1,0:T(8,128)(2,1)} %get-tuple-element.99), channel_id=1, source_target_pairs={{0,1},{1,0},{2,3},{3,2},{4,5},{5,4},{6,7},{7,6},{8,9},{9,8},{10,11... | collective-permute-start | bytes 294920 | tf_op jit(solution)/shard_map/ppermute | solution.py:288
  28.5 14.9 %collective-permute-start.27 = (bf16[2,48,512]{2,1,0:T(8,128)(2,1)}, bf16[2,48,512]{2,1,0:T(8,128)(2,1)S(1)}, u32[]{:S(2)}, u32[]{:S(2)}) collective-permute-start(bf16[2,48,512]{2,1,0:T(8,128)(2,1)} %get-tuple-element.100), channel_id=1, source_target_pairs={{0,11},{1,10},{2,9},{3,8},{4,15},{5,14},{6,13},{7,12},{8,3},{9,2},... | collective-permute-start | bytes 294920 | tf_op jit(solution)/shard_map/ppermute | solution.py:288
  31.7 16.8 %collective-permute-start.28 = (bf16[2,48,512]{2,1,0:T(8,128)(2,1)}, bf16[2,48,512]{2,1,0:T(8,128)(2,1)S(1)}, u32[]{:S(2)}, u32[]{:S(2)}) collective-permute-start(bf16[2,48,512]{2,1,0:T(8,128)(2,1)} %get-tuple-element.101), channel_id=1, source_target_pairs={{0,4},{1,5},{2,6},{3,7},{4,0},{5,1},{6,2},{7,3},{8,12},{9,13},{10,... | collective-permute-start | bytes 294920 | tf_op jit(solution)/shard_map/ppermute | solution.py:288
  34.4 14.0 %collective-permute-start.29 = (bf16[2,48,512]{2,1,0:T(8,128)(2,1)}, bf16[2,48,512]{2,1,0:T(8,128)(2,1)S(1)}, u32[]{:S(2)}, u32[]{:S(2)}) collective-permute-start(bf16[2,48,512]{2,1,0:T(8,128)(2,1)} %get-tuple-element.102), channel_id=1, source_target_pairs={{0,15},{1,14},{2,13},{3,12},{4,11},{5,10},{6,9},{7,8},{8,7},{9,6},... | collective-permute-start | bytes 294920 | tf_op jit(solution)/shard_map/ppermute | solution.py:288
  40.7 9.8 %collective-permute-start.2 = (bf16[32,1792]{1,0:T(8,128)(2,1)S(1)}, bf16[32,1792]{1,0:T(8,128)(2,1)S(1)}, u32[]{:S(2)}, u32[]{:S(2)}) collective-permute-start(bf16[32,1792]{1,0:T(8,128)(2,1)S(1)} %get-tuple-element.74), channel_id=1, source_target_pairs={{0,7},{1,6},{2,5},{3,4},{4,3},{5,2},{6,1},{7,0},{8,15},{9,14},{10,... | collective-permute-start | bytes 344072 | tf_op jit(solution)/shard_map/ppermute | solution.py:288
  43.4 12.7 %collective-permute-start.3 = (bf16[32,1792]{1,0:T(8,128)(2,1)S(1)}, bf16[32,1792]{1,0:T(8,128)(2,1)S(1)}, u32[]{:S(2)}, u32[]{:S(2)}) collective-permute-start(bf16[32,1792]{1,0:T(8,128)(2,1)S(1)} %get-tuple-element.75), channel_id=1, source_target_pairs={{0,12},{1,13},{2,14},{3,15},{4,8},{5,9},{6,10},{7,11},{8,4},{9,5},... | collective-permute-start | bytes 344072 | tf_op jit(solution)/shard_map/ppermute | solution.py:288
  48.4 12.1 %collective-permute-start.5 = (bf16[32,1792]{1,0:T(8,128)(2,1)S(1)}, bf16[32,1792]{1,0:T(8,128)(2,1)S(1)}, u32[]{:S(2)}, u32[]{:S(2)}) collective-permute-start(bf16[32,1792]{1,0:T(8,128)(2,1)S(1)} %get-tuple-element.77), channel_id=1, source_target_pairs={{0,9},{1,8},{2,11},{3,10},{4,13},{5,12},{6,15},{7,14},{8,1},{9,0},... | collective-permute-start | bytes 344072 | tf_op jit(solution)/shard_map/ppermute | solution.py:288
  49.0 11.5 %collective-permute-start.6 = (bf16[32,1792]{1,0:T(8,128)(2,1)S(1)}, bf16[32,1792]{1,0:T(8,128)(2,1)S(1)}, u32[]{:S(2)}, u32[]{:S(2)}) collective-permute-start(bf16[32,1792]{1,0:T(8,128)(2,1)S(1)} %get-tuple-element.78), channel_id=1, source_target_pairs={{0,6},{1,7},{2,4},{3,5},{4,2},{5,3},{6,0},{7,1},{8,14},{9,15},{10,... | collective-permute-start | bytes 344072 | tf_op jit(solution)/shard_map/ppermute | solution.py:288
  50.4 13.8 %collective-permute-start.7 = (bf16[32,1792]{1,0:T(8,128)(2,1)S(1)}, bf16[32,1792]{1,0:T(8,128)(2,1)S(1)}, u32[]{:S(2)}, u32[]{:S(2)}) collective-permute-start(bf16[32,1792]{1,0:T(8,128)(2,1)S(1)} %get-tuple-element.79), channel_id=1, source_target_pairs={{0,13},{1,12},{2,15},{3,14},{4,9},{5,8},{6,11},{7,10},{8,5},{9,4},... | collective-permute-start | bytes 344072 | tf_op jit(solution)/shard_map/ppermute | solution.py:288
  56.1 12.9 %collective-permute-start.9 = (bf16[32,1792]{1,0:T(8,128)(2,1)S(1)}, bf16[32,1792]{1,0:T(8,128)(2,1)S(1)}, u32[]{:S(2)}, u32[]{:S(2)}) collective-permute-start(bf16[32,1792]{1,0:T(8,128)(2,1)S(1)} %get-tuple-element.81), channel_id=1, source_target_pairs={{0,10},{1,11},{2,8},{3,9},{4,14},{5,15},{6,12},{7,13},{8,2},{9,3},... | collective-permute-start | bytes 344072 | tf_op jit(solution)/shard_map/ppermute | solution.py:288
  60.5 10.6 %collective-permute-start.10 = (bf16[32,1792]{1,0:T(8,128)(2,1)S(1)}, bf16[32,1792]{1,0:T(8,128)(2,1)S(1)}, u32[]{:S(2)}, u32[]{:S(2)}) collective-permute-start(bf16[32,1792]{1,0:T(8,128)(2,1)S(1)} %get-tuple-element.82), channel_id=1, source_target_pairs={{0,5},{1,4},{2,7},{3,6},{4,1},{5,0},{6,3},{7,2},{8,13},{9,12},{10,... | collective-permute-start | bytes 344072 | tf_op jit(solution)/shard_map/ppermute | solution.py:288
  60.5 16.0 %collective-permute-start.11 = (bf16[32,1792]{1,0:T(8,128)(2,1)S(1)}, bf16[32,1792]{1,0:T(8,128)(2,1)S(1)}, u32[]{:S(2)}, u32[]{:S(2)}) collective-permute-start(bf16[32,1792]{1,0:T(8,128)(2,1)S(1)} %get-tuple-element.83), channel_id=1, source_target_pairs={{0,14},{1,15},{2,12},{3,13},{4,10},{5,11},{6,8},{7,9},{8,6},{9,7},... | collective-permute-start | bytes 344072 | tf_op jit(solution)/shard_map/ppermute | solution.py:288
  64.3 14.7 %collective-permute-start.12 = (bf16[32,1792]{1,0:T(8,128)(2,1)S(1)}, bf16[32,1792]{1,0:T(8,128)(2,1)S(1)}, u32[]{:S(2)}, u32[]{:S(2)}) collective-permute-start(bf16[32,1792]{1,0:T(8,128)(2,1)S(1)} %get-tuple-element.84), channel_id=1, source_target_pairs={{0,1},{1,0},{2,3},{3,2},{4,5},{5,4},{6,7},{7,6},{8,9},{9,8},{10,11... | collective-permute-start | bytes 344072 | tf_op jit(solution)/shard_map/ppermute | solution.py:288
  64.6 16.2 %collective-permute-start.13 = (bf16[32,1792]{1,0:T(8,128)(2,1)S(1)}, bf16[32,1792]{1,0:T(8,128)(2,1)S(1)}, u32[]{:S(2)}, u32[]{:S(2)}) collective-permute-start(bf16[32,1792]{1,0:T(8,128)(2,1)S(1)} %get-tuple-element.85), channel_id=1, source_target_pairs={{0,11},{1,10},{2,9},{3,8},{4,15},{5,14},{6,13},{7,12},{8,3},{9,2},... | collective-permute-start | bytes 344072 | tf_op jit(solution)/shard_map/ppermute | solution.py:288
  69.0 14.0 %collective-permute-start.14 = (bf16[32,1792]{1,0:T(8,128)(2,1)S(1)}, bf16[32,1792]{1,0:T(8,128)(2,1)S(1)}, u32[]{:S(2)}, u32[]{:S(2)}) collective-permute-start(bf16[32,1792]{1,0:T(8,128)(2,1)S(1)} %get-tuple-element.86), channel_id=1, source_target_pairs={{0,4},{1,5},{2,6},{3,7},{4,0},{5,1},{6,2},{7,3},{8,12},{9,13},{10,... | collective-permute-start | bytes 344072 | tf_op jit(solution)/shard_map/ppermute | solution.py:288
  71.1 15.4 %collective-permute-start.15 = (bf16[32,1792]{1,0:T(8,128)(2,1)S(1)}, bf16[32,1792]{1,0:T(8,128)(2,1)S(1)}, u32[]{:S(2)}, u32[]{:S(2)}) collective-permute-start(bf16[32,1792]{1,0:T(8,128)(2,1)S(1)} %get-tuple-element.87), channel_id=1, source_target_pairs={{0,15},{1,14},{2,13},{3,12},{4,11},{5,10},{6,9},{7,8},{8,7},{9,6},... | collective-permute-start | bytes 344072 | tf_op jit(solution)/shard_map/ppermute | solution.py:288
  76.5 14.2 %collective-permute-start.30 = (bf16[2,48,512]{2,1,0:T(8,128)(2,1)S(1)}, bf16[2,48,512]{2,1,0:T(8,128)(2,1)S(1)}, u32[]{:S(2)}, u32[]{:S(2)}) collective-permute-start(bf16[2,48,512]{2,1,0:T(8,128)(2,1)S(1)} %get-tuple-element.104), channel_id=1, source_target_pairs={{0,8},{1,9},{2,10},{3,11},{4,12},{5,13},{6,14},{7,15},{8,0},{9,1},... | collective-permute-start | bytes 294920 | tf_op jit(solution)/shard_map/ppermute | solution.py:288
  78.9 11.8 %collective-permute-start.31 = (bf16[2,48,512]{2,1,0:T(8,128)(2,1)S(1)}, bf16[2,48,512]{2,1,0:T(8,128)(2,1)S(1)}, u32[]{:S(2)}, u32[]{:S(2)}) collective-permute-start(bf16[2,48,512]{2,1,0:T(8,128)(2,1)S(1)} %get-tuple-element.105), channel_id=1, source_target_pairs={{0,7},{1,6},{2,5},{3,4},{4,3},{5,2},{6,1},{7,0},{8,15},{9,14},{10,... | collective-permute-start | bytes 294920 | tf_op jit(solution)/shard_map/ppermute | solution.py:288
  80.8 11.7 %collective-permute-start.32 = (bf16[2,48,512]{2,1,0:T(8,128)(2,1)S(1)}, bf16[2,48,512]{2,1,0:T(8,128)(2,1)S(1)}, u32[]{:S(2)}, u32[]{:S(2)}) collective-permute-start(bf16[2,48,512]{2,1,0:T(8,128)(2,1)S(1)} %get-tuple-element.106), channel_id=1, source_target_pairs={{0,12},{1,13},{2,14},{3,15},{4,8},{5,9},{6,10},{7,11},{8,4},{9,5},... | collective-permute-start | bytes 294920 | tf_op jit(solution)/shard_map/ppermute | solution.py:288
  82.9 11.0 %collective-permute-start.33 = (bf16[2,48,512]{2,1,0:T(8,128)(2,1)S(1)}, bf16[2,48,512]{2,1,0:T(8,128)(2,1)S(1)}, u32[]{:S(2)}, u32[]{:S(2)}) collective-permute-start(bf16[2,48,512]{2,1,0:T(8,128)(2,1)S(1)} %get-tuple-element.107), channel_id=1, source_target_pairs={{0,3},{1,2},{2,1},{3,0},{4,7},{5,6},{6,5},{7,4},{8,11},{9,10},{10,... | collective-permute-start | bytes 294920 | tf_op jit(solution)/shard_map/ppermute | solution.py:288
  86.5 11.2 %collective-permute-start.34 = (bf16[2,48,512]{2,1,0:T(8,128)(2,1)S(1)}, bf16[2,48,512]{2,1,0:T(8,128)(2,1)S(1)}, u32[]{:S(2)}, u32[]{:S(2)}) collective-permute-start(bf16[2,48,512]{2,1,0:T(8,128)(2,1)S(1)} %get-tuple-element.108), channel_id=1, source_target_pairs={{0,9},{1,8},{2,11},{3,10},{4,13},{5,12},{6,15},{7,14},{8,1},{9,0},... | collective-permute-start | bytes 294920 | tf_op jit(solution)/shard_map/ppermute | solution.py:288
  90.7 9.5 %collective-permute-start.35 = (bf16[2,48,512]{2,1,0:T(8,128)(2,1)S(1)}, bf16[2,48,512]{2,1,0:T(8,128)(2,1)S(1)}, u32[]{:S(2)}, u32[]{:S(2)}) collective-permute-start(bf16[2,48,512]{2,1,0:T(8,128)(2,1)S(1)} %get-tuple-element.109), channel_id=1, source_target_pairs={{0,6},{1,7},{2,4},{3,5},{4,2},{5,3},{6,0},{7,1},{8,14},{9,15},{10,... | collective-permute-start | bytes 294920 | tf_op jit(solution)/shard_map/ppermute | solution.py:288
  90.8 12.1 %collective-permute-start.36 = (bf16[2,48,512]{2,1,0:T(8,128)(2,1)S(1)}, bf16[2,48,512]{2,1,0:T(8,128)(2,1)S(1)}, u32[]{:S(2)}, u32[]{:S(2)}) collective-permute-start(bf16[2,48,512]{2,1,0:T(8,128)(2,1)S(1)} %get-tuple-element.110), channel_id=1, source_target_pairs={{0,13},{1,12},{2,15},{3,14},{4,9},{5,8},{6,11},{7,10},{8,5},{9,4},... | collective-permute-start | bytes 294920 | tf_op jit(solution)/shard_map/ppermute | solution.py:288
  92.5 10.3 %collective-permute-start.37 = (bf16[2,48,512]{2,1,0:T(8,128)(2,1)S(1)}, bf16[2,48,512]{2,1,0:T(8,128)(2,1)S(1)}, u32[]{:S(2)}, u32[]{:S(2)}) collective-permute-start(bf16[2,48,512]{2,1,0:T(8,128)(2,1)S(1)} %get-tuple-element.111), channel_id=1, source_target_pairs={{0,2},{1,3},{2,0},{3,1},{4,6},{5,7},{6,4},{7,5},{8,10},{9,11},{10,... | collective-permute-start | bytes 294920 | tf_op jit(solution)/shard_map/ppermute | solution.py:288
  94.0 12.6 %collective-permute-start.38 = (bf16[2,48,512]{2,1,0:T(8,128)(2,1)S(1)}, bf16[2,48,512]{2,1,0:T(8,128)(2,1)S(1)}, u32[]{:S(2)}, u32[]{:S(2)}) collective-permute-start(bf16[2,48,512]{2,1,0:T(8,128)(2,1)S(1)} %get-tuple-element.112), channel_id=1, source_target_pairs={{0,10},{1,11},{2,8},{3,9},{4,14},{5,15},{6,12},{7,13},{8,2},{9,3},... | collective-permute-start | bytes 294920 | tf_op jit(solution)/shard_map/ppermute | solution.py:288
  102.9 12.3 %collective-permute-start.42 = (bf16[2,48,512]{2,1,0:T(8,128)(2,1)S(1)}, bf16[2,48,512]{2,1,0:T(8,128)(2,1)S(1)}, u32[]{:S(2)}, u32[]{:S(2)}) collective-permute-start(bf16[2,48,512]{2,1,0:T(8,128)(2,1)S(1)} %get-tuple-element.116), channel_id=1, source_target_pairs={{0,11},{1,10},{2,9},{3,8},{4,15},{5,14},{6,13},{7,12},{8,3},{9,2},... | collective-permute-start | bytes 294920 | tf_op jit(solution)/shard_map/ppermute | solution.py:288
  (36 other events, 391.7 us)
